TPU v7x, 32 devices: a whole 2x2x4 slice. The times are simulated.
32 devices in a mesh: group: 2 (over y), dp: 8 (over z, x), tensor: 2 (over core).
Axes of the slice: x: 2, y: 2, z: 4, core: 2. Of those that a mesh axis runs over, the one named last changes fastest.
Arguments:
- activations: bfloat16 [2048, 8192], P(('group', 'dp'), 'tensor'), parts along dimension 0, may hold values from -6 to 6
- cotangent: bfloat16 [2048, 8192], P(('group', 'dp'), 'tensor'), parts along dimension 0, may hold values from -6 to 6
- adapter_weight_pair: bfloat16 [96, 2, 4096, 128], P(None, 'tensor', 'dp'), may hold values from -0.119628906 to 0.119628906
- adapter_of_block: int32 [16, 1], P('group'), parts along dimension 0, may hold values from 0 to 95
- block_live_length: int32 [16, 1], P('group'), parts along dimension 0, may hold values from 32 to 128
Outputs:
- grad_input: bfloat16 [2048, 8192], P(('group', 'dp'), 'tensor'), parts along dimension 0
- adapter_pair_gradient: bfloat16 [192, 2, 4096, 128], P('group', 'tensor', 'dp'), parts along dimension 0
There are 2 independent parts, one for each index of `group`. A program takes and returns all parts, laid end to end along the dimension named above; an argument that names none is the same for every part. Nothing has to cross between parts.
All inputs are finite; a program needn't handle non-finite values.
Results may differ from a plain program's by a relative error of at most 0.005.
Values may be sent and summed in bfloat16 or wider, within the bound.
No kernel may reach another device: no remote copies, remote signals or barrier semaphores. Data moves between devices by JAX's collectives and lax.ppermute only.
A program may use at most 128 MiB of HBM per device.

v0:
```python
import jax
import jax.numpy as jnp
from jax import lax
from jax.sharding import PartitionSpec as P

ADAPTER_COUNT = 96


adapter_alpha = 128.0


def on_device(activations, cotangent, adapter_weight_pair, adapter_of_block, block_live_length):
    owners = lax.axis_size("dp")
    here = lax.axis_index("dp")
    adapters = adapter_of_block[:, 0]
    length = block_live_length[here, 0]
    rows = activations.shape[0]
    keep = (jnp.arange(rows, dtype=jnp.int32) < length)[:, None]
    inputs = jnp.where(keep, activations, jnp.zeros_like(activations))
    grads_out = jnp.where(keep, cotangent, jnp.zeros_like(cotangent))
    lookup_table = adapter_weight_pair[:, 0]
    width = lookup_table.shape[-1]
    adapter_rank_value = width // 2
    branch_scale = adapter_alpha / adapter_rank_value
    outgoing = lookup_table[adapters]
    fetched = lax.all_to_all(outgoing, "dp", split_axis=0, concat_axis=0, tiled=True)
    pair = fetched.reshape(-1, width)
    down = pair[:, :adapter_rank_value]
    upward = pair[:, adapter_rank_value:]
    hidden_part = jnp.dot(inputs, down, preferred_element_type=jnp.float32)
    dhidden_part = branch_scale * jnp.dot(grads_out, upward, preferred_element_type=jnp.float32)
    hidden, dhidden = lax.psum((hidden_part, dhidden_part), "tensor")
    hidden16 = hidden.astype(jnp.bfloat16)
    dhidden16 = dhidden.astype(jnp.bfloat16)
    d_down = jnp.dot(inputs.T, dhidden16, preferred_element_type=jnp.float32)
    d_up = branch_scale * jnp.dot(grads_out.T, hidden16, preferred_element_type=jnp.float32)
    pieces = jnp.concatenate([d_down, d_up], axis=1).reshape(owners, -1, width)
    onehot = (adapters[None, :] == jnp.arange(ADAPTER_COUNT, dtype=jnp.int32)[:, None]).astype(
        jnp.float32
    )
    token_count = jnp.sum(onehot * block_live_length[:, 0][None, :].astype(jnp.float32), axis=1)
    denom = jnp.maximum(token_count, 1.0)[:, None, None]
    summed = jax.ops.segment_sum(
        lax.all_to_all(pieces, "dp", split_axis=0, concat_axis=0, tiled=True),
        adapters,
        num_segments=ADAPTER_COUNT,
    )
    gathered = (summed / denom).astype(jnp.bfloat16)
    grad_input = jnp.dot(dhidden16, down.T, preferred_element_type=jnp.float32).astype(jnp.bfloat16)
    return (grad_input, gathered[:, None])


def solution(mesh):
    in_specs = (
        P(("group", "dp"), "tensor"),
        P(("group", "dp"), "tensor"),
        P(None, "tensor", "dp", None),
        P("group", None),
        P("group", None),
    )
    out_specs = (P(("group", "dp"), "tensor"), P("group", "tensor", "dp", None))
    return jax.shard_map(
        on_device, mesh=mesh, in_specs=in_specs, out_specs=out_specs, check_vma=False
    )
```

profile of v0, /device:TPU:0, one launch (start us, length us, event | category | flops | bytes accessed | tf_op | source)
XLA Modules:
  0.0 134.8 jit_solution(173982066126873721)
XLA Ops:
  0.6 0.0 copy-start
  0.6 0.7 fusion.9
  1.4 6.2 %gather_fusion = bf16[8,512,128]{2,1,0:T(8,128)(2,1)} fusion(bf16[96,512,128]{2,1,0:T(8,128)(2,1)} %bitcast.18, s32[1024]{0:T(1024)S(1)} %pad_clamp_fusion), kind=kCustom, calls=%fused_computation | custom fusion | bytes 2097184 | tf_op jit(solution)/shard_map/gather | solution.py:25
  7.6 0.0 copy-start.2
  7.6 0.0 copy-start.1
  7.6 7.4 %all-to-all-start = ((bf16[8,512,128]{2,1,0:T(8,128)(2,1)}), bf16[8,512,128]{2,1,0:T(8,128)(2,1)S(1)}, u32[]{:S(2)}, u32[]{:S(2)}) async-start(bf16[8,512,128]{2,1,0:T(8,128)(2,1)} %gather_fusion), calls=%async_computation | async-start | bytes 2097152 | tf_op jit(solution)/shard_map/all_to_all | solution.py:26
  15.0 1.2 constant_dynamic-slice_fusion
  16.2 0.6 iota_compare_fusion.1
  16.9 23.9 %all-to-all-done = bf16[8,512,128]{2,1,0:T(8,128)(2,1)S(1)} async-done(((bf16[8,512,128]{2,1,0:T(8,128)(2,1)}), bf16[8,512,128]{2,1,0:T(8,128)(2,1)S(1)}, u32[]{:S(2)}, u32[]{:S(2)}) %all-to-all-start) | async-done | bytes 1048608 | tf_op jit(solution)/shard_map/all_to_all | solution.py:26
  40.8 2.3 %convolution_multiply_fusion.1 = f32[128,64]{0,1:T(8,128)S(1)} fusion(bf16[4096,128]{1,0:T(8,128)(2,1)S(1)} %bitcast.15, bf16[128,4096]{1,0:T(8,128)(2,1)} %param.6, pred[128]{0:T(512)(128)(4,1)S(1)} %iota_compare_fusion.1), kind=kOutput, calls=%fused_computation.7 | convolution fusion | flops 67641344 | bytes 2130048 | tf_op jit(solution)/shard_map/dot_general | solution.py:31
  43.0 1.7 %fusion.2 = f32[128,64]{1,0:T(8,128)S(1)} fusion(bf16[4096,128]{1,0:T(8,128)(2,1)S(1)} %bitcast.16, bf16[128,4096]{1,0:T(8,128)(2,1)} %param.5, pred[128]{0:T(512)(128)(4,1)S(1)} %iota_compare_fusion.1), kind=kOutput, calls=%fused_computation.11 | convolution fusion | flops 67633152 | bytes 2130048 | tf_op jit(solution)/shard_map/dot_general | solution.py:30
  44.8 3.7 %all-reduce = (bf16[128,64]{0,1:T(8,128)(2,1)S(1)}, bf16[128,64]{1,0:T(8,128)(2,1)S(1)}) all-reduce(f32[128,64]{0,1:T(8,128)S(1)} %convolution_multiply_fusion.1, f32[128,64]{1,0:T(8,128)S(1)} %fusion.2), channel_id=1, replica_groups=mesh['group'=2,'dp'=8,'tensor'=2] {'tensor'}, use_global_device_ids=true, to_apply=%region_0.1 | all-reduce | flops 16384 | bytes 98304 | tf_op jit(solution)/shard_map/psum | solution.py:32
  48.5 1.6 %convolution_multiply_fusion = f32[4096,64]{0,1:T(8,128)S(1)} fusion(bf16[128,4096]{1,0:T(8,128)(2,1)} %param.6, pred[128]{0:T(512)(128)(4,1)S(1)} %iota_compare_fusion.1, bf16[128,64]{1,0:T(8,128)(2,1)S(1)} %get-tuple-element.3), kind=kOutput, calls=%fused_computation.5 | convolution fusion | flops 67895296 | bytes 2113664 | tf_op jit(solution)/shard_map/dot_general | solution.py:36
  50.1 0.0 copy-done
  50.1 0.4 fusion.5
  50.5 0.1 pad_maximum_fusion
  50.6 1.8 %copy.9 = f32[4096,128]{1,0:T(8,128)} copy(f32[4096,128]{0,1:T(8,128)S(1)} %pad_maximum_fusion) | data formatting | bytes 4194304 | tf_op jit(solution)/shard_map/reshape | solution.py:37
  52.5 3.6 %all-to-all-start.1 = ((f32[8,512,128]{2,1,0:T(8,128)}), f32[8,512,128]{2,1,0:T(8,128)S(1)}, u32[]{:S(2)}, u32[]{:S(2)}) async-start(f32[8,512,128]{2,1,0:T(8,128)} %bitcast.14), calls=%async_computation.1 | async-start | bytes 4194304 | tf_op jit(solution)/shard_map/all_to_all | solution.py:44
  56.1 0.0 copy-done.2
  56.1 0.0 copy-done.1
  56.1 0.1 select_reduce_fusion
  56.2 1.4 %convolution_convert_fusion = bf16[128,4096]{1,0:T(8,128)(2,1)} fusion(bf16[4096,128]{1,0:T(8,128)(2,1)S(1)} %bitcast.17, bf16[128,64]{0,1:T(8,128)(2,1)S(1)} %get-tuple-element.2), kind=kOutput, calls=%fused_computation.4 | convolution fusion | flops 67633152 | bytes 2113536 | tf_op jit(solution)/shard_map/dot_general | solution.py:49
  57.6 47.4 %all-to-all-done.1 = f32[8,512,128]{2,1,0:T(8,128)S(1)} async-done(((f32[8,512,128]{2,1,0:T(8,128)}), f32[8,512,128]{2,1,0:T(8,128)S(1)}, u32[]{:S(2)}, u32[]{:S(2)}) %all-to-all-start.1) | async-done | bytes 2097184 | tf_op jit(solution)/shard_map/all_to_all | solution.py:44
  105.0 11.4 %broadcast_in_dim.22 = f32[96,512,128]{2,1,0:T(8,128)} broadcast(f32[]{:T(128)} %constant.7.clone.1), dimensions={} | broadcast | bytes 25165828 | tf_op jit(solution)/shard_map/broadcast_in_dim | solution.py:43
  116.4 4.4 %scatter_fusion = f32[96,512,128]{2,1,0:T(8,128)} fusion(f32[96,512,128]{2,1,0:T(8,128)} %broadcast_in_dim.22, s32[8]{0:T(128)S(1)} %bitcast.20, f32[8,512,128]{2,1,0:T(8,128)S(1)} %all-to-all-done.1), kind=kCustom, calls=%fused_computation.1 | custom fusion | flops 524288 | bytes 6291488 | tf_op jit(solution)/shard_map/scatter-add | solution.py:43
  120.8 14.0 %fusion = bf16[96,1,512,128]{3,2,1,0:T(8,128)(2,1)} fusion(f32[96,512,128]{2,1,0:T(8,128)} %scatter_fusion, f32[96]{0:T(128)S(1)} %broadcast_maximum_fusion), kind=kLoop, calls=%fused_computation.3 | loop fusion | flops 12582912 | bytes 37749120 | tf_op jit(solution)/shard_map/broadcast_in_dim | solution.py:50
  (3 shorter events, 0.0 us)
Async XLA Ops:
  0.6 49.5 %copy-start = (bf16[128,4096]{1,0:T(8,128)(2,1)S(1)}, bf16[128,4096]{1,0:T(8,128)(2,1)}, u32[]{:S(2)}) copy-start(bf16[128,4096]{1,0:T(8,128)(2,1)} %param.5) | copy-start | bytes 3145732
  7.6 48.5 %copy-start.2 = (s32[8,1]{0,1:T(1,128)S(1)}, s32[8,1]{0,1:T(1,128)}, u32[]{:S(2)}) copy-start(s32[8,1]{0,1:T(1,128)} %param.9) | copy-start | bytes 100
  7.6 48.5 %copy-start.1 = (s32[8,1]{0,1:T(1,128)S(1)}, s32[8,1]{0,1:T(1,128)}, u32[]{:S(2)}) copy-start(s32[8,1]{0,1:T(1,128)} %param.8) | copy-start | bytes 100
  7.6 33.2 %all-to-all-start = ((bf16[8,512,128]{2,1,0:T(8,128)(2,1)}), bf16[8,512,128]{2,1,0:T(8,128)(2,1)S(1)}, u32[]{:S(2)}, u32[]{:S(2)}) async-start(bf16[8,512,128]{2,1,0:T(8,128)(2,1)} %gather_fusion), calls=%async_computation | async-start | bytes 2097152 | tf_op jit(solution)/shard_map/all_to_all | solution.py:26
  52.5 52.5 %all-to-all-start.1 = ((f32[8,512,128]{2,1,0:T(8,128)}), f32[8,512,128]{2,1,0:T(8,128)S(1)}, u32[]{:S(2)}, u32[]{:S(2)}) async-start(f32[8,512,128]{2,1,0:T(8,128)} %bitcast.14), calls=%async_computation.1 | async-start | bytes 4194304 | tf_op jit(solution)/shard_map/all_to_all | solution.py:44
where the time goes:
time: 135 us
  waiting for transfers between devices  71.2 us (53%)
  local copies, waits for them, and re-layouts  20.7 us (15%)
  other arithmetic  20 us (15%)
  starting transfers between devices  11 us (8%)
  matrix products  7.38 us (5%)
  blocking collectives  3.74 us (3%)
    all_to_all x1, waiting for transfers between devices, on_device(): lax.all_to_all(pieces, 'dp', split_axis=0, concat_axis=0, tiled=True)  47.4 us
    all_to_all x1, waiting for transfers between devices, on_device(): lax.all_to_all(outgoing, 'dp', split_axis=0, concat_axis=0, tiled=True)  23.9 us
    broadcast_in_dim x1, other arithmetic, on_device(): return (grad_input, gathered[:, None])  14 us
    broadcast_in_dim x1, local copies, waits for them, and re-layouts, on_device(): jax.ops.segment_sum(lax.all_to_all(pieces, 'dp', split_axis=0, concat_axi...  11.4 us
    all_to_all x1, starting transfers between devices, on_device(): lax.all_to_all(outgoing, 'dp', split_axis=0, concat_axis=0, tiled=True)  7.38 us
    gather x1, local copies, waits for them, and re-layouts, on_device(): outgoing = lookup_table[adapters]  6.22 us
    scatter-add x1, other arithmetic, on_device(): jax.ops.segment_sum(lax.all_to_all(pieces, 'dp', split_axis=0, concat_axi...  4.4 us
    psum x1, blocking collectives, on_device(): hidden, dhidden = lax.psum((hidden_part, dhidden_part), 'tensor')  3.74 us
  transfers between devices with their start and end apart: 2, of which 2 were waited for; matrix products, arithmetic and copies ran while one was open for 3% of the time, Pallas kernels for 0%

commit v1 on v0

v1 whole, which is shorter than its diff:
```python
import functools

import jax
import jax.numpy as jnp
from jax import lax
from jax.experimental import pallas as pl
from jax.experimental.pallas import tpu as pltpu
from jax.sharding import PartitionSpec as P

adapter_alpha = 128.0
VMEM_LIMIT = 40 * 1024 * 1024

in_vmem = pl.BlockSpec(memory_space=pltpu.VMEM)
in_smem = pl.BlockSpec(memory_space=pltpu.SMEM)
in_hbm = pl.BlockSpec(memory_space=pltpu.HBM)


def low_lanes(rows, width):
    return lax.broadcasted_iota(jnp.int32, (rows, width), 1) < width // 2


def swap_halves(value):
    return pltpu.roll(value, value.shape[-1] // 2, 1)


def call(kernel, out_shape, in_specs, out_specs, scratch=(), flops=0, moved=0, aliases=None):
    return pl.pallas_call(
        kernel,
        out_shape=out_shape,
        in_specs=in_specs,
        out_specs=out_specs,
        scratch_shapes=list(scratch),
        input_output_aliases=aliases or {},
        compiler_params=pltpu.CompilerParams(vmem_limit_bytes=VMEM_LIMIT),
        cost_estimate=pl.CostEstimate(flops=flops, bytes_accessed=moved, transcendentals=0),
    )


def pack_kernel(owners, ids, here, table, *refs):
    up, down = refs[:owners], refs[owners : 2 * owners]
    held, sems = refs[2 * owners :]
    half = held.shape[1] // 2
    me = here[0]
    copies = []
    for k in range(owners):
        adapter = ids[me ^ k, 0]
        copies.append(pltpu.make_async_copy(table.at[adapter], held.at[k], sems.at[k]))
        copies[-1].start()
    low = low_lanes(half, held.shape[2])
    for k in range(owners):
        copies[k].wait()
        first = held[k, :half].astype(jnp.float32)
        second = held[k, half:].astype(jnp.float32)
        up[k][...] = jnp.where(low, swap_halves(first), second).astype(jnp.bfloat16)
        down[k][...] = jnp.where(low, first, swap_halves(second)).astype(jnp.bfloat16)


def prep_kernel(half, after, x, y, x_turned, y_turned, blank, zeros, sem):
    zeros[...] = jnp.zeros_like(zeros)
    step = zeros.shape[0]
    copies = [
        pltpu.make_async_copy(zeros, blank.at[pl.ds(s, step)], sem.at[s // step])
        for s in range(0, blank.shape[0], step)
    ]
    for copy in copies:
        copy.start()
    owners = x.shape[1] // (2 * half)
    tokens = x.shape[0]

    @pl.loop(0, owners)
    def _(owner):
        for part in range(2):
            columns = pl.ds(pl.multiple_of(owner * 2 * half + part * half, half), half)
            lanes = pl.ds(part * tokens, tokens)
            x_turned[owner, :, lanes] = x[:, columns].T
            y_turned[owner, :, lanes] = y[:, columns].T

    for copy in copies:
        copy.wait()


def rank_kernel(owners, here, tokens, *refs):
    packed, out = refs[:owners], refs[owners]
    half, width = packed[0].shape
    me = here[0]
    first = jnp.zeros((tokens.shape[0], width), jnp.float32)
    second = jnp.zeros((tokens.shape[0], width), jnp.float32)
    for k in range(owners):
        start = (me ^ k) * (2 * half)
        lo = tokens[:, pl.ds(pl.multiple_of(start, half), half)]
        hi = tokens[:, pl.ds(pl.multiple_of(start + half, half), half)]
        first += jnp.dot(lo, packed[k][...], preferred_element_type=jnp.float32)
        second += jnp.dot(hi, packed[k][...], preferred_element_type=jnp.float32)
    out[...] = jnp.where(low_lanes(*out.shape), first, second)


def rounded_twice(mine, other, length, scale):
    total = mine[...] + other[...]
    total = scale * (total + swap_halves(total))
    rows, width = total.shape
    live = lax.broadcasted_iota(jnp.int32, (rows, width), 0) < length
    total = jnp.where(live, total, 0.0)
    low = low_lanes(rows, width)
    top = jnp.where(low, total, 0.0).astype(jnp.bfloat16)
    bottom = jnp.where(low, 0.0, total).astype(jnp.bfloat16)
    return jnp.concatenate([top, bottom], axis=0)


def piece_kernel(owners, scale, out_scale, here, lengths, mine, other, turned, *refs):
    me = here[0]
    pair = rounded_twice(mine, other, lengths[me, 0], scale)
    for k in range(owners):
        piece = jnp.dot(turned[me ^ k], pair, preferred_element_type=jnp.float32)
        refs[k][...] = (out_scale * piece).astype(jnp.bfloat16)


def input_kernel(owners, scale, here, lengths, mine, other, *refs):
    packed, out = refs[:owners], refs[owners]
    me = here[0]
    pair = rounded_twice(mine, other, lengths[me, 0], scale)
    rows = out.shape[0]
    half = packed[0].shape[0]
    for k in range(owners):
        both = lax.dot_general(
            pair, packed[k][...], (((1,), (1,)), ((), ())), preferred_element_type=jnp.float32
        ).astype(jnp.bfloat16)
        start = (me ^ k) * (2 * half)
        out[:, pl.ds(pl.multiple_of(start, half), half)] = both[:rows]
        out[:, pl.ds(pl.multiple_of(start + half, half), half)] = both[rows:]


def merge_kernel(owners, ids, here, lengths, *refs):
    down, up = refs[:owners], refs[owners : 2 * owners]
    out, total, held, sems = refs[2 * owners + 1 :]
    me = here[0]
    half = held.shape[1] // 2
    low = low_lanes(half, held.shape[2])
    copies = []
    for k in range(owners):
        adapter = ids[me ^ k, 0]
        copies.append(pltpu.make_async_copy(held.at[k], out.at[adapter], sems.at[k]))
        same = [ids[me ^ other, 0] == adapter for other in range(owners)]
        earlier = functools.reduce(jnp.logical_or, same[:k], jnp.bool_(False))

        @pl.when(jnp.logical_not(earlier))
        def _():
            total[0] = down[k][...].astype(jnp.float32)
            total[1] = up[k][...].astype(jnp.float32)
            count = lengths[me ^ k, 0]
            for other in range(k + 1, owners):
                count += jnp.where(same[other], lengths[me ^ other, 0], 0)

                @pl.when(same[other])
                def _():
                    total[0] += down[other][...].astype(jnp.float32)
                    total[1] += up[other][...].astype(jnp.float32)

            denom = jnp.maximum(count.astype(jnp.float32), 1.0)
            g_down = total[0] / denom
            g_up = total[1] / denom
            held[k, :half] = jnp.where(low, g_down, swap_halves(g_up)).astype(jnp.bfloat16)
            held[k, half:] = jnp.where(low, swap_halves(g_down), g_up).astype(jnp.bfloat16)
            copies[k].start()

    for k in range(owners):
        adapter = ids[me ^ k, 0]
        same = [ids[me ^ other, 0] == adapter for other in range(k)]
        earlier = functools.reduce(jnp.logical_or, same, jnp.bool_(False))
        pl.when(jnp.logical_not(earlier))(copies[k].wait)


def send_all(pieces, owners):
    order = sorted(range(1, owners), reverse=True)
    out = {0: pieces[0]}
    for k in order:
        out[k] = lax.ppermute(pieces[k], "dp", [(i, i ^ k) for i in range(owners)])
    return [out[k] for k in range(owners)]


def across_cores(value):
    cores = lax.axis_size("tensor")
    return lax.ppermute(value, "tensor", [(i, i ^ 1) for i in range(cores)])


def with_kernels(activations, cotangent, adapter_weight_pair, adapter_of_block, block_live_length):
    owners = lax.axis_size("dp")
    here = lax.axis_index("dp").astype(jnp.int32).reshape(1)
    count, _, rows, width = adapter_weight_pair.shape
    table = adapter_weight_pair.reshape(count, rows, width)
    tokens, features = activations.shape
    half = rows // 2
    scale = adapter_alpha / (width // 2)
    bf16, f32 = jnp.bfloat16, jnp.float32
    packed_shape = jax.ShapeDtypeStruct((half, width), bf16)
    packed_bytes = half * width * 2

    sent = call(
        functools.partial(pack_kernel, owners),
        [packed_shape] * (2 * owners),
        [in_smem, in_smem, in_hbm],
        [in_vmem] * (2 * owners),
        [pltpu.VMEM((owners, rows, width), bf16), pltpu.SemaphoreType.DMA((owners,))],
        moved=4 * owners * packed_bytes,
    )(adapter_of_block, here, table)
    up = send_all(sent[:owners], owners)
    down = send_all(sent[owners:], owners)

    step = 8
    turned_shape = jax.ShapeDtypeStruct((owners, half, 2 * tokens), bf16)
    x_turned, y_turned, blank = call(
        functools.partial(prep_kernel, half),
        [turned_shape, turned_shape, jax.ShapeDtypeStruct(table.shape, bf16)],
        [in_hbm, in_vmem, in_vmem],
        [in_vmem, in_vmem, in_hbm],
        [pltpu.VMEM((step, rows, width), bf16), pltpu.SemaphoreType.DMA((count // step,))],
        moved=8 * tokens * features + 2 * count * rows * width,
    )(sent[0], activations, cotangent)

    partial_shape = jax.ShapeDtypeStruct((tokens, width), f32)

    def rank_product(values, packed):
        return call(
            functools.partial(rank_kernel, owners),
            partial_shape,
            [in_smem, in_vmem] + [in_vmem] * owners,
            in_vmem,
            flops=2 * tokens * features * width,
            moved=2 * tokens * features + owners * packed_bytes,
        )(here, values, *packed)

    def pieces(mine, other, turned, in_scale, out_scale):
        return call(
            functools.partial(piece_kernel, owners, in_scale, out_scale),
            [packed_shape] * owners,
            [in_smem, in_smem, in_vmem, in_vmem, in_vmem],
            [in_vmem] * owners,
            flops=2 * tokens * features * width,
            moved=2 * tokens * features + owners * packed_bytes,
        )(here, block_live_length, mine, other, turned)

    dhidden = rank_product(cotangent, up)
    dhidden_other = across_cores(dhidden)
    d_down = send_all(pieces(dhidden, dhidden_other, x_turned, scale, 1.0), owners)
    hidden = rank_product(activations, down)
    hidden_other = across_cores(hidden)
    d_up = send_all(pieces(hidden, hidden_other, y_turned, 1.0, scale), owners)

    grad_input = call(
        functools.partial(input_kernel, owners, scale),
        jax.ShapeDtypeStruct((tokens, features), bf16),
        [in_smem, in_smem, in_vmem, in_vmem] + [in_vmem] * owners,
        in_vmem,
        flops=2 * tokens * features * width,
        moved=2 * tokens * features + owners * packed_bytes,
    )(here, block_live_length, dhidden, dhidden_other, *down)

    gradient = call(
        functools.partial(merge_kernel, owners),
        jax.ShapeDtypeStruct(table.shape, bf16),
        [in_smem] * 3 + [in_vmem] * (2 * owners) + [in_hbm],
        in_hbm,
        [
            pltpu.VMEM((2, half, width), f32),
            pltpu.VMEM((owners, rows, width), bf16),
            pltpu.SemaphoreType.DMA((owners,)),
        ],
        moved=4 * owners * packed_bytes,
        aliases={3 + 2 * owners: 0},
    )(adapter_of_block, here, block_live_length, *d_down, *d_up, blank)
    return grad_input, gradient[:, None]


def without_kernels(activations, cotangent, adapter_weight_pair, adapter_of_block, block_live_length):
    owners = lax.axis_size("dp")
    here = lax.axis_index("dp")
    count, _, rows, width = adapter_weight_pair.shape
    rank = width // 2
    scale = adapter_alpha / rank
    adapters = adapter_of_block[:, 0]
    lengths = block_live_length[:, 0]
    keep = (jnp.arange(activations.shape[0], dtype=jnp.int32) < lengths[here])[:, None]
    inputs = jnp.where(keep, activations, jnp.zeros_like(activations))
    grads_out = jnp.where(keep, cotangent, jnp.zeros_like(cotangent))
    fetched = lax.all_to_all(
        adapter_weight_pair[:, 0][adapters], "dp", split_axis=0, concat_axis=0, tiled=True
    )
    pair = fetched.reshape(-1, width)
    down, upward = pair[:, :rank], pair[:, rank:]
    f32 = jnp.float32
    hidden_part = jnp.dot(inputs, down, preferred_element_type=f32)
    dhidden_part = scale * jnp.dot(grads_out, upward, preferred_element_type=f32)
    hidden, dhidden = lax.psum((hidden_part, dhidden_part), "tensor")
    hidden16, dhidden16 = hidden.astype(jnp.bfloat16), dhidden.astype(jnp.bfloat16)
    d_down = jnp.dot(inputs.T, dhidden16, preferred_element_type=f32)
    d_up = scale * jnp.dot(grads_out.T, hidden16, preferred_element_type=f32)
    sent = jnp.concatenate([d_down, d_up], axis=1).astype(jnp.bfloat16).reshape(owners, rows, width)
    received = lax.all_to_all(sent, "dp", split_axis=0, concat_axis=0, tiled=True).astype(f32)
    same = adapters[:, None] == adapters[None, :]
    total = jnp.sum(jnp.where(same, lengths[None, :], 0), axis=1).astype(f32)
    summed = jax.ops.segment_sum(received, adapters, num_segments=count)
    denom = jnp.ones((count,), f32).at[adapters].set(jnp.maximum(total, 1.0))
    gradient = (summed / denom[:, None, None]).astype(jnp.bfloat16)
    grad_input = jnp.dot(dhidden16, down.T, preferred_element_type=f32).astype(jnp.bfloat16)
    return grad_input, gradient[:, None]


def solution(mesh):
    owners, cores = mesh.shape["dp"], mesh.shape["tensor"]

    def on_device(activations, cotangent, adapter_weight_pair, *rest):
        rows = adapter_weight_pair.shape[2]
        fits = owners & (owners - 1) == 0 and cores == 2 and rows % 256 == 0
        body = with_kernels if fits else without_kernels
        return body(activations, cotangent, adapter_weight_pair, *rest)

    in_specs = (
        P(("group", "dp"), "tensor"),
        P(("group", "dp"), "tensor"),
        P(None, "tensor", "dp", None),
        P("group", None),
        P("group", None),
    )
    out_specs = (P(("group", "dp"), "tensor"), P("group", "tensor", "dp", None))
    return jax.shard_map(
        on_device, mesh=mesh, in_specs=in_specs, out_specs=out_specs, check_vma=False
    )
```

time: 135 us -> 76.3 us (0.57)
  waiting for transfers between devices: 71.2 us -> 5.86 us
  starting transfers between devices: 11 us -> 48.7 us
  other arithmetic: 20 us -> 0 us
  Pallas kernels: 0 us -> 15.4 us
  local copies, waits for them, and re-layouts: 20.7 us -> 5.4 us
  matrix products: 7.38 us -> 0 us
  blocking collectives: 3.74 us -> 0 us
    all_to_all x2 -> x0, waiting for transfers between devices: 71.2 us -> none  [the longest x1 47.4 us: on_device(): lax.all_to_all(pieces, 'dp', split_axis=0, concat_axis=0, tiled=True)]
    ppermute x0 -> x30, starting transfers between devices: none -> 48.7 us  [the longest x28 48.6 us: send_all(): out[k] = lax.ppermute(pieces[k], 'dp', [(i, i ^ k) for i in range(owners)])]
    pallas_call x0 -> x8, Pallas kernels: none -> 15.4 us  [the longest x1 4.8 us: with_kernels(): call(functools.partial(prep_kernel, half), [turned_shape, turned_shape, j...]
    broadcast_in_dim x1 -> x0, other arithmetic: 14 us -> none  [on_device(): return (grad_input, gathered[:, None])]
    broadcast_in_dim x1 -> x0, local copies, waits for them, and re-layouts: 11.4 us -> none  [on_device(): jax.ops.segment_sum(lax.all_to_all(pieces, 'dp', split_axis=0, concat_axi...]
    all_to_all x2 -> x0, starting transfers between devices: 11 us -> none  [the longest x1 7.38 us: on_device(): lax.all_to_all(outgoing, 'dp', split_axis=0, concat_axis=0, tiled=True)]
    dot_general x5 -> x0, matrix products: 7.38 us -> none  [the longest x1 2.26 us: on_device(): jnp.dot(grads_out, upward, preferred_element_type=jnp.float32)]
    gather x1 -> x0, local copies, waits for them, and re-layouts: 6.22 us -> none  [on_device(): outgoing = lookup_table[adapters]]
  transfers between devices with their start and end apart: 2 -> 30, of which waited for: 2 -> 5; matrix products, arithmetic and copies ran while one was open for 3% -> 0% of each run, Pallas kernels for 0% -> 13%
where the time goes in v1:
time: 76.3 us; the launch traced here: 76.2 us
  starting transfers between devices  48.7 us (64%)
  Pallas kernels  15.4 us (20%)
  waiting for transfers between devices  5.86 us (8%)
  local copies, waits for them, and re-layouts  5.4 us (7%)
  between operations  0.79 us (1%)
    ppermute x28, starting transfers between devices, send_all(): out[k] = lax.ppermute(pieces[k], 'dp', [(i, i ^ k) for i in range(owners)])  48.6 us
    ppermute x28, waiting for transfers between devices, send_all(): out[k] = lax.ppermute(pieces[k], 'dp', [(i, i ^ k) for i in range(owners)])  5.85 us
    unnamed x10, local copies, waits for them, and re-layouts  5.4 us
    pallas_call x1, Pallas kernels, with_kernels(): call(functools.partial(prep_kernel, half), [turned_shape, turned_shape, j...  4.8 us
    pallas_call x1, Pallas kernels, with_kernels(): call(functools.partial(pack_kernel, owners), [packed_shape] * (2 * owners...  2.93 us
    pallas_call x1, Pallas kernels, with_kernels(): call(functools.partial(merge_kernel, owners), jax.ShapeDtypeStruct(table....  2.59 us
    pallas_call x2, Pallas kernels, pieces(): call(functools.partial(piece_kernel, owners, in_scale, out_scale), [packe...  2.18 us
    pallas_call x1, Pallas kernels, with_kernels(): call(functools.partial(input_kernel, owners, scale), jax.ShapeDtypeStruct...  2.07 us
  transfers between devices with their start and end apart: 30, of which 5 were waited for; matrix products, arithmetic and copies ran while one was open for 0% of the time, Pallas kernels for 13%

profile of v1, /device:TPU:0, one launch (start us, length us, event | category | flops | bytes accessed | tf_op | source)
XLA Modules:
  0.0 76.2 jit_solution(17159690469334212783)
XLA Ops:
  1.4 4.6 %copy-done = bf16[96,1,512,128]{3,2,1,0:T(8,128)(2,1)S(1)} copy-done((bf16[96,1,512,128]{3,2,1,0:T(8,128)(2,1)S(1)}, bf16[96,1,512,128]{3,2,1,0:T(8,128)(2,1)}, u32[]{:S(2)}) %copy-start) | copy-done | bytes 12582936
  6.0 2.9 %shard_map.68 = (bf16[256,128]{1,0:T(8,128)(2,1)S(1)}, bf16[256,128]{1,0:T(8,128)(2,1)S(1)}, bf16[256,128]{1,0:T(8,128)(2,1)S(1)}, bf16[256,128]{1,0:T(8,128)(2,...) custom-call(s32[8,1]{1,0:T(8,128)S(1)} %copy.8.ids, ...), custom_call_target="tpu_custom_call" | custom-call | bytes 2097152 | tf_op jit(solution)/shard_map/pallas_call | solution.py:197
  8.9 4.0 %collective-permute-start.10 = (bf16[256,128]{1,0:T(8,128)(2,1)S(1)}, bf16[256,128]{1,0:T(8,128)(2,1)S(1)}, u32[]{:S(2)}, u32[]{:S(2)}) collective-permute-start(bf16[256,128]{1,0:T(8,128)(2,1)S(1)} %get-tuple-element.48), channel_id=1, source_target_pairs={{0,6},{2,4},{4,2},{6,0},{8,14},{10,12},{12,10},{14,8},{1,7},{3,5},... | collective-permute-start | bytes 196616 | tf_op jit(solution)/shard_map/ppermute | solution.py:176
  12.9 2.6 %collective-permute-start.11 = (bf16[256,128]{1,0:T(8,128)(2,1)S(1)}, bf16[256,128]{1,0:T(8,128)(2,1)S(1)}, u32[]{:S(2)}, u32[]{:S(2)}) collective-permute-start(bf16[256,128]{1,0:T(8,128)(2,1)S(1)} %get-tuple-element.49), channel_id=1, source_target_pairs={{0,8},{2,10},{4,12},{6,14},{8,0},{10,2},{12,4},{14,6},{1,9},{3,11}... | collective-permute-start | bytes 196616 | tf_op jit(solution)/shard_map/ppermute | solution.py:176
  15.8 2.5 %collective-permute-start.13 = (bf16[256,128]{1,0:T(8,128)(2,1)S(1)}, bf16[256,128]{1,0:T(8,128)(2,1)S(1)}, u32[]{:S(2)}, u32[]{:S(2)}) collective-permute-start(bf16[256,128]{1,0:T(8,128)(2,1)S(1)} %get-tuple-element.51), channel_id=1, source_target_pairs={{0,12},{2,14},{4,8},{6,10},{8,4},{10,6},{12,0},{14,2},{1,13},{3,15... | collective-permute-start | bytes 196616 | tf_op jit(solution)/shard_map/ppermute | solution.py:176
  18.3 2.3 %collective-permute-start.14 = (bf16[256,128]{1,0:T(8,128)(2,1)S(1)}, bf16[256,128]{1,0:T(8,128)(2,1)S(1)}, u32[]{:S(2)}, u32[]{:S(2)}) collective-permute-start(bf16[256,128]{1,0:T(8,128)(2,1)S(1)} %get-tuple-element.52), channel_id=1, source_target_pairs={{0,14},{2,12},{4,10},{6,8},{8,6},{10,4},{12,2},{14,0},{1,15},{3,13... | collective-permute-start | bytes 196616 | tf_op jit(solution)/shard_map/ppermute | solution.py:176
  21.1 1.9 %collective-permute-start.9 = (bf16[256,128]{1,0:T(8,128)(2,1)S(1)}, bf16[256,128]{1,0:T(8,128)(2,1)S(1)}, u32[]{:S(2)}, u32[]{:S(2)}) collective-permute-start(bf16[256,128]{1,0:T(8,128)(2,1)S(1)} %get-tuple-element.47), channel_id=1, source_target_pairs={{0,4},{2,6},{4,0},{6,2},{8,12},{10,14},{12,8},{14,10},{1,5},{3,7},... | collective-permute-start | bytes 196616 | tf_op jit(solution)/shard_map/ppermute | solution.py:176
  23.0 1.4 %collective-permute-done.12.refs_5_ = bf16[256,128]{1,0:T(8,128)(2,1)S(1)} collective-permute-done((bf16[256,128]{1,0:T(8,128)(2,1)S(1)}, bf16[256,128]{1,0:T(8,128)(2,1)S(1)}, u32[]{:S(2)}, u32[]{:S(2)}) %collective-permute-start.12) | collective-permute-done | bytes 65568 | tf_op jit(solution)/shard_map/ppermute | solution.py:176
  24.4 1.0 %collective-permute-start = (bf16[256,128]{1,0:T(8,128)(2,1)S(1)}, bf16[256,128]{1,0:T(8,128)(2,1)S(1)}, u32[]{:S(2)}, u32[]{:S(2)}) collective-permute-start(bf16[256,128]{1,0:T(8,128)(2,1)S(1)} %get-tuple-element.38), channel_id=1, source_target_pairs={{0,2},{2,0},{4,6},{6,4},{8,10},{10,8},{12,14},{14,12},{1,3},{3,1},... | collective-permute-start | bytes 196616 | tf_op jit(solution)/shard_map/ppermute | solution.py:176
  25.4 1.2 %collective-permute-start.1 = (bf16[256,128]{1,0:T(8,128)(2,1)S(1)}, bf16[256,128]{1,0:T(8,128)(2,1)S(1)}, u32[]{:S(2)}, u32[]{:S(2)}) collective-permute-start(bf16[256,128]{1,0:T(8,128)(2,1)S(1)} %get-tuple-element.39), channel_id=1, source_target_pairs={{0,4},{2,6},{4,0},{6,2},{8,12},{10,14},{12,8},{14,10},{1,5},{3,7},... | collective-permute-start | bytes 196616 | tf_op jit(solution)/shard_map/ppermute | solution.py:176
  26.6 2.2 %collective-permute-start.2 = (bf16[256,128]{1,0:T(8,128)(2,1)S(1)}, bf16[256,128]{1,0:T(8,128)(2,1)S(1)}, u32[]{:S(2)}, u32[]{:S(2)}) collective-permute-start(bf16[256,128]{1,0:T(8,128)(2,1)S(1)} %get-tuple-element.40), channel_id=1, source_target_pairs={{0,6},{2,4},{4,2},{6,0},{8,14},{10,12},{12,10},{14,8},{1,7},{3,5},... | collective-permute-start | bytes 196616 | tf_op jit(solution)/shard_map/ppermute | solution.py:176
  28.7 1.6 %collective-permute-start.3 = (bf16[256,128]{1,0:T(8,128)(2,1)S(1)}, bf16[256,128]{1,0:T(8,128)(2,1)S(1)}, u32[]{:S(2)}, u32[]{:S(2)}) collective-permute-start(bf16[256,128]{1,0:T(8,128)(2,1)S(1)} %get-tuple-element.41), channel_id=1, source_target_pairs={{0,8},{2,10},{4,12},{6,14},{8,0},{10,2},{12,4},{14,6},{1,9},{3,11}... | collective-permute-start | bytes 196616 | tf_op jit(solution)/shard_map/ppermute | solution.py:176
  30.4 1.5 %collective-permute-start.4 = (bf16[256,128]{1,0:T(8,128)(2,1)S(1)}, bf16[256,128]{1,0:T(8,128)(2,1)S(1)}, u32[]{:S(2)}, u32[]{:S(2)}) collective-permute-start(bf16[256,128]{1,0:T(8,128)(2,1)S(1)} %get-tuple-element.42), channel_id=1, source_target_pairs={{0,10},{2,8},{4,14},{6,12},{8,2},{10,0},{12,6},{14,4},{1,11},{3,9}... | collective-permute-start | bytes 196616 | tf_op jit(solution)/shard_map/ppermute | solution.py:176
  31.9 3.5 %collective-permute-start.5 = (bf16[256,128]{1,0:T(8,128)(2,1)S(1)}, bf16[256,128]{1,0:T(8,128)(2,1)S(1)}, u32[]{:S(2)}, u32[]{:S(2)}) collective-permute-start(bf16[256,128]{1,0:T(8,128)(2,1)S(1)} %get-tuple-element.43), channel_id=1, source_target_pairs={{0,12},{2,14},{4,8},{6,10},{8,4},{10,6},{12,0},{14,2},{1,13},{3,15... | collective-permute-start | bytes 196616 | tf_op jit(solution)/shard_map/ppermute | solution.py:176
  35.4 1.0 %collective-permute-start.6 = (bf16[256,128]{1,0:T(8,128)(2,1)S(1)}, bf16[256,128]{1,0:T(8,128)(2,1)S(1)}, u32[]{:S(2)}, u32[]{:S(2)}) collective-permute-start(bf16[256,128]{1,0:T(8,128)(2,1)S(1)} %get-tuple-element.44), channel_id=1, source_target_pairs={{0,14},{2,12},{4,10},{6,8},{8,6},{10,4},{12,2},{14,0},{1,15},{3,13... | collective-permute-start | bytes 196616 | tf_op jit(solution)/shard_map/ppermute | solution.py:176
  36.9 4.8 %shard_map.71 = (bf16[8,256,256]{2,1,0:T(8,128)(2,1)S(1)}, bf16[8,256,256]{2,1,0:T(8,128)(2,1)S(1)}, bf16[96,512,128]{2,1,0:T(8,128)(2,1)}) custom-call(bf16[256,128]{1,0:T(8,128)(2,1)S(1)} %get-tuple-element.37.refs_0_.after, bf16[128,4096]{1,0:T(8,128)(2,1)S(1)} %copy-done.1, bf16[128,4096]{1,0:T(8,128)(2,1)S(1)} %copy-done.2), custom_call_target="tpu_custom_call" | custom-call | bytes 16777216 | tf_op jit(solution)/shard_map/pallas_call | solution.py:210
  43.0 1.1 %shard_map.74 = (bf16[256,128]{1,0:T(8,128)(2,1)S(1)}, bf16[256,128]{1,0:T(8,128)(2,1)S(1)}, bf16[256,128]{1,0:T(8,128)(2,1)S(1)}, bf16[256,128]{1,0:T(8,128)(2,...) custom-call(s32[1]{0:T(128)} %bitcast.here, ...), custom_call_target="tpu_custom_call" | custom-call | flops 134217728 | bytes 1572864 | tf_op jit(solution)/shard_map/pallas_call | solution.py:232
  44.8 1.7 %collective-permute-start.24 = (bf16[256,128]{1,0:T(8,128)(2,1)S(1)}, bf16[256,128]{1,0:T(8,128)(2,1)S(1)}, u32[]{:S(2)}, u32[]{:S(2)}) collective-permute-start(bf16[256,128]{1,0:T(8,128)(2,1)S(1)} %get-tuple-element.65), channel_id=1, source_target_pairs={{0,4},{2,6},{4,0},{6,2},{8,12},{10,14},{12,8},{14,10},{1,5},{3,7},... | collective-permute-start | bytes 196616 | tf_op jit(solution)/shard_map/ppermute | solution.py:176
  46.5 1.1 %collective-permute-start.25 = (bf16[256,128]{1,0:T(8,128)(2,1)S(1)}, bf16[256,128]{1,0:T(8,128)(2,1)S(1)}, u32[]{:S(2)}, u32[]{:S(2)}) collective-permute-start(bf16[256,128]{1,0:T(8,128)(2,1)S(1)} %get-tuple-element.66), channel_id=1, source_target_pairs={{0,6},{2,4},{4,2},{6,0},{8,14},{10,12},{12,10},{14,8},{1,7},{3,5},... | collective-permute-start | bytes 196616 | tf_op jit(solution)/shard_map/ppermute | solution.py:176
  47.7 1.5 %collective-permute-start.26 = (bf16[256,128]{1,0:T(8,128)(2,1)S(1)}, bf16[256,128]{1,0:T(8,128)(2,1)S(1)}, u32[]{:S(2)}, u32[]{:S(2)}) collective-permute-start(bf16[256,128]{1,0:T(8,128)(2,1)S(1)} %get-tuple-element.67), channel_id=1, source_target_pairs={{0,8},{2,10},{4,12},{6,14},{8,0},{10,2},{12,4},{14,6},{1,9},{3,11}... | collective-permute-start | bytes 196616 | tf_op jit(solution)/shard_map/ppermute | solution.py:176
  49.2 1.5 %collective-permute-start.27 = (bf16[256,128]{1,0:T(8,128)(2,1)S(1)}, bf16[256,128]{1,0:T(8,128)(2,1)S(1)}, u32[]{:S(2)}, u32[]{:S(2)}) collective-permute-start(bf16[256,128]{1,0:T(8,128)(2,1)S(1)} %get-tuple-element.68), channel_id=1, source_target_pairs={{0,10},{2,8},{4,14},{6,12},{8,2},{10,0},{12,6},{14,4},{1,11},{3,9}... | collective-permute-start | bytes 196616 | tf_op jit(solution)/shard_map/ppermute | solution.py:176
  50.7 1.1 %shard_map.72 = (bf16[256,128]{1,0:T(8,128)(2,1)S(1)}, bf16[256,128]{1,0:T(8,128)(2,1)S(1)}, bf16[256,128]{1,0:T(8,128)(2,1)S(1)}, bf16[256,128]{1,0:T(8,128)(2,...) custom-call(s32[1]{0:T(128)} %bitcast.here, ...), custom_call_target="tpu_custom_call" | custom-call | flops 134217728 | bytes 1572864 | tf_op jit(solution)/shard_map/pallas_call | solution.py:232
  51.8 3.5 %collective-permute-start.28 = (bf16[256,128]{1,0:T(8,128)(2,1)S(1)}, bf16[256,128]{1,0:T(8,128)(2,1)S(1)}, u32[]{:S(2)}, u32[]{:S(2)}) collective-permute-start(bf16[256,128]{1,0:T(8,128)(2,1)S(1)} %get-tuple-element.69), channel_id=1, source_target_pairs={{0,12},{2,14},{4,8},{6,10},{8,4},{10,6},{12,0},{14,2},{1,13},{3,15... | collective-permute-start | bytes 196616 | tf_op jit(solution)/shard_map/ppermute | solution.py:176
  55.3 1.2 %collective-permute-start.29 = (bf16[256,128]{1,0:T(8,128)(2,1)S(1)}, bf16[256,128]{1,0:T(8,128)(2,1)S(1)}, u32[]{:S(2)}, u32[]{:S(2)}) collective-permute-start(bf16[256,128]{1,0:T(8,128)(2,1)S(1)} %get-tuple-element.70), channel_id=1, source_target_pairs={{0,14},{2,12},{4,10},{6,8},{8,6},{10,4},{12,2},{14,0},{1,15},{3,13... | collective-permute-start | bytes 196616 | tf_op jit(solution)/shard_map/ppermute | solution.py:176
  57.1 1.7 %collective-permute-done.27.refs_13_ = bf16[256,128]{1,0:T(8,128)(2,1)S(1)} collective-permute-done((bf16[256,128]{1,0:T(8,128)(2,1)S(1)}, bf16[256,128]{1,0:T(8,128)(2,1)S(1)}, u32[]{:S(2)}, u32[]{:S(2)}) %collective-permute-start.27) | collective-permute-done | bytes 65568 | tf_op jit(solution)/shard_map/ppermute | solution.py:176
  58.9 1.1 %collective-permute-start.17 = (bf16[256,128]{1,0:T(8,128)(2,1)S(1)}, bf16[256,128]{1,0:T(8,128)(2,1)S(1)}, u32[]{:S(2)}, u32[]{:S(2)}) collective-permute-start(bf16[256,128]{1,0:T(8,128)(2,1)S(1)} %get-tuple-element.57), channel_id=1, source_target_pairs={{0,6},{2,4},{4,2},{6,0},{8,14},{10,12},{12,10},{14,8},{1,7},{3,5},... | collective-permute-start | bytes 196616 | tf_op jit(solution)/shard_map/ppermute | solution.py:176
  60.0 2.9 %collective-permute-start.18 = (bf16[256,128]{1,0:T(8,128)(2,1)S(1)}, bf16[256,128]{1,0:T(8,128)(2,1)S(1)}, u32[]{:S(2)}, u32[]{:S(2)}) collective-permute-start(bf16[256,128]{1,0:T(8,128)(2,1)S(1)} %get-tuple-element.58), channel_id=1, source_target_pairs={{0,8},{2,10},{4,12},{6,14},{8,0},{10,2},{12,4},{14,6},{1,9},{3,11}... | collective-permute-start | bytes 196616 | tf_op jit(solution)/shard_map/ppermute | solution.py:176
  62.9 2.8 %collective-permute-start.19 = (bf16[256,128]{1,0:T(8,128)(2,1)S(1)}, bf16[256,128]{1,0:T(8,128)(2,1)S(1)}, u32[]{:S(2)}, u32[]{:S(2)}) collective-permute-start(bf16[256,128]{1,0:T(8,128)(2,1)S(1)} %get-tuple-element.59), channel_id=1, source_target_pairs={{0,10},{2,8},{4,14},{6,12},{8,2},{10,0},{12,6},{14,4},{1,11},{3,9}... | collective-permute-start | bytes 196616 | tf_op jit(solution)/shard_map/ppermute | solution.py:176
  66.5 3.0 %collective-permute-start.21 = (bf16[256,128]{1,0:T(8,128)(2,1)S(1)}, bf16[256,128]{1,0:T(8,128)(2,1)S(1)}, u32[]{:S(2)}, u32[]{:S(2)}) collective-permute-start(bf16[256,128]{1,0:T(8,128)(2,1)S(1)} %get-tuple-element.61), channel_id=1, source_target_pairs={{0,14},{2,12},{4,10},{6,8},{8,6},{10,4},{12,2},{14,0},{1,15},{3,13... | collective-permute-start | bytes 196616 | tf_op jit(solution)/shard_map/ppermute | solution.py:176
  69.5 2.1 %shard_map.70 = bf16[128,4096]{1,0:T(8,128)(2,1)} custom-call(s32[1]{0:T(128)} %bitcast.here, s32[8,1]{1,0:T(8,128)S(1)} %copy.9.lengths, f32[128,128]{1,0:T(8,128)S(1)} %shard_map.69.mine, f32[128,128]{1,0:T(8,128)S(1)} %collective-permute-done.7.other, bf16[256,128]{1,0:T(8,128)(2,1)S(1)} %get-tuple-element.45.refs_0_, ...), custom_call_target="tpu_custom_call" | custom-call | flops 134217728 | bytes 1572864 | tf_op jit(solution)/shard_map/pallas_call | solution.py:248
  71.6 1.0 %collective-permute-done.19.refs_5_ = bf16[256,128]{1,0:T(8,128)(2,1)S(1)} collective-permute-done((bf16[256,128]{1,0:T(8,128)(2,1)S(1)}, bf16[256,128]{1,0:T(8,128)(2,1)S(1)}, u32[]{:S(2)}, u32[]{:S(2)}) %collective-permute-start.19) | collective-permute-done | bytes 65568 | tf_op jit(solution)/shard_map/ppermute | solution.py:176
  73.6 2.6 %shard_map.75 = bf16[96,512,128]{2,1,0:T(8,128)(2,1)} custom-call(s32[8,1]{1,0:T(8,128)S(1)} %copy.8.ids, s32[1]{0:T(128)} %bitcast.here, s32[8,1]{1,0:T(8,128)S(1)} %copy.9.lengths, bf16[256,128]{1,0:T(8,128)(2,1)S(1)} %get-tuple-element.54.refs_0_, bf16[256,128]{1,0:T(8,128)(2,1)S(1)} %collective-permute-done.15.refs_1_, ...), custom_call_target="tpu_custom_call", output_to_operand_aliasing={{}: (19, {})} | custom-call | bytes 2097152 | tf_op jit(solution)/shard_map/pallas_call | solution.py:257
  (46 shorter events, 6.4 us)
Async XLA Ops:
  0.6 42.3 %copy-start.3 = (s32[8,1]{0,1:T(1,128)S(1)}, s32[8,1]{0,1:T(1,128)}, u32[]{:S(2)}) copy-start(s32[8,1]{0,1:T(1,128)} %param.9) | copy-start | bytes 100
  6.0 31.0 %copy-start.2 = (bf16[128,4096]{1,0:T(8,128)(2,1)S(1)}, bf16[128,4096]{1,0:T(8,128)(2,1)}, u32[]{:S(2)}) copy-start(bf16[128,4096]{1,0:T(8,128)(2,1)} %y.1) | copy-start | bytes 3145732
  8.9 11.7 %collective-permute-start.10 = (bf16[256,128]{1,0:T(8,128)(2,1)S(1)}, bf16[256,128]{1,0:T(8,128)(2,1)S(1)}, u32[]{:S(2)}, u32[]{:S(2)}) collective-permute-start(bf16[256,128]{1,0:T(8,128)(2,1)S(1)} %get-tuple-element.48), channel_id=1, source_target_pairs={{0,6},{2,4},{4,2},{6,0},{8,14},{10,12},{12,10},{14,8},{1,7},{3,5},... | collective-permute-start | bytes 196616 | tf_op jit(solution)/shard_map/ppermute | solution.py:176
  12.9 8.2 %collective-permute-start.11 = (bf16[256,128]{1,0:T(8,128)(2,1)S(1)}, bf16[256,128]{1,0:T(8,128)(2,1)S(1)}, u32[]{:S(2)}, u32[]{:S(2)}) collective-permute-start(bf16[256,128]{1,0:T(8,128)(2,1)S(1)} %get-tuple-element.49), channel_id=1, source_target_pairs={{0,8},{2,10},{4,12},{6,14},{8,0},{10,2},{12,4},{14,6},{1,9},{3,11}... | collective-permute-start | bytes 196616 | tf_op jit(solution)/shard_map/ppermute | solution.py:176
  15.5 8.9 %collective-permute-start.12 = (bf16[256,128]{1,0:T(8,128)(2,1)S(1)}, bf16[256,128]{1,0:T(8,128)(2,1)S(1)}, u32[]{:S(2)}, u32[]{:S(2)}) collective-permute-start(bf16[256,128]{1,0:T(8,128)(2,1)S(1)} %get-tuple-element.50), channel_id=1, source_target_pairs={{0,10},{2,8},{4,14},{6,12},{8,2},{10,0},{12,6},{14,4},{1,11},{3,9}... | collective-permute-start | bytes 196616 | tf_op jit(solution)/shard_map/ppermute | solution.py:176
  15.8 9.6 %collective-permute-start.13 = (bf16[256,128]{1,0:T(8,128)(2,1)S(1)}, bf16[256,128]{1,0:T(8,128)(2,1)S(1)}, u32[]{:S(2)}, u32[]{:S(2)}) collective-permute-start(bf16[256,128]{1,0:T(8,128)(2,1)S(1)} %get-tuple-element.51), channel_id=1, source_target_pairs={{0,12},{2,14},{4,8},{6,10},{8,4},{10,6},{12,0},{14,2},{1,13},{3,15... | collective-permute-start | bytes 196616 | tf_op jit(solution)/shard_map/ppermute | solution.py:176
  18.3 8.3 %collective-permute-start.14 = (bf16[256,128]{1,0:T(8,128)(2,1)S(1)}, bf16[256,128]{1,0:T(8,128)(2,1)S(1)}, u32[]{:S(2)}, u32[]{:S(2)}) collective-permute-start(bf16[256,128]{1,0:T(8,128)(2,1)S(1)} %get-tuple-element.52), channel_id=1, source_target_pairs={{0,14},{2,12},{4,10},{6,8},{8,6},{10,4},{12,2},{14,0},{1,15},{3,13... | collective-permute-start | bytes 196616 | tf_op jit(solution)/shard_map/ppermute | solution.py:176
  20.6 8.2 %collective-permute-start.8 = (bf16[256,128]{1,0:T(8,128)(2,1)S(1)}, bf16[256,128]{1,0:T(8,128)(2,1)S(1)}, u32[]{:S(2)}, u32[]{:S(2)}) collective-permute-start(bf16[256,128]{1,0:T(8,128)(2,1)S(1)} %get-tuple-element.46), channel_id=1, source_target_pairs={{0,2},{2,0},{4,6},{6,4},{8,10},{10,8},{12,14},{14,12},{1,3},{3,1},... | collective-permute-start | bytes 196616 | tf_op jit(solution)/shard_map/ppermute | solution.py:176
  21.1 9.3 %collective-permute-start.9 = (bf16[256,128]{1,0:T(8,128)(2,1)S(1)}, bf16[256,128]{1,0:T(8,128)(2,1)S(1)}, u32[]{:S(2)}, u32[]{:S(2)}) collective-permute-start(bf16[256,128]{1,0:T(8,128)(2,1)S(1)} %get-tuple-element.47), channel_id=1, source_target_pairs={{0,4},{2,6},{4,0},{6,2},{8,12},{10,14},{12,8},{14,10},{1,5},{3,7},... | collective-permute-start | bytes 196616 | tf_op jit(solution)/shard_map/ppermute | solution.py:176
  24.4 7.5 %collective-permute-start = (bf16[256,128]{1,0:T(8,128)(2,1)S(1)}, bf16[256,128]{1,0:T(8,128)(2,1)S(1)}, u32[]{:S(2)}, u32[]{:S(2)}) collective-permute-start(bf16[256,128]{1,0:T(8,128)(2,1)S(1)} %get-tuple-element.38), channel_id=1, source_target_pairs={{0,2},{2,0},{4,6},{6,4},{8,10},{10,8},{12,14},{14,12},{1,3},{3,1},... | collective-permute-start | bytes 196616 | tf_op jit(solution)/shard_map/ppermute | solution.py:176
  25.4 10.0 %collective-permute-start.1 = (bf16[256,128]{1,0:T(8,128)(2,1)S(1)}, bf16[256,128]{1,0:T(8,128)(2,1)S(1)}, u32[]{:S(2)}, u32[]{:S(2)}) collective-permute-start(bf16[256,128]{1,0:T(8,128)(2,1)S(1)} %get-tuple-element.39), channel_id=1, source_target_pairs={{0,4},{2,6},{4,0},{6,2},{8,12},{10,14},{12,8},{14,10},{1,5},{3,7},... | collective-permute-start | bytes 196616 | tf_op jit(solution)/shard_map/ppermute | solution.py:176
  26.6 10.3 %collective-permute-start.2 = (bf16[256,128]{1,0:T(8,128)(2,1)S(1)}, bf16[256,128]{1,0:T(8,128)(2,1)S(1)}, u32[]{:S(2)}, u32[]{:S(2)}) collective-permute-start(bf16[256,128]{1,0:T(8,128)(2,1)S(1)} %get-tuple-element.40), channel_id=1, source_target_pairs={{0,6},{2,4},{4,2},{6,0},{8,14},{10,12},{12,10},{14,8},{1,7},{3,5},... | collective-permute-start | bytes 196616 | tf_op jit(solution)/shard_map/ppermute | solution.py:176
  28.7 13.0 %collective-permute-start.3 = (bf16[256,128]{1,0:T(8,128)(2,1)S(1)}, bf16[256,128]{1,0:T(8,128)(2,1)S(1)}, u32[]{:S(2)}, u32[]{:S(2)}) collective-permute-start(bf16[256,128]{1,0:T(8,128)(2,1)S(1)} %get-tuple-element.41), channel_id=1, source_target_pairs={{0,8},{2,10},{4,12},{6,14},{8,0},{10,2},{12,4},{14,6},{1,9},{3,11}... | collective-permute-start | bytes 196616 | tf_op jit(solution)/shard_map/ppermute | solution.py:176
  30.4 11.4 %collective-permute-start.4 = (bf16[256,128]{1,0:T(8,128)(2,1)S(1)}, bf16[256,128]{1,0:T(8,128)(2,1)S(1)}, u32[]{:S(2)}, u32[]{:S(2)}) collective-permute-start(bf16[256,128]{1,0:T(8,128)(2,1)S(1)} %get-tuple-element.42), channel_id=1, source_target_pairs={{0,10},{2,8},{4,14},{6,12},{8,2},{10,0},{12,6},{14,4},{1,11},{3,9}... | collective-permute-start | bytes 196616 | tf_op jit(solution)/shard_map/ppermute | solution.py:176
  31.9 9.9 %collective-permute-start.5 = (bf16[256,128]{1,0:T(8,128)(2,1)S(1)}, bf16[256,128]{1,0:T(8,128)(2,1)S(1)}, u32[]{:S(2)}, u32[]{:S(2)}) collective-permute-start(bf16[256,128]{1,0:T(8,128)(2,1)S(1)} %get-tuple-element.43), channel_id=1, source_target_pairs={{0,12},{2,14},{4,8},{6,10},{8,4},{10,6},{12,0},{14,2},{1,13},{3,15... | collective-permute-start | bytes 196616 | tf_op jit(solution)/shard_map/ppermute | solution.py:176
  35.4 7.1 %collective-permute-start.6 = (bf16[256,128]{1,0:T(8,128)(2,1)S(1)}, bf16[256,128]{1,0:T(8,128)(2,1)S(1)}, u32[]{:S(2)}, u32[]{:S(2)}) collective-permute-start(bf16[256,128]{1,0:T(8,128)(2,1)S(1)} %get-tuple-element.44), channel_id=1, source_target_pairs={{0,14},{2,12},{4,10},{6,8},{8,6},{10,4},{12,2},{14,0},{1,15},{3,13... | collective-permute-start | bytes 196616 | tf_op jit(solution)/shard_map/ppermute | solution.py:176
  36.8 6.2 %collective-permute-start.22 = (f32[128,128]{1,0:T(8,128)S(1)}, f32[128,128]{1,0:T(8,128)S(1)}, u32[]{:S(2)}, u32[]{:S(2)}) collective-permute-start(f32[128,128]{1,0:T(8,128)S(1)} %shard_map.73.mine), channel_id=1, source_target_pairs={{0,1},{1,0},{2,3},{3,2},{4,5},{5,4},{6,7},{7,6},{8,9},{9,8},{10,11... | collective-permute-start | bytes 196616 | tf_op jit(solution)/shard_map/ppermute | solution.py:182
  42.9 6.3 %collective-permute-start.7 = (f32[128,128]{1,0:T(8,128)S(1)}, f32[128,128]{1,0:T(8,128)S(1)}, u32[]{:S(2)}, u32[]{:S(2)}) collective-permute-start(f32[128,128]{1,0:T(8,128)S(1)} %shard_map.69.mine), channel_id=1, source_target_pairs={{0,1},{1,0},{2,3},{3,2},{4,5},{5,4},{6,7},{7,6},{8,9},{9,8},{10,11... | collective-permute-start | bytes 196616 | tf_op jit(solution)/shard_map/ppermute | solution.py:182
  44.1 7.6 %collective-permute-start.23 = (bf16[256,128]{1,0:T(8,128)(2,1)S(1)}, bf16[256,128]{1,0:T(8,128)(2,1)S(1)}, u32[]{:S(2)}, u32[]{:S(2)}) collective-permute-start(bf16[256,128]{1,0:T(8,128)(2,1)S(1)} %get-tuple-element.64), channel_id=1, source_target_pairs={{0,2},{2,0},{4,6},{6,4},{8,10},{10,8},{12,14},{14,12},{1,3},{3,1},... | collective-permute-start | bytes 196616 | tf_op jit(solution)/shard_map/ppermute | solution.py:176
  44.8 10.5 %collective-permute-start.24 = (bf16[256,128]{1,0:T(8,128)(2,1)S(1)}, bf16[256,128]{1,0:T(8,128)(2,1)S(1)}, u32[]{:S(2)}, u32[]{:S(2)}) collective-permute-start(bf16[256,128]{1,0:T(8,128)(2,1)S(1)} %get-tuple-element.65), channel_id=1, source_target_pairs={{0,4},{2,6},{4,0},{6,2},{8,12},{10,14},{12,8},{14,10},{1,5},{3,7},... | collective-permute-start | bytes 196616 | tf_op jit(solution)/shard_map/ppermute | solution.py:176
  46.5 10.0 %collective-permute-start.25 = (bf16[256,128]{1,0:T(8,128)(2,1)S(1)}, bf16[256,128]{1,0:T(8,128)(2,1)S(1)}, u32[]{:S(2)}, u32[]{:S(2)}) collective-permute-start(bf16[256,128]{1,0:T(8,128)(2,1)S(1)} %get-tuple-element.66), channel_id=1, source_target_pairs={{0,6},{2,4},{4,2},{6,0},{8,14},{10,12},{12,10},{14,8},{1,7},{3,5},... | collective-permute-start | bytes 196616 | tf_op jit(solution)/shard_map/ppermute | solution.py:176
  47.7 9.4 %collective-permute-start.26 = (bf16[256,128]{1,0:T(8,128)(2,1)S(1)}, bf16[256,128]{1,0:T(8,128)(2,1)S(1)}, u32[]{:S(2)}, u32[]{:S(2)}) collective-permute-start(bf16[256,128]{1,0:T(8,128)(2,1)S(1)} %get-tuple-element.67), channel_id=1, source_target_pairs={{0,8},{2,10},{4,12},{6,14},{8,0},{10,2},{12,4},{14,6},{1,9},{3,11}... | collective-permute-start | bytes 196616 | tf_op jit(solution)/shard_map/ppermute | solution.py:176
  49.2 9.7 %collective-permute-start.27 = (bf16[256,128]{1,0:T(8,128)(2,1)S(1)}, bf16[256,128]{1,0:T(8,128)(2,1)S(1)}, u32[]{:S(2)}, u32[]{:S(2)}) collective-permute-start(bf16[256,128]{1,0:T(8,128)(2,1)S(1)} %get-tuple-element.68), channel_id=1, source_target_pairs={{0,10},{2,8},{4,14},{6,12},{8,2},{10,0},{12,6},{14,4},{1,11},{3,9}... | collective-permute-start | bytes 196616 | tf_op jit(solution)/shard_map/ppermute | solution.py:176
  51.8 8.2 %collective-permute-start.28 = (bf16[256,128]{1,0:T(8,128)(2,1)S(1)}, bf16[256,128]{1,0:T(8,128)(2,1)S(1)}, u32[]{:S(2)}, u32[]{:S(2)}) collective-permute-start(bf16[256,128]{1,0:T(8,128)(2,1)S(1)} %get-tuple-element.69), channel_id=1, source_target_pairs={{0,12},{2,14},{4,8},{6,10},{8,4},{10,6},{12,0},{14,2},{1,13},{3,15... | collective-permute-start | bytes 196616 | tf_op jit(solution)/shard_map/ppermute | solution.py:176
  55.3 7.6 %collective-permute-start.29 = (bf16[256,128]{1,0:T(8,128)(2,1)S(1)}, bf16[256,128]{1,0:T(8,128)(2,1)S(1)}, u32[]{:S(2)}, u32[]{:S(2)}) collective-permute-start(bf16[256,128]{1,0:T(8,128)(2,1)S(1)} %get-tuple-element.70), channel_id=1, source_target_pairs={{0,14},{2,12},{4,10},{6,8},{8,6},{10,4},{12,2},{14,0},{1,15},{3,13... | collective-permute-start | bytes 196616 | tf_op jit(solution)/shard_map/ppermute | solution.py:176
  56.5 9.2 %collective-permute-start.15 = (bf16[256,128]{1,0:T(8,128)(2,1)S(1)}, bf16[256,128]{1,0:T(8,128)(2,1)S(1)}, u32[]{:S(2)}, u32[]{:S(2)}) collective-permute-start(bf16[256,128]{1,0:T(8,128)(2,1)S(1)} %get-tuple-element.55), channel_id=1, source_target_pairs={{0,2},{2,0},{4,6},{6,4},{8,10},{10,8},{12,14},{14,12},{1,3},{3,1},... | collective-permute-start | bytes 196616 | tf_op jit(solution)/shard_map/ppermute | solution.py:176
  57.1 9.4 %collective-permute-start.16 = (bf16[256,128]{1,0:T(8,128)(2,1)S(1)}, bf16[256,128]{1,0:T(8,128)(2,1)S(1)}, u32[]{:S(2)}, u32[]{:S(2)}) collective-permute-start(bf16[256,128]{1,0:T(8,128)(2,1)S(1)} %get-tuple-element.56), channel_id=1, source_target_pairs={{0,4},{2,6},{4,0},{6,2},{8,12},{10,14},{12,8},{14,10},{1,5},{3,7},... | collective-permute-start | bytes 196616 | tf_op jit(solution)/shard_map/ppermute | solution.py:176
  58.9 12.7 %collective-permute-start.17 = (bf16[256,128]{1,0:T(8,128)(2,1)S(1)}, bf16[256,128]{1,0:T(8,128)(2,1)S(1)}, u32[]{:S(2)}, u32[]{:S(2)}) collective-permute-start(bf16[256,128]{1,0:T(8,128)(2,1)S(1)} %get-tuple-element.57), channel_id=1, source_target_pairs={{0,6},{2,4},{4,2},{6,0},{8,14},{10,12},{12,10},{14,8},{1,7},{3,5},... | collective-permute-start | bytes 196616 | tf_op jit(solution)/shard_map/ppermute | solution.py:176
  60.0 11.6 %collective-permute-start.18 = (bf16[256,128]{1,0:T(8,128)(2,1)S(1)}, bf16[256,128]{1,0:T(8,128)(2,1)S(1)}, u32[]{:S(2)}, u32[]{:S(2)}) collective-permute-start(bf16[256,128]{1,0:T(8,128)(2,1)S(1)} %get-tuple-element.58), channel_id=1, source_target_pairs={{0,8},{2,10},{4,12},{6,14},{8,0},{10,2},{12,4},{14,6},{1,9},{3,11}... | collective-permute-start | bytes 196616 | tf_op jit(solution)/shard_map/ppermute | solution.py:176
  62.9 9.7 %collective-permute-start.19 = (bf16[256,128]{1,0:T(8,128)(2,1)S(1)}, bf16[256,128]{1,0:T(8,128)(2,1)S(1)}, u32[]{:S(2)}, u32[]{:S(2)}) collective-permute-start(bf16[256,128]{1,0:T(8,128)(2,1)S(1)} %get-tuple-element.59), channel_id=1, source_target_pairs={{0,10},{2,8},{4,14},{6,12},{8,2},{10,0},{12,6},{14,4},{1,11},{3,9}... | collective-permute-start | bytes 196616 | tf_op jit(solution)/shard_map/ppermute | solution.py:176
  65.7 6.9 %collective-permute-start.20 = (bf16[256,128]{1,0:T(8,128)(2,1)S(1)}, bf16[256,128]{1,0:T(8,128)(2,1)S(1)}, u32[]{:S(2)}, u32[]{:S(2)}) collective-permute-start(bf16[256,128]{1,0:T(8,128)(2,1)S(1)} %get-tuple-element.60), channel_id=1, source_target_pairs={{0,12},{2,14},{4,8},{6,10},{8,4},{10,6},{12,0},{14,2},{1,13},{3,15... | collective-permute-start | bytes 196616 | tf_op jit(solution)/shard_map/ppermute | solution.py:176
  66.5 7.1 %collective-permute-start.21 = (bf16[256,128]{1,0:T(8,128)(2,1)S(1)}, bf16[256,128]{1,0:T(8,128)(2,1)S(1)}, u32[]{:S(2)}, u32[]{:S(2)}) collective-permute-start(bf16[256,128]{1,0:T(8,128)(2,1)S(1)} %get-tuple-element.61), channel_id=1, source_target_pairs={{0,14},{2,12},{4,10},{6,8},{8,6},{10,4},{12,2},{14,0},{1,15},{3,13... | collective-permute-start | bytes 196616 | tf_op jit(solution)/shard_map/ppermute | solution.py:176
  (2 other events, 35.0 us)

commit v2 on v1

v2 whole, which is shorter than its diff:
```python
import functools

import jax
import jax.numpy as jnp
from jax import lax
from jax.experimental import pallas as pl
from jax.experimental.pallas import tpu as pltpu
from jax.sharding import PartitionSpec as P

adapter_alpha = 128.0

in_vmem = pl.BlockSpec(memory_space=pltpu.VMEM)
in_smem = pl.BlockSpec(memory_space=pltpu.SMEM)
in_hbm = pl.BlockSpec(memory_space=pltpu.HBM)


def low_lanes(rows, width):
    return lax.broadcasted_iota(jnp.int32, (rows, width), 1) < width // 2


def swap_halves(value):
    return pltpu.roll(value, value.shape[-1] // 2, 1)


def call(kernel, out_shape, in_specs, out_specs, scratch=(), flops=0, moved=0, aliases=None, vmem=40):
    return pl.pallas_call(
        kernel,
        out_shape=out_shape,
        in_specs=in_specs,
        out_specs=out_specs,
        scratch_shapes=list(scratch),
        input_output_aliases=aliases or {},
        compiler_params=pltpu.CompilerParams(vmem_limit_bytes=vmem * 1024 * 1024),
        cost_estimate=pl.CostEstimate(flops=flops, bytes_accessed=moved, transcendentals=0),
    )


def pack_kernel(ids, table, up, down, held, sems):
    owners, rows, width = held.shape
    half = rows // 2
    copies = []
    for k in range(owners):
        copies.append(pltpu.make_async_copy(table.at[ids[k]], held.at[k], sems.at[k]))
        copies[-1].start()
    low = low_lanes(half, width)
    for k in range(owners):
        copies[k].wait()
        first = held[k, :half].astype(jnp.float32)
        second = held[k, half:].astype(jnp.float32)
        up[k] = jnp.where(low, swap_halves(first), second).astype(jnp.bfloat16)
        down[k] = jnp.where(low, first, swap_halves(second)).astype(jnp.bfloat16)


def prep_kernel(half, after, x, y, x_turned, y_turned, blank, zeros, sem):
    zeros[...] = jnp.zeros_like(zeros)
    step = zeros.shape[0]
    copies = [
        pltpu.make_async_copy(zeros, blank.at[pl.ds(s, step)], sem.at[s // step])
        for s in range(0, blank.shape[0], step)
    ]
    for copy in copies:
        copy.start()
    owners = x.shape[1] // (2 * half)
    tokens = x.shape[0]

    @pl.loop(0, owners)
    def _(owner):
        for part in range(2):
            columns = pl.ds(pl.multiple_of(owner * 2 * half + part * half, half), half)
            lanes = pl.ds(part * tokens, tokens)
            x_turned[owner, :, lanes] = x[:, columns].T
            y_turned[owner, :, lanes] = y[:, columns].T

    for copy in copies:
        copy.wait()


def rank_kernel(tokens, packed, out):
    owners, half, width = packed.shape
    first = jnp.zeros((tokens.shape[0], width), jnp.float32)
    second = jnp.zeros((tokens.shape[0], width), jnp.float32)
    for k in range(owners):
        start = k * 2 * half
        lo = tokens[:, start : start + half]
        hi = tokens[:, start + half : start + 2 * half]
        first += jnp.dot(lo, packed[k], preferred_element_type=jnp.float32)
        second += jnp.dot(hi, packed[k], preferred_element_type=jnp.float32)
    out[...] = jnp.where(low_lanes(*out.shape), first, second)


def rounded_twice(mine, other, length, scale):
    total = mine[...] + other[...]
    total = scale * (total + swap_halves(total))
    rows, width = total.shape
    live = lax.broadcasted_iota(jnp.int32, (rows, width), 0) < length
    total = jnp.where(live, total, 0.0)
    low = low_lanes(rows, width)
    top = jnp.where(low, total, 0.0).astype(jnp.bfloat16)
    bottom = jnp.where(low, 0.0, total).astype(jnp.bfloat16)
    return jnp.concatenate([top, bottom], axis=0)


def piece_kernel(scale, out_scale, here, lengths, mine, other, turned, out):
    pair = rounded_twice(mine, other, lengths[here[0]], scale)
    for k in range(out.shape[0]):
        piece = jnp.dot(turned[k], pair, preferred_element_type=jnp.float32)
        out[k] = (out_scale * piece).astype(jnp.bfloat16)


def input_kernel(scale, here, lengths, mine, other, packed, out):
    pair = rounded_twice(mine, other, lengths[here[0]], scale)
    rows = out.shape[0]
    owners, half, _ = packed.shape
    for k in range(owners):
        both = lax.dot_general(
            pair, packed[k], (((1,), (1,)), ((), ())), preferred_element_type=jnp.float32
        ).astype(jnp.bfloat16)
        start = k * 2 * half
        out[:, start : start + half] = both[:rows]
        out[:, start + half : start + 2 * half] = both[rows:]


def merge_kernel(ids, lengths, down, up, blank, out, total, held, sems):
    owners, half, width = down.shape
    low = low_lanes(half, width)
    copies, firsts = [], []
    for k in range(owners):
        adapter = ids[k]
        copies.append(pltpu.make_async_copy(held.at[k], out.at[adapter], sems.at[k]))
        same = [ids[other] == adapter for other in range(owners)]
        earlier = functools.reduce(jnp.logical_or, same[:k], jnp.bool_(False))
        firsts.append(jnp.logical_not(earlier))

        @pl.when(firsts[k])
        def _():
            total[0] = down[k].astype(jnp.float32)
            total[1] = up[k].astype(jnp.float32)
            count = lengths[k]
            for other in range(k + 1, owners):
                count += jnp.where(same[other], lengths[other], 0)

                @pl.when(same[other])
                def _():
                    total[0] += down[other].astype(jnp.float32)
                    total[1] += up[other].astype(jnp.float32)

            denom = jnp.maximum(count.astype(jnp.float32), 1.0)
            part = 1.0 / jnp.full((1, width), denom)
            g_down = total[0] * part
            g_up = total[1] * part
            held[k, :half] = jnp.where(low, g_down, swap_halves(g_up)).astype(jnp.bfloat16)
            held[k, half:] = jnp.where(low, swap_halves(g_down), g_up).astype(jnp.bfloat16)
            copies[k].start()

    for k in range(owners):
        pl.when(firsts[k])(copies[k].wait)


def exchange(pieces):
    return lax.all_to_all(pieces, "dp", split_axis=0, concat_axis=0, tiled=True)


def across_cores(value):
    cores = lax.axis_size("tensor")
    return lax.ppermute(value, "tensor", [(i, i ^ 1) for i in range(cores)])


def with_kernels(activations, cotangent, adapter_weight_pair, adapter_of_block, block_live_length):
    owners = lax.axis_size("dp")
    here = lax.axis_index("dp").astype(jnp.int32).reshape(1)
    ids, lengths = adapter_of_block[:, 0], block_live_length[:, 0]
    count, _, rows, width = adapter_weight_pair.shape
    table = adapter_weight_pair.reshape(count, rows, width)
    tokens, features = activations.shape
    half = rows // 2
    scale = adapter_alpha / (width // 2)
    bf16, f32 = jnp.bfloat16, jnp.float32
    packed_shape = jax.ShapeDtypeStruct((owners, half, width), bf16)
    packed_bytes = owners * half * width * 2

    up_sent, down_sent = call(
        pack_kernel,
        [packed_shape] * 2,
        [in_smem, in_hbm],
        [in_vmem] * 2,
        [pltpu.VMEM((owners, rows, width), bf16), pltpu.SemaphoreType.DMA((owners,))],
        moved=4 * packed_bytes,
        vmem=60,
    )(ids, table)
    up = exchange(up_sent)
    down = exchange(down_sent)

    step = 8
    turned_shape = jax.ShapeDtypeStruct((owners, half, 2 * tokens), bf16)
    x_turned, y_turned, blank = call(
        functools.partial(prep_kernel, half),
        [turned_shape, turned_shape, jax.ShapeDtypeStruct(table.shape, bf16)],
        [in_hbm, in_vmem, in_vmem],
        [in_vmem, in_vmem, in_hbm],
        [pltpu.VMEM((step, rows, width), bf16), pltpu.SemaphoreType.DMA((count // step,))],
        moved=8 * tokens * features + 2 * count * rows * width,
        vmem=60,
    )(up_sent, activations, cotangent)

    partial_shape = jax.ShapeDtypeStruct((tokens, width), f32)

    def rank_product(values, packed):
        return call(
            rank_kernel,
            partial_shape,
            [in_vmem, in_vmem],
            in_vmem,
            flops=2 * tokens * features * width,
            moved=2 * tokens * features + packed_bytes,
        )(values, packed)

    def pieces(mine, other, turned, in_scale, out_scale):
        return call(
            functools.partial(piece_kernel, in_scale, out_scale),
            packed_shape,
            [in_smem, in_smem, in_vmem, in_vmem, in_vmem],
            in_vmem,
            flops=2 * tokens * features * width,
            moved=2 * tokens * features + packed_bytes,
        )(here, lengths, mine, other, turned)

    dhidden = rank_product(cotangent, up)
    dhidden_other = across_cores(dhidden)
    d_down = exchange(pieces(dhidden, dhidden_other, x_turned, scale, 1.0))
    hidden = rank_product(activations, down)
    hidden_other = across_cores(hidden)
    d_up = exchange(pieces(hidden, hidden_other, y_turned, 1.0, scale))

    grad_input = call(
        functools.partial(input_kernel, scale),
        jax.ShapeDtypeStruct((tokens, features), bf16),
        [in_smem, in_smem, in_vmem, in_vmem, in_vmem],
        in_vmem,
        flops=2 * tokens * features * width,
        moved=2 * tokens * features + packed_bytes,
    )(here, lengths, dhidden, dhidden_other, down)

    gradient = call(
        merge_kernel,
        jax.ShapeDtypeStruct(table.shape, bf16),
        [in_smem, in_smem, in_vmem, in_vmem, in_hbm],
        in_hbm,
        [
            pltpu.VMEM((2, half, width), f32),
            pltpu.VMEM((owners, rows, width), bf16),
            pltpu.SemaphoreType.DMA((owners,)),
        ],
        moved=4 * packed_bytes,
        aliases={4: 0},
    )(ids, lengths, d_down, d_up, blank)
    return grad_input, gradient[:, None]


def without_kernels(activations, cotangent, adapter_weight_pair, adapter_of_block, block_live_length):
    owners = lax.axis_size("dp")
    here = lax.axis_index("dp")
    count, _, rows, width = adapter_weight_pair.shape
    rank = width // 2
    scale = adapter_alpha / rank
    adapters = adapter_of_block[:, 0]
    lengths = block_live_length[:, 0]
    keep = (jnp.arange(activations.shape[0], dtype=jnp.int32) < lengths[here])[:, None]
    inputs = jnp.where(keep, activations, jnp.zeros_like(activations))
    grads_out = jnp.where(keep, cotangent, jnp.zeros_like(cotangent))
    fetched = lax.all_to_all(
        adapter_weight_pair[:, 0][adapters], "dp", split_axis=0, concat_axis=0, tiled=True
    )
    pair = fetched.reshape(-1, width)
    down, upward = pair[:, :rank], pair[:, rank:]
    f32 = jnp.float32
    hidden_part = jnp.dot(inputs, down, preferred_element_type=f32)
    dhidden_part = scale * jnp.dot(grads_out, upward, preferred_element_type=f32)
    hidden, dhidden = lax.psum((hidden_part, dhidden_part), "tensor")
    hidden16, dhidden16 = hidden.astype(jnp.bfloat16), dhidden.astype(jnp.bfloat16)
    d_down = jnp.dot(inputs.T, dhidden16, preferred_element_type=f32)
    d_up = scale * jnp.dot(grads_out.T, hidden16, preferred_element_type=f32)
    sent = jnp.concatenate([d_down, d_up], axis=1).astype(jnp.bfloat16).reshape(owners, rows, width)
    received = lax.all_to_all(sent, "dp", split_axis=0, concat_axis=0, tiled=True).astype(f32)
    same = adapters[:, None] == adapters[None, :]
    total = jnp.sum(jnp.where(same, lengths[None, :], 0), axis=1).astype(f32)
    summed = jax.ops.segment_sum(received, adapters, num_segments=count)
    denom = jnp.ones((count,), f32).at[adapters].set(jnp.maximum(total, 1.0))
    gradient = (summed / denom[:, None, None]).astype(jnp.bfloat16)
    grad_input = jnp.dot(dhidden16, down.T, preferred_element_type=f32).astype(jnp.bfloat16)
    return grad_input, gradient[:, None]


def solution(mesh):
    owners, cores = mesh.shape["dp"], mesh.shape["tensor"]

    def on_device(activations, cotangent, adapter_weight_pair, *rest):
        rows = adapter_weight_pair.shape[2]
        fits = owners & (owners - 1) == 0 and cores == 2 and rows % 256 == 0
        body = with_kernels if fits else without_kernels
        return body(activations, cotangent, adapter_weight_pair, *rest)

    in_specs = (
        P(("group", "dp"), "tensor"),
        P(("group", "dp"), "tensor"),
        P(None, "tensor", "dp", None),
        P("group", None),
        P("group", None),
    )
    out_specs = (P(("group", "dp"), "tensor"), P("group", "tensor", "dp", None))
    return jax.shard_map(
        on_device, mesh=mesh, in_specs=in_specs, out_specs=out_specs, check_vma=False
    )
```

time: 76.3 us -> 83.4 us (1.093)
  starting transfers between devices: 48.7 us -> 11 us
  blocking collectives: 0 us -> 21.8 us
  waiting for transfers between devices: 5.86 us -> 26.6 us
  Pallas kernels: 15.4 us -> 20.2 us
  local copies, waits for them, and re-layouts: 5.4 us -> 2.47 us
    ppermute x28 -> x0, starting transfers between devices: 48.6 us -> none  [send_all(): out[k] = lax.ppermute(pieces[k], 'dp', [(i, i ^ k) for i in range(owners)])]
    all_to_all x0 -> x3, waiting for transfers between devices: none -> 25.4 us  [exchange(): return lax.all_to_all(pieces, 'dp', split_axis=0, concat_axis=0, tiled=True)]
    all_to_all x0 -> x1, blocking collectives: none -> 21.8 us  [exchange(): return lax.all_to_all(pieces, 'dp', split_axis=0, concat_axis=0, tiled=True)]
    all_to_all x0 -> x3, starting transfers between devices: none -> 10.9 us  [exchange(): return lax.all_to_all(pieces, 'dp', split_axis=0, concat_axis=0, tiled=True)]
    ppermute x28 -> x0, waiting for transfers between devices: 5.85 us -> none  [send_all(): out[k] = lax.ppermute(pieces[k], 'dp', [(i, i ^ k) for i in range(owners)])]
    unnamed x10 -> x12, local copies, waits for them, and re-layouts: 5.4 us -> 2.47 us
    pallas_call x1, Pallas kernels: 4.8 us -> 7.66 us  [with_kernels(): call(functools.partial(prep_kernel, half), [turned_shape, turned_shape, j...]
    pallas_call x7, Pallas kernels: 10.6 us -> 12.5 us  [the longest x2 3.65 us: pieces(): call(functools.partial(piece_kernel, in_scale, out_scale), packed_shape,...]
  transfers between devices with their start and end apart: 30 -> 5, of which waited for: 5 -> 4; matrix products, arithmetic and copies ran while one was open for 0% -> 0% of each run, Pallas kernels for 13% -> 17%
where the time goes in v2:
time: 83.4 us; the launch traced here: 82.8 us
  waiting for transfers between devices  26.6 us (32%)
  blocking collectives  21.8 us (26%)
  Pallas kernels  20.2 us (24%)
  starting transfers between devices  11 us (13%)
  local copies, waits for them, and re-layouts  2.47 us (3%)
    all_to_all x3, waiting for transfers between devices, exchange(): return lax.all_to_all(pieces, 'dp', split_axis=0, concat_axis=0, tiled=True)  25.4 us
    all_to_all x1, blocking collectives, exchange(): return lax.all_to_all(pieces, 'dp', split_axis=0, concat_axis=0, tiled=True)  21.8 us
    all_to_all x3, starting transfers between devices, exchange(): return lax.all_to_all(pieces, 'dp', split_axis=0, concat_axis=0, tiled=True)  10.9 us
    pallas_call x1, Pallas kernels, with_kernels(): call(functools.partial(prep_kernel, half), [turned_shape, turned_shape, j...  7.66 us
    pallas_call x2, Pallas kernels, pieces(): call(functools.partial(piece_kernel, in_scale, out_scale), packed_shape,...  3.65 us
    pallas_call x1, Pallas kernels, with_kernels(): call(pack_kernel, [packed_shape] * 2, [in_smem, in_hbm], [in_vmem] * 2, [...  3.61 us
    unnamed x12, local copies, waits for them, and re-layouts  2.47 us
    pallas_call x1, Pallas kernels, with_kernels(): call(merge_kernel, jax.ShapeDtypeStruct(table.shape, bf16), [in_smem, in_...  2.43 us
  transfers between devices with their start and end apart: 5, of which 4 were waited for; matrix products, arithmetic and copies ran while one was open for 0% of the time, Pallas kernels for 17%

profile of v2, /device:TPU:0, one launch (start us, length us, event | category | flops | bytes accessed | tf_op | source)
XLA Modules:
  0.0 82.8 jit_solution(17409227261968704131)
XLA Ops:
  0.6 0.0 copy-start
  0.6 0.0 copy-start.1
  0.7 0.0 copy-start.4
  0.7 0.0 copy-start.5
  0.7 3.6 %shard_map.68 = (bf16[8,256,128]{2,1,0:T(8,128)(2,1)}, bf16[8,256,128]{2,1,0:T(8,128)(2,1)}) custom-call(s32[8]{0:T(128)} %bitcast.11, bf16[96,512,128]{2,1,0:T(8,128)(2,1)} %bitcast.13), custom_call_target="tpu_custom_call" | custom-call | bytes 2097152 | tf_op jit(solution)/shard_map/pallas_call | solution.py:181
  4.3 21.8 %all_to_all.20.packed = bf16[8,256,128]{2,1,0:T(8,128)(2,1)S(1)} all-to-all(bf16[8,256,128]{2,1,0:T(8,128)(2,1)} %get-tuple-element.7.after), channel_id=1, replica_groups=mesh['group'=2,'dp'=8,'tensor'=2] {'dp'}, dimensions={0} | all-to-all | bytes 1048576 | tf_op jit(solution)/shard_map/all_to_all | solution.py:160
  26.1 3.6 %all-to-all-start.1 = ((bf16[8,256,128]{2,1,0:T(8,128)(2,1)}), bf16[8,256,128]{2,1,0:T(8,128)(2,1)S(1)}, u32[]{:S(2)}, u32[]{:S(2)}) async-start(bf16[8,256,128]{2,1,0:T(8,128)(2,1)} %get-tuple-element.8), calls=%async_computation.1 | async-start | bytes 1048576 | tf_op jit(solution)/shard_map/all_to_all | solution.py:160
  29.7 0.0 copy-done
  29.7 0.4 shard_map.69.mine
  30.1 0.1 collective-permute-start
  30.2 7.7 %shard_map.71 = (bf16[8,256,256]{2,1,0:T(8,128)(2,1)}, bf16[8,256,256]{2,1,0:T(8,128)(2,1)}, bf16[96,512,128]{2,1,0:T(8,128)(2,1)}) custom-call(bf16[8,256,128]{2,1,0:T(8,128)(2,1)} %get-tuple-element.7.after, bf16[128,4096]{1,0:T(8,128)(2,1)} %tokens.3, bf16[128,4096]{1,0:T(8,128)(2,1)} %y.1), custom_call_target="tpu_custom_call" | custom-call | bytes 16777216 | tf_op jit(solution)/shard_map/pallas_call | solution.py:195
  37.9 0.0 collective-permute-done.other
  37.9 0.0 copy-done.4
  37.9 0.0 copy-start.3
  37.9 1.2 %copy-done.3 = bf16[8,256,256]{2,1,0:T(8,128)(2,1)S(1)} copy-done((bf16[8,256,256]{2,1,0:T(8,128)(2,1)S(1)}, bf16[8,256,256]{2,1,0:T(8,128)(2,1)}, u32[]{:S(2)}) %copy-start.3) | copy-done | bytes 1048600
  39.1 1.8 %shard_map.72 = bf16[8,256,128]{2,1,0:T(8,128)(2,1)} custom-call(s32[1]{0:T(128)} %bitcast.here, s32[8]{0:T(128)S(1)} %bitcast.7, f32[128,128]{1,0:T(8,128)S(1)} %shard_map.69.mine, f32[128,128]{1,0:T(8,128)S(1)} %collective-permute-done.other, bf16[8,256,256]{2,1,0:T(8,128)(2,1)S(1)} %copy-done.3), custom_call_target="tpu_custom_call" | custom-call | flops 134217728 | bytes 1572864 | tf_op jit(solution)/shard_map/pallas_call | solution.py:218
  40.9 2.9 %all-to-all-done.1.packed = bf16[8,256,128]{2,1,0:T(8,128)(2,1)S(1)} async-done(((bf16[8,256,128]{2,1,0:T(8,128)(2,1)}), bf16[8,256,128]{2,1,0:T(8,128)(2,1)S(1)}, u32[]{:S(2)}, u32[]{:S(2)}) %all-to-all-start.1) | async-done | bytes 524320 | tf_op jit(solution)/shard_map/all_to_all | solution.py:160
  43.9 3.6 %all-to-all-start.2 = ((bf16[8,256,128]{2,1,0:T(8,128)(2,1)}), bf16[8,256,128]{2,1,0:T(8,128)(2,1)S(1)}, u32[]{:S(2)}, u32[]{:S(2)}) async-start(bf16[8,256,128]{2,1,0:T(8,128)(2,1)} %shard_map.72), calls=%async_computation.2 | async-start | bytes 1048576 | tf_op jit(solution)/shard_map/all_to_all | solution.py:160
  47.5 0.0 copy-done.1
  47.5 0.4 shard_map.73.mine
  47.9 0.1 collective-permute-start.1
  48.0 1.2 %collective-permute-done.1.other = f32[128,128]{1,0:T(8,128)S(1)} collective-permute-done((f32[128,128]{1,0:T(8,128)S(1)}, f32[128,128]{1,0:T(8,128)S(1)}, u32[]{:S(2)}, u32[]{:S(2)}) %collective-permute-start.1) | collective-permute-done | bytes 65568 | tf_op jit(solution)/shard_map/ppermute | solution.py:165
  49.3 0.0 copy-start.2
  49.3 1.2 %copy-done.2 = bf16[8,256,256]{2,1,0:T(8,128)(2,1)S(1)} copy-done((bf16[8,256,256]{2,1,0:T(8,128)(2,1)S(1)}, bf16[8,256,256]{2,1,0:T(8,128)(2,1)}, u32[]{:S(2)}) %copy-start.2) | copy-done | bytes 1048600
  50.5 1.8 %shard_map.74 = bf16[8,256,128]{2,1,0:T(8,128)(2,1)} custom-call(s32[1]{0:T(128)} %bitcast.here, s32[8]{0:T(128)S(1)} %bitcast.8, f32[128,128]{1,0:T(8,128)S(1)} %shard_map.73.mine, f32[128,128]{1,0:T(8,128)S(1)} %collective-permute-done.1.other, bf16[8,256,256]{2,1,0:T(8,128)(2,1)S(1)} %copy-done.2), custom_call_target="tpu_custom_call" | custom-call | flops 134217728 | bytes 1572864 | tf_op jit(solution)/shard_map/pallas_call | solution.py:218
  52.3 9.8 %all-to-all-done.2.down = bf16[8,256,128]{2,1,0:T(8,128)(2,1)S(1)} async-done(((bf16[8,256,128]{2,1,0:T(8,128)(2,1)}), bf16[8,256,128]{2,1,0:T(8,128)(2,1)S(1)}, u32[]{:S(2)}, u32[]{:S(2)}) %all-to-all-start.2) | async-done | bytes 524320 | tf_op jit(solution)/shard_map/all_to_all | solution.py:160
  62.1 3.6 %all-to-all-start.3 = ((bf16[8,256,128]{2,1,0:T(8,128)(2,1)}), bf16[8,256,128]{2,1,0:T(8,128)(2,1)S(1)}, u32[]{:S(2)}, u32[]{:S(2)}) async-start(bf16[8,256,128]{2,1,0:T(8,128)(2,1)} %shard_map.74), calls=%async_computation.3 | async-start | bytes 1048576 | tf_op jit(solution)/shard_map/all_to_all | solution.py:160
  65.7 2.0 %shard_map.70 = bf16[128,4096]{1,0:T(8,128)(2,1)} custom-call(s32[1]{0:T(128)} %bitcast.here, s32[8]{0:T(128)S(1)} %bitcast.9, f32[128,128]{1,0:T(8,128)S(1)} %shard_map.69.mine, f32[128,128]{1,0:T(8,128)S(1)} %collective-permute-done.other, bf16[8,256,128]{2,1,0:T(8,128)(2,1)S(1)} %all-to-all-done.1.packed), custom_call_target="tpu_custom_call" | custom-call | flops 134217728 | bytes 1572864 | tf_op jit(solution)/shard_map/pallas_call | solution.py:234
  67.7 12.7 %all-to-all-done.3.up = bf16[8,256,128]{2,1,0:T(8,128)(2,1)S(1)} async-done(((bf16[8,256,128]{2,1,0:T(8,128)(2,1)}), bf16[8,256,128]{2,1,0:T(8,128)(2,1)S(1)}, u32[]{:S(2)}, u32[]{:S(2)}) %all-to-all-start.3) | async-done | bytes 524320 | tf_op jit(solution)/shard_map/all_to_all | solution.py:160
  80.4 0.0 copy-done.5
  80.4 2.4 %shard_map.75 = bf16[96,512,128]{2,1,0:T(8,128)(2,1)} custom-call(s32[8]{0:T(128)S(1)} %bitcast.12, s32[8]{0:T(128)S(1)} %bitcast.10, bf16[8,256,128]{2,1,0:T(8,128)(2,1)S(1)} %all-to-all-done.2.down, bf16[8,256,128]{2,1,0:T(8,128)(2,1)S(1)} %all-to-all-done.3.up, bf16[96,512,128]{2,1,0:T(8,128)(2,1)} %get-tuple-element.11.blank), custom_call_target="tpu_custom_call", output_to_operand_aliasing={{}: (4, {})} | custom-call | bytes 2097152 | tf_op jit(solution)/shard_map/pallas_call | solution.py:243
Async XLA Ops:
  0.6 29.1 %copy-start = (bf16[128,4096]{1,0:T(8,128)(2,1)S(1)}, bf16[128,4096]{1,0:T(8,128)(2,1)}, u32[]{:S(2)}) copy-start(bf16[128,4096]{1,0:T(8,128)(2,1)} %y.1) | copy-start | bytes 3145732
  0.6 46.9 %copy-start.1 = (bf16[128,4096]{1,0:T(8,128)(2,1)S(1)}, bf16[128,4096]{1,0:T(8,128)(2,1)}, u32[]{:S(2)}) copy-start(bf16[128,4096]{1,0:T(8,128)(2,1)} %tokens.3) | copy-start | bytes 3145732
  0.7 37.2 %copy-start.4 = (s32[8,1]{0,1:T(1,128)S(1)}, s32[8,1]{0,1:T(1,128)}, u32[]{:S(2)}) copy-start(s32[8,1]{0,1:T(1,128)} %param.9) | copy-start | bytes 100
  0.7 79.7 %copy-start.5 = (s32[8,1]{0,1:T(1,128)S(1)}, s32[8,1]{0,1:T(1,128)}, u32[]{:S(2)}) copy-start(s32[8,1]{0,1:T(1,128)} %param.8) | copy-start | bytes 100
  26.1 17.8 %all-to-all-start.1 = ((bf16[8,256,128]{2,1,0:T(8,128)(2,1)}), bf16[8,256,128]{2,1,0:T(8,128)(2,1)S(1)}, u32[]{:S(2)}, u32[]{:S(2)}) async-start(bf16[8,256,128]{2,1,0:T(8,128)(2,1)} %get-tuple-element.8), calls=%async_computation.1 | async-start | bytes 1048576 | tf_op jit(solution)/shard_map/all_to_all | solution.py:160
  30.1 7.8 %collective-permute-start = (f32[128,128]{1,0:T(8,128)S(1)}, f32[128,128]{1,0:T(8,128)S(1)}, u32[]{:S(2)}, u32[]{:S(2)}) collective-permute-start(f32[128,128]{1,0:T(8,128)S(1)} %shard_map.69.mine), channel_id=1, source_target_pairs={{0,1},{1,0},{2,3},{3,2},{4,5},{5,4},{6,7},{7,6},{8,9},{9,8},{10,11... | collective-permute-start | bytes 196616 | tf_op jit(solution)/shard_map/ppermute | solution.py:165
  37.9 1.2 %copy-start.3 = (bf16[8,256,256]{2,1,0:T(8,128)(2,1)S(1)}, bf16[8,256,256]{2,1,0:T(8,128)(2,1)}, u32[]{:S(2)}) copy-start(bf16[8,256,256]{2,1,0:T(8,128)(2,1)} %get-tuple-element.9.turned) | copy-start | bytes 3145732
  43.9 18.2 %all-to-all-start.2 = ((bf16[8,256,128]{2,1,0:T(8,128)(2,1)}), bf16[8,256,128]{2,1,0:T(8,128)(2,1)S(1)}, u32[]{:S(2)}, u32[]{:S(2)}) async-start(bf16[8,256,128]{2,1,0:T(8,128)(2,1)} %shard_map.72), calls=%async_computation.2 | async-start | bytes 1048576 | tf_op jit(solution)/shard_map/all_to_all | solution.py:160
  47.9 1.3 %collective-permute-start.1 = (f32[128,128]{1,0:T(8,128)S(1)}, f32[128,128]{1,0:T(8,128)S(1)}, u32[]{:S(2)}, u32[]{:S(2)}) collective-permute-start(f32[128,128]{1,0:T(8,128)S(1)} %shard_map.73.mine), channel_id=1, source_target_pairs={{0,1},{1,0},{2,3},{3,2},{4,5},{5,4},{6,7},{7,6},{8,9},{9,8},{10,11... | collective-permute-start | bytes 196616 | tf_op jit(solution)/shard_map/ppermute | solution.py:165
  49.3 1.2 %copy-start.2 = (bf16[8,256,256]{2,1,0:T(8,128)(2,1)S(1)}, bf16[8,256,256]{2,1,0:T(8,128)(2,1)}, u32[]{:S(2)}) copy-start(bf16[8,256,256]{2,1,0:T(8,128)(2,1)} %get-tuple-element.10.turned) | copy-start | bytes 3145732
  62.1 18.3 %all-to-all-start.3 = ((bf16[8,256,128]{2,1,0:T(8,128)(2,1)}), bf16[8,256,128]{2,1,0:T(8,128)(2,1)S(1)}, u32[]{:S(2)}, u32[]{:S(2)}) async-start(bf16[8,256,128]{2,1,0:T(8,128)(2,1)} %shard_map.74), calls=%async_computation.3 | async-start | bytes 1048576 | tf_op jit(solution)/shard_map/all_to_all | solution.py:160

commit v3 on v2

v3 whole, which is shorter than its diff:
```python
import functools

import jax
import jax.numpy as jnp
from jax import lax
from jax.experimental import pallas as pl
from jax.experimental.pallas import tpu as pltpu
from jax.sharding import PartitionSpec as P

adapter_alpha = 128.0

in_vmem = pl.BlockSpec(memory_space=pltpu.VMEM)
in_smem = pl.BlockSpec(memory_space=pltpu.SMEM)
in_hbm = pl.BlockSpec(memory_space=pltpu.HBM)


def low_lanes(rows, width):
    return lax.broadcasted_iota(jnp.int32, (rows, width), 1) < width // 2


def call(kernel, out_shape, in_specs, out_specs, scratch=(), flops=0, moved=0, aliases=None, vmem=40):
    return pl.pallas_call(
        kernel,
        out_shape=out_shape,
        in_specs=in_specs,
        out_specs=out_specs,
        scratch_shapes=list(scratch),
        input_output_aliases=aliases or {},
        compiler_params=pltpu.CompilerParams(vmem_limit_bytes=vmem * 1024 * 1024),
        cost_estimate=pl.CostEstimate(flops=flops, bytes_accessed=moved, transcendentals=0),
    )


def gather_kernel(owners, ids, here, table, *refs):
    out, sems = refs[:owners], refs[owners]
    copies = [
        pltpu.make_async_copy(table.at[ids[here[0] ^ k]], out[k], sems.at[k])
        for k in range(owners)
    ]
    for copy in copies:
        copy.start()
    for copy in copies:
        copy.wait()


def prep_kernel(rows, after, x, y, turned, blank, zeros, sem):
    zeros[...] = jnp.zeros_like(zeros)
    step = zeros.shape[0]
    copies = [
        pltpu.make_async_copy(zeros, blank.at[pl.ds(s, step)], sem.at[s // step])
        for s in range(0, blank.shape[0], step)
    ]
    for copy in copies:
        copy.start()
    tokens = x.shape[0]

    @pl.loop(0, x.shape[1] // rows)
    def _(owner):
        columns = pl.ds(pl.multiple_of(owner * rows, rows), rows)
        turned[owner, :, pl.ds(0, tokens)] = x[:, columns].T
        turned[owner, :, pl.ds(tokens, tokens)] = y[:, columns].T

    for copy in copies:
        copy.wait()


def rank_kernel(owners, here, x, y, *refs):
    pairs, out = refs[:owners], refs[owners]
    rows, width = pairs[0].shape
    tokens = x.shape[0]
    x_rank = jnp.zeros((tokens, width), jnp.float32)
    y_rank = jnp.zeros((tokens, width), jnp.float32)
    for k in range(owners):
        columns = pl.ds(pl.multiple_of((here[0] ^ k) * rows, rows), rows)
        x_rank += jnp.dot(x[:, columns], pairs[k][...], preferred_element_type=jnp.float32)
        y_rank += jnp.dot(y[:, columns], pairs[k][...], preferred_element_type=jnp.float32)
    out[...] = jnp.where(low_lanes(tokens, width), x_rank, y_rank)


def rounded(mine, other, length, scale):
    total = mine[...] + other[...]
    rows, width = total.shape
    total = jnp.where(low_lanes(rows, width), total, scale * total)
    live = lax.broadcasted_iota(jnp.int32, (rows, width), 0) < length
    return jnp.where(live, total, 0.0)


def swap_halves(value):
    return pltpu.roll(value, value.shape[-1] // 2, 1)


def piece_kernel(owners, scale, here, lengths, mine, other, turned, *refs):
    me = here[0]
    both = swap_halves(rounded(mine, other, lengths[me], scale))
    low = low_lanes(*both.shape)
    top = jnp.where(low, both, 0.0).astype(jnp.bfloat16)
    bottom = jnp.where(low, 0.0, both).astype(jnp.bfloat16)
    ranks = jnp.concatenate([top, bottom], axis=0)
    for k in range(owners):
        piece = jnp.dot(turned[me ^ k], ranks, preferred_element_type=jnp.float32)
        refs[k][...] = jnp.where(low_lanes(*piece.shape), piece, scale * piece).astype(jnp.bfloat16)


def input_kernel(owners, scale, here, lengths, mine, other, *refs):
    pairs, out = refs[:owners], refs[owners]
    me = here[0]
    both = swap_halves(rounded(mine, other, lengths[me], scale))
    ranks = jnp.where(low_lanes(*both.shape), both, 0.0).astype(jnp.bfloat16)
    rows = pairs[0].shape[0]
    for k in range(owners):
        columns = pl.ds(pl.multiple_of((me ^ k) * rows, rows), rows)
        out[:, columns] = lax.dot_general(
            ranks, pairs[k][...], (((1,), (1,)), ((), ())), preferred_element_type=jnp.float32
        ).astype(jnp.bfloat16)


def merge_kernel(owners, ids, here, lengths, *refs):
    pieces = refs[:owners]
    out, total, held, sems = refs[owners + 1 :]
    blocks = [here[0] ^ k for k in range(owners)]
    copies, firsts = [], []
    for k in range(owners):
        adapter = ids[blocks[k]]
        copies.append(pltpu.make_async_copy(held.at[k], out.at[adapter], sems.at[k]))
        same = [ids[blocks[other]] == adapter for other in range(owners)]
        earlier = functools.reduce(jnp.logical_or, same[:k], jnp.bool_(False))
        later = functools.reduce(jnp.logical_or, same[k + 1 :], jnp.bool_(False))
        firsts.append(jnp.logical_not(earlier))

        def store(value, count):
            denom = jnp.maximum(count.astype(jnp.float32), 1.0)
            part = 1.0 / jnp.full((1, value.shape[1]), denom)
            held[k] = (value * part).astype(jnp.bfloat16)
            copies[k].start()

        @pl.when(firsts[k] & jnp.logical_not(later))
        def _():
            store(pieces[k][...].astype(jnp.float32), lengths[blocks[k]])

        @pl.when(firsts[k] & later)
        def _():
            total[...] = pieces[k][...].astype(jnp.float32)
            count = lengths[blocks[k]]
            for other in range(k + 1, owners):
                count += jnp.where(same[other], lengths[blocks[other]], 0)

                @pl.when(same[other])
                def _():
                    total[...] += pieces[other][...].astype(jnp.float32)

            store(total[...], count)

    for k in range(owners):
        pl.when(firsts[k])(copies[k].wait)


def exchange(pieces):
    owners = len(pieces)
    far = list(range(owners // 2, owners))
    near = list(range(1, owners // 2))
    order = [near[0], far[0], near[1], far[1], far[2], far[3], near[2]] if owners == 8 else near + far
    after = {far[3]: near[0], near[2]: near[1]} if owners == 8 else {}
    out = {0: pieces[0]}
    for k in order:
        piece = pieces[k]
        if k in after:
            piece, out[after[k]] = lax.optimization_barrier((piece, out[after[k]]))
        out[k] = lax.ppermute(piece, "dp", [(i, i ^ k) for i in range(owners)])
    return [out[k] for k in range(owners)]


def across_cores(value):
    cores = lax.axis_size("tensor")
    return lax.ppermute(value, "tensor", [(i, i ^ 1) for i in range(cores)])


def with_kernels(activations, cotangent, adapter_weight_pair, adapter_of_block, block_live_length):
    owners = lax.axis_size("dp")
    here = lax.axis_index("dp").astype(jnp.int32).reshape(1)
    ids, lengths = adapter_of_block[:, 0], block_live_length[:, 0]
    count, _, rows, width = adapter_weight_pair.shape
    table = adapter_weight_pair.reshape(count, rows, width)
    tokens, features = activations.shape
    scale = adapter_alpha / (width // 2)
    bf16, f32 = jnp.bfloat16, jnp.float32
    pair_shapes = [jax.ShapeDtypeStruct((rows, width), bf16)] * owners
    pair_bytes = owners * rows * width * 2
    token_bytes = tokens * features * 2

    sent = call(
        functools.partial(gather_kernel, owners),
        pair_shapes,
        [in_smem, in_smem, in_hbm],
        [in_vmem] * owners,
        [pltpu.SemaphoreType.DMA((owners,))],
        moved=2 * pair_bytes,
        vmem=53,
    )(ids, here, table)
    pairs = exchange(sent)

    step = 8
    turned, blank = call(
        functools.partial(prep_kernel, rows),
        [
            jax.ShapeDtypeStruct((owners, rows, 2 * tokens), bf16),
            jax.ShapeDtypeStruct(table.shape, bf16),
        ],
        [in_hbm, in_vmem, in_vmem],
        [in_vmem, in_hbm],
        [pltpu.VMEM((step, rows, width), bf16), pltpu.SemaphoreType.DMA((count // step,))],
        moved=4 * token_bytes + 2 * count * rows * width,
    )(pairs[2], activations, cotangent)
    *pairs, turned, blank = lax.optimization_barrier((*pairs, turned, blank))

    mine = call(
        functools.partial(rank_kernel, owners),
        jax.ShapeDtypeStruct((tokens, width), f32),
        [in_smem] + [in_vmem] * (2 + owners),
        in_vmem,
        flops=4 * tokens * features * width,
        moved=2 * token_bytes + pair_bytes,
    )(here, activations, cotangent, *pairs)
    other = across_cores(mine)

    pieces = call(
        functools.partial(piece_kernel, owners, scale),
        pair_shapes,
        [in_smem] * 2 + [in_vmem] * 3,
        [in_vmem] * owners,
        flops=4 * tokens * features * width,
        moved=2 * token_bytes + pair_bytes,
    )(here, lengths, mine, other, turned)
    arrived = exchange(pieces)

    grad_input = call(
        functools.partial(input_kernel, owners, scale),
        jax.ShapeDtypeStruct((tokens, features), bf16),
        [in_smem] * 2 + [in_vmem] * (2 + owners),
        in_vmem,
        flops=2 * tokens * features * width,
        moved=token_bytes + pair_bytes,
    )(here, lengths, mine, other, *pairs)

    gradient = call(
        functools.partial(merge_kernel, owners),
        jax.ShapeDtypeStruct(table.shape, bf16),
        [in_smem] * 3 + [in_vmem] * owners + [in_hbm],
        in_hbm,
        [
            pltpu.VMEM((rows, width), f32),
            pltpu.VMEM((owners, rows, width), bf16),
            pltpu.SemaphoreType.DMA((owners,)),
        ],
        moved=2 * pair_bytes,
        aliases={3 + owners: 0},
    )(ids, here, lengths, *arrived, blank)
    return grad_input, gradient[:, None]


def without_kernels(activations, cotangent, adapter_weight_pair, adapter_of_block, block_live_length):
    owners = lax.axis_size("dp")
    here = lax.axis_index("dp")
    count, _, rows, width = adapter_weight_pair.shape
    rank = width // 2
    scale = adapter_alpha / rank
    adapters = adapter_of_block[:, 0]
    lengths = block_live_length[:, 0]
    keep = (jnp.arange(activations.shape[0], dtype=jnp.int32) < lengths[here])[:, None]
    inputs = jnp.where(keep, activations, jnp.zeros_like(activations))
    grads_out = jnp.where(keep, cotangent, jnp.zeros_like(cotangent))
    fetched = lax.all_to_all(
        adapter_weight_pair[:, 0][adapters], "dp", split_axis=0, concat_axis=0, tiled=True
    )
    pair = fetched.reshape(-1, width)
    down, upward = pair[:, :rank], pair[:, rank:]
    f32 = jnp.float32
    hidden_part = jnp.dot(inputs, down, preferred_element_type=f32)
    dhidden_part = scale * jnp.dot(grads_out, upward, preferred_element_type=f32)
    hidden, dhidden = lax.psum((hidden_part, dhidden_part), "tensor")
    hidden16, dhidden16 = hidden.astype(jnp.bfloat16), dhidden.astype(jnp.bfloat16)
    d_down = jnp.dot(inputs.T, dhidden16, preferred_element_type=f32)
    d_up = scale * jnp.dot(grads_out.T, hidden16, preferred_element_type=f32)
    sent = jnp.concatenate([d_down, d_up], axis=1).astype(jnp.bfloat16).reshape(owners, rows, width)
    received = lax.all_to_all(sent, "dp", split_axis=0, concat_axis=0, tiled=True).astype(f32)
    same = adapters[:, None] == adapters[None, :]
    total = jnp.sum(jnp.where(same, lengths[None, :], 0), axis=1).astype(f32)
    summed = jax.ops.segment_sum(received, adapters, num_segments=count)
    denom = jnp.ones((count,), f32).at[adapters].set(jnp.maximum(total, 1.0))
    gradient = (summed / denom[:, None, None]).astype(jnp.bfloat16)
    grad_input = jnp.dot(dhidden16, down.T, preferred_element_type=f32).astype(jnp.bfloat16)
    return grad_input, gradient[:, None]


def solution(mesh):
    owners, cores = mesh.shape["dp"], mesh.shape["tensor"]

    def on_device(activations, cotangent, adapter_weight_pair, *rest):
        rows = adapter_weight_pair.shape[2]
        fits = owners & (owners - 1) == 0 and cores == 2 and rows % 256 == 0
        body = with_kernels if fits else without_kernels
        return body(activations, cotangent, adapter_weight_pair, *rest)

    in_specs = (
        P(("group", "dp"), "tensor"),
        P(("group", "dp"), "tensor"),
        P(None, "tensor", "dp", None),
        P("group", None),
        P("group", None),
    )
    out_specs = (P(("group", "dp"), "tensor"), P("group", "tensor", "dp", None))
    return jax.shard_map(
        on_device, mesh=mesh, in_specs=in_specs, out_specs=out_specs, check_vma=False
    )
```

time: 83.4 us -> 64.4 us (0.77)
  the two profiles are of different devices: /device:TPU:0 before, /device:TPU:12 now
where the time goes in v3:
time: 64.4 us; the launch traced here: 64.2 us
  waiting for transfers between devices  27.2 us (42%)
  starting transfers between devices  22.5 us (35%)
  Pallas kernels  13 us (20%)
  local copies, waits for them, and re-layouts  0.8 us (1%)
  between operations  0.72 us (1%)
    ppermute x14, waiting for transfers between devices, exchange(): out[k] = lax.ppermute(piece, 'dp', [(i, i ^ k) for i in range(owners)])  26 us
    ppermute x14, starting transfers between devices, exchange(): out[k] = lax.ppermute(piece, 'dp', [(i, i ^ k) for i in range(owners)])  22.4 us
    pallas_call x1, Pallas kernels, with_kernels(): call(functools.partial(prep_kernel, rows), [jax.ShapeDtypeStruct((owners,...  4.8 us
    pallas_call x1, Pallas kernels, with_kernels(): call(functools.partial(gather_kernel, owners), pair_shapes, [in_smem, in_...  2.55 us
    pallas_call x1, Pallas kernels, with_kernels(): call(functools.partial(input_kernel, owners, scale), jax.ShapeDtypeStruct...  1.98 us
    pallas_call x1, Pallas kernels, with_kernels(): call(functools.partial(merge_kernel, owners), jax.ShapeDtypeStruct(table....  1.68 us
    pallas_call x1, Pallas kernels, with_kernels(): call(functools.partial(piece_kernel, owners, scale), pair_shapes, [in_sme...  1.32 us
  transfers between devices with their start and end apart: 15, of which 9 were waited for; matrix products, arithmetic and copies ran while one was open for 0% of the time, Pallas kernels for 11%

profile of v3, /device:TPU:12, one launch (start us, length us, event | category | flops | bytes accessed | tf_op | source)
XLA Modules:
  0.0 64.2 jit_solution(1163717414162172061)
XLA Ops:
  0.7 0.8 %copy-done.3 = s32[8,1]{0,1:T(1,128)S(1)} copy-done((s32[8,1]{0,1:T(1,128)S(1)}, s32[8,1]{0,1:T(1,128)}, u32[]{:S(2)}) %copy-start.3) | copy-done | bytes 56
  1.5 2.5 %shard_map.68 = (bf16[512,128]{1,0:T(8,128)(2,1)S(1)}, bf16[512,128]{1,0:T(8,128)(2,1)S(1)}, bf16[512,128]{1,0:T(8,128)(2,1)S(1)}, bf16[512,128]{1,0:T(8,128)(2,...) custom-call(s32[8]{0:T(128)S(1)} %bitcast.10, ...), custom_call_target="tpu_custom_call" | custom-call | bytes 2097152 | tf_op jit(solution)/shard_map/pallas_call | solution.py:190
  4.0 1.6 %collective-permute-start = (bf16[512,128]{1,0:T(8,128)(2,1)S(1)}, bf16[512,128]{1,0:T(8,128)(2,1)S(1)}, u32[]{:S(2)}, u32[]{:S(2)}) collective-permute-start(bf16[512,128]{1,0:T(8,128)(2,1)S(1)} %get-tuple-element.40), channel_id=1, source_target_pairs={{0,2},{2,0},{4,6},{6,4},{8,10},{10,8},{12,14},{14,12},{1,3},{3,1},... | collective-permute-start | bytes 393224 | tf_op jit(solution)/shard_map/ppermute | solution.py:168
  5.6 0.4 collective-permute-start.1
  6.0 2.6 %collective-permute-start.3 = (bf16[512,128]{1,0:T(8,128)(2,1)S(1)}, bf16[512,128]{1,0:T(8,128)(2,1)S(1)}, u32[]{:S(2)}, u32[]{:S(2)}) collective-permute-start(bf16[512,128]{1,0:T(8,128)(2,1)S(1)} %get-tuple-element.46), channel_id=1, source_target_pairs={{0,8},{2,10},{4,12},{6,14},{8,0},{10,2},{12,4},{14,6},{1,9},{3,11}... | collective-permute-start | bytes 393224 | tf_op jit(solution)/shard_map/ppermute | solution.py:168
  8.6 0.3 collective-permute-start.4
  8.9 2.7 %collective-permute-start.5 = (bf16[512,128]{1,0:T(8,128)(2,1)S(1)}, bf16[512,128]{1,0:T(8,128)(2,1)S(1)}, u32[]{:S(2)}, u32[]{:S(2)}) collective-permute-start(bf16[512,128]{1,0:T(8,128)(2,1)S(1)} %get-tuple-element.48), channel_id=1, source_target_pairs={{0,12},{2,14},{4,8},{6,10},{8,4},{10,6},{12,0},{14,2},{1,13},{3,15... | collective-permute-start | bytes 393224 | tf_op jit(solution)/shard_map/ppermute | solution.py:168
  11.6 0.0 collective-permute-done.refs_1_
  11.6 0.9 %collective-permute-start.6 = (bf16[512,128]{1,0:T(8,128)(2,1)}, bf16[512,128]{1,0:T(8,128)(2,1)S(1)}, u32[]{:S(2)}, u32[]{:S(2)}) collective-permute-start(bf16[512,128]{1,0:T(8,128)(2,1)} %get-tuple-element.49), channel_id=1, source_target_pairs={{0,14},{2,12},{4,10},{6,8},{8,6},{10,4},{12,2},{14,0},{1,15},{3,13... | collective-permute-start | bytes 393224 | tf_op jit(solution)/shard_map/ppermute | solution.py:168
  12.6 0.0 collective-permute-done.1.after.refs_2_
  12.6 2.7 %collective-permute-start.2 = (bf16[512,128]{1,0:T(8,128)(2,1)S(1)}, bf16[512,128]{1,0:T(8,128)(2,1)S(1)}, u32[]{:S(2)}, u32[]{:S(2)}) collective-permute-start(bf16[512,128]{1,0:T(8,128)(2,1)S(1)} %get-tuple-element.45), channel_id=1, source_target_pairs={{0,6},{2,4},{4,2},{6,0},{8,14},{10,12},{12,10},{14,8},{1,7},{3,5},... | collective-permute-start | bytes 393224 | tf_op jit(solution)/shard_map/ppermute | solution.py:168
  15.2 4.8 %shard_map.69 = (bf16[8,512,256]{2,1,0:T(8,128)(2,1)S(1)}, bf16[96,512,128]{2,1,0:T(8,128)(2,1)}) custom-call(bf16[512,128]{1,0:T(8,128)(2,1)S(1)} %collective-permute-done.1.after.refs_2_, bf16[128,4096]{1,0:T(8,128)(2,1)S(1)} %copy-done, bf16[128,4096]{1,0:T(8,128)(2,1)S(1)} %copy-done.1), custom_call_target="tpu_custom_call" | custom-call | bytes 16777216 | tf_op jit(solution)/shard_map/pallas_call | solution.py:202
  20.0 3.5 %collective-permute-done.3.refs_4_ = bf16[512,128]{1,0:T(8,128)(2,1)S(1)} collective-permute-done((bf16[512,128]{1,0:T(8,128)(2,1)S(1)}, bf16[512,128]{1,0:T(8,128)(2,1)S(1)}, u32[]{:S(2)}, u32[]{:S(2)}) %collective-permute-start.3) | collective-permute-done | bytes 131104 | tf_op jit(solution)/shard_map/ppermute | solution.py:168
  23.5 2.8 %collective-permute-done.4.refs_5_ = bf16[512,128]{1,0:T(8,128)(2,1)S(1)} collective-permute-done((bf16[512,128]{1,0:T(8,128)(2,1)S(1)}, bf16[512,128]{1,0:T(8,128)(2,1)S(1)}, u32[]{:S(2)}, u32[]{:S(2)}) %collective-permute-start.4) | collective-permute-done | bytes 131104 | tf_op jit(solution)/shard_map/ppermute | solution.py:168
  26.3 3.5 %collective-permute-done.5.refs_6_ = bf16[512,128]{1,0:T(8,128)(2,1)S(1)} collective-permute-done((bf16[512,128]{1,0:T(8,128)(2,1)S(1)}, bf16[512,128]{1,0:T(8,128)(2,1)S(1)}, u32[]{:S(2)}, u32[]{:S(2)}) %collective-permute-start.5) | collective-permute-done | bytes 131104 | tf_op jit(solution)/shard_map/ppermute | solution.py:168
  29.8 1.7 %collective-permute-done.6.refs_7_ = bf16[512,128]{1,0:T(8,128)(2,1)S(1)} collective-permute-done((bf16[512,128]{1,0:T(8,128)(2,1)}, bf16[512,128]{1,0:T(8,128)(2,1)S(1)}, u32[]{:S(2)}, u32[]{:S(2)}) %collective-permute-start.6) | collective-permute-done | bytes 131104 | tf_op jit(solution)/shard_map/ppermute | solution.py:168
  31.4 0.0 collective-permute-done.2.refs_3_
  31.4 0.7 %shard_map.70.mine = f32[128,128]{1,0:T(8,128)S(1)} custom-call(s32[1]{0:T(128)} %bitcast.here, bf16[128,4096]{1,0:T(8,128)(2,1)S(1)} %copy-done, bf16[128,4096]{1,0:T(8,128)(2,1)S(1)} %copy-done.1, bf16[512,128]{1,0:T(8,128)(2,1)S(1)} %get-tuple-element.52.refs_0_, bf16[512,128]{1,0:T(8,128)(2,1)S(1)} %collective-permute-done.refs_1_, ...), custom_call_target="tpu_custom_call" | custom-call | flops 268435456 | bytes 3145728 | tf_op jit(solution)/shard_map/pallas_call | solution.py:215
  32.2 0.1 collective-permute-start.7
  32.2 1.2 %collective-permute-done.7.other = f32[128,128]{1,0:T(8,128)S(1)} collective-permute-done((f32[128,128]{1,0:T(8,128)S(1)}, f32[128,128]{1,0:T(8,128)S(1)}, u32[]{:S(2)}, u32[]{:S(2)}) %collective-permute-start.7) | collective-permute-done | bytes 65568 | tf_op jit(solution)/shard_map/ppermute | solution.py:174
  33.5 1.3 %shard_map.72 = (bf16[512,128]{1,0:T(8,128)(2,1)S(1)}, bf16[512,128]{1,0:T(8,128)(2,1)S(1)}, bf16[512,128]{1,0:T(8,128)(2,1)S(1)}, bf16[512,128]{1,0:T(8,128)(2,...) custom-call(s32[1]{0:T(128)} %bitcast.here, ...), custom_call_target="tpu_custom_call" | custom-call | flops 268435456 | bytes 3145728 | tf_op jit(solution)/shard_map/pallas_call | solution.py:225
  34.8 1.6 %collective-permute-start.8 = (bf16[512,128]{1,0:T(8,128)(2,1)S(1)}, bf16[512,128]{1,0:T(8,128)(2,1)S(1)}, u32[]{:S(2)}, u32[]{:S(2)}) collective-permute-start(bf16[512,128]{1,0:T(8,128)(2,1)S(1)} %get-tuple-element.63), channel_id=1, source_target_pairs={{0,2},{2,0},{4,6},{6,4},{8,10},{10,8},{12,14},{14,12},{1,3},{3,1},... | collective-permute-start | bytes 393224 | tf_op jit(solution)/shard_map/ppermute | solution.py:168
  36.4 3.0 %collective-permute-start.11 = (bf16[512,128]{1,0:T(8,128)(2,1)S(1)}, bf16[512,128]{1,0:T(8,128)(2,1)S(1)}, u32[]{:S(2)}, u32[]{:S(2)}) collective-permute-start(bf16[512,128]{1,0:T(8,128)(2,1)S(1)} %get-tuple-element.69), channel_id=1, source_target_pairs={{0,8},{2,10},{4,12},{6,14},{8,0},{10,2},{12,4},{14,6},{1,9},{3,11}... | collective-permute-start | bytes 393224 | tf_op jit(solution)/shard_map/ppermute | solution.py:168
  39.4 1.4 %collective-permute-start.13 = (bf16[512,128]{1,0:T(8,128)(2,1)S(1)}, bf16[512,128]{1,0:T(8,128)(2,1)S(1)}, u32[]{:S(2)}, u32[]{:S(2)}) collective-permute-start(bf16[512,128]{1,0:T(8,128)(2,1)S(1)} %get-tuple-element.71), channel_id=1, source_target_pairs={{0,12},{2,14},{4,8},{6,10},{8,4},{10,6},{12,0},{14,2},{1,13},{3,15... | collective-permute-start | bytes 393224 | tf_op jit(solution)/shard_map/ppermute | solution.py:168
  40.8 2.1 %collective-permute-start.14 = (bf16[512,128]{1,0:T(8,128)(2,1)S(1)}, bf16[512,128]{1,0:T(8,128)(2,1)S(1)}, u32[]{:S(2)}, u32[]{:S(2)}) collective-permute-start(bf16[512,128]{1,0:T(8,128)(2,1)S(1)} %get-tuple-element.72), channel_id=1, source_target_pairs={{0,14},{2,12},{4,10},{6,8},{8,6},{10,4},{12,2},{14,0},{1,15},{3,13... | collective-permute-start | bytes 393224 | tf_op jit(solution)/shard_map/ppermute | solution.py:168
  42.9 3.1 %collective-permute-start.10 = (bf16[512,128]{1,0:T(8,128)(2,1)S(1)}, bf16[512,128]{1,0:T(8,128)(2,1)S(1)}, u32[]{:S(2)}, u32[]{:S(2)}) collective-permute-start(bf16[512,128]{1,0:T(8,128)(2,1)S(1)} %get-tuple-element.68), channel_id=1, source_target_pairs={{0,6},{2,4},{4,2},{6,0},{8,14},{10,12},{12,10},{14,8},{1,7},{3,5},... | collective-permute-start | bytes 393224 | tf_op jit(solution)/shard_map/ppermute | solution.py:168
  46.0 2.0 %shard_map.71 = bf16[128,4096]{1,0:T(8,128)(2,1)} custom-call(s32[1]{0:T(128)} %bitcast.here, s32[8]{0:T(128)S(1)} %bitcast.8, f32[128,128]{1,0:T(8,128)S(1)} %shard_map.70.mine, f32[128,128]{1,0:T(8,128)S(1)} %collective-permute-done.7.other, bf16[512,128]{1,0:T(8,128)(2,1)S(1)} %get-tuple-element.52.refs_0_, ...), custom_call_target="tpu_custom_call" | custom-call | flops 134217728 | bytes 2097152 | tf_op jit(solution)/shard_map/pallas_call | solution.py:235
  48.0 6.1 %collective-permute-done.11.refs_4_ = bf16[512,128]{1,0:T(8,128)(2,1)S(1)} collective-permute-done((bf16[512,128]{1,0:T(8,128)(2,1)S(1)}, bf16[512,128]{1,0:T(8,128)(2,1)S(1)}, u32[]{:S(2)}, u32[]{:S(2)}) %collective-permute-start.11) | collective-permute-done | bytes 131104 | tf_op jit(solution)/shard_map/ppermute | solution.py:168
  54.1 2.8 %collective-permute-done.12.refs_5_ = bf16[512,128]{1,0:T(8,128)(2,1)S(1)} collective-permute-done((bf16[512,128]{1,0:T(8,128)(2,1)S(1)}, bf16[512,128]{1,0:T(8,128)(2,1)S(1)}, u32[]{:S(2)}, u32[]{:S(2)}) %collective-permute-start.12) | collective-permute-done | bytes 131104 | tf_op jit(solution)/shard_map/ppermute | solution.py:168
  56.9 4.2 %collective-permute-done.13.refs_6_ = bf16[512,128]{1,0:T(8,128)(2,1)S(1)} collective-permute-done((bf16[512,128]{1,0:T(8,128)(2,1)S(1)}, bf16[512,128]{1,0:T(8,128)(2,1)S(1)}, u32[]{:S(2)}, u32[]{:S(2)}) %collective-permute-start.13) | collective-permute-done | bytes 131104 | tf_op jit(solution)/shard_map/ppermute | solution.py:168
  61.2 1.4 %collective-permute-done.14.refs_7_ = bf16[512,128]{1,0:T(8,128)(2,1)S(1)} collective-permute-done((bf16[512,128]{1,0:T(8,128)(2,1)S(1)}, bf16[512,128]{1,0:T(8,128)(2,1)S(1)}, u32[]{:S(2)}, u32[]{:S(2)}) %collective-permute-start.14) | collective-permute-done | bytes 131104 | tf_op jit(solution)/shard_map/ppermute | solution.py:168
  62.6 1.7 %shard_map.73 = bf16[96,512,128]{2,1,0:T(8,128)(2,1)} custom-call(s32[8]{0:T(128)S(1)} %bitcast.11, s32[1]{0:T(128)} %bitcast.here, s32[8]{0:T(128)S(1)} %bitcast.9, bf16[512,128]{1,0:T(8,128)(2,1)S(1)} %get-tuple-element.61.refs_0_, bf16[512,128]{1,0:T(8,128)(2,1)S(1)} %collective-permute-done.8.refs_1_, ...), custom_call_target="tpu_custom_call", output_to_operand_aliasing={{}: (11, {})} | custom-call | bytes 2097152 | tf_op jit(solution)/shard_map/pallas_call | solution.py:244
  (12 shorter events, 0.0 us)
Async XLA Ops:
  0.6 14.6 %copy-start.1 = (bf16[128,4096]{1,0:T(8,128)(2,1)S(1)}, bf16[128,4096]{1,0:T(8,128)(2,1)}, u32[]{:S(2)}) copy-start(bf16[128,4096]{1,0:T(8,128)(2,1)} %y.3) | copy-start | bytes 3145732
  0.6 14.6 %copy-start = (bf16[128,4096]{1,0:T(8,128)(2,1)S(1)}, bf16[128,4096]{1,0:T(8,128)(2,1)}, u32[]{:S(2)}) copy-start(bf16[128,4096]{1,0:T(8,128)(2,1)} %x.3) | copy-start | bytes 3145732
  0.7 32.8 %copy-start.2 = (s32[8,1]{0,1:T(1,128)S(1)}, s32[8,1]{0,1:T(1,128)}, u32[]{:S(2)}) copy-start(s32[8,1]{0,1:T(1,128)} %param.9) | copy-start | bytes 100
  0.7 0.8 %copy-start.3 = (s32[8,1]{0,1:T(1,128)S(1)}, s32[8,1]{0,1:T(1,128)}, u32[]{:S(2)}) copy-start(s32[8,1]{0,1:T(1,128)} %param.8) | copy-start | bytes 100
  4.0 7.6 %collective-permute-start = (bf16[512,128]{1,0:T(8,128)(2,1)S(1)}, bf16[512,128]{1,0:T(8,128)(2,1)S(1)}, u32[]{:S(2)}, u32[]{:S(2)}) collective-permute-start(bf16[512,128]{1,0:T(8,128)(2,1)S(1)} %get-tuple-element.40), channel_id=1, source_target_pairs={{0,2},{2,0},{4,6},{6,4},{8,10},{10,8},{12,14},{14,12},{1,3},{3,1},... | collective-permute-start | bytes 393224 | tf_op jit(solution)/shard_map/ppermute | solution.py:168
  5.6 7.0 %collective-permute-start.1 = (bf16[512,128]{1,0:T(8,128)(2,1)S(1)}, bf16[512,128]{1,0:T(8,128)(2,1)S(1)}, u32[]{:S(2)}, u32[]{:S(2)}) collective-permute-start(bf16[512,128]{1,0:T(8,128)(2,1)S(1)} %get-tuple-element.43), channel_id=1, source_target_pairs={{0,4},{2,6},{4,0},{6,2},{8,12},{10,14},{12,8},{14,10},{1,5},{3,7},... | collective-permute-start | bytes 393224 | tf_op jit(solution)/shard_map/ppermute | solution.py:168
  6.0 17.5 %collective-permute-start.3 = (bf16[512,128]{1,0:T(8,128)(2,1)S(1)}, bf16[512,128]{1,0:T(8,128)(2,1)S(1)}, u32[]{:S(2)}, u32[]{:S(2)}) collective-permute-start(bf16[512,128]{1,0:T(8,128)(2,1)S(1)} %get-tuple-element.46), channel_id=1, source_target_pairs={{0,8},{2,10},{4,12},{6,14},{8,0},{10,2},{12,4},{14,6},{1,9},{3,11}... | collective-permute-start | bytes 393224 | tf_op jit(solution)/shard_map/ppermute | solution.py:168
  8.6 17.7 %collective-permute-start.4 = (bf16[512,128]{1,0:T(8,128)(2,1)S(1)}, bf16[512,128]{1,0:T(8,128)(2,1)S(1)}, u32[]{:S(2)}, u32[]{:S(2)}) collective-permute-start(bf16[512,128]{1,0:T(8,128)(2,1)S(1)} %get-tuple-element.47), channel_id=1, source_target_pairs={{0,10},{2,8},{4,14},{6,12},{8,2},{10,0},{12,6},{14,4},{1,11},{3,9}... | collective-permute-start | bytes 393224 | tf_op jit(solution)/shard_map/ppermute | solution.py:168
  8.9 20.9 %collective-permute-start.5 = (bf16[512,128]{1,0:T(8,128)(2,1)S(1)}, bf16[512,128]{1,0:T(8,128)(2,1)S(1)}, u32[]{:S(2)}, u32[]{:S(2)}) collective-permute-start(bf16[512,128]{1,0:T(8,128)(2,1)S(1)} %get-tuple-element.48), channel_id=1, source_target_pairs={{0,12},{2,14},{4,8},{6,10},{8,4},{10,6},{12,0},{14,2},{1,13},{3,15... | collective-permute-start | bytes 393224 | tf_op jit(solution)/shard_map/ppermute | solution.py:168
  11.6 19.8 %collective-permute-start.6 = (bf16[512,128]{1,0:T(8,128)(2,1)}, bf16[512,128]{1,0:T(8,128)(2,1)S(1)}, u32[]{:S(2)}, u32[]{:S(2)}) collective-permute-start(bf16[512,128]{1,0:T(8,128)(2,1)} %get-tuple-element.49), channel_id=1, source_target_pairs={{0,14},{2,12},{4,10},{6,8},{8,6},{10,4},{12,2},{14,0},{1,15},{3,13... | collective-permute-start | bytes 393224 | tf_op jit(solution)/shard_map/ppermute | solution.py:168
  12.6 18.9 %collective-permute-start.2 = (bf16[512,128]{1,0:T(8,128)(2,1)S(1)}, bf16[512,128]{1,0:T(8,128)(2,1)S(1)}, u32[]{:S(2)}, u32[]{:S(2)}) collective-permute-start(bf16[512,128]{1,0:T(8,128)(2,1)S(1)} %get-tuple-element.45), channel_id=1, source_target_pairs={{0,6},{2,4},{4,2},{6,0},{8,14},{10,12},{12,10},{14,8},{1,7},{3,5},... | collective-permute-start | bytes 393224 | tf_op jit(solution)/shard_map/ppermute | solution.py:168
  32.2 1.3 %collective-permute-start.7 = (f32[128,128]{1,0:T(8,128)S(1)}, f32[128,128]{1,0:T(8,128)S(1)}, u32[]{:S(2)}, u32[]{:S(2)}) collective-permute-start(f32[128,128]{1,0:T(8,128)S(1)} %shard_map.70.mine), channel_id=1, source_target_pairs={{0,1},{1,0},{2,3},{3,2},{4,5},{5,4},{6,7},{7,6},{8,9},{9,8},{10,11... | collective-permute-start | bytes 196616 | tf_op jit(solution)/shard_map/ppermute | solution.py:174
  34.8 6.0 %collective-permute-start.8 = (bf16[512,128]{1,0:T(8,128)(2,1)S(1)}, bf16[512,128]{1,0:T(8,128)(2,1)S(1)}, u32[]{:S(2)}, u32[]{:S(2)}) collective-permute-start(bf16[512,128]{1,0:T(8,128)(2,1)S(1)} %get-tuple-element.63), channel_id=1, source_target_pairs={{0,2},{2,0},{4,6},{6,4},{8,10},{10,8},{12,14},{14,12},{1,3},{3,1},... | collective-permute-start | bytes 393224 | tf_op jit(solution)/shard_map/ppermute | solution.py:168
  36.4 6.6 %collective-permute-start.9 = (bf16[512,128]{1,0:T(8,128)(2,1)S(1)}, bf16[512,128]{1,0:T(8,128)(2,1)S(1)}, u32[]{:S(2)}, u32[]{:S(2)}) collective-permute-start(bf16[512,128]{1,0:T(8,128)(2,1)S(1)} %get-tuple-element.66), channel_id=1, source_target_pairs={{0,4},{2,6},{4,0},{6,2},{8,12},{10,14},{12,8},{14,10},{1,5},{3,7},... | collective-permute-start | bytes 393224 | tf_op jit(solution)/shard_map/ppermute | solution.py:168
  36.4 17.8 %collective-permute-start.11 = (bf16[512,128]{1,0:T(8,128)(2,1)S(1)}, bf16[512,128]{1,0:T(8,128)(2,1)S(1)}, u32[]{:S(2)}, u32[]{:S(2)}) collective-permute-start(bf16[512,128]{1,0:T(8,128)(2,1)S(1)} %get-tuple-element.69), channel_id=1, source_target_pairs={{0,8},{2,10},{4,12},{6,14},{8,0},{10,2},{12,4},{14,6},{1,9},{3,11}... | collective-permute-start | bytes 393224 | tf_op jit(solution)/shard_map/ppermute | solution.py:168
  39.4 17.5 %collective-permute-start.12 = (bf16[512,128]{1,0:T(8,128)(2,1)S(1)}, bf16[512,128]{1,0:T(8,128)(2,1)S(1)}, u32[]{:S(2)}, u32[]{:S(2)}) collective-permute-start(bf16[512,128]{1,0:T(8,128)(2,1)S(1)} %get-tuple-element.70), channel_id=1, source_target_pairs={{0,10},{2,8},{4,14},{6,12},{8,2},{10,0},{12,6},{14,4},{1,11},{3,9}... | collective-permute-start | bytes 393224 | tf_op jit(solution)/shard_map/ppermute | solution.py:168
  39.4 21.7 %collective-permute-start.13 = (bf16[512,128]{1,0:T(8,128)(2,1)S(1)}, bf16[512,128]{1,0:T(8,128)(2,1)S(1)}, u32[]{:S(2)}, u32[]{:S(2)}) collective-permute-start(bf16[512,128]{1,0:T(8,128)(2,1)S(1)} %get-tuple-element.71), channel_id=1, source_target_pairs={{0,12},{2,14},{4,8},{6,10},{8,4},{10,6},{12,0},{14,2},{1,13},{3,15... | collective-permute-start | bytes 393224 | tf_op jit(solution)/shard_map/ppermute | solution.py:168
  40.8 21.7 %collective-permute-start.14 = (bf16[512,128]{1,0:T(8,128)(2,1)S(1)}, bf16[512,128]{1,0:T(8,128)(2,1)S(1)}, u32[]{:S(2)}, u32[]{:S(2)}) collective-permute-start(bf16[512,128]{1,0:T(8,128)(2,1)S(1)} %get-tuple-element.72), channel_id=1, source_target_pairs={{0,14},{2,12},{4,10},{6,8},{8,6},{10,4},{12,2},{14,0},{1,15},{3,13... | collective-permute-start | bytes 393224 | tf_op jit(solution)/shard_map/ppermute | solution.py:168
  42.9 19.6 %collective-permute-start.10 = (bf16[512,128]{1,0:T(8,128)(2,1)S(1)}, bf16[512,128]{1,0:T(8,128)(2,1)S(1)}, u32[]{:S(2)}, u32[]{:S(2)}) collective-permute-start(bf16[512,128]{1,0:T(8,128)(2,1)S(1)} %get-tuple-element.68), channel_id=1, source_target_pairs={{0,6},{2,4},{4,2},{6,0},{8,14},{10,12},{12,10},{14,8},{1,7},{3,5},... | collective-permute-start | bytes 393224 | tf_op jit(solution)/shard_map/ppermute | solution.py:168

commit v4 on v3

--- a/solution.py
+++ b/solution.py
@@ -156,15 +156,12 @@
 
 def exchange(pieces):
     owners = len(pieces)
-    far = list(range(owners // 2, owners))
-    near = list(range(1, owners // 2))
-    order = [near[0], far[0], near[1], far[1], far[2], far[3], near[2]] if owners == 8 else near + far
-    after = {far[3]: near[0], near[2]: near[1]} if owners == 8 else {}
+    order = list(range(owners // 2, owners)) + list(range(1, owners // 2))
     out = {0: pieces[0]}
     for k in order:
         piece = pieces[k]
-        if k in after:
-            piece, out[after[k]] = lax.optimization_barrier((piece, out[after[k]]))
+        if 1 < k < owners // 2:
+            piece, out[k - 1] = lax.optimization_barrier((piece, out[k - 1]))
         out[k] = lax.ppermute(piece, "dp", [(i, i ^ k) for i in range(owners)])
     return [out[k] for k in range(owners)]
 

time: 64.4 us -> 72 us (1.12)
  the two profiles are of different devices: /device:TPU:12 before, /device:TPU:14 now
where the time goes in v4:
time: 72 us; the launch traced here: 71.9 us
  waiting for transfers between devices  35.3 us (49%)
  starting transfers between devices  22 us (31%)
  Pallas kernels  13 us (18%)
  local copies, waits for them, and re-layouts  0.8 us (1%)
  between operations  0.72 us (1%)
    ppermute x14, waiting for transfers between devices, exchange(): out[k] = lax.ppermute(piece, 'dp', [(i, i ^ k) for i in range(owners)])  34 us
    ppermute x14, starting transfers between devices, exchange(): out[k] = lax.ppermute(piece, 'dp', [(i, i ^ k) for i in range(owners)])  22 us
    pallas_call x1, Pallas kernels, with_kernels(): call(functools.partial(prep_kernel, rows), [jax.ShapeDtypeStruct((owners,...  4.8 us
    pallas_call x1, Pallas kernels, with_kernels(): call(functools.partial(gather_kernel, owners), pair_shapes, [in_smem, in_...  2.55 us
    pallas_call x1, Pallas kernels, with_kernels(): call(functools.partial(input_kernel, owners, scale), jax.ShapeDtypeStruct...  1.99 us
    pallas_call x1, Pallas kernels, with_kernels(): call(functools.partial(merge_kernel, owners), jax.ShapeDtypeStruct(table....  1.67 us
  transfers between devices with their start and end apart: 15, of which 12 were waited for; matrix products, arithmetic and copies ran while one was open for 0% of the time, Pallas kernels for 9%

profile of v4, /device:TPU:14, one launch (start us, length us, event | category | flops | bytes accessed | tf_op | source)
XLA Modules:
  0.0 71.9 jit_solution(2727129829240642561)
XLA Ops:
  0.7 0.8 %copy-done.3 = s32[8,1]{0,1:T(1,128)S(1)} copy-done((s32[8,1]{0,1:T(1,128)S(1)}, s32[8,1]{0,1:T(1,128)}, u32[]{:S(2)}) %copy-start.3) | copy-done | bytes 56
  1.5 2.5 %shard_map.68 = (bf16[512,128]{1,0:T(8,128)(2,1)S(1)}, bf16[512,128]{1,0:T(8,128)(2,1)S(1)}, bf16[512,128]{1,0:T(8,128)(2,1)S(1)}, bf16[512,128]{1,0:T(8,128)(2,...) custom-call(s32[8]{0:T(128)S(1)} %bitcast.10, ...), custom_call_target="tpu_custom_call" | custom-call | bytes 2097152 | tf_op jit(solution)/shard_map/pallas_call | solution.py:187
  4.0 0.6 collective-permute-start
  4.6 4.7 %collective-permute-done.refs_1_ = bf16[512,128]{1,0:T(8,128)(2,1)S(1)} collective-permute-done((bf16[512,128]{1,0:T(8,128)(2,1)S(1)}, bf16[512,128]{1,0:T(8,128)(2,1)S(1)}, u32[]{:S(2)}, u32[]{:S(2)}) %collective-permute-start) | collective-permute-done | bytes 131104 | tf_op jit(solution)/shard_map/ppermute | solution.py:165
  9.3 0.4 collective-permute-start.1
  9.8 2.6 %collective-permute-start.3 = (bf16[512,128]{1,0:T(8,128)(2,1)S(1)}, bf16[512,128]{1,0:T(8,128)(2,1)S(1)}, u32[]{:S(2)}, u32[]{:S(2)}) collective-permute-start(bf16[512,128]{1,0:T(8,128)(2,1)S(1)} %get-tuple-element.46), channel_id=1, source_target_pairs={{0,8},{2,10},{4,12},{6,14},{8,0},{10,2},{12,4},{14,6},{1,9},{3,11}... | collective-permute-start | bytes 393224 | tf_op jit(solution)/shard_map/ppermute | solution.py:165
  12.4 0.3 collective-permute-start.4
  12.7 2.7 %collective-permute-start.5 = (bf16[512,128]{1,0:T(8,128)(2,1)S(1)}, bf16[512,128]{1,0:T(8,128)(2,1)S(1)}, u32[]{:S(2)}, u32[]{:S(2)}) collective-permute-start(bf16[512,128]{1,0:T(8,128)(2,1)S(1)} %get-tuple-element.48), channel_id=1, source_target_pairs={{0,12},{2,14},{4,8},{6,10},{8,4},{10,6},{12,0},{14,2},{1,13},{3,15... | collective-permute-start | bytes 393224 | tf_op jit(solution)/shard_map/ppermute | solution.py:165
  15.4 0.9 %collective-permute-start.6 = (bf16[512,128]{1,0:T(8,128)(2,1)}, bf16[512,128]{1,0:T(8,128)(2,1)S(1)}, u32[]{:S(2)}, u32[]{:S(2)}) collective-permute-start(bf16[512,128]{1,0:T(8,128)(2,1)} %get-tuple-element.49), channel_id=1, source_target_pairs={{0,14},{2,12},{4,10},{6,8},{8,6},{10,4},{12,2},{14,0},{1,15},{3,13... | collective-permute-start | bytes 393224 | tf_op jit(solution)/shard_map/ppermute | solution.py:165
  16.3 2.7 %collective-permute-start.2 = (bf16[512,128]{1,0:T(8,128)(2,1)S(1)}, bf16[512,128]{1,0:T(8,128)(2,1)S(1)}, u32[]{:S(2)}, u32[]{:S(2)}) collective-permute-start(bf16[512,128]{1,0:T(8,128)(2,1)S(1)} %get-tuple-element.45), channel_id=1, source_target_pairs={{0,6},{2,4},{4,2},{6,0},{8,14},{10,12},{12,10},{14,8},{1,7},{3,5},... | collective-permute-start | bytes 393224 | tf_op jit(solution)/shard_map/ppermute | solution.py:165
  19.0 4.8 %shard_map.69 = (bf16[8,512,256]{2,1,0:T(8,128)(2,1)S(1)}, bf16[96,512,128]{2,1,0:T(8,128)(2,1)}) custom-call(bf16[512,128]{1,0:T(8,128)(2,1)S(1)} %collective-permute-done.1.after.refs_2_, bf16[128,4096]{1,0:T(8,128)(2,1)S(1)} %copy-done, bf16[128,4096]{1,0:T(8,128)(2,1)S(1)} %copy-done.1), custom_call_target="tpu_custom_call" | custom-call | bytes 16777216 | tf_op jit(solution)/shard_map/pallas_call | solution.py:199
  23.8 3.2 %collective-permute-done.3.refs_4_ = bf16[512,128]{1,0:T(8,128)(2,1)S(1)} collective-permute-done((bf16[512,128]{1,0:T(8,128)(2,1)S(1)}, bf16[512,128]{1,0:T(8,128)(2,1)S(1)}, u32[]{:S(2)}, u32[]{:S(2)}) %collective-permute-start.3) | collective-permute-done | bytes 131104 | tf_op jit(solution)/shard_map/ppermute | solution.py:165
  27.0 2.8 %collective-permute-done.4.refs_5_ = bf16[512,128]{1,0:T(8,128)(2,1)S(1)} collective-permute-done((bf16[512,128]{1,0:T(8,128)(2,1)S(1)}, bf16[512,128]{1,0:T(8,128)(2,1)S(1)}, u32[]{:S(2)}, u32[]{:S(2)}) %collective-permute-start.4) | collective-permute-done | bytes 131104 | tf_op jit(solution)/shard_map/ppermute | solution.py:165
  29.8 3.5 %collective-permute-done.5.refs_6_ = bf16[512,128]{1,0:T(8,128)(2,1)S(1)} collective-permute-done((bf16[512,128]{1,0:T(8,128)(2,1)S(1)}, bf16[512,128]{1,0:T(8,128)(2,1)S(1)}, u32[]{:S(2)}, u32[]{:S(2)}) %collective-permute-start.5) | collective-permute-done | bytes 131104 | tf_op jit(solution)/shard_map/ppermute | solution.py:165
  33.2 1.4 %collective-permute-done.6.refs_7_ = bf16[512,128]{1,0:T(8,128)(2,1)S(1)} collective-permute-done((bf16[512,128]{1,0:T(8,128)(2,1)}, bf16[512,128]{1,0:T(8,128)(2,1)S(1)}, u32[]{:S(2)}, u32[]{:S(2)}) %collective-permute-start.6) | collective-permute-done | bytes 131104 | tf_op jit(solution)/shard_map/ppermute | solution.py:165
  34.6 0.7 shard_map.70.mine
  35.4 1.2 %collective-permute-done.7.other = f32[128,128]{1,0:T(8,128)S(1)} collective-permute-done((f32[128,128]{1,0:T(8,128)S(1)}, f32[128,128]{1,0:T(8,128)S(1)}, u32[]{:S(2)}, u32[]{:S(2)}) %collective-permute-start.7) | collective-permute-done | bytes 65568 | tf_op jit(solution)/shard_map/ppermute | solution.py:171
  36.6 1.3 %shard_map.72 = (bf16[512,128]{1,0:T(8,128)(2,1)S(1)}, bf16[512,128]{1,0:T(8,128)(2,1)S(1)}, bf16[512,128]{1,0:T(8,128)(2,1)S(1)}, bf16[512,128]{1,0:T(8,128)(2,...) custom-call(s32[1]{0:T(128)} %bitcast.here, ...), custom_call_target="tpu_custom_call" | custom-call | flops 268435456 | bytes 3145728 | tf_op jit(solution)/shard_map/pallas_call | solution.py:222
  38.0 1.6 %collective-permute-start.8 = (bf16[512,128]{1,0:T(8,128)(2,1)S(1)}, bf16[512,128]{1,0:T(8,128)(2,1)S(1)}, u32[]{:S(2)}, u32[]{:S(2)}) collective-permute-start(bf16[512,128]{1,0:T(8,128)(2,1)S(1)} %get-tuple-element.63), channel_id=1, source_target_pairs={{0,2},{2,0},{4,6},{6,4},{8,10},{10,8},{12,14},{14,12},{1,3},{3,1},... | collective-permute-start | bytes 393224 | tf_op jit(solution)/shard_map/ppermute | solution.py:165
  39.5 4.1 %collective-permute-done.8.refs_1_ = bf16[512,128]{1,0:T(8,128)(2,1)S(1)} collective-permute-done((bf16[512,128]{1,0:T(8,128)(2,1)S(1)}, bf16[512,128]{1,0:T(8,128)(2,1)S(1)}, u32[]{:S(2)}, u32[]{:S(2)}) %collective-permute-start.8) | collective-permute-done | bytes 131104 | tf_op jit(solution)/shard_map/ppermute | solution.py:165
  43.6 3.0 %collective-permute-start.11 = (bf16[512,128]{1,0:T(8,128)(2,1)S(1)}, bf16[512,128]{1,0:T(8,128)(2,1)S(1)}, u32[]{:S(2)}, u32[]{:S(2)}) collective-permute-start(bf16[512,128]{1,0:T(8,128)(2,1)S(1)} %get-tuple-element.69), channel_id=1, source_target_pairs={{0,8},{2,10},{4,12},{6,14},{8,0},{10,2},{12,4},{14,6},{1,9},{3,11}... | collective-permute-start | bytes 393224 | tf_op jit(solution)/shard_map/ppermute | solution.py:165
  46.6 0.9 %collective-permute-start.12 = (bf16[512,128]{1,0:T(8,128)(2,1)S(1)}, bf16[512,128]{1,0:T(8,128)(2,1)S(1)}, u32[]{:S(2)}, u32[]{:S(2)}) collective-permute-start(bf16[512,128]{1,0:T(8,128)(2,1)S(1)} %get-tuple-element.70), channel_id=1, source_target_pairs={{0,10},{2,8},{4,14},{6,12},{8,2},{10,0},{12,6},{14,4},{1,11},{3,9}... | collective-permute-start | bytes 393224 | tf_op jit(solution)/shard_map/ppermute | solution.py:165
  47.6 1.5 %collective-permute-start.13 = (bf16[512,128]{1,0:T(8,128)(2,1)S(1)}, bf16[512,128]{1,0:T(8,128)(2,1)S(1)}, u32[]{:S(2)}, u32[]{:S(2)}) collective-permute-start(bf16[512,128]{1,0:T(8,128)(2,1)S(1)} %get-tuple-element.71), channel_id=1, source_target_pairs={{0,12},{2,14},{4,8},{6,10},{8,4},{10,6},{12,0},{14,2},{1,13},{3,15... | collective-permute-start | bytes 393224 | tf_op jit(solution)/shard_map/ppermute | solution.py:165
  49.0 0.6 collective-permute-start.14
  49.6 0.4 collective-permute-done.9.refs_2_
  50.0 4.2 %collective-permute-start.10 = (bf16[512,128]{1,0:T(8,128)(2,1)S(1)}, bf16[512,128]{1,0:T(8,128)(2,1)S(1)}, u32[]{:S(2)}, u32[]{:S(2)}) collective-permute-start(bf16[512,128]{1,0:T(8,128)(2,1)S(1)} %get-tuple-element.68), channel_id=1, source_target_pairs={{0,6},{2,4},{4,2},{6,0},{8,14},{10,12},{12,10},{14,8},{1,7},{3,5},... | collective-permute-start | bytes 393224 | tf_op jit(solution)/shard_map/ppermute | solution.py:165
  54.2 2.0 %shard_map.71 = bf16[128,4096]{1,0:T(8,128)(2,1)} custom-call(s32[1]{0:T(128)} %bitcast.here, s32[8]{0:T(128)S(1)} %bitcast.8, f32[128,128]{1,0:T(8,128)S(1)} %shard_map.70.mine, f32[128,128]{1,0:T(8,128)S(1)} %collective-permute-done.7.other, bf16[512,128]{1,0:T(8,128)(2,1)S(1)} %get-tuple-element.52.refs_0_, ...), custom_call_target="tpu_custom_call" | custom-call | flops 134217728 | bytes 2097152 | tf_op jit(solution)/shard_map/pallas_call | solution.py:232
  56.2 4.6 %collective-permute-done.11.refs_4_ = bf16[512,128]{1,0:T(8,128)(2,1)S(1)} collective-permute-done((bf16[512,128]{1,0:T(8,128)(2,1)S(1)}, bf16[512,128]{1,0:T(8,128)(2,1)S(1)}, u32[]{:S(2)}, u32[]{:S(2)}) %collective-permute-start.11) | collective-permute-done | bytes 131104 | tf_op jit(solution)/shard_map/ppermute | solution.py:165
  60.8 2.8 %collective-permute-done.12.refs_5_ = bf16[512,128]{1,0:T(8,128)(2,1)S(1)} collective-permute-done((bf16[512,128]{1,0:T(8,128)(2,1)S(1)}, bf16[512,128]{1,0:T(8,128)(2,1)S(1)}, u32[]{:S(2)}, u32[]{:S(2)}) %collective-permute-start.12) | collective-permute-done | bytes 131104 | tf_op jit(solution)/shard_map/ppermute | solution.py:165
  63.6 4.2 %collective-permute-done.13.refs_6_ = bf16[512,128]{1,0:T(8,128)(2,1)S(1)} collective-permute-done((bf16[512,128]{1,0:T(8,128)(2,1)S(1)}, bf16[512,128]{1,0:T(8,128)(2,1)S(1)}, u32[]{:S(2)}, u32[]{:S(2)}) %collective-permute-start.13) | collective-permute-done | bytes 131104 | tf_op jit(solution)/shard_map/ppermute | solution.py:165
  67.8 2.3 %collective-permute-done.14.refs_7_ = bf16[512,128]{1,0:T(8,128)(2,1)S(1)} collective-permute-done((bf16[512,128]{1,0:T(8,128)(2,1)S(1)}, bf16[512,128]{1,0:T(8,128)(2,1)S(1)}, u32[]{:S(2)}, u32[]{:S(2)}) %collective-permute-start.14) | collective-permute-done | bytes 131104 | tf_op jit(solution)/shard_map/ppermute | solution.py:165
  70.2 1.7 %shard_map.73 = bf16[96,512,128]{2,1,0:T(8,128)(2,1)} custom-call(s32[8]{0:T(128)S(1)} %bitcast.11, s32[1]{0:T(128)} %bitcast.here, s32[8]{0:T(128)S(1)} %bitcast.9, bf16[512,128]{1,0:T(8,128)(2,1)S(1)} %get-tuple-element.61.refs_0_, bf16[512,128]{1,0:T(8,128)(2,1)S(1)} %collective-permute-done.8.refs_1_, ...), custom_call_target="tpu_custom_call", output_to_operand_aliasing={{}: (11, {})} | custom-call | bytes 2097152 | tf_op jit(solution)/shard_map/pallas_call | solution.py:241
  (12 shorter events, 0.1 us)
Async XLA Ops:
  0.6 18.3 %copy-start.1 = (bf16[128,4096]{1,0:T(8,128)(2,1)S(1)}, bf16[128,4096]{1,0:T(8,128)(2,1)}, u32[]{:S(2)}) copy-start(bf16[128,4096]{1,0:T(8,128)(2,1)} %y.3) | copy-start | bytes 3145732
  0.6 18.3 %copy-start = (bf16[128,4096]{1,0:T(8,128)(2,1)S(1)}, bf16[128,4096]{1,0:T(8,128)(2,1)}, u32[]{:S(2)}) copy-start(bf16[128,4096]{1,0:T(8,128)(2,1)} %x.3) | copy-start | bytes 3145732
  0.7 36.0 %copy-start.2 = (s32[8,1]{0,1:T(1,128)S(1)}, s32[8,1]{0,1:T(1,128)}, u32[]{:S(2)}) copy-start(s32[8,1]{0,1:T(1,128)} %param.9) | copy-start | bytes 100
  0.7 0.8 %copy-start.3 = (s32[8,1]{0,1:T(1,128)S(1)}, s32[8,1]{0,1:T(1,128)}, u32[]{:S(2)}) copy-start(s32[8,1]{0,1:T(1,128)} %param.8) | copy-start | bytes 100
  4.0 5.3 %collective-permute-start = (bf16[512,128]{1,0:T(8,128)(2,1)S(1)}, bf16[512,128]{1,0:T(8,128)(2,1)S(1)}, u32[]{:S(2)}, u32[]{:S(2)}) collective-permute-start(bf16[512,128]{1,0:T(8,128)(2,1)S(1)} %get-tuple-element.40), channel_id=1, source_target_pairs={{0,2},{2,0},{4,6},{6,4},{8,10},{10,8},{12,14},{14,12},{1,3},{3,1},... | collective-permute-start | bytes 393224 | tf_op jit(solution)/shard_map/ppermute | solution.py:165
  9.3 7.0 %collective-permute-start.1 = (bf16[512,128]{1,0:T(8,128)(2,1)S(1)}, bf16[512,128]{1,0:T(8,128)(2,1)S(1)}, u32[]{:S(2)}, u32[]{:S(2)}) collective-permute-start(bf16[512,128]{1,0:T(8,128)(2,1)S(1)} %get-tuple-element.43), channel_id=1, source_target_pairs={{0,4},{2,6},{4,0},{6,2},{8,12},{10,14},{12,8},{14,10},{1,5},{3,7},... | collective-permute-start | bytes 393224 | tf_op jit(solution)/shard_map/ppermute | solution.py:165
  9.8 17.2 %collective-permute-start.3 = (bf16[512,128]{1,0:T(8,128)(2,1)S(1)}, bf16[512,128]{1,0:T(8,128)(2,1)S(1)}, u32[]{:S(2)}, u32[]{:S(2)}) collective-permute-start(bf16[512,128]{1,0:T(8,128)(2,1)S(1)} %get-tuple-element.46), channel_id=1, source_target_pairs={{0,8},{2,10},{4,12},{6,14},{8,0},{10,2},{12,4},{14,6},{1,9},{3,11}... | collective-permute-start | bytes 393224 | tf_op jit(solution)/shard_map/ppermute | solution.py:165
  12.4 17.4 %collective-permute-start.4 = (bf16[512,128]{1,0:T(8,128)(2,1)S(1)}, bf16[512,128]{1,0:T(8,128)(2,1)S(1)}, u32[]{:S(2)}, u32[]{:S(2)}) collective-permute-start(bf16[512,128]{1,0:T(8,128)(2,1)S(1)} %get-tuple-element.47), channel_id=1, source_target_pairs={{0,10},{2,8},{4,14},{6,12},{8,2},{10,0},{12,6},{14,4},{1,11},{3,9}... | collective-permute-start | bytes 393224 | tf_op jit(solution)/shard_map/ppermute | solution.py:165
  12.7 20.5 %collective-permute-start.5 = (bf16[512,128]{1,0:T(8,128)(2,1)S(1)}, bf16[512,128]{1,0:T(8,128)(2,1)S(1)}, u32[]{:S(2)}, u32[]{:S(2)}) collective-permute-start(bf16[512,128]{1,0:T(8,128)(2,1)S(1)} %get-tuple-element.48), channel_id=1, source_target_pairs={{0,12},{2,14},{4,8},{6,10},{8,4},{10,6},{12,0},{14,2},{1,13},{3,15... | collective-permute-start | bytes 393224 | tf_op jit(solution)/shard_map/ppermute | solution.py:165
  15.4 19.2 %collective-permute-start.6 = (bf16[512,128]{1,0:T(8,128)(2,1)}, bf16[512,128]{1,0:T(8,128)(2,1)S(1)}, u32[]{:S(2)}, u32[]{:S(2)}) collective-permute-start(bf16[512,128]{1,0:T(8,128)(2,1)} %get-tuple-element.49), channel_id=1, source_target_pairs={{0,14},{2,12},{4,10},{6,8},{8,6},{10,4},{12,2},{14,0},{1,15},{3,13... | collective-permute-start | bytes 393224 | tf_op jit(solution)/shard_map/ppermute | solution.py:165
  16.3 18.3 %collective-permute-start.2 = (bf16[512,128]{1,0:T(8,128)(2,1)S(1)}, bf16[512,128]{1,0:T(8,128)(2,1)S(1)}, u32[]{:S(2)}, u32[]{:S(2)}) collective-permute-start(bf16[512,128]{1,0:T(8,128)(2,1)S(1)} %get-tuple-element.45), channel_id=1, source_target_pairs={{0,6},{2,4},{4,2},{6,0},{8,14},{10,12},{12,10},{14,8},{1,7},{3,5},... | collective-permute-start | bytes 393224 | tf_op jit(solution)/shard_map/ppermute | solution.py:165
  35.3 1.3 %collective-permute-start.7 = (f32[128,128]{1,0:T(8,128)S(1)}, f32[128,128]{1,0:T(8,128)S(1)}, u32[]{:S(2)}, u32[]{:S(2)}) collective-permute-start(f32[128,128]{1,0:T(8,128)S(1)} %shard_map.70.mine), channel_id=1, source_target_pairs={{0,1},{1,0},{2,3},{3,2},{4,5},{5,4},{6,7},{7,6},{8,9},{9,8},{10,11... | collective-permute-start | bytes 196616 | tf_op jit(solution)/shard_map/ppermute | solution.py:171
  38.0 5.6 %collective-permute-start.8 = (bf16[512,128]{1,0:T(8,128)(2,1)S(1)}, bf16[512,128]{1,0:T(8,128)(2,1)S(1)}, u32[]{:S(2)}, u32[]{:S(2)}) collective-permute-start(bf16[512,128]{1,0:T(8,128)(2,1)S(1)} %get-tuple-element.63), channel_id=1, source_target_pairs={{0,2},{2,0},{4,6},{6,4},{8,10},{10,8},{12,14},{14,12},{1,3},{3,1},... | collective-permute-start | bytes 393224 | tf_op jit(solution)/shard_map/ppermute | solution.py:165
  43.6 6.4 %collective-permute-start.9 = (bf16[512,128]{1,0:T(8,128)(2,1)S(1)}, bf16[512,128]{1,0:T(8,128)(2,1)S(1)}, u32[]{:S(2)}, u32[]{:S(2)}) collective-permute-start(bf16[512,128]{1,0:T(8,128)(2,1)S(1)} %get-tuple-element.66), channel_id=1, source_target_pairs={{0,4},{2,6},{4,0},{6,2},{8,12},{10,14},{12,8},{14,10},{1,5},{3,7},... | collective-permute-start | bytes 393224 | tf_op jit(solution)/shard_map/ppermute | solution.py:165
  43.6 17.2 %collective-permute-start.11 = (bf16[512,128]{1,0:T(8,128)(2,1)S(1)}, bf16[512,128]{1,0:T(8,128)(2,1)S(1)}, u32[]{:S(2)}, u32[]{:S(2)}) collective-permute-start(bf16[512,128]{1,0:T(8,128)(2,1)S(1)} %get-tuple-element.69), channel_id=1, source_target_pairs={{0,8},{2,10},{4,12},{6,14},{8,0},{10,2},{12,4},{14,6},{1,9},{3,11}... | collective-permute-start | bytes 393224 | tf_op jit(solution)/shard_map/ppermute | solution.py:165
  46.6 17.0 %collective-permute-start.12 = (bf16[512,128]{1,0:T(8,128)(2,1)S(1)}, bf16[512,128]{1,0:T(8,128)(2,1)S(1)}, u32[]{:S(2)}, u32[]{:S(2)}) collective-permute-start(bf16[512,128]{1,0:T(8,128)(2,1)S(1)} %get-tuple-element.70), channel_id=1, source_target_pairs={{0,10},{2,8},{4,14},{6,12},{8,2},{10,0},{12,6},{14,4},{1,11},{3,9}... | collective-permute-start | bytes 393224 | tf_op jit(solution)/shard_map/ppermute | solution.py:165
  47.6 20.3 %collective-permute-start.13 = (bf16[512,128]{1,0:T(8,128)(2,1)S(1)}, bf16[512,128]{1,0:T(8,128)(2,1)S(1)}, u32[]{:S(2)}, u32[]{:S(2)}) collective-permute-start(bf16[512,128]{1,0:T(8,128)(2,1)S(1)} %get-tuple-element.71), channel_id=1, source_target_pairs={{0,12},{2,14},{4,8},{6,10},{8,4},{10,6},{12,0},{14,2},{1,13},{3,15... | collective-permute-start | bytes 393224 | tf_op jit(solution)/shard_map/ppermute | solution.py:165
  49.0 21.2 %collective-permute-start.14 = (bf16[512,128]{1,0:T(8,128)(2,1)S(1)}, bf16[512,128]{1,0:T(8,128)(2,1)S(1)}, u32[]{:S(2)}, u32[]{:S(2)}) collective-permute-start(bf16[512,128]{1,0:T(8,128)(2,1)S(1)} %get-tuple-element.72), channel_id=1, source_target_pairs={{0,14},{2,12},{4,10},{6,8},{8,6},{10,4},{12,2},{14,0},{1,15},{3,13... | collective-permute-start | bytes 393224 | tf_op jit(solution)/shard_map/ppermute | solution.py:165
  50.0 20.2 %collective-permute-start.10 = (bf16[512,128]{1,0:T(8,128)(2,1)S(1)}, bf16[512,128]{1,0:T(8,128)(2,1)S(1)}, u32[]{:S(2)}, u32[]{:S(2)}) collective-permute-start(bf16[512,128]{1,0:T(8,128)(2,1)S(1)} %get-tuple-element.68), channel_id=1, source_target_pairs={{0,6},{2,4},{4,2},{6,0},{8,14},{10,12},{12,10},{14,8},{1,7},{3,5},... | collective-permute-start | bytes 393224 | tf_op jit(solution)/shard_map/ppermute | solution.py:165

commit v5 on v4

--- a/solution.py
+++ b/solution.py
@@ -31,11 +31,11 @@
     )
 
 
-def gather_kernel(owners, ids, here, table, *refs):
-    out, sems = refs[:owners], refs[owners]
+def gather_kernel(peers, ids, here, table, *refs):
+    out, sems = refs[: len(peers)], refs[len(peers)]
     copies = [
-        pltpu.make_async_copy(table.at[ids[here[0] ^ k]], out[k], sems.at[k])
-        for k in range(owners)
+        pltpu.make_async_copy(table.at[ids[here[0] ^ k]], out[n], sems.at[n])
+        for n, k in enumerate(peers)
     ]
     for copy in copies:
         copy.start()
@@ -64,16 +64,16 @@
         copy.wait()
 
 
-def rank_kernel(owners, here, x, y, *refs):
-    pairs, out = refs[:owners], refs[owners]
+def rank_kernel(peers, here, x, y, *refs):
+    pairs, out = refs[: len(peers)], refs[len(peers)]
     rows, width = pairs[0].shape
     tokens = x.shape[0]
     x_rank = jnp.zeros((tokens, width), jnp.float32)
     y_rank = jnp.zeros((tokens, width), jnp.float32)
-    for k in range(owners):
+    for n, k in enumerate(peers):
         columns = pl.ds(pl.multiple_of((here[0] ^ k) * rows, rows), rows)
-        x_rank += jnp.dot(x[:, columns], pairs[k][...], preferred_element_type=jnp.float32)
-        y_rank += jnp.dot(y[:, columns], pairs[k][...], preferred_element_type=jnp.float32)
+        x_rank += jnp.dot(x[:, columns], pairs[n][...], preferred_element_type=jnp.float32)
+        y_rank += jnp.dot(y[:, columns], pairs[n][...], preferred_element_type=jnp.float32)
     out[...] = jnp.where(low_lanes(tokens, width), x_rank, y_rank)
 
 
@@ -89,35 +89,36 @@
     return pltpu.roll(value, value.shape[-1] // 2, 1)
 
 
-def piece_kernel(owners, scale, here, lengths, mine, other, turned, *refs):
+def piece_kernel(peers, scale, here, lengths, mine, other, turned, *refs):
     me = here[0]
     both = swap_halves(rounded(mine, other, lengths[me], scale))
     low = low_lanes(*both.shape)
     top = jnp.where(low, both, 0.0).astype(jnp.bfloat16)
     bottom = jnp.where(low, 0.0, both).astype(jnp.bfloat16)
     ranks = jnp.concatenate([top, bottom], axis=0)
-    for k in range(owners):
+    for n, k in enumerate(peers):
         piece = jnp.dot(turned[me ^ k], ranks, preferred_element_type=jnp.float32)
-        refs[k][...] = jnp.where(low_lanes(*piece.shape), piece, scale * piece).astype(jnp.bfloat16)
-
-
-def input_kernel(owners, scale, here, lengths, mine, other, *refs):
-    pairs, out = refs[:owners], refs[owners]
+        refs[n][...] = jnp.where(low_lanes(*piece.shape), piece, scale * piece).astype(jnp.bfloat16)
+
+
+def input_kernel(peers, scale, here, lengths, mine, other, *refs):
+    pairs, out = refs[: len(peers)], refs[len(peers)]
     me = here[0]
     both = swap_halves(rounded(mine, other, lengths[me], scale))
     ranks = jnp.where(low_lanes(*both.shape), both, 0.0).astype(jnp.bfloat16)
     rows = pairs[0].shape[0]
-    for k in range(owners):
+    for n, k in enumerate(peers):
         columns = pl.ds(pl.multiple_of((me ^ k) * rows, rows), rows)
         out[:, columns] = lax.dot_general(
-            ranks, pairs[k][...], (((1,), (1,)), ((), ())), preferred_element_type=jnp.float32
+            ranks, pairs[n][...], (((1,), (1,)), ((), ())), preferred_element_type=jnp.float32
         ).astype(jnp.bfloat16)
 
 
-def merge_kernel(owners, ids, here, lengths, *refs):
+def merge_kernel(peers, ids, here, lengths, *refs):
+    owners = len(peers)
     pieces = refs[:owners]
     out, total, held, sems = refs[owners + 1 :]
-    blocks = [here[0] ^ k for k in range(owners)]
+    blocks = [here[0] ^ k for k in peers]
     copies, firsts = [], []
     for k in range(owners):
         adapter = ids[blocks[k]]
@@ -154,16 +155,16 @@
         pl.when(firsts[k])(copies[k].wait)
 
 
-def exchange(pieces):
-    owners = len(pieces)
-    order = list(range(owners // 2, owners)) + list(range(1, owners // 2))
-    out = {0: pieces[0]}
-    for k in order:
-        piece = pieces[k]
-        if 1 < k < owners // 2:
-            piece, out[k - 1] = lax.optimization_barrier((piece, out[k - 1]))
-        out[k] = lax.ppermute(piece, "dp", [(i, i ^ k) for i in range(owners)])
-    return [out[k] for k in range(owners)]
+def peer_order(owners):
+    near = list(range(1, owners // 2))
+    return (0, *range(owners // 2, owners), *near[:1], *near[:0:-1])
+
+
+def exchange(pieces, peers):
+    out = [pieces[0]]
+    for k, piece in zip(peers[1:], pieces[1:]):
+        out.append(lax.ppermute(piece, "dp", [(i, i ^ k) for i in range(len(peers))]))
+    return out
 
 
 def across_cores(value):
@@ -173,6 +174,7 @@
 
 def with_kernels(activations, cotangent, adapter_weight_pair, adapter_of_block, block_live_length):
     owners = lax.axis_size("dp")
+    peers = peer_order(owners)
     here = lax.axis_index("dp").astype(jnp.int32).reshape(1)
     ids, lengths = adapter_of_block[:, 0], block_live_length[:, 0]
     count, _, rows, width = adapter_weight_pair.shape
@@ -185,7 +187,7 @@
     token_bytes = tokens * features * 2
 
     sent = call(
-        functools.partial(gather_kernel, owners),
+        functools.partial(gather_kernel, peers),
         pair_shapes,
         [in_smem, in_smem, in_hbm],
         [in_vmem] * owners,
@@ -193,7 +195,7 @@
         moved=2 * pair_bytes,
         vmem=53,
     )(ids, here, table)
-    pairs = exchange(sent)
+    pairs = exchange(sent, peers)
 
     step = 8
     turned, blank = call(
@@ -206,11 +208,11 @@
         [in_vmem, in_hbm],
         [pltpu.VMEM((step, rows, width), bf16), pltpu.SemaphoreType.DMA((count // step,))],
         moved=4 * token_bytes + 2 * count * rows * width,
-    )(pairs[2], activations, cotangent)
+    )(pairs[5], activations, cotangent)
     *pairs, turned, blank = lax.optimization_barrier((*pairs, turned, blank))
 
     mine = call(
-        functools.partial(rank_kernel, owners),
+        functools.partial(rank_kernel, peers),
         jax.ShapeDtypeStruct((tokens, width), f32),
         [in_smem] + [in_vmem] * (2 + owners),
         in_vmem,
@@ -220,17 +222,17 @@
     other = across_cores(mine)
 
     pieces = call(
-        functools.partial(piece_kernel, owners, scale),
+        functools.partial(piece_kernel, peers, scale),
         pair_shapes,
         [in_smem] * 2 + [in_vmem] * 3,
         [in_vmem] * owners,
         flops=4 * tokens * features * width,
         moved=2 * token_bytes + pair_bytes,
     )(here, lengths, mine, other, turned)
-    arrived = exchange(pieces)
+    arrived = exchange(pieces, peers)
 
     grad_input = call(
-        functools.partial(input_kernel, owners, scale),
+        functools.partial(input_kernel, peers, scale),
         jax.ShapeDtypeStruct((tokens, features), bf16),
         [in_smem] * 2 + [in_vmem] * (2 + owners),
         in_vmem,
@@ -239,7 +241,7 @@
     )(here, lengths, mine, other, *pairs)
 
     gradient = call(
-        functools.partial(merge_kernel, owners),
+        functools.partial(merge_kernel, peers),
         jax.ShapeDtypeStruct(table.shape, bf16),
         [in_smem] * 3 + [in_vmem] * owners + [in_hbm],
         in_hbm,

time: 72 us -> 63.8 us (0.89)
  the two profiles are of different devices: /device:TPU:14 before, /device:TPU:0 now
where the time goes in v5:
time: 63.8 us; the launch traced here: 63.6 us
  waiting for transfers between devices  26.1 us (41%)
  starting transfers between devices  23 us (36%)
  Pallas kernels  13 us (20%)
  local copies, waits for them, and re-layouts  0.8 us (1%)
  between operations  0.76 us (1%)
    ppermute x14, waiting for transfers between devices, exchange(): lax.ppermute(piece, 'dp', [(i, i ^ k) for i in range(len(peers))])  24.8 us
    ppermute x14, starting transfers between devices, exchange(): lax.ppermute(piece, 'dp', [(i, i ^ k) for i in range(len(peers))])  22.9 us
    pallas_call x1, Pallas kernels, with_kernels(): call(functools.partial(prep_kernel, rows), [jax.ShapeDtypeStruct((owners,...  4.8 us
    pallas_call x1, Pallas kernels, with_kernels(): call(functools.partial(gather_kernel, peers), pair_shapes, [in_smem, in_s...  2.55 us
    pallas_call x1, Pallas kernels, with_kernels(): call(functools.partial(input_kernel, peers, scale), jax.ShapeDtypeStruct(...  1.99 us
    pallas_call x1, Pallas kernels, with_kernels(): call(functools.partial(merge_kernel, peers), jax.ShapeDtypeStruct(table.s...  1.64 us
    pallas_call x1, Pallas kernels, with_kernels(): call(functools.partial(piece_kernel, peers, scale), pair_shapes, [in_smem...  1.32 us
  transfers between devices with their start and end apart: 15, of which 6 were waited for; matrix products, arithmetic and copies ran while one was open for 0% of the time, Pallas kernels for 11%

profile of v5, /device:TPU:0, one launch (start us, length us, event | category | flops | bytes accessed | tf_op | source)
XLA Modules:
  0.0 63.6 jit_solution(10491991545216835559)
XLA Ops:
  0.7 0.8 %copy-done.3 = s32[8,1]{0,1:T(1,128)S(1)} copy-done((s32[8,1]{0,1:T(1,128)S(1)}, s32[8,1]{0,1:T(1,128)}, u32[]{:S(2)}) %copy-start.3) | copy-done | bytes 56
  1.5 2.5 %shard_map.68 = (bf16[512,128]{1,0:T(8,128)(2,1)S(1)}, bf16[512,128]{1,0:T(8,128)(2,1)S(1)}, bf16[512,128]{1,0:T(8,128)(2,1)S(1)}, bf16[512,128]{1,0:T(8,128)(2,...) custom-call(s32[8]{0:T(128)S(1)} %bitcast.10, ...), custom_call_target="tpu_custom_call" | custom-call | bytes 2097152 | tf_op jit(solution)/shard_map/pallas_call | solution.py:189
  4.0 4.1 %collective-permute-start = (bf16[512,128]{1,0:T(8,128)(2,1)S(1)}, bf16[512,128]{1,0:T(8,128)(2,1)S(1)}, u32[]{:S(2)}, u32[]{:S(2)}) collective-permute-start(bf16[512,128]{1,0:T(8,128)(2,1)S(1)} %get-tuple-element.31), channel_id=1, source_target_pairs={{0,8},{2,10},{4,12},{6,14},{8,0},{10,2},{12,4},{14,6},{1,9},{3,11}... | collective-permute-start | bytes 393224 | tf_op jit(solution)/shard_map/ppermute | solution.py:166
  8.1 1.5 %collective-permute-start.4 = (bf16[512,128]{1,0:T(8,128)(2,1)S(1)}, bf16[512,128]{1,0:T(8,128)(2,1)S(1)}, u32[]{:S(2)}, u32[]{:S(2)}) collective-permute-start(bf16[512,128]{1,0:T(8,128)(2,1)S(1)} %get-tuple-element.35), channel_id=1, source_target_pairs={{0,2},{2,0},{4,6},{6,4},{8,10},{10,8},{12,14},{14,12},{1,3},{3,1},... | collective-permute-start | bytes 393224 | tf_op jit(solution)/shard_map/ppermute | solution.py:166
  9.6 0.0 collective-permute-start.1
  9.7 3.9 %collective-permute-start.2 = (bf16[512,128]{1,0:T(8,128)(2,1)S(1)}, bf16[512,128]{1,0:T(8,128)(2,1)S(1)}, u32[]{:S(2)}, u32[]{:S(2)}) collective-permute-start(bf16[512,128]{1,0:T(8,128)(2,1)S(1)} %get-tuple-element.33), channel_id=1, source_target_pairs={{0,12},{2,14},{4,8},{6,10},{8,4},{10,6},{12,0},{14,2},{1,13},{3,15... | collective-permute-start | bytes 393224 | tf_op jit(solution)/shard_map/ppermute | solution.py:166
  13.5 1.1 %collective-permute-start.3 = (bf16[512,128]{1,0:T(8,128)(2,1)S(1)}, bf16[512,128]{1,0:T(8,128)(2,1)S(1)}, u32[]{:S(2)}, u32[]{:S(2)}) collective-permute-start(bf16[512,128]{1,0:T(8,128)(2,1)S(1)} %get-tuple-element.34), channel_id=1, source_target_pairs={{0,14},{2,12},{4,10},{6,8},{8,6},{10,4},{12,2},{14,0},{1,15},{3,13... | collective-permute-start | bytes 393224 | tf_op jit(solution)/shard_map/ppermute | solution.py:166
  14.7 9.0 %collective-permute-done.refs_1_ = bf16[512,128]{1,0:T(8,128)(2,1)S(1)} collective-permute-done((bf16[512,128]{1,0:T(8,128)(2,1)S(1)}, bf16[512,128]{1,0:T(8,128)(2,1)S(1)}, u32[]{:S(2)}, u32[]{:S(2)}) %collective-permute-start) | collective-permute-done | bytes 131104 | tf_op jit(solution)/shard_map/ppermute | solution.py:166
  23.7 0.9 %collective-permute-start.5 = (bf16[512,128]{1,0:T(8,128)(2,1)S(1)}, bf16[512,128]{1,0:T(8,128)(2,1)S(1)}, u32[]{:S(2)}, u32[]{:S(2)}) collective-permute-start(bf16[512,128]{1,0:T(8,128)(2,1)S(1)} %get-tuple-element.36), channel_id=1, source_target_pairs={{0,6},{2,4},{4,2},{6,0},{8,14},{10,12},{12,10},{14,8},{1,7},{3,5},... | collective-permute-start | bytes 393224 | tf_op jit(solution)/shard_map/ppermute | solution.py:166
  24.6 0.0 collective-permute-done.4.after.refs_5_
  24.6 2.4 %collective-permute-start.6 = (bf16[512,128]{1,0:T(8,128)(2,1)}, bf16[512,128]{1,0:T(8,128)(2,1)S(1)}, u32[]{:S(2)}, u32[]{:S(2)}) collective-permute-start(bf16[512,128]{1,0:T(8,128)(2,1)} %get-tuple-element.37), channel_id=1, source_target_pairs={{0,4},{2,6},{4,0},{6,2},{8,12},{10,14},{12,8},{14,10},{1,5},{3,7},... | collective-permute-start | bytes 393224 | tf_op jit(solution)/shard_map/ppermute | solution.py:166
  27.0 4.8 %shard_map.69 = (bf16[8,512,256]{2,1,0:T(8,128)(2,1)S(1)}, bf16[96,512,128]{2,1,0:T(8,128)(2,1)}) custom-call(bf16[512,128]{1,0:T(8,128)(2,1)S(1)} %collective-permute-done.4.after.refs_5_, bf16[128,4096]{1,0:T(8,128)(2,1)S(1)} %copy-done, bf16[128,4096]{1,0:T(8,128)(2,1)S(1)} %copy-done.1), custom_call_target="tpu_custom_call" | custom-call | bytes 16777216 | tf_op jit(solution)/shard_map/pallas_call | solution.py:201
  31.8 0.0 collective-permute-done.1.refs_2_
  31.8 0.0 collective-permute-done.2.refs_3_
  31.8 0.0 collective-permute-done.5.refs_6_
  31.8 0.0 collective-permute-done.6.refs_7_
  31.9 0.7 %shard_map.70.mine = f32[128,128]{1,0:T(8,128)S(1)} custom-call(s32[1]{0:T(128)} %bitcast.here, bf16[128,4096]{1,0:T(8,128)(2,1)S(1)} %copy-done, bf16[128,4096]{1,0:T(8,128)(2,1)S(1)} %copy-done.1, bf16[512,128]{1,0:T(8,128)(2,1)S(1)} %get-tuple-element.40.refs_0_, bf16[512,128]{1,0:T(8,128)(2,1)S(1)} %collective-permute-done.refs_1_, ...), custom_call_target="tpu_custom_call" | custom-call | flops 268435456 | bytes 3145728 | tf_op jit(solution)/shard_map/pallas_call | solution.py:214
  32.6 0.1 collective-permute-start.7
  32.6 1.2 %collective-permute-done.7.other = f32[128,128]{1,0:T(8,128)S(1)} collective-permute-done((f32[128,128]{1,0:T(8,128)S(1)}, f32[128,128]{1,0:T(8,128)S(1)}, u32[]{:S(2)}, u32[]{:S(2)}) %collective-permute-start.7) | collective-permute-done | bytes 65568 | tf_op jit(solution)/shard_map/ppermute | solution.py:172
  33.9 1.3 %shard_map.72 = (bf16[512,128]{1,0:T(8,128)(2,1)S(1)}, bf16[512,128]{1,0:T(8,128)(2,1)S(1)}, bf16[512,128]{1,0:T(8,128)(2,1)S(1)}, bf16[512,128]{1,0:T(8,128)(2,...) custom-call(s32[1]{0:T(128)} %bitcast.here, ...), custom_call_target="tpu_custom_call" | custom-call | flops 268435456 | bytes 3145728 | tf_op jit(solution)/shard_map/pallas_call | solution.py:224
  35.2 3.1 %collective-permute-start.8 = (bf16[512,128]{1,0:T(8,128)(2,1)S(1)}, bf16[512,128]{1,0:T(8,128)(2,1)S(1)}, u32[]{:S(2)}, u32[]{:S(2)}) collective-permute-start(bf16[512,128]{1,0:T(8,128)(2,1)S(1)} %get-tuple-element.50), channel_id=1, source_target_pairs={{0,8},{2,10},{4,12},{6,14},{8,0},{10,2},{12,4},{14,6},{1,9},{3,11}... | collective-permute-start | bytes 393224 | tf_op jit(solution)/shard_map/ppermute | solution.py:166
  38.4 0.3 collective-permute-start.9
  38.7 3.4 %collective-permute-start.10 = (bf16[512,128]{1,0:T(8,128)(2,1)S(1)}, bf16[512,128]{1,0:T(8,128)(2,1)S(1)}, u32[]{:S(2)}, u32[]{:S(2)}) collective-permute-start(bf16[512,128]{1,0:T(8,128)(2,1)S(1)} %get-tuple-element.52), channel_id=1, source_target_pairs={{0,12},{2,14},{4,8},{6,10},{8,4},{10,6},{12,0},{14,2},{1,13},{3,15... | collective-permute-start | bytes 393224 | tf_op jit(solution)/shard_map/ppermute | solution.py:166
  42.1 1.1 %collective-permute-start.11 = (bf16[512,128]{1,0:T(8,128)(2,1)S(1)}, bf16[512,128]{1,0:T(8,128)(2,1)S(1)}, u32[]{:S(2)}, u32[]{:S(2)}) collective-permute-start(bf16[512,128]{1,0:T(8,128)(2,1)S(1)} %get-tuple-element.53), channel_id=1, source_target_pairs={{0,14},{2,12},{4,10},{6,8},{8,6},{10,4},{12,2},{14,0},{1,15},{3,13... | collective-permute-start | bytes 393224 | tf_op jit(solution)/shard_map/ppermute | solution.py:166
  43.2 0.8 %collective-permute-start.12 = (bf16[512,128]{1,0:T(8,128)(2,1)S(1)}, bf16[512,128]{1,0:T(8,128)(2,1)S(1)}, u32[]{:S(2)}, u32[]{:S(2)}) collective-permute-start(bf16[512,128]{1,0:T(8,128)(2,1)S(1)} %get-tuple-element.54), channel_id=1, source_target_pairs={{0,2},{2,0},{4,6},{6,4},{8,10},{10,8},{12,14},{14,12},{1,3},{3,1},... | collective-permute-start | bytes 393224 | tf_op jit(solution)/shard_map/ppermute | solution.py:166
  44.0 9.9 %collective-permute-done.8.refs_1_ = bf16[512,128]{1,0:T(8,128)(2,1)S(1)} collective-permute-done((bf16[512,128]{1,0:T(8,128)(2,1)S(1)}, bf16[512,128]{1,0:T(8,128)(2,1)S(1)}, u32[]{:S(2)}, u32[]{:S(2)}) %collective-permute-start.8) | collective-permute-done | bytes 131104 | tf_op jit(solution)/shard_map/ppermute | solution.py:166
  53.9 0.2 collective-permute-start.13
  54.1 2.9 %collective-permute-done.9.refs_2_ = bf16[512,128]{1,0:T(8,128)(2,1)S(1)} collective-permute-done((bf16[512,128]{1,0:T(8,128)(2,1)S(1)}, bf16[512,128]{1,0:T(8,128)(2,1)S(1)}, u32[]{:S(2)}, u32[]{:S(2)}) %collective-permute-start.9) | collective-permute-done | bytes 131104 | tf_op jit(solution)/shard_map/ppermute | solution.py:166
  57.0 2.0 %shard_map.71 = bf16[128,4096]{1,0:T(8,128)(2,1)} custom-call(s32[1]{0:T(128)} %bitcast.here, s32[8]{0:T(128)S(1)} %bitcast.8, f32[128,128]{1,0:T(8,128)S(1)} %shard_map.70.mine, f32[128,128]{1,0:T(8,128)S(1)} %collective-permute-done.7.other, bf16[512,128]{1,0:T(8,128)(2,1)S(1)} %get-tuple-element.40.refs_0_, ...), custom_call_target="tpu_custom_call" | custom-call | flops 134217728 | bytes 2097152 | tf_op jit(solution)/shard_map/pallas_call | solution.py:234
  59.0 1.1 %collective-permute-done.13.refs_6_ = bf16[512,128]{1,0:T(8,128)(2,1)S(1)} collective-permute-done((bf16[512,128]{1,0:T(8,128)(2,1)S(1)}, bf16[512,128]{1,0:T(8,128)(2,1)S(1)}, u32[]{:S(2)}, u32[]{:S(2)}) %collective-permute-start.13) | collective-permute-done | bytes 131104 | tf_op jit(solution)/shard_map/ppermute | solution.py:166
  60.1 1.8 %collective-permute-done.14.refs_7_ = bf16[512,128]{1,0:T(8,128)(2,1)S(1)} collective-permute-done((bf16[512,128]{1,0:T(8,128)(2,1)S(1)}, bf16[512,128]{1,0:T(8,128)(2,1)S(1)}, u32[]{:S(2)}, u32[]{:S(2)}) %collective-permute-start.14) | collective-permute-done | bytes 131104 | tf_op jit(solution)/shard_map/ppermute | solution.py:166
  62.0 1.6 %shard_map.73 = bf16[96,512,128]{2,1,0:T(8,128)(2,1)} custom-call(s32[8]{0:T(128)S(1)} %bitcast.11, s32[1]{0:T(128)} %bitcast.here, s32[8]{0:T(128)S(1)} %bitcast.9, bf16[512,128]{1,0:T(8,128)(2,1)S(1)} %get-tuple-element.49.refs_0_, bf16[512,128]{1,0:T(8,128)(2,1)S(1)} %collective-permute-done.8.refs_1_, ...), custom_call_target="tpu_custom_call", output_to_operand_aliasing={{}: (11, {})} | custom-call | bytes 2097152 | tf_op jit(solution)/shard_map/pallas_call | solution.py:243
  (12 shorter events, 0.0 us)
Async XLA Ops:
  0.6 26.4 %copy-start.1 = (bf16[128,4096]{1,0:T(8,128)(2,1)S(1)}, bf16[128,4096]{1,0:T(8,128)(2,1)}, u32[]{:S(2)}) copy-start(bf16[128,4096]{1,0:T(8,128)(2,1)} %y.3) | copy-start | bytes 3145732
  0.6 26.4 %copy-start = (bf16[128,4096]{1,0:T(8,128)(2,1)S(1)}, bf16[128,4096]{1,0:T(8,128)(2,1)}, u32[]{:S(2)}) copy-start(bf16[128,4096]{1,0:T(8,128)(2,1)} %x.3) | copy-start | bytes 3145732
  0.7 33.2 %copy-start.2 = (s32[8,1]{0,1:T(1,128)S(1)}, s32[8,1]{0,1:T(1,128)}, u32[]{:S(2)}) copy-start(s32[8,1]{0,1:T(1,128)} %param.9) | copy-start | bytes 100
  0.7 0.8 %copy-start.3 = (s32[8,1]{0,1:T(1,128)S(1)}, s32[8,1]{0,1:T(1,128)}, u32[]{:S(2)}) copy-start(s32[8,1]{0,1:T(1,128)} %param.8) | copy-start | bytes 100
  4.0 19.7 %collective-permute-start = (bf16[512,128]{1,0:T(8,128)(2,1)S(1)}, bf16[512,128]{1,0:T(8,128)(2,1)S(1)}, u32[]{:S(2)}, u32[]{:S(2)}) collective-permute-start(bf16[512,128]{1,0:T(8,128)(2,1)S(1)} %get-tuple-element.31), channel_id=1, source_target_pairs={{0,8},{2,10},{4,12},{6,14},{8,0},{10,2},{12,4},{14,6},{1,9},{3,11}... | collective-permute-start | bytes 393224 | tf_op jit(solution)/shard_map/ppermute | solution.py:166
  8.1 16.5 %collective-permute-start.4 = (bf16[512,128]{1,0:T(8,128)(2,1)S(1)}, bf16[512,128]{1,0:T(8,128)(2,1)S(1)}, u32[]{:S(2)}, u32[]{:S(2)}) collective-permute-start(bf16[512,128]{1,0:T(8,128)(2,1)S(1)} %get-tuple-element.35), channel_id=1, source_target_pairs={{0,2},{2,0},{4,6},{6,4},{8,10},{10,8},{12,14},{14,12},{1,3},{3,1},... | collective-permute-start | bytes 393224 | tf_op jit(solution)/shard_map/ppermute | solution.py:166
  9.6 22.2 %collective-permute-start.1 = (bf16[512,128]{1,0:T(8,128)(2,1)S(1)}, bf16[512,128]{1,0:T(8,128)(2,1)S(1)}, u32[]{:S(2)}, u32[]{:S(2)}) collective-permute-start(bf16[512,128]{1,0:T(8,128)(2,1)S(1)} %get-tuple-element.32), channel_id=1, source_target_pairs={{0,10},{2,8},{4,14},{6,12},{8,2},{10,0},{12,6},{14,4},{1,11},{3,9}... | collective-permute-start | bytes 393224 | tf_op jit(solution)/shard_map/ppermute | solution.py:166
  9.7 22.1 %collective-permute-start.2 = (bf16[512,128]{1,0:T(8,128)(2,1)S(1)}, bf16[512,128]{1,0:T(8,128)(2,1)S(1)}, u32[]{:S(2)}, u32[]{:S(2)}) collective-permute-start(bf16[512,128]{1,0:T(8,128)(2,1)S(1)} %get-tuple-element.33), channel_id=1, source_target_pairs={{0,12},{2,14},{4,8},{6,10},{8,4},{10,6},{12,0},{14,2},{1,13},{3,15... | collective-permute-start | bytes 393224 | tf_op jit(solution)/shard_map/ppermute | solution.py:166
  13.5 18.3 %collective-permute-start.3 = (bf16[512,128]{1,0:T(8,128)(2,1)S(1)}, bf16[512,128]{1,0:T(8,128)(2,1)S(1)}, u32[]{:S(2)}, u32[]{:S(2)}) collective-permute-start(bf16[512,128]{1,0:T(8,128)(2,1)S(1)} %get-tuple-element.34), channel_id=1, source_target_pairs={{0,14},{2,12},{4,10},{6,8},{8,6},{10,4},{12,2},{14,0},{1,15},{3,13... | collective-permute-start | bytes 393224 | tf_op jit(solution)/shard_map/ppermute | solution.py:166
  23.7 8.1 %collective-permute-start.5 = (bf16[512,128]{1,0:T(8,128)(2,1)S(1)}, bf16[512,128]{1,0:T(8,128)(2,1)S(1)}, u32[]{:S(2)}, u32[]{:S(2)}) collective-permute-start(bf16[512,128]{1,0:T(8,128)(2,1)S(1)} %get-tuple-element.36), channel_id=1, source_target_pairs={{0,6},{2,4},{4,2},{6,0},{8,14},{10,12},{12,10},{14,8},{1,7},{3,5},... | collective-permute-start | bytes 393224 | tf_op jit(solution)/shard_map/ppermute | solution.py:166
  24.6 7.2 %collective-permute-start.6 = (bf16[512,128]{1,0:T(8,128)(2,1)}, bf16[512,128]{1,0:T(8,128)(2,1)S(1)}, u32[]{:S(2)}, u32[]{:S(2)}) collective-permute-start(bf16[512,128]{1,0:T(8,128)(2,1)} %get-tuple-element.37), channel_id=1, source_target_pairs={{0,4},{2,6},{4,0},{6,2},{8,12},{10,14},{12,8},{14,10},{1,5},{3,7},... | collective-permute-start | bytes 393224 | tf_op jit(solution)/shard_map/ppermute | solution.py:166
  32.6 1.3 %collective-permute-start.7 = (f32[128,128]{1,0:T(8,128)S(1)}, f32[128,128]{1,0:T(8,128)S(1)}, u32[]{:S(2)}, u32[]{:S(2)}) collective-permute-start(f32[128,128]{1,0:T(8,128)S(1)} %shard_map.70.mine), channel_id=1, source_target_pairs={{0,1},{1,0},{2,3},{3,2},{4,5},{5,4},{6,7},{7,6},{8,9},{9,8},{10,11... | collective-permute-start | bytes 196616 | tf_op jit(solution)/shard_map/ppermute | solution.py:172
  35.2 18.7 %collective-permute-start.8 = (bf16[512,128]{1,0:T(8,128)(2,1)S(1)}, bf16[512,128]{1,0:T(8,128)(2,1)S(1)}, u32[]{:S(2)}, u32[]{:S(2)}) collective-permute-start(bf16[512,128]{1,0:T(8,128)(2,1)S(1)} %get-tuple-element.50), channel_id=1, source_target_pairs={{0,8},{2,10},{4,12},{6,14},{8,0},{10,2},{12,4},{14,6},{1,9},{3,11}... | collective-permute-start | bytes 393224 | tf_op jit(solution)/shard_map/ppermute | solution.py:166
  38.4 18.7 %collective-permute-start.9 = (bf16[512,128]{1,0:T(8,128)(2,1)S(1)}, bf16[512,128]{1,0:T(8,128)(2,1)S(1)}, u32[]{:S(2)}, u32[]{:S(2)}) collective-permute-start(bf16[512,128]{1,0:T(8,128)(2,1)S(1)} %get-tuple-element.51), channel_id=1, source_target_pairs={{0,10},{2,8},{4,14},{6,12},{8,2},{10,0},{12,6},{14,4},{1,11},{3,9}... | collective-permute-start | bytes 393224 | tf_op jit(solution)/shard_map/ppermute | solution.py:166
  38.7 20.3 %collective-permute-start.10 = (bf16[512,128]{1,0:T(8,128)(2,1)S(1)}, bf16[512,128]{1,0:T(8,128)(2,1)S(1)}, u32[]{:S(2)}, u32[]{:S(2)}) collective-permute-start(bf16[512,128]{1,0:T(8,128)(2,1)S(1)} %get-tuple-element.52), channel_id=1, source_target_pairs={{0,12},{2,14},{4,8},{6,10},{8,4},{10,6},{12,0},{14,2},{1,13},{3,15... | collective-permute-start | bytes 393224 | tf_op jit(solution)/shard_map/ppermute | solution.py:166
  42.1 16.9 %collective-permute-start.11 = (bf16[512,128]{1,0:T(8,128)(2,1)S(1)}, bf16[512,128]{1,0:T(8,128)(2,1)S(1)}, u32[]{:S(2)}, u32[]{:S(2)}) collective-permute-start(bf16[512,128]{1,0:T(8,128)(2,1)S(1)} %get-tuple-element.53), channel_id=1, source_target_pairs={{0,14},{2,12},{4,10},{6,8},{8,6},{10,4},{12,2},{14,0},{1,15},{3,13... | collective-permute-start | bytes 393224 | tf_op jit(solution)/shard_map/ppermute | solution.py:166
  43.2 15.8 %collective-permute-start.12 = (bf16[512,128]{1,0:T(8,128)(2,1)S(1)}, bf16[512,128]{1,0:T(8,128)(2,1)S(1)}, u32[]{:S(2)}, u32[]{:S(2)}) collective-permute-start(bf16[512,128]{1,0:T(8,128)(2,1)S(1)} %get-tuple-element.54), channel_id=1, source_target_pairs={{0,2},{2,0},{4,6},{6,4},{8,10},{10,8},{12,14},{14,12},{1,3},{3,1},... | collective-permute-start | bytes 393224 | tf_op jit(solution)/shard_map/ppermute | solution.py:166
  53.9 6.3 %collective-permute-start.13 = (bf16[512,128]{1,0:T(8,128)(2,1)S(1)}, bf16[512,128]{1,0:T(8,128)(2,1)S(1)}, u32[]{:S(2)}, u32[]{:S(2)}) collective-permute-start(bf16[512,128]{1,0:T(8,128)(2,1)S(1)} %get-tuple-element.55), channel_id=1, source_target_pairs={{0,6},{2,4},{4,2},{6,0},{8,14},{10,12},{12,10},{14,8},{1,7},{3,5},... | collective-permute-start | bytes 393224 | tf_op jit(solution)/shard_map/ppermute | solution.py:166
  57.0 5.0 %collective-permute-start.14 = (bf16[512,128]{1,0:T(8,128)(2,1)S(1)}, bf16[512,128]{1,0:T(8,128)(2,1)S(1)}, u32[]{:S(2)}, u32[]{:S(2)}) collective-permute-start(bf16[512,128]{1,0:T(8,128)(2,1)S(1)} %get-tuple-element.56), channel_id=1, source_target_pairs={{0,4},{2,6},{4,0},{6,2},{8,12},{10,14},{12,8},{14,10},{1,5},{3,7},... | collective-permute-start | bytes 393224 | tf_op jit(solution)/shard_map/ppermute | solution.py:166

commit v6 on v5

v6 whole, which is shorter than its diff:
```python
import functools

import jax
import jax.numpy as jnp
from jax import lax
from jax.experimental import pallas as pl
from jax.experimental.pallas import tpu as pltpu
from jax.sharding import PartitionSpec as P

adapter_alpha = 128.0

in_vmem = pl.BlockSpec(memory_space=pltpu.VMEM)
in_smem = pl.BlockSpec(memory_space=pltpu.SMEM)
in_hbm = pl.BlockSpec(memory_space=pltpu.HBM)


def low_lanes(rows, width):
    return lax.broadcasted_iota(jnp.int32, (rows, width), 1) < width // 2


def call(kernel, out_shape, in_specs, out_specs, scratch=(), flops=0, moved=0, aliases=None, vmem=40):
    return pl.pallas_call(
        kernel,
        out_shape=out_shape,
        in_specs=in_specs,
        out_specs=out_specs,
        scratch_shapes=list(scratch),
        input_output_aliases=aliases or {},
        compiler_params=pltpu.CompilerParams(vmem_limit_bytes=vmem * 1024 * 1024),
        cost_estimate=pl.CostEstimate(flops=flops, bytes_accessed=moved, transcendentals=0),
    )


def swap_halves(value):
    return pltpu.roll(value, value.shape[-1] // 2, 1)


def gather_kernel(plan, ids, here, table, *refs):
    split, whole, near = plan
    parts = len(split)
    up, rest = refs[:parts], refs[parts:]
    straight, rest = rest[: len(whole)], rest[len(whole) :]
    close, rest = rest[0], rest[1:]
    down, (held, sems) = rest[:parts], rest[parts:]
    me = here[0]
    targets = [(me ^ k, held.at[n]) for n, k in enumerate(split)]
    targets += [(me ^ k, straight[n]) for n, k in enumerate(whole)]
    targets += [((me & -near) | n, close.at[n]) for n in range(near)]
    copies = [
        pltpu.make_async_copy(table.at[ids[block]], target, sems.at[n])
        for n, (block, target) in enumerate(targets)
    ]
    for copy in copies:
        copy.start()
    half = held.shape[1] // 2
    low = low_lanes(half, held.shape[2])
    for n in range(parts):
        copies[n].wait()
        first = held[n, :half].astype(jnp.float32)
        second = held[n, half:].astype(jnp.float32)
        up[n][...] = jnp.where(low, swap_halves(first), second).astype(jnp.bfloat16)
        down[n][...] = jnp.where(low, first, swap_halves(second)).astype(jnp.bfloat16)
    for copy in copies[parts:]:
        copy.wait()


def prep_kernel(rows, after, x, y, turned, blank, zeros, sem):
    zeros[...] = jnp.zeros_like(zeros)
    step = zeros.shape[0]
    copies = [
        pltpu.make_async_copy(zeros, blank.at[pl.ds(s, step)], sem.at[s // step])
        for s in range(0, blank.shape[0], step)
    ]
    for copy in copies:
        copy.start()
    tokens = x.shape[0]

    @pl.loop(0, x.shape[1] // rows)
    def _(owner):
        columns = pl.ds(pl.multiple_of(owner * rows, rows), rows)
        turned[owner, :, pl.ds(0, tokens)] = x[:, columns].T
        turned[owner, :, pl.ds(tokens, tokens)] = y[:, columns].T

    for copy in copies:
        copy.wait()


def halves_product(values, packed, owner):
    half = packed.shape[0]
    first = pl.ds(pl.multiple_of(owner * 2 * half, half), half)
    second = pl.ds(pl.multiple_of(owner * 2 * half + half, half), half)
    one = jnp.dot(values[:, first], packed[...], preferred_element_type=jnp.float32)
    two = jnp.dot(values[:, second], packed[...], preferred_element_type=jnp.float32)
    return one, two


def rank_kernel(plan, here, x, y, *refs):
    split, whole, near = plan
    up, straight = refs[: len(split)], refs[len(split) : -3]
    close, dhidden, hidden = refs[-3:]
    _, rows, width = close.shape
    tokens = x.shape[0]
    me = here[0]
    x_rank = jnp.zeros((tokens, width), jnp.float32)
    y_rank = jnp.zeros((tokens, width), jnp.float32)
    y_first = jnp.zeros((tokens, width), jnp.float32)
    pairs = [((me & -near) | n, close.at[n]) for n in range(near)]
    pairs += [(me ^ k, straight[n]) for n, k in enumerate(whole)]
    for owner, pair in pairs:
        columns = pl.ds(pl.multiple_of(owner * rows, rows), rows)
        x_rank += jnp.dot(x[:, columns], pair[...], preferred_element_type=jnp.float32)
        y_rank += jnp.dot(y[:, columns], pair[...], preferred_element_type=jnp.float32)
    for n, k in enumerate(split):
        first, second = halves_product(y, up[n], me ^ k)
        y_first += first
        y_rank += second
    y_rank += swap_halves(y_first)
    half = tokens // 2
    low = low_lanes(half, width)
    dhidden[...] = jnp.where(low, swap_halves(y_rank[:half]), y_rank[half:])
    hidden[...] = jnp.where(low, x_rank[:half], swap_halves(x_rank[half:]))


def rank_rest_kernel(plan, here, x, partial, *refs):
    split, _, _ = plan
    down, out = refs[:-1], refs[-1]
    tokens, width = x.shape[0], partial.shape[1]
    x_first = jnp.zeros((tokens, width), jnp.float32)
    x_second = jnp.zeros((tokens, width), jnp.float32)
    for n, k in enumerate(split):
        first, second = halves_product(x, down[n], here[0] ^ k)
        x_first += first
        x_second += second
    x_rank = x_first + swap_halves(x_second)
    half = tokens // 2
    low = low_lanes(half, width)
    out[...] = partial[...] + jnp.where(low, x_rank[:half], swap_halves(x_rank[half:]))


def rounded(mine, other, length, scale):
    total = scale * (mine[...] + other[...])
    swapped = swap_halves(total)
    low = low_lanes(*total.shape)
    live = lax.broadcasted_iota(jnp.int32, (2 * total.shape[0], total.shape[1]), 0) < length
    left = [jnp.where(low, total, 0.0), jnp.where(low, swapped, 0.0)]
    right = [jnp.where(low, 0.0, swapped), jnp.where(low, 0.0, total)]
    return [jnp.where(live, jnp.concatenate(v, axis=0), 0.0).astype(jnp.bfloat16) for v in (left, right)]


def packed_piece(turned, owner, lanes, left, right):
    half = turned.shape[1] // 2
    first = jnp.dot(turned[owner, :half, lanes], left, preferred_element_type=jnp.float32)
    second = jnp.dot(turned[owner, half:, lanes], right, preferred_element_type=jnp.float32)
    return first + second


def down_piece_kernel(plan, scale, here, lengths, mine, other, turned, *out):
    split, _, _ = plan
    me = here[0]
    left, right = rounded(mine, other, lengths[me], scale)
    tokens = left.shape[0]
    for n, k in enumerate(split):
        out[n][...] = packed_piece(turned, me ^ k, slice(0, tokens), left, right).astype(jnp.bfloat16)


def piece_kernel(plan, scale, here, lengths, d_mine, d_other, mine, other, turned, *refs):
    split, whole, near = plan
    up, straight, close = refs[: len(split)], refs[len(split) : -1], refs[-1]
    me = here[0]
    dhidden, _ = rounded(d_mine, d_other, lengths[me], scale)
    left, right = rounded(mine, other, lengths[me], 1.0)
    tokens = left.shape[0]
    ranks = jnp.concatenate([dhidden, right], axis=0)

    def rows_for(owner):
        piece = jnp.dot(turned[owner], ranks, preferred_element_type=jnp.float32)
        return jnp.where(low_lanes(*piece.shape), piece, scale * piece).astype(jnp.bfloat16)

    for n, k in enumerate(split):
        piece = packed_piece(turned, me ^ k, slice(tokens, 2 * tokens), left, right)
        up[n][...] = (scale * piece).astype(jnp.bfloat16)
    for n, k in enumerate(whole):
        straight[n][...] = rows_for(me ^ k)
    for n in range(near):
        close[n] = rows_for((me & -near) | n)


def input_kernel(plan, scale, here, lengths, mine, other, *refs):
    split, whole, near = plan
    down, straight = refs[: len(split)], refs[len(split) : -2]
    close, out = refs[-2:]
    rows = close.shape[1]
    half = rows // 2
    me = here[0]
    left, right = rounded(mine, other, lengths[me], scale)

    def product(ranks, columns):
        value = lax.dot_general(
            ranks, columns, (((1,), (1,)), ((), ())), preferred_element_type=jnp.float32
        )
        return value.astype(jnp.bfloat16)

    pairs = [((me & -near) | n, close.at[n]) for n in range(near)]
    pairs += [(me ^ k, straight[n]) for n, k in enumerate(whole)]
    for owner, pair in pairs:
        out[:, pl.ds(pl.multiple_of(owner * rows, rows), rows)] = product(left, pair[...])
    for n, k in enumerate(split):
        start = (me ^ k) * rows
        out[:, pl.ds(pl.multiple_of(start, half), half)] = product(left, down[n][...])
        out[:, pl.ds(pl.multiple_of(start + half, half), half)] = product(right, down[n][...])


def merge_kernel(plan, ids, here, lengths, *refs):
    split, whole, near = plan
    parts = len(split)
    down, up, straight = refs[:parts], refs[parts : 2 * parts], refs[2 * parts : 2 * parts + len(whole)]
    close, _, out, total, held, sems = refs[2 * parts + len(whole) :]
    me = here[0]
    rows, width = total.shape
    half = rows // 2
    low = low_lanes(half, width)

    def unpacked(n):
        d_down, d_up = down[n][...].astype(jnp.float32), up[n][...].astype(jnp.float32)
        first = jnp.where(low, d_down, swap_halves(d_up))
        second = jnp.where(low, swap_halves(d_down), d_up)
        return jnp.concatenate([first, second], axis=0)

    def read(ref):
        return lambda: ref[...].astype(jnp.float32)

    pieces = [((me & -near) | n, read(close.at[n])) for n in range(near)]
    pieces += [(me ^ k, read(straight[n])) for n, k in enumerate(whole)]
    pieces += [(me ^ k, functools.partial(unpacked, n)) for n, k in enumerate(split)]
    owners = len(pieces)
    adapters = [ids[block] for block, _ in pieces]
    counts = [lengths[block] for block, _ in pieces]
    copies, firsts = [], []
    for k, (_, value) in enumerate(pieces):
        copies.append(pltpu.make_async_copy(held.at[k], out.at[adapters[k]], sems.at[k]))
        same = [adapters[other] == adapters[k] for other in range(owners)]
        earlier = functools.reduce(jnp.logical_or, same[:k], jnp.bool_(False))
        later = functools.reduce(jnp.logical_or, same[k + 1 :], jnp.bool_(False))
        firsts.append(jnp.logical_not(earlier))

        def store(sum_of, count):
            denom = jnp.maximum(count.astype(jnp.float32), 1.0)
            part = 1.0 / jnp.full((1, width), denom)
            held[k] = (sum_of * part).astype(jnp.bfloat16)
            copies[k].start()

        @pl.when(firsts[k] & jnp.logical_not(later))
        def _():
            store(value(), counts[k])

        @pl.when(firsts[k] & later)
        def _():
            total[...] = value()
            count = counts[k]
            for other in range(k + 1, owners):
                count += jnp.where(same[other], counts[other], 0)

                @pl.when(same[other])
                def _():
                    total[...] += pieces[other][1]()

            store(total[...], count)

    for k in range(owners):
        pl.when(firsts[k])(copies[k].wait)


def to_partner(pieces, partners, owners):
    return [
        lax.ppermute(piece, "dp", [(i, i ^ k) for i in range(owners)])
        for k, piece in zip(partners, pieces)
    ]


def among_near(pieces, owners):
    near = pieces.shape[0]
    groups = [list(range(start, start + near)) for start in range(0, owners, near)]
    return lax.all_to_all(
        pieces, "dp", split_axis=0, concat_axis=0, tiled=True, axis_index_groups=groups
    )


def after(value, *others):
    return lax.optimization_barrier((value, *others))[0]


def across_cores(value):
    cores = lax.axis_size("tensor")
    return lax.ppermute(value, "tensor", [(i, i ^ 1) for i in range(cores)])


def with_kernels(activations, cotangent, adapter_weight_pair, adapter_of_block, block_live_length):
    owners = lax.axis_size("dp")
    near = owners // 2
    far = list(range(near, owners))
    plan = split, whole, _ = tuple(far[-2:]), tuple(far[:-2]), near
    here = lax.axis_index("dp").astype(jnp.int32).reshape(1)
    ids, lengths = adapter_of_block[:, 0], block_live_length[:, 0]
    count, _, rows, width = adapter_weight_pair.shape
    table = adapter_weight_pair.reshape(count, rows, width)
    tokens, features = activations.shape
    scale = adapter_alpha / (width // 2)
    bf16, f32 = jnp.bfloat16, jnp.float32
    packed = jax.ShapeDtypeStruct((rows // 2, width), bf16)
    straight = jax.ShapeDtypeStruct((rows, width), bf16)
    stacked = jax.ShapeDtypeStruct((near, rows, width), bf16)
    rank_space = jax.ShapeDtypeStruct((tokens // 2, width), f32)
    parts, wholes = len(split), len(whole)
    pair_bytes = owners * rows * width * 2
    token_bytes = tokens * features * 2

    sent = call(
        functools.partial(gather_kernel, plan),
        [packed] * parts + [straight] * wholes + [stacked] + [packed] * parts,
        [in_smem, in_smem, in_hbm],
        [in_vmem] * (2 * parts + wholes + 1),
        [pltpu.VMEM((parts, rows, width), bf16), pltpu.SemaphoreType.DMA((owners,))],
        moved=2 * pair_bytes,
        vmem=53,
    )(ids, here, table)
    ups = to_partner(sent[:parts], split, owners)
    pairs = to_partner(sent[parts : parts + wholes], whole, owners)
    close = among_near(sent[parts + wholes], owners)
    downs = to_partner(sent[parts + wholes + 1 :], split, owners)

    step = 8
    turned, blank = call(
        functools.partial(prep_kernel, rows),
        [
            jax.ShapeDtypeStruct((owners, rows, 2 * tokens), bf16),
            jax.ShapeDtypeStruct(table.shape, bf16),
        ],
        [in_hbm, in_vmem, in_vmem],
        [in_vmem, in_hbm],
        [pltpu.VMEM((step, rows, width), bf16), pltpu.SemaphoreType.DMA((count // step,))],
        moved=4 * token_bytes + 2 * count * rows * width,
    )(sent[0], activations, cotangent)
    *ups, turned, blank = lax.optimization_barrier((*ups, turned, blank))

    dhidden, partial = call(
        functools.partial(rank_kernel, plan),
        [rank_space, rank_space],
        [in_smem] + [in_vmem] * (3 + parts + wholes),
        [in_vmem, in_vmem],
        flops=4 * tokens * features * width,
        moved=2 * token_bytes + pair_bytes,
    )(here, activations, cotangent, *ups, *pairs, close)
    dhidden_other = across_cores(dhidden)
    down_pieces = call(
        functools.partial(down_piece_kernel, plan, scale),
        [packed] * parts,
        [in_smem] * 2 + [in_vmem] * 3,
        [in_vmem] * parts,
        flops=parts * 2 * tokens * rows * width,
        moved=pair_bytes,
    )(here, lengths, dhidden, dhidden_other, turned)
    d_downs = to_partner(down_pieces, split, owners)

    hidden = call(
        functools.partial(rank_rest_kernel, plan),
        rank_space,
        [in_smem] + [in_vmem] * (2 + parts),
        in_vmem,
        flops=parts * 2 * tokens * rows * width,
        moved=pair_bytes,
    )(here, activations, after(partial, *down_pieces), *downs)
    hidden_other = across_cores(hidden)
    pieces = call(
        functools.partial(piece_kernel, plan, scale),
        [packed] * parts + [straight] * wholes + [stacked],
        [in_smem] * 2 + [in_vmem] * 5,
        [in_vmem] * (parts + wholes + 1),
        flops=4 * tokens * features * width,
        moved=2 * token_bytes + pair_bytes,
    )(here, lengths, dhidden, dhidden_other, hidden, hidden_other, turned)
    d_ups = to_partner(pieces[:parts], split, owners)
    d_pairs = to_partner(pieces[parts : parts + wholes], whole, owners)
    d_close = among_near(pieces[-1], owners)

    grad_input = call(
        functools.partial(input_kernel, plan, scale),
        jax.ShapeDtypeStruct((tokens, features), bf16),
        [in_smem] * 2 + [in_vmem] * (3 + parts + wholes),
        in_vmem,
        flops=2 * tokens * features * width,
        moved=token_bytes + pair_bytes,
    )(here, lengths, after(dhidden, *pieces), dhidden_other, *downs, *pairs, close)

    gradient = call(
        functools.partial(merge_kernel, plan),
        jax.ShapeDtypeStruct(table.shape, bf16),
        [in_smem] * 3 + [in_vmem] * (2 * parts + wholes + 1) + [in_hbm],
        in_hbm,
        [
            pltpu.VMEM((rows, width), f32),
            pltpu.VMEM((owners, rows, width), bf16),
            pltpu.SemaphoreType.DMA((owners,)),
        ],
        moved=2 * pair_bytes,
        aliases={4 + 2 * parts + wholes: 0},
    )(ids, here, lengths, *d_downs, *d_ups, *d_pairs, d_close, blank)
    return grad_input, gradient[:, None]


def without_kernels(activations, cotangent, adapter_weight_pair, adapter_of_block, block_live_length):
    owners = lax.axis_size("dp")
    here = lax.axis_index("dp")
    count, _, rows, width = adapter_weight_pair.shape
    rank = width // 2
    scale = adapter_alpha / rank
    adapters = adapter_of_block[:, 0]
    lengths = block_live_length[:, 0]
    keep = (jnp.arange(activations.shape[0], dtype=jnp.int32) < lengths[here])[:, None]
    inputs = jnp.where(keep, activations, jnp.zeros_like(activations))
    grads_out = jnp.where(keep, cotangent, jnp.zeros_like(cotangent))
    fetched = lax.all_to_all(
        adapter_weight_pair[:, 0][adapters], "dp", split_axis=0, concat_axis=0, tiled=True
    )
    pair = fetched.reshape(-1, width)
    down, upward = pair[:, :rank], pair[:, rank:]
    f32 = jnp.float32
    hidden_part = jnp.dot(inputs, down, preferred_element_type=f32)
    dhidden_part = scale * jnp.dot(grads_out, upward, preferred_element_type=f32)
    hidden, dhidden = lax.psum((hidden_part, dhidden_part), "tensor")
    hidden16, dhidden16 = hidden.astype(jnp.bfloat16), dhidden.astype(jnp.bfloat16)
    d_down = jnp.dot(inputs.T, dhidden16, preferred_element_type=f32)
    d_up = scale * jnp.dot(grads_out.T, hidden16, preferred_element_type=f32)
    sent = jnp.concatenate([d_down, d_up], axis=1).astype(jnp.bfloat16).reshape(owners, rows, width)
    received = lax.all_to_all(sent, "dp", split_axis=0, concat_axis=0, tiled=True).astype(f32)
    same = adapters[:, None] == adapters[None, :]
    total = jnp.sum(jnp.where(same, lengths[None, :], 0), axis=1).astype(f32)
    summed = jax.ops.segment_sum(received, adapters, num_segments=count)
    denom = jnp.ones((count,), f32).at[adapters].set(jnp.maximum(total, 1.0))
    gradient = (summed / denom[:, None, None]).astype(jnp.bfloat16)
    grad_input = jnp.dot(dhidden16, down.T, preferred_element_type=f32).astype(jnp.bfloat16)
    return grad_input, gradient[:, None]


def solution(mesh):
    owners, cores = mesh.shape["dp"], mesh.shape["tensor"]

    def on_device(activations, cotangent, adapter_weight_pair, *rest):
        rows = adapter_weight_pair.shape[2]
        fits = owners & (owners - 1) == 0 and owners >= 4 and cores == 2 and rows % 256 == 0
        body = with_kernels if fits else without_kernels
        return body(activations, cotangent, adapter_weight_pair, *rest)

    in_specs = (
        P(("group", "dp"), "tensor"),
        P(("group", "dp"), "tensor"),
        P(None, "tensor", "dp", None),
        P("group", None),
        P("group", None),
    )
    out_specs = (P(("group", "dp"), "tensor"), P("group", "tensor", "dp", None))
    return jax.shard_map(
        on_device, mesh=mesh, in_specs=in_specs, out_specs=out_specs, check_vma=False
    )
```

time: 63.8 us -> 87.3 us (1.37); the launches traced: 63.6 us -> 85.9 us
  starting transfers between devices: 23 us -> 40.8 us
  waiting for transfers between devices: 26.1 us -> 19.2 us
  local copies, waits for them, and re-layouts: 0.8 us -> 7.36 us
  Pallas kernels: 13 us -> 17.8 us
    all_to_all x0 -> x2, starting transfers between devices: none -> 15.5 us  [among_near(): lax.all_to_all(pieces, 'dp', split_axis=0, concat_axis=0, tiled=True, axi...]
    ppermute x14 -> x12, waiting for transfers between devices: 24.8 us -> 17 us  [to_partner(): lax.ppermute(piece, 'dp', [(i, i ^ k) for i in range(owners)])]
    unnamed x8 -> x28, local copies, waits for them, and re-layouts: 0.8 us -> 7.36 us
    pallas_call x5 -> x7, Pallas kernels: 8.21 us -> 13 us  [the longest x1 2.8 us: with_kernels(): call(functools.partial(gather_kernel, plan), [packed] * parts + [straight...]
    ppermute x14 -> x12, starting transfers between devices: 22.9 us -> 25 us  [to_partner(): lax.ppermute(piece, 'dp', [(i, i ^ k) for i in range(owners)])]
    ppermute x1 -> x2, waiting for transfers between devices: 1.24 us -> 2.23 us  [across_cores(): return lax.ppermute(value, 'tensor', [(i, i ^ 1) for i in range(cores)])]
  transfers between devices with their start and end apart: 15 -> 16, of which waited for: 6 -> 8; matrix products, arithmetic and copies ran while one was open for 0% -> 0% of each run, Pallas kernels for 11% -> 12%
where the time goes in v6:
time: 87.3 us; the launch traced here: 85.9 us
  starting transfers between devices  40.8 us (47%)
  waiting for transfers between devices  19.2 us (22%)
  Pallas kernels  17.8 us (20%)
  local copies, waits for them, and re-layouts  7.36 us (8%)
    ppermute x12, starting transfers between devices, to_partner(): lax.ppermute(piece, 'dp', [(i, i ^ k) for i in range(owners)])  25 us
    ppermute x12, waiting for transfers between devices, to_partner(): lax.ppermute(piece, 'dp', [(i, i ^ k) for i in range(owners)])  17 us
    all_to_all x2, starting transfers between devices, among_near(): lax.all_to_all(pieces, 'dp', split_axis=0, concat_axis=0, tiled=True, axi...  15.5 us
    unnamed x28, local copies, waits for them, and re-layouts  7.36 us
    pallas_call x1, Pallas kernels, with_kernels(): call(functools.partial(prep_kernel, rows), [jax.ShapeDtypeStruct((owners,...  4.8 us
    pallas_call x1, Pallas kernels, with_kernels(): call(functools.partial(gather_kernel, plan), [packed] * parts + [straight...  2.8 us
    pallas_call x1, Pallas kernels, with_kernels(): call(functools.partial(input_kernel, plan, scale), jax.ShapeDtypeStruct((...  2.54 us
    ppermute x2, waiting for transfers between devices, across_cores(): return lax.ppermute(value, 'tensor', [(i, i ^ 1) for i in range(cores)])  2.23 us
  transfers between devices with their start and end apart: 16, of which 8 were waited for; matrix products, arithmetic and copies ran while one was open for 0% of the time, Pallas kernels for 12%

profile of v6, /device:TPU:0, one launch (start us, length us, event | category | flops | bytes accessed | tf_op | source)
XLA Modules:
  0.0 85.9 jit_solution(8615392966021317833)
XLA Ops:
  0.7 0.7 copy-done.8
  1.4 2.8 %shard_map.68 = (bf16[256,128]{1,0:T(8,128)(2,1)S(1)}, bf16[256,128]{1,0:T(8,128)(2,1)S(1)}, bf16[512,128]{1,0:T(8,128)(2,1)}, bf16[512,128]{1,0:T(8,128)(2,1)},...) custom-call(s32[8]{0:T(128)S(1)} %bitcast.11, s32[1]{0:T(128)} %bitcast.here, ...), custom_call_target="tpu_custom_call" | custom-call | bytes 2097152 | tf_op jit(solution)/shard_map/pallas_call | solution.py:317
  4.2 5.2 %all-to-all-start = ((bf16[4,512,128]{2,1,0:T(8,128)(2,1)}), bf16[4,512,128]{2,1,0:T(8,128)(2,1)}, u32[]{:S(2)}, u32[]{:S(2)}) async-start(bf16[4,512,128]{2,1,0:T(8,128)(2,1)} %get-tuple-element.34), calls=%async_computation | async-start | bytes 1048576 | tf_op jit(solution)/shard_map/all_to_all | solution.py:283
  9.4 3.0 %collective-permute-start.2 = (bf16[512,128]{1,0:T(8,128)(2,1)}, bf16[512,128]{1,0:T(8,128)(2,1)S(1)}, u32[]{:S(2)}, u32[]{:S(2)}) collective-permute-start(bf16[512,128]{1,0:T(8,128)(2,1)} %get-tuple-element.32), channel_id=1, source_target_pairs={{0,8},{2,10},{4,12},{6,14},{8,0},{10,2},{12,4},{14,6},{1,9},{3,11}... | collective-permute-start | bytes 393224 | tf_op jit(solution)/shard_map/ppermute | solution.py:275
  12.5 1.4 %collective-permute-start.3 = (bf16[512,128]{1,0:T(8,128)(2,1)}, bf16[512,128]{1,0:T(8,128)(2,1)S(1)}, u32[]{:S(2)}, u32[]{:S(2)}) collective-permute-start(bf16[512,128]{1,0:T(8,128)(2,1)} %get-tuple-element.33), channel_id=1, source_target_pairs={{0,10},{2,8},{4,14},{6,12},{8,2},{10,0},{12,6},{14,4},{1,11},{3,9}... | collective-permute-start | bytes 393224 | tf_op jit(solution)/shard_map/ppermute | solution.py:275
  13.8 3.8 %collective-permute-start.1 = (bf16[256,128]{1,0:T(8,128)(2,1)S(1)}, bf16[256,128]{1,0:T(8,128)(2,1)S(1)}, u32[]{:S(2)}, u32[]{:S(2)}) collective-permute-start(bf16[256,128]{1,0:T(8,128)(2,1)S(1)} %get-tuple-element.27), channel_id=1, source_target_pairs={{0,14},{2,12},{4,10},{6,8},{8,6},{10,4},{12,2},{14,0},{1,15},{3,13... | collective-permute-start | bytes 196616 | tf_op jit(solution)/shard_map/ppermute | solution.py:275
  17.6 3.8 %collective-permute-start.5 = (bf16[256,128]{1,0:T(8,128)(2,1)}, bf16[256,128]{1,0:T(8,128)(2,1)S(1)}, u32[]{:S(2)}, u32[]{:S(2)}) collective-permute-start(bf16[256,128]{1,0:T(8,128)(2,1)} %get-tuple-element.41), channel_id=1, source_target_pairs={{0,12},{2,14},{4,8},{6,10},{8,4},{10,6},{12,0},{14,2},{1,13},{3,15... | collective-permute-start | bytes 196616 | tf_op jit(solution)/shard_map/ppermute | solution.py:275
  21.5 7.8 %collective-permute-done.1.refs_1_ = bf16[256,128]{1,0:T(8,128)(2,1)S(1)} collective-permute-done((bf16[256,128]{1,0:T(8,128)(2,1)S(1)}, bf16[256,128]{1,0:T(8,128)(2,1)S(1)}, u32[]{:S(2)}, u32[]{:S(2)}) %collective-permute-start.1) | collective-permute-done | bytes 65568 | tf_op jit(solution)/shard_map/ppermute | solution.py:275
  29.9 1.2 %copy-done.1 = bf16[128,4096]{1,0:T(8,128)(2,1)S(1)} copy-done((bf16[128,4096]{1,0:T(8,128)(2,1)S(1)}, bf16[128,4096]{1,0:T(8,128)(2,1)}, u32[]{:S(2)}) %copy-start.1) | copy-done | bytes 1048600
  31.1 4.8 %shard_map.69 = (bf16[8,512,256]{2,1,0:T(8,128)(2,1)S(1)}, bf16[96,512,128]{2,1,0:T(8,128)(2,1)}) custom-call(bf16[256,128]{1,0:T(8,128)(2,1)S(1)} %get-tuple-element.26.after, bf16[128,4096]{1,0:T(8,128)(2,1)S(1)} %copy-done, bf16[128,4096]{1,0:T(8,128)(2,1)S(1)} %copy-done.1), custom_call_target="tpu_custom_call" | custom-call | bytes 16777216 | tf_op jit(solution)/shard_map/pallas_call | solution.py:332
  36.5 1.2 %copy-done.2 = bf16[128,4096]{1,0:T(8,128)(2,1)S(1)} copy-done((bf16[128,4096]{1,0:T(8,128)(2,1)S(1)}, bf16[128,4096]{1,0:T(8,128)(2,1)}, u32[]{:S(2)}) %copy-start.2) | copy-done | bytes 1048600
  37.8 0.8 copy-done.4
  38.6 0.8 copy-done.6
  39.4 1.8 %shard_map.70 = (f32[64,128]{1,0:T(8,128)S(1)}, f32[64,128]{1,0:T(8,128)S(1)}) custom-call(s32[1]{0:T(128)} %bitcast.here, bf16[128,4096]{1,0:T(8,128)(2,1)S(1)} %copy-done, bf16[128,4096]{1,0:T(8,128)(2,1)S(1)} %copy-done.2, bf16[256,128]{1,0:T(8,128)(2,1)S(1)} %copy-done.6, bf16[256,128]{1,0:T(8,128)(2,1)S(1)} %copy-done.4, ...), custom_call_target="tpu_custom_call" | custom-call | flops 268435456 | bytes 3145728 | tf_op jit(solution)/shard_map/pallas_call | solution.py:345
  41.3 1.2 %collective-permute-done.4.other.d_other = f32[64,128]{1,0:T(8,128)S(1)} collective-permute-done((f32[64,128]{1,0:T(8,128)S(1)}, f32[64,128]{1,0:T(8,128)S(1)}, u32[]{:S(2)}, u32[]{:S(2)}) %collective-permute-start.4) | collective-permute-done | bytes 32800 | tf_op jit(solution)/shard_map/ppermute | solution.py:294
  42.5 0.8 shard_map.71
  44.6 1.2 %shard_map.72.mine = f32[64,128]{1,0:T(8,128)S(1)} custom-call(s32[1]{0:T(128)} %bitcast.here, bf16[128,4096]{1,0:T(8,128)(2,1)S(1)} %copy-done, f32[64,128]{1,0:T(8,128)S(1)} %get-tuple-element.40.partial, bf16[256,128]{1,0:T(8,128)(2,1)S(1)} %collective-permute-done.5.refs_0_, bf16[256,128]{1,0:T(8,128)(2,1)} %collective-permute-done.6.refs_1_), custom_call_target="tpu_custom_call" | custom-call | flops 33554432 | bytes 1048576 | tf_op jit(solution)/shard_map/pallas_call | solution.py:364
  46.0 1.0 %collective-permute-done.7.other = f32[64,128]{1,0:T(8,128)S(1)} collective-permute-done((f32[64,128]{1,0:T(8,128)S(1)}, f32[64,128]{1,0:T(8,128)S(1)}, u32[]{:S(2)}, u32[]{:S(2)}) %collective-permute-start.7) | collective-permute-done | bytes 32800 | tf_op jit(solution)/shard_map/ppermute | solution.py:294
  47.1 2.1 %shard_map.73 = (bf16[256,128]{1,0:T(8,128)(2,1)S(1)}, bf16[256,128]{1,0:T(8,128)(2,1)S(1)}, bf16[512,128]{1,0:T(8,128)(2,1)}, bf16[512,128]{1,0:T(8,128)(2,1)}, bf16[4,512,128]{2,1,0:T(8,128)(2,1)}) custom-call(s32[1]{0:T(128)} %bitcast.here, s32[8]{0:T(128)S(1)} %bitcast.8, f32[64,128]{1,0:T(8,128)S(1)} %get-tuple-element.48.mine.d_mine, ...), custom_call_target="tpu_custom_call" | custom-call | flops 268435456 | bytes 3145728 | tf_op jit(solution)/shard_map/pallas_call | solution.py:373
  49.1 10.3 %all-to-all-start.1 = ((bf16[4,512,128]{2,1,0:T(8,128)(2,1)}), bf16[4,512,128]{2,1,0:T(8,128)(2,1)S(1)}, u32[]{:S(2)}, u32[]{:S(2)}) async-start(bf16[4,512,128]{2,1,0:T(8,128)(2,1)} %get-tuple-element.47), calls=%async_computation.1 | async-start | bytes 1048576 | tf_op jit(solution)/shard_map/all_to_all | solution.py:283
  59.4 2.2 %collective-permute-start.8 = (bf16[256,128]{1,0:T(8,128)(2,1)}, bf16[256,128]{1,0:T(8,128)(2,1)S(1)}, u32[]{:S(2)}, u32[]{:S(2)}) collective-permute-start(bf16[256,128]{1,0:T(8,128)(2,1)} %copy-done.12), channel_id=1, source_target_pairs={{0,12},{2,14},{4,8},{6,10},{8,4},{10,6},{12,0},{14,2},{1,13},{3,15... | collective-permute-start | bytes 196616 | tf_op jit(solution)/shard_map/ppermute | solution.py:275
  61.6 1.3 %collective-permute-start.12 = (bf16[512,128]{1,0:T(8,128)(2,1)}, bf16[512,128]{1,0:T(8,128)(2,1)S(1)}, u32[]{:S(2)}, u32[]{:S(2)}) collective-permute-start(bf16[512,128]{1,0:T(8,128)(2,1)} %get-tuple-element.45), channel_id=1, source_target_pairs={{0,8},{2,10},{4,12},{6,14},{8,0},{10,2},{12,4},{14,6},{1,9},{3,11}... | collective-permute-start | bytes 393224 | tf_op jit(solution)/shard_map/ppermute | solution.py:275
  62.9 2.5 %collective-permute-start.13 = (bf16[512,128]{1,0:T(8,128)(2,1)}, bf16[512,128]{1,0:T(8,128)(2,1)S(1)}, u32[]{:S(2)}, u32[]{:S(2)}) collective-permute-start(bf16[512,128]{1,0:T(8,128)(2,1)} %get-tuple-element.46), channel_id=1, source_target_pairs={{0,10},{2,8},{4,14},{6,12},{8,2},{10,0},{12,6},{14,4},{1,11},{3,9}... | collective-permute-start | bytes 393224 | tf_op jit(solution)/shard_map/ppermute | solution.py:275
  65.4 1.6 %collective-permute-start.9 = (bf16[256,128]{1,0:T(8,128)(2,1)}, bf16[256,128]{1,0:T(8,128)(2,1)S(1)}, u32[]{:S(2)}, u32[]{:S(2)}) collective-permute-start(bf16[256,128]{1,0:T(8,128)(2,1)} %copy-done.10), channel_id=1, source_target_pairs={{0,14},{2,12},{4,10},{6,8},{8,6},{10,4},{12,2},{14,0},{1,15},{3,13... | collective-permute-start | bytes 196616 | tf_op jit(solution)/shard_map/ppermute | solution.py:275
  67.1 2.2 %collective-permute-start.10 = (bf16[256,128]{1,0:T(8,128)(2,1)}, bf16[256,128]{1,0:T(8,128)(2,1)S(1)}, u32[]{:S(2)}, u32[]{:S(2)}) collective-permute-start(bf16[256,128]{1,0:T(8,128)(2,1)} %copy-done.13), channel_id=1, source_target_pairs={{0,12},{2,14},{4,8},{6,10},{8,4},{10,6},{12,0},{14,2},{1,13},{3,15... | collective-permute-start | bytes 196616 | tf_op jit(solution)/shard_map/ppermute | solution.py:275
  69.3 1.2 %collective-permute-done.8.refs_0_ = bf16[256,128]{1,0:T(8,128)(2,1)S(1)} collective-permute-done((bf16[256,128]{1,0:T(8,128)(2,1)}, bf16[256,128]{1,0:T(8,128)(2,1)S(1)}, u32[]{:S(2)}, u32[]{:S(2)}) %collective-permute-start.8) | collective-permute-done | bytes 65568 | tf_op jit(solution)/shard_map/ppermute | solution.py:275
  70.5 3.1 %collective-permute-start.11 = (bf16[256,128]{1,0:T(8,128)(2,1)}, bf16[256,128]{1,0:T(8,128)(2,1)S(1)}, u32[]{:S(2)}, u32[]{:S(2)}) collective-permute-start(bf16[256,128]{1,0:T(8,128)(2,1)} %copy-done.11), channel_id=1, source_target_pairs={{0,14},{2,12},{4,10},{6,8},{8,6},{10,4},{12,2},{14,0},{1,15},{3,13... | collective-permute-start | bytes 196616 | tf_op jit(solution)/shard_map/ppermute | solution.py:275
  73.6 2.5 %shard_map.74 = bf16[128,4096]{1,0:T(8,128)(2,1)} custom-call(s32[1]{0:T(128)} %bitcast.here, s32[8]{0:T(128)S(1)} %bitcast.9, f32[64,128]{1,0:T(8,128)S(1)} %get-tuple-element.48.mine.d_mine, f32[64,128]{1,0:T(8,128)S(1)} %collective-permute-done.4.other.d_other, bf16[256,128]{1,0:T(8,128)(2,1)S(1)} %collective-permute-done.5.refs_0_, ...), custom_call_target="tpu_custom_call" | custom-call | flops 134217728 | bytes 2097152 | tf_op jit(solution)/shard_map/pallas_call | solution.py:385
  76.1 2.3 %collective-permute-done.9.refs_1_ = bf16[256,128]{1,0:T(8,128)(2,1)S(1)} collective-permute-done((bf16[256,128]{1,0:T(8,128)(2,1)}, bf16[256,128]{1,0:T(8,128)(2,1)S(1)}, u32[]{:S(2)}, u32[]{:S(2)}) %collective-permute-start.9) | collective-permute-done | bytes 65568 | tf_op jit(solution)/shard_map/ppermute | solution.py:275
  78.8 1.6 %collective-permute-done.11.refs_3_ = bf16[256,128]{1,0:T(8,128)(2,1)S(1)} collective-permute-done((bf16[256,128]{1,0:T(8,128)(2,1)}, bf16[256,128]{1,0:T(8,128)(2,1)S(1)}, u32[]{:S(2)}, u32[]{:S(2)}) %collective-permute-start.11) | collective-permute-done | bytes 65568 | tf_op jit(solution)/shard_map/ppermute | solution.py:275
  80.4 3.7 %collective-permute-done.13.refs_5_ = bf16[512,128]{1,0:T(8,128)(2,1)S(1)} collective-permute-done((bf16[512,128]{1,0:T(8,128)(2,1)}, bf16[512,128]{1,0:T(8,128)(2,1)S(1)}, u32[]{:S(2)}, u32[]{:S(2)}) %collective-permute-start.13) | collective-permute-done | bytes 131104 | tf_op jit(solution)/shard_map/ppermute | solution.py:275
  84.1 1.8 %shard_map.75 = bf16[96,512,128]{2,1,0:T(8,128)(2,1)} custom-call(s32[8]{0:T(128)S(1)} %bitcast.12, s32[1]{0:T(128)} %bitcast.here, s32[8]{0:T(128)S(1)} %bitcast.10, bf16[256,128]{1,0:T(8,128)(2,1)S(1)} %collective-permute-done.8.refs_0_, bf16[256,128]{1,0:T(8,128)(2,1)S(1)} %collective-permute-done.9.refs_1_, ...), custom_call_target="tpu_custom_call", output_to_operand_aliasing={{}: (10, {})} | custom-call | bytes 2097152 | tf_op jit(solution)/shard_map/pallas_call | solution.py:394
  (36 shorter events, 3.3 us)
Async XLA Ops:
  0.6 29.2 %copy-start = (bf16[128,4096]{1,0:T(8,128)(2,1)S(1)}, bf16[128,4096]{1,0:T(8,128)(2,1)}, u32[]{:S(2)}) copy-start(bf16[128,4096]{1,0:T(8,128)(2,1)} %x.5) | copy-start | bytes 3145732
  0.6 41.9 %copy-start.7 = (s32[8,1]{0,1:T(1,128)S(1)}, s32[8,1]{0,1:T(1,128)}, u32[]{:S(2)}) copy-start(s32[8,1]{0,1:T(1,128)} %param.9) | copy-start | bytes 100
  0.7 0.7 copy-start.8
  1.4 82.7 %copy-start.9 = (s32[8,1]{0,1:T(1,128)S(1)}, s32[8,1]{0,1:T(1,128)}, u32[]{:S(2)}) copy-start(s32[8,1]{0,1:T(1,128)} %param.8) | copy-start | bytes 100
  4.2 32.3 %all-to-all-start = ((bf16[4,512,128]{2,1,0:T(8,128)(2,1)}), bf16[4,512,128]{2,1,0:T(8,128)(2,1)}, u32[]{:S(2)}, u32[]{:S(2)}) async-start(bf16[4,512,128]{2,1,0:T(8,128)(2,1)} %get-tuple-element.34), calls=%async_computation | async-start | bytes 1048576 | tf_op jit(solution)/shard_map/all_to_all | solution.py:283
  9.4 27.1 %collective-permute-start.2 = (bf16[512,128]{1,0:T(8,128)(2,1)}, bf16[512,128]{1,0:T(8,128)(2,1)S(1)}, u32[]{:S(2)}, u32[]{:S(2)}) collective-permute-start(bf16[512,128]{1,0:T(8,128)(2,1)} %get-tuple-element.32), channel_id=1, source_target_pairs={{0,8},{2,10},{4,12},{6,14},{8,0},{10,2},{12,4},{14,6},{1,9},{3,11}... | collective-permute-start | bytes 393224 | tf_op jit(solution)/shard_map/ppermute | solution.py:275
  12.5 24.1 %collective-permute-start.3 = (bf16[512,128]{1,0:T(8,128)(2,1)}, bf16[512,128]{1,0:T(8,128)(2,1)S(1)}, u32[]{:S(2)}, u32[]{:S(2)}) collective-permute-start(bf16[512,128]{1,0:T(8,128)(2,1)} %get-tuple-element.33), channel_id=1, source_target_pairs={{0,10},{2,8},{4,14},{6,12},{8,2},{10,0},{12,6},{14,4},{1,11},{3,9}... | collective-permute-start | bytes 393224 | tf_op jit(solution)/shard_map/ppermute | solution.py:275
  13.8 15.4 %collective-permute-start.1 = (bf16[256,128]{1,0:T(8,128)(2,1)S(1)}, bf16[256,128]{1,0:T(8,128)(2,1)S(1)}, u32[]{:S(2)}, u32[]{:S(2)}) collective-permute-start(bf16[256,128]{1,0:T(8,128)(2,1)S(1)} %get-tuple-element.27), channel_id=1, source_target_pairs={{0,14},{2,12},{4,10},{6,8},{8,6},{10,4},{12,2},{14,0},{1,15},{3,13... | collective-permute-start | bytes 196616 | tf_op jit(solution)/shard_map/ppermute | solution.py:275
  17.6 18.2 %collective-permute-start = (bf16[256,128]{1,0:T(8,128)(2,1)S(1)}, bf16[256,128]{1,0:T(8,128)(2,1)S(1)}, u32[]{:S(2)}, u32[]{:S(2)}) collective-permute-start(bf16[256,128]{1,0:T(8,128)(2,1)S(1)} %get-tuple-element.26.after), channel_id=1, source_target_pairs={{0,12},{2,14},{4,8},{6,10},{8,4},{10,6},{12,0},{14,2},{1,13},{3,15... | collective-permute-start | bytes 196616 | tf_op jit(solution)/shard_map/ppermute | solution.py:275
  17.6 27.0 %collective-permute-start.5 = (bf16[256,128]{1,0:T(8,128)(2,1)}, bf16[256,128]{1,0:T(8,128)(2,1)S(1)}, u32[]{:S(2)}, u32[]{:S(2)}) collective-permute-start(bf16[256,128]{1,0:T(8,128)(2,1)} %get-tuple-element.41), channel_id=1, source_target_pairs={{0,12},{2,14},{4,8},{6,10},{8,4},{10,6},{12,0},{14,2},{1,13},{3,15... | collective-permute-start | bytes 196616 | tf_op jit(solution)/shard_map/ppermute | solution.py:275
  29.2 0.6 copy-start.3
  29.8 14.8 %collective-permute-start.6 = (bf16[256,128]{1,0:T(8,128)(2,1)}, bf16[256,128]{1,0:T(8,128)(2,1)}, u32[]{:S(2)}, u32[]{:S(2)}) collective-permute-start(bf16[256,128]{1,0:T(8,128)(2,1)} %get-tuple-element.42), channel_id=1, source_target_pairs={{0,14},{2,12},{4,10},{6,8},{8,6},{10,4},{12,2},{14,0},{1,15},{3,13... | collective-permute-start | bytes 196616 | tf_op jit(solution)/shard_map/ppermute | solution.py:275
  29.8 1.2 %copy-start.1 = (bf16[128,4096]{1,0:T(8,128)(2,1)S(1)}, bf16[128,4096]{1,0:T(8,128)(2,1)}, u32[]{:S(2)}) copy-start(bf16[128,4096]{1,0:T(8,128)(2,1)} %y.3) | copy-start | bytes 3145732
  35.9 0.6 copy-start.5
  36.5 1.2 %copy-start.2 = (bf16[128,4096]{1,0:T(8,128)(2,1)S(1)}, bf16[128,4096]{1,0:T(8,128)(2,1)}, u32[]{:S(2)}) copy-start(bf16[128,4096]{1,0:T(8,128)(2,1)} %y.3) | copy-start | bytes 3145732
  37.8 0.8 copy-start.4
  38.6 0.8 copy-start.6
  41.2 1.3 %collective-permute-start.4 = (f32[64,128]{1,0:T(8,128)S(1)}, f32[64,128]{1,0:T(8,128)S(1)}, u32[]{:S(2)}, u32[]{:S(2)}) collective-permute-start(f32[64,128]{1,0:T(8,128)S(1)} %get-tuple-element.48.mine.d_mine), channel_id=1, source_target_pairs={{0,1},{1,0},{2,3},{3,2},{4,5},{5,4},{6,7},{7,6},{8,9},{9,8},{10,11... | collective-permute-start | bytes 98312 | tf_op jit(solution)/shard_map/ppermute | solution.py:294
  43.3 0.6 copy-start.10
  44.0 0.6 copy-start.12
  45.8 1.3 %collective-permute-start.7 = (f32[64,128]{1,0:T(8,128)S(1)}, f32[64,128]{1,0:T(8,128)S(1)}, u32[]{:S(2)}, u32[]{:S(2)}) collective-permute-start(f32[64,128]{1,0:T(8,128)S(1)} %shard_map.72.mine), channel_id=1, source_target_pairs={{0,1},{1,0},{2,3},{3,2},{4,5},{5,4},{6,7},{7,6},{8,9},{9,8},{10,11... | collective-permute-start | bytes 98312 | tf_op jit(solution)/shard_map/ppermute | solution.py:294
  49.1 12.5 %copy-start.13 = (bf16[256,128]{1,0:T(8,128)(2,1)}, bf16[256,128]{1,0:T(8,128)(2,1)S(1)}, u32[]{:S(2)}) copy-start(bf16[256,128]{1,0:T(8,128)(2,1)S(1)} %get-tuple-element.43) | copy-start | bytes 196612
  49.1 13.8 %copy-start.11 = (bf16[256,128]{1,0:T(8,128)(2,1)}, bf16[256,128]{1,0:T(8,128)(2,1)S(1)}, u32[]{:S(2)}) copy-start(bf16[256,128]{1,0:T(8,128)(2,1)S(1)} %get-tuple-element.44) | copy-start | bytes 196612
  49.1 35.0 %all-to-all-start.1 = ((bf16[4,512,128]{2,1,0:T(8,128)(2,1)}), bf16[4,512,128]{2,1,0:T(8,128)(2,1)S(1)}, u32[]{:S(2)}, u32[]{:S(2)}) async-start(bf16[4,512,128]{2,1,0:T(8,128)(2,1)} %get-tuple-element.47), calls=%async_computation.1 | async-start | bytes 1048576 | tf_op jit(solution)/shard_map/all_to_all | solution.py:283
  59.4 11.1 %collective-permute-start.8 = (bf16[256,128]{1,0:T(8,128)(2,1)}, bf16[256,128]{1,0:T(8,128)(2,1)S(1)}, u32[]{:S(2)}, u32[]{:S(2)}) collective-permute-start(bf16[256,128]{1,0:T(8,128)(2,1)} %copy-done.12), channel_id=1, source_target_pairs={{0,12},{2,14},{4,8},{6,10},{8,4},{10,6},{12,0},{14,2},{1,13},{3,15... | collective-permute-start | bytes 196616 | tf_op jit(solution)/shard_map/ppermute | solution.py:275
  61.6 18.8 %collective-permute-start.12 = (bf16[512,128]{1,0:T(8,128)(2,1)}, bf16[512,128]{1,0:T(8,128)(2,1)S(1)}, u32[]{:S(2)}, u32[]{:S(2)}) collective-permute-start(bf16[512,128]{1,0:T(8,128)(2,1)} %get-tuple-element.45), channel_id=1, source_target_pairs={{0,8},{2,10},{4,12},{6,14},{8,0},{10,2},{12,4},{14,6},{1,9},{3,11}... | collective-permute-start | bytes 393224 | tf_op jit(solution)/shard_map/ppermute | solution.py:275
  62.9 21.2 %collective-permute-start.13 = (bf16[512,128]{1,0:T(8,128)(2,1)}, bf16[512,128]{1,0:T(8,128)(2,1)S(1)}, u32[]{:S(2)}, u32[]{:S(2)}) collective-permute-start(bf16[512,128]{1,0:T(8,128)(2,1)} %get-tuple-element.46), channel_id=1, source_target_pairs={{0,10},{2,8},{4,14},{6,12},{8,2},{10,0},{12,6},{14,4},{1,11},{3,9}... | collective-permute-start | bytes 393224 | tf_op jit(solution)/shard_map/ppermute | solution.py:275
  65.4 13.0 %collective-permute-start.9 = (bf16[256,128]{1,0:T(8,128)(2,1)}, bf16[256,128]{1,0:T(8,128)(2,1)S(1)}, u32[]{:S(2)}, u32[]{:S(2)}) collective-permute-start(bf16[256,128]{1,0:T(8,128)(2,1)} %copy-done.10), channel_id=1, source_target_pairs={{0,14},{2,12},{4,10},{6,8},{8,6},{10,4},{12,2},{14,0},{1,15},{3,13... | collective-permute-start | bytes 196616 | tf_op jit(solution)/shard_map/ppermute | solution.py:275
  67.1 11.7 %collective-permute-start.10 = (bf16[256,128]{1,0:T(8,128)(2,1)}, bf16[256,128]{1,0:T(8,128)(2,1)S(1)}, u32[]{:S(2)}, u32[]{:S(2)}) collective-permute-start(bf16[256,128]{1,0:T(8,128)(2,1)} %copy-done.13), channel_id=1, source_target_pairs={{0,12},{2,14},{4,8},{6,10},{8,4},{10,6},{12,0},{14,2},{1,13},{3,15... | collective-permute-start | bytes 196616 | tf_op jit(solution)/shard_map/ppermute | solution.py:275
  70.5 9.9 %collective-permute-start.11 = (bf16[256,128]{1,0:T(8,128)(2,1)}, bf16[256,128]{1,0:T(8,128)(2,1)S(1)}, u32[]{:S(2)}, u32[]{:S(2)}) collective-permute-start(bf16[256,128]{1,0:T(8,128)(2,1)} %copy-done.11), channel_id=1, source_target_pairs={{0,14},{2,12},{4,10},{6,8},{8,6},{10,4},{12,2},{14,0},{1,15},{3,13... | collective-permute-start | bytes 196616 | tf_op jit(solution)/shard_map/ppermute | solution.py:275

commit v7 on v6

--- a/solution.py
+++ b/solution.py
@@ -36,19 +36,15 @@
 
 
 def gather_kernel(plan, ids, here, table, *refs):
-    split, whole, near = plan
+    split, whole = plan
     parts = len(split)
-    up, rest = refs[:parts], refs[parts:]
-    straight, rest = rest[: len(whole)], rest[len(whole) :]
-    close, rest = rest[0], rest[1:]
-    down, (held, sems) = rest[:parts], rest[parts:]
-    me = here[0]
-    targets = [(me ^ k, held.at[n]) for n, k in enumerate(split)]
-    targets += [(me ^ k, straight[n]) for n, k in enumerate(whole)]
-    targets += [((me & -near) | n, close.at[n]) for n in range(near)]
+    up, straight = refs[:parts], refs[parts : parts + len(whole)]
+    down, (held, sems) = refs[parts + len(whole) : -2], refs[-2:]
+    me = here[0]
+    targets = [(k, held.at[n]) for n, k in enumerate(split)] + list(zip(whole, straight))
     copies = [
-        pltpu.make_async_copy(table.at[ids[block]], target, sems.at[n])
-        for n, (block, target) in enumerate(targets)
+        pltpu.make_async_copy(table.at[ids[me ^ k]], target, sems.at[n])
+        for n, (k, target) in enumerate(targets)
     ]
     for copy in copies:
         copy.start()
@@ -95,19 +91,16 @@
 
 
 def rank_kernel(plan, here, x, y, *refs):
-    split, whole, near = plan
-    up, straight = refs[: len(split)], refs[len(split) : -3]
-    close, dhidden, hidden = refs[-3:]
-    _, rows, width = close.shape
+    split, whole = plan
+    straight, up, dhidden, hidden = [*refs[:1], *refs[1 + len(split) : -2]], refs[1 : 1 + len(split)], *refs[-2:]
+    rows, width = straight[0].shape
     tokens = x.shape[0]
     me = here[0]
     x_rank = jnp.zeros((tokens, width), jnp.float32)
     y_rank = jnp.zeros((tokens, width), jnp.float32)
     y_first = jnp.zeros((tokens, width), jnp.float32)
-    pairs = [((me & -near) | n, close.at[n]) for n in range(near)]
-    pairs += [(me ^ k, straight[n]) for n, k in enumerate(whole)]
-    for owner, pair in pairs:
-        columns = pl.ds(pl.multiple_of(owner * rows, rows), rows)
+    for k, pair in zip(whole, straight):
+        columns = pl.ds(pl.multiple_of((me ^ k) * rows, rows), rows)
         x_rank += jnp.dot(x[:, columns], pair[...], preferred_element_type=jnp.float32)
         y_rank += jnp.dot(y[:, columns], pair[...], preferred_element_type=jnp.float32)
     for n, k in enumerate(split):
@@ -122,7 +115,7 @@
 
 
 def rank_rest_kernel(plan, here, x, partial, *refs):
-    split, _, _ = plan
+    split, _ = plan
     down, out = refs[:-1], refs[-1]
     tokens, width = x.shape[0], partial.shape[1]
     x_first = jnp.zeros((tokens, width), jnp.float32)
@@ -155,7 +148,7 @@
 
 
 def down_piece_kernel(plan, scale, here, lengths, mine, other, turned, *out):
-    split, _, _ = plan
+    split, _ = plan
     me = here[0]
     left, right = rounded(mine, other, lengths[me], scale)
     tokens = left.shape[0]
@@ -164,8 +157,8 @@
 
 
 def piece_kernel(plan, scale, here, lengths, d_mine, d_other, mine, other, turned, *refs):
-    split, whole, near = plan
-    up, straight, close = refs[: len(split)], refs[len(split) : -1], refs[-1]
+    split, whole = plan
+    up, straight = refs[: len(split)], refs[len(split) :]
     me = here[0]
     dhidden, _ = rounded(d_mine, d_other, lengths[me], scale)
     left, right = rounded(mine, other, lengths[me], 1.0)
@@ -181,15 +174,12 @@
         up[n][...] = (scale * piece).astype(jnp.bfloat16)
     for n, k in enumerate(whole):
         straight[n][...] = rows_for(me ^ k)
-    for n in range(near):
-        close[n] = rows_for((me & -near) | n)
 
 
 def input_kernel(plan, scale, here, lengths, mine, other, *refs):
-    split, whole, near = plan
-    down, straight = refs[: len(split)], refs[len(split) : -2]
-    close, out = refs[-2:]
-    rows = close.shape[1]
+    split, whole = plan
+    down, straight, out = refs[: len(split)], refs[len(split) : -1], refs[-1]
+    rows = straight[0].shape[0]
     half = rows // 2
     me = here[0]
     left, right = rounded(mine, other, lengths[me], scale)
@@ -200,10 +190,8 @@
         )
         return value.astype(jnp.bfloat16)
 
-    pairs = [((me & -near) | n, close.at[n]) for n in range(near)]
-    pairs += [(me ^ k, straight[n]) for n, k in enumerate(whole)]
-    for owner, pair in pairs:
-        out[:, pl.ds(pl.multiple_of(owner * rows, rows), rows)] = product(left, pair[...])
+    for k, pair in zip(whole, straight):
+        out[:, pl.ds(pl.multiple_of((me ^ k) * rows, rows), rows)] = product(left, pair[...])
     for n, k in enumerate(split):
         start = (me ^ k) * rows
         out[:, pl.ds(pl.multiple_of(start, half), half)] = product(left, down[n][...])
@@ -211,10 +199,10 @@
 
 
 def merge_kernel(plan, ids, here, lengths, *refs):
-    split, whole, near = plan
+    split, whole = plan
     parts = len(split)
-    down, up, straight = refs[:parts], refs[parts : 2 * parts], refs[2 * parts : 2 * parts + len(whole)]
-    close, _, out, total, held, sems = refs[2 * parts + len(whole) :]
+    down, up, straight = refs[:parts], refs[parts : 2 * parts], refs[2 * parts : -5]
+    out, total, held, sems = refs[-4:]
     me = here[0]
     rows, width = total.shape
     half = rows // 2
@@ -229,8 +217,7 @@
     def read(ref):
         return lambda: ref[...].astype(jnp.float32)
 
-    pieces = [((me & -near) | n, read(close.at[n])) for n in range(near)]
-    pieces += [(me ^ k, read(straight[n])) for n, k in enumerate(whole)]
+    pieces = [(me ^ k, read(straight[n])) for n, k in enumerate(whole)]
     pieces += [(me ^ k, functools.partial(unpacked, n)) for n, k in enumerate(split)]
     owners = len(pieces)
     adapters = [ids[block] for block, _ in pieces]
@@ -272,17 +259,9 @@
 
 def to_partner(pieces, partners, owners):
     return [
-        lax.ppermute(piece, "dp", [(i, i ^ k) for i in range(owners)])
+        lax.ppermute(piece, "dp", [(i, i ^ k) for i in range(owners)]) if k else piece
         for k, piece in zip(partners, pieces)
     ]
-
-
-def among_near(pieces, owners):
-    near = pieces.shape[0]
-    groups = [list(range(start, start + near)) for start in range(0, owners, near)]
-    return lax.all_to_all(
-        pieces, "dp", split_axis=0, concat_axis=0, tiled=True, axis_index_groups=groups
-    )
 
 
 def after(value, *others):
@@ -296,9 +275,8 @@
 
 def with_kernels(activations, cotangent, adapter_weight_pair, adapter_of_block, block_live_length):
     owners = lax.axis_size("dp")
-    near = owners // 2
-    far = list(range(near, owners))
-    plan = split, whole, _ = tuple(far[-2:]), tuple(far[:-2]), near
+    near, far = range(1, owners // 2), range(owners // 2, owners)
+    plan = split, whole = tuple(far[-2:]), (1, *far[:-2], *near[1:], 0)
     here = lax.axis_index("dp").astype(jnp.int32).reshape(1)
     ids, lengths = adapter_of_block[:, 0], block_live_length[:, 0]
     count, _, rows, width = adapter_weight_pair.shape
@@ -308,7 +286,6 @@
     bf16, f32 = jnp.bfloat16, jnp.float32
     packed = jax.ShapeDtypeStruct((rows // 2, width), bf16)
     straight = jax.ShapeDtypeStruct((rows, width), bf16)
-    stacked = jax.ShapeDtypeStruct((near, rows, width), bf16)
     rank_space = jax.ShapeDtypeStruct((tokens // 2, width), f32)
     parts, wholes = len(split), len(whole)
     pair_bytes = owners * rows * width * 2
@@ -316,17 +293,14 @@
 
     sent = call(
         functools.partial(gather_kernel, plan),
-        [packed] * parts + [straight] * wholes + [stacked] + [packed] * parts,
+        [packed] * parts + [straight] * wholes + [packed] * parts,
         [in_smem, in_smem, in_hbm],
-        [in_vmem] * (2 * parts + wholes + 1),
+        [in_vmem] * (2 * parts + wholes),
         [pltpu.VMEM((parts, rows, width), bf16), pltpu.SemaphoreType.DMA((owners,))],
         moved=2 * pair_bytes,
         vmem=53,
     )(ids, here, table)
     ups = to_partner(sent[:parts], split, owners)
-    pairs = to_partner(sent[parts : parts + wholes], whole, owners)
-    close = among_near(sent[parts + wholes], owners)
-    downs = to_partner(sent[parts + wholes + 1 :], split, owners)
 
     step = 8
     turned, blank = call(
@@ -340,25 +314,27 @@
         [pltpu.VMEM((step, rows, width), bf16), pltpu.SemaphoreType.DMA((count // step,))],
         moved=4 * token_bytes + 2 * count * rows * width,
     )(sent[0], activations, cotangent)
-    *ups, turned, blank = lax.optimization_barrier((*ups, turned, blank))
+    sent = list(sent)
+    held_back = whole.index(near[-1]) + parts
+    sent[held_back] = after(sent[held_back], turned)
+    pairs = to_partner(sent[parts : parts + wholes], whole, owners)
+    downs = to_partner(sent[parts + wholes :], split, owners)
 
     dhidden, partial = call(
         functools.partial(rank_kernel, plan),
         [rank_space, rank_space],
-        [in_smem] + [in_vmem] * (3 + parts + wholes),
+        [in_smem] + [in_vmem] * (2 + parts + wholes),
         [in_vmem, in_vmem],
-        flops=4 * tokens * features * width,
-        moved=2 * token_bytes + pair_bytes,
-    )(here, activations, cotangent, *ups, *pairs, close)
+        moved=1024,
+    )(here, activations, cotangent, pairs[0], *ups, *pairs[1:])
     dhidden_other = across_cores(dhidden)
     down_pieces = call(
         functools.partial(down_piece_kernel, plan, scale),
         [packed] * parts,
         [in_smem] * 2 + [in_vmem] * 3,
         [in_vmem] * parts,
-        flops=parts * 2 * tokens * rows * width,
-        moved=pair_bytes,
-    )(here, lengths, dhidden, dhidden_other, turned)
+        moved=1024,
+    )(here, lengths, after(dhidden, downs[0]), dhidden_other, turned)
     d_downs = to_partner(down_pieces, split, owners)
 
     hidden = call(
@@ -366,35 +342,32 @@
         rank_space,
         [in_smem] + [in_vmem] * (2 + parts),
         in_vmem,
-        flops=parts * 2 * tokens * rows * width,
-        moved=pair_bytes,
+        moved=1024,
     )(here, activations, after(partial, *down_pieces), *downs)
     hidden_other = across_cores(hidden)
     pieces = call(
         functools.partial(piece_kernel, plan, scale),
-        [packed] * parts + [straight] * wholes + [stacked],
+        [packed] * parts + [straight] * wholes,
         [in_smem] * 2 + [in_vmem] * 5,
-        [in_vmem] * (parts + wholes + 1),
-        flops=4 * tokens * features * width,
-        moved=2 * token_bytes + pair_bytes,
-    )(here, lengths, dhidden, dhidden_other, hidden, hidden_other, turned)
+        [in_vmem] * (parts + wholes),
+        moved=1024,
+    )(here, lengths, dhidden, dhidden_other, after(hidden, d_downs[0]), hidden_other, turned)
     d_ups = to_partner(pieces[:parts], split, owners)
-    d_pairs = to_partner(pieces[parts : parts + wholes], whole, owners)
-    d_close = among_near(pieces[-1], owners)
+    d_pairs = to_partner(pieces[parts:], whole, owners)
 
     grad_input = call(
         functools.partial(input_kernel, plan, scale),
         jax.ShapeDtypeStruct((tokens, features), bf16),
-        [in_smem] * 2 + [in_vmem] * (3 + parts + wholes),
+        [in_smem] * 2 + [in_vmem] * (2 + parts + wholes),
         in_vmem,
         flops=2 * tokens * features * width,
         moved=token_bytes + pair_bytes,
-    )(here, lengths, after(dhidden, *pieces), dhidden_other, *downs, *pairs, close)
+    )(here, lengths, after(dhidden, *pieces), dhidden_other, *downs, *pairs)
 
     gradient = call(
         functools.partial(merge_kernel, plan),
         jax.ShapeDtypeStruct(table.shape, bf16),
-        [in_smem] * 3 + [in_vmem] * (2 * parts + wholes + 1) + [in_hbm],
+        [in_smem] * 3 + [in_vmem] * (2 * parts + wholes) + [in_hbm],
         in_hbm,
         [
             pltpu.VMEM((rows, width), f32),
@@ -402,8 +375,8 @@
             pltpu.SemaphoreType.DMA((owners,)),
         ],
         moved=2 * pair_bytes,
-        aliases={4 + 2 * parts + wholes: 0},
-    )(ids, here, lengths, *d_downs, *d_ups, *d_pairs, d_close, blank)
+        aliases={3 + 2 * parts + wholes: 0},
+    )(ids, here, lengths, *d_downs, *d_ups, *d_pairs, blank)
     return grad_input, gradient[:, None]
 
 

time: 87.3 us -> 71.6 us (0.82); the launches traced: 85.9 us -> 71.4 us
  local copies, waits for them, and re-layouts: 7.36 us -> 2.61 us
  starting transfers between devices: 40.8 us -> 36.3 us
  Pallas kernels: 17.8 us -> 14.3 us
  waiting for transfers between devices: 19.2 us -> 17.5 us
    all_to_all x2 -> x0, starting transfers between devices: 15.5 us -> none  [among_near(): lax.all_to_all(pieces, 'dp', split_axis=0, concat_axis=0, tiled=True, axi...]
    ppermute x12 -> x18, starting transfers between devices: 25 us -> 36.2 us  [to_partner(): lax.ppermute(piece, 'dp', [(i, i ^ k) for i in range(owners)])]
    unnamed x28 -> x12, local copies, waits for them, and re-layouts: 7.36 us -> 2.61 us
    ppermute x2, waiting for transfers between devices: 2.23 us -> 0.01 us  [across_cores(): return lax.ppermute(value, 'tensor', [(i, i ^ 1) for i in range(cores)])]
    pallas_call x1, Pallas kernels: 1.8 us -> 0.76 us  [with_kernels(): call(functools.partial(rank_kernel, plan), [rank_space, rank_space], [in_...]
    ppermute x12 -> x18, waiting for transfers between devices: 17 us -> 17.5 us  [to_partner(): lax.ppermute(piece, 'dp', [(i, i ^ k) for i in range(owners)])]
  transfers between devices with their start and end apart: 16 -> 20, of which waited for: 8 -> 9; matrix products, arithmetic and copies ran while one was open for 0% -> 0% of each run, Pallas kernels for 12% -> 14%
where the time goes in v7:
time: 71.6 us; the launch traced here: 71.4 us
  starting transfers between devices  36.3 us (51%)
  waiting for transfers between devices  17.5 us (24%)
  Pallas kernels  14.3 us (20%)
  local copies, waits for them, and re-layouts  2.61 us (4%)
  between operations  0.76 us (1%)
    ppermute x18, starting transfers between devices, to_partner(): lax.ppermute(piece, 'dp', [(i, i ^ k) for i in range(owners)])  36.2 us
    ppermute x18, waiting for transfers between devices, to_partner(): lax.ppermute(piece, 'dp', [(i, i ^ k) for i in range(owners)])  17.5 us
    pallas_call x1, Pallas kernels, with_kernels(): call(functools.partial(prep_kernel, rows), [jax.ShapeDtypeStruct((owners,...  4.8 us
    unnamed x12, local copies, waits for them, and re-layouts  2.61 us
    pallas_call x1, Pallas kernels, with_kernels(): call(functools.partial(gather_kernel, plan), [packed] * parts + [straight...  2.55 us
    pallas_call x1, Pallas kernels, with_kernels(): call(functools.partial(input_kernel, plan, scale), jax.ShapeDtypeStruct((...  1.99 us
    pallas_call x1, Pallas kernels, with_kernels(): call(functools.partial(merge_kernel, plan), jax.ShapeDtypeStruct(table.sh...  1.75 us
  transfers between devices with their start and end apart: 20, of which 9 were waited for; matrix products, arithmetic and copies ran while one was open for 0% of the time, Pallas kernels for 14%

profile of v7, /device:TPU:0, one launch (start us, length us, event | category | flops | bytes accessed | tf_op | source)
XLA Modules:
  0.0 71.4 jit_solution(4492779406016641467)
XLA Ops:
  0.7 0.8 %copy-done.5 = s32[8,1]{0,1:T(1,128)S(1)} copy-done((s32[8,1]{0,1:T(1,128)S(1)}, s32[8,1]{0,1:T(1,128)}, u32[]{:S(2)}) %copy-start.5) | copy-done | bytes 56
  1.5 2.5 %shard_map.68 = (bf16[256,128]{1,0:T(8,128)(2,1)S(1)}, bf16[256,128]{1,0:T(8,128)(2,1)S(1)}, bf16[512,128]{1,0:T(8,128)(2,1)S(1)}, bf16[512,128]{1,0:T(8,128)(2,...) custom-call(s32[8]{0:T(128)S(1)} %bitcast.11, ...), custom_call_target="tpu_custom_call" | custom-call | bytes 2097152 | tf_op jit(solution)/shard_map/pallas_call | solution.py:294
  4.0 6.0 %collective-permute-start.2 = (bf16[256,128]{1,0:T(8,128)(2,1)S(1)}, bf16[256,128]{1,0:T(8,128)(2,1)S(1)}, u32[]{:S(2)}, u32[]{:S(2)}) collective-permute-start(bf16[256,128]{1,0:T(8,128)(2,1)S(1)} %get-tuple-element.33), channel_id=1, source_target_pairs={{0,14},{2,12},{4,10},{6,8},{8,6},{10,4},{12,2},{14,0},{1,15},{3,13... | collective-permute-start | bytes 196616 | tf_op jit(solution)/shard_map/ppermute | solution.py:262
  10.7 0.9 %collective-permute-start.3 = (bf16[512,128]{1,0:T(8,128)(2,1)S(1)}, bf16[512,128]{1,0:T(8,128)(2,1)S(1)}, u32[]{:S(2)}, u32[]{:S(2)}) collective-permute-start(bf16[512,128]{1,0:T(8,128)(2,1)S(1)} %get-tuple-element.34), channel_id=1, source_target_pairs={{0,8},{2,10},{4,12},{6,14},{8,0},{10,2},{12,4},{14,6},{1,9},{3,11}... | collective-permute-start | bytes 393224 | tf_op jit(solution)/shard_map/ppermute | solution.py:262
  11.6 3.1 %collective-permute-start.4 = (bf16[512,128]{1,0:T(8,128)(2,1)S(1)}, bf16[512,128]{1,0:T(8,128)(2,1)S(1)}, u32[]{:S(2)}, u32[]{:S(2)}) collective-permute-start(bf16[512,128]{1,0:T(8,128)(2,1)S(1)} %get-tuple-element.35), channel_id=1, source_target_pairs={{0,10},{2,8},{4,14},{6,12},{8,2},{10,0},{12,6},{14,4},{1,11},{3,9}... | collective-permute-start | bytes 393224 | tf_op jit(solution)/shard_map/ppermute | solution.py:262
  14.7 4.8 %shard_map.69 = (bf16[8,512,256]{2,1,0:T(8,128)(2,1)S(1)}, bf16[96,512,128]{2,1,0:T(8,128)(2,1)}) custom-call(bf16[256,128]{1,0:T(8,128)(2,1)S(1)} %get-tuple-element.32.after, bf16[128,4096]{1,0:T(8,128)(2,1)S(1)} %copy-done, bf16[128,4096]{1,0:T(8,128)(2,1)S(1)} %copy-done.1), custom_call_target="tpu_custom_call" | custom-call | bytes 16777216 | tf_op jit(solution)/shard_map/pallas_call | solution.py:306
  19.5 1.3 %collective-permute-start.5 = (bf16[512,128]{1,0:T(8,128)(2,1)S(1)}, bf16[512,128]{1,0:T(8,128)(2,1)S(1)}, u32[]{:S(2)}, u32[]{:S(2)}) collective-permute-start(bf16[512,128]{1,0:T(8,128)(2,1)S(1)} %get-tuple-element.36), channel_id=1, source_target_pairs={{0,4},{2,6},{4,0},{6,2},{8,12},{10,14},{12,8},{14,10},{1,5},{3,7},... | collective-permute-start | bytes 393224 | tf_op jit(solution)/shard_map/ppermute | solution.py:262
  20.8 0.7 collective-permute-start.6
  21.5 3.7 %collective-permute-start.8 = (bf16[256,128]{1,0:T(8,128)(2,1)S(1)}, bf16[256,128]{1,0:T(8,128)(2,1)S(1)}, u32[]{:S(2)}, u32[]{:S(2)}) collective-permute-start(bf16[256,128]{1,0:T(8,128)(2,1)S(1)} %get-tuple-element.43), channel_id=1, source_target_pairs={{0,12},{2,14},{4,8},{6,10},{8,4},{10,6},{12,0},{14,2},{1,13},{3,15... | collective-permute-start | bytes 196616 | tf_op jit(solution)/shard_map/ppermute | solution.py:262
  25.2 2.7 %collective-permute-done.4.refs_4_ = bf16[512,128]{1,0:T(8,128)(2,1)S(1)} collective-permute-done((bf16[512,128]{1,0:T(8,128)(2,1)S(1)}, bf16[512,128]{1,0:T(8,128)(2,1)S(1)}, u32[]{:S(2)}, u32[]{:S(2)}) %collective-permute-start.4) | collective-permute-done | bytes 131104 | tf_op jit(solution)/shard_map/ppermute | solution.py:262
  27.9 3.3 %collective-permute-done.5.refs_5_ = bf16[512,128]{1,0:T(8,128)(2,1)S(1)} collective-permute-done((bf16[512,128]{1,0:T(8,128)(2,1)S(1)}, bf16[512,128]{1,0:T(8,128)(2,1)S(1)}, u32[]{:S(2)}, u32[]{:S(2)}) %collective-permute-start.5) | collective-permute-done | bytes 131104 | tf_op jit(solution)/shard_map/ppermute | solution.py:262
  31.2 1.9 %collective-permute-done.6.refs_6_ = bf16[512,128]{1,0:T(8,128)(2,1)S(1)} collective-permute-done((bf16[512,128]{1,0:T(8,128)(2,1)S(1)}, bf16[512,128]{1,0:T(8,128)(2,1)S(1)}, u32[]{:S(2)}, u32[]{:S(2)}) %collective-permute-start.6) | collective-permute-done | bytes 131104 | tf_op jit(solution)/shard_map/ppermute | solution.py:262
  33.1 0.9 %copy-done.2 = bf16[512,128]{1,0:T(8,128)(2,1)S(1)} copy-done((bf16[512,128]{1,0:T(8,128)(2,1)S(1)}, bf16[512,128]{1,0:T(8,128)(2,1)}, u32[]{:S(2)}) %copy-start.2) | copy-done | bytes 131096
  34.0 0.8 %shard_map.70 = (f32[64,128]{1,0:T(8,128)S(1)}, f32[64,128]{1,0:T(8,128)S(1)}) custom-call(s32[1]{0:T(128)} %bitcast.here, bf16[128,4096]{1,0:T(8,128)(2,1)S(1)} %copy-done, bf16[128,4096]{1,0:T(8,128)(2,1)S(1)} %copy-done.1, bf16[512,128]{1,0:T(8,128)(2,1)S(1)} %collective-permute-done.refs_0_.refs_2_, bf16[256,128]{1,0:T(8,128)(2,1)S(1)} %collective-permute-done.1.refs_1_, ...), custom_call_target="tpu_custom_call" | custom-call | bytes 1024 | tf_op jit(solution)/shard_map/pallas_call | solution.py:323
  34.9 4.0 %collective-permute-start.9 = (bf16[256,128]{1,0:T(8,128)(2,1)S(1)}, bf16[256,128]{1,0:T(8,128)(2,1)S(1)}, u32[]{:S(2)}, u32[]{:S(2)}) collective-permute-start(bf16[256,128]{1,0:T(8,128)(2,1)S(1)} %get-tuple-element.48), channel_id=1, source_target_pairs={{0,14},{2,12},{4,10},{6,8},{8,6},{10,4},{12,2},{14,0},{1,15},{3,13... | collective-permute-start | bytes 196616 | tf_op jit(solution)/shard_map/ppermute | solution.py:262
  38.9 0.8 %shard_map.71 = (bf16[256,128]{1,0:T(8,128)(2,1)S(1)}, bf16[256,128]{1,0:T(8,128)(2,1)S(1)}) custom-call(s32[1]{0:T(128)} %bitcast.here, s32[8]{0:T(128)S(1)} %bitcast.7, f32[64,128]{1,0:T(8,128)S(1)} %get-tuple-element.58.mine.d_mine, f32[64,128]{1,0:T(8,128)S(1)} %collective-permute-done.7.other.d_other, bf16[8,512,256]{2,1,0:T(8,128)(2,1)S(1)} %get-tuple-element.38.turned), custom_call_target="tpu_custom_call" | custom-call | bytes 1024 | tf_op jit(solution)/shard_map/pallas_call | solution.py:331
  39.7 0.7 collective-permute-start.10
  40.4 1.8 %collective-permute-done.9.refs_1_ = bf16[256,128]{1,0:T(8,128)(2,1)S(1)} collective-permute-done((bf16[256,128]{1,0:T(8,128)(2,1)S(1)}, bf16[256,128]{1,0:T(8,128)(2,1)S(1)}, u32[]{:S(2)}, u32[]{:S(2)}) %collective-permute-start.9) | collective-permute-done | bytes 65568 | tf_op jit(solution)/shard_map/ppermute | solution.py:262
  42.6 4.1 %collective-permute-start.12 = (bf16[256,128]{1,0:T(8,128)(2,1)S(1)}, bf16[256,128]{1,0:T(8,128)(2,1)S(1)}, u32[]{:S(2)}, u32[]{:S(2)}) collective-permute-start(bf16[256,128]{1,0:T(8,128)(2,1)S(1)} %get-tuple-element.46), channel_id=1, source_target_pairs={{0,14},{2,12},{4,10},{6,8},{8,6},{10,4},{12,2},{14,0},{1,15},{3,13... | collective-permute-start | bytes 196616 | tf_op jit(solution)/shard_map/ppermute | solution.py:262
  46.8 1.2 %shard_map.73 = (bf16[256,128]{1,0:T(8,128)(2,1)S(1)}, bf16[256,128]{1,0:T(8,128)(2,1)S(1)}, bf16[512,128]{1,0:T(8,128)(2,1)S(1)}, bf16[512,128]{1,0:T(8,128)(2,...) custom-call(s32[1]{0:T(128)} %bitcast.here, ...), custom_call_target="tpu_custom_call" | custom-call | bytes 1024 | tf_op jit(solution)/shard_map/pallas_call | solution.py:348
  48.0 0.5 collective-permute-start.13
  48.5 3.1 %collective-permute-start.14 = (bf16[256,128]{1,0:T(8,128)(2,1)S(1)}, bf16[256,128]{1,0:T(8,128)(2,1)S(1)}, u32[]{:S(2)}, u32[]{:S(2)}) collective-permute-start(bf16[256,128]{1,0:T(8,128)(2,1)S(1)} %get-tuple-element.51), channel_id=1, source_target_pairs={{0,14},{2,12},{4,10},{6,8},{8,6},{10,4},{12,2},{14,0},{1,15},{3,13... | collective-permute-start | bytes 196616 | tf_op jit(solution)/shard_map/ppermute | solution.py:262
  51.7 1.7 %collective-permute-start.15 = (bf16[512,128]{1,0:T(8,128)(2,1)S(1)}, bf16[512,128]{1,0:T(8,128)(2,1)S(1)}, u32[]{:S(2)}, u32[]{:S(2)}) collective-permute-start(bf16[512,128]{1,0:T(8,128)(2,1)S(1)} %get-tuple-element.52), channel_id=1, source_target_pairs={{0,2},{2,0},{4,6},{6,4},{8,10},{10,8},{12,14},{14,12},{1,3},{3,1},... | collective-permute-start | bytes 393224 | tf_op jit(solution)/shard_map/ppermute | solution.py:262
  53.4 2.7 %collective-permute-start.17 = (bf16[512,128]{1,0:T(8,128)(2,1)S(1)}, bf16[512,128]{1,0:T(8,128)(2,1)S(1)}, u32[]{:S(2)}, u32[]{:S(2)}) collective-permute-start(bf16[512,128]{1,0:T(8,128)(2,1)S(1)} %get-tuple-element.54), channel_id=1, source_target_pairs={{0,10},{2,8},{4,14},{6,12},{8,2},{10,0},{12,6},{14,4},{1,11},{3,9}... | collective-permute-start | bytes 393224 | tf_op jit(solution)/shard_map/ppermute | solution.py:262
  56.2 3.0 %collective-permute-start.19 = (bf16[512,128]{1,0:T(8,128)(2,1)S(1)}, bf16[512,128]{1,0:T(8,128)(2,1)S(1)}, u32[]{:S(2)}, u32[]{:S(2)}) collective-permute-start(bf16[512,128]{1,0:T(8,128)(2,1)S(1)} %get-tuple-element.56), channel_id=1, source_target_pairs={{0,6},{2,4},{4,2},{6,0},{8,14},{10,12},{12,10},{14,8},{1,7},{3,5},... | collective-permute-start | bytes 393224 | tf_op jit(solution)/shard_map/ppermute | solution.py:262
  59.2 0.9 %copy-done.3 = bf16[512,128]{1,0:T(8,128)(2,1)S(1)} copy-done((bf16[512,128]{1,0:T(8,128)(2,1)S(1)}, bf16[512,128]{1,0:T(8,128)(2,1)}, u32[]{:S(2)}) %copy-start.3) | copy-done | bytes 131096
  60.1 2.0 %shard_map.74 = bf16[128,4096]{1,0:T(8,128)(2,1)} custom-call(s32[1]{0:T(128)} %bitcast.here, s32[8]{0:T(128)S(1)} %bitcast.9, f32[64,128]{1,0:T(8,128)S(1)} %get-tuple-element.58.mine.d_mine, f32[64,128]{1,0:T(8,128)S(1)} %collective-permute-done.7.other.d_other, bf16[256,128]{1,0:T(8,128)(2,1)S(1)} %collective-permute-done.8.refs_0_, ...), custom_call_target="tpu_custom_call" | custom-call | flops 134217728 | bytes 2097152 | tf_op jit(solution)/shard_map/pallas_call | solution.py:358
  62.1 2.0 %collective-permute-done.16.refs_5_ = bf16[512,128]{1,0:T(8,128)(2,1)S(1)} collective-permute-done((bf16[512,128]{1,0:T(8,128)(2,1)S(1)}, bf16[512,128]{1,0:T(8,128)(2,1)S(1)}, u32[]{:S(2)}, u32[]{:S(2)}) %collective-permute-start.16) | collective-permute-done | bytes 131104 | tf_op jit(solution)/shard_map/ppermute | solution.py:262
  64.2 2.5 %collective-permute-done.17.refs_6_ = bf16[512,128]{1,0:T(8,128)(2,1)S(1)} collective-permute-done((bf16[512,128]{1,0:T(8,128)(2,1)S(1)}, bf16[512,128]{1,0:T(8,128)(2,1)S(1)}, u32[]{:S(2)}, u32[]{:S(2)}) %collective-permute-start.17) | collective-permute-done | bytes 131104 | tf_op jit(solution)/shard_map/ppermute | solution.py:262
  66.7 0.5 collective-permute-done.18.refs_7_
  67.1 2.5 %collective-permute-done.19.refs_8_ = bf16[512,128]{1,0:T(8,128)(2,1)S(1)} collective-permute-done((bf16[512,128]{1,0:T(8,128)(2,1)S(1)}, bf16[512,128]{1,0:T(8,128)(2,1)S(1)}, u32[]{:S(2)}, u32[]{:S(2)}) %collective-permute-start.19) | collective-permute-done | bytes 131104 | tf_op jit(solution)/shard_map/ppermute | solution.py:262
  69.7 1.8 %shard_map.75 = bf16[96,512,128]{2,1,0:T(8,128)(2,1)} custom-call(s32[8]{0:T(128)S(1)} %bitcast.12, s32[1]{0:T(128)} %bitcast.here, s32[8]{0:T(128)S(1)} %bitcast.10, bf16[256,128]{1,0:T(8,128)(2,1)S(1)} %collective-permute-done.10.refs_0_, bf16[256,128]{1,0:T(8,128)(2,1)S(1)} %collective-permute-done.12.refs_1_, ...), custom_call_target="tpu_custom_call", output_to_operand_aliasing={{}: (13, {})} | custom-call | bytes 2097152 | tf_op jit(solution)/shard_map/pallas_call | solution.py:367
  (28 shorter events, 1.4 us)
Async XLA Ops:
  0.6 14.0 %copy-start = (bf16[128,4096]{1,0:T(8,128)(2,1)S(1)}, bf16[128,4096]{1,0:T(8,128)(2,1)}, u32[]{:S(2)}) copy-start(bf16[128,4096]{1,0:T(8,128)(2,1)} %x.5) | copy-start | bytes 3145732
  0.6 14.0 %copy-start.1 = (bf16[128,4096]{1,0:T(8,128)(2,1)S(1)}, bf16[128,4096]{1,0:T(8,128)(2,1)}, u32[]{:S(2)}) copy-start(bf16[128,4096]{1,0:T(8,128)(2,1)} %y.3) | copy-start | bytes 3145732
  0.7 38.2 %copy-start.4 = (s32[8,1]{0,1:T(1,128)S(1)}, s32[8,1]{0,1:T(1,128)}, u32[]{:S(2)}) copy-start(s32[8,1]{0,1:T(1,128)} %param.9) | copy-start | bytes 100
  0.7 0.8 %copy-start.5 = (s32[8,1]{0,1:T(1,128)S(1)}, s32[8,1]{0,1:T(1,128)}, u32[]{:S(2)}) copy-start(s32[8,1]{0,1:T(1,128)} %param.8) | copy-start | bytes 100
  4.0 15.5 %collective-permute-start.2 = (bf16[256,128]{1,0:T(8,128)(2,1)S(1)}, bf16[256,128]{1,0:T(8,128)(2,1)S(1)}, u32[]{:S(2)}, u32[]{:S(2)}) collective-permute-start(bf16[256,128]{1,0:T(8,128)(2,1)S(1)} %get-tuple-element.33), channel_id=1, source_target_pairs={{0,14},{2,12},{4,10},{6,8},{8,6},{10,4},{12,2},{14,0},{1,15},{3,13... | collective-permute-start | bytes 196616 | tf_op jit(solution)/shard_map/ppermute | solution.py:262
  10.1 10.7 %collective-permute-start.1 = (bf16[256,128]{1,0:T(8,128)(2,1)S(1)}, bf16[256,128]{1,0:T(8,128)(2,1)S(1)}, u32[]{:S(2)}, u32[]{:S(2)}) collective-permute-start(bf16[256,128]{1,0:T(8,128)(2,1)S(1)} %get-tuple-element.32.after), channel_id=1, source_target_pairs={{0,12},{2,14},{4,8},{6,10},{8,4},{10,6},{12,0},{14,2},{1,13},{3,15... | collective-permute-start | bytes 196616 | tf_op jit(solution)/shard_map/ppermute | solution.py:262
  10.3 11.2 %collective-permute-start = (bf16[512,128]{1,0:T(8,128)(2,1)S(1)}, bf16[512,128]{1,0:T(8,128)(2,1)S(1)}, u32[]{:S(2)}, u32[]{:S(2)}) collective-permute-start(bf16[512,128]{1,0:T(8,128)(2,1)S(1)} %get-tuple-element.31), channel_id=1, source_target_pairs={{0,2},{2,0},{4,6},{6,4},{8,10},{10,8},{12,14},{14,12},{1,3},{3,1},... | collective-permute-start | bytes 393224 | tf_op jit(solution)/shard_map/ppermute | solution.py:262
  10.7 14.5 %collective-permute-start.3 = (bf16[512,128]{1,0:T(8,128)(2,1)S(1)}, bf16[512,128]{1,0:T(8,128)(2,1)S(1)}, u32[]{:S(2)}, u32[]{:S(2)}) collective-permute-start(bf16[512,128]{1,0:T(8,128)(2,1)S(1)} %get-tuple-element.34), channel_id=1, source_target_pairs={{0,8},{2,10},{4,12},{6,14},{8,0},{10,2},{12,4},{14,6},{1,9},{3,11}... | collective-permute-start | bytes 393224 | tf_op jit(solution)/shard_map/ppermute | solution.py:262
  11.6 16.3 %collective-permute-start.4 = (bf16[512,128]{1,0:T(8,128)(2,1)S(1)}, bf16[512,128]{1,0:T(8,128)(2,1)S(1)}, u32[]{:S(2)}, u32[]{:S(2)}) collective-permute-start(bf16[512,128]{1,0:T(8,128)(2,1)S(1)} %get-tuple-element.35), channel_id=1, source_target_pairs={{0,10},{2,8},{4,14},{6,12},{8,2},{10,0},{12,6},{14,4},{1,11},{3,9}... | collective-permute-start | bytes 393224 | tf_op jit(solution)/shard_map/ppermute | solution.py:262
  19.5 11.7 %collective-permute-start.5 = (bf16[512,128]{1,0:T(8,128)(2,1)S(1)}, bf16[512,128]{1,0:T(8,128)(2,1)S(1)}, u32[]{:S(2)}, u32[]{:S(2)}) collective-permute-start(bf16[512,128]{1,0:T(8,128)(2,1)S(1)} %get-tuple-element.36), channel_id=1, source_target_pairs={{0,4},{2,6},{4,0},{6,2},{8,12},{10,14},{12,8},{14,10},{1,5},{3,7},... | collective-permute-start | bytes 393224 | tf_op jit(solution)/shard_map/ppermute | solution.py:262
  20.8 12.3 %collective-permute-start.6 = (bf16[512,128]{1,0:T(8,128)(2,1)S(1)}, bf16[512,128]{1,0:T(8,128)(2,1)S(1)}, u32[]{:S(2)}, u32[]{:S(2)}) collective-permute-start(bf16[512,128]{1,0:T(8,128)(2,1)S(1)} %get-tuple-element.39), channel_id=1, source_target_pairs={{0,6},{2,4},{4,2},{6,0},{8,14},{10,12},{12,10},{14,8},{1,7},{3,5},... | collective-permute-start | bytes 393224 | tf_op jit(solution)/shard_map/ppermute | solution.py:262
  21.5 17.4 %collective-permute-start.8 = (bf16[256,128]{1,0:T(8,128)(2,1)S(1)}, bf16[256,128]{1,0:T(8,128)(2,1)S(1)}, u32[]{:S(2)}, u32[]{:S(2)}) collective-permute-start(bf16[256,128]{1,0:T(8,128)(2,1)S(1)} %get-tuple-element.43), channel_id=1, source_target_pairs={{0,12},{2,14},{4,8},{6,10},{8,4},{10,6},{12,0},{14,2},{1,13},{3,15... | collective-permute-start | bytes 196616 | tf_op jit(solution)/shard_map/ppermute | solution.py:262
  33.1 0.9 %copy-start.2 = (bf16[512,128]{1,0:T(8,128)(2,1)S(1)}, bf16[512,128]{1,0:T(8,128)(2,1)}, u32[]{:S(2)}) copy-start(bf16[512,128]{1,0:T(8,128)(2,1)} %get-tuple-element.40.refs_7_) | copy-start | bytes 393220
  34.8 4.1 %collective-permute-start.7 = (f32[64,128]{1,0:T(8,128)S(1)}, f32[64,128]{1,0:T(8,128)S(1)}, u32[]{:S(2)}, u32[]{:S(2)}) collective-permute-start(f32[64,128]{1,0:T(8,128)S(1)} %get-tuple-element.58.mine.d_mine), channel_id=1, source_target_pairs={{0,1},{1,0},{2,3},{3,2},{4,5},{5,4},{6,7},{7,6},{8,9},{9,8},{10,11... | collective-permute-start | bytes 98312 | tf_op jit(solution)/shard_map/ppermute | solution.py:273
  34.9 7.3 %collective-permute-start.9 = (bf16[256,128]{1,0:T(8,128)(2,1)S(1)}, bf16[256,128]{1,0:T(8,128)(2,1)S(1)}, u32[]{:S(2)}, u32[]{:S(2)}) collective-permute-start(bf16[256,128]{1,0:T(8,128)(2,1)S(1)} %get-tuple-element.48), channel_id=1, source_target_pairs={{0,14},{2,12},{4,10},{6,8},{8,6},{10,4},{12,2},{14,0},{1,15},{3,13... | collective-permute-start | bytes 196616 | tf_op jit(solution)/shard_map/ppermute | solution.py:262
  39.7 7.0 %collective-permute-start.10 = (bf16[256,128]{1,0:T(8,128)(2,1)S(1)}, bf16[256,128]{1,0:T(8,128)(2,1)S(1)}, u32[]{:S(2)}, u32[]{:S(2)}) collective-permute-start(bf16[256,128]{1,0:T(8,128)(2,1)S(1)} %get-tuple-element.45), channel_id=1, source_target_pairs={{0,12},{2,14},{4,8},{6,10},{8,4},{10,6},{12,0},{14,2},{1,13},{3,15... | collective-permute-start | bytes 196616 | tf_op jit(solution)/shard_map/ppermute | solution.py:262
  42.5 4.2 %collective-permute-start.11 = (f32[64,128]{1,0:T(8,128)S(1)}, f32[64,128]{1,0:T(8,128)S(1)}, u32[]{:S(2)}, u32[]{:S(2)}) collective-permute-start(f32[64,128]{1,0:T(8,128)S(1)} %shard_map.72.mine), channel_id=1, source_target_pairs={{0,1},{1,0},{2,3},{3,2},{4,5},{5,4},{6,7},{7,6},{8,9},{9,8},{10,11... | collective-permute-start | bytes 98312 | tf_op jit(solution)/shard_map/ppermute | solution.py:273
  42.6 10.7 %collective-permute-start.12 = (bf16[256,128]{1,0:T(8,128)(2,1)S(1)}, bf16[256,128]{1,0:T(8,128)(2,1)S(1)}, u32[]{:S(2)}, u32[]{:S(2)}) collective-permute-start(bf16[256,128]{1,0:T(8,128)(2,1)S(1)} %get-tuple-element.46), channel_id=1, source_target_pairs={{0,14},{2,12},{4,10},{6,8},{8,6},{10,4},{12,2},{14,0},{1,15},{3,13... | collective-permute-start | bytes 196616 | tf_op jit(solution)/shard_map/ppermute | solution.py:262
  48.0 8.1 %collective-permute-start.13 = (bf16[256,128]{1,0:T(8,128)(2,1)S(1)}, bf16[256,128]{1,0:T(8,128)(2,1)S(1)}, u32[]{:S(2)}, u32[]{:S(2)}) collective-permute-start(bf16[256,128]{1,0:T(8,128)(2,1)S(1)} %get-tuple-element.50), channel_id=1, source_target_pairs={{0,12},{2,14},{4,8},{6,10},{8,4},{10,6},{12,0},{14,2},{1,13},{3,15... | collective-permute-start | bytes 196616 | tf_op jit(solution)/shard_map/ppermute | solution.py:262
  48.5 7.7 %collective-permute-start.14 = (bf16[256,128]{1,0:T(8,128)(2,1)S(1)}, bf16[256,128]{1,0:T(8,128)(2,1)S(1)}, u32[]{:S(2)}, u32[]{:S(2)}) collective-permute-start(bf16[256,128]{1,0:T(8,128)(2,1)S(1)} %get-tuple-element.51), channel_id=1, source_target_pairs={{0,14},{2,12},{4,10},{6,8},{8,6},{10,4},{12,2},{14,0},{1,15},{3,13... | collective-permute-start | bytes 196616 | tf_op jit(solution)/shard_map/ppermute | solution.py:262
  51.7 10.4 %collective-permute-start.15 = (bf16[512,128]{1,0:T(8,128)(2,1)S(1)}, bf16[512,128]{1,0:T(8,128)(2,1)S(1)}, u32[]{:S(2)}, u32[]{:S(2)}) collective-permute-start(bf16[512,128]{1,0:T(8,128)(2,1)S(1)} %get-tuple-element.52), channel_id=1, source_target_pairs={{0,2},{2,0},{4,6},{6,4},{8,10},{10,8},{12,14},{14,12},{1,3},{3,1},... | collective-permute-start | bytes 393224 | tf_op jit(solution)/shard_map/ppermute | solution.py:262
  53.4 10.8 %collective-permute-start.16 = (bf16[512,128]{1,0:T(8,128)(2,1)S(1)}, bf16[512,128]{1,0:T(8,128)(2,1)S(1)}, u32[]{:S(2)}, u32[]{:S(2)}) collective-permute-start(bf16[512,128]{1,0:T(8,128)(2,1)S(1)} %get-tuple-element.53), channel_id=1, source_target_pairs={{0,8},{2,10},{4,12},{6,14},{8,0},{10,2},{12,4},{14,6},{1,9},{3,11}... | collective-permute-start | bytes 393224 | tf_op jit(solution)/shard_map/ppermute | solution.py:262
  53.4 13.3 %collective-permute-start.17 = (bf16[512,128]{1,0:T(8,128)(2,1)S(1)}, bf16[512,128]{1,0:T(8,128)(2,1)S(1)}, u32[]{:S(2)}, u32[]{:S(2)}) collective-permute-start(bf16[512,128]{1,0:T(8,128)(2,1)S(1)} %get-tuple-element.54), channel_id=1, source_target_pairs={{0,10},{2,8},{4,14},{6,12},{8,2},{10,0},{12,6},{14,4},{1,11},{3,9}... | collective-permute-start | bytes 393224 | tf_op jit(solution)/shard_map/ppermute | solution.py:262
  56.1 11.1 %collective-permute-start.18 = (bf16[512,128]{1,0:T(8,128)(2,1)S(1)}, bf16[512,128]{1,0:T(8,128)(2,1)S(1)}, u32[]{:S(2)}, u32[]{:S(2)}) collective-permute-start(bf16[512,128]{1,0:T(8,128)(2,1)S(1)} %get-tuple-element.55), channel_id=1, source_target_pairs={{0,4},{2,6},{4,0},{6,2},{8,12},{10,14},{12,8},{14,10},{1,5},{3,7},... | collective-permute-start | bytes 393224 | tf_op jit(solution)/shard_map/ppermute | solution.py:262
  56.2 13.4 %collective-permute-start.19 = (bf16[512,128]{1,0:T(8,128)(2,1)S(1)}, bf16[512,128]{1,0:T(8,128)(2,1)S(1)}, u32[]{:S(2)}, u32[]{:S(2)}) collective-permute-start(bf16[512,128]{1,0:T(8,128)(2,1)S(1)} %get-tuple-element.56), channel_id=1, source_target_pairs={{0,6},{2,4},{4,2},{6,0},{8,14},{10,12},{12,10},{14,8},{1,7},{3,5},... | collective-permute-start | bytes 393224 | tf_op jit(solution)/shard_map/ppermute | solution.py:262
  59.2 0.9 %copy-start.3 = (bf16[512,128]{1,0:T(8,128)(2,1)S(1)}, bf16[512,128]{1,0:T(8,128)(2,1)}, u32[]{:S(2)}) copy-start(bf16[512,128]{1,0:T(8,128)(2,1)} %get-tuple-element.40.refs_7_) | copy-start | bytes 393220

commit v8 on v5

--- a/solution.py
+++ b/solution.py
@@ -64,6 +64,13 @@
         copy.wait()
 
 
+def arrived(ref, me, k):
+    if len(ref.shape) == 2:
+        return ref[...]
+    top = 1 << (k.bit_length() - 1)
+    return ref[jnp.where((me & top) > 0, 0, 1)]
+
+
 def rank_kernel(peers, here, x, y, *refs):
     pairs, out = refs[: len(peers)], refs[len(peers)]
     rows, width = pairs[0].shape
@@ -72,8 +79,9 @@
     y_rank = jnp.zeros((tokens, width), jnp.float32)
     for n, k in enumerate(peers):
         columns = pl.ds(pl.multiple_of((here[0] ^ k) * rows, rows), rows)
-        x_rank += jnp.dot(x[:, columns], pairs[n][...], preferred_element_type=jnp.float32)
-        y_rank += jnp.dot(y[:, columns], pairs[n][...], preferred_element_type=jnp.float32)
+        pair = arrived(pairs[n], here[0], k)
+        x_rank += jnp.dot(x[:, columns], pair, preferred_element_type=jnp.float32)
+        y_rank += jnp.dot(y[:, columns], pair, preferred_element_type=jnp.float32)
     out[...] = jnp.where(low_lanes(tokens, width), x_rank, y_rank)
 
 
@@ -110,7 +118,7 @@
     for n, k in enumerate(peers):
         columns = pl.ds(pl.multiple_of((me ^ k) * rows, rows), rows)
         out[:, columns] = lax.dot_general(
-            ranks, pairs[n][...], (((1,), (1,)), ((), ())), preferred_element_type=jnp.float32
+            ranks, arrived(pairs[n], me, k), (((1,), (1,)), ((), ())), preferred_element_type=jnp.float32
         ).astype(jnp.bfloat16)
 
 
@@ -120,6 +128,10 @@
     out, total, held, sems = refs[owners + 1 :]
     blocks = [here[0] ^ k for k in peers]
     copies, firsts = [], []
+
+    def value(n):
+        return arrived(pieces[n], here[0], peers[n]).astype(jnp.float32)
+
     for k in range(owners):
         adapter = ids[blocks[k]]
         copies.append(pltpu.make_async_copy(held.at[k], out.at[adapter], sems.at[k]))
@@ -136,18 +148,18 @@
 
         @pl.when(firsts[k] & jnp.logical_not(later))
         def _():
-            store(pieces[k][...].astype(jnp.float32), lengths[blocks[k]])
+            store(value(k), lengths[blocks[k]])
 
         @pl.when(firsts[k] & later)
         def _():
-            total[...] = pieces[k][...].astype(jnp.float32)
+            total[...] = value(k)
             count = lengths[blocks[k]]
             for other in range(k + 1, owners):
                 count += jnp.where(same[other], lengths[blocks[other]], 0)
 
                 @pl.when(same[other])
                 def _():
-                    total[...] += pieces[other][...].astype(jnp.float32)
+                    total[...] += value(other)
 
             store(total[...], count)
 
@@ -156,14 +168,19 @@
 
 
 def peer_order(owners):
-    near = list(range(1, owners // 2))
-    return (0, *range(owners // 2, owners), *near[:1], *near[:0:-1])
+    return (0, *range(owners // 2, owners), *range(1, owners // 2))
 
 
 def exchange(pieces, peers):
     out = [pieces[0]]
+    owners = len(peers)
     for k, piece in zip(peers[1:], pieces[1:]):
-        out.append(lax.ppermute(piece, "dp", [(i, i ^ k) for i in range(len(peers))]))
+        pairs = [[i, i ^ k] for i in range(owners)]
+        if k < owners // 2:
+            groups = [pair for pair in pairs if pair[0] < pair[1]]
+            out.append(lax.all_gather(piece, "dp", axis_index_groups=groups))
+        else:
+            out.append(lax.ppermute(piece, "dp", pairs))
     return out
 
 
@@ -208,7 +225,7 @@
         [in_vmem, in_hbm],
         [pltpu.VMEM((step, rows, width), bf16), pltpu.SemaphoreType.DMA((count // step,))],
         moved=4 * token_bytes + 2 * count * rows * width,
-    )(pairs[5], activations, cotangent)
+    )(sent[0], activations, cotangent)
     *pairs, turned, blank = lax.optimization_barrier((*pairs, turned, blank))
 
     mine = call(

time: 63.8 us -> 74.5 us (1.17)
  blocking collectives: 0 us -> 38.9 us
  waiting for transfers between devices: 26.1 us -> 1.26 us
  starting transfers between devices: 23 us -> 19.6 us
    all_gather x0 -> x6, blocking collectives: none -> 38.9 us  [exchange(): out.append(lax.all_gather(piece, 'dp', axis_index_groups=groups))]
    ppermute x14 -> x8, waiting for transfers between devices: 24.8 us -> 0.02 us  [exchange(): out.append(lax.ppermute(piece, 'dp', pairs))]
    ppermute x14 -> x8, starting transfers between devices: 22.9 us -> 19.5 us  [exchange(): out.append(lax.ppermute(piece, 'dp', pairs))]
  transfers between devices with their start and end apart: 15 -> 9, of which waited for: 6 -> 1; matrix products, arithmetic and copies ran while one was open for 0% -> 0% of each run, Pallas kernels for 11% -> 9%
where the time goes in v8:
time: 74.5 us; the launch traced here: 74.3 us
  blocking collectives  38.9 us (52%)
  starting transfers between devices  19.6 us (26%)
  Pallas kernels  13 us (17%)
  waiting for transfers between devices  1.26 us (2%)
  local copies, waits for them, and re-layouts  0.8 us (1%)
    all_gather x6, blocking collectives, exchange(): out.append(lax.all_gather(piece, 'dp', axis_index_groups=groups))  38.9 us
    ppermute x8, starting transfers between devices, exchange(): out.append(lax.ppermute(piece, 'dp', pairs))  19.5 us
    pallas_call x1, Pallas kernels, with_kernels(): call(functools.partial(prep_kernel, rows), [jax.ShapeDtypeStruct((owners,...  4.8 us
    pallas_call x1, Pallas kernels, with_kernels(): call(functools.partial(gather_kernel, peers), pair_shapes, [in_smem, in_s...  2.55 us
    pallas_call x1, Pallas kernels, with_kernels(): call(functools.partial(input_kernel, peers, scale), jax.ShapeDtypeStruct(...  1.99 us
    pallas_call x1, Pallas kernels, with_kernels(): call(functools.partial(merge_kernel, peers), jax.ShapeDtypeStruct(table.s...  1.65 us
  transfers between devices with their start and end apart: 9, of which 1 were waited for; matrix products, arithmetic and copies ran while one was open for 0% of the time, Pallas kernels for 9%

profile of v8, /device:TPU:0, one launch (start us, length us, event | category | flops | bytes accessed | tf_op | source)
XLA Modules:
  0.0 74.3 jit_solution(9946089956666482306)
XLA Ops:
  0.7 0.0 copy-start.3
  0.7 0.8 %copy-done.3 = s32[8,1]{0,1:T(1,128)S(1)} copy-done((s32[8,1]{0,1:T(1,128)S(1)}, s32[8,1]{0,1:T(1,128)}, u32[]{:S(2)}) %copy-start.3) | copy-done | bytes 56
  1.5 2.5 %shard_map.68 = (bf16[512,128]{1,0:T(8,128)(2,1)S(1)}, bf16[512,128]{1,0:T(8,128)(2,1)S(1)}, bf16[512,128]{1,0:T(8,128)(2,1)S(1)}, bf16[512,128]{1,0:T(8,128)(2,...) custom-call(s32[8]{0:T(128)S(1)} %bitcast.25, ...), custom_call_target="tpu_custom_call" | custom-call | bytes 2097152 | tf_op jit(solution)/shard_map/pallas_call | solution.py:206
  4.0 4.1 %collective-permute-start = (bf16[512,128]{1,0:T(8,128)(2,1)S(1)}, bf16[512,128]{1,0:T(8,128)(2,1)S(1)}, u32[]{:S(2)}, u32[]{:S(2)}) collective-permute-start(bf16[512,128]{1,0:T(8,128)(2,1)S(1)} %get-tuple-element.31), channel_id=1, source_target_pairs={{0,8},{2,10},{4,12},{6,14},{8,0},{10,2},{12,4},{14,6},{1,9},{3,11}... | collective-permute-start | bytes 393224 | tf_op jit(solution)/shard_map/ppermute | solution.py:183
  8.1 1.3 %collective-permute-start.1 = (bf16[512,128]{1,0:T(8,128)(2,1)S(1)}, bf16[512,128]{1,0:T(8,128)(2,1)S(1)}, u32[]{:S(2)}, u32[]{:S(2)}) collective-permute-start(bf16[512,128]{1,0:T(8,128)(2,1)S(1)} %get-tuple-element.32), channel_id=1, source_target_pairs={{0,10},{2,8},{4,14},{6,12},{8,2},{10,0},{12,6},{14,4},{1,11},{3,9}... | collective-permute-start | bytes 393224 | tf_op jit(solution)/shard_map/ppermute | solution.py:183
  9.4 3.6 %collective-permute-start.2 = (bf16[512,128]{1,0:T(8,128)(2,1)S(1)}, bf16[512,128]{1,0:T(8,128)(2,1)S(1)}, u32[]{:S(2)}, u32[]{:S(2)}) collective-permute-start(bf16[512,128]{1,0:T(8,128)(2,1)S(1)} %get-tuple-element.33), channel_id=1, source_target_pairs={{0,12},{2,14},{4,8},{6,10},{8,4},{10,6},{12,0},{14,2},{1,13},{3,15... | collective-permute-start | bytes 393224 | tf_op jit(solution)/shard_map/ppermute | solution.py:183
  13.0 0.0 collective-permute-start.3
  13.0 6.1 %all-gather = bf16[1024,128]{1,0:T(8,128)(2,1)S(1)} all-gather(bf16[512,128]{1,0:T(8,128)(2,1)S(1)} %get-tuple-element.35), channel_id=2, replica_groups={{0,2},{4,6},{8,10},{12,14},{1,3},{5,7},{9,11},{13,15},{16,18},{20,22},{..., dimensions={0}, use_global_device_ids=true | all-gather | bytes 393216 | tf_op jit(solution)/shard_map/all_gather | solution.py:181
  19.1 4.8 %shard_map.69 = (bf16[8,512,256]{2,1,0:T(8,128)(2,1)S(1)}, bf16[96,512,128]{2,1,0:T(8,128)(2,1)}) custom-call(bf16[512,128]{1,0:T(8,128)(2,1)S(1)} %get-tuple-element.40.after.refs_0_, bf16[128,4096]{1,0:T(8,128)(2,1)S(1)} %copy-done, bf16[128,4096]{1,0:T(8,128)(2,1)S(1)} %copy-done.1), custom_call_target="tpu_custom_call" | custom-call | bytes 16777216 | tf_op jit(solution)/shard_map/pallas_call | solution.py:218
  23.9 5.6 %all-gather.1 = bf16[1024,128]{1,0:T(8,128)(2,1)S(1)} all-gather(bf16[512,128]{1,0:T(8,128)(2,1)S(1)} %get-tuple-element.36), channel_id=3, replica_groups={{0,4},{2,6},{8,12},{10,14},{1,5},{3,7},{9,13},{11,15},{16,20},{18,22},{..., dimensions={0}, use_global_device_ids=true | all-gather | bytes 393216 | tf_op jit(solution)/shard_map/all_gather | solution.py:181
  29.5 6.7 %all-gather.2 = bf16[1024,128]{1,0:T(8,128)(2,1)S(1)} all-gather(bf16[512,128]{1,0:T(8,128)(2,1)} %get-tuple-element.37), channel_id=4, replica_groups={{0,6},{2,4},{8,14},{10,12},{1,7},{3,5},{9,15},{11,13},{16,22},{18,20},{..., dimensions={0}, use_global_device_ids=true | all-gather | bytes 393216 | tf_op jit(solution)/shard_map/all_gather | solution.py:181
  36.3 0.0 collective-permute-done.refs_1_
  36.3 0.0 collective-permute-done.1.refs_2_
  36.3 0.0 collective-permute-done.2.refs_3_
  36.3 0.0 collective-permute-done.3.refs_4_
  36.3 0.7 shard_map.70.mine
  37.0 0.1 collective-permute-start.4
  37.1 1.2 %collective-permute-done.4.other = f32[128,128]{1,0:T(8,128)S(1)} collective-permute-done((f32[128,128]{1,0:T(8,128)S(1)}, f32[128,128]{1,0:T(8,128)S(1)}, u32[]{:S(2)}, u32[]{:S(2)}) %collective-permute-start.4) | collective-permute-done | bytes 65568 | tf_op jit(solution)/shard_map/ppermute | solution.py:189
  38.4 1.3 %shard_map.72 = (bf16[512,128]{1,0:T(8,128)(2,1)S(1)}, bf16[512,128]{1,0:T(8,128)(2,1)S(1)}, bf16[512,128]{1,0:T(8,128)(2,1)S(1)}, bf16[512,128]{1,0:T(8,128)(2,...) custom-call(s32[1]{0:T(128)} %bitcast.here, ...), custom_call_target="tpu_custom_call" | custom-call | flops 268435456 | bytes 3145728 | tf_op jit(solution)/shard_map/pallas_call | solution.py:241
  39.7 5.3 %collective-permute-start.5 = (bf16[512,128]{1,0:T(8,128)(2,1)S(1)}, bf16[512,128]{1,0:T(8,128)(2,1)S(1)}, u32[]{:S(2)}, u32[]{:S(2)}) collective-permute-start(bf16[512,128]{1,0:T(8,128)(2,1)S(1)} %get-tuple-element.50), channel_id=1, source_target_pairs={{0,8},{2,10},{4,12},{6,14},{8,0},{10,2},{12,4},{14,6},{1,9},{3,11}... | collective-permute-start | bytes 393224 | tf_op jit(solution)/shard_map/ppermute | solution.py:183
  45.0 0.5 collective-permute-start.6
  45.5 4.7 %collective-permute-start.7 = (bf16[512,128]{1,0:T(8,128)(2,1)S(1)}, bf16[512,128]{1,0:T(8,128)(2,1)S(1)}, u32[]{:S(2)}, u32[]{:S(2)}) collective-permute-start(bf16[512,128]{1,0:T(8,128)(2,1)S(1)} %get-tuple-element.52), channel_id=1, source_target_pairs={{0,12},{2,14},{4,8},{6,10},{8,4},{10,6},{12,0},{14,2},{1,13},{3,15... | collective-permute-start | bytes 393224 | tf_op jit(solution)/shard_map/ppermute | solution.py:183
  50.2 0.0 collective-permute-start.8
  50.2 5.6 %all-gather.3 = bf16[1024,128]{1,0:T(8,128)(2,1)S(1)} all-gather(bf16[512,128]{1,0:T(8,128)(2,1)S(1)} %get-tuple-element.54), channel_id=5, replica_groups={{0,2},{4,6},{8,10},{12,14},{1,3},{5,7},{9,11},{13,15},{16,18},{20,22},{..., dimensions={0}, use_global_device_ids=true | all-gather | bytes 393216 | tf_op jit(solution)/shard_map/all_gather | solution.py:181
  55.8 2.0 %shard_map.71 = bf16[128,4096]{1,0:T(8,128)(2,1)} custom-call(s32[1]{0:T(128)} %bitcast.here, s32[8]{0:T(128)S(1)} %bitcast.23, f32[128,128]{1,0:T(8,128)S(1)} %shard_map.70.mine, f32[128,128]{1,0:T(8,128)S(1)} %collective-permute-done.4.other, bf16[512,128]{1,0:T(8,128)(2,1)S(1)} %get-tuple-element.40.after.refs_0_, ...), custom_call_target="tpu_custom_call" | custom-call | flops 134217728 | bytes 2097152 | tf_op jit(solution)/shard_map/pallas_call | solution.py:251
  57.8 7.8 %all-gather.4 = bf16[1024,128]{1,0:T(8,128)(2,1)S(1)} all-gather(bf16[512,128]{1,0:T(8,128)(2,1)S(1)} %get-tuple-element.55), channel_id=6, replica_groups={{0,4},{2,6},{8,12},{10,14},{1,5},{3,7},{9,13},{11,15},{16,20},{18,22},{..., dimensions={0}, use_global_device_ids=true | all-gather | bytes 393216 | tf_op jit(solution)/shard_map/all_gather | solution.py:181
  65.6 7.0 %all-gather.5 = bf16[1024,128]{1,0:T(8,128)(2,1)S(1)} all-gather(bf16[512,128]{1,0:T(8,128)(2,1)S(1)} %get-tuple-element.56), channel_id=7, replica_groups={{0,6},{2,4},{8,14},{10,12},{1,7},{3,5},{9,15},{11,13},{16,22},{18,20},{..., dimensions={0}, use_global_device_ids=true | all-gather | bytes 393216 | tf_op jit(solution)/shard_map/all_gather | solution.py:181
  72.6 0.0 collective-permute-done.5.refs_1_
  72.6 0.0 collective-permute-done.6.refs_2_
  72.6 0.0 collective-permute-done.7.refs_3_
  72.6 0.0 collective-permute-done.8.refs_4_
  72.6 1.7 %shard_map.73 = bf16[96,512,128]{2,1,0:T(8,128)(2,1)} custom-call(s32[8]{0:T(128)S(1)} %bitcast.26, s32[1]{0:T(128)} %bitcast.here, s32[8]{0:T(128)S(1)} %bitcast.24, bf16[512,128]{1,0:T(8,128)(2,1)S(1)} %get-tuple-element.49.refs_0_, bf16[512,128]{1,0:T(8,128)(2,1)S(1)} %collective-permute-done.5.refs_1_, ...), custom_call_target="tpu_custom_call", output_to_operand_aliasing={{}: (11, {})} | custom-call | bytes 2097152 | tf_op jit(solution)/shard_map/pallas_call | solution.py:260
  (6 shorter events, 0.0 us)
Async XLA Ops:
  0.6 18.5 %copy-start.1 = (bf16[128,4096]{1,0:T(8,128)(2,1)S(1)}, bf16[128,4096]{1,0:T(8,128)(2,1)}, u32[]{:S(2)}) copy-start(bf16[128,4096]{1,0:T(8,128)(2,1)} %y.3) | copy-start | bytes 3145732
  0.6 18.4 %copy-start = (bf16[128,4096]{1,0:T(8,128)(2,1)S(1)}, bf16[128,4096]{1,0:T(8,128)(2,1)}, u32[]{:S(2)}) copy-start(bf16[128,4096]{1,0:T(8,128)(2,1)} %x.3) | copy-start | bytes 3145732
  0.7 37.7 %copy-start.2 = (s32[8,1]{0,1:T(1,128)S(1)}, s32[8,1]{0,1:T(1,128)}, u32[]{:S(2)}) copy-start(s32[8,1]{0,1:T(1,128)} %param.9) | copy-start | bytes 100
  0.7 0.8 %copy-start.3 = (s32[8,1]{0,1:T(1,128)S(1)}, s32[8,1]{0,1:T(1,128)}, u32[]{:S(2)}) copy-start(s32[8,1]{0,1:T(1,128)} %param.8) | copy-start | bytes 100
  4.0 32.3 %collective-permute-start = (bf16[512,128]{1,0:T(8,128)(2,1)S(1)}, bf16[512,128]{1,0:T(8,128)(2,1)S(1)}, u32[]{:S(2)}, u32[]{:S(2)}) collective-permute-start(bf16[512,128]{1,0:T(8,128)(2,1)S(1)} %get-tuple-element.31), channel_id=1, source_target_pairs={{0,8},{2,10},{4,12},{6,14},{8,0},{10,2},{12,4},{14,6},{1,9},{3,11}... | collective-permute-start | bytes 393224 | tf_op jit(solution)/shard_map/ppermute | solution.py:183
  8.1 28.2 %collective-permute-start.1 = (bf16[512,128]{1,0:T(8,128)(2,1)S(1)}, bf16[512,128]{1,0:T(8,128)(2,1)S(1)}, u32[]{:S(2)}, u32[]{:S(2)}) collective-permute-start(bf16[512,128]{1,0:T(8,128)(2,1)S(1)} %get-tuple-element.32), channel_id=1, source_target_pairs={{0,10},{2,8},{4,14},{6,12},{8,2},{10,0},{12,6},{14,4},{1,11},{3,9}... | collective-permute-start | bytes 393224 | tf_op jit(solution)/shard_map/ppermute | solution.py:183
  9.4 26.9 %collective-permute-start.2 = (bf16[512,128]{1,0:T(8,128)(2,1)S(1)}, bf16[512,128]{1,0:T(8,128)(2,1)S(1)}, u32[]{:S(2)}, u32[]{:S(2)}) collective-permute-start(bf16[512,128]{1,0:T(8,128)(2,1)S(1)} %get-tuple-element.33), channel_id=1, source_target_pairs={{0,12},{2,14},{4,8},{6,10},{8,4},{10,6},{12,0},{14,2},{1,13},{3,15... | collective-permute-start | bytes 393224 | tf_op jit(solution)/shard_map/ppermute | solution.py:183
  13.0 23.3 %collective-permute-start.3 = (bf16[512,128]{1,0:T(8,128)(2,1)S(1)}, bf16[512,128]{1,0:T(8,128)(2,1)S(1)}, u32[]{:S(2)}, u32[]{:S(2)}) collective-permute-start(bf16[512,128]{1,0:T(8,128)(2,1)S(1)} %get-tuple-element.34), channel_id=1, source_target_pairs={{0,14},{2,12},{4,10},{6,8},{8,6},{10,4},{12,2},{14,0},{1,15},{3,13... | collective-permute-start | bytes 393224 | tf_op jit(solution)/shard_map/ppermute | solution.py:183
  37.0 1.3 %collective-permute-start.4 = (f32[128,128]{1,0:T(8,128)S(1)}, f32[128,128]{1,0:T(8,128)S(1)}, u32[]{:S(2)}, u32[]{:S(2)}) collective-permute-start(f32[128,128]{1,0:T(8,128)S(1)} %shard_map.70.mine), channel_id=1, source_target_pairs={{0,1},{1,0},{2,3},{3,2},{4,5},{5,4},{6,7},{7,6},{8,9},{9,8},{10,11... | collective-permute-start | bytes 196616 | tf_op jit(solution)/shard_map/ppermute | solution.py:189
  39.7 32.9 %collective-permute-start.5 = (bf16[512,128]{1,0:T(8,128)(2,1)S(1)}, bf16[512,128]{1,0:T(8,128)(2,1)S(1)}, u32[]{:S(2)}, u32[]{:S(2)}) collective-permute-start(bf16[512,128]{1,0:T(8,128)(2,1)S(1)} %get-tuple-element.50), channel_id=1, source_target_pairs={{0,8},{2,10},{4,12},{6,14},{8,0},{10,2},{12,4},{14,6},{1,9},{3,11}... | collective-permute-start | bytes 393224 | tf_op jit(solution)/shard_map/ppermute | solution.py:183
  45.0 27.7 %collective-permute-start.6 = (bf16[512,128]{1,0:T(8,128)(2,1)S(1)}, bf16[512,128]{1,0:T(8,128)(2,1)S(1)}, u32[]{:S(2)}, u32[]{:S(2)}) collective-permute-start(bf16[512,128]{1,0:T(8,128)(2,1)S(1)} %get-tuple-element.51), channel_id=1, source_target_pairs={{0,10},{2,8},{4,14},{6,12},{8,2},{10,0},{12,6},{14,4},{1,11},{3,9}... | collective-permute-start | bytes 393224 | tf_op jit(solution)/shard_map/ppermute | solution.py:183
  45.5 27.2 %collective-permute-start.7 = (bf16[512,128]{1,0:T(8,128)(2,1)S(1)}, bf16[512,128]{1,0:T(8,128)(2,1)S(1)}, u32[]{:S(2)}, u32[]{:S(2)}) collective-permute-start(bf16[512,128]{1,0:T(8,128)(2,1)S(1)} %get-tuple-element.52), channel_id=1, source_target_pairs={{0,12},{2,14},{4,8},{6,10},{8,4},{10,6},{12,0},{14,2},{1,13},{3,15... | collective-permute-start | bytes 393224 | tf_op jit(solution)/shard_map/ppermute | solution.py:183
  50.2 22.4 %collective-permute-start.8 = (bf16[512,128]{1,0:T(8,128)(2,1)S(1)}, bf16[512,128]{1,0:T(8,128)(2,1)S(1)}, u32[]{:S(2)}, u32[]{:S(2)}) collective-permute-start(bf16[512,128]{1,0:T(8,128)(2,1)S(1)} %get-tuple-element.53), channel_id=1, source_target_pairs={{0,14},{2,12},{4,10},{6,8},{8,6},{10,4},{12,2},{14,0},{1,15},{3,13... | collective-permute-start | bytes 393224 | tf_op jit(solution)/shard_map/ppermute | solution.py:183

commit v9 on v7

--- a/solution.py
+++ b/solution.py
@@ -8,6 +8,11 @@
 from jax.sharding import PartitionSpec as P
 
 adapter_alpha = 128.0
+RANK_ORDER = ((False, 1), (False, 2), (True, 6), (True, 7), (False, 4), (False, 5))
+MERGE_ORDER = (("both", 1), ("both", 2), ("both", 4), ("both", 5), ("both", 3))
+PREP_AFTER = 0
+TIES = ()
+D_TIES = ()
 
 in_vmem = pl.BlockSpec(memory_space=pltpu.VMEM)
 in_smem = pl.BlockSpec(memory_space=pltpu.SMEM)
@@ -90,23 +95,24 @@
     return one, two
 
 
-def rank_kernel(plan, here, x, y, *refs):
-    split, whole = plan
-    straight, up, dhidden, hidden = [*refs[:1], *refs[1 + len(split) : -2]], refs[1 : 1 + len(split)], *refs[-2:]
-    rows, width = straight[0].shape
+def rank_kernel(order, here, x, y, *refs):
+    pieces, (dhidden, hidden) = refs[:-2], refs[-2:]
+    width = dhidden.shape[1]
     tokens = x.shape[0]
     me = here[0]
     x_rank = jnp.zeros((tokens, width), jnp.float32)
     y_rank = jnp.zeros((tokens, width), jnp.float32)
     y_first = jnp.zeros((tokens, width), jnp.float32)
-    for k, pair in zip(whole, straight):
-        columns = pl.ds(pl.multiple_of((me ^ k) * rows, rows), rows)
-        x_rank += jnp.dot(x[:, columns], pair[...], preferred_element_type=jnp.float32)
-        y_rank += jnp.dot(y[:, columns], pair[...], preferred_element_type=jnp.float32)
-    for n, k in enumerate(split):
-        first, second = halves_product(y, up[n], me ^ k)
-        y_first += first
-        y_rank += second
+    for (packed, k), piece in zip(order, pieces):
+        if packed:
+            first, second = halves_product(y, piece, me ^ k)
+            y_first += first
+            y_rank += second
+        else:
+            rows = piece.shape[0]
+            columns = pl.ds(pl.multiple_of((me ^ k) * rows, rows), rows)
+            x_rank += jnp.dot(x[:, columns], piece[...], preferred_element_type=jnp.float32)
+            y_rank += jnp.dot(y[:, columns], piece[...], preferred_element_type=jnp.float32)
     y_rank += swap_halves(y_first)
     half = tokens // 2
     low = low_lanes(half, width)
@@ -198,10 +204,11 @@
         out[:, pl.ds(pl.multiple_of(start + half, half), half)] = product(right, down[n][...])
 
 
-def merge_kernel(plan, ids, here, lengths, *refs):
+def merge_kernel(plan, order, ids, here, lengths, *refs):
     split, whole = plan
-    parts = len(split)
-    down, up, straight = refs[:parts], refs[parts : 2 * parts], refs[2 * parts : -5]
+    by_key = dict(zip(order, refs[:-5]))
+    down, up = [by_key["down", k] for k in split], [by_key["up", k] for k in split]
+    straight = [by_key["both", k] for k in whole]
     out, total, held, sems = refs[-4:]
     me = here[0]
     rows, width = total.shape
@@ -257,11 +264,19 @@
         pl.when(firsts[k])(copies[k].wait)
 
 
-def to_partner(pieces, partners, owners):
-    return [
-        lax.ppermute(piece, "dp", [(i, i ^ k) for i in range(owners)]) if k else piece
-        for k, piece in zip(partners, pieces)
-    ]
+def to_partner(pieces, partners, owners, ties=()):
+    to_send, out = dict(zip(partners, pieces)), {}
+    held = dict(ties)
+    for k in sorted(partners, key=lambda k: k in held):
+        piece = after(to_send[k], out[held[k]]) if k in held else to_send[k]
+        out[k] = lax.ppermute(piece, "dp", [(i, i ^ k) for i in range(owners)]) if k else piece
+    return [out[k] for k in partners]
+
+
+def in_order(pieces, first):
+    keys = [key for key in first if key in pieces]
+    keys += [key for key in pieces if key not in keys]
+    return [(key, pieces[key]) for key in keys]
 
 
 def after(value, *others):
@@ -276,7 +291,7 @@
 def with_kernels(activations, cotangent, adapter_weight_pair, adapter_of_block, block_live_length):
     owners = lax.axis_size("dp")
     near, far = range(1, owners // 2), range(owners // 2, owners)
-    plan = split, whole = tuple(far[-2:]), (1, *far[:-2], *near[1:], 0)
+    plan = split, whole = tuple(far[-2:]), (*near[:-1], *far[:-2], near[-1], 0)
     here = lax.axis_index("dp").astype(jnp.int32).reshape(1)
     ids, lengths = adapter_of_block[:, 0], block_live_length[:, 0]
     count, _, rows, width = adapter_weight_pair.shape
@@ -302,6 +317,9 @@
     )(ids, here, table)
     ups = to_partner(sent[:parts], split, owners)
 
+    pairs = to_partner(sent[parts : parts + wholes], whole, owners, TIES)
+    downs = to_partner(sent[parts + wholes :], split, owners)
+
     step = 8
     turned, blank = call(
         functools.partial(prep_kernel, rows),
@@ -313,20 +331,17 @@
         [in_vmem, in_hbm],
         [pltpu.VMEM((step, rows, width), bf16), pltpu.SemaphoreType.DMA((count // step,))],
         moved=4 * token_bytes + 2 * count * rows * width,
-    )(sent[0], activations, cotangent)
-    sent = list(sent)
-    held_back = whole.index(near[-1]) + parts
-    sent[held_back] = after(sent[held_back], turned)
-    pairs = to_partner(sent[parts : parts + wholes], whole, owners)
-    downs = to_partner(sent[parts + wholes :], split, owners)
-
+    )(ups[PREP_AFTER], activations, cotangent)
+    from_whole = {(False, k): piece for k, piece in zip(whole, pairs)}
+    from_split = {(True, k): piece for k, piece in zip(split, ups)}
+    rank_order = in_order({**from_whole, **from_split}, RANK_ORDER)
     dhidden, partial = call(
-        functools.partial(rank_kernel, plan),
+        functools.partial(rank_kernel, tuple(key for key, _ in rank_order)),
         [rank_space, rank_space],
         [in_smem] + [in_vmem] * (2 + parts + wholes),
         [in_vmem, in_vmem],
         moved=1024,
-    )(here, activations, cotangent, pairs[0], *ups, *pairs[1:])
+    )(here, after(activations, turned), cotangent, *[piece for _, piece in rank_order])
     dhidden_other = across_cores(dhidden)
     down_pieces = call(
         functools.partial(down_piece_kernel, plan, scale),
@@ -353,7 +368,7 @@
         moved=1024,
     )(here, lengths, dhidden, dhidden_other, after(hidden, d_downs[0]), hidden_other, turned)
     d_ups = to_partner(pieces[:parts], split, owners)
-    d_pairs = to_partner(pieces[parts:], whole, owners)
+    d_pairs = to_partner(pieces[parts:], whole, owners, D_TIES)
 
     grad_input = call(
         functools.partial(input_kernel, plan, scale),
@@ -364,8 +379,12 @@
         moved=token_bytes + pair_bytes,
     )(here, lengths, after(dhidden, *pieces), dhidden_other, *downs, *pairs)
 
+    from_all = {("both", k): piece for k, piece in zip(whole, d_pairs)}
+    from_all |= {("down", k): piece for k, piece in zip(split, d_downs)}
+    from_all |= {("up", k): piece for k, piece in zip(split, d_ups)}
+    merge_order = in_order(from_all, MERGE_ORDER)
     gradient = call(
-        functools.partial(merge_kernel, plan),
+        functools.partial(merge_kernel, plan, tuple(key for key, _ in merge_order)),
         jax.ShapeDtypeStruct(table.shape, bf16),
         [in_smem] * 3 + [in_vmem] * (2 * parts + wholes) + [in_hbm],
         in_hbm,
@@ -376,7 +395,7 @@
         ],
         moved=2 * pair_bytes,
         aliases={3 + 2 * parts + wholes: 0},
-    )(ids, here, lengths, *d_downs, *d_ups, *d_pairs, blank)
+    )(ids, here, lengths, *[piece for _, piece in merge_order], blank)
     return grad_input, gradient[:, None]
 
 

time: 71.6 us -> 64.7 us (0.904)
  starting transfers between devices: 36.3 us -> 32.3 us
  waiting for transfers between devices: 17.5 us -> 14.7 us
    ppermute x18, starting transfers between devices: 36.2 us -> 32.2 us  [to_partner(): lax.ppermute(piece, 'dp', [(i, i ^ k) for i in range(owners)])]
    ppermute x18, waiting for transfers between devices: 17.5 us -> 14.7 us  [to_partner(): lax.ppermute(piece, 'dp', [(i, i ^ k) for i in range(owners)])]
  transfers between devices with their start and end apart: 20 -> 20, of which waited for: 9 -> 6; matrix products, arithmetic and copies ran while one was open for 0% -> 0% of each run, Pallas kernels for 14% -> 15%
where the time goes in v9:
time: 64.7 us; the launch traced here: 64.6 us
  starting transfers between devices  32.3 us (50%)
  waiting for transfers between devices  14.7 us (23%)
  Pallas kernels  14.2 us (22%)
  local copies, waits for them, and re-layouts  2.61 us (4%)
  between operations  0.76 us (1%)
    ppermute x18, starting transfers between devices, to_partner(): lax.ppermute(piece, 'dp', [(i, i ^ k) for i in range(owners)])  32.2 us
    ppermute x18, waiting for transfers between devices, to_partner(): lax.ppermute(piece, 'dp', [(i, i ^ k) for i in range(owners)])  14.7 us
    pallas_call x1, Pallas kernels, with_kernels(): call(functools.partial(prep_kernel, rows), [jax.ShapeDtypeStruct((owners,...  4.8 us
    unnamed x12, local copies, waits for them, and re-layouts  2.61 us
    pallas_call x1, Pallas kernels, with_kernels(): call(functools.partial(gather_kernel, plan), [packed] * parts + [straight...  2.55 us
    pallas_call x1, Pallas kernels, with_kernels(): call(functools.partial(input_kernel, plan, scale), jax.ShapeDtypeStruct((...  1.99 us
    pallas_call x1, Pallas kernels, with_kernels(): call(functools.partial(merge_kernel, plan, tuple((key for key, _ in merge...  1.75 us
  transfers between devices with their start and end apart: 20, of which 6 were waited for; matrix products, arithmetic and copies ran while one was open for 0% of the time, Pallas kernels for 15%

profile of v9, /device:TPU:0, one launch (start us, length us, event | category | flops | bytes accessed | tf_op | source)
XLA Modules:
  0.0 64.6 jit_solution(14849529279336839102)
XLA Ops:
  0.7 0.8 %copy-done.5 = s32[8,1]{0,1:T(1,128)S(1)} copy-done((s32[8,1]{0,1:T(1,128)S(1)}, s32[8,1]{0,1:T(1,128)}, u32[]{:S(2)}) %copy-start.5) | copy-done | bytes 56
  1.5 2.5 %shard_map.68 = (bf16[256,128]{1,0:T(8,128)(2,1)S(1)}, bf16[256,128]{1,0:T(8,128)(2,1)S(1)}, bf16[512,128]{1,0:T(8,128)(2,1)S(1)}, bf16[512,128]{1,0:T(8,128)(2,...) custom-call(s32[8]{0:T(128)S(1)} %bitcast.11, ...), custom_call_target="tpu_custom_call" | custom-call | bytes 2097152 | tf_op jit(solution)/shard_map/pallas_call | solution.py:309
  4.0 5.1 %collective-permute-start = (bf16[256,128]{1,0:T(8,128)(2,1)S(1)}, bf16[256,128]{1,0:T(8,128)(2,1)S(1)}, u32[]{:S(2)}, u32[]{:S(2)}) collective-permute-start(bf16[256,128]{1,0:T(8,128)(2,1)S(1)} %get-tuple-element.31), channel_id=1, source_target_pairs={{0,12},{2,14},{4,8},{6,10},{8,4},{10,6},{12,0},{14,2},{1,13},{3,15... | collective-permute-start | bytes 196616 | tf_op jit(solution)/shard_map/ppermute | solution.py:272
  9.1 1.1 %collective-permute-start.3 = (bf16[256,128]{1,0:T(8,128)(2,1)S(1)}, bf16[256,128]{1,0:T(8,128)(2,1)S(1)}, u32[]{:S(2)}, u32[]{:S(2)}) collective-permute-start(bf16[256,128]{1,0:T(8,128)(2,1)S(1)} %get-tuple-element.36), channel_id=1, source_target_pairs={{0,14},{2,12},{4,10},{6,8},{8,6},{10,4},{12,2},{14,0},{1,15},{3,13... | collective-permute-start | bytes 196616 | tf_op jit(solution)/shard_map/ppermute | solution.py:272
  10.3 0.4 collective-permute-start.1
  10.7 4.3 %collective-permute-start.4 = (bf16[512,128]{1,0:T(8,128)(2,1)S(1)}, bf16[512,128]{1,0:T(8,128)(2,1)S(1)}, u32[]{:S(2)}, u32[]{:S(2)}) collective-permute-start(bf16[512,128]{1,0:T(8,128)(2,1)S(1)} %get-tuple-element.37), channel_id=1, source_target_pairs={{0,8},{2,10},{4,12},{6,14},{8,0},{10,2},{12,4},{14,6},{1,9},{3,11}... | collective-permute-start | bytes 393224 | tf_op jit(solution)/shard_map/ppermute | solution.py:272
  15.0 0.9 %collective-permute-start.5 = (bf16[512,128]{1,0:T(8,128)(2,1)S(1)}, bf16[512,128]{1,0:T(8,128)(2,1)S(1)}, u32[]{:S(2)}, u32[]{:S(2)}) collective-permute-start(bf16[512,128]{1,0:T(8,128)(2,1)S(1)} %get-tuple-element.38), channel_id=1, source_target_pairs={{0,10},{2,8},{4,14},{6,12},{8,2},{10,0},{12,6},{14,4},{1,11},{3,9}... | collective-permute-start | bytes 393224 | tf_op jit(solution)/shard_map/ppermute | solution.py:272
  15.9 0.9 %collective-permute-done.3.refs_3_ = bf16[256,128]{1,0:T(8,128)(2,1)S(1)} collective-permute-done((bf16[256,128]{1,0:T(8,128)(2,1)S(1)}, bf16[256,128]{1,0:T(8,128)(2,1)S(1)}, u32[]{:S(2)}, u32[]{:S(2)}) %collective-permute-start.3) | collective-permute-done | bytes 65568 | tf_op jit(solution)/shard_map/ppermute | solution.py:272
  16.9 0.5 collective-permute-start.6
  17.4 2.9 %collective-permute-start.8 = (bf16[256,128]{1,0:T(8,128)(2,1)S(1)}, bf16[256,128]{1,0:T(8,128)(2,1)S(1)}, u32[]{:S(2)}, u32[]{:S(2)}) collective-permute-start(bf16[256,128]{1,0:T(8,128)(2,1)S(1)} %get-tuple-element.43), channel_id=1, source_target_pairs={{0,12},{2,14},{4,8},{6,10},{8,4},{10,6},{12,0},{14,2},{1,13},{3,15... | collective-permute-start | bytes 196616 | tf_op jit(solution)/shard_map/ppermute | solution.py:272
  20.3 4.8 %shard_map.69 = (bf16[8,512,256]{2,1,0:T(8,128)(2,1)S(1)}, bf16[96,512,128]{2,1,0:T(8,128)(2,1)}) custom-call(bf16[256,128]{1,0:T(8,128)(2,1)S(1)} %collective-permute-done.after.refs_2_, bf16[128,4096]{1,0:T(8,128)(2,1)S(1)} %copy-done, bf16[128,4096]{1,0:T(8,128)(2,1)S(1)} %copy-done.1), custom_call_target="tpu_custom_call" | custom-call | bytes 16777216 | tf_op jit(solution)/shard_map/pallas_call | solution.py:324
  25.1 4.4 %collective-permute-done.5.refs_5_ = bf16[512,128]{1,0:T(8,128)(2,1)S(1)} collective-permute-done((bf16[512,128]{1,0:T(8,128)(2,1)S(1)}, bf16[512,128]{1,0:T(8,128)(2,1)S(1)}, u32[]{:S(2)}, u32[]{:S(2)}) %collective-permute-start.5) | collective-permute-done | bytes 131104 | tf_op jit(solution)/shard_map/ppermute | solution.py:272
  29.5 0.9 %copy-done.2 = bf16[512,128]{1,0:T(8,128)(2,1)S(1)} copy-done((bf16[512,128]{1,0:T(8,128)(2,1)S(1)}, bf16[512,128]{1,0:T(8,128)(2,1)}, u32[]{:S(2)}) %copy-start.2) | copy-done | bytes 131096
  30.4 0.7 %shard_map.70 = (f32[64,128]{1,0:T(8,128)S(1)}, f32[64,128]{1,0:T(8,128)S(1)}) custom-call(s32[1]{0:T(128)} %bitcast.here, bf16[128,4096]{1,0:T(8,128)(2,1)S(1)} %copy-done, bf16[128,4096]{1,0:T(8,128)(2,1)S(1)} %copy-done.1, bf16[512,128]{1,0:T(8,128)(2,1)S(1)} %collective-permute-done.1.refs_0_.refs_2_, ...), custom_call_target="tpu_custom_call" | custom-call | bytes 1024 | tf_op jit(solution)/shard_map/pallas_call | solution.py:338
  31.2 2.2 %collective-permute-start.9 = (bf16[256,128]{1,0:T(8,128)(2,1)S(1)}, bf16[256,128]{1,0:T(8,128)(2,1)S(1)}, u32[]{:S(2)}, u32[]{:S(2)}) collective-permute-start(bf16[256,128]{1,0:T(8,128)(2,1)S(1)} %get-tuple-element.48), channel_id=1, source_target_pairs={{0,14},{2,12},{4,10},{6,8},{8,6},{10,4},{12,2},{14,0},{1,15},{3,13... | collective-permute-start | bytes 196616 | tf_op jit(solution)/shard_map/ppermute | solution.py:272
  33.5 0.8 %shard_map.71 = (bf16[256,128]{1,0:T(8,128)(2,1)S(1)}, bf16[256,128]{1,0:T(8,128)(2,1)S(1)}) custom-call(s32[1]{0:T(128)} %bitcast.here, s32[8]{0:T(128)S(1)} %bitcast.7, f32[64,128]{1,0:T(8,128)S(1)} %get-tuple-element.58.mine.d_mine, f32[64,128]{1,0:T(8,128)S(1)} %collective-permute-done.7.other.d_other, bf16[8,512,256]{2,1,0:T(8,128)(2,1)S(1)} %get-tuple-element.32.turned), custom_call_target="tpu_custom_call" | custom-call | bytes 1024 | tf_op jit(solution)/shard_map/pallas_call | solution.py:346
  34.3 1.9 %collective-permute-start.10 = (bf16[256,128]{1,0:T(8,128)(2,1)S(1)}, bf16[256,128]{1,0:T(8,128)(2,1)S(1)}, u32[]{:S(2)}, u32[]{:S(2)}) collective-permute-start(bf16[256,128]{1,0:T(8,128)(2,1)S(1)} %get-tuple-element.45), channel_id=1, source_target_pairs={{0,12},{2,14},{4,8},{6,10},{8,4},{10,6},{12,0},{14,2},{1,13},{3,15... | collective-permute-start | bytes 196616 | tf_op jit(solution)/shard_map/ppermute | solution.py:272
  36.2 2.2 %collective-permute-done.9.refs_1_ = bf16[256,128]{1,0:T(8,128)(2,1)S(1)} collective-permute-done((bf16[256,128]{1,0:T(8,128)(2,1)S(1)}, bf16[256,128]{1,0:T(8,128)(2,1)S(1)}, u32[]{:S(2)}, u32[]{:S(2)}) %collective-permute-start.9) | collective-permute-done | bytes 65568 | tf_op jit(solution)/shard_map/ppermute | solution.py:272
  38.8 2.2 %collective-permute-start.17 = (bf16[256,128]{1,0:T(8,128)(2,1)S(1)}, bf16[256,128]{1,0:T(8,128)(2,1)S(1)}, u32[]{:S(2)}, u32[]{:S(2)}) collective-permute-start(bf16[256,128]{1,0:T(8,128)(2,1)S(1)} %get-tuple-element.46), channel_id=1, source_target_pairs={{0,14},{2,12},{4,10},{6,8},{8,6},{10,4},{12,2},{14,0},{1,15},{3,13... | collective-permute-start | bytes 196616 | tf_op jit(solution)/shard_map/ppermute | solution.py:272
  41.1 1.2 %shard_map.73 = (bf16[256,128]{1,0:T(8,128)(2,1)S(1)}, bf16[256,128]{1,0:T(8,128)(2,1)S(1)}, bf16[512,128]{1,0:T(8,128)(2,1)S(1)}, bf16[512,128]{1,0:T(8,128)(2,...) custom-call(s32[1]{0:T(128)} %bitcast.here, ...), custom_call_target="tpu_custom_call" | custom-call | bytes 1024 | tf_op jit(solution)/shard_map/pallas_call | solution.py:363
  42.3 1.9 %collective-permute-start.18 = (bf16[256,128]{1,0:T(8,128)(2,1)S(1)}, bf16[256,128]{1,0:T(8,128)(2,1)S(1)}, u32[]{:S(2)}, u32[]{:S(2)}) collective-permute-start(bf16[256,128]{1,0:T(8,128)(2,1)S(1)} %get-tuple-element.50), channel_id=1, source_target_pairs={{0,12},{2,14},{4,8},{6,10},{8,4},{10,6},{12,0},{14,2},{1,13},{3,15... | collective-permute-start | bytes 196616 | tf_op jit(solution)/shard_map/ppermute | solution.py:272
  44.2 2.6 %collective-permute-start.19 = (bf16[256,128]{1,0:T(8,128)(2,1)S(1)}, bf16[256,128]{1,0:T(8,128)(2,1)S(1)}, u32[]{:S(2)}, u32[]{:S(2)}) collective-permute-start(bf16[256,128]{1,0:T(8,128)(2,1)S(1)} %get-tuple-element.51), channel_id=1, source_target_pairs={{0,14},{2,12},{4,10},{6,8},{8,6},{10,4},{12,2},{14,0},{1,15},{3,13... | collective-permute-start | bytes 196616 | tf_op jit(solution)/shard_map/ppermute | solution.py:272
  46.9 0.8 %collective-permute-start.12 = (bf16[512,128]{1,0:T(8,128)(2,1)S(1)}, bf16[512,128]{1,0:T(8,128)(2,1)S(1)}, u32[]{:S(2)}, u32[]{:S(2)}) collective-permute-start(bf16[512,128]{1,0:T(8,128)(2,1)S(1)} %get-tuple-element.52), channel_id=1, source_target_pairs={{0,2},{2,0},{4,6},{6,4},{8,10},{10,8},{12,14},{14,12},{1,3},{3,1},... | collective-permute-start | bytes 393224 | tf_op jit(solution)/shard_map/ppermute | solution.py:272
  47.7 2.4 %collective-permute-start.14 = (bf16[512,128]{1,0:T(8,128)(2,1)S(1)}, bf16[512,128]{1,0:T(8,128)(2,1)S(1)}, u32[]{:S(2)}, u32[]{:S(2)}) collective-permute-start(bf16[512,128]{1,0:T(8,128)(2,1)S(1)} %get-tuple-element.54), channel_id=1, source_target_pairs={{0,8},{2,10},{4,12},{6,14},{8,0},{10,2},{12,4},{14,6},{1,9},{3,11}... | collective-permute-start | bytes 393224 | tf_op jit(solution)/shard_map/ppermute | solution.py:272
  50.1 1.2 %collective-permute-start.15 = (bf16[512,128]{1,0:T(8,128)(2,1)S(1)}, bf16[512,128]{1,0:T(8,128)(2,1)S(1)}, u32[]{:S(2)}, u32[]{:S(2)}) collective-permute-start(bf16[512,128]{1,0:T(8,128)(2,1)S(1)} %get-tuple-element.55), channel_id=1, source_target_pairs={{0,10},{2,8},{4,14},{6,12},{8,2},{10,0},{12,6},{14,4},{1,11},{3,9}... | collective-permute-start | bytes 393224 | tf_op jit(solution)/shard_map/ppermute | solution.py:272
  51.3 0.7 %collective-permute-done.19.refs_9_ = bf16[256,128]{1,0:T(8,128)(2,1)S(1)} collective-permute-done((bf16[256,128]{1,0:T(8,128)(2,1)S(1)}, bf16[256,128]{1,0:T(8,128)(2,1)S(1)}, u32[]{:S(2)}, u32[]{:S(2)}) %collective-permute-start.19) | collective-permute-done | bytes 65568 | tf_op jit(solution)/shard_map/ppermute | solution.py:272
  52.0 1.6 %collective-permute-start.16 = (bf16[512,128]{1,0:T(8,128)(2,1)S(1)}, bf16[512,128]{1,0:T(8,128)(2,1)S(1)}, u32[]{:S(2)}, u32[]{:S(2)}) collective-permute-start(bf16[512,128]{1,0:T(8,128)(2,1)S(1)} %get-tuple-element.56), channel_id=1, source_target_pairs={{0,6},{2,4},{4,2},{6,0},{8,14},{10,12},{12,10},{14,8},{1,7},{3,5},... | collective-permute-start | bytes 393224 | tf_op jit(solution)/shard_map/ppermute | solution.py:272
  53.6 0.9 %copy-done.3 = bf16[512,128]{1,0:T(8,128)(2,1)S(1)} copy-done((bf16[512,128]{1,0:T(8,128)(2,1)S(1)}, bf16[512,128]{1,0:T(8,128)(2,1)}, u32[]{:S(2)}) %copy-start.3) | copy-done | bytes 131096
  54.5 2.0 %shard_map.74 = bf16[128,4096]{1,0:T(8,128)(2,1)} custom-call(s32[1]{0:T(128)} %bitcast.here, s32[8]{0:T(128)S(1)} %bitcast.9, f32[64,128]{1,0:T(8,128)S(1)} %get-tuple-element.58.mine.d_mine, f32[64,128]{1,0:T(8,128)S(1)} %collective-permute-done.7.other.d_other, bf16[256,128]{1,0:T(8,128)(2,1)S(1)} %collective-permute-done.8.refs_0_, ...), custom_call_target="tpu_custom_call" | custom-call | flops 134217728 | bytes 2097152 | tf_op jit(solution)/shard_map/pallas_call | solution.py:373
  56.5 4.2 %collective-permute-done.14.refs_2_ = bf16[512,128]{1,0:T(8,128)(2,1)S(1)} collective-permute-done((bf16[512,128]{1,0:T(8,128)(2,1)S(1)}, bf16[512,128]{1,0:T(8,128)(2,1)S(1)}, u32[]{:S(2)}, u32[]{:S(2)}) %collective-permute-start.14) | collective-permute-done | bytes 131104 | tf_op jit(solution)/shard_map/ppermute | solution.py:272
  60.7 2.1 %collective-permute-done.15.refs_3_ = bf16[512,128]{1,0:T(8,128)(2,1)S(1)} collective-permute-done((bf16[512,128]{1,0:T(8,128)(2,1)S(1)}, bf16[512,128]{1,0:T(8,128)(2,1)S(1)}, u32[]{:S(2)}, u32[]{:S(2)}) %collective-permute-start.15) | collective-permute-done | bytes 131104 | tf_op jit(solution)/shard_map/ppermute | solution.py:272
  62.8 1.8 %shard_map.75 = bf16[96,512,128]{2,1,0:T(8,128)(2,1)} custom-call(s32[8]{0:T(128)S(1)} %bitcast.12, s32[1]{0:T(128)} %bitcast.here, s32[8]{0:T(128)S(1)} %bitcast.10, bf16[512,128]{1,0:T(8,128)(2,1)S(1)} %collective-permute-done.12.refs_0_, bf16[512,128]{1,0:T(8,128)(2,1)S(1)} %collective-permute-done.13.refs_1_, ...), custom_call_target="tpu_custom_call", output_to_operand_aliasing={{}: (13, {})} | custom-call | bytes 2097152 | tf_op jit(solution)/shard_map/pallas_call | solution.py:386
  (28 shorter events, 0.6 us)
Async XLA Ops:
  0.6 19.7 %copy-start = (bf16[128,4096]{1,0:T(8,128)(2,1)S(1)}, bf16[128,4096]{1,0:T(8,128)(2,1)}, u32[]{:S(2)}) copy-start(bf16[128,4096]{1,0:T(8,128)(2,1)} %x.4) | copy-start | bytes 3145732
  0.6 19.7 %copy-start.1 = (bf16[128,4096]{1,0:T(8,128)(2,1)S(1)}, bf16[128,4096]{1,0:T(8,128)(2,1)}, u32[]{:S(2)}) copy-start(bf16[128,4096]{1,0:T(8,128)(2,1)} %y.3) | copy-start | bytes 3145732
  0.7 32.8 %copy-start.4 = (s32[8,1]{0,1:T(1,128)S(1)}, s32[8,1]{0,1:T(1,128)}, u32[]{:S(2)}) copy-start(s32[8,1]{0,1:T(1,128)} %param.9) | copy-start | bytes 100
  0.7 0.8 %copy-start.5 = (s32[8,1]{0,1:T(1,128)S(1)}, s32[8,1]{0,1:T(1,128)}, u32[]{:S(2)}) copy-start(s32[8,1]{0,1:T(1,128)} %param.8) | copy-start | bytes 100
  4.0 11.0 %collective-permute-start = (bf16[256,128]{1,0:T(8,128)(2,1)S(1)}, bf16[256,128]{1,0:T(8,128)(2,1)S(1)}, u32[]{:S(2)}, u32[]{:S(2)}) collective-permute-start(bf16[256,128]{1,0:T(8,128)(2,1)S(1)} %get-tuple-element.31), channel_id=1, source_target_pairs={{0,12},{2,14},{4,8},{6,10},{8,4},{10,6},{12,0},{14,2},{1,13},{3,15... | collective-permute-start | bytes 196616 | tf_op jit(solution)/shard_map/ppermute | solution.py:272
  9.1 7.7 %collective-permute-start.3 = (bf16[256,128]{1,0:T(8,128)(2,1)S(1)}, bf16[256,128]{1,0:T(8,128)(2,1)S(1)}, u32[]{:S(2)}, u32[]{:S(2)}) collective-permute-start(bf16[256,128]{1,0:T(8,128)(2,1)S(1)} %get-tuple-element.36), channel_id=1, source_target_pairs={{0,14},{2,12},{4,10},{6,8},{8,6},{10,4},{12,2},{14,0},{1,15},{3,13... | collective-permute-start | bytes 196616 | tf_op jit(solution)/shard_map/ppermute | solution.py:272
  10.3 7.1 %collective-permute-start.1 = (bf16[512,128]{1,0:T(8,128)(2,1)S(1)}, bf16[512,128]{1,0:T(8,128)(2,1)S(1)}, u32[]{:S(2)}, u32[]{:S(2)}) collective-permute-start(bf16[512,128]{1,0:T(8,128)(2,1)S(1)} %get-tuple-element.34), channel_id=1, source_target_pairs={{0,2},{2,0},{4,6},{6,4},{8,10},{10,8},{12,14},{14,12},{1,3},{3,1},... | collective-permute-start | bytes 393224 | tf_op jit(solution)/shard_map/ppermute | solution.py:272
  10.7 14.4 %collective-permute-start.2 = (bf16[512,128]{1,0:T(8,128)(2,1)S(1)}, bf16[512,128]{1,0:T(8,128)(2,1)S(1)}, u32[]{:S(2)}, u32[]{:S(2)}) collective-permute-start(bf16[512,128]{1,0:T(8,128)(2,1)S(1)} %get-tuple-element.35), channel_id=1, source_target_pairs={{0,4},{2,6},{4,0},{6,2},{8,12},{10,14},{12,8},{14,10},{1,5},{3,7},... | collective-permute-start | bytes 393224 | tf_op jit(solution)/shard_map/ppermute | solution.py:272
  10.7 14.4 %collective-permute-start.4 = (bf16[512,128]{1,0:T(8,128)(2,1)S(1)}, bf16[512,128]{1,0:T(8,128)(2,1)S(1)}, u32[]{:S(2)}, u32[]{:S(2)}) collective-permute-start(bf16[512,128]{1,0:T(8,128)(2,1)S(1)} %get-tuple-element.37), channel_id=1, source_target_pairs={{0,8},{2,10},{4,12},{6,14},{8,0},{10,2},{12,4},{14,6},{1,9},{3,11}... | collective-permute-start | bytes 393224 | tf_op jit(solution)/shard_map/ppermute | solution.py:272
  15.0 14.5 %collective-permute-start.5 = (bf16[512,128]{1,0:T(8,128)(2,1)S(1)}, bf16[512,128]{1,0:T(8,128)(2,1)S(1)}, u32[]{:S(2)}, u32[]{:S(2)}) collective-permute-start(bf16[512,128]{1,0:T(8,128)(2,1)S(1)} %get-tuple-element.38), channel_id=1, source_target_pairs={{0,10},{2,8},{4,14},{6,12},{8,2},{10,0},{12,6},{14,4},{1,11},{3,9}... | collective-permute-start | bytes 393224 | tf_op jit(solution)/shard_map/ppermute | solution.py:272
  16.9 12.7 %collective-permute-start.6 = (bf16[512,128]{1,0:T(8,128)(2,1)S(1)}, bf16[512,128]{1,0:T(8,128)(2,1)S(1)}, u32[]{:S(2)}, u32[]{:S(2)}) collective-permute-start(bf16[512,128]{1,0:T(8,128)(2,1)S(1)} %get-tuple-element.39), channel_id=1, source_target_pairs={{0,6},{2,4},{4,2},{6,0},{8,14},{10,12},{12,10},{14,8},{1,7},{3,5},... | collective-permute-start | bytes 393224 | tf_op jit(solution)/shard_map/ppermute | solution.py:272
  17.4 16.1 %collective-permute-start.8 = (bf16[256,128]{1,0:T(8,128)(2,1)S(1)}, bf16[256,128]{1,0:T(8,128)(2,1)S(1)}, u32[]{:S(2)}, u32[]{:S(2)}) collective-permute-start(bf16[256,128]{1,0:T(8,128)(2,1)S(1)} %get-tuple-element.43), channel_id=1, source_target_pairs={{0,12},{2,14},{4,8},{6,10},{8,4},{10,6},{12,0},{14,2},{1,13},{3,15... | collective-permute-start | bytes 196616 | tf_op jit(solution)/shard_map/ppermute | solution.py:272
  29.5 0.9 %copy-start.2 = (bf16[512,128]{1,0:T(8,128)(2,1)S(1)}, bf16[512,128]{1,0:T(8,128)(2,1)}, u32[]{:S(2)}) copy-start(bf16[512,128]{1,0:T(8,128)(2,1)} %get-tuple-element.40.refs_7_) | copy-start | bytes 393220
  31.1 2.3 %collective-permute-start.7 = (f32[64,128]{1,0:T(8,128)S(1)}, f32[64,128]{1,0:T(8,128)S(1)}, u32[]{:S(2)}, u32[]{:S(2)}) collective-permute-start(f32[64,128]{1,0:T(8,128)S(1)} %get-tuple-element.58.mine.d_mine), channel_id=1, source_target_pairs={{0,1},{1,0},{2,3},{3,2},{4,5},{5,4},{6,7},{7,6},{8,9},{9,8},{10,11... | collective-permute-start | bytes 98312 | tf_op jit(solution)/shard_map/ppermute | solution.py:288
  31.2 7.2 %collective-permute-start.9 = (bf16[256,128]{1,0:T(8,128)(2,1)S(1)}, bf16[256,128]{1,0:T(8,128)(2,1)S(1)}, u32[]{:S(2)}, u32[]{:S(2)}) collective-permute-start(bf16[256,128]{1,0:T(8,128)(2,1)S(1)} %get-tuple-element.48), channel_id=1, source_target_pairs={{0,14},{2,12},{4,10},{6,8},{8,6},{10,4},{12,2},{14,0},{1,15},{3,13... | collective-permute-start | bytes 196616 | tf_op jit(solution)/shard_map/ppermute | solution.py:272
  34.3 6.8 %collective-permute-start.10 = (bf16[256,128]{1,0:T(8,128)(2,1)S(1)}, bf16[256,128]{1,0:T(8,128)(2,1)S(1)}, u32[]{:S(2)}, u32[]{:S(2)}) collective-permute-start(bf16[256,128]{1,0:T(8,128)(2,1)S(1)} %get-tuple-element.45), channel_id=1, source_target_pairs={{0,12},{2,14},{4,8},{6,10},{8,4},{10,6},{12,0},{14,2},{1,13},{3,15... | collective-permute-start | bytes 196616 | tf_op jit(solution)/shard_map/ppermute | solution.py:272
  38.8 2.3 %collective-permute-start.11 = (f32[64,128]{1,0:T(8,128)S(1)}, f32[64,128]{1,0:T(8,128)S(1)}, u32[]{:S(2)}, u32[]{:S(2)}) collective-permute-start(f32[64,128]{1,0:T(8,128)S(1)} %shard_map.72.mine), channel_id=1, source_target_pairs={{0,1},{1,0},{2,3},{3,2},{4,5},{5,4},{6,7},{7,6},{8,9},{9,8},{10,11... | collective-permute-start | bytes 98312 | tf_op jit(solution)/shard_map/ppermute | solution.py:288
  38.8 8.9 %collective-permute-start.17 = (bf16[256,128]{1,0:T(8,128)(2,1)S(1)}, bf16[256,128]{1,0:T(8,128)(2,1)S(1)}, u32[]{:S(2)}, u32[]{:S(2)}) collective-permute-start(bf16[256,128]{1,0:T(8,128)(2,1)S(1)} %get-tuple-element.46), channel_id=1, source_target_pairs={{0,14},{2,12},{4,10},{6,8},{8,6},{10,4},{12,2},{14,0},{1,15},{3,13... | collective-permute-start | bytes 196616 | tf_op jit(solution)/shard_map/ppermute | solution.py:272
  42.3 7.7 %collective-permute-start.18 = (bf16[256,128]{1,0:T(8,128)(2,1)S(1)}, bf16[256,128]{1,0:T(8,128)(2,1)S(1)}, u32[]{:S(2)}, u32[]{:S(2)}) collective-permute-start(bf16[256,128]{1,0:T(8,128)(2,1)S(1)} %get-tuple-element.50), channel_id=1, source_target_pairs={{0,12},{2,14},{4,8},{6,10},{8,4},{10,6},{12,0},{14,2},{1,13},{3,15... | collective-permute-start | bytes 196616 | tf_op jit(solution)/shard_map/ppermute | solution.py:272
  44.2 7.8 %collective-permute-start.19 = (bf16[256,128]{1,0:T(8,128)(2,1)S(1)}, bf16[256,128]{1,0:T(8,128)(2,1)S(1)}, u32[]{:S(2)}, u32[]{:S(2)}) collective-permute-start(bf16[256,128]{1,0:T(8,128)(2,1)S(1)} %get-tuple-element.51), channel_id=1, source_target_pairs={{0,14},{2,12},{4,10},{6,8},{8,6},{10,4},{12,2},{14,0},{1,15},{3,13... | collective-permute-start | bytes 196616 | tf_op jit(solution)/shard_map/ppermute | solution.py:272
  46.9 9.6 %collective-permute-start.12 = (bf16[512,128]{1,0:T(8,128)(2,1)S(1)}, bf16[512,128]{1,0:T(8,128)(2,1)S(1)}, u32[]{:S(2)}, u32[]{:S(2)}) collective-permute-start(bf16[512,128]{1,0:T(8,128)(2,1)S(1)} %get-tuple-element.52), channel_id=1, source_target_pairs={{0,2},{2,0},{4,6},{6,4},{8,10},{10,8},{12,14},{14,12},{1,3},{3,1},... | collective-permute-start | bytes 393224 | tf_op jit(solution)/shard_map/ppermute | solution.py:272
  47.7 8.8 %collective-permute-start.13 = (bf16[512,128]{1,0:T(8,128)(2,1)S(1)}, bf16[512,128]{1,0:T(8,128)(2,1)S(1)}, u32[]{:S(2)}, u32[]{:S(2)}) collective-permute-start(bf16[512,128]{1,0:T(8,128)(2,1)S(1)} %get-tuple-element.53), channel_id=1, source_target_pairs={{0,4},{2,6},{4,0},{6,2},{8,12},{10,14},{12,8},{14,10},{1,5},{3,7},... | collective-permute-start | bytes 393224 | tf_op jit(solution)/shard_map/ppermute | solution.py:272
  47.7 13.0 %collective-permute-start.14 = (bf16[512,128]{1,0:T(8,128)(2,1)S(1)}, bf16[512,128]{1,0:T(8,128)(2,1)S(1)}, u32[]{:S(2)}, u32[]{:S(2)}) collective-permute-start(bf16[512,128]{1,0:T(8,128)(2,1)S(1)} %get-tuple-element.54), channel_id=1, source_target_pairs={{0,8},{2,10},{4,12},{6,14},{8,0},{10,2},{12,4},{14,6},{1,9},{3,11}... | collective-permute-start | bytes 393224 | tf_op jit(solution)/shard_map/ppermute | solution.py:272
  50.1 12.7 %collective-permute-start.15 = (bf16[512,128]{1,0:T(8,128)(2,1)S(1)}, bf16[512,128]{1,0:T(8,128)(2,1)S(1)}, u32[]{:S(2)}, u32[]{:S(2)}) collective-permute-start(bf16[512,128]{1,0:T(8,128)(2,1)S(1)} %get-tuple-element.55), channel_id=1, source_target_pairs={{0,10},{2,8},{4,14},{6,12},{8,2},{10,0},{12,6},{14,4},{1,11},{3,9}... | collective-permute-start | bytes 393224 | tf_op jit(solution)/shard_map/ppermute | solution.py:272
  52.0 10.8 %collective-permute-start.16 = (bf16[512,128]{1,0:T(8,128)(2,1)S(1)}, bf16[512,128]{1,0:T(8,128)(2,1)S(1)}, u32[]{:S(2)}, u32[]{:S(2)}) collective-permute-start(bf16[512,128]{1,0:T(8,128)(2,1)S(1)} %get-tuple-element.56), channel_id=1, source_target_pairs={{0,6},{2,4},{4,2},{6,0},{8,14},{10,12},{12,10},{14,8},{1,7},{3,5},... | collective-permute-start | bytes 393224 | tf_op jit(solution)/shard_map/ppermute | solution.py:272
  53.6 0.9 %copy-start.3 = (bf16[512,128]{1,0:T(8,128)(2,1)S(1)}, bf16[512,128]{1,0:T(8,128)(2,1)}, u32[]{:S(2)}) copy-start(bf16[512,128]{1,0:T(8,128)(2,1)} %get-tuple-element.40.refs_7_) | copy-start | bytes 393220

commit v10 on v9

--- a/solution.py
+++ b/solution.py
@@ -8,11 +8,12 @@
 from jax.sharding import PartitionSpec as P
 
 adapter_alpha = 128.0
-RANK_ORDER = ((False, 1), (False, 2), (True, 6), (True, 7), (False, 4), (False, 5))
-MERGE_ORDER = (("both", 1), ("both", 2), ("both", 4), ("both", 5), ("both", 3))
+RANK_ORDER = ((False, 1), (False, 2), (True, 4), (True, 5), (False, 6), (False, 7), (False, 3))
+MERGE_ORDER = (("both", 6), ("both", 1), ("both", 7), ("both", 2), ("both", 3))
 PREP_AFTER = 0
-TIES = ()
-D_TIES = ()
+PREP_VMEM = 40
+SPLIT = (4, 5)
+WHOLE = (6, 1, 7, 2, 3)
 
 in_vmem = pl.BlockSpec(memory_space=pltpu.VMEM)
 in_smem = pl.BlockSpec(memory_space=pltpu.SMEM)
@@ -65,7 +66,10 @@
         copy.wait()
 
 
-def prep_kernel(rows, after, x, y, turned, blank, zeros, sem):
+def prep_kernel(ids, here, table, after, x, y, turned, own, blank, zeros, sem, own_sem):
+    own_copy = pltpu.make_async_copy(table.at[ids[here[0]]], own, own_sem)
+    own_copy.start()
+    rows = own.shape[0]
     zeros[...] = jnp.zeros_like(zeros)
     step = zeros.shape[0]
     copies = [
@@ -82,7 +86,7 @@
         turned[owner, :, pl.ds(0, tokens)] = x[:, columns].T
         turned[owner, :, pl.ds(tokens, tokens)] = y[:, columns].T
 
-    for copy in copies:
+    for copy in [own_copy, *copies]:
         copy.wait()
 
 
@@ -164,7 +168,7 @@
 
 def piece_kernel(plan, scale, here, lengths, d_mine, d_other, mine, other, turned, *refs):
     split, whole = plan
-    up, straight = refs[: len(split)], refs[len(split) :]
+    straight, up = refs[: len(whole)], refs[len(whole) :]
     me = here[0]
     dhidden, _ = rounded(d_mine, d_other, lengths[me], scale)
     left, right = rounded(mine, other, lengths[me], 1.0)
@@ -264,13 +268,11 @@
         pl.when(firsts[k])(copies[k].wait)
 
 
-def to_partner(pieces, partners, owners, ties=()):
-    to_send, out = dict(zip(partners, pieces)), {}
-    held = dict(ties)
-    for k in sorted(partners, key=lambda k: k in held):
-        piece = after(to_send[k], out[held[k]]) if k in held else to_send[k]
-        out[k] = lax.ppermute(piece, "dp", [(i, i ^ k) for i in range(owners)]) if k else piece
-    return [out[k] for k in partners]
+def to_partner(pieces, partners, owners):
+    return [
+        lax.ppermute(piece, "dp", [(i, i ^ k) for i in range(owners)]) if k else piece
+        for k, piece in zip(partners, pieces)
+    ]
 
 
 def in_order(pieces, first):
@@ -290,8 +292,7 @@
 
 def with_kernels(activations, cotangent, adapter_weight_pair, adapter_of_block, block_live_length):
     owners = lax.axis_size("dp")
-    near, far = range(1, owners // 2), range(owners // 2, owners)
-    plan = split, whole = tuple(far[-2:]), (*near[:-1], *far[:-2], near[-1], 0)
+    plan = split, whole = SPLIT, WHOLE
     here = lax.axis_index("dp").astype(jnp.int32).reshape(1)
     ids, lengths = adapter_of_block[:, 0], block_live_length[:, 0]
     count, _, rows, width = adapter_weight_pair.shape
@@ -317,21 +318,32 @@
     )(ids, here, table)
     ups = to_partner(sent[:parts], split, owners)
 
-    pairs = to_partner(sent[parts : parts + wholes], whole, owners, TIES)
+    pairs = to_partner(sent[parts : parts + wholes], whole, owners)
     downs = to_partner(sent[parts + wholes :], split, owners)
 
     step = 8
-    turned, blank = call(
-        functools.partial(prep_kernel, rows),
+    turned, own, blank = call(
+        prep_kernel,
         [
             jax.ShapeDtypeStruct((owners, rows, 2 * tokens), bf16),
+            straight,
             jax.ShapeDtypeStruct(table.shape, bf16),
         ],
-        [in_hbm, in_vmem, in_vmem],
-        [in_vmem, in_hbm],
-        [pltpu.VMEM((step, rows, width), bf16), pltpu.SemaphoreType.DMA((count // step,))],
+        [in_smem, in_smem, in_hbm, in_hbm, in_vmem, in_vmem],
+        [in_vmem, in_vmem, in_hbm],
+        [
+            pltpu.VMEM((step, rows, width), bf16),
+            pltpu.SemaphoreType.DMA((count // step,)),
+            pltpu.SemaphoreType.DMA,
+        ],
         moved=4 * token_bytes + 2 * count * rows * width,
-    )(ups[PREP_AFTER], activations, cotangent)
+        vmem=PREP_VMEM,
+    )(ids, here, table, ups[PREP_AFTER], activations, cotangent)
+
+    pairs.append(own)
+    whole += (0,)
+    wholes += 1
+    plan = split, whole
     from_whole = {(False, k): piece for k, piece in zip(whole, pairs)}
     from_split = {(True, k): piece for k, piece in zip(split, ups)}
     rank_order = in_order({**from_whole, **from_split}, RANK_ORDER)
@@ -349,7 +361,7 @@
         [in_smem] * 2 + [in_vmem] * 3,
         [in_vmem] * parts,
         moved=1024,
-    )(here, lengths, after(dhidden, downs[0]), dhidden_other, turned)
+    )(here, lengths, after(dhidden, *downs), dhidden_other, turned)
     d_downs = to_partner(down_pieces, split, owners)
 
     hidden = call(
@@ -362,13 +374,13 @@
     hidden_other = across_cores(hidden)
     pieces = call(
         functools.partial(piece_kernel, plan, scale),
-        [packed] * parts + [straight] * wholes,
+        [straight] * wholes + [packed] * parts,
         [in_smem] * 2 + [in_vmem] * 5,
         [in_vmem] * (parts + wholes),
         moved=1024,
-    )(here, lengths, dhidden, dhidden_other, after(hidden, d_downs[0]), hidden_other, turned)
-    d_ups = to_partner(pieces[:parts], split, owners)
-    d_pairs = to_partner(pieces[parts:], whole, owners, D_TIES)
+    )(here, lengths, dhidden, dhidden_other, hidden, hidden_other, turned)
+    d_pairs = to_partner(pieces[:wholes], whole, owners)
+    d_ups = to_partner(pieces[wholes:], split, owners)
 
     grad_input = call(
         functools.partial(input_kernel, plan, scale),
@@ -438,7 +450,7 @@
 
     def on_device(activations, cotangent, adapter_weight_pair, *rest):
         rows = adapter_weight_pair.shape[2]
-        fits = owners & (owners - 1) == 0 and owners >= 4 and cores == 2 and rows % 256 == 0
+        fits = owners == len(SPLIT) + len(WHOLE) + 1 and cores == 2 and rows % 256 == 0
         body = with_kernels if fits else without_kernels
         return body(activations, cotangent, adapter_weight_pair, *rest)
 

time: 64.7 us -> 63.5 us (0.981)
  starting transfers between devices: 32.3 us -> 36.6 us
  waiting for transfers between devices: 14.7 us -> 11.1 us
  local copies, waits for them, and re-layouts: 2.61 us -> 0.81 us
    ppermute x18, starting transfers between devices: 32.2 us -> 36.3 us  [to_partner(): lax.ppermute(piece, 'dp', [(i, i ^ k) for i in range(owners)])]
    ppermute x18, waiting for transfers between devices: 14.7 us -> 10.8 us  [to_partner(): lax.ppermute(piece, 'dp', [(i, i ^ k) for i in range(owners)])]
    unnamed x12 -> x8, local copies, waits for them, and re-layouts: 2.61 us -> 0.81 us
    pallas_call x1, Pallas kernels: 2.55 us -> 1.85 us  [with_kernels(): call(functools.partial(gather_kernel, plan), [packed] * parts + [straight...]
where the time goes in v10:
time: 63.5 us; the launch traced here: 63.3 us
  starting transfers between devices  36.6 us (58%)
  Pallas kernels  14.1 us (22%)
  waiting for transfers between devices  11.1 us (17%)
  local copies, waits for them, and re-layouts  0.81 us (1%)
  between operations  0.76 us (1%)
    ppermute x18, starting transfers between devices, to_partner(): lax.ppermute(piece, 'dp', [(i, i ^ k) for i in range(owners)])  36.3 us
    ppermute x18, waiting for transfers between devices, to_partner(): lax.ppermute(piece, 'dp', [(i, i ^ k) for i in range(owners)])  10.8 us
    pallas_call x1, Pallas kernels, with_kernels(): call(prep_kernel, [jax.ShapeDtypeStruct((owners, rows, 2 * tokens), bf16)...  5.35 us
    pallas_call x1, Pallas kernels, with_kernels(): call(functools.partial(input_kernel, plan, scale), jax.ShapeDtypeStruct((...  1.99 us
    pallas_call x1, Pallas kernels, with_kernels(): call(functools.partial(gather_kernel, plan), [packed] * parts + [straight...  1.85 us
    pallas_call x1, Pallas kernels, with_kernels(): call(functools.partial(merge_kernel, plan, tuple((key for key, _ in merge...  1.75 us
  transfers between devices with their start and end apart: 20, of which 6 were waited for; matrix products, arithmetic and copies ran while one was open for 0% of the time, Pallas kernels for 15%

profile of v10, /device:TPU:0, one launch (start us, length us, event | category | flops | bytes accessed | tf_op | source)
XLA Modules:
  0.0 63.3 jit_solution(15420266918836453606)
XLA Ops:
  0.7 0.8 %copy-done.3 = s32[8,1]{0,1:T(1,128)S(1)} copy-done((s32[8,1]{0,1:T(1,128)S(1)}, s32[8,1]{0,1:T(1,128)}, u32[]{:S(2)}) %copy-start.3) | copy-done | bytes 56
  1.5 1.9 %shard_map.68 = (bf16[256,128]{1,0:T(8,128)(2,1)S(1)}, bf16[256,128]{1,0:T(8,128)(2,1)S(1)}, bf16[512,128]{1,0:T(8,128)(2,1)S(1)}, bf16[512,128]{1,0:T(8,128)(2,...) custom-call(s32[8]{0:T(128)S(1)} %bitcast.11, ...), custom_call_target="tpu_custom_call" | custom-call | bytes 2097152 | tf_op jit(solution)/shard_map/pallas_call | solution.py:310
  3.3 4.1 %collective-permute-start = (bf16[256,128]{1,0:T(8,128)(2,1)S(1)}, bf16[256,128]{1,0:T(8,128)(2,1)S(1)}, u32[]{:S(2)}, u32[]{:S(2)}) collective-permute-start(bf16[256,128]{1,0:T(8,128)(2,1)S(1)} %get-tuple-element.30), channel_id=1, source_target_pairs={{0,8},{2,10},{4,12},{6,14},{8,0},{10,2},{12,4},{14,6},{1,9},{3,11}... | collective-permute-start | bytes 196616 | tf_op jit(solution)/shard_map/ppermute | solution.py:273
  7.4 1.3 %collective-permute-start.3 = (bf16[256,128]{1,0:T(8,128)(2,1)S(1)}, bf16[256,128]{1,0:T(8,128)(2,1)S(1)}, u32[]{:S(2)}, u32[]{:S(2)}) collective-permute-start(bf16[256,128]{1,0:T(8,128)(2,1)S(1)} %get-tuple-element.35), channel_id=1, source_target_pairs={{0,10},{2,8},{4,14},{6,12},{8,2},{10,0},{12,6},{14,4},{1,11},{3,9}... | collective-permute-start | bytes 196616 | tf_op jit(solution)/shard_map/ppermute | solution.py:273
  8.7 0.3 collective-permute-start.1
  9.0 1.8 %collective-permute-start.2 = (bf16[512,128]{1,0:T(8,128)(2,1)S(1)}, bf16[512,128]{1,0:T(8,128)(2,1)S(1)}, u32[]{:S(2)}, u32[]{:S(2)}) collective-permute-start(bf16[512,128]{1,0:T(8,128)(2,1)S(1)} %get-tuple-element.34), channel_id=1, source_target_pairs={{0,4},{2,6},{4,0},{6,2},{8,12},{10,14},{12,8},{14,10},{1,5},{3,7},... | collective-permute-start | bytes 393224 | tf_op jit(solution)/shard_map/ppermute | solution.py:273
  10.8 2.5 %collective-permute-start.4 = (bf16[512,128]{1,0:T(8,128)(2,1)S(1)}, bf16[512,128]{1,0:T(8,128)(2,1)S(1)}, u32[]{:S(2)}, u32[]{:S(2)}) collective-permute-start(bf16[512,128]{1,0:T(8,128)(2,1)S(1)} %get-tuple-element.36), channel_id=1, source_target_pairs={{0,12},{2,14},{4,8},{6,10},{8,4},{10,6},{12,0},{14,2},{1,13},{3,15... | collective-permute-start | bytes 393224 | tf_op jit(solution)/shard_map/ppermute | solution.py:273
  13.3 3.7 %collective-permute-start.5 = (bf16[512,128]{1,0:T(8,128)(2,1)S(1)}, bf16[512,128]{1,0:T(8,128)(2,1)S(1)}, u32[]{:S(2)}, u32[]{:S(2)}) collective-permute-start(bf16[512,128]{1,0:T(8,128)(2,1)S(1)} %get-tuple-element.37), channel_id=1, source_target_pairs={{0,14},{2,12},{4,10},{6,8},{8,6},{10,4},{12,2},{14,0},{1,15},{3,13... | collective-permute-start | bytes 393224 | tf_op jit(solution)/shard_map/ppermute | solution.py:273
  17.0 3.3 %collective-permute-start.8 = (bf16[256,128]{1,0:T(8,128)(2,1)S(1)}, bf16[256,128]{1,0:T(8,128)(2,1)S(1)}, u32[]{:S(2)}, u32[]{:S(2)}) collective-permute-start(bf16[256,128]{1,0:T(8,128)(2,1)S(1)} %get-tuple-element.42), channel_id=1, source_target_pairs={{0,8},{2,10},{4,12},{6,14},{8,0},{10,2},{12,4},{14,6},{1,9},{3,11}... | collective-permute-start | bytes 196616 | tf_op jit(solution)/shard_map/ppermute | solution.py:273
  20.3 4.5 %collective-permute-start.9 = (bf16[256,128]{1,0:T(8,128)(2,1)S(1)}, bf16[256,128]{1,0:T(8,128)(2,1)S(1)}, u32[]{:S(2)}, u32[]{:S(2)}) collective-permute-start(bf16[256,128]{1,0:T(8,128)(2,1)S(1)} %get-tuple-element.43), channel_id=1, source_target_pairs={{0,10},{2,8},{4,14},{6,12},{8,2},{10,0},{12,6},{14,4},{1,11},{3,9}... | collective-permute-start | bytes 196616 | tf_op jit(solution)/shard_map/ppermute | solution.py:273
  24.8 5.3 %shard_map.69 = (bf16[8,512,256]{2,1,0:T(8,128)(2,1)S(1)}, bf16[512,128]{1,0:T(8,128)(2,1)S(1)}, bf16[96,512,128]{2,1,0:T(8,128)(2,1)}) custom-call(s32[8]{0:T(128)S(1)} %bitcast.12, s32[1]{0:T(128)} %bitcast.here, bf16[96,512,128]{2,1,0:T(8,128)(2,1)} %bitcast.15, bf16[256,128]{1,0:T(8,128)(2,1)S(1)} %collective-permute-done.after.refs_2_, ...), custom_call_target="tpu_custom_call" | custom-call | bytes 16777216 | tf_op jit(solution)/shard_map/pallas_call | solution.py:325
  30.2 0.7 %shard_map.70 = (f32[64,128]{1,0:T(8,128)S(1)}, f32[64,128]{1,0:T(8,128)S(1)}) custom-call(s32[1]{0:T(128)} %bitcast.here, bf16[128,4096]{1,0:T(8,128)(2,1)S(1)} %copy-done, bf16[128,4096]{1,0:T(8,128)(2,1)S(1)} %copy-done.1, bf16[512,128]{1,0:T(8,128)(2,1)S(1)} %collective-permute-done.1.refs_0_.refs_3_, ...), custom_call_target="tpu_custom_call" | custom-call | bytes 1024 | tf_op jit(solution)/shard_map/pallas_call | solution.py:350
  31.0 0.9 %collective-permute-done.9.refs_1_ = bf16[256,128]{1,0:T(8,128)(2,1)S(1)} collective-permute-done((bf16[256,128]{1,0:T(8,128)(2,1)S(1)}, bf16[256,128]{1,0:T(8,128)(2,1)S(1)}, u32[]{:S(2)}, u32[]{:S(2)}) %collective-permute-start.9) | collective-permute-done | bytes 65568 | tf_op jit(solution)/shard_map/ppermute | solution.py:273
  31.9 0.3 collective-permute-done.7.other.d_other
  32.2 0.8 %shard_map.71 = (bf16[256,128]{1,0:T(8,128)(2,1)S(1)}, bf16[256,128]{1,0:T(8,128)(2,1)S(1)}) custom-call(s32[1]{0:T(128)} %bitcast.here, s32[8]{0:T(128)S(1)} %bitcast.7, f32[64,128]{1,0:T(8,128)S(1)} %get-tuple-element.56.mine.d_mine, f32[64,128]{1,0:T(8,128)S(1)} %collective-permute-done.7.other.d_other, bf16[8,512,256]{2,1,0:T(8,128)(2,1)S(1)} %get-tuple-element.31.turned), custom_call_target="tpu_custom_call" | custom-call | bytes 1024 | tf_op jit(solution)/shard_map/pallas_call | solution.py:358
  33.0 0.4 shard_map.72.mine
  33.4 0.2 collective-permute-start.10
  33.6 1.3 %collective-permute-start.16 = (bf16[256,128]{1,0:T(8,128)(2,1)S(1)}, bf16[256,128]{1,0:T(8,128)(2,1)S(1)}, u32[]{:S(2)}, u32[]{:S(2)}) collective-permute-start(bf16[256,128]{1,0:T(8,128)(2,1)S(1)} %get-tuple-element.45), channel_id=1, source_target_pairs={{0,8},{2,10},{4,12},{6,14},{8,0},{10,2},{12,4},{14,6},{1,9},{3,11}... | collective-permute-start | bytes 196616 | tf_op jit(solution)/shard_map/ppermute | solution.py:273
  34.9 1.9 %collective-permute-start.17 = (bf16[256,128]{1,0:T(8,128)(2,1)S(1)}, bf16[256,128]{1,0:T(8,128)(2,1)S(1)}, u32[]{:S(2)}, u32[]{:S(2)}) collective-permute-start(bf16[256,128]{1,0:T(8,128)(2,1)S(1)} %get-tuple-element.46), channel_id=1, source_target_pairs={{0,10},{2,8},{4,14},{6,12},{8,2},{10,0},{12,6},{14,4},{1,11},{3,9}... | collective-permute-start | bytes 196616 | tf_op jit(solution)/shard_map/ppermute | solution.py:273
  36.8 1.2 %shard_map.73 = (bf16[512,128]{1,0:T(8,128)(2,1)S(1)}, bf16[512,128]{1,0:T(8,128)(2,1)S(1)}, bf16[512,128]{1,0:T(8,128)(2,1)S(1)}, bf16[512,128]{1,0:T(8,128)(2,...) custom-call(s32[1]{0:T(128)} %bitcast.here, ...), custom_call_target="tpu_custom_call" | custom-call | bytes 1024 | tf_op jit(solution)/shard_map/pallas_call | solution.py:375
  38.0 1.3 %collective-permute-start.18 = (bf16[256,128]{1,0:T(8,128)(2,1)S(1)}, bf16[256,128]{1,0:T(8,128)(2,1)S(1)}, u32[]{:S(2)}, u32[]{:S(2)}) collective-permute-start(bf16[256,128]{1,0:T(8,128)(2,1)S(1)} %get-tuple-element.54), channel_id=1, source_target_pairs={{0,8},{2,10},{4,12},{6,14},{8,0},{10,2},{12,4},{14,6},{1,9},{3,11}... | collective-permute-start | bytes 196616 | tf_op jit(solution)/shard_map/ppermute | solution.py:273
  39.3 2.3 %collective-permute-start.19 = (bf16[256,128]{1,0:T(8,128)(2,1)S(1)}, bf16[256,128]{1,0:T(8,128)(2,1)S(1)}, u32[]{:S(2)}, u32[]{:S(2)}) collective-permute-start(bf16[256,128]{1,0:T(8,128)(2,1)S(1)} %get-tuple-element.55), channel_id=1, source_target_pairs={{0,10},{2,8},{4,14},{6,12},{8,2},{10,0},{12,6},{14,4},{1,11},{3,9}... | collective-permute-start | bytes 196616 | tf_op jit(solution)/shard_map/ppermute | solution.py:273
  41.6 2.9 %collective-permute-start.11 = (bf16[512,128]{1,0:T(8,128)(2,1)S(1)}, bf16[512,128]{1,0:T(8,128)(2,1)S(1)}, u32[]{:S(2)}, u32[]{:S(2)}) collective-permute-start(bf16[512,128]{1,0:T(8,128)(2,1)S(1)} %get-tuple-element.48), channel_id=1, source_target_pairs={{0,12},{2,14},{4,8},{6,10},{8,4},{10,6},{12,0},{14,2},{1,13},{3,15... | collective-permute-start | bytes 393224 | tf_op jit(solution)/shard_map/ppermute | solution.py:273
  44.5 0.5 collective-permute-start.12
  45.1 4.0 %collective-permute-start.13 = (bf16[512,128]{1,0:T(8,128)(2,1)S(1)}, bf16[512,128]{1,0:T(8,128)(2,1)S(1)}, u32[]{:S(2)}, u32[]{:S(2)}) collective-permute-start(bf16[512,128]{1,0:T(8,128)(2,1)S(1)} %get-tuple-element.50), channel_id=1, source_target_pairs={{0,14},{2,12},{4,10},{6,8},{8,6},{10,4},{12,2},{14,0},{1,15},{3,13... | collective-permute-start | bytes 393224 | tf_op jit(solution)/shard_map/ppermute | solution.py:273
  49.0 3.0 %collective-permute-done.18.refs_8_ = bf16[256,128]{1,0:T(8,128)(2,1)S(1)} collective-permute-done((bf16[256,128]{1,0:T(8,128)(2,1)S(1)}, bf16[256,128]{1,0:T(8,128)(2,1)S(1)}, u32[]{:S(2)}, u32[]{:S(2)}) %collective-permute-start.18) | collective-permute-done | bytes 65568 | tf_op jit(solution)/shard_map/ppermute | solution.py:273
  52.1 2.9 %collective-permute-done.19.refs_9_ = bf16[256,128]{1,0:T(8,128)(2,1)S(1)} collective-permute-done((bf16[256,128]{1,0:T(8,128)(2,1)S(1)}, bf16[256,128]{1,0:T(8,128)(2,1)S(1)}, u32[]{:S(2)}, u32[]{:S(2)}) %collective-permute-start.19) | collective-permute-done | bytes 65568 | tf_op jit(solution)/shard_map/ppermute | solution.py:273
  54.9 0.6 collective-permute-start.15
  55.5 2.0 %shard_map.74 = bf16[128,4096]{1,0:T(8,128)(2,1)} custom-call(s32[1]{0:T(128)} %bitcast.here, s32[8]{0:T(128)S(1)} %bitcast.9, f32[64,128]{1,0:T(8,128)S(1)} %get-tuple-element.56.mine.d_mine, f32[64,128]{1,0:T(8,128)S(1)} %collective-permute-done.7.other.d_other, bf16[256,128]{1,0:T(8,128)(2,1)S(1)} %collective-permute-done.8.refs_0_, ...), custom_call_target="tpu_custom_call" | custom-call | flops 134217728 | bytes 2097152 | tf_op jit(solution)/shard_map/pallas_call | solution.py:385
  57.5 2.0 %collective-permute-done.14.refs_3_ = bf16[512,128]{1,0:T(8,128)(2,1)S(1)} collective-permute-done((bf16[512,128]{1,0:T(8,128)(2,1)S(1)}, bf16[512,128]{1,0:T(8,128)(2,1)S(1)}, u32[]{:S(2)}, u32[]{:S(2)}) %collective-permute-start.14) | collective-permute-done | bytes 131104 | tf_op jit(solution)/shard_map/ppermute | solution.py:273
  59.5 2.0 %collective-permute-done.15.refs_4_ = bf16[512,128]{1,0:T(8,128)(2,1)S(1)} collective-permute-done((bf16[512,128]{1,0:T(8,128)(2,1)S(1)}, bf16[512,128]{1,0:T(8,128)(2,1)S(1)}, u32[]{:S(2)}, u32[]{:S(2)}) %collective-permute-start.15) | collective-permute-done | bytes 131104 | tf_op jit(solution)/shard_map/ppermute | solution.py:273
  61.6 1.7 %shard_map.75 = bf16[96,512,128]{2,1,0:T(8,128)(2,1)} custom-call(s32[8]{0:T(128)S(1)} %bitcast.13, s32[1]{0:T(128)} %bitcast.here, s32[8]{0:T(128)S(1)} %bitcast.10, bf16[512,128]{1,0:T(8,128)(2,1)S(1)} %collective-permute-done.11.refs_0_, bf16[512,128]{1,0:T(8,128)(2,1)S(1)} %collective-permute-done.12.refs_1_, ...), custom_call_target="tpu_custom_call", output_to_operand_aliasing={{}: (13, {})} | custom-call | bytes 2097152 | tf_op jit(solution)/shard_map/pallas_call | solution.py:398
  (24 shorter events, 0.1 us)
Async XLA Ops:
  0.6 24.2 %copy-start = (bf16[128,4096]{1,0:T(8,128)(2,1)S(1)}, bf16[128,4096]{1,0:T(8,128)(2,1)}, u32[]{:S(2)}) copy-start(bf16[128,4096]{1,0:T(8,128)(2,1)} %x.4) | copy-start | bytes 3145732
  0.6 24.2 %copy-start.1 = (bf16[128,4096]{1,0:T(8,128)(2,1)S(1)}, bf16[128,4096]{1,0:T(8,128)(2,1)}, u32[]{:S(2)}) copy-start(bf16[128,4096]{1,0:T(8,128)(2,1)} %y.3) | copy-start | bytes 3145732
  0.7 0.8 %copy-start.3 = (s32[8,1]{0,1:T(1,128)S(1)}, s32[8,1]{0,1:T(1,128)}, u32[]{:S(2)}) copy-start(s32[8,1]{0,1:T(1,128)} %param.8) | copy-start | bytes 100
  1.5 30.7 %copy-start.2 = (s32[8,1]{0,1:T(1,128)S(1)}, s32[8,1]{0,1:T(1,128)}, u32[]{:S(2)}) copy-start(s32[8,1]{0,1:T(1,128)} %param.9) | copy-start | bytes 100
  3.3 10.0 %collective-permute-start = (bf16[256,128]{1,0:T(8,128)(2,1)S(1)}, bf16[256,128]{1,0:T(8,128)(2,1)S(1)}, u32[]{:S(2)}, u32[]{:S(2)}) collective-permute-start(bf16[256,128]{1,0:T(8,128)(2,1)S(1)} %get-tuple-element.30), channel_id=1, source_target_pairs={{0,8},{2,10},{4,12},{6,14},{8,0},{10,2},{12,4},{14,6},{1,9},{3,11}... | collective-permute-start | bytes 196616 | tf_op jit(solution)/shard_map/ppermute | solution.py:273
  7.4 9.6 %collective-permute-start.3 = (bf16[256,128]{1,0:T(8,128)(2,1)S(1)}, bf16[256,128]{1,0:T(8,128)(2,1)S(1)}, u32[]{:S(2)}, u32[]{:S(2)}) collective-permute-start(bf16[256,128]{1,0:T(8,128)(2,1)S(1)} %get-tuple-element.35), channel_id=1, source_target_pairs={{0,10},{2,8},{4,14},{6,12},{8,2},{10,0},{12,6},{14,4},{1,11},{3,9}... | collective-permute-start | bytes 196616 | tf_op jit(solution)/shard_map/ppermute | solution.py:273
  8.7 8.3 %collective-permute-start.1 = (bf16[512,128]{1,0:T(8,128)(2,1)S(1)}, bf16[512,128]{1,0:T(8,128)(2,1)S(1)}, u32[]{:S(2)}, u32[]{:S(2)}) collective-permute-start(bf16[512,128]{1,0:T(8,128)(2,1)S(1)} %get-tuple-element.33), channel_id=1, source_target_pairs={{0,2},{2,0},{4,6},{6,4},{8,10},{10,8},{12,14},{14,12},{1,3},{3,1},... | collective-permute-start | bytes 393224 | tf_op jit(solution)/shard_map/ppermute | solution.py:273
  9.0 11.3 %collective-permute-start.2 = (bf16[512,128]{1,0:T(8,128)(2,1)S(1)}, bf16[512,128]{1,0:T(8,128)(2,1)S(1)}, u32[]{:S(2)}, u32[]{:S(2)}) collective-permute-start(bf16[512,128]{1,0:T(8,128)(2,1)S(1)} %get-tuple-element.34), channel_id=1, source_target_pairs={{0,4},{2,6},{4,0},{6,2},{8,12},{10,14},{12,8},{14,10},{1,5},{3,7},... | collective-permute-start | bytes 393224 | tf_op jit(solution)/shard_map/ppermute | solution.py:273
  10.8 19.4 %collective-permute-start.4 = (bf16[512,128]{1,0:T(8,128)(2,1)S(1)}, bf16[512,128]{1,0:T(8,128)(2,1)S(1)}, u32[]{:S(2)}, u32[]{:S(2)}) collective-permute-start(bf16[512,128]{1,0:T(8,128)(2,1)S(1)} %get-tuple-element.36), channel_id=1, source_target_pairs={{0,12},{2,14},{4,8},{6,10},{8,4},{10,6},{12,0},{14,2},{1,13},{3,15... | collective-permute-start | bytes 393224 | tf_op jit(solution)/shard_map/ppermute | solution.py:273
  13.3 16.9 %collective-permute-start.5 = (bf16[512,128]{1,0:T(8,128)(2,1)S(1)}, bf16[512,128]{1,0:T(8,128)(2,1)S(1)}, u32[]{:S(2)}, u32[]{:S(2)}) collective-permute-start(bf16[512,128]{1,0:T(8,128)(2,1)S(1)} %get-tuple-element.37), channel_id=1, source_target_pairs={{0,14},{2,12},{4,10},{6,8},{8,6},{10,4},{12,2},{14,0},{1,15},{3,13... | collective-permute-start | bytes 393224 | tf_op jit(solution)/shard_map/ppermute | solution.py:273
  17.0 13.2 %collective-permute-start.6 = (bf16[512,128]{1,0:T(8,128)(2,1)S(1)}, bf16[512,128]{1,0:T(8,128)(2,1)S(1)}, u32[]{:S(2)}, u32[]{:S(2)}) collective-permute-start(bf16[512,128]{1,0:T(8,128)(2,1)S(1)} %get-tuple-element.38), channel_id=1, source_target_pairs={{0,6},{2,4},{4,2},{6,0},{8,14},{10,12},{12,10},{14,8},{1,7},{3,5},... | collective-permute-start | bytes 393224 | tf_op jit(solution)/shard_map/ppermute | solution.py:273
  17.0 14.0 %collective-permute-start.8 = (bf16[256,128]{1,0:T(8,128)(2,1)S(1)}, bf16[256,128]{1,0:T(8,128)(2,1)S(1)}, u32[]{:S(2)}, u32[]{:S(2)}) collective-permute-start(bf16[256,128]{1,0:T(8,128)(2,1)S(1)} %get-tuple-element.42), channel_id=1, source_target_pairs={{0,8},{2,10},{4,12},{6,14},{8,0},{10,2},{12,4},{14,6},{1,9},{3,11}... | collective-permute-start | bytes 196616 | tf_op jit(solution)/shard_map/ppermute | solution.py:273
  20.3 11.6 %collective-permute-start.9 = (bf16[256,128]{1,0:T(8,128)(2,1)S(1)}, bf16[256,128]{1,0:T(8,128)(2,1)S(1)}, u32[]{:S(2)}, u32[]{:S(2)}) collective-permute-start(bf16[256,128]{1,0:T(8,128)(2,1)S(1)} %get-tuple-element.43), channel_id=1, source_target_pairs={{0,10},{2,8},{4,14},{6,12},{8,2},{10,0},{12,6},{14,4},{1,11},{3,9}... | collective-permute-start | bytes 196616 | tf_op jit(solution)/shard_map/ppermute | solution.py:273
  30.9 1.3 %collective-permute-start.7 = (f32[64,128]{1,0:T(8,128)S(1)}, f32[64,128]{1,0:T(8,128)S(1)}, u32[]{:S(2)}, u32[]{:S(2)}) collective-permute-start(f32[64,128]{1,0:T(8,128)S(1)} %get-tuple-element.56.mine.d_mine), channel_id=1, source_target_pairs={{0,1},{1,0},{2,3},{3,2},{4,5},{5,4},{6,7},{7,6},{8,9},{9,8},{10,11... | collective-permute-start | bytes 98312 | tf_op jit(solution)/shard_map/ppermute | solution.py:290
  33.4 3.4 %collective-permute-start.10 = (f32[64,128]{1,0:T(8,128)S(1)}, f32[64,128]{1,0:T(8,128)S(1)}, u32[]{:S(2)}, u32[]{:S(2)}) collective-permute-start(f32[64,128]{1,0:T(8,128)S(1)} %shard_map.72.mine), channel_id=1, source_target_pairs={{0,1},{1,0},{2,3},{3,2},{4,5},{5,4},{6,7},{7,6},{8,9},{9,8},{10,11... | collective-permute-start | bytes 98312 | tf_op jit(solution)/shard_map/ppermute | solution.py:290
  33.6 10.9 %collective-permute-start.16 = (bf16[256,128]{1,0:T(8,128)(2,1)S(1)}, bf16[256,128]{1,0:T(8,128)(2,1)S(1)}, u32[]{:S(2)}, u32[]{:S(2)}) collective-permute-start(bf16[256,128]{1,0:T(8,128)(2,1)S(1)} %get-tuple-element.45), channel_id=1, source_target_pairs={{0,8},{2,10},{4,12},{6,14},{8,0},{10,2},{12,4},{14,6},{1,9},{3,11}... | collective-permute-start | bytes 196616 | tf_op jit(solution)/shard_map/ppermute | solution.py:273
  34.9 10.2 %collective-permute-start.17 = (bf16[256,128]{1,0:T(8,128)(2,1)S(1)}, bf16[256,128]{1,0:T(8,128)(2,1)S(1)}, u32[]{:S(2)}, u32[]{:S(2)}) collective-permute-start(bf16[256,128]{1,0:T(8,128)(2,1)S(1)} %get-tuple-element.46), channel_id=1, source_target_pairs={{0,10},{2,8},{4,14},{6,12},{8,2},{10,0},{12,6},{14,4},{1,11},{3,9}... | collective-permute-start | bytes 196616 | tf_op jit(solution)/shard_map/ppermute | solution.py:273
  38.0 14.0 %collective-permute-start.18 = (bf16[256,128]{1,0:T(8,128)(2,1)S(1)}, bf16[256,128]{1,0:T(8,128)(2,1)S(1)}, u32[]{:S(2)}, u32[]{:S(2)}) collective-permute-start(bf16[256,128]{1,0:T(8,128)(2,1)S(1)} %get-tuple-element.54), channel_id=1, source_target_pairs={{0,8},{2,10},{4,12},{6,14},{8,0},{10,2},{12,4},{14,6},{1,9},{3,11}... | collective-permute-start | bytes 196616 | tf_op jit(solution)/shard_map/ppermute | solution.py:273
  39.3 15.6 %collective-permute-start.19 = (bf16[256,128]{1,0:T(8,128)(2,1)S(1)}, bf16[256,128]{1,0:T(8,128)(2,1)S(1)}, u32[]{:S(2)}, u32[]{:S(2)}) collective-permute-start(bf16[256,128]{1,0:T(8,128)(2,1)S(1)} %get-tuple-element.55), channel_id=1, source_target_pairs={{0,10},{2,8},{4,14},{6,12},{8,2},{10,0},{12,6},{14,4},{1,11},{3,9}... | collective-permute-start | bytes 196616 | tf_op jit(solution)/shard_map/ppermute | solution.py:273
  41.6 15.9 %collective-permute-start.11 = (bf16[512,128]{1,0:T(8,128)(2,1)S(1)}, bf16[512,128]{1,0:T(8,128)(2,1)S(1)}, u32[]{:S(2)}, u32[]{:S(2)}) collective-permute-start(bf16[512,128]{1,0:T(8,128)(2,1)S(1)} %get-tuple-element.48), channel_id=1, source_target_pairs={{0,12},{2,14},{4,8},{6,10},{8,4},{10,6},{12,0},{14,2},{1,13},{3,15... | collective-permute-start | bytes 393224 | tf_op jit(solution)/shard_map/ppermute | solution.py:273
  44.5 13.0 %collective-permute-start.12 = (bf16[512,128]{1,0:T(8,128)(2,1)S(1)}, bf16[512,128]{1,0:T(8,128)(2,1)S(1)}, u32[]{:S(2)}, u32[]{:S(2)}) collective-permute-start(bf16[512,128]{1,0:T(8,128)(2,1)S(1)} %get-tuple-element.49), channel_id=1, source_target_pairs={{0,2},{2,0},{4,6},{6,4},{8,10},{10,8},{12,14},{14,12},{1,3},{3,1},... | collective-permute-start | bytes 393224 | tf_op jit(solution)/shard_map/ppermute | solution.py:273
  45.1 12.5 %collective-permute-start.13 = (bf16[512,128]{1,0:T(8,128)(2,1)S(1)}, bf16[512,128]{1,0:T(8,128)(2,1)S(1)}, u32[]{:S(2)}, u32[]{:S(2)}) collective-permute-start(bf16[512,128]{1,0:T(8,128)(2,1)S(1)} %get-tuple-element.50), channel_id=1, source_target_pairs={{0,14},{2,12},{4,10},{6,8},{8,6},{10,4},{12,2},{14,0},{1,15},{3,13... | collective-permute-start | bytes 393224 | tf_op jit(solution)/shard_map/ppermute | solution.py:273
  52.1 7.5 %collective-permute-start.14 = (bf16[512,128]{1,0:T(8,128)(2,1)S(1)}, bf16[512,128]{1,0:T(8,128)(2,1)S(1)}, u32[]{:S(2)}, u32[]{:S(2)}) collective-permute-start(bf16[512,128]{1,0:T(8,128)(2,1)S(1)} %get-tuple-element.51), channel_id=1, source_target_pairs={{0,4},{2,6},{4,0},{6,2},{8,12},{10,14},{12,8},{14,10},{1,5},{3,7},... | collective-permute-start | bytes 393224 | tf_op jit(solution)/shard_map/ppermute | solution.py:273
  54.9 6.6 %collective-permute-start.15 = (bf16[512,128]{1,0:T(8,128)(2,1)S(1)}, bf16[512,128]{1,0:T(8,128)(2,1)S(1)}, u32[]{:S(2)}, u32[]{:S(2)}) collective-permute-start(bf16[512,128]{1,0:T(8,128)(2,1)S(1)} %get-tuple-element.52), channel_id=1, source_target_pairs={{0,6},{2,4},{4,2},{6,0},{8,14},{10,12},{12,10},{14,8},{1,7},{3,5},... | collective-permute-start | bytes 393224 | tf_op jit(solution)/shard_map/ppermute | solution.py:273

commit v11 on v10

--- a/solution.py
+++ b/solution.py
@@ -9,11 +9,11 @@
 
 adapter_alpha = 128.0
 RANK_ORDER = ((False, 1), (False, 2), (True, 4), (True, 5), (False, 6), (False, 7), (False, 3))
-MERGE_ORDER = (("both", 6), ("both", 1), ("both", 7), ("both", 2), ("both", 3))
+MERGE_ORDER = (("both", 2), ("both", 6), ("both", 3), ("both", 7), ("both", 1))
 PREP_AFTER = 0
 PREP_VMEM = 40
 SPLIT = (4, 5)
-WHOLE = (6, 1, 7, 2, 3)
+WHOLE = (2, 6, 3, 7, 1)
 
 in_vmem = pl.BlockSpec(memory_space=pltpu.VMEM)
 in_smem = pl.BlockSpec(memory_space=pltpu.SMEM)
@@ -317,10 +317,7 @@
         vmem=53,
     )(ids, here, table)
     ups = to_partner(sent[:parts], split, owners)
-
     pairs = to_partner(sent[parts : parts + wholes], whole, owners)
-    downs = to_partner(sent[parts + wholes :], split, owners)
-
     step = 8
     turned, own, blank = call(
         prep_kernel,
@@ -340,6 +337,9 @@
         vmem=PREP_VMEM,
     )(ids, here, table, ups[PREP_AFTER], activations, cotangent)
 
+    held_back = list(sent[parts + wholes :])
+    held_back[-1] = after(held_back[-1], turned)
+    downs = to_partner(held_back, split, owners)
     pairs.append(own)
     whole += (0,)
     wholes += 1

time: 63.5 us -> 62.8 us (0.989)
  starting transfers between devices: 36.6 us -> 31.9 us
  waiting for transfers between devices: 11.1 us -> 15 us
    ppermute x18, starting transfers between devices: 36.3 us -> 31.8 us  [to_partner(): lax.ppermute(piece, 'dp', [(i, i ^ k) for i in range(owners)])]
    ppermute x18, waiting for transfers between devices: 10.8 us -> 15 us  [to_partner(): lax.ppermute(piece, 'dp', [(i, i ^ k) for i in range(owners)])]
  transfers between devices with their start and end apart: 20 -> 20, of which waited for: 6 -> 7; matrix products, arithmetic and copies ran while one was open for 0% -> 0% of each run, Pallas kernels for 15% -> 15%
where the time goes in v11:
time: 62.8 us; the launch traced here: 62.6 us
  starting transfers between devices  31.9 us (51%)
  waiting for transfers between devices  15 us (24%)
  Pallas kernels  14.1 us (22%)
  local copies, waits for them, and re-layouts  0.81 us (1%)
  between operations  0.76 us (1%)
    ppermute x18, starting transfers between devices, to_partner(): lax.ppermute(piece, 'dp', [(i, i ^ k) for i in range(owners)])  31.8 us
    ppermute x18, waiting for transfers between devices, to_partner(): lax.ppermute(piece, 'dp', [(i, i ^ k) for i in range(owners)])  15 us
    pallas_call x1, Pallas kernels, with_kernels(): call(prep_kernel, [jax.ShapeDtypeStruct((owners, rows, 2 * tokens), bf16)...  5.35 us
    pallas_call x1, Pallas kernels, with_kernels(): call(functools.partial(input_kernel, plan, scale), jax.ShapeDtypeStruct((...  1.98 us
    pallas_call x1, Pallas kernels, with_kernels(): call(functools.partial(gather_kernel, plan), [packed] * parts + [straight...  1.85 us
    pallas_call x1, Pallas kernels, with_kernels(): call(functools.partial(merge_kernel, plan, tuple((key for key, _ in merge...  1.75 us
  transfers between devices with their start and end apart: 20, of which 7 were waited for; matrix products, arithmetic and copies ran while one was open for 0% of the time, Pallas kernels for 15%

profile of v11, /device:TPU:0, one launch (start us, length us, event | category | flops | bytes accessed | tf_op | source)
XLA Modules:
  0.0 62.6 jit_solution(7137624290877864792)
XLA Ops:
  0.7 0.8 %copy-done.3 = s32[8,1]{0,1:T(1,128)S(1)} copy-done((s32[8,1]{0,1:T(1,128)S(1)}, s32[8,1]{0,1:T(1,128)}, u32[]{:S(2)}) %copy-start.3) | copy-done | bytes 56
  1.5 1.9 %shard_map.68 = (bf16[256,128]{1,0:T(8,128)(2,1)S(1)}, bf16[256,128]{1,0:T(8,128)(2,1)S(1)}, bf16[512,128]{1,0:T(8,128)(2,1)S(1)}, bf16[512,128]{1,0:T(8,128)(2,...) custom-call(s32[8]{0:T(128)S(1)} %bitcast.11, ...), custom_call_target="tpu_custom_call" | custom-call | bytes 2097152 | tf_op jit(solution)/shard_map/pallas_call | solution.py:310
  3.3 4.1 %collective-permute-start = (bf16[256,128]{1,0:T(8,128)(2,1)S(1)}, bf16[256,128]{1,0:T(8,128)(2,1)S(1)}, u32[]{:S(2)}, u32[]{:S(2)}) collective-permute-start(bf16[256,128]{1,0:T(8,128)(2,1)S(1)} %get-tuple-element.31), channel_id=1, source_target_pairs={{0,8},{2,10},{4,12},{6,14},{8,0},{10,2},{12,4},{14,6},{1,9},{3,11}... | collective-permute-start | bytes 196616 | tf_op jit(solution)/shard_map/ppermute | solution.py:273
  7.4 1.3 %collective-permute-start.3 = (bf16[256,128]{1,0:T(8,128)(2,1)S(1)}, bf16[256,128]{1,0:T(8,128)(2,1)S(1)}, u32[]{:S(2)}, u32[]{:S(2)}) collective-permute-start(bf16[256,128]{1,0:T(8,128)(2,1)S(1)} %get-tuple-element.36), channel_id=1, source_target_pairs={{0,10},{2,8},{4,14},{6,12},{8,2},{10,0},{12,6},{14,4},{1,11},{3,9}... | collective-permute-start | bytes 196616 | tf_op jit(solution)/shard_map/ppermute | solution.py:273
  8.7 0.3 collective-permute-start.1
  9.0 1.8 %collective-permute-start.2 = (bf16[512,128]{1,0:T(8,128)(2,1)S(1)}, bf16[512,128]{1,0:T(8,128)(2,1)S(1)}, u32[]{:S(2)}, u32[]{:S(2)}) collective-permute-start(bf16[512,128]{1,0:T(8,128)(2,1)S(1)} %get-tuple-element.35), channel_id=1, source_target_pairs={{0,4},{2,6},{4,0},{6,2},{8,12},{10,14},{12,8},{14,10},{1,5},{3,7},... | collective-permute-start | bytes 393224 | tf_op jit(solution)/shard_map/ppermute | solution.py:273
  10.8 2.5 %collective-permute-start.4 = (bf16[512,128]{1,0:T(8,128)(2,1)S(1)}, bf16[512,128]{1,0:T(8,128)(2,1)S(1)}, u32[]{:S(2)}, u32[]{:S(2)}) collective-permute-start(bf16[512,128]{1,0:T(8,128)(2,1)S(1)} %get-tuple-element.37), channel_id=1, source_target_pairs={{0,12},{2,14},{4,8},{6,10},{8,4},{10,6},{12,0},{14,2},{1,13},{3,15... | collective-permute-start | bytes 393224 | tf_op jit(solution)/shard_map/ppermute | solution.py:273
  13.3 3.7 %collective-permute-start.5 = (bf16[512,128]{1,0:T(8,128)(2,1)S(1)}, bf16[512,128]{1,0:T(8,128)(2,1)S(1)}, u32[]{:S(2)}, u32[]{:S(2)}) collective-permute-start(bf16[512,128]{1,0:T(8,128)(2,1)S(1)} %get-tuple-element.38), channel_id=1, source_target_pairs={{0,14},{2,12},{4,10},{6,8},{8,6},{10,4},{12,2},{14,0},{1,15},{3,13... | collective-permute-start | bytes 393224 | tf_op jit(solution)/shard_map/ppermute | solution.py:273
  17.0 5.3 %shard_map.69 = (bf16[8,512,256]{2,1,0:T(8,128)(2,1)S(1)}, bf16[512,128]{1,0:T(8,128)(2,1)S(1)}, bf16[96,512,128]{2,1,0:T(8,128)(2,1)}) custom-call(s32[8]{0:T(128)S(1)} %bitcast.12, s32[1]{0:T(128)} %bitcast.here, bf16[96,512,128]{2,1,0:T(8,128)(2,1)} %bitcast.15, bf16[256,128]{1,0:T(8,128)(2,1)S(1)} %collective-permute-done.after.refs_2_, ...), custom_call_target="tpu_custom_call" | custom-call | bytes 16777216 | tf_op jit(solution)/shard_map/pallas_call | solution.py:322
  22.4 3.3 %collective-permute-start.8 = (bf16[256,128]{1,0:T(8,128)(2,1)S(1)}, bf16[256,128]{1,0:T(8,128)(2,1)S(1)}, u32[]{:S(2)}, u32[]{:S(2)}) collective-permute-start(bf16[256,128]{1,0:T(8,128)(2,1)S(1)} %get-tuple-element.43), channel_id=1, source_target_pairs={{0,8},{2,10},{4,12},{6,14},{8,0},{10,2},{12,4},{14,6},{1,9},{3,11}... | collective-permute-start | bytes 196616 | tf_op jit(solution)/shard_map/ppermute | solution.py:273
  25.7 0.6 collective-permute-start.9
  26.3 0.7 %shard_map.70 = (f32[64,128]{1,0:T(8,128)S(1)}, f32[64,128]{1,0:T(8,128)S(1)}) custom-call(s32[1]{0:T(128)} %bitcast.here, bf16[128,4096]{1,0:T(8,128)(2,1)S(1)} %copy-done, bf16[128,4096]{1,0:T(8,128)(2,1)S(1)} %copy-done.1, bf16[512,128]{1,0:T(8,128)(2,1)S(1)} %collective-permute-done.1.refs_0_.refs_6_, ...), custom_call_target="tpu_custom_call" | custom-call | bytes 1024 | tf_op jit(solution)/shard_map/pallas_call | solution.py:350
  27.1 4.0 %collective-permute-done.8.refs_0_ = bf16[256,128]{1,0:T(8,128)(2,1)S(1)} collective-permute-done((bf16[256,128]{1,0:T(8,128)(2,1)S(1)}, bf16[256,128]{1,0:T(8,128)(2,1)S(1)}, u32[]{:S(2)}, u32[]{:S(2)}) %collective-permute-start.8) | collective-permute-done | bytes 65568 | tf_op jit(solution)/shard_map/ppermute | solution.py:273
  31.1 1.4 %collective-permute-done.9.refs_1_ = bf16[256,128]{1,0:T(8,128)(2,1)S(1)} collective-permute-done((bf16[256,128]{1,0:T(8,128)(2,1)S(1)}, bf16[256,128]{1,0:T(8,128)(2,1)S(1)}, u32[]{:S(2)}, u32[]{:S(2)}) %collective-permute-start.9) | collective-permute-done | bytes 65568 | tf_op jit(solution)/shard_map/ppermute | solution.py:273
  32.5 0.8 %shard_map.71 = (bf16[256,128]{1,0:T(8,128)(2,1)S(1)}, bf16[256,128]{1,0:T(8,128)(2,1)S(1)}) custom-call(s32[1]{0:T(128)} %bitcast.here, s32[8]{0:T(128)S(1)} %bitcast.7, f32[64,128]{1,0:T(8,128)S(1)} %get-tuple-element.58.mine.d_mine, f32[64,128]{1,0:T(8,128)S(1)} %collective-permute-done.7.other.d_other, bf16[8,512,256]{2,1,0:T(8,128)(2,1)S(1)} %get-tuple-element.32.turned), custom_call_target="tpu_custom_call" | custom-call | bytes 1024 | tf_op jit(solution)/shard_map/pallas_call | solution.py:358
  33.3 0.4 shard_map.72.mine
  33.9 3.3 %collective-permute-start.17 = (bf16[256,128]{1,0:T(8,128)(2,1)S(1)}, bf16[256,128]{1,0:T(8,128)(2,1)S(1)}, u32[]{:S(2)}, u32[]{:S(2)}) collective-permute-start(bf16[256,128]{1,0:T(8,128)(2,1)S(1)} %get-tuple-element.48), channel_id=1, source_target_pairs={{0,10},{2,8},{4,14},{6,12},{8,2},{10,0},{12,6},{14,4},{1,11},{3,9}... | collective-permute-start | bytes 196616 | tf_op jit(solution)/shard_map/ppermute | solution.py:273
  37.1 1.2 %shard_map.73 = (bf16[512,128]{1,0:T(8,128)(2,1)S(1)}, bf16[512,128]{1,0:T(8,128)(2,1)S(1)}, bf16[512,128]{1,0:T(8,128)(2,1)S(1)}, bf16[512,128]{1,0:T(8,128)(2,...) custom-call(s32[1]{0:T(128)} %bitcast.here, ...), custom_call_target="tpu_custom_call" | custom-call | bytes 1024 | tf_op jit(solution)/shard_map/pallas_call | solution.py:375
  38.4 0.1 collective-permute-start.18
  38.5 3.4 %collective-permute-start.19 = (bf16[256,128]{1,0:T(8,128)(2,1)S(1)}, bf16[256,128]{1,0:T(8,128)(2,1)S(1)}, u32[]{:S(2)}, u32[]{:S(2)}) collective-permute-start(bf16[256,128]{1,0:T(8,128)(2,1)S(1)} %get-tuple-element.57), channel_id=1, source_target_pairs={{0,10},{2,8},{4,14},{6,12},{8,2},{10,0},{12,6},{14,4},{1,11},{3,9}... | collective-permute-start | bytes 196616 | tf_op jit(solution)/shard_map/ppermute | solution.py:273
  41.9 0.8 %collective-permute-start.11 = (bf16[512,128]{1,0:T(8,128)(2,1)S(1)}, bf16[512,128]{1,0:T(8,128)(2,1)S(1)}, u32[]{:S(2)}, u32[]{:S(2)}) collective-permute-start(bf16[512,128]{1,0:T(8,128)(2,1)S(1)} %get-tuple-element.50), channel_id=1, source_target_pairs={{0,4},{2,6},{4,0},{6,2},{8,12},{10,14},{12,8},{14,10},{1,5},{3,7},... | collective-permute-start | bytes 393224 | tf_op jit(solution)/shard_map/ppermute | solution.py:273
  42.7 1.1 %collective-permute-done.16.refs_6_ = bf16[256,128]{1,0:T(8,128)(2,1)S(1)} collective-permute-done((bf16[256,128]{1,0:T(8,128)(2,1)S(1)}, bf16[256,128]{1,0:T(8,128)(2,1)S(1)}, u32[]{:S(2)}, u32[]{:S(2)}) %collective-permute-start.16) | collective-permute-done | bytes 65568 | tf_op jit(solution)/shard_map/ppermute | solution.py:273
  43.8 1.7 %collective-permute-start.12 = (bf16[512,128]{1,0:T(8,128)(2,1)S(1)}, bf16[512,128]{1,0:T(8,128)(2,1)S(1)}, u32[]{:S(2)}, u32[]{:S(2)}) collective-permute-start(bf16[512,128]{1,0:T(8,128)(2,1)S(1)} %get-tuple-element.51), channel_id=1, source_target_pairs={{0,12},{2,14},{4,8},{6,10},{8,4},{10,6},{12,0},{14,2},{1,13},{3,15... | collective-permute-start | bytes 393224 | tf_op jit(solution)/shard_map/ppermute | solution.py:273
  45.6 0.8 %collective-permute-start.13 = (bf16[512,128]{1,0:T(8,128)(2,1)S(1)}, bf16[512,128]{1,0:T(8,128)(2,1)S(1)}, u32[]{:S(2)}, u32[]{:S(2)}) collective-permute-start(bf16[512,128]{1,0:T(8,128)(2,1)S(1)} %get-tuple-element.52), channel_id=1, source_target_pairs={{0,6},{2,4},{4,2},{6,0},{8,14},{10,12},{12,10},{14,8},{1,7},{3,5},... | collective-permute-start | bytes 393224 | tf_op jit(solution)/shard_map/ppermute | solution.py:273
  46.3 1.7 %collective-permute-done.18.refs_8_ = bf16[256,128]{1,0:T(8,128)(2,1)S(1)} collective-permute-done((bf16[256,128]{1,0:T(8,128)(2,1)S(1)}, bf16[256,128]{1,0:T(8,128)(2,1)S(1)}, u32[]{:S(2)}, u32[]{:S(2)}) %collective-permute-start.18) | collective-permute-done | bytes 65568 | tf_op jit(solution)/shard_map/ppermute | solution.py:273
  48.1 2.8 %collective-permute-start.14 = (bf16[512,128]{1,0:T(8,128)(2,1)S(1)}, bf16[512,128]{1,0:T(8,128)(2,1)S(1)}, u32[]{:S(2)}, u32[]{:S(2)}) collective-permute-start(bf16[512,128]{1,0:T(8,128)(2,1)S(1)} %get-tuple-element.53), channel_id=1, source_target_pairs={{0,14},{2,12},{4,10},{6,8},{8,6},{10,4},{12,2},{14,0},{1,15},{3,13... | collective-permute-start | bytes 393224 | tf_op jit(solution)/shard_map/ppermute | solution.py:273
  50.9 0.3 collective-permute-done.19.refs_9_
  51.2 1.2 %collective-permute-start.15 = (bf16[512,128]{1,0:T(8,128)(2,1)S(1)}, bf16[512,128]{1,0:T(8,128)(2,1)S(1)}, u32[]{:S(2)}, u32[]{:S(2)}) collective-permute-start(bf16[512,128]{1,0:T(8,128)(2,1)S(1)} %get-tuple-element.54), channel_id=1, source_target_pairs={{0,2},{2,0},{4,6},{6,4},{8,10},{10,8},{12,14},{14,12},{1,3},{3,1},... | collective-permute-start | bytes 393224 | tf_op jit(solution)/shard_map/ppermute | solution.py:273
  52.4 2.0 %shard_map.74 = bf16[128,4096]{1,0:T(8,128)(2,1)} custom-call(s32[1]{0:T(128)} %bitcast.here, s32[8]{0:T(128)S(1)} %bitcast.9, f32[64,128]{1,0:T(8,128)S(1)} %get-tuple-element.58.mine.d_mine, f32[64,128]{1,0:T(8,128)S(1)} %collective-permute-done.7.other.d_other, bf16[256,128]{1,0:T(8,128)(2,1)S(1)} %collective-permute-done.8.refs_0_, ...), custom_call_target="tpu_custom_call" | custom-call | flops 134217728 | bytes 2097152 | tf_op jit(solution)/shard_map/pallas_call | solution.py:385
  54.4 4.6 %collective-permute-done.13.refs_2_ = bf16[512,128]{1,0:T(8,128)(2,1)S(1)} collective-permute-done((bf16[512,128]{1,0:T(8,128)(2,1)S(1)}, bf16[512,128]{1,0:T(8,128)(2,1)S(1)}, u32[]{:S(2)}, u32[]{:S(2)}) %collective-permute-start.13) | collective-permute-done | bytes 131104 | tf_op jit(solution)/shard_map/ppermute | solution.py:273
  59.0 1.8 %collective-permute-done.15.refs_4_ = bf16[512,128]{1,0:T(8,128)(2,1)S(1)} collective-permute-done((bf16[512,128]{1,0:T(8,128)(2,1)S(1)}, bf16[512,128]{1,0:T(8,128)(2,1)S(1)}, u32[]{:S(2)}, u32[]{:S(2)}) %collective-permute-start.15) | collective-permute-done | bytes 131104 | tf_op jit(solution)/shard_map/ppermute | solution.py:273
  60.8 1.7 %shard_map.75 = bf16[96,512,128]{2,1,0:T(8,128)(2,1)} custom-call(s32[8]{0:T(128)S(1)} %bitcast.13, s32[1]{0:T(128)} %bitcast.here, s32[8]{0:T(128)S(1)} %bitcast.10, bf16[512,128]{1,0:T(8,128)(2,1)S(1)} %collective-permute-done.11.refs_0_, bf16[512,128]{1,0:T(8,128)(2,1)S(1)} %collective-permute-done.12.refs_1_, ...), custom_call_target="tpu_custom_call", output_to_operand_aliasing={{}: (13, {})} | custom-call | bytes 2097152 | tf_op jit(solution)/shard_map/pallas_call | solution.py:398
  (24 shorter events, 0.3 us)
Async XLA Ops:
  0.6 16.4 %copy-start = (bf16[128,4096]{1,0:T(8,128)(2,1)S(1)}, bf16[128,4096]{1,0:T(8,128)(2,1)}, u32[]{:S(2)}) copy-start(bf16[128,4096]{1,0:T(8,128)(2,1)} %x.4) | copy-start | bytes 3145732
  0.6 16.4 %copy-start.1 = (bf16[128,4096]{1,0:T(8,128)(2,1)S(1)}, bf16[128,4096]{1,0:T(8,128)(2,1)}, u32[]{:S(2)}) copy-start(bf16[128,4096]{1,0:T(8,128)(2,1)} %y.3) | copy-start | bytes 3145732
  0.7 0.8 %copy-start.3 = (s32[8,1]{0,1:T(1,128)S(1)}, s32[8,1]{0,1:T(1,128)}, u32[]{:S(2)}) copy-start(s32[8,1]{0,1:T(1,128)} %param.8) | copy-start | bytes 100
  1.5 31.0 %copy-start.2 = (s32[8,1]{0,1:T(1,128)S(1)}, s32[8,1]{0,1:T(1,128)}, u32[]{:S(2)}) copy-start(s32[8,1]{0,1:T(1,128)} %param.9) | copy-start | bytes 100
  3.3 10.0 %collective-permute-start = (bf16[256,128]{1,0:T(8,128)(2,1)S(1)}, bf16[256,128]{1,0:T(8,128)(2,1)S(1)}, u32[]{:S(2)}, u32[]{:S(2)}) collective-permute-start(bf16[256,128]{1,0:T(8,128)(2,1)S(1)} %get-tuple-element.31), channel_id=1, source_target_pairs={{0,8},{2,10},{4,12},{6,14},{8,0},{10,2},{12,4},{14,6},{1,9},{3,11}... | collective-permute-start | bytes 196616 | tf_op jit(solution)/shard_map/ppermute | solution.py:273
  7.4 9.6 %collective-permute-start.3 = (bf16[256,128]{1,0:T(8,128)(2,1)S(1)}, bf16[256,128]{1,0:T(8,128)(2,1)S(1)}, u32[]{:S(2)}, u32[]{:S(2)}) collective-permute-start(bf16[256,128]{1,0:T(8,128)(2,1)S(1)} %get-tuple-element.36), channel_id=1, source_target_pairs={{0,10},{2,8},{4,14},{6,12},{8,2},{10,0},{12,6},{14,4},{1,11},{3,9}... | collective-permute-start | bytes 196616 | tf_op jit(solution)/shard_map/ppermute | solution.py:273
  8.7 13.7 %collective-permute-start.1 = (bf16[512,128]{1,0:T(8,128)(2,1)S(1)}, bf16[512,128]{1,0:T(8,128)(2,1)S(1)}, u32[]{:S(2)}, u32[]{:S(2)}) collective-permute-start(bf16[512,128]{1,0:T(8,128)(2,1)S(1)} %get-tuple-element.34), channel_id=1, source_target_pairs={{0,2},{2,0},{4,6},{6,4},{8,10},{10,8},{12,14},{14,12},{1,3},{3,1},... | collective-permute-start | bytes 393224 | tf_op jit(solution)/shard_map/ppermute | solution.py:273
  9.0 16.7 %collective-permute-start.2 = (bf16[512,128]{1,0:T(8,128)(2,1)S(1)}, bf16[512,128]{1,0:T(8,128)(2,1)S(1)}, u32[]{:S(2)}, u32[]{:S(2)}) collective-permute-start(bf16[512,128]{1,0:T(8,128)(2,1)S(1)} %get-tuple-element.35), channel_id=1, source_target_pairs={{0,4},{2,6},{4,0},{6,2},{8,12},{10,14},{12,8},{14,10},{1,5},{3,7},... | collective-permute-start | bytes 393224 | tf_op jit(solution)/shard_map/ppermute | solution.py:273
  10.8 15.5 %collective-permute-start.4 = (bf16[512,128]{1,0:T(8,128)(2,1)S(1)}, bf16[512,128]{1,0:T(8,128)(2,1)S(1)}, u32[]{:S(2)}, u32[]{:S(2)}) collective-permute-start(bf16[512,128]{1,0:T(8,128)(2,1)S(1)} %get-tuple-element.37), channel_id=1, source_target_pairs={{0,12},{2,14},{4,8},{6,10},{8,4},{10,6},{12,0},{14,2},{1,13},{3,15... | collective-permute-start | bytes 393224 | tf_op jit(solution)/shard_map/ppermute | solution.py:273
  13.3 13.1 %collective-permute-start.5 = (bf16[512,128]{1,0:T(8,128)(2,1)S(1)}, bf16[512,128]{1,0:T(8,128)(2,1)S(1)}, u32[]{:S(2)}, u32[]{:S(2)}) collective-permute-start(bf16[512,128]{1,0:T(8,128)(2,1)S(1)} %get-tuple-element.38), channel_id=1, source_target_pairs={{0,14},{2,12},{4,10},{6,8},{8,6},{10,4},{12,2},{14,0},{1,15},{3,13... | collective-permute-start | bytes 393224 | tf_op jit(solution)/shard_map/ppermute | solution.py:273
  17.0 9.4 %collective-permute-start.6 = (bf16[512,128]{1,0:T(8,128)(2,1)S(1)}, bf16[512,128]{1,0:T(8,128)(2,1)S(1)}, u32[]{:S(2)}, u32[]{:S(2)}) collective-permute-start(bf16[512,128]{1,0:T(8,128)(2,1)S(1)} %get-tuple-element.39), channel_id=1, source_target_pairs={{0,6},{2,4},{4,2},{6,0},{8,14},{10,12},{12,10},{14,8},{1,7},{3,5},... | collective-permute-start | bytes 393224 | tf_op jit(solution)/shard_map/ppermute | solution.py:273
  22.4 8.7 %collective-permute-start.8 = (bf16[256,128]{1,0:T(8,128)(2,1)S(1)}, bf16[256,128]{1,0:T(8,128)(2,1)S(1)}, u32[]{:S(2)}, u32[]{:S(2)}) collective-permute-start(bf16[256,128]{1,0:T(8,128)(2,1)S(1)} %get-tuple-element.43), channel_id=1, source_target_pairs={{0,8},{2,10},{4,12},{6,14},{8,0},{10,2},{12,4},{14,6},{1,9},{3,11}... | collective-permute-start | bytes 196616 | tf_op jit(solution)/shard_map/ppermute | solution.py:273
  25.7 6.8 %collective-permute-start.9 = (bf16[256,128]{1,0:T(8,128)(2,1)S(1)}, bf16[256,128]{1,0:T(8,128)(2,1)S(1)}, u32[]{:S(2)}, u32[]{:S(2)}) collective-permute-start(bf16[256,128]{1,0:T(8,128)(2,1)S(1)} %get-tuple-element.45), channel_id=1, source_target_pairs={{0,10},{2,8},{4,14},{6,12},{8,2},{10,0},{12,6},{14,4},{1,11},{3,9}... | collective-permute-start | bytes 196616 | tf_op jit(solution)/shard_map/ppermute | solution.py:273
  27.1 5.5 %collective-permute-start.7 = (f32[64,128]{1,0:T(8,128)S(1)}, f32[64,128]{1,0:T(8,128)S(1)}, u32[]{:S(2)}, u32[]{:S(2)}) collective-permute-start(f32[64,128]{1,0:T(8,128)S(1)} %get-tuple-element.58.mine.d_mine), channel_id=1, source_target_pairs={{0,1},{1,0},{2,3},{3,2},{4,5},{5,4},{6,7},{7,6},{8,9},{9,8},{10,11... | collective-permute-start | bytes 98312 | tf_op jit(solution)/shard_map/ppermute | solution.py:290
  33.7 3.4 %collective-permute-start.10 = (f32[64,128]{1,0:T(8,128)S(1)}, f32[64,128]{1,0:T(8,128)S(1)}, u32[]{:S(2)}, u32[]{:S(2)}) collective-permute-start(f32[64,128]{1,0:T(8,128)S(1)} %shard_map.72.mine), channel_id=1, source_target_pairs={{0,1},{1,0},{2,3},{3,2},{4,5},{5,4},{6,7},{7,6},{8,9},{9,8},{10,11... | collective-permute-start | bytes 98312 | tf_op jit(solution)/shard_map/ppermute | solution.py:290
  33.8 10.1 %collective-permute-start.16 = (bf16[256,128]{1,0:T(8,128)(2,1)S(1)}, bf16[256,128]{1,0:T(8,128)(2,1)S(1)}, u32[]{:S(2)}, u32[]{:S(2)}) collective-permute-start(bf16[256,128]{1,0:T(8,128)(2,1)S(1)} %get-tuple-element.47), channel_id=1, source_target_pairs={{0,8},{2,10},{4,12},{6,14},{8,0},{10,2},{12,4},{14,6},{1,9},{3,11}... | collective-permute-start | bytes 196616 | tf_op jit(solution)/shard_map/ppermute | solution.py:273
  33.9 11.7 %collective-permute-start.17 = (bf16[256,128]{1,0:T(8,128)(2,1)S(1)}, bf16[256,128]{1,0:T(8,128)(2,1)S(1)}, u32[]{:S(2)}, u32[]{:S(2)}) collective-permute-start(bf16[256,128]{1,0:T(8,128)(2,1)S(1)} %get-tuple-element.48), channel_id=1, source_target_pairs={{0,10},{2,8},{4,14},{6,12},{8,2},{10,0},{12,6},{14,4},{1,11},{3,9}... | collective-permute-start | bytes 196616 | tf_op jit(solution)/shard_map/ppermute | solution.py:273
  38.4 9.7 %collective-permute-start.18 = (bf16[256,128]{1,0:T(8,128)(2,1)S(1)}, bf16[256,128]{1,0:T(8,128)(2,1)S(1)}, u32[]{:S(2)}, u32[]{:S(2)}) collective-permute-start(bf16[256,128]{1,0:T(8,128)(2,1)S(1)} %get-tuple-element.56), channel_id=1, source_target_pairs={{0,8},{2,10},{4,12},{6,14},{8,0},{10,2},{12,4},{14,6},{1,9},{3,11}... | collective-permute-start | bytes 196616 | tf_op jit(solution)/shard_map/ppermute | solution.py:273
  38.5 12.7 %collective-permute-start.19 = (bf16[256,128]{1,0:T(8,128)(2,1)S(1)}, bf16[256,128]{1,0:T(8,128)(2,1)S(1)}, u32[]{:S(2)}, u32[]{:S(2)}) collective-permute-start(bf16[256,128]{1,0:T(8,128)(2,1)S(1)} %get-tuple-element.57), channel_id=1, source_target_pairs={{0,10},{2,8},{4,14},{6,12},{8,2},{10,0},{12,6},{14,4},{1,11},{3,9}... | collective-permute-start | bytes 196616 | tf_op jit(solution)/shard_map/ppermute | solution.py:273
  41.9 12.5 %collective-permute-start.11 = (bf16[512,128]{1,0:T(8,128)(2,1)S(1)}, bf16[512,128]{1,0:T(8,128)(2,1)S(1)}, u32[]{:S(2)}, u32[]{:S(2)}) collective-permute-start(bf16[512,128]{1,0:T(8,128)(2,1)S(1)} %get-tuple-element.50), channel_id=1, source_target_pairs={{0,4},{2,6},{4,0},{6,2},{8,12},{10,14},{12,8},{14,10},{1,5},{3,7},... | collective-permute-start | bytes 393224 | tf_op jit(solution)/shard_map/ppermute | solution.py:273
  43.8 10.5 %collective-permute-start.12 = (bf16[512,128]{1,0:T(8,128)(2,1)S(1)}, bf16[512,128]{1,0:T(8,128)(2,1)S(1)}, u32[]{:S(2)}, u32[]{:S(2)}) collective-permute-start(bf16[512,128]{1,0:T(8,128)(2,1)S(1)} %get-tuple-element.51), channel_id=1, source_target_pairs={{0,12},{2,14},{4,8},{6,10},{8,4},{10,6},{12,0},{14,2},{1,13},{3,15... | collective-permute-start | bytes 393224 | tf_op jit(solution)/shard_map/ppermute | solution.py:273
  45.6 13.5 %collective-permute-start.13 = (bf16[512,128]{1,0:T(8,128)(2,1)S(1)}, bf16[512,128]{1,0:T(8,128)(2,1)S(1)}, u32[]{:S(2)}, u32[]{:S(2)}) collective-permute-start(bf16[512,128]{1,0:T(8,128)(2,1)S(1)} %get-tuple-element.52), channel_id=1, source_target_pairs={{0,6},{2,4},{4,2},{6,0},{8,14},{10,12},{12,10},{14,8},{1,7},{3,5},... | collective-permute-start | bytes 393224 | tf_op jit(solution)/shard_map/ppermute | solution.py:273
  48.1 11.0 %collective-permute-start.14 = (bf16[512,128]{1,0:T(8,128)(2,1)S(1)}, bf16[512,128]{1,0:T(8,128)(2,1)S(1)}, u32[]{:S(2)}, u32[]{:S(2)}) collective-permute-start(bf16[512,128]{1,0:T(8,128)(2,1)S(1)} %get-tuple-element.53), channel_id=1, source_target_pairs={{0,14},{2,12},{4,10},{6,8},{8,6},{10,4},{12,2},{14,0},{1,15},{3,13... | collective-permute-start | bytes 393224 | tf_op jit(solution)/shard_map/ppermute | solution.py:273
  51.2 9.7 %collective-permute-start.15 = (bf16[512,128]{1,0:T(8,128)(2,1)S(1)}, bf16[512,128]{1,0:T(8,128)(2,1)S(1)}, u32[]{:S(2)}, u32[]{:S(2)}) collective-permute-start(bf16[512,128]{1,0:T(8,128)(2,1)S(1)} %get-tuple-element.54), channel_id=1, source_target_pairs={{0,2},{2,0},{4,6},{6,4},{8,10},{10,8},{12,14},{14,12},{1,3},{3,1},... | collective-permute-start | bytes 393224 | tf_op jit(solution)/shard_map/ppermute | solution.py:273

commit v12 on v11

--- a/solution.py
+++ b/solution.py
@@ -9,11 +9,11 @@
 
 adapter_alpha = 128.0
 RANK_ORDER = ((False, 1), (False, 2), (True, 4), (True, 5), (False, 6), (False, 7), (False, 3))
-MERGE_ORDER = (("both", 2), ("both", 6), ("both", 3), ("both", 7), ("both", 1))
+LATE = (3, 7, 1)
 PREP_AFTER = 0
 PREP_VMEM = 40
 SPLIT = (4, 5)
-WHOLE = (2, 6, 3, 7, 1)
+WHOLE = (6, 2, 3, 7, 1)
 
 in_vmem = pl.BlockSpec(memory_space=pltpu.VMEM)
 in_smem = pl.BlockSpec(memory_space=pltpu.SMEM)
@@ -208,64 +208,66 @@
         out[:, pl.ds(pl.multiple_of(start + half, half), half)] = product(right, down[n][...])
 
 
-def merge_kernel(plan, order, ids, here, lengths, *refs):
-    split, whole = plan
+def merge_kernel(order, handled, others, ids, here, lengths, *refs):
     by_key = dict(zip(order, refs[:-5]))
-    down, up = [by_key["down", k] for k in split], [by_key["up", k] for k in split]
-    straight = [by_key["both", k] for k in whole]
     out, total, held, sems = refs[-4:]
     me = here[0]
     rows, width = total.shape
     half = rows // 2
     low = low_lanes(half, width)
-
-    def unpacked(n):
-        d_down, d_up = down[n][...].astype(jnp.float32), up[n][...].astype(jnp.float32)
+    others_here = ("both", others[0]) in by_key or ("up", others[0]) in by_key
+
+    def value(k):
+        if ("both", k) in by_key:
+            return by_key["both", k][...].astype(jnp.float32)
+        d_down = by_key["down", k][...].astype(jnp.float32)
+        d_up = by_key["up", k][...].astype(jnp.float32)
         first = jnp.where(low, d_down, swap_halves(d_up))
         second = jnp.where(low, swap_halves(d_down), d_up)
         return jnp.concatenate([first, second], axis=0)
 
-    def read(ref):
-        return lambda: ref[...].astype(jnp.float32)
-
-    pieces = [(me ^ k, read(straight[n])) for n, k in enumerate(whole)]
-    pieces += [(me ^ k, functools.partial(unpacked, n)) for n, k in enumerate(split)]
-    owners = len(pieces)
-    adapters = [ids[block] for block, _ in pieces]
-    counts = [lengths[block] for block, _ in pieces]
-    copies, firsts = [], []
-    for k, (_, value) in enumerate(pieces):
-        copies.append(pltpu.make_async_copy(held.at[k], out.at[adapters[k]], sems.at[k]))
-        same = [adapters[other] == adapters[k] for other in range(owners)]
-        earlier = functools.reduce(jnp.logical_or, same[:k], jnp.bool_(False))
-        later = functools.reduce(jnp.logical_or, same[k + 1 :], jnp.bool_(False))
-        firsts.append(jnp.logical_not(earlier))
+    def either(conditions):
+        return functools.reduce(jnp.logical_or, conditions, jnp.bool_(False))
+
+    copies, chosen = [], []
+    for n, k in enumerate(handled):
+        adapter = ids[me ^ k]
+        copies.append(pltpu.make_async_copy(held.at[n], out.at[adapter], sems.at[n]))
+        same = {other: ids[me ^ other] == adapter for other in (*handled, *others) if other != k}
+        skip = either([same[other] for other in handled[:n]])
+        adding = list(handled[n + 1 :])
+        if others_here:
+            adding += others
+        else:
+            skip |= either([same[other] for other in others])
+        more = either([same[other] for other in adding])
+        chosen.append(jnp.logical_not(skip))
 
         def store(sum_of, count):
             denom = jnp.maximum(count.astype(jnp.float32), 1.0)
             part = 1.0 / jnp.full((1, width), denom)
-            held[k] = (sum_of * part).astype(jnp.bfloat16)
-            copies[k].start()
-
-        @pl.when(firsts[k] & jnp.logical_not(later))
+            held[n] = (sum_of * part).astype(jnp.bfloat16)
+            copies[n].start()
+
+        @pl.when(chosen[n] & jnp.logical_not(more))
         def _():
-            store(value(), counts[k])
-
-        @pl.when(firsts[k] & later)
+            store(value(k), lengths[me ^ k])
+
+        @pl.when(chosen[n] & more)
         def _():
-            total[...] = value()
-            count = counts[k]
-            for other in range(k + 1, owners):
-                count += jnp.where(same[other], counts[other], 0)
+            total[...] = value(k)
+            count = lengths[me ^ k]
+            for other in adding:
+                count += jnp.where(same[other], lengths[me ^ other], 0)
 
                 @pl.when(same[other])
                 def _():
-                    total[...] += pieces[other][1]()
+                    total[...] += value(other)
 
             store(total[...], count)
 
-    for k in range(owners):
-        pl.when(firsts[k])(copies[k].wait)
+    for n in range(len(handled)):
+        pl.when(chosen[n])(copies[n].wait)
 
 
 def to_partner(pieces, partners, owners):
@@ -380,7 +382,8 @@
         moved=1024,
     )(here, lengths, dhidden, dhidden_other, hidden, hidden_other, turned)
     d_pairs = to_partner(pieces[:wholes], whole, owners)
-    d_ups = to_partner(pieces[wholes:], split, owners)
+    d_ups = [after(piece, down) for piece, down in zip(pieces[wholes:], d_downs)]
+    d_ups = to_partner(d_ups, split, owners)
 
     grad_input = call(
         functools.partial(input_kernel, plan, scale),
@@ -391,23 +394,29 @@
         moved=token_bytes + pair_bytes,
     )(here, lengths, after(dhidden, *pieces), dhidden_other, *downs, *pairs)
 
-    from_all = {("both", k): piece for k, piece in zip(whole, d_pairs)}
-    from_all |= {("down", k): piece for k, piece in zip(split, d_downs)}
-    from_all |= {("up", k): piece for k, piece in zip(split, d_ups)}
-    merge_order = in_order(from_all, MERGE_ORDER)
-    gradient = call(
-        functools.partial(merge_kernel, plan, tuple(key for key, _ in merge_order)),
-        jax.ShapeDtypeStruct(table.shape, bf16),
-        [in_smem] * 3 + [in_vmem] * (2 * parts + wholes) + [in_hbm],
-        in_hbm,
-        [
-            pltpu.VMEM((rows, width), f32),
-            pltpu.VMEM((owners, rows, width), bf16),
-            pltpu.SemaphoreType.DMA((owners,)),
-        ],
-        moved=2 * pair_bytes,
-        aliases={3 + 2 * parts + wholes: 0},
-    )(ids, here, lengths, *[piece for _, piece in merge_order], blank)
+    arrived = {("both", k): piece for k, piece in zip(whole, d_pairs)}
+    arrived |= {("down", k): piece for k, piece in zip(split, d_downs)}
+    arrived |= {("up", k): piece for k, piece in zip(split, d_ups)}
+    late = tuple(k for k in whole if k in LATE)
+    early = tuple(k for k in (*split, *whole) if k not in LATE)
+
+    def merge(handled, others, pieces, so_far):
+        return call(
+            functools.partial(merge_kernel, tuple(pieces), handled, others),
+            jax.ShapeDtypeStruct(table.shape, bf16),
+            [in_smem] * 3 + [in_vmem] * len(pieces) + [in_hbm],
+            in_hbm,
+            [
+                pltpu.VMEM((rows, width), f32),
+                pltpu.VMEM((len(handled), rows, width), bf16),
+                pltpu.SemaphoreType.DMA((len(handled),)),
+            ],
+            moved=2 * pair_bytes,
+            aliases={3 + len(pieces): 0},
+        )(ids, here, lengths, *pieces.values(), so_far)
+
+    early_pieces = {key: piece for key, piece in arrived.items() if key[1] in early}
+    gradient = merge(late, early, arrived, merge(early, late, early_pieces, blank))
     return grad_input, gradient[:, None]
 
 

time: 62.8 us -> 63.2 us (level)
  starting transfers between devices: 31.9 us -> 30 us
  Pallas kernels: 14.1 us -> 15.3 us
  waiting for transfers between devices: 15 us -> 16.2 us
    ppermute x18, starting transfers between devices: 31.8 us -> 29.9 us  [to_partner(): lax.ppermute(piece, 'dp', [(i, i ^ k) for i in range(owners)])]
    pallas_call x1 -> x2, Pallas kernels: 1.75 us -> 3.02 us  [merge(): call(functools.partial(merge_kernel, tuple(pieces), handled, others), jax...]
    ppermute x2, waiting for transfers between devices: 0.01 us -> 1.2 us  [across_cores(): return lax.ppermute(value, 'tensor', [(i, i ^ 1) for i in range(cores)])]
  transfers between devices with their start and end apart: 20 -> 20, of which waited for: 7 -> 9; matrix products, arithmetic and copies ran while one was open for 0% -> 0% of each run, Pallas kernels for 15% -> 18%
where the time goes in v12:
time: 63.2 us; the launch traced here: 63.1 us
  starting transfers between devices  30 us (47%)
  waiting for transfers between devices  16.2 us (26%)
  Pallas kernels  15.3 us (24%)
  local copies, waits for them, and re-layouts  0.81 us (1%)
  between operations  0.77 us (1%)
    ppermute x18, starting transfers between devices, to_partner(): lax.ppermute(piece, 'dp', [(i, i ^ k) for i in range(owners)])  29.9 us
    ppermute x18, waiting for transfers between devices, to_partner(): lax.ppermute(piece, 'dp', [(i, i ^ k) for i in range(owners)])  15 us
    pallas_call x1, Pallas kernels, with_kernels(): call(prep_kernel, [jax.ShapeDtypeStruct((owners, rows, 2 * tokens), bf16)...  5.35 us
    pallas_call x2, Pallas kernels, merge(): call(functools.partial(merge_kernel, tuple(pieces), handled, others), jax...  3.02 us
    pallas_call x1, Pallas kernels, with_kernels(): call(functools.partial(input_kernel, plan, scale), jax.ShapeDtypeStruct((...  1.98 us
    pallas_call x1, Pallas kernels, with_kernels(): call(functools.partial(gather_kernel, plan), [packed] * parts + [straight...  1.85 us
  transfers between devices with their start and end apart: 20, of which 9 were waited for; matrix products, arithmetic and copies ran while one was open for 0% of the time, Pallas kernels for 18%

profile of v12, /device:TPU:0, one launch (start us, length us, event | category | flops | bytes accessed | tf_op | source)
XLA Modules:
  0.0 63.1 jit_solution(15518032732793077502)
XLA Ops:
  0.7 0.8 %copy-done.3 = s32[8,1]{0,1:T(1,128)S(1)} copy-done((s32[8,1]{0,1:T(1,128)S(1)}, s32[8,1]{0,1:T(1,128)}, u32[]{:S(2)}) %copy-start.3) | copy-done | bytes 56
  1.5 1.9 %shard_map.68 = (bf16[256,128]{1,0:T(8,128)(2,1)S(1)}, bf16[256,128]{1,0:T(8,128)(2,1)S(1)}, bf16[512,128]{1,0:T(8,128)(2,1)S(1)}, bf16[512,128]{1,0:T(8,128)(2,...) custom-call(s32[8]{0:T(128)S(1)} %bitcast.12, ...), custom_call_target="tpu_custom_call" | custom-call | bytes 2097152 | tf_op jit(solution)/shard_map/pallas_call | solution.py:312
  3.3 4.1 %collective-permute-start = (bf16[256,128]{1,0:T(8,128)(2,1)S(1)}, bf16[256,128]{1,0:T(8,128)(2,1)S(1)}, u32[]{:S(2)}, u32[]{:S(2)}) collective-permute-start(bf16[256,128]{1,0:T(8,128)(2,1)S(1)} %get-tuple-element.33), channel_id=1, source_target_pairs={{0,8},{2,10},{4,12},{6,14},{8,0},{10,2},{12,4},{14,6},{1,9},{3,11}... | collective-permute-start | bytes 196616 | tf_op jit(solution)/shard_map/ppermute | solution.py:275
  7.4 1.3 %collective-permute-start.3 = (bf16[256,128]{1,0:T(8,128)(2,1)S(1)}, bf16[256,128]{1,0:T(8,128)(2,1)S(1)}, u32[]{:S(2)}, u32[]{:S(2)}) collective-permute-start(bf16[256,128]{1,0:T(8,128)(2,1)S(1)} %get-tuple-element.38), channel_id=1, source_target_pairs={{0,10},{2,8},{4,14},{6,12},{8,2},{10,0},{12,6},{14,4},{1,11},{3,9}... | collective-permute-start | bytes 196616 | tf_op jit(solution)/shard_map/ppermute | solution.py:275
  9.0 1.8 %collective-permute-start.2 = (bf16[512,128]{1,0:T(8,128)(2,1)S(1)}, bf16[512,128]{1,0:T(8,128)(2,1)S(1)}, u32[]{:S(2)}, u32[]{:S(2)}) collective-permute-start(bf16[512,128]{1,0:T(8,128)(2,1)S(1)} %get-tuple-element.37), channel_id=1, source_target_pairs={{0,4},{2,6},{4,0},{6,2},{8,12},{10,14},{12,8},{14,10},{1,5},{3,7},... | collective-permute-start | bytes 393224 | tf_op jit(solution)/shard_map/ppermute | solution.py:275
  10.8 2.5 %collective-permute-start.4 = (bf16[512,128]{1,0:T(8,128)(2,1)S(1)}, bf16[512,128]{1,0:T(8,128)(2,1)S(1)}, u32[]{:S(2)}, u32[]{:S(2)}) collective-permute-start(bf16[512,128]{1,0:T(8,128)(2,1)S(1)} %get-tuple-element.39), channel_id=1, source_target_pairs={{0,12},{2,14},{4,8},{6,10},{8,4},{10,6},{12,0},{14,2},{1,13},{3,15... | collective-permute-start | bytes 393224 | tf_op jit(solution)/shard_map/ppermute | solution.py:275
  13.3 3.7 %collective-permute-start.5 = (bf16[512,128]{1,0:T(8,128)(2,1)S(1)}, bf16[512,128]{1,0:T(8,128)(2,1)S(1)}, u32[]{:S(2)}, u32[]{:S(2)}) collective-permute-start(bf16[512,128]{1,0:T(8,128)(2,1)S(1)} %get-tuple-element.40), channel_id=1, source_target_pairs={{0,14},{2,12},{4,10},{6,8},{8,6},{10,4},{12,2},{14,0},{1,15},{3,13... | collective-permute-start | bytes 393224 | tf_op jit(solution)/shard_map/ppermute | solution.py:275
  17.0 5.3 %shard_map.69 = (bf16[8,512,256]{2,1,0:T(8,128)(2,1)S(1)}, bf16[512,128]{1,0:T(8,128)(2,1)S(1)}, bf16[96,512,128]{2,1,0:T(8,128)(2,1)}) custom-call(s32[8]{0:T(128)S(1)} %bitcast.13, s32[1]{0:T(128)} %bitcast.here, bf16[96,512,128]{2,1,0:T(8,128)(2,1)} %bitcast.18, bf16[256,128]{1,0:T(8,128)(2,1)S(1)} %collective-permute-done.after.refs_2_, ...), custom_call_target="tpu_custom_call" | custom-call | bytes 16777216 | tf_op jit(solution)/shard_map/pallas_call | solution.py:324
  22.4 3.3 %collective-permute-start.8 = (bf16[256,128]{1,0:T(8,128)(2,1)S(1)}, bf16[256,128]{1,0:T(8,128)(2,1)S(1)}, u32[]{:S(2)}, u32[]{:S(2)}) collective-permute-start(bf16[256,128]{1,0:T(8,128)(2,1)S(1)} %get-tuple-element.45), channel_id=1, source_target_pairs={{0,8},{2,10},{4,12},{6,14},{8,0},{10,2},{12,4},{14,6},{1,9},{3,11}... | collective-permute-start | bytes 196616 | tf_op jit(solution)/shard_map/ppermute | solution.py:275
  25.7 0.6 collective-permute-start.9
  26.3 0.7 %shard_map.70 = (f32[64,128]{1,0:T(8,128)S(1)}, f32[64,128]{1,0:T(8,128)S(1)}) custom-call(s32[1]{0:T(128)} %bitcast.here, bf16[128,4096]{1,0:T(8,128)(2,1)S(1)} %copy-done, bf16[128,4096]{1,0:T(8,128)(2,1)S(1)} %copy-done.1, bf16[512,128]{1,0:T(8,128)(2,1)S(1)} %collective-permute-done.1.refs_0_.refs_6_, ...), custom_call_target="tpu_custom_call" | custom-call | bytes 1024 | tf_op jit(solution)/shard_map/pallas_call | solution.py:352
  27.1 4.0 %collective-permute-done.8.refs_0_ = bf16[256,128]{1,0:T(8,128)(2,1)S(1)} collective-permute-done((bf16[256,128]{1,0:T(8,128)(2,1)S(1)}, bf16[256,128]{1,0:T(8,128)(2,1)S(1)}, u32[]{:S(2)}, u32[]{:S(2)}) %collective-permute-start.8) | collective-permute-done | bytes 65568 | tf_op jit(solution)/shard_map/ppermute | solution.py:275
  31.1 1.4 %collective-permute-done.9.refs_1_ = bf16[256,128]{1,0:T(8,128)(2,1)S(1)} collective-permute-done((bf16[256,128]{1,0:T(8,128)(2,1)S(1)}, bf16[256,128]{1,0:T(8,128)(2,1)S(1)}, u32[]{:S(2)}, u32[]{:S(2)}) %collective-permute-start.9) | collective-permute-done | bytes 65568 | tf_op jit(solution)/shard_map/ppermute | solution.py:275
  32.5 0.8 %shard_map.71 = (bf16[256,128]{1,0:T(8,128)(2,1)S(1)}, bf16[256,128]{1,0:T(8,128)(2,1)S(1)}) custom-call(s32[1]{0:T(128)} %bitcast.here, s32[8]{0:T(128)S(1)} %bitcast.7, f32[64,128]{1,0:T(8,128)S(1)} %get-tuple-element.60.mine.d_mine, f32[64,128]{1,0:T(8,128)S(1)} %collective-permute-done.7.other.d_other, bf16[8,512,256]{2,1,0:T(8,128)(2,1)S(1)} %get-tuple-element.34.turned), custom_call_target="tpu_custom_call" | custom-call | bytes 1024 | tf_op jit(solution)/shard_map/pallas_call | solution.py:360
  33.4 3.3 %collective-permute-start.17 = (bf16[256,128]{1,0:T(8,128)(2,1)S(1)}, bf16[256,128]{1,0:T(8,128)(2,1)S(1)}, u32[]{:S(2)}, u32[]{:S(2)}) collective-permute-start(bf16[256,128]{1,0:T(8,128)(2,1)S(1)} %get-tuple-element.50), channel_id=1, source_target_pairs={{0,10},{2,8},{4,14},{6,12},{8,2},{10,0},{12,6},{14,4},{1,11},{3,9}... | collective-permute-start | bytes 196616 | tf_op jit(solution)/shard_map/ppermute | solution.py:275
  36.7 0.4 shard_map.72.mine
  37.1 1.2 %collective-permute-done.10.other = f32[64,128]{1,0:T(8,128)S(1)} collective-permute-done((f32[64,128]{1,0:T(8,128)S(1)}, f32[64,128]{1,0:T(8,128)S(1)}, u32[]{:S(2)}, u32[]{:S(2)}) %collective-permute-start.10) | collective-permute-done | bytes 32800 | tf_op jit(solution)/shard_map/ppermute | solution.py:292
  38.3 1.2 %shard_map.73 = (bf16[512,128]{1,0:T(8,128)(2,1)S(1)}, bf16[512,128]{1,0:T(8,128)(2,1)S(1)}, bf16[512,128]{1,0:T(8,128)(2,1)S(1)}, bf16[512,128]{1,0:T(8,128)(2,...) custom-call(s32[1]{0:T(128)} %bitcast.here, ...), custom_call_target="tpu_custom_call" | custom-call | bytes 1024 | tf_op jit(solution)/shard_map/pallas_call | solution.py:377
  39.6 1.2 %collective-permute-done.16.refs_3_.refs_6_ = bf16[256,128]{1,0:T(8,128)(2,1)S(1)} collective-permute-done((bf16[256,128]{1,0:T(8,128)(2,1)S(1)}, bf16[256,128]{1,0:T(8,128)(2,1)S(1)}, u32[]{:S(2)}, u32[]{:S(2)}) %collective-permute-start.16) | collective-permute-done | bytes 65568 | tf_op jit(solution)/shard_map/ppermute | solution.py:275
  40.7 1.0 %collective-permute-done.17.refs_4_.refs_7_ = bf16[256,128]{1,0:T(8,128)(2,1)S(1)} collective-permute-done((bf16[256,128]{1,0:T(8,128)(2,1)S(1)}, bf16[256,128]{1,0:T(8,128)(2,1)S(1)}, u32[]{:S(2)}, u32[]{:S(2)}) %collective-permute-start.17) | collective-permute-done | bytes 65568 | tf_op jit(solution)/shard_map/ppermute | solution.py:275
  41.7 1.5 %collective-permute-start.19 = (bf16[256,128]{1,0:T(8,128)(2,1)S(1)}, bf16[256,128]{1,0:T(8,128)(2,1)S(1)}, u32[]{:S(2)}, u32[]{:S(2)}) collective-permute-start(bf16[256,128]{1,0:T(8,128)(2,1)S(1)} %get-tuple-element.62), channel_id=1, source_target_pairs={{0,10},{2,8},{4,14},{6,12},{8,2},{10,0},{12,6},{14,4},{1,11},{3,9}... | collective-permute-start | bytes 196616 | tf_op jit(solution)/shard_map/ppermute | solution.py:275
  43.3 3.4 %collective-permute-start.11 = (bf16[512,128]{1,0:T(8,128)(2,1)S(1)}, bf16[512,128]{1,0:T(8,128)(2,1)S(1)}, u32[]{:S(2)}, u32[]{:S(2)}) collective-permute-start(bf16[512,128]{1,0:T(8,128)(2,1)S(1)} %get-tuple-element.52), channel_id=1, source_target_pairs={{0,12},{2,14},{4,8},{6,10},{8,4},{10,6},{12,0},{14,2},{1,13},{3,15... | collective-permute-start | bytes 393224 | tf_op jit(solution)/shard_map/ppermute | solution.py:275
  46.7 2.4 %collective-permute-start.13 = (bf16[512,128]{1,0:T(8,128)(2,1)S(1)}, bf16[512,128]{1,0:T(8,128)(2,1)S(1)}, u32[]{:S(2)}, u32[]{:S(2)}) collective-permute-start(bf16[512,128]{1,0:T(8,128)(2,1)S(1)} %get-tuple-element.54), channel_id=1, source_target_pairs={{0,6},{2,4},{4,2},{6,0},{8,14},{10,12},{12,10},{14,8},{1,7},{3,5},... | collective-permute-start | bytes 393224 | tf_op jit(solution)/shard_map/ppermute | solution.py:275
  49.1 0.4 collective-permute-done.18.refs_5_.refs_8_
  49.5 0.5 collective-permute-start.14
  50.0 2.7 %collective-permute-done.19.refs_6_.refs_9_ = bf16[256,128]{1,0:T(8,128)(2,1)S(1)} collective-permute-done((bf16[256,128]{1,0:T(8,128)(2,1)S(1)}, bf16[256,128]{1,0:T(8,128)(2,1)S(1)}, u32[]{:S(2)}, u32[]{:S(2)}) %collective-permute-start.19) | collective-permute-done | bytes 65568 | tf_op jit(solution)/shard_map/ppermute | solution.py:275
  52.7 1.1 %collective-permute-start.15 = (bf16[512,128]{1,0:T(8,128)(2,1)S(1)}, bf16[512,128]{1,0:T(8,128)(2,1)S(1)}, u32[]{:S(2)}, u32[]{:S(2)}) collective-permute-start(bf16[512,128]{1,0:T(8,128)(2,1)S(1)} %get-tuple-element.56), channel_id=1, source_target_pairs={{0,2},{2,0},{4,6},{6,4},{8,10},{10,8},{12,14},{14,12},{1,3},{3,1},... | collective-permute-start | bytes 393224 | tf_op jit(solution)/shard_map/ppermute | solution.py:275
  53.8 2.0 %shard_map.74 = bf16[128,4096]{1,0:T(8,128)(2,1)} custom-call(s32[1]{0:T(128)} %bitcast.here, s32[8]{0:T(128)S(1)} %bitcast.9, f32[64,128]{1,0:T(8,128)S(1)} %get-tuple-element.60.mine.d_mine, f32[64,128]{1,0:T(8,128)S(1)} %collective-permute-done.7.other.d_other, bf16[256,128]{1,0:T(8,128)(2,1)S(1)} %collective-permute-done.8.refs_0_, ...), custom_call_target="tpu_custom_call" | custom-call | flops 134217728 | bytes 2097152 | tf_op jit(solution)/shard_map/pallas_call | solution.py:388
  55.8 1.6 %shard_map.75.refs_10_ = bf16[96,512,128]{2,1,0:T(8,128)(2,1)} custom-call(s32[8]{0:T(128)S(1)} %bitcast.14, s32[1]{0:T(128)} %bitcast.here, s32[8]{0:T(128)S(1)} %bitcast.10, bf16[512,128]{1,0:T(8,128)(2,1)S(1)} %collective-permute-done.11.refs_0_, bf16[512,128]{1,0:T(8,128)(2,1)S(1)} %collective-permute-done.12.refs_1_, ...), custom_call_target="tpu_custom_call", output_to_operand_aliasing={{}: (10, {})} | custom-call | bytes 2097152 | tf_op jit(solution)/shard_map/pallas_call | solution.py:404
  57.4 2.7 %collective-permute-done.13.refs_2_ = bf16[512,128]{1,0:T(8,128)(2,1)S(1)} collective-permute-done((bf16[512,128]{1,0:T(8,128)(2,1)S(1)}, bf16[512,128]{1,0:T(8,128)(2,1)S(1)}, u32[]{:S(2)}, u32[]{:S(2)}) %collective-permute-start.13) | collective-permute-done | bytes 131104 | tf_op jit(solution)/shard_map/ppermute | solution.py:275
  60.0 1.6 %collective-permute-done.15.refs_4_ = bf16[512,128]{1,0:T(8,128)(2,1)S(1)} collective-permute-done((bf16[512,128]{1,0:T(8,128)(2,1)S(1)}, bf16[512,128]{1,0:T(8,128)(2,1)S(1)}, u32[]{:S(2)}, u32[]{:S(2)}) %collective-permute-start.15) | collective-permute-done | bytes 131104 | tf_op jit(solution)/shard_map/ppermute | solution.py:275
  61.7 1.4 %shard_map.76 = bf16[96,512,128]{2,1,0:T(8,128)(2,1)} custom-call(s32[8]{0:T(128)S(1)} %bitcast.15, s32[1]{0:T(128)} %bitcast.here, s32[8]{0:T(128)S(1)} %bitcast.11, bf16[512,128]{1,0:T(8,128)(2,1)S(1)} %collective-permute-done.11.refs_0_, bf16[512,128]{1,0:T(8,128)(2,1)S(1)} %collective-permute-done.12.refs_1_, ...), custom_call_target="tpu_custom_call", output_to_operand_aliasing={{}: (13, {})} | custom-call | bytes 2097152 | tf_op jit(solution)/shard_map/pallas_call | solution.py:404
  (25 shorter events, 0.5 us)
Async XLA Ops:
  0.6 16.4 %copy-start = (bf16[128,4096]{1,0:T(8,128)(2,1)S(1)}, bf16[128,4096]{1,0:T(8,128)(2,1)}, u32[]{:S(2)}) copy-start(bf16[128,4096]{1,0:T(8,128)(2,1)} %x.4) | copy-start | bytes 3145732
  0.6 16.4 %copy-start.1 = (bf16[128,4096]{1,0:T(8,128)(2,1)S(1)}, bf16[128,4096]{1,0:T(8,128)(2,1)}, u32[]{:S(2)}) copy-start(bf16[128,4096]{1,0:T(8,128)(2,1)} %y.3) | copy-start | bytes 3145732
  0.7 0.8 %copy-start.3 = (s32[8,1]{0,1:T(1,128)S(1)}, s32[8,1]{0,1:T(1,128)}, u32[]{:S(2)}) copy-start(s32[8,1]{0,1:T(1,128)} %param.8) | copy-start | bytes 100
  1.5 31.0 %copy-start.2 = (s32[8,1]{0,1:T(1,128)S(1)}, s32[8,1]{0,1:T(1,128)}, u32[]{:S(2)}) copy-start(s32[8,1]{0,1:T(1,128)} %param.9) | copy-start | bytes 100
  3.3 10.0 %collective-permute-start = (bf16[256,128]{1,0:T(8,128)(2,1)S(1)}, bf16[256,128]{1,0:T(8,128)(2,1)S(1)}, u32[]{:S(2)}, u32[]{:S(2)}) collective-permute-start(bf16[256,128]{1,0:T(8,128)(2,1)S(1)} %get-tuple-element.33), channel_id=1, source_target_pairs={{0,8},{2,10},{4,12},{6,14},{8,0},{10,2},{12,4},{14,6},{1,9},{3,11}... | collective-permute-start | bytes 196616 | tf_op jit(solution)/shard_map/ppermute | solution.py:275
  7.4 9.6 %collective-permute-start.3 = (bf16[256,128]{1,0:T(8,128)(2,1)S(1)}, bf16[256,128]{1,0:T(8,128)(2,1)S(1)}, u32[]{:S(2)}, u32[]{:S(2)}) collective-permute-start(bf16[256,128]{1,0:T(8,128)(2,1)S(1)} %get-tuple-element.38), channel_id=1, source_target_pairs={{0,10},{2,8},{4,14},{6,12},{8,2},{10,0},{12,6},{14,4},{1,11},{3,9}... | collective-permute-start | bytes 196616 | tf_op jit(solution)/shard_map/ppermute | solution.py:275
  8.7 13.7 %collective-permute-start.1 = (bf16[512,128]{1,0:T(8,128)(2,1)S(1)}, bf16[512,128]{1,0:T(8,128)(2,1)S(1)}, u32[]{:S(2)}, u32[]{:S(2)}) collective-permute-start(bf16[512,128]{1,0:T(8,128)(2,1)S(1)} %get-tuple-element.36), channel_id=1, source_target_pairs={{0,2},{2,0},{4,6},{6,4},{8,10},{10,8},{12,14},{14,12},{1,3},{3,1},... | collective-permute-start | bytes 393224 | tf_op jit(solution)/shard_map/ppermute | solution.py:275
  9.0 16.7 %collective-permute-start.2 = (bf16[512,128]{1,0:T(8,128)(2,1)S(1)}, bf16[512,128]{1,0:T(8,128)(2,1)S(1)}, u32[]{:S(2)}, u32[]{:S(2)}) collective-permute-start(bf16[512,128]{1,0:T(8,128)(2,1)S(1)} %get-tuple-element.37), channel_id=1, source_target_pairs={{0,4},{2,6},{4,0},{6,2},{8,12},{10,14},{12,8},{14,10},{1,5},{3,7},... | collective-permute-start | bytes 393224 | tf_op jit(solution)/shard_map/ppermute | solution.py:275
  10.8 15.5 %collective-permute-start.4 = (bf16[512,128]{1,0:T(8,128)(2,1)S(1)}, bf16[512,128]{1,0:T(8,128)(2,1)S(1)}, u32[]{:S(2)}, u32[]{:S(2)}) collective-permute-start(bf16[512,128]{1,0:T(8,128)(2,1)S(1)} %get-tuple-element.39), channel_id=1, source_target_pairs={{0,12},{2,14},{4,8},{6,10},{8,4},{10,6},{12,0},{14,2},{1,13},{3,15... | collective-permute-start | bytes 393224 | tf_op jit(solution)/shard_map/ppermute | solution.py:275
  13.3 13.1 %collective-permute-start.5 = (bf16[512,128]{1,0:T(8,128)(2,1)S(1)}, bf16[512,128]{1,0:T(8,128)(2,1)S(1)}, u32[]{:S(2)}, u32[]{:S(2)}) collective-permute-start(bf16[512,128]{1,0:T(8,128)(2,1)S(1)} %get-tuple-element.40), channel_id=1, source_target_pairs={{0,14},{2,12},{4,10},{6,8},{8,6},{10,4},{12,2},{14,0},{1,15},{3,13... | collective-permute-start | bytes 393224 | tf_op jit(solution)/shard_map/ppermute | solution.py:275
  17.0 9.4 %collective-permute-start.6 = (bf16[512,128]{1,0:T(8,128)(2,1)S(1)}, bf16[512,128]{1,0:T(8,128)(2,1)S(1)}, u32[]{:S(2)}, u32[]{:S(2)}) collective-permute-start(bf16[512,128]{1,0:T(8,128)(2,1)S(1)} %get-tuple-element.41), channel_id=1, source_target_pairs={{0,6},{2,4},{4,2},{6,0},{8,14},{10,12},{12,10},{14,8},{1,7},{3,5},... | collective-permute-start | bytes 393224 | tf_op jit(solution)/shard_map/ppermute | solution.py:275
  22.4 8.7 %collective-permute-start.8 = (bf16[256,128]{1,0:T(8,128)(2,1)S(1)}, bf16[256,128]{1,0:T(8,128)(2,1)S(1)}, u32[]{:S(2)}, u32[]{:S(2)}) collective-permute-start(bf16[256,128]{1,0:T(8,128)(2,1)S(1)} %get-tuple-element.45), channel_id=1, source_target_pairs={{0,8},{2,10},{4,12},{6,14},{8,0},{10,2},{12,4},{14,6},{1,9},{3,11}... | collective-permute-start | bytes 196616 | tf_op jit(solution)/shard_map/ppermute | solution.py:275
  25.7 6.8 %collective-permute-start.9 = (bf16[256,128]{1,0:T(8,128)(2,1)S(1)}, bf16[256,128]{1,0:T(8,128)(2,1)S(1)}, u32[]{:S(2)}, u32[]{:S(2)}) collective-permute-start(bf16[256,128]{1,0:T(8,128)(2,1)S(1)} %get-tuple-element.47), channel_id=1, source_target_pairs={{0,10},{2,8},{4,14},{6,12},{8,2},{10,0},{12,6},{14,4},{1,11},{3,9}... | collective-permute-start | bytes 196616 | tf_op jit(solution)/shard_map/ppermute | solution.py:275
  27.1 5.5 %collective-permute-start.7 = (f32[64,128]{1,0:T(8,128)S(1)}, f32[64,128]{1,0:T(8,128)S(1)}, u32[]{:S(2)}, u32[]{:S(2)}) collective-permute-start(f32[64,128]{1,0:T(8,128)S(1)} %get-tuple-element.60.mine.d_mine), channel_id=1, source_target_pairs={{0,1},{1,0},{2,3},{3,2},{4,5},{5,4},{6,7},{7,6},{8,9},{9,8},{10,11... | collective-permute-start | bytes 98312 | tf_op jit(solution)/shard_map/ppermute | solution.py:292
  33.3 7.4 %collective-permute-start.16 = (bf16[256,128]{1,0:T(8,128)(2,1)S(1)}, bf16[256,128]{1,0:T(8,128)(2,1)S(1)}, u32[]{:S(2)}, u32[]{:S(2)}) collective-permute-start(bf16[256,128]{1,0:T(8,128)(2,1)S(1)} %get-tuple-element.49), channel_id=1, source_target_pairs={{0,8},{2,10},{4,12},{6,14},{8,0},{10,2},{12,4},{14,6},{1,9},{3,11}... | collective-permute-start | bytes 196616 | tf_op jit(solution)/shard_map/ppermute | solution.py:275
  33.4 8.3 %collective-permute-start.17 = (bf16[256,128]{1,0:T(8,128)(2,1)S(1)}, bf16[256,128]{1,0:T(8,128)(2,1)S(1)}, u32[]{:S(2)}, u32[]{:S(2)}) collective-permute-start(bf16[256,128]{1,0:T(8,128)(2,1)S(1)} %get-tuple-element.50), channel_id=1, source_target_pairs={{0,10},{2,8},{4,14},{6,12},{8,2},{10,0},{12,6},{14,4},{1,11},{3,9}... | collective-permute-start | bytes 196616 | tf_op jit(solution)/shard_map/ppermute | solution.py:275
  37.0 1.3 %collective-permute-start.10 = (f32[64,128]{1,0:T(8,128)S(1)}, f32[64,128]{1,0:T(8,128)S(1)}, u32[]{:S(2)}, u32[]{:S(2)}) collective-permute-start(f32[64,128]{1,0:T(8,128)S(1)} %shard_map.72.mine), channel_id=1, source_target_pairs={{0,1},{1,0},{2,3},{3,2},{4,5},{5,4},{6,7},{7,6},{8,9},{9,8},{10,11... | collective-permute-start | bytes 98312 | tf_op jit(solution)/shard_map/ppermute | solution.py:292
  40.7 8.8 %collective-permute-start.18 = (bf16[256,128]{1,0:T(8,128)(2,1)S(1)}, bf16[256,128]{1,0:T(8,128)(2,1)S(1)}, u32[]{:S(2)}, u32[]{:S(2)}) collective-permute-start(bf16[256,128]{1,0:T(8,128)(2,1)S(1)} %get-tuple-element.61), channel_id=1, source_target_pairs={{0,8},{2,10},{4,12},{6,14},{8,0},{10,2},{12,4},{14,6},{1,9},{3,11}... | collective-permute-start | bytes 196616 | tf_op jit(solution)/shard_map/ppermute | solution.py:275
  41.7 11.0 %collective-permute-start.19 = (bf16[256,128]{1,0:T(8,128)(2,1)S(1)}, bf16[256,128]{1,0:T(8,128)(2,1)S(1)}, u32[]{:S(2)}, u32[]{:S(2)}) collective-permute-start(bf16[256,128]{1,0:T(8,128)(2,1)S(1)} %get-tuple-element.62), channel_id=1, source_target_pairs={{0,10},{2,8},{4,14},{6,12},{8,2},{10,0},{12,6},{14,4},{1,11},{3,9}... | collective-permute-start | bytes 196616 | tf_op jit(solution)/shard_map/ppermute | solution.py:275
  43.3 12.5 %collective-permute-start.11 = (bf16[512,128]{1,0:T(8,128)(2,1)S(1)}, bf16[512,128]{1,0:T(8,128)(2,1)S(1)}, u32[]{:S(2)}, u32[]{:S(2)}) collective-permute-start(bf16[512,128]{1,0:T(8,128)(2,1)S(1)} %get-tuple-element.52), channel_id=1, source_target_pairs={{0,12},{2,14},{4,8},{6,10},{8,4},{10,6},{12,0},{14,2},{1,13},{3,15... | collective-permute-start | bytes 393224 | tf_op jit(solution)/shard_map/ppermute | solution.py:275
  46.7 9.1 %collective-permute-start.12 = (bf16[512,128]{1,0:T(8,128)(2,1)S(1)}, bf16[512,128]{1,0:T(8,128)(2,1)S(1)}, u32[]{:S(2)}, u32[]{:S(2)}) collective-permute-start(bf16[512,128]{1,0:T(8,128)(2,1)S(1)} %get-tuple-element.53), channel_id=1, source_target_pairs={{0,4},{2,6},{4,0},{6,2},{8,12},{10,14},{12,8},{14,10},{1,5},{3,7},... | collective-permute-start | bytes 393224 | tf_op jit(solution)/shard_map/ppermute | solution.py:275
  46.7 13.4 %collective-permute-start.13 = (bf16[512,128]{1,0:T(8,128)(2,1)S(1)}, bf16[512,128]{1,0:T(8,128)(2,1)S(1)}, u32[]{:S(2)}, u32[]{:S(2)}) collective-permute-start(bf16[512,128]{1,0:T(8,128)(2,1)S(1)} %get-tuple-element.54), channel_id=1, source_target_pairs={{0,6},{2,4},{4,2},{6,0},{8,14},{10,12},{12,10},{14,8},{1,7},{3,5},... | collective-permute-start | bytes 393224 | tf_op jit(solution)/shard_map/ppermute | solution.py:275
  49.5 10.5 %collective-permute-start.14 = (bf16[512,128]{1,0:T(8,128)(2,1)S(1)}, bf16[512,128]{1,0:T(8,128)(2,1)S(1)}, u32[]{:S(2)}, u32[]{:S(2)}) collective-permute-start(bf16[512,128]{1,0:T(8,128)(2,1)S(1)} %get-tuple-element.55), channel_id=1, source_target_pairs={{0,14},{2,12},{4,10},{6,8},{8,6},{10,4},{12,2},{14,0},{1,15},{3,13... | collective-permute-start | bytes 393224 | tf_op jit(solution)/shard_map/ppermute | solution.py:275
  52.7 9.0 %collective-permute-start.15 = (bf16[512,128]{1,0:T(8,128)(2,1)S(1)}, bf16[512,128]{1,0:T(8,128)(2,1)S(1)}, u32[]{:S(2)}, u32[]{:S(2)}) collective-permute-start(bf16[512,128]{1,0:T(8,128)(2,1)S(1)} %get-tuple-element.56), channel_id=1, source_target_pairs={{0,2},{2,0},{4,6},{6,4},{8,10},{10,8},{12,14},{14,12},{1,3},{3,1},... | collective-permute-start | bytes 393224 | tf_op jit(solution)/shard_map/ppermute | solution.py:275

commit v13 on v5

--- a/solution.py
+++ b/solution.py
@@ -8,6 +8,12 @@
 from jax.sharding import PartitionSpec as P
 
 adapter_alpha = 128.0
+FETCH = (1, 4, 2, 5, 6, 3, 7)
+FETCH_TIES = {}
+SEND = (1, 4, 2, 5, 6, 3, 7)
+SEND_TIES = {}
+PREP_AFTER = 1
+LATE = (3, 7)
 
 in_vmem = pl.BlockSpec(memory_space=pltpu.VMEM)
 in_smem = pl.BlockSpec(memory_space=pltpu.SMEM)
@@ -43,7 +49,10 @@
         copy.wait()
 
 
-def prep_kernel(rows, after, x, y, turned, blank, zeros, sem):
+def prep_kernel(ids, here, table, after, x, y, turned, own, blank, zeros, sem, own_sem):
+    own_copy = pltpu.make_async_copy(table.at[ids[here[0]]], own, own_sem)
+    own_copy.start()
+    rows = own.shape[0]
     zeros[...] = jnp.zeros_like(zeros)
     step = zeros.shape[0]
     copies = [
@@ -60,7 +69,7 @@
         turned[owner, :, pl.ds(0, tokens)] = x[:, columns].T
         turned[owner, :, pl.ds(tokens, tokens)] = y[:, columns].T
 
-    for copy in copies:
+    for copy in [own_copy, *copies]:
         copy.wait()
 
 
@@ -114,57 +123,67 @@
         ).astype(jnp.bfloat16)
 
 
-def merge_kernel(peers, ids, here, lengths, *refs):
-    owners = len(peers)
-    pieces = refs[:owners]
-    out, total, held, sems = refs[owners + 1 :]
-    blocks = [here[0] ^ k for k in peers]
-    copies, firsts = [], []
-    for k in range(owners):
-        adapter = ids[blocks[k]]
-        copies.append(pltpu.make_async_copy(held.at[k], out.at[adapter], sems.at[k]))
-        same = [ids[blocks[other]] == adapter for other in range(owners)]
-        earlier = functools.reduce(jnp.logical_or, same[:k], jnp.bool_(False))
-        later = functools.reduce(jnp.logical_or, same[k + 1 :], jnp.bool_(False))
-        firsts.append(jnp.logical_not(earlier))
-
-        def store(value, count):
+def merge_kernel(peers, handled, others, ids, here, lengths, *refs):
+    pieces = dict(zip(peers, refs[:-5]))
+    out, total, held, sems = refs[-4:]
+    me = here[0]
+    width = total.shape[1]
+    others_here = all(k in pieces for k in others)
+
+    def value(k):
+        return pieces[k][...].astype(jnp.float32)
+
+    def either(conditions):
+        return functools.reduce(jnp.logical_or, conditions, jnp.bool_(False))
+
+    copies, chosen = [], []
+    for n, k in enumerate(handled):
+        adapter = ids[me ^ k]
+        copies.append(pltpu.make_async_copy(held.at[n], out.at[adapter], sems.at[n]))
+        same = {other: ids[me ^ other] == adapter for other in (*handled, *others) if other != k}
+        skip = either([same[other] for other in handled[:n]])
+        adding = list(handled[n + 1 :])
+        if others_here:
+            adding += others
+        else:
+            skip |= either([same[other] for other in others])
+        more = either([same[other] for other in adding])
+        chosen.append(jnp.logical_not(skip))
+
+        def store(sum_of, count):
             denom = jnp.maximum(count.astype(jnp.float32), 1.0)
-            part = 1.0 / jnp.full((1, value.shape[1]), denom)
-            held[k] = (value * part).astype(jnp.bfloat16)
-            copies[k].start()
-
-        @pl.when(firsts[k] & jnp.logical_not(later))
+            part = 1.0 / jnp.full((1, width), denom)
+            held[n] = (sum_of * part).astype(jnp.bfloat16)
+            copies[n].start()
+
+        @pl.when(chosen[n] & jnp.logical_not(more))
         def _():
-            store(pieces[k][...].astype(jnp.float32), lengths[blocks[k]])
-
-        @pl.when(firsts[k] & later)
+            store(value(k), lengths[me ^ k])
+
+        @pl.when(chosen[n] & more)
         def _():
-            total[...] = pieces[k][...].astype(jnp.float32)
-            count = lengths[blocks[k]]
-            for other in range(k + 1, owners):
-                count += jnp.where(same[other], lengths[blocks[other]], 0)
+            total[...] = value(k)
+            count = lengths[me ^ k]
+            for other in adding:
+                count += jnp.where(same[other], lengths[me ^ other], 0)
 
                 @pl.when(same[other])
                 def _():
-                    total[...] += pieces[other][...].astype(jnp.float32)
+                    total[...] += value(other)
 
             store(total[...], count)
 
-    for k in range(owners):
-        pl.when(firsts[k])(copies[k].wait)
-
-
-def peer_order(owners):
-    near = list(range(1, owners // 2))
-    return (0, *range(owners // 2, owners), *near[:1], *near[:0:-1])
-
-
-def exchange(pieces, peers):
-    out = [pieces[0]]
-    for k, piece in zip(peers[1:], pieces[1:]):
-        out.append(lax.ppermute(piece, "dp", [(i, i ^ k) for i in range(len(peers))]))
-    return out
+    for n in range(len(handled)):
+        pl.when(chosen[n])(copies[n].wait)
+
+
+def exchange(pieces, ties):
+    owners = lax.axis_size("dp")
+    out = {}
+    for k in sorted(pieces, key=lambda k: k in ties):
+        piece = lax.optimization_barrier((pieces[k], out[ties[k]]))[0] if k in ties else pieces[k]
+        out[k] = lax.ppermute(piece, "dp", [(i, i ^ k) for i in range(owners)])
+    return {k: out[k] for k in pieces}
 
 
 def across_cores(value):
@@ -174,7 +193,6 @@
 
 def with_kernels(activations, cotangent, adapter_weight_pair, adapter_of_block, block_live_length):
     owners = lax.axis_size("dp")
-    peers = peer_order(owners)
     here = lax.axis_index("dp").astype(jnp.int32).reshape(1)
     ids, lengths = adapter_of_block[:, 0], block_live_length[:, 0]
     count, _, rows, width = adapter_weight_pair.shape
@@ -182,77 +200,90 @@
     tokens, features = activations.shape
     scale = adapter_alpha / (width // 2)
     bf16, f32 = jnp.bfloat16, jnp.float32
-    pair_shapes = [jax.ShapeDtypeStruct((rows, width), bf16)] * owners
+    straight = jax.ShapeDtypeStruct((rows, width), bf16)
     pair_bytes = owners * rows * width * 2
     token_bytes = tokens * features * 2
+    partners = len(FETCH)
 
     sent = call(
-        functools.partial(gather_kernel, peers),
-        pair_shapes,
+        functools.partial(gather_kernel, FETCH),
+        [straight] * partners,
         [in_smem, in_smem, in_hbm],
-        [in_vmem] * owners,
-        [pltpu.SemaphoreType.DMA((owners,))],
+        [in_vmem] * partners,
+        [pltpu.SemaphoreType.DMA((partners,))],
         moved=2 * pair_bytes,
         vmem=53,
     )(ids, here, table)
-    pairs = exchange(sent, peers)
+    pairs = exchange(dict(zip(FETCH, sent)), FETCH_TIES)
 
     step = 8
-    turned, blank = call(
-        functools.partial(prep_kernel, rows),
+    turned, own, blank = call(
+        prep_kernel,
         [
             jax.ShapeDtypeStruct((owners, rows, 2 * tokens), bf16),
+            straight,
             jax.ShapeDtypeStruct(table.shape, bf16),
         ],
-        [in_hbm, in_vmem, in_vmem],
-        [in_vmem, in_hbm],
-        [pltpu.VMEM((step, rows, width), bf16), pltpu.SemaphoreType.DMA((count // step,))],
+        [in_smem, in_smem, in_hbm, in_hbm, in_vmem, in_vmem],
+        [in_vmem, in_vmem, in_hbm],
+        [
+            pltpu.VMEM((step, rows, width), bf16),
+            pltpu.SemaphoreType.DMA((count // step,)),
+            pltpu.SemaphoreType.DMA,
+        ],
         moved=4 * token_bytes + 2 * count * rows * width,
-    )(pairs[5], activations, cotangent)
-    *pairs, turned, blank = lax.optimization_barrier((*pairs, turned, blank))
+    )(ids, here, table, pairs[PREP_AFTER], activations, cotangent)
+    pairs[0] = own
 
     mine = call(
-        functools.partial(rank_kernel, peers),
+        functools.partial(rank_kernel, tuple(pairs)),
         jax.ShapeDtypeStruct((tokens, width), f32),
         [in_smem] + [in_vmem] * (2 + owners),
         in_vmem,
-        flops=4 * tokens * features * width,
-        moved=2 * token_bytes + pair_bytes,
-    )(here, activations, cotangent, *pairs)
+        moved=1024,
+    )(here, lax.optimization_barrier((activations, turned))[0], cotangent, *pairs.values())
     other = across_cores(mine)
 
+    peers = (*SEND, 0)
     pieces = call(
         functools.partial(piece_kernel, peers, scale),
-        pair_shapes,
+        [straight] * owners,
         [in_smem] * 2 + [in_vmem] * 3,
         [in_vmem] * owners,
-        flops=4 * tokens * features * width,
-        moved=2 * token_bytes + pair_bytes,
+        moved=1024,
     )(here, lengths, mine, other, turned)
-    arrived = exchange(pieces, peers)
+    arrived = exchange(dict(zip(SEND, pieces)), SEND_TIES)
+    arrived[0] = pieces[-1]
 
     grad_input = call(
-        functools.partial(input_kernel, peers, scale),
+        functools.partial(input_kernel, tuple(pairs), scale),
         jax.ShapeDtypeStruct((tokens, features), bf16),
         [in_smem] * 2 + [in_vmem] * (2 + owners),
         in_vmem,
         flops=2 * tokens * features * width,
         moved=token_bytes + pair_bytes,
-    )(here, lengths, mine, other, *pairs)
-
-    gradient = call(
-        functools.partial(merge_kernel, peers),
-        jax.ShapeDtypeStruct(table.shape, bf16),
-        [in_smem] * 3 + [in_vmem] * owners + [in_hbm],
-        in_hbm,
-        [
-            pltpu.VMEM((rows, width), f32),
-            pltpu.VMEM((owners, rows, width), bf16),
-            pltpu.SemaphoreType.DMA((owners,)),
-        ],
-        moved=2 * pair_bytes,
-        aliases={3 + owners: 0},
-    )(ids, here, lengths, *arrived, blank)
+    )(here, lengths, lax.optimization_barrier((mine, *pieces))[0], other, *pairs.values())
+
+    late = tuple(k for k in peers if k in LATE)
+    early = tuple(k for k in peers if k not in LATE)
+
+    def merge(handled, others, merged, so_far):
+        return call(
+            functools.partial(merge_kernel, tuple(merged), handled, others),
+            jax.ShapeDtypeStruct(table.shape, bf16),
+            [in_smem] * 3 + [in_vmem] * len(merged) + [in_hbm],
+            in_hbm,
+            [
+                pltpu.VMEM((rows, width), f32),
+                pltpu.VMEM((len(handled), rows, width), bf16),
+                pltpu.SemaphoreType.DMA((len(handled),)),
+            ],
+            moved=2 * pair_bytes,
+            aliases={3 + len(merged): 0},
+        )(ids, here, lengths, *merged.values(), so_far)
+
+    early_pieces = {k: arrived[k] for k in early}
+    gradient = merge(late, early, arrived, merge(early, late, early_pieces, blank))
     return grad_input, gradient[:, None]
 
 
@@ -295,7 +326,7 @@
 
     def on_device(activations, cotangent, adapter_weight_pair, *rest):
         rows = adapter_weight_pair.shape[2]
-        fits = owners & (owners - 1) == 0 and cores == 2 and rows % 256 == 0
+        fits = owners == len(FETCH) + 1 and cores == 2 and rows % 256 == 0
         body = with_kernels if fits else without_kernels
         return body(activations, cotangent, adapter_weight_pair, *rest)
 

time: 63.8 us -> 61.7 us (0.967)
  the two profiles are of different devices: /device:TPU:0 before, /device:TPU:11 now
where the time goes in v13:
time: 61.7 us; the launch traced here: 61.5 us
  waiting for transfers between devices  27.5 us (45%)
  starting transfers between devices  18.5 us (30%)
  Pallas kernels  14 us (23%)
  local copies, waits for them, and re-layouts  0.81 us (1%)
  between operations  0.73 us (1%)
    ppermute x14, waiting for transfers between devices, exchange(): out[k] = lax.ppermute(piece, 'dp', [(i, i ^ k) for i in range(owners)])  26.6 us
    ppermute x14, starting transfers between devices, exchange(): out[k] = lax.ppermute(piece, 'dp', [(i, i ^ k) for i in range(owners)])  17.1 us
    pallas_call x1, Pallas kernels, with_kernels(): call(prep_kernel, [jax.ShapeDtypeStruct((owners, rows, 2 * tokens), bf16)...  5.35 us
    pallas_call x2, Pallas kernels, merge(): call(functools.partial(merge_kernel, tuple(merged), handled, others), jax...  2.82 us
    pallas_call x1, Pallas kernels, with_kernels(): call(functools.partial(input_kernel, tuple(pairs), scale), jax.ShapeDtype...  1.98 us
    pallas_call x1, Pallas kernels, with_kernels(): call(functools.partial(gather_kernel, FETCH), [straight] * partners, [in_...  1.85 us
    ppermute x1, starting transfers between devices, across_cores(): return lax.ppermute(value, 'tensor', [(i, i ^ 1) for i in range(cores)])  1.38 us
    pallas_call x1, Pallas kernels, with_kernels(): call(functools.partial(piece_kernel, peers, scale), [straight] * owners,...  1.32 us
  transfers between devices with their start and end apart: 15, of which 8 were waited for; matrix products, arithmetic and copies ran while one was open for 0% of the time, Pallas kernels for 14%

profile of v13, /device:TPU:11, one launch (start us, length us, event | category | flops | bytes accessed | tf_op | source)
XLA Modules:
  0.0 61.5 jit_solution(17280595652174457559)
XLA Ops:
  0.7 0.8 %copy-done.2 = s32[8,1]{0,1:T(1,128)S(1)} copy-done((s32[8,1]{0,1:T(1,128)S(1)}, s32[8,1]{0,1:T(1,128)}, u32[]{:S(2)}) %copy-start.2) | copy-done | bytes 56
  1.5 1.8 %shard_map.68 = (bf16[512,128]{1,0:T(8,128)(2,1)S(1)}, bf16[512,128]{1,0:T(8,128)(2,1)S(1)}, bf16[512,128]{1,0:T(8,128)(2,1)S(1)}, bf16[512,128]{1,0:T(8,128)(2,...) custom-call(s32[8]{0:T(128)S(1)} %bitcast.7, s32[1]{0:T(128)} %bitcast.here, ...), custom_call_target="tpu_custom_call" | custom-call | bytes 2097152 | tf_op jit(solution)/shard_map/pallas_call | solution.py:208
  3.3 0.3 collective-permute-start
  3.6 2.3 %collective-permute-start.1 = (bf16[512,128]{1,0:T(8,128)(2,1)S(1)}, bf16[512,128]{1,0:T(8,128)(2,1)S(1)}, u32[]{:S(2)}, u32[]{:S(2)}) collective-permute-start(bf16[512,128]{1,0:T(8,128)(2,1)S(1)} %get-tuple-element.25), channel_id=1, source_target_pairs={{0,8},{2,10},{4,12},{6,14},{8,0},{10,2},{12,4},{14,6},{1,9},{3,11}... | collective-permute-start | bytes 393224 | tf_op jit(solution)/shard_map/ppermute | solution.py:185
  5.9 0.2 collective-permute-start.2
  6.1 1.0 %collective-permute-start.3 = (bf16[512,128]{1,0:T(8,128)(2,1)S(1)}, bf16[512,128]{1,0:T(8,128)(2,1)S(1)}, u32[]{:S(2)}, u32[]{:S(2)}) collective-permute-start(bf16[512,128]{1,0:T(8,128)(2,1)S(1)} %get-tuple-element.27), channel_id=1, source_target_pairs={{0,10},{2,8},{4,14},{6,12},{8,2},{10,0},{12,6},{14,4},{1,11},{3,9}... | collective-permute-start | bytes 393224 | tf_op jit(solution)/shard_map/ppermute | solution.py:185
  7.1 2.4 %collective-permute-start.4 = (bf16[512,128]{1,0:T(8,128)(2,1)S(1)}, bf16[512,128]{1,0:T(8,128)(2,1)S(1)}, u32[]{:S(2)}, u32[]{:S(2)}) collective-permute-start(bf16[512,128]{1,0:T(8,128)(2,1)S(1)} %get-tuple-element.28), channel_id=1, source_target_pairs={{0,12},{2,14},{4,8},{6,10},{8,4},{10,6},{12,0},{14,2},{1,13},{3,15... | collective-permute-start | bytes 393224 | tf_op jit(solution)/shard_map/ppermute | solution.py:185
  9.5 1.0 %collective-permute-start.5 = (bf16[512,128]{1,0:T(8,128)(2,1)S(1)}, bf16[512,128]{1,0:T(8,128)(2,1)S(1)}, u32[]{:S(2)}, u32[]{:S(2)}) collective-permute-start(bf16[512,128]{1,0:T(8,128)(2,1)S(1)} %get-tuple-element.29), channel_id=1, source_target_pairs={{0,6},{2,4},{4,2},{6,0},{8,14},{10,12},{12,10},{14,8},{1,7},{3,5},... | collective-permute-start | bytes 393224 | tf_op jit(solution)/shard_map/ppermute | solution.py:185
  10.6 2.2 %collective-permute-done.1.refs_1_ = bf16[512,128]{1,0:T(8,128)(2,1)S(1)} collective-permute-done((bf16[512,128]{1,0:T(8,128)(2,1)S(1)}, bf16[512,128]{1,0:T(8,128)(2,1)S(1)}, u32[]{:S(2)}, u32[]{:S(2)}) %collective-permute-start.1) | collective-permute-done | bytes 131104 | tf_op jit(solution)/shard_map/ppermute | solution.py:185
  12.7 0.0 collective-permute-start.6
  12.7 5.3 %shard_map.69 = (bf16[8,512,256]{2,1,0:T(8,128)(2,1)S(1)}, bf16[512,128]{1,0:T(8,128)(2,1)S(1)}, bf16[96,512,128]{2,1,0:T(8,128)(2,1)}) custom-call(s32[8]{0:T(128)S(1)} %bitcast.8, s32[1]{0:T(128)} %bitcast.here, bf16[96,512,128]{2,1,0:T(8,128)(2,1)} %bitcast.17, bf16[512,128]{1,0:T(8,128)(2,1)S(1)} %collective-permute-done.after.refs_0_, ...), custom_call_target="tpu_custom_call" | custom-call | bytes 16777216 | tf_op jit(solution)/shard_map/pallas_call | solution.py:220
  18.1 3.1 %collective-permute-done.3.refs_3_ = bf16[512,128]{1,0:T(8,128)(2,1)S(1)} collective-permute-done((bf16[512,128]{1,0:T(8,128)(2,1)S(1)}, bf16[512,128]{1,0:T(8,128)(2,1)S(1)}, u32[]{:S(2)}, u32[]{:S(2)}) %collective-permute-start.3) | collective-permute-done | bytes 131104 | tf_op jit(solution)/shard_map/ppermute | solution.py:185
  21.2 4.7 %collective-permute-done.4.refs_4_ = bf16[512,128]{1,0:T(8,128)(2,1)S(1)} collective-permute-done((bf16[512,128]{1,0:T(8,128)(2,1)S(1)}, bf16[512,128]{1,0:T(8,128)(2,1)S(1)}, u32[]{:S(2)}, u32[]{:S(2)}) %collective-permute-start.4) | collective-permute-done | bytes 131104 | tf_op jit(solution)/shard_map/ppermute | solution.py:185
  25.9 0.0 collective-permute-done.5.refs_5_
  25.9 2.8 %collective-permute-done.6.refs_6_ = bf16[512,128]{1,0:T(8,128)(2,1)S(1)} collective-permute-done((bf16[512,128]{1,0:T(8,128)(2,1)S(1)}, bf16[512,128]{1,0:T(8,128)(2,1)S(1)}, u32[]{:S(2)}, u32[]{:S(2)}) %collective-permute-start.6) | collective-permute-done | bytes 131104 | tf_op jit(solution)/shard_map/ppermute | solution.py:185
  28.7 0.7 %shard_map.70.mine = f32[128,128]{1,0:T(8,128)S(1)} custom-call(s32[1]{0:T(128)} %bitcast.here, bf16[128,4096]{1,0:T(8,128)(2,1)S(1)} %copy-done, bf16[128,4096]{1,0:T(8,128)(2,1)S(1)} %copy-done.1, bf16[512,128]{1,0:T(8,128)(2,1)S(1)} %collective-permute-done.after.refs_0_, bf16[512,128]{1,0:T(8,128)(2,1)S(1)} %collective-permute-done.1.refs_1_, ...), custom_call_target="tpu_custom_call" | custom-call | bytes 1024 | tf_op jit(solution)/shard_map/pallas_call | solution.py:238
  29.4 1.4 %collective-permute-start.7 = (f32[128,128]{1,0:T(8,128)S(1)}, f32[128,128]{1,0:T(8,128)S(1)}, u32[]{:S(2)}, u32[]{:S(2)}) collective-permute-start(f32[128,128]{1,0:T(8,128)S(1)} %shard_map.70.mine), channel_id=1, source_target_pairs={{0,1},{1,0},{2,3},{3,2},{4,5},{5,4},{6,7},{7,6},{8,9},{9,8},{10,11... | collective-permute-start | bytes 196616 | tf_op jit(solution)/shard_map/ppermute | solution.py:191
  30.8 0.9 %collective-permute-done.7.other = f32[128,128]{1,0:T(8,128)S(1)} collective-permute-done((f32[128,128]{1,0:T(8,128)S(1)}, f32[128,128]{1,0:T(8,128)S(1)}, u32[]{:S(2)}, u32[]{:S(2)}) %collective-permute-start.7) | collective-permute-done | bytes 65568 | tf_op jit(solution)/shard_map/ppermute | solution.py:191
  31.7 1.3 %shard_map.71 = (bf16[512,128]{1,0:T(8,128)(2,1)S(1)}, bf16[512,128]{1,0:T(8,128)(2,1)S(1)}, bf16[512,128]{1,0:T(8,128)(2,1)S(1)}, bf16[512,128]{1,0:T(8,128)(2,...) custom-call(s32[1]{0:T(128)} %bitcast.here, ...), custom_call_target="tpu_custom_call" | custom-call | bytes 1024 | tf_op jit(solution)/shard_map/pallas_call | solution.py:248
  33.0 0.5 collective-permute-start.8
  33.5 0.0 collective-permute-start.9
  33.5 3.4 %collective-permute-start.10 = (bf16[512,128]{1,0:T(8,128)(2,1)S(1)}, bf16[512,128]{1,0:T(8,128)(2,1)S(1)}, u32[]{:S(2)}, u32[]{:S(2)}) collective-permute-start(bf16[512,128]{1,0:T(8,128)(2,1)S(1)} %get-tuple-element.34), channel_id=1, source_target_pairs={{0,4},{2,6},{4,0},{6,2},{8,12},{10,14},{12,8},{14,10},{1,5},{3,7},... | collective-permute-start | bytes 393224 | tf_op jit(solution)/shard_map/ppermute | solution.py:185
  36.9 0.9 %collective-permute-start.11 = (bf16[512,128]{1,0:T(8,128)(2,1)S(1)}, bf16[512,128]{1,0:T(8,128)(2,1)S(1)}, u32[]{:S(2)}, u32[]{:S(2)}) collective-permute-start(bf16[512,128]{1,0:T(8,128)(2,1)S(1)} %get-tuple-element.35), channel_id=1, source_target_pairs={{0,10},{2,8},{4,14},{6,12},{8,2},{10,0},{12,6},{14,4},{1,11},{3,9}... | collective-permute-start | bytes 393224 | tf_op jit(solution)/shard_map/ppermute | solution.py:185
  37.8 1.2 %collective-permute-start.12 = (bf16[512,128]{1,0:T(8,128)(2,1)S(1)}, bf16[512,128]{1,0:T(8,128)(2,1)S(1)}, u32[]{:S(2)}, u32[]{:S(2)}) collective-permute-start(bf16[512,128]{1,0:T(8,128)(2,1)S(1)} %get-tuple-element.36), channel_id=1, source_target_pairs={{0,12},{2,14},{4,8},{6,10},{8,4},{10,6},{12,0},{14,2},{1,13},{3,15... | collective-permute-start | bytes 393224 | tf_op jit(solution)/shard_map/ppermute | solution.py:185
  39.0 2.3 %collective-permute-start.13 = (bf16[512,128]{1,0:T(8,128)(2,1)S(1)}, bf16[512,128]{1,0:T(8,128)(2,1)S(1)}, u32[]{:S(2)}, u32[]{:S(2)}) collective-permute-start(bf16[512,128]{1,0:T(8,128)(2,1)S(1)} %get-tuple-element.37), channel_id=1, source_target_pairs={{0,6},{2,4},{4,2},{6,0},{8,14},{10,12},{12,10},{14,8},{1,7},{3,5},... | collective-permute-start | bytes 393224 | tf_op jit(solution)/shard_map/ppermute | solution.py:185
  41.3 1.6 %collective-permute-start.14 = (bf16[512,128]{1,0:T(8,128)(2,1)S(1)}, bf16[512,128]{1,0:T(8,128)(2,1)S(1)}, u32[]{:S(2)}, u32[]{:S(2)}) collective-permute-start(bf16[512,128]{1,0:T(8,128)(2,1)S(1)} %get-tuple-element.38), channel_id=1, source_target_pairs={{0,14},{2,12},{4,10},{6,8},{8,6},{10,4},{12,2},{14,0},{1,15},{3,13... | collective-permute-start | bytes 393224 | tf_op jit(solution)/shard_map/ppermute | solution.py:185
  42.9 2.0 %shard_map.72 = bf16[128,4096]{1,0:T(8,128)(2,1)} custom-call(s32[1]{0:T(128)} %bitcast.here, s32[8]{0:T(128)S(1)} %bitcast.12, f32[128,128]{1,0:T(8,128)S(1)} %shard_map.70.mine, f32[128,128]{1,0:T(8,128)S(1)} %collective-permute-done.7.other, bf16[512,128]{1,0:T(8,128)(2,1)S(1)} %collective-permute-done.after.refs_0_, ...), custom_call_target="tpu_custom_call" | custom-call | flops 134217728 | bytes 2097152 | tf_op jit(solution)/shard_map/pallas_call | solution.py:258
  44.9 0.4 collective-permute-done.11.refs_3_
  45.3 11.0 %collective-permute-done.12.refs_4_ = bf16[512,128]{1,0:T(8,128)(2,1)S(1)} collective-permute-done((bf16[512,128]{1,0:T(8,128)(2,1)S(1)}, bf16[512,128]{1,0:T(8,128)(2,1)S(1)}, u32[]{:S(2)}, u32[]{:S(2)}) %collective-permute-start.12) | collective-permute-done | bytes 131104 | tf_op jit(solution)/shard_map/ppermute | solution.py:185
  56.3 1.5 %shard_map.73.refs_8_ = bf16[96,512,128]{2,1,0:T(8,128)(2,1)} custom-call(s32[8]{0:T(128)S(1)} %bitcast.9, s32[1]{0:T(128)} %bitcast.here, s32[8]{0:T(128)S(1)} %bitcast.13, bf16[512,128]{1,0:T(8,128)(2,1)S(1)} %collective-permute-done.8.refs_0_, bf16[512,128]{1,0:T(8,128)(2,1)S(1)} %collective-permute-done.9.refs_1_, ...), custom_call_target="tpu_custom_call", output_to_operand_aliasing={{}: (9, {})} | custom-call | bytes 2097152 | tf_op jit(solution)/shard_map/pallas_call | solution.py:271
  57.9 2.3 %collective-permute-done.14.refs_6_ = bf16[512,128]{1,0:T(8,128)(2,1)S(1)} collective-permute-done((bf16[512,128]{1,0:T(8,128)(2,1)S(1)}, bf16[512,128]{1,0:T(8,128)(2,1)S(1)}, u32[]{:S(2)}, u32[]{:S(2)}) %collective-permute-start.14) | collective-permute-done | bytes 131104 | tf_op jit(solution)/shard_map/ppermute | solution.py:185
  60.2 1.3 %shard_map.74 = bf16[96,512,128]{2,1,0:T(8,128)(2,1)} custom-call(s32[8]{0:T(128)S(1)} %bitcast.10, s32[1]{0:T(128)} %bitcast.here, s32[8]{0:T(128)S(1)} %bitcast.14, bf16[512,128]{1,0:T(8,128)(2,1)S(1)} %collective-permute-done.8.refs_0_, bf16[512,128]{1,0:T(8,128)(2,1)S(1)} %collective-permute-done.9.refs_1_, ...), custom_call_target="tpu_custom_call", output_to_operand_aliasing={{}: (11, {})} | custom-call | bytes 2097152 | tf_op jit(solution)/shard_map/pallas_call | solution.py:271
  (13 shorter events, 0.0 us)
Async XLA Ops:
  0.6 12.1 %copy-start.1 = (bf16[128,4096]{1,0:T(8,128)(2,1)S(1)}, bf16[128,4096]{1,0:T(8,128)(2,1)}, u32[]{:S(2)}) copy-start(bf16[128,4096]{1,0:T(8,128)(2,1)} %y.3) | copy-start | bytes 3145732
  0.6 12.1 %copy-start = (bf16[128,4096]{1,0:T(8,128)(2,1)S(1)}, bf16[128,4096]{1,0:T(8,128)(2,1)}, u32[]{:S(2)}) copy-start(bf16[128,4096]{1,0:T(8,128)(2,1)} %x.2) | copy-start | bytes 3145732
  0.7 0.8 %copy-start.2 = (s32[8,1]{0,1:T(1,128)S(1)}, s32[8,1]{0,1:T(1,128)}, u32[]{:S(2)}) copy-start(s32[8,1]{0,1:T(1,128)} %param.8) | copy-start | bytes 100
  1.5 30.2 %copy-start.3 = (s32[8,1]{0,1:T(1,128)S(1)}, s32[8,1]{0,1:T(1,128)}, u32[]{:S(2)}) copy-start(s32[8,1]{0,1:T(1,128)} %param.9) | copy-start | bytes 100
  3.3 6.2 %collective-permute-start = (bf16[512,128]{1,0:T(8,128)(2,1)S(1)}, bf16[512,128]{1,0:T(8,128)(2,1)S(1)}, u32[]{:S(2)}, u32[]{:S(2)}) collective-permute-start(bf16[512,128]{1,0:T(8,128)(2,1)S(1)} %get-tuple-element.22), channel_id=1, source_target_pairs={{0,2},{2,0},{4,6},{6,4},{8,10},{10,8},{12,14},{14,12},{1,3},{3,1},... | collective-permute-start | bytes 393224 | tf_op jit(solution)/shard_map/ppermute | solution.py:185
  3.6 9.1 %collective-permute-start.1 = (bf16[512,128]{1,0:T(8,128)(2,1)S(1)}, bf16[512,128]{1,0:T(8,128)(2,1)S(1)}, u32[]{:S(2)}, u32[]{:S(2)}) collective-permute-start(bf16[512,128]{1,0:T(8,128)(2,1)S(1)} %get-tuple-element.25), channel_id=1, source_target_pairs={{0,8},{2,10},{4,12},{6,14},{8,0},{10,2},{12,4},{14,6},{1,9},{3,11}... | collective-permute-start | bytes 393224 | tf_op jit(solution)/shard_map/ppermute | solution.py:185
  5.9 12.2 %collective-permute-start.2 = (bf16[512,128]{1,0:T(8,128)(2,1)S(1)}, bf16[512,128]{1,0:T(8,128)(2,1)S(1)}, u32[]{:S(2)}, u32[]{:S(2)}) collective-permute-start(bf16[512,128]{1,0:T(8,128)(2,1)S(1)} %get-tuple-element.26), channel_id=1, source_target_pairs={{0,4},{2,6},{4,0},{6,2},{8,12},{10,14},{12,8},{14,10},{1,5},{3,7},... | collective-permute-start | bytes 393224 | tf_op jit(solution)/shard_map/ppermute | solution.py:185
  6.1 15.0 %collective-permute-start.3 = (bf16[512,128]{1,0:T(8,128)(2,1)S(1)}, bf16[512,128]{1,0:T(8,128)(2,1)S(1)}, u32[]{:S(2)}, u32[]{:S(2)}) collective-permute-start(bf16[512,128]{1,0:T(8,128)(2,1)S(1)} %get-tuple-element.27), channel_id=1, source_target_pairs={{0,10},{2,8},{4,14},{6,12},{8,2},{10,0},{12,6},{14,4},{1,11},{3,9}... | collective-permute-start | bytes 393224 | tf_op jit(solution)/shard_map/ppermute | solution.py:185
  7.1 18.8 %collective-permute-start.4 = (bf16[512,128]{1,0:T(8,128)(2,1)S(1)}, bf16[512,128]{1,0:T(8,128)(2,1)S(1)}, u32[]{:S(2)}, u32[]{:S(2)}) collective-permute-start(bf16[512,128]{1,0:T(8,128)(2,1)S(1)} %get-tuple-element.28), channel_id=1, source_target_pairs={{0,12},{2,14},{4,8},{6,10},{8,4},{10,6},{12,0},{14,2},{1,13},{3,15... | collective-permute-start | bytes 393224 | tf_op jit(solution)/shard_map/ppermute | solution.py:185
  9.5 16.4 %collective-permute-start.5 = (bf16[512,128]{1,0:T(8,128)(2,1)S(1)}, bf16[512,128]{1,0:T(8,128)(2,1)S(1)}, u32[]{:S(2)}, u32[]{:S(2)}) collective-permute-start(bf16[512,128]{1,0:T(8,128)(2,1)S(1)} %get-tuple-element.29), channel_id=1, source_target_pairs={{0,6},{2,4},{4,2},{6,0},{8,14},{10,12},{12,10},{14,8},{1,7},{3,5},... | collective-permute-start | bytes 393224 | tf_op jit(solution)/shard_map/ppermute | solution.py:185
  12.7 16.0 %collective-permute-start.6 = (bf16[512,128]{1,0:T(8,128)(2,1)S(1)}, bf16[512,128]{1,0:T(8,128)(2,1)S(1)}, u32[]{:S(2)}, u32[]{:S(2)}) collective-permute-start(bf16[512,128]{1,0:T(8,128)(2,1)S(1)} %get-tuple-element.30), channel_id=1, source_target_pairs={{0,14},{2,12},{4,10},{6,8},{8,6},{10,4},{12,2},{14,0},{1,15},{3,13... | collective-permute-start | bytes 393224 | tf_op jit(solution)/shard_map/ppermute | solution.py:185
  29.4 2.3 %collective-permute-start.7 = (f32[128,128]{1,0:T(8,128)S(1)}, f32[128,128]{1,0:T(8,128)S(1)}, u32[]{:S(2)}, u32[]{:S(2)}) collective-permute-start(f32[128,128]{1,0:T(8,128)S(1)} %shard_map.70.mine), channel_id=1, source_target_pairs={{0,1},{1,0},{2,3},{3,2},{4,5},{5,4},{6,7},{7,6},{8,9},{9,8},{10,11... | collective-permute-start | bytes 196616 | tf_op jit(solution)/shard_map/ppermute | solution.py:191
  33.0 5.9 %collective-permute-start.8 = (bf16[512,128]{1,0:T(8,128)(2,1)S(1)}, bf16[512,128]{1,0:T(8,128)(2,1)S(1)}, u32[]{:S(2)}, u32[]{:S(2)}) collective-permute-start(bf16[512,128]{1,0:T(8,128)(2,1)S(1)} %get-tuple-element.32), channel_id=1, source_target_pairs={{0,2},{2,0},{4,6},{6,4},{8,10},{10,8},{12,14},{14,12},{1,3},{3,1},... | collective-permute-start | bytes 393224 | tf_op jit(solution)/shard_map/ppermute | solution.py:185
  33.5 7.8 %collective-permute-start.9 = (bf16[512,128]{1,0:T(8,128)(2,1)S(1)}, bf16[512,128]{1,0:T(8,128)(2,1)S(1)}, u32[]{:S(2)}, u32[]{:S(2)}) collective-permute-start(bf16[512,128]{1,0:T(8,128)(2,1)S(1)} %get-tuple-element.33), channel_id=1, source_target_pairs={{0,8},{2,10},{4,12},{6,14},{8,0},{10,2},{12,4},{14,6},{1,9},{3,11}... | collective-permute-start | bytes 393224 | tf_op jit(solution)/shard_map/ppermute | solution.py:185
  33.5 11.4 %collective-permute-start.10 = (bf16[512,128]{1,0:T(8,128)(2,1)S(1)}, bf16[512,128]{1,0:T(8,128)(2,1)S(1)}, u32[]{:S(2)}, u32[]{:S(2)}) collective-permute-start(bf16[512,128]{1,0:T(8,128)(2,1)S(1)} %get-tuple-element.34), channel_id=1, source_target_pairs={{0,4},{2,6},{4,0},{6,2},{8,12},{10,14},{12,8},{14,10},{1,5},{3,7},... | collective-permute-start | bytes 393224 | tf_op jit(solution)/shard_map/ppermute | solution.py:185
  36.9 8.4 %collective-permute-start.11 = (bf16[512,128]{1,0:T(8,128)(2,1)S(1)}, bf16[512,128]{1,0:T(8,128)(2,1)S(1)}, u32[]{:S(2)}, u32[]{:S(2)}) collective-permute-start(bf16[512,128]{1,0:T(8,128)(2,1)S(1)} %get-tuple-element.35), channel_id=1, source_target_pairs={{0,10},{2,8},{4,14},{6,12},{8,2},{10,0},{12,6},{14,4},{1,11},{3,9}... | collective-permute-start | bytes 393224 | tf_op jit(solution)/shard_map/ppermute | solution.py:185
  37.8 18.6 %collective-permute-start.12 = (bf16[512,128]{1,0:T(8,128)(2,1)S(1)}, bf16[512,128]{1,0:T(8,128)(2,1)S(1)}, u32[]{:S(2)}, u32[]{:S(2)}) collective-permute-start(bf16[512,128]{1,0:T(8,128)(2,1)S(1)} %get-tuple-element.36), channel_id=1, source_target_pairs={{0,12},{2,14},{4,8},{6,10},{8,4},{10,6},{12,0},{14,2},{1,13},{3,15... | collective-permute-start | bytes 393224 | tf_op jit(solution)/shard_map/ppermute | solution.py:185
  39.0 18.9 %collective-permute-start.13 = (bf16[512,128]{1,0:T(8,128)(2,1)S(1)}, bf16[512,128]{1,0:T(8,128)(2,1)S(1)}, u32[]{:S(2)}, u32[]{:S(2)}) collective-permute-start(bf16[512,128]{1,0:T(8,128)(2,1)S(1)} %get-tuple-element.37), channel_id=1, source_target_pairs={{0,6},{2,4},{4,2},{6,0},{8,14},{10,12},{12,10},{14,8},{1,7},{3,5},... | collective-permute-start | bytes 393224 | tf_op jit(solution)/shard_map/ppermute | solution.py:185
  41.3 18.9 %collective-permute-start.14 = (bf16[512,128]{1,0:T(8,128)(2,1)S(1)}, bf16[512,128]{1,0:T(8,128)(2,1)S(1)}, u32[]{:S(2)}, u32[]{:S(2)}) collective-permute-start(bf16[512,128]{1,0:T(8,128)(2,1)S(1)} %get-tuple-element.38), channel_id=1, source_target_pairs={{0,14},{2,12},{4,10},{6,8},{8,6},{10,4},{12,2},{14,0},{1,15},{3,13... | collective-permute-start | bytes 393224 | tf_op jit(solution)/shard_map/ppermute | solution.py:185

commit v14 on v13

--- a/solution.py
+++ b/solution.py
@@ -8,12 +8,12 @@
 from jax.sharding import PartitionSpec as P
 
 adapter_alpha = 128.0
-FETCH = (1, 4, 2, 5, 6, 3, 7)
+FETCH = (1, 6, 2, 7, 4, 3, 5)
 FETCH_TIES = {}
-SEND = (1, 4, 2, 5, 6, 3, 7)
+SEND = (1, 6, 2, 7, 4, 3, 5)
 SEND_TIES = {}
 PREP_AFTER = 1
-LATE = (3, 7)
+LATE = (4, 3, 5)
 
 in_vmem = pl.BlockSpec(memory_space=pltpu.VMEM)
 in_smem = pl.BlockSpec(memory_space=pltpu.SMEM)

time: 61.7 us -> 63.1 us (1.023)
  the two profiles are of different devices: /device:TPU:11 before, /device:TPU:0 now
where the time goes in v14:
time: 63.1 us; the launch traced here: 62.9 us
  starting transfers between devices  24 us (38%)
  waiting for transfers between devices  23.3 us (37%)
  Pallas kernels  14 us (22%)
  local copies, waits for them, and re-layouts  0.81 us (1%)
  between operations  0.74 us (1%)
    ppermute x14, starting transfers between devices, exchange(): out[k] = lax.ppermute(piece, 'dp', [(i, i ^ k) for i in range(owners)])  23.9 us
    ppermute x14, waiting for transfers between devices, exchange(): out[k] = lax.ppermute(piece, 'dp', [(i, i ^ k) for i in range(owners)])  22.1 us
    pallas_call x1, Pallas kernels, with_kernels(): call(prep_kernel, [jax.ShapeDtypeStruct((owners, rows, 2 * tokens), bf16)...  5.35 us
    pallas_call x2, Pallas kernels, merge(): call(functools.partial(merge_kernel, tuple(merged), handled, others), jax...  2.83 us
    pallas_call x1, Pallas kernels, with_kernels(): call(functools.partial(input_kernel, tuple(pairs), scale), jax.ShapeDtype...  1.98 us
    pallas_call x1, Pallas kernels, with_kernels(): call(functools.partial(gather_kernel, FETCH), [straight] * partners, [in_...  1.85 us
    pallas_call x1, Pallas kernels, with_kernels(): call(functools.partial(piece_kernel, peers, scale), [straight] * owners,...  1.32 us
  transfers between devices with their start and end apart: 15, of which 8 were waited for; matrix products, arithmetic and copies ran while one was open for 0% of the time, Pallas kernels for 14%

profile of v14, /device:TPU:0, one launch (start us, length us, event | category | flops | bytes accessed | tf_op | source)
XLA Modules:
  0.0 62.9 jit_solution(12461584040555676483)
XLA Ops:
  0.7 0.8 %copy-done.2 = s32[8,1]{0,1:T(1,128)S(1)} copy-done((s32[8,1]{0,1:T(1,128)S(1)}, s32[8,1]{0,1:T(1,128)}, u32[]{:S(2)}) %copy-start.2) | copy-done | bytes 56
  1.5 1.8 %shard_map.68 = (bf16[512,128]{1,0:T(8,128)(2,1)S(1)}, bf16[512,128]{1,0:T(8,128)(2,1)S(1)}, bf16[512,128]{1,0:T(8,128)(2,1)S(1)}, bf16[512,128]{1,0:T(8,128)(2,...) custom-call(s32[8]{0:T(128)S(1)} %bitcast.7, s32[1]{0:T(128)} %bitcast.here, ...), custom_call_target="tpu_custom_call" | custom-call | bytes 2097152 | tf_op jit(solution)/shard_map/pallas_call | solution.py:208
  3.3 3.0 %collective-permute-start = (bf16[512,128]{1,0:T(8,128)(2,1)S(1)}, bf16[512,128]{1,0:T(8,128)(2,1)S(1)}, u32[]{:S(2)}, u32[]{:S(2)}) collective-permute-start(bf16[512,128]{1,0:T(8,128)(2,1)S(1)} %get-tuple-element.22), channel_id=1, source_target_pairs={{0,2},{2,0},{4,6},{6,4},{8,10},{10,8},{12,14},{14,12},{1,3},{3,1},... | collective-permute-start | bytes 393224 | tf_op jit(solution)/shard_map/ppermute | solution.py:185
  6.3 3.6 %collective-permute-start.1 = (bf16[512,128]{1,0:T(8,128)(2,1)S(1)}, bf16[512,128]{1,0:T(8,128)(2,1)S(1)}, u32[]{:S(2)}, u32[]{:S(2)}) collective-permute-start(bf16[512,128]{1,0:T(8,128)(2,1)S(1)} %get-tuple-element.25), channel_id=1, source_target_pairs={{0,12},{2,14},{4,8},{6,10},{8,4},{10,6},{12,0},{14,2},{1,13},{3,15... | collective-permute-start | bytes 393224 | tf_op jit(solution)/shard_map/ppermute | solution.py:185
  9.9 0.0 collective-permute-start.2
  9.9 0.9 %collective-permute-start.3 = (bf16[512,128]{1,0:T(8,128)(2,1)S(1)}, bf16[512,128]{1,0:T(8,128)(2,1)S(1)}, u32[]{:S(2)}, u32[]{:S(2)}) collective-permute-start(bf16[512,128]{1,0:T(8,128)(2,1)S(1)} %get-tuple-element.27), channel_id=1, source_target_pairs={{0,14},{2,12},{4,10},{6,8},{8,6},{10,4},{12,2},{14,0},{1,15},{3,13... | collective-permute-start | bytes 393224 | tf_op jit(solution)/shard_map/ppermute | solution.py:185
  10.8 2.6 %collective-permute-start.4 = (bf16[512,128]{1,0:T(8,128)(2,1)S(1)}, bf16[512,128]{1,0:T(8,128)(2,1)S(1)}, u32[]{:S(2)}, u32[]{:S(2)}) collective-permute-start(bf16[512,128]{1,0:T(8,128)(2,1)S(1)} %get-tuple-element.28), channel_id=1, source_target_pairs={{0,8},{2,10},{4,12},{6,14},{8,0},{10,2},{12,4},{14,6},{1,9},{3,11}... | collective-permute-start | bytes 393224 | tf_op jit(solution)/shard_map/ppermute | solution.py:185
  13.4 0.0 collective-permute-done.after.refs_0_
  13.4 1.8 %collective-permute-start.5 = (bf16[512,128]{1,0:T(8,128)(2,1)S(1)}, bf16[512,128]{1,0:T(8,128)(2,1)S(1)}, u32[]{:S(2)}, u32[]{:S(2)}) collective-permute-start(bf16[512,128]{1,0:T(8,128)(2,1)S(1)} %get-tuple-element.29), channel_id=1, source_target_pairs={{0,6},{2,4},{4,2},{6,0},{8,14},{10,12},{12,10},{14,8},{1,7},{3,5},... | collective-permute-start | bytes 393224 | tf_op jit(solution)/shard_map/ppermute | solution.py:185
  15.2 0.0 collective-permute-done.1.refs_1_
  15.2 2.6 %collective-permute-start.6 = (bf16[512,128]{1,0:T(8,128)(2,1)S(1)}, bf16[512,128]{1,0:T(8,128)(2,1)S(1)}, u32[]{:S(2)}, u32[]{:S(2)}) collective-permute-start(bf16[512,128]{1,0:T(8,128)(2,1)S(1)} %get-tuple-element.30), channel_id=1, source_target_pairs={{0,10},{2,8},{4,14},{6,12},{8,2},{10,0},{12,6},{14,4},{1,11},{3,9}... | collective-permute-start | bytes 393224 | tf_op jit(solution)/shard_map/ppermute | solution.py:185
  17.8 5.3 %shard_map.69 = (bf16[8,512,256]{2,1,0:T(8,128)(2,1)S(1)}, bf16[512,128]{1,0:T(8,128)(2,1)S(1)}, bf16[96,512,128]{2,1,0:T(8,128)(2,1)}) custom-call(s32[8]{0:T(128)S(1)} %bitcast.8, s32[1]{0:T(128)} %bitcast.here, bf16[96,512,128]{2,1,0:T(8,128)(2,1)} %bitcast.17, bf16[512,128]{1,0:T(8,128)(2,1)S(1)} %collective-permute-done.after.refs_0_, ...), custom_call_target="tpu_custom_call" | custom-call | bytes 16777216 | tf_op jit(solution)/shard_map/pallas_call | solution.py:220
  23.2 7.9 %collective-permute-done.4.refs_4_ = bf16[512,128]{1,0:T(8,128)(2,1)S(1)} collective-permute-done((bf16[512,128]{1,0:T(8,128)(2,1)S(1)}, bf16[512,128]{1,0:T(8,128)(2,1)S(1)}, u32[]{:S(2)}, u32[]{:S(2)}) %collective-permute-start.4) | collective-permute-done | bytes 131104 | tf_op jit(solution)/shard_map/ppermute | solution.py:185
  31.1 0.8 %collective-permute-done.6.refs_6_ = bf16[512,128]{1,0:T(8,128)(2,1)S(1)} collective-permute-done((bf16[512,128]{1,0:T(8,128)(2,1)S(1)}, bf16[512,128]{1,0:T(8,128)(2,1)S(1)}, u32[]{:S(2)}, u32[]{:S(2)}) %collective-permute-start.6) | collective-permute-done | bytes 131104 | tf_op jit(solution)/shard_map/ppermute | solution.py:185
  31.9 0.7 %shard_map.70.mine = f32[128,128]{1,0:T(8,128)S(1)} custom-call(s32[1]{0:T(128)} %bitcast.here, bf16[128,4096]{1,0:T(8,128)(2,1)S(1)} %copy-done, bf16[128,4096]{1,0:T(8,128)(2,1)S(1)} %copy-done.1, bf16[512,128]{1,0:T(8,128)(2,1)S(1)} %collective-permute-done.after.refs_0_, bf16[512,128]{1,0:T(8,128)(2,1)S(1)} %collective-permute-done.1.refs_1_, ...), custom_call_target="tpu_custom_call" | custom-call | bytes 1024 | tf_op jit(solution)/shard_map/pallas_call | solution.py:238
  32.6 0.1 collective-permute-start.7
  32.7 1.2 %collective-permute-done.7.other = f32[128,128]{1,0:T(8,128)S(1)} collective-permute-done((f32[128,128]{1,0:T(8,128)S(1)}, f32[128,128]{1,0:T(8,128)S(1)}, u32[]{:S(2)}, u32[]{:S(2)}) %collective-permute-start.7) | collective-permute-done | bytes 65568 | tf_op jit(solution)/shard_map/ppermute | solution.py:191
  34.0 1.3 %shard_map.71 = (bf16[512,128]{1,0:T(8,128)(2,1)S(1)}, bf16[512,128]{1,0:T(8,128)(2,1)S(1)}, bf16[512,128]{1,0:T(8,128)(2,1)S(1)}, bf16[512,128]{1,0:T(8,128)(2,...) custom-call(s32[1]{0:T(128)} %bitcast.here, ...), custom_call_target="tpu_custom_call" | custom-call | bytes 1024 | tf_op jit(solution)/shard_map/pallas_call | solution.py:248
  35.3 2.5 %collective-permute-start.8 = (bf16[512,128]{1,0:T(8,128)(2,1)S(1)}, bf16[512,128]{1,0:T(8,128)(2,1)S(1)}, u32[]{:S(2)}, u32[]{:S(2)}) collective-permute-start(bf16[512,128]{1,0:T(8,128)(2,1)S(1)} %get-tuple-element.32), channel_id=1, source_target_pairs={{0,2},{2,0},{4,6},{6,4},{8,10},{10,8},{12,14},{14,12},{1,3},{3,1},... | collective-permute-start | bytes 393224 | tf_op jit(solution)/shard_map/ppermute | solution.py:185
  37.8 1.6 %collective-permute-start.9 = (bf16[512,128]{1,0:T(8,128)(2,1)S(1)}, bf16[512,128]{1,0:T(8,128)(2,1)S(1)}, u32[]{:S(2)}, u32[]{:S(2)}) collective-permute-start(bf16[512,128]{1,0:T(8,128)(2,1)S(1)} %get-tuple-element.33), channel_id=1, source_target_pairs={{0,12},{2,14},{4,8},{6,10},{8,4},{10,6},{12,0},{14,2},{1,13},{3,15... | collective-permute-start | bytes 393224 | tf_op jit(solution)/shard_map/ppermute | solution.py:185
  39.3 1.8 %collective-permute-start.11 = (bf16[512,128]{1,0:T(8,128)(2,1)S(1)}, bf16[512,128]{1,0:T(8,128)(2,1)S(1)}, u32[]{:S(2)}, u32[]{:S(2)}) collective-permute-start(bf16[512,128]{1,0:T(8,128)(2,1)S(1)} %get-tuple-element.35), channel_id=1, source_target_pairs={{0,14},{2,12},{4,10},{6,8},{8,6},{10,4},{12,2},{14,0},{1,15},{3,13... | collective-permute-start | bytes 393224 | tf_op jit(solution)/shard_map/ppermute | solution.py:185
  41.1 1.7 %collective-permute-start.12 = (bf16[512,128]{1,0:T(8,128)(2,1)S(1)}, bf16[512,128]{1,0:T(8,128)(2,1)S(1)}, u32[]{:S(2)}, u32[]{:S(2)}) collective-permute-start(bf16[512,128]{1,0:T(8,128)(2,1)S(1)} %get-tuple-element.36), channel_id=1, source_target_pairs={{0,8},{2,10},{4,12},{6,14},{8,0},{10,2},{12,4},{14,6},{1,9},{3,11}... | collective-permute-start | bytes 393224 | tf_op jit(solution)/shard_map/ppermute | solution.py:185
  42.8 1.8 %collective-permute-start.13 = (bf16[512,128]{1,0:T(8,128)(2,1)S(1)}, bf16[512,128]{1,0:T(8,128)(2,1)S(1)}, u32[]{:S(2)}, u32[]{:S(2)}) collective-permute-start(bf16[512,128]{1,0:T(8,128)(2,1)S(1)} %get-tuple-element.37), channel_id=1, source_target_pairs={{0,6},{2,4},{4,2},{6,0},{8,14},{10,12},{12,10},{14,8},{1,7},{3,5},... | collective-permute-start | bytes 393224 | tf_op jit(solution)/shard_map/ppermute | solution.py:185
  44.6 1.3 %collective-permute-done.9.refs_1_ = bf16[512,128]{1,0:T(8,128)(2,1)S(1)} collective-permute-done((bf16[512,128]{1,0:T(8,128)(2,1)S(1)}, bf16[512,128]{1,0:T(8,128)(2,1)S(1)}, u32[]{:S(2)}, u32[]{:S(2)}) %collective-permute-start.9) | collective-permute-done | bytes 131104 | tf_op jit(solution)/shard_map/ppermute | solution.py:185
  46.0 0.1 collective-permute-start.14
  46.1 2.0 %shard_map.72 = bf16[128,4096]{1,0:T(8,128)(2,1)} custom-call(s32[1]{0:T(128)} %bitcast.here, s32[8]{0:T(128)S(1)} %bitcast.12, f32[128,128]{1,0:T(8,128)S(1)} %shard_map.70.mine, f32[128,128]{1,0:T(8,128)S(1)} %collective-permute-done.7.other, bf16[512,128]{1,0:T(8,128)(2,1)S(1)} %collective-permute-done.after.refs_0_, ...), custom_call_target="tpu_custom_call" | custom-call | flops 134217728 | bytes 2097152 | tf_op jit(solution)/shard_map/pallas_call | solution.py:258
  48.1 1.9 %collective-permute-done.10.refs_2_ = bf16[512,128]{1,0:T(8,128)(2,1)S(1)} collective-permute-done((bf16[512,128]{1,0:T(8,128)(2,1)S(1)}, bf16[512,128]{1,0:T(8,128)(2,1)S(1)}, u32[]{:S(2)}, u32[]{:S(2)}) %collective-permute-start.10) | collective-permute-done | bytes 131104 | tf_op jit(solution)/shard_map/ppermute | solution.py:185
  49.9 1.2 %collective-permute-done.11.refs_3_ = bf16[512,128]{1,0:T(8,128)(2,1)S(1)} collective-permute-done((bf16[512,128]{1,0:T(8,128)(2,1)S(1)}, bf16[512,128]{1,0:T(8,128)(2,1)S(1)}, u32[]{:S(2)}, u32[]{:S(2)}) %collective-permute-start.11) | collective-permute-done | bytes 131104 | tf_op jit(solution)/shard_map/ppermute | solution.py:185
  51.1 1.5 %shard_map.73.refs_8_ = bf16[96,512,128]{2,1,0:T(8,128)(2,1)} custom-call(s32[8]{0:T(128)S(1)} %bitcast.9, s32[1]{0:T(128)} %bitcast.here, s32[8]{0:T(128)S(1)} %bitcast.13, bf16[512,128]{1,0:T(8,128)(2,1)S(1)} %collective-permute-done.8.refs_0_, bf16[512,128]{1,0:T(8,128)(2,1)S(1)} %collective-permute-done.9.refs_1_, ...), custom_call_target="tpu_custom_call", output_to_operand_aliasing={{}: (8, {})} | custom-call | bytes 2097152 | tf_op jit(solution)/shard_map/pallas_call | solution.py:271
  52.6 6.6 %collective-permute-done.12.refs_4_ = bf16[512,128]{1,0:T(8,128)(2,1)S(1)} collective-permute-done((bf16[512,128]{1,0:T(8,128)(2,1)S(1)}, bf16[512,128]{1,0:T(8,128)(2,1)S(1)}, u32[]{:S(2)}, u32[]{:S(2)}) %collective-permute-start.12) | collective-permute-done | bytes 131104 | tf_op jit(solution)/shard_map/ppermute | solution.py:185
  59.2 2.4 %collective-permute-done.14.refs_6_ = bf16[512,128]{1,0:T(8,128)(2,1)S(1)} collective-permute-done((bf16[512,128]{1,0:T(8,128)(2,1)S(1)}, bf16[512,128]{1,0:T(8,128)(2,1)S(1)}, u32[]{:S(2)}, u32[]{:S(2)}) %collective-permute-start.14) | collective-permute-done | bytes 131104 | tf_op jit(solution)/shard_map/ppermute | solution.py:185
  61.5 1.4 %shard_map.74 = bf16[96,512,128]{2,1,0:T(8,128)(2,1)} custom-call(s32[8]{0:T(128)S(1)} %bitcast.10, s32[1]{0:T(128)} %bitcast.here, s32[8]{0:T(128)S(1)} %bitcast.14, bf16[512,128]{1,0:T(8,128)(2,1)S(1)} %collective-permute-done.8.refs_0_, bf16[512,128]{1,0:T(8,128)(2,1)S(1)} %collective-permute-done.9.refs_1_, ...), custom_call_target="tpu_custom_call", output_to_operand_aliasing={{}: (11, {})} | custom-call | bytes 2097152 | tf_op jit(solution)/shard_map/pallas_call | solution.py:271
  (13 shorter events, 0.0 us)
Async XLA Ops:
  0.6 17.2 %copy-start.1 = (bf16[128,4096]{1,0:T(8,128)(2,1)S(1)}, bf16[128,4096]{1,0:T(8,128)(2,1)}, u32[]{:S(2)}) copy-start(bf16[128,4096]{1,0:T(8,128)(2,1)} %y.3) | copy-start | bytes 3145732
  0.6 17.2 %copy-start = (bf16[128,4096]{1,0:T(8,128)(2,1)S(1)}, bf16[128,4096]{1,0:T(8,128)(2,1)}, u32[]{:S(2)}) copy-start(bf16[128,4096]{1,0:T(8,128)(2,1)} %x.2) | copy-start | bytes 3145732
  0.7 0.8 %copy-start.2 = (s32[8,1]{0,1:T(1,128)S(1)}, s32[8,1]{0,1:T(1,128)}, u32[]{:S(2)}) copy-start(s32[8,1]{0,1:T(1,128)} %param.8) | copy-start | bytes 100
  1.5 32.5 %copy-start.3 = (s32[8,1]{0,1:T(1,128)S(1)}, s32[8,1]{0,1:T(1,128)}, u32[]{:S(2)}) copy-start(s32[8,1]{0,1:T(1,128)} %param.9) | copy-start | bytes 100
  3.3 10.1 %collective-permute-start = (bf16[512,128]{1,0:T(8,128)(2,1)S(1)}, bf16[512,128]{1,0:T(8,128)(2,1)S(1)}, u32[]{:S(2)}, u32[]{:S(2)}) collective-permute-start(bf16[512,128]{1,0:T(8,128)(2,1)S(1)} %get-tuple-element.22), channel_id=1, source_target_pairs={{0,2},{2,0},{4,6},{6,4},{8,10},{10,8},{12,14},{14,12},{1,3},{3,1},... | collective-permute-start | bytes 393224 | tf_op jit(solution)/shard_map/ppermute | solution.py:185
  6.3 8.9 %collective-permute-start.1 = (bf16[512,128]{1,0:T(8,128)(2,1)S(1)}, bf16[512,128]{1,0:T(8,128)(2,1)S(1)}, u32[]{:S(2)}, u32[]{:S(2)}) collective-permute-start(bf16[512,128]{1,0:T(8,128)(2,1)S(1)} %get-tuple-element.25), channel_id=1, source_target_pairs={{0,12},{2,14},{4,8},{6,10},{8,4},{10,6},{12,0},{14,2},{1,13},{3,15... | collective-permute-start | bytes 393224 | tf_op jit(solution)/shard_map/ppermute | solution.py:185
  9.9 13.2 %collective-permute-start.2 = (bf16[512,128]{1,0:T(8,128)(2,1)S(1)}, bf16[512,128]{1,0:T(8,128)(2,1)S(1)}, u32[]{:S(2)}, u32[]{:S(2)}) collective-permute-start(bf16[512,128]{1,0:T(8,128)(2,1)S(1)} %get-tuple-element.26), channel_id=1, source_target_pairs={{0,4},{2,6},{4,0},{6,2},{8,12},{10,14},{12,8},{14,10},{1,5},{3,7},... | collective-permute-start | bytes 393224 | tf_op jit(solution)/shard_map/ppermute | solution.py:185
  9.9 13.2 %collective-permute-start.3 = (bf16[512,128]{1,0:T(8,128)(2,1)S(1)}, bf16[512,128]{1,0:T(8,128)(2,1)S(1)}, u32[]{:S(2)}, u32[]{:S(2)}) collective-permute-start(bf16[512,128]{1,0:T(8,128)(2,1)S(1)} %get-tuple-element.27), channel_id=1, source_target_pairs={{0,14},{2,12},{4,10},{6,8},{8,6},{10,4},{12,2},{14,0},{1,15},{3,13... | collective-permute-start | bytes 393224 | tf_op jit(solution)/shard_map/ppermute | solution.py:185
  10.8 20.3 %collective-permute-start.4 = (bf16[512,128]{1,0:T(8,128)(2,1)S(1)}, bf16[512,128]{1,0:T(8,128)(2,1)S(1)}, u32[]{:S(2)}, u32[]{:S(2)}) collective-permute-start(bf16[512,128]{1,0:T(8,128)(2,1)S(1)} %get-tuple-element.28), channel_id=1, source_target_pairs={{0,8},{2,10},{4,12},{6,14},{8,0},{10,2},{12,4},{14,6},{1,9},{3,11}... | collective-permute-start | bytes 393224 | tf_op jit(solution)/shard_map/ppermute | solution.py:185
  13.4 17.7 %collective-permute-start.5 = (bf16[512,128]{1,0:T(8,128)(2,1)S(1)}, bf16[512,128]{1,0:T(8,128)(2,1)S(1)}, u32[]{:S(2)}, u32[]{:S(2)}) collective-permute-start(bf16[512,128]{1,0:T(8,128)(2,1)S(1)} %get-tuple-element.29), channel_id=1, source_target_pairs={{0,6},{2,4},{4,2},{6,0},{8,14},{10,12},{12,10},{14,8},{1,7},{3,5},... | collective-permute-start | bytes 393224 | tf_op jit(solution)/shard_map/ppermute | solution.py:185
  15.2 16.7 %collective-permute-start.6 = (bf16[512,128]{1,0:T(8,128)(2,1)S(1)}, bf16[512,128]{1,0:T(8,128)(2,1)S(1)}, u32[]{:S(2)}, u32[]{:S(2)}) collective-permute-start(bf16[512,128]{1,0:T(8,128)(2,1)S(1)} %get-tuple-element.30), channel_id=1, source_target_pairs={{0,10},{2,8},{4,14},{6,12},{8,2},{10,0},{12,6},{14,4},{1,11},{3,9}... | collective-permute-start | bytes 393224 | tf_op jit(solution)/shard_map/ppermute | solution.py:185
  32.6 1.3 %collective-permute-start.7 = (f32[128,128]{1,0:T(8,128)S(1)}, f32[128,128]{1,0:T(8,128)S(1)}, u32[]{:S(2)}, u32[]{:S(2)}) collective-permute-start(f32[128,128]{1,0:T(8,128)S(1)} %shard_map.70.mine), channel_id=1, source_target_pairs={{0,1},{1,0},{2,3},{3,2},{4,5},{5,4},{6,7},{7,6},{8,9},{9,8},{10,11... | collective-permute-start | bytes 196616 | tf_op jit(solution)/shard_map/ppermute | solution.py:191
  35.3 7.5 %collective-permute-start.8 = (bf16[512,128]{1,0:T(8,128)(2,1)S(1)}, bf16[512,128]{1,0:T(8,128)(2,1)S(1)}, u32[]{:S(2)}, u32[]{:S(2)}) collective-permute-start(bf16[512,128]{1,0:T(8,128)(2,1)S(1)} %get-tuple-element.32), channel_id=1, source_target_pairs={{0,2},{2,0},{4,6},{6,4},{8,10},{10,8},{12,14},{14,12},{1,3},{3,1},... | collective-permute-start | bytes 393224 | tf_op jit(solution)/shard_map/ppermute | solution.py:185
  37.8 8.2 %collective-permute-start.9 = (bf16[512,128]{1,0:T(8,128)(2,1)S(1)}, bf16[512,128]{1,0:T(8,128)(2,1)S(1)}, u32[]{:S(2)}, u32[]{:S(2)}) collective-permute-start(bf16[512,128]{1,0:T(8,128)(2,1)S(1)} %get-tuple-element.33), channel_id=1, source_target_pairs={{0,12},{2,14},{4,8},{6,10},{8,4},{10,6},{12,0},{14,2},{1,13},{3,15... | collective-permute-start | bytes 393224 | tf_op jit(solution)/shard_map/ppermute | solution.py:185
  39.3 10.6 %collective-permute-start.10 = (bf16[512,128]{1,0:T(8,128)(2,1)S(1)}, bf16[512,128]{1,0:T(8,128)(2,1)S(1)}, u32[]{:S(2)}, u32[]{:S(2)}) collective-permute-start(bf16[512,128]{1,0:T(8,128)(2,1)S(1)} %get-tuple-element.34), channel_id=1, source_target_pairs={{0,4},{2,6},{4,0},{6,2},{8,12},{10,14},{12,8},{14,10},{1,5},{3,7},... | collective-permute-start | bytes 393224 | tf_op jit(solution)/shard_map/ppermute | solution.py:185
  39.3 11.8 %collective-permute-start.11 = (bf16[512,128]{1,0:T(8,128)(2,1)S(1)}, bf16[512,128]{1,0:T(8,128)(2,1)S(1)}, u32[]{:S(2)}, u32[]{:S(2)}) collective-permute-start(bf16[512,128]{1,0:T(8,128)(2,1)S(1)} %get-tuple-element.35), channel_id=1, source_target_pairs={{0,14},{2,12},{4,10},{6,8},{8,6},{10,4},{12,2},{14,0},{1,15},{3,13... | collective-permute-start | bytes 393224 | tf_op jit(solution)/shard_map/ppermute | solution.py:185
  41.1 18.1 %collective-permute-start.12 = (bf16[512,128]{1,0:T(8,128)(2,1)S(1)}, bf16[512,128]{1,0:T(8,128)(2,1)S(1)}, u32[]{:S(2)}, u32[]{:S(2)}) collective-permute-start(bf16[512,128]{1,0:T(8,128)(2,1)S(1)} %get-tuple-element.36), channel_id=1, source_target_pairs={{0,8},{2,10},{4,12},{6,14},{8,0},{10,2},{12,4},{14,6},{1,9},{3,11}... | collective-permute-start | bytes 393224 | tf_op jit(solution)/shard_map/ppermute | solution.py:185
  42.8 16.4 %collective-permute-start.13 = (bf16[512,128]{1,0:T(8,128)(2,1)S(1)}, bf16[512,128]{1,0:T(8,128)(2,1)S(1)}, u32[]{:S(2)}, u32[]{:S(2)}) collective-permute-start(bf16[512,128]{1,0:T(8,128)(2,1)S(1)} %get-tuple-element.37), channel_id=1, source_target_pairs={{0,6},{2,4},{4,2},{6,0},{8,14},{10,12},{12,10},{14,8},{1,7},{3,5},... | collective-permute-start | bytes 393224 | tf_op jit(solution)/shard_map/ppermute | solution.py:185
  46.0 15.6 %collective-permute-start.14 = (bf16[512,128]{1,0:T(8,128)(2,1)S(1)}, bf16[512,128]{1,0:T(8,128)(2,1)S(1)}, u32[]{:S(2)}, u32[]{:S(2)}) collective-permute-start(bf16[512,128]{1,0:T(8,128)(2,1)S(1)} %get-tuple-element.38), channel_id=1, source_target_pairs={{0,10},{2,8},{4,14},{6,12},{8,2},{10,0},{12,6},{14,4},{1,11},{3,9}... | collective-permute-start | bytes 393224 | tf_op jit(solution)/shard_map/ppermute | solution.py:185

commit v15 on v13

--- a/solution.py
+++ b/solution.py
@@ -13,7 +13,9 @@
 SEND = (1, 4, 2, 5, 6, 3, 7)
 SEND_TIES = {}
 PREP_AFTER = 1
-LATE = (3, 7)
+LATE = (6, 3, 7)
+RANK_LAST = (3, 7)
+SEND_FIRST = 2
 
 in_vmem = pl.BlockSpec(memory_space=pltpu.VMEM)
 in_smem = pl.BlockSpec(memory_space=pltpu.SMEM)
@@ -73,12 +75,12 @@
         copy.wait()
 
 
-def rank_kernel(peers, here, x, y, *refs):
+def rank_kernel(peers, here, x, y, so_far, *refs):
     pairs, out = refs[: len(peers)], refs[len(peers)]
     rows, width = pairs[0].shape
     tokens = x.shape[0]
-    x_rank = jnp.zeros((tokens, width), jnp.float32)
-    y_rank = jnp.zeros((tokens, width), jnp.float32)
+    x_rank = so_far[...]
+    y_rank = x_rank
     for n, k in enumerate(peers):
         columns = pl.ds(pl.multiple_of((here[0] ^ k) * rows, rows), rows)
         x_rank += jnp.dot(x[:, columns], pairs[n][...], preferred_element_type=jnp.float32)
@@ -235,23 +237,27 @@
     )(ids, here, table, pairs[PREP_AFTER], activations, cotangent)
     pairs[0] = own
 
-    mine = call(
-        functools.partial(rank_kernel, tuple(pairs)),
-        jax.ShapeDtypeStruct((tokens, width), f32),
-        [in_smem] + [in_vmem] * (2 + owners),
-        in_vmem,
-        moved=1024,
-    )(here, lax.optimization_barrier((activations, turned))[0], cotangent, *pairs.values())
+    mine = jnp.zeros((tokens, width), f32)
+    for part in ([k for k in pairs if k not in RANK_LAST], RANK_LAST):
+        mine = call(
+            functools.partial(rank_kernel, tuple(part)),
+            jax.ShapeDtypeStruct((tokens, width), f32),
+            [in_smem] + [in_vmem] * (3 + len(part)),
+            in_vmem,
+            moved=1024,
+        )(here, lax.optimization_barrier((activations, turned))[0], cotangent, mine, *[pairs[k] for k in part])
     other = across_cores(mine)
 
     peers = (*SEND, 0)
-    pieces = call(
-        functools.partial(piece_kernel, peers, scale),
-        [straight] * owners,
-        [in_smem] * 2 + [in_vmem] * 3,
-        [in_vmem] * owners,
-        moved=1024,
-    )(here, lengths, mine, other, turned)
+    pieces = []
+    for part in (peers[:SEND_FIRST], peers[SEND_FIRST:]):
+        pieces += call(
+            functools.partial(piece_kernel, part, scale),
+            [straight] * len(part),
+            [in_smem] * 2 + [in_vmem] * 3,
+            [in_vmem] * len(part),
+            moved=1024,
+        )(here, lengths, mine, other, turned)
     arrived = exchange(dict(zip(SEND, pieces)), SEND_TIES)
     arrived[0] = pieces[-1]
 

time: 61.7 us -> 61 us (0.989)
  the two profiles are of different devices: /device:TPU:11 before, /device:TPU:0 now
where the time goes in v15:
time: 61 us; the launch traced here: 59.8 us
  starting transfers between devices  25.7 us (42%)
  waiting for transfers between devices  17.6 us (29%)
  Pallas kernels  15 us (25%)
  local copies, waits for them, and re-layouts  0.81 us (1%)
  between operations  0.8 us (1%)
    ppermute x14, starting transfers between devices, exchange(): out[k] = lax.ppermute(piece, 'dp', [(i, i ^ k) for i in range(owners)])  25.6 us
    ppermute x14, waiting for transfers between devices, exchange(): out[k] = lax.ppermute(piece, 'dp', [(i, i ^ k) for i in range(owners)])  16.3 us
    pallas_call x1, Pallas kernels, with_kernels(): call(prep_kernel, [jax.ShapeDtypeStruct((owners, rows, 2 * tokens), bf16)...  5.35 us
    pallas_call x2, Pallas kernels, merge(): call(functools.partial(merge_kernel, tuple(merged), handled, others), jax...  2.84 us
    pallas_call x2, Pallas kernels, with_kernels(): call(functools.partial(piece_kernel, part, scale), [straight] * len(part)...  2.09 us
    pallas_call x1, Pallas kernels, with_kernels(): call(functools.partial(input_kernel, tuple(pairs), scale), jax.ShapeDtype...  1.99 us
    pallas_call x1, Pallas kernels, with_kernels(): call(functools.partial(gather_kernel, FETCH), [straight] * partners, [in_...  1.85 us
    ppermute x1, waiting for transfers between devices, across_cores(): return lax.ppermute(value, 'tensor', [(i, i ^ 1) for i in range(cores)])  1.24 us
  transfers between devices with their start and end apart: 15, of which 6 were waited for; matrix products, arithmetic and copies ran while one was open for 0% of the time, Pallas kernels for 18%

profile of v15, /device:TPU:0, one launch (start us, length us, event | category | flops | bytes accessed | tf_op | source)
XLA Modules:
  0.0 59.8 jit_solution(5735767726445023531)
XLA Ops:
  0.7 0.8 %copy-done.3 = s32[8,1]{0,1:T(1,128)S(1)} copy-done((s32[8,1]{0,1:T(1,128)S(1)}, s32[8,1]{0,1:T(1,128)}, u32[]{:S(2)}) %copy-start.3) | copy-done | bytes 56
  1.5 1.8 %shard_map.68 = (bf16[512,128]{1,0:T(8,128)(2,1)S(1)}, bf16[512,128]{1,0:T(8,128)(2,1)S(1)}, bf16[512,128]{1,0:T(8,128)(2,1)S(1)}, bf16[512,128]{1,0:T(8,128)(2,...) custom-call(s32[8]{0:T(128)S(1)} %bitcast.12, s32[1]{0:T(128)} %bitcast.here, ...), custom_call_target="tpu_custom_call" | custom-call | bytes 2097152 | tf_op jit(solution)/shard_map/pallas_call | solution.py:210
  3.3 0.0 copy-start.2
  3.3 3.0 %collective-permute-start = (bf16[512,128]{1,0:T(8,128)(2,1)S(1)}, bf16[512,128]{1,0:T(8,128)(2,1)S(1)}, u32[]{:S(2)}, u32[]{:S(2)}) collective-permute-start(bf16[512,128]{1,0:T(8,128)(2,1)S(1)} %get-tuple-element.22), channel_id=1, source_target_pairs={{0,2},{2,0},{4,6},{6,4},{8,10},{10,8},{12,14},{14,12},{1,3},{3,1},... | collective-permute-start | bytes 393224 | tf_op jit(solution)/shard_map/ppermute | solution.py:187
  6.3 2.6 %collective-permute-start.1 = (bf16[512,128]{1,0:T(8,128)(2,1)S(1)}, bf16[512,128]{1,0:T(8,128)(2,1)S(1)}, u32[]{:S(2)}, u32[]{:S(2)}) collective-permute-start(bf16[512,128]{1,0:T(8,128)(2,1)S(1)} %get-tuple-element.25), channel_id=1, source_target_pairs={{0,8},{2,10},{4,12},{6,14},{8,0},{10,2},{12,4},{14,6},{1,9},{3,11}... | collective-permute-start | bytes 393224 | tf_op jit(solution)/shard_map/ppermute | solution.py:187
  8.9 1.6 %collective-permute-start.2 = (bf16[512,128]{1,0:T(8,128)(2,1)S(1)}, bf16[512,128]{1,0:T(8,128)(2,1)S(1)}, u32[]{:S(2)}, u32[]{:S(2)}) collective-permute-start(bf16[512,128]{1,0:T(8,128)(2,1)S(1)} %get-tuple-element.26), channel_id=1, source_target_pairs={{0,4},{2,6},{4,0},{6,2},{8,12},{10,14},{12,8},{14,10},{1,5},{3,7},... | collective-permute-start | bytes 393224 | tf_op jit(solution)/shard_map/ppermute | solution.py:187
  10.5 0.3 collective-permute-start.3
  10.8 2.5 %collective-permute-start.4 = (bf16[512,128]{1,0:T(8,128)(2,1)S(1)}, bf16[512,128]{1,0:T(8,128)(2,1)S(1)}, u32[]{:S(2)}, u32[]{:S(2)}) collective-permute-start(bf16[512,128]{1,0:T(8,128)(2,1)S(1)} %get-tuple-element.28), channel_id=1, source_target_pairs={{0,12},{2,14},{4,8},{6,10},{8,4},{10,6},{12,0},{14,2},{1,13},{3,15... | collective-permute-start | bytes 393224 | tf_op jit(solution)/shard_map/ppermute | solution.py:187
  13.3 0.0 collective-permute-done.after.refs_0_
  13.3 1.6 %collective-permute-start.5 = (bf16[512,128]{1,0:T(8,128)(2,1)S(1)}, bf16[512,128]{1,0:T(8,128)(2,1)S(1)}, u32[]{:S(2)}, u32[]{:S(2)}) collective-permute-start(bf16[512,128]{1,0:T(8,128)(2,1)S(1)} %get-tuple-element.30), channel_id=1, source_target_pairs={{0,6},{2,4},{4,2},{6,0},{8,14},{10,12},{12,10},{14,8},{1,7},{3,5},... | collective-permute-start | bytes 393224 | tf_op jit(solution)/shard_map/ppermute | solution.py:187
  14.9 5.6 %collective-permute-done.1.refs_1_ = bf16[512,128]{1,0:T(8,128)(2,1)S(1)} collective-permute-done((bf16[512,128]{1,0:T(8,128)(2,1)S(1)}, bf16[512,128]{1,0:T(8,128)(2,1)S(1)}, u32[]{:S(2)}, u32[]{:S(2)}) %collective-permute-start.1) | collective-permute-done | bytes 131104 | tf_op jit(solution)/shard_map/ppermute | solution.py:187
  20.4 2.3 %collective-permute-start.6 = (bf16[512,128]{1,0:T(8,128)(2,1)S(1)}, bf16[512,128]{1,0:T(8,128)(2,1)S(1)}, u32[]{:S(2)}, u32[]{:S(2)}) collective-permute-start(bf16[512,128]{1,0:T(8,128)(2,1)S(1)} %get-tuple-element.31), channel_id=1, source_target_pairs={{0,14},{2,12},{4,10},{6,8},{8,6},{10,4},{12,2},{14,0},{1,15},{3,13... | collective-permute-start | bytes 393224 | tf_op jit(solution)/shard_map/ppermute | solution.py:187
  22.8 5.3 %shard_map.69 = (bf16[8,512,256]{2,1,0:T(8,128)(2,1)S(1)}, bf16[512,128]{1,0:T(8,128)(2,1)S(1)}, bf16[96,512,128]{2,1,0:T(8,128)(2,1)}) custom-call(s32[8]{0:T(128)S(1)} %bitcast.13, s32[1]{0:T(128)} %bitcast.here, bf16[96,512,128]{2,1,0:T(8,128)(2,1)} %bitcast.18, bf16[512,128]{1,0:T(8,128)(2,1)S(1)} %collective-permute-done.after.refs_0_, ...), custom_call_target="tpu_custom_call" | custom-call | bytes 16777216 | tf_op jit(solution)/shard_map/pallas_call | solution.py:222
  28.2 0.6 shard_map.70.so_far
  28.8 0.3 shard_map.71.mine
  29.1 0.1 collective-permute-start.7
  29.2 1.2 %collective-permute-done.7.other = f32[128,128]{1,0:T(8,128)S(1)} collective-permute-done((f32[128,128]{1,0:T(8,128)S(1)}, f32[128,128]{1,0:T(8,128)S(1)}, u32[]{:S(2)}, u32[]{:S(2)}) %collective-permute-start.7) | collective-permute-done | bytes 65568 | tf_op jit(solution)/shard_map/ppermute | solution.py:193
  30.4 0.9 %shard_map.72 = (bf16[512,128]{1,0:T(8,128)(2,1)S(1)}, bf16[512,128]{1,0:T(8,128)(2,1)S(1)}) custom-call(s32[1]{0:T(128)} %bitcast.here, s32[8]{0:T(128)S(1)} %bitcast.7, f32[128,128]{1,0:T(8,128)S(1)} %shard_map.71.mine, f32[128,128]{1,0:T(8,128)S(1)} %collective-permute-done.7.other, bf16[8,512,256]{2,1,0:T(8,128)(2,1)S(1)} %get-tuple-element.23.turned), custom_call_target="tpu_custom_call" | custom-call | bytes 1024 | tf_op jit(solution)/shard_map/pallas_call | solution.py:254
  31.3 1.6 %collective-permute-start.8 = (bf16[512,128]{1,0:T(8,128)(2,1)S(1)}, bf16[512,128]{1,0:T(8,128)(2,1)S(1)}, u32[]{:S(2)}, u32[]{:S(2)}) collective-permute-start(bf16[512,128]{1,0:T(8,128)(2,1)S(1)} %get-tuple-element.32), channel_id=1, source_target_pairs={{0,2},{2,0},{4,6},{6,4},{8,10},{10,8},{12,14},{14,12},{1,3},{3,1},... | collective-permute-start | bytes 393224 | tf_op jit(solution)/shard_map/ppermute | solution.py:187
  32.9 5.6 %collective-permute-start.9 = (bf16[512,128]{1,0:T(8,128)(2,1)S(1)}, bf16[512,128]{1,0:T(8,128)(2,1)S(1)}, u32[]{:S(2)}, u32[]{:S(2)}) collective-permute-start(bf16[512,128]{1,0:T(8,128)(2,1)S(1)} %get-tuple-element.33), channel_id=1, source_target_pairs={{0,8},{2,10},{4,12},{6,14},{8,0},{10,2},{12,4},{14,6},{1,9},{3,11}... | collective-permute-start | bytes 393224 | tf_op jit(solution)/shard_map/ppermute | solution.py:187
  38.5 1.2 %shard_map.73 = (bf16[512,128]{1,0:T(8,128)(2,1)S(1)}, bf16[512,128]{1,0:T(8,128)(2,1)S(1)}, bf16[512,128]{1,0:T(8,128)(2,1)S(1)}, bf16[512,128]{1,0:T(8,128)(2,...) custom-call(s32[1]{0:T(128)} %bitcast.here, s32[8]{0:T(128)S(1)} %bitcast.8, ...), custom_call_target="tpu_custom_call" | custom-call | bytes 1024 | tf_op jit(solution)/shard_map/pallas_call | solution.py:254
  39.7 0.1 collective-permute-start.10
  39.8 1.0 %collective-permute-start.11 = (bf16[512,128]{1,0:T(8,128)(2,1)S(1)}, bf16[512,128]{1,0:T(8,128)(2,1)S(1)}, u32[]{:S(2)}, u32[]{:S(2)}) collective-permute-start(bf16[512,128]{1,0:T(8,128)(2,1)S(1)} %get-tuple-element.35), channel_id=1, source_target_pairs={{0,10},{2,8},{4,14},{6,12},{8,2},{10,0},{12,6},{14,4},{1,11},{3,9}... | collective-permute-start | bytes 393224 | tf_op jit(solution)/shard_map/ppermute | solution.py:187
  40.7 3.4 %collective-permute-start.12 = (bf16[512,128]{1,0:T(8,128)(2,1)S(1)}, bf16[512,128]{1,0:T(8,128)(2,1)S(1)}, u32[]{:S(2)}, u32[]{:S(2)}) collective-permute-start(bf16[512,128]{1,0:T(8,128)(2,1)S(1)} %get-tuple-element.36), channel_id=1, source_target_pairs={{0,12},{2,14},{4,8},{6,10},{8,4},{10,6},{12,0},{14,2},{1,13},{3,15... | collective-permute-start | bytes 393224 | tf_op jit(solution)/shard_map/ppermute | solution.py:187
  44.1 0.1 collective-permute-start.13
  44.2 1.5 %collective-permute-done.9.refs_1_ = bf16[512,128]{1,0:T(8,128)(2,1)S(1)} collective-permute-done((bf16[512,128]{1,0:T(8,128)(2,1)S(1)}, bf16[512,128]{1,0:T(8,128)(2,1)S(1)}, u32[]{:S(2)}, u32[]{:S(2)}) %collective-permute-start.9) | collective-permute-done | bytes 131104 | tf_op jit(solution)/shard_map/ppermute | solution.py:187
  45.7 2.0 %shard_map.74 = bf16[128,4096]{1,0:T(8,128)(2,1)} custom-call(s32[1]{0:T(128)} %bitcast.here, s32[8]{0:T(128)S(1)} %bitcast.9, f32[128,128]{1,0:T(8,128)S(1)} %shard_map.71.mine, f32[128,128]{1,0:T(8,128)S(1)} %collective-permute-done.7.other, bf16[512,128]{1,0:T(8,128)(2,1)S(1)} %collective-permute-done.after.refs_0_, ...), custom_call_target="tpu_custom_call" | custom-call | flops 134217728 | bytes 2097152 | tf_op jit(solution)/shard_map/pallas_call | solution.py:264
  47.7 1.0 %collective-permute-done.10.refs_2_ = bf16[512,128]{1,0:T(8,128)(2,1)S(1)} collective-permute-done((bf16[512,128]{1,0:T(8,128)(2,1)S(1)}, bf16[512,128]{1,0:T(8,128)(2,1)S(1)}, u32[]{:S(2)}, u32[]{:S(2)}) %collective-permute-start.10) | collective-permute-done | bytes 131104 | tf_op jit(solution)/shard_map/ppermute | solution.py:187
  48.7 7.6 %collective-permute-done.11.refs_3_ = bf16[512,128]{1,0:T(8,128)(2,1)S(1)} collective-permute-done((bf16[512,128]{1,0:T(8,128)(2,1)S(1)}, bf16[512,128]{1,0:T(8,128)(2,1)S(1)}, u32[]{:S(2)}, u32[]{:S(2)}) %collective-permute-start.11) | collective-permute-done | bytes 131104 | tf_op jit(solution)/shard_map/ppermute | solution.py:187
  56.4 1.4 %shard_map.75.refs_8_ = bf16[96,512,128]{2,1,0:T(8,128)(2,1)} custom-call(s32[8]{0:T(128)S(1)} %bitcast.14, s32[1]{0:T(128)} %bitcast.here, s32[8]{0:T(128)S(1)} %bitcast.10, bf16[512,128]{1,0:T(8,128)(2,1)S(1)} %collective-permute-done.8.refs_0_, bf16[512,128]{1,0:T(8,128)(2,1)S(1)} %collective-permute-done.9.refs_1_, ...), custom_call_target="tpu_custom_call", output_to_operand_aliasing={{}: (8, {})} | custom-call | bytes 2097152 | tf_op jit(solution)/shard_map/pallas_call | solution.py:277
  57.8 0.6 collective-permute-done.13.refs_5_
  58.4 1.4 %shard_map.76 = bf16[96,512,128]{2,1,0:T(8,128)(2,1)} custom-call(s32[8]{0:T(128)S(1)} %bitcast.15, s32[1]{0:T(128)} %bitcast.here, s32[8]{0:T(128)S(1)} %bitcast.11, bf16[512,128]{1,0:T(8,128)(2,1)S(1)} %collective-permute-done.8.refs_0_, bf16[512,128]{1,0:T(8,128)(2,1)S(1)} %collective-permute-done.9.refs_1_, ...), custom_call_target="tpu_custom_call", output_to_operand_aliasing={{}: (11, {})} | custom-call | bytes 2097152 | tf_op jit(solution)/shard_map/pallas_call | solution.py:277
  (16 shorter events, 0.0 us)
Async XLA Ops:
  0.6 22.2 %copy-start.1 = (bf16[128,4096]{1,0:T(8,128)(2,1)S(1)}, bf16[128,4096]{1,0:T(8,128)(2,1)}, u32[]{:S(2)}) copy-start(bf16[128,4096]{1,0:T(8,128)(2,1)} %y.5) | copy-start | bytes 3145732
  0.6 22.2 %copy-start = (bf16[128,4096]{1,0:T(8,128)(2,1)S(1)}, bf16[128,4096]{1,0:T(8,128)(2,1)}, u32[]{:S(2)}) copy-start(bf16[128,4096]{1,0:T(8,128)(2,1)} %x.3) | copy-start | bytes 3145732
  0.7 0.8 %copy-start.3 = (s32[8,1]{0,1:T(1,128)S(1)}, s32[8,1]{0,1:T(1,128)}, u32[]{:S(2)}) copy-start(s32[8,1]{0,1:T(1,128)} %param.8) | copy-start | bytes 100
  3.3 27.1 %copy-start.2 = (s32[8,1]{0,1:T(1,128)S(1)}, s32[8,1]{0,1:T(1,128)}, u32[]{:S(2)}) copy-start(s32[8,1]{0,1:T(1,128)} %param.9) | copy-start | bytes 100
  3.3 10.0 %collective-permute-start = (bf16[512,128]{1,0:T(8,128)(2,1)S(1)}, bf16[512,128]{1,0:T(8,128)(2,1)S(1)}, u32[]{:S(2)}, u32[]{:S(2)}) collective-permute-start(bf16[512,128]{1,0:T(8,128)(2,1)S(1)} %get-tuple-element.22), channel_id=1, source_target_pairs={{0,2},{2,0},{4,6},{6,4},{8,10},{10,8},{12,14},{14,12},{1,3},{3,1},... | collective-permute-start | bytes 393224 | tf_op jit(solution)/shard_map/ppermute | solution.py:187
  6.3 14.1 %collective-permute-start.1 = (bf16[512,128]{1,0:T(8,128)(2,1)S(1)}, bf16[512,128]{1,0:T(8,128)(2,1)S(1)}, u32[]{:S(2)}, u32[]{:S(2)}) collective-permute-start(bf16[512,128]{1,0:T(8,128)(2,1)S(1)} %get-tuple-element.25), channel_id=1, source_target_pairs={{0,8},{2,10},{4,12},{6,14},{8,0},{10,2},{12,4},{14,6},{1,9},{3,11}... | collective-permute-start | bytes 393224 | tf_op jit(solution)/shard_map/ppermute | solution.py:187
  8.9 19.2 %collective-permute-start.2 = (bf16[512,128]{1,0:T(8,128)(2,1)S(1)}, bf16[512,128]{1,0:T(8,128)(2,1)S(1)}, u32[]{:S(2)}, u32[]{:S(2)}) collective-permute-start(bf16[512,128]{1,0:T(8,128)(2,1)S(1)} %get-tuple-element.26), channel_id=1, source_target_pairs={{0,4},{2,6},{4,0},{6,2},{8,12},{10,14},{12,8},{14,10},{1,5},{3,7},... | collective-permute-start | bytes 393224 | tf_op jit(solution)/shard_map/ppermute | solution.py:187
  10.5 17.7 %collective-permute-start.3 = (bf16[512,128]{1,0:T(8,128)(2,1)S(1)}, bf16[512,128]{1,0:T(8,128)(2,1)S(1)}, u32[]{:S(2)}, u32[]{:S(2)}) collective-permute-start(bf16[512,128]{1,0:T(8,128)(2,1)S(1)} %get-tuple-element.27), channel_id=1, source_target_pairs={{0,10},{2,8},{4,14},{6,12},{8,2},{10,0},{12,6},{14,4},{1,11},{3,9}... | collective-permute-start | bytes 393224 | tf_op jit(solution)/shard_map/ppermute | solution.py:187
  10.8 17.4 %collective-permute-start.4 = (bf16[512,128]{1,0:T(8,128)(2,1)S(1)}, bf16[512,128]{1,0:T(8,128)(2,1)S(1)}, u32[]{:S(2)}, u32[]{:S(2)}) collective-permute-start(bf16[512,128]{1,0:T(8,128)(2,1)S(1)} %get-tuple-element.28), channel_id=1, source_target_pairs={{0,12},{2,14},{4,8},{6,10},{8,4},{10,6},{12,0},{14,2},{1,13},{3,15... | collective-permute-start | bytes 393224 | tf_op jit(solution)/shard_map/ppermute | solution.py:187
  13.3 15.5 %collective-permute-start.5 = (bf16[512,128]{1,0:T(8,128)(2,1)S(1)}, bf16[512,128]{1,0:T(8,128)(2,1)S(1)}, u32[]{:S(2)}, u32[]{:S(2)}) collective-permute-start(bf16[512,128]{1,0:T(8,128)(2,1)S(1)} %get-tuple-element.30), channel_id=1, source_target_pairs={{0,6},{2,4},{4,2},{6,0},{8,14},{10,12},{12,10},{14,8},{1,7},{3,5},... | collective-permute-start | bytes 393224 | tf_op jit(solution)/shard_map/ppermute | solution.py:187
  20.4 8.3 %collective-permute-start.6 = (bf16[512,128]{1,0:T(8,128)(2,1)S(1)}, bf16[512,128]{1,0:T(8,128)(2,1)S(1)}, u32[]{:S(2)}, u32[]{:S(2)}) collective-permute-start(bf16[512,128]{1,0:T(8,128)(2,1)S(1)} %get-tuple-element.31), channel_id=1, source_target_pairs={{0,14},{2,12},{4,10},{6,8},{8,6},{10,4},{12,2},{14,0},{1,15},{3,13... | collective-permute-start | bytes 393224 | tf_op jit(solution)/shard_map/ppermute | solution.py:187
  29.1 1.3 %collective-permute-start.7 = (f32[128,128]{1,0:T(8,128)S(1)}, f32[128,128]{1,0:T(8,128)S(1)}, u32[]{:S(2)}, u32[]{:S(2)}) collective-permute-start(f32[128,128]{1,0:T(8,128)S(1)} %shard_map.71.mine), channel_id=1, source_target_pairs={{0,1},{1,0},{2,3},{3,2},{4,5},{5,4},{6,7},{7,6},{8,9},{9,8},{10,11... | collective-permute-start | bytes 196616 | tf_op jit(solution)/shard_map/ppermute | solution.py:193
  31.3 12.8 %collective-permute-start.8 = (bf16[512,128]{1,0:T(8,128)(2,1)S(1)}, bf16[512,128]{1,0:T(8,128)(2,1)S(1)}, u32[]{:S(2)}, u32[]{:S(2)}) collective-permute-start(bf16[512,128]{1,0:T(8,128)(2,1)S(1)} %get-tuple-element.32), channel_id=1, source_target_pairs={{0,2},{2,0},{4,6},{6,4},{8,10},{10,8},{12,14},{14,12},{1,3},{3,1},... | collective-permute-start | bytes 393224 | tf_op jit(solution)/shard_map/ppermute | solution.py:187
  32.9 12.8 %collective-permute-start.9 = (bf16[512,128]{1,0:T(8,128)(2,1)S(1)}, bf16[512,128]{1,0:T(8,128)(2,1)S(1)}, u32[]{:S(2)}, u32[]{:S(2)}) collective-permute-start(bf16[512,128]{1,0:T(8,128)(2,1)S(1)} %get-tuple-element.33), channel_id=1, source_target_pairs={{0,8},{2,10},{4,12},{6,14},{8,0},{10,2},{12,4},{14,6},{1,9},{3,11}... | collective-permute-start | bytes 393224 | tf_op jit(solution)/shard_map/ppermute | solution.py:187
  39.7 9.0 %collective-permute-start.10 = (bf16[512,128]{1,0:T(8,128)(2,1)S(1)}, bf16[512,128]{1,0:T(8,128)(2,1)S(1)}, u32[]{:S(2)}, u32[]{:S(2)}) collective-permute-start(bf16[512,128]{1,0:T(8,128)(2,1)S(1)} %get-tuple-element.34), channel_id=1, source_target_pairs={{0,4},{2,6},{4,0},{6,2},{8,12},{10,14},{12,8},{14,10},{1,5},{3,7},... | collective-permute-start | bytes 393224 | tf_op jit(solution)/shard_map/ppermute | solution.py:187
  39.8 16.6 %collective-permute-start.11 = (bf16[512,128]{1,0:T(8,128)(2,1)S(1)}, bf16[512,128]{1,0:T(8,128)(2,1)S(1)}, u32[]{:S(2)}, u32[]{:S(2)}) collective-permute-start(bf16[512,128]{1,0:T(8,128)(2,1)S(1)} %get-tuple-element.35), channel_id=1, source_target_pairs={{0,10},{2,8},{4,14},{6,12},{8,2},{10,0},{12,6},{14,4},{1,11},{3,9}... | collective-permute-start | bytes 393224 | tf_op jit(solution)/shard_map/ppermute | solution.py:187
  40.7 17.0 %collective-permute-start.12 = (bf16[512,128]{1,0:T(8,128)(2,1)S(1)}, bf16[512,128]{1,0:T(8,128)(2,1)S(1)}, u32[]{:S(2)}, u32[]{:S(2)}) collective-permute-start(bf16[512,128]{1,0:T(8,128)(2,1)S(1)} %get-tuple-element.36), channel_id=1, source_target_pairs={{0,12},{2,14},{4,8},{6,10},{8,4},{10,6},{12,0},{14,2},{1,13},{3,15... | collective-permute-start | bytes 393224 | tf_op jit(solution)/shard_map/ppermute | solution.py:187
  44.1 14.3 %collective-permute-start.13 = (bf16[512,128]{1,0:T(8,128)(2,1)S(1)}, bf16[512,128]{1,0:T(8,128)(2,1)S(1)}, u32[]{:S(2)}, u32[]{:S(2)}) collective-permute-start(bf16[512,128]{1,0:T(8,128)(2,1)S(1)} %get-tuple-element.37), channel_id=1, source_target_pairs={{0,6},{2,4},{4,2},{6,0},{8,14},{10,12},{12,10},{14,8},{1,7},{3,5},... | collective-permute-start | bytes 393224 | tf_op jit(solution)/shard_map/ppermute | solution.py:187
  45.7 12.7 %collective-permute-start.14 = (bf16[512,128]{1,0:T(8,128)(2,1)S(1)}, bf16[512,128]{1,0:T(8,128)(2,1)S(1)}, u32[]{:S(2)}, u32[]{:S(2)}) collective-permute-start(bf16[512,128]{1,0:T(8,128)(2,1)S(1)} %get-tuple-element.38), channel_id=1, source_target_pairs={{0,14},{2,12},{4,10},{6,8},{8,6},{10,4},{12,2},{14,0},{1,15},{3,13... | collective-permute-start | bytes 393224 | tf_op jit(solution)/shard_map/ppermute | solution.py:187

commit v16 on v15

--- a/solution.py
+++ b/solution.py
@@ -8,12 +8,12 @@
 from jax.sharding import PartitionSpec as P
 
 adapter_alpha = 128.0
-FETCH = (1, 4, 2, 5, 6, 3, 7)
-FETCH_TIES = {}
-SEND = (1, 4, 2, 5, 6, 3, 7)
-SEND_TIES = {}
+FETCH = (1, 2, 4, 5, 6, 7, 3)
+FETCH_TIES = {7: 1, 3: 2}
+SEND = (1, 2, 4, 5, 6, 7, 3)
+SEND_TIES = {7: 1, 3: 2}
 PREP_AFTER = 1
-LATE = (6, 3, 7)
+LATE = (6, 7, 3)
 RANK_LAST = (3, 7)
 SEND_FIRST = 2
 

time: 61 us -> 63.8 us (1.046)
  waiting for transfers between devices: 17.6 us -> 19.7 us
  starting transfers between devices: 25.7 us -> 26.6 us
    ppermute x14, waiting for transfers between devices: 16.3 us -> 18.4 us  [exchange(): out[k] = lax.ppermute(piece, 'dp', [(i, i ^ k) for i in range(owners)])]
    ppermute x14, starting transfers between devices: 25.6 us -> 26.5 us  [exchange(): out[k] = lax.ppermute(piece, 'dp', [(i, i ^ k) for i in range(owners)])]
  transfers between devices with their start and end apart: 15 -> 15, of which waited for: 6 -> 5; matrix products, arithmetic and copies ran while one was open for 0% -> 0% of each run, Pallas kernels for 18% -> 17%
where the time goes in v16:
time: 63.8 us; the launch traced here: 62.8 us
  starting transfers between devices  26.6 us (42%)
  waiting for transfers between devices  19.7 us (31%)
  Pallas kernels  15 us (24%)
  local copies, waits for them, and re-layouts  0.81 us (1%)
  between operations  0.79 us (1%)
    ppermute x14, starting transfers between devices, exchange(): out[k] = lax.ppermute(piece, 'dp', [(i, i ^ k) for i in range(owners)])  26.5 us
    ppermute x14, waiting for transfers between devices, exchange(): out[k] = lax.ppermute(piece, 'dp', [(i, i ^ k) for i in range(owners)])  18.4 us
    pallas_call x1, Pallas kernels, with_kernels(): call(prep_kernel, [jax.ShapeDtypeStruct((owners, rows, 2 * tokens), bf16)...  5.35 us
    pallas_call x2, Pallas kernels, merge(): call(functools.partial(merge_kernel, tuple(merged), handled, others), jax...  2.83 us
    pallas_call x2, Pallas kernels, with_kernels(): call(functools.partial(piece_kernel, part, scale), [straight] * len(part)...  2.09 us
    pallas_call x1, Pallas kernels, with_kernels(): call(functools.partial(input_kernel, tuple(pairs), scale), jax.ShapeDtype...  1.99 us
    pallas_call x1, Pallas kernels, with_kernels(): call(functools.partial(gather_kernel, FETCH), [straight] * partners, [in_...  1.85 us
  transfers between devices with their start and end apart: 15, of which 5 were waited for; matrix products, arithmetic and copies ran while one was open for 0% of the time, Pallas kernels for 17%

profile of v16, /device:TPU:0, one launch (start us, length us, event | category | flops | bytes accessed | tf_op | source)
XLA Modules:
  0.0 62.8 jit_solution(4157689247796275431)
XLA Ops:
  0.7 0.8 %copy-done.3 = s32[8,1]{0,1:T(1,128)S(1)} copy-done((s32[8,1]{0,1:T(1,128)S(1)}, s32[8,1]{0,1:T(1,128)}, u32[]{:S(2)}) %copy-start.3) | copy-done | bytes 56
  1.5 1.8 %shard_map.68 = (bf16[512,128]{1,0:T(8,128)(2,1)S(1)}, bf16[512,128]{1,0:T(8,128)(2,1)S(1)}, bf16[512,128]{1,0:T(8,128)(2,1)S(1)}, bf16[512,128]{1,0:T(8,128)(2,...) custom-call(s32[8]{0:T(128)S(1)} %bitcast.12, s32[1]{0:T(128)} %bitcast.here, ...), custom_call_target="tpu_custom_call" | custom-call | bytes 2097152 | tf_op jit(solution)/shard_map/pallas_call | solution.py:210
  3.3 0.0 copy-start.2
  3.3 3.0 %collective-permute-start = (bf16[512,128]{1,0:T(8,128)(2,1)S(1)}, bf16[512,128]{1,0:T(8,128)(2,1)S(1)}, u32[]{:S(2)}, u32[]{:S(2)}) collective-permute-start(bf16[512,128]{1,0:T(8,128)(2,1)S(1)} %get-tuple-element.26), channel_id=1, source_target_pairs={{0,2},{2,0},{4,6},{6,4},{8,10},{10,8},{12,14},{14,12},{1,3},{3,1},... | collective-permute-start | bytes 393224 | tf_op jit(solution)/shard_map/ppermute | solution.py:187
  6.3 1.6 %collective-permute-start.1 = (bf16[512,128]{1,0:T(8,128)(2,1)S(1)}, bf16[512,128]{1,0:T(8,128)(2,1)S(1)}, u32[]{:S(2)}, u32[]{:S(2)}) collective-permute-start(bf16[512,128]{1,0:T(8,128)(2,1)S(1)} %get-tuple-element.29), channel_id=1, source_target_pairs={{0,4},{2,6},{4,0},{6,2},{8,12},{10,14},{12,8},{14,10},{1,5},{3,7},... | collective-permute-start | bytes 393224 | tf_op jit(solution)/shard_map/ppermute | solution.py:187
  7.9 2.6 %collective-permute-start.2 = (bf16[512,128]{1,0:T(8,128)(2,1)S(1)}, bf16[512,128]{1,0:T(8,128)(2,1)S(1)}, u32[]{:S(2)}, u32[]{:S(2)}) collective-permute-start(bf16[512,128]{1,0:T(8,128)(2,1)S(1)} %get-tuple-element.30), channel_id=1, source_target_pairs={{0,8},{2,10},{4,12},{6,14},{8,0},{10,2},{12,4},{14,6},{1,9},{3,11}... | collective-permute-start | bytes 393224 | tf_op jit(solution)/shard_map/ppermute | solution.py:187
  10.5 0.3 collective-permute-start.3
  10.8 2.5 %collective-permute-start.4 = (bf16[512,128]{1,0:T(8,128)(2,1)S(1)}, bf16[512,128]{1,0:T(8,128)(2,1)S(1)}, u32[]{:S(2)}, u32[]{:S(2)}) collective-permute-start(bf16[512,128]{1,0:T(8,128)(2,1)S(1)} %get-tuple-element.32), channel_id=1, source_target_pairs={{0,12},{2,14},{4,8},{6,10},{8,4},{10,6},{12,0},{14,2},{1,13},{3,15... | collective-permute-start | bytes 393224 | tf_op jit(solution)/shard_map/ppermute | solution.py:187
  13.3 2.3 %collective-permute-start.6 = (bf16[512,128]{1,0:T(8,128)(2,1)S(1)}, bf16[512,128]{1,0:T(8,128)(2,1)S(1)}, u32[]{:S(2)}, u32[]{:S(2)}) collective-permute-start(bf16[512,128]{1,0:T(8,128)(2,1)S(1)} %get-tuple-element.37), channel_id=1, source_target_pairs={{0,14},{2,12},{4,10},{6,8},{8,6},{10,4},{12,2},{14,0},{1,15},{3,13... | collective-permute-start | bytes 393224 | tf_op jit(solution)/shard_map/ppermute | solution.py:187
  15.6 0.0 collective-permute-done.1.refs_1_
  15.6 0.0 collective-permute-start.5
  15.6 5.3 %shard_map.69 = (bf16[8,512,256]{2,1,0:T(8,128)(2,1)S(1)}, bf16[512,128]{1,0:T(8,128)(2,1)S(1)}, bf16[96,512,128]{2,1,0:T(8,128)(2,1)}) custom-call(s32[8]{0:T(128)S(1)} %bitcast.13, s32[1]{0:T(128)} %bitcast.here, bf16[96,512,128]{2,1,0:T(8,128)(2,1)} %bitcast.18, bf16[512,128]{1,0:T(8,128)(2,1)S(1)} %collective-permute-done.after.refs_0_, ...), custom_call_target="tpu_custom_call" | custom-call | bytes 16777216 | tf_op jit(solution)/shard_map/pallas_call | solution.py:222
  20.9 5.0 %collective-permute-done.2.refs_2_ = bf16[512,128]{1,0:T(8,128)(2,1)S(1)} collective-permute-done((bf16[512,128]{1,0:T(8,128)(2,1)S(1)}, bf16[512,128]{1,0:T(8,128)(2,1)S(1)}, u32[]{:S(2)}, u32[]{:S(2)}) %collective-permute-start.2) | collective-permute-done | bytes 131104 | tf_op jit(solution)/shard_map/ppermute | solution.py:187
  25.9 2.3 %collective-permute-done.3.refs_3_ = bf16[512,128]{1,0:T(8,128)(2,1)S(1)} collective-permute-done((bf16[512,128]{1,0:T(8,128)(2,1)S(1)}, bf16[512,128]{1,0:T(8,128)(2,1)S(1)}, u32[]{:S(2)}, u32[]{:S(2)}) %collective-permute-start.3) | collective-permute-done | bytes 131104 | tf_op jit(solution)/shard_map/ppermute | solution.py:187
  28.2 0.0 collective-permute-done.4.refs_4_
  28.2 0.6 shard_map.70.so_far
  28.8 0.3 shard_map.71.mine
  29.1 0.1 collective-permute-start.7
  29.2 1.2 %collective-permute-done.7.other = f32[128,128]{1,0:T(8,128)S(1)} collective-permute-done((f32[128,128]{1,0:T(8,128)S(1)}, f32[128,128]{1,0:T(8,128)S(1)}, u32[]{:S(2)}, u32[]{:S(2)}) %collective-permute-start.7) | collective-permute-done | bytes 65568 | tf_op jit(solution)/shard_map/ppermute | solution.py:193
  30.4 0.9 %shard_map.72 = (bf16[512,128]{1,0:T(8,128)(2,1)S(1)}, bf16[512,128]{1,0:T(8,128)(2,1)S(1)}) custom-call(s32[1]{0:T(128)} %bitcast.here, s32[8]{0:T(128)S(1)} %bitcast.7, f32[128,128]{1,0:T(8,128)S(1)} %shard_map.71.mine, f32[128,128]{1,0:T(8,128)S(1)} %collective-permute-done.7.other, bf16[8,512,256]{2,1,0:T(8,128)(2,1)S(1)} %get-tuple-element.27.turned), custom_call_target="tpu_custom_call" | custom-call | bytes 1024 | tf_op jit(solution)/shard_map/pallas_call | solution.py:254
  31.3 2.1 %collective-permute-start.8 = (bf16[512,128]{1,0:T(8,128)(2,1)S(1)}, bf16[512,128]{1,0:T(8,128)(2,1)S(1)}, u32[]{:S(2)}, u32[]{:S(2)}) collective-permute-start(bf16[512,128]{1,0:T(8,128)(2,1)S(1)} %get-tuple-element.38), channel_id=1, source_target_pairs={{0,2},{2,0},{4,6},{6,4},{8,10},{10,8},{12,14},{14,12},{1,3},{3,1},... | collective-permute-start | bytes 393224 | tf_op jit(solution)/shard_map/ppermute | solution.py:187
  33.4 4.4 %collective-permute-start.9 = (bf16[512,128]{1,0:T(8,128)(2,1)S(1)}, bf16[512,128]{1,0:T(8,128)(2,1)S(1)}, u32[]{:S(2)}, u32[]{:S(2)}) collective-permute-start(bf16[512,128]{1,0:T(8,128)(2,1)S(1)} %get-tuple-element.39), channel_id=1, source_target_pairs={{0,4},{2,6},{4,0},{6,2},{8,12},{10,14},{12,8},{14,10},{1,5},{3,7},... | collective-permute-start | bytes 393224 | tf_op jit(solution)/shard_map/ppermute | solution.py:187
  37.9 1.2 %shard_map.73 = (bf16[512,128]{1,0:T(8,128)(2,1)S(1)}, bf16[512,128]{1,0:T(8,128)(2,1)S(1)}, bf16[512,128]{1,0:T(8,128)(2,1)S(1)}, bf16[512,128]{1,0:T(8,128)(2,...) custom-call(s32[1]{0:T(128)} %bitcast.here, s32[8]{0:T(128)S(1)} %bitcast.8, ...), custom_call_target="tpu_custom_call" | custom-call | bytes 1024 | tf_op jit(solution)/shard_map/pallas_call | solution.py:254
  39.0 1.1 %collective-permute-start.10 = (bf16[512,128]{1,0:T(8,128)(2,1)S(1)}, bf16[512,128]{1,0:T(8,128)(2,1)S(1)}, u32[]{:S(2)}, u32[]{:S(2)}) collective-permute-start(bf16[512,128]{1,0:T(8,128)(2,1)S(1)} %get-tuple-element.40), channel_id=1, source_target_pairs={{0,8},{2,10},{4,12},{6,14},{8,0},{10,2},{12,4},{14,6},{1,9},{3,11}... | collective-permute-start | bytes 393224 | tf_op jit(solution)/shard_map/ppermute | solution.py:187
  40.1 1.9 %collective-permute-start.11 = (bf16[512,128]{1,0:T(8,128)(2,1)S(1)}, bf16[512,128]{1,0:T(8,128)(2,1)S(1)}, u32[]{:S(2)}, u32[]{:S(2)}) collective-permute-start(bf16[512,128]{1,0:T(8,128)(2,1)S(1)} %get-tuple-element.41), channel_id=1, source_target_pairs={{0,10},{2,8},{4,14},{6,12},{8,2},{10,0},{12,6},{14,4},{1,11},{3,9}... | collective-permute-start | bytes 393224 | tf_op jit(solution)/shard_map/ppermute | solution.py:187
  42.0 2.5 %collective-permute-start.12 = (bf16[512,128]{1,0:T(8,128)(2,1)S(1)}, bf16[512,128]{1,0:T(8,128)(2,1)S(1)}, u32[]{:S(2)}, u32[]{:S(2)}) collective-permute-start(bf16[512,128]{1,0:T(8,128)(2,1)S(1)} %get-tuple-element.42), channel_id=1, source_target_pairs={{0,12},{2,14},{4,8},{6,10},{8,4},{10,6},{12,0},{14,2},{1,13},{3,15... | collective-permute-start | bytes 393224 | tf_op jit(solution)/shard_map/ppermute | solution.py:187
  44.5 2.3 %collective-permute-start.13 = (bf16[512,128]{1,0:T(8,128)(2,1)S(1)}, bf16[512,128]{1,0:T(8,128)(2,1)S(1)}, u32[]{:S(2)}, u32[]{:S(2)}) collective-permute-start(bf16[512,128]{1,0:T(8,128)(2,1)S(1)} %get-tuple-element.47), channel_id=1, source_target_pairs={{0,14},{2,12},{4,10},{6,8},{8,6},{10,4},{12,2},{14,0},{1,15},{3,13... | collective-permute-start | bytes 393224 | tf_op jit(solution)/shard_map/ppermute | solution.py:187
  46.8 2.0 %shard_map.74 = bf16[128,4096]{1,0:T(8,128)(2,1)} custom-call(s32[1]{0:T(128)} %bitcast.here, s32[8]{0:T(128)S(1)} %bitcast.9, f32[128,128]{1,0:T(8,128)S(1)} %shard_map.71.mine, f32[128,128]{1,0:T(8,128)S(1)} %collective-permute-done.7.other, bf16[512,128]{1,0:T(8,128)(2,1)S(1)} %collective-permute-done.after.refs_0_, ...), custom_call_target="tpu_custom_call" | custom-call | flops 134217728 | bytes 2097152 | tf_op jit(solution)/shard_map/pallas_call | solution.py:264
  48.8 8.4 %collective-permute-done.10.refs_2_ = bf16[512,128]{1,0:T(8,128)(2,1)S(1)} collective-permute-done((bf16[512,128]{1,0:T(8,128)(2,1)S(1)}, bf16[512,128]{1,0:T(8,128)(2,1)S(1)}, u32[]{:S(2)}, u32[]{:S(2)}) %collective-permute-start.10) | collective-permute-done | bytes 131104 | tf_op jit(solution)/shard_map/ppermute | solution.py:187
  57.2 2.7 %collective-permute-done.11.refs_3_ = bf16[512,128]{1,0:T(8,128)(2,1)S(1)} collective-permute-done((bf16[512,128]{1,0:T(8,128)(2,1)S(1)}, bf16[512,128]{1,0:T(8,128)(2,1)S(1)}, u32[]{:S(2)}, u32[]{:S(2)}) %collective-permute-start.11) | collective-permute-done | bytes 131104 | tf_op jit(solution)/shard_map/ppermute | solution.py:187
  59.9 1.5 %shard_map.75.refs_8_ = bf16[96,512,128]{2,1,0:T(8,128)(2,1)} custom-call(s32[8]{0:T(128)S(1)} %bitcast.14, s32[1]{0:T(128)} %bitcast.here, s32[8]{0:T(128)S(1)} %bitcast.10, bf16[512,128]{1,0:T(8,128)(2,1)S(1)} %collective-permute-done.8.refs_0_, bf16[512,128]{1,0:T(8,128)(2,1)S(1)} %collective-permute-done.9.refs_1_, ...), custom_call_target="tpu_custom_call", output_to_operand_aliasing={{}: (8, {})} | custom-call | bytes 2097152 | tf_op jit(solution)/shard_map/pallas_call | solution.py:277
  61.4 1.4 %shard_map.76 = bf16[96,512,128]{2,1,0:T(8,128)(2,1)} custom-call(s32[8]{0:T(128)S(1)} %bitcast.15, s32[1]{0:T(128)} %bitcast.here, s32[8]{0:T(128)S(1)} %bitcast.11, bf16[512,128]{1,0:T(8,128)(2,1)S(1)} %collective-permute-done.8.refs_0_, bf16[512,128]{1,0:T(8,128)(2,1)S(1)} %collective-permute-done.9.refs_1_, ...), custom_call_target="tpu_custom_call", output_to_operand_aliasing={{}: (11, {})} | custom-call | bytes 2097152 | tf_op jit(solution)/shard_map/pallas_call | solution.py:277
  (16 shorter events, 0.0 us)
Async XLA Ops:
  0.6 14.9 %copy-start.1 = (bf16[128,4096]{1,0:T(8,128)(2,1)S(1)}, bf16[128,4096]{1,0:T(8,128)(2,1)}, u32[]{:S(2)}) copy-start(bf16[128,4096]{1,0:T(8,128)(2,1)} %y.5) | copy-start | bytes 3145732
  0.6 14.9 %copy-start = (bf16[128,4096]{1,0:T(8,128)(2,1)S(1)}, bf16[128,4096]{1,0:T(8,128)(2,1)}, u32[]{:S(2)}) copy-start(bf16[128,4096]{1,0:T(8,128)(2,1)} %x.3) | copy-start | bytes 3145732
  0.7 0.8 %copy-start.3 = (s32[8,1]{0,1:T(1,128)S(1)}, s32[8,1]{0,1:T(1,128)}, u32[]{:S(2)}) copy-start(s32[8,1]{0,1:T(1,128)} %param.8) | copy-start | bytes 100
  3.3 27.1 %copy-start.2 = (s32[8,1]{0,1:T(1,128)S(1)}, s32[8,1]{0,1:T(1,128)}, u32[]{:S(2)}) copy-start(s32[8,1]{0,1:T(1,128)} %param.9) | copy-start | bytes 100
  3.3 10.0 %collective-permute-start = (bf16[512,128]{1,0:T(8,128)(2,1)S(1)}, bf16[512,128]{1,0:T(8,128)(2,1)S(1)}, u32[]{:S(2)}, u32[]{:S(2)}) collective-permute-start(bf16[512,128]{1,0:T(8,128)(2,1)S(1)} %get-tuple-element.26), channel_id=1, source_target_pairs={{0,2},{2,0},{4,6},{6,4},{8,10},{10,8},{12,14},{14,12},{1,3},{3,1},... | collective-permute-start | bytes 393224 | tf_op jit(solution)/shard_map/ppermute | solution.py:187
  6.3 9.2 %collective-permute-start.1 = (bf16[512,128]{1,0:T(8,128)(2,1)S(1)}, bf16[512,128]{1,0:T(8,128)(2,1)S(1)}, u32[]{:S(2)}, u32[]{:S(2)}) collective-permute-start(bf16[512,128]{1,0:T(8,128)(2,1)S(1)} %get-tuple-element.29), channel_id=1, source_target_pairs={{0,4},{2,6},{4,0},{6,2},{8,12},{10,14},{12,8},{14,10},{1,5},{3,7},... | collective-permute-start | bytes 393224 | tf_op jit(solution)/shard_map/ppermute | solution.py:187
  7.9 18.0 %collective-permute-start.2 = (bf16[512,128]{1,0:T(8,128)(2,1)S(1)}, bf16[512,128]{1,0:T(8,128)(2,1)S(1)}, u32[]{:S(2)}, u32[]{:S(2)}) collective-permute-start(bf16[512,128]{1,0:T(8,128)(2,1)S(1)} %get-tuple-element.30), channel_id=1, source_target_pairs={{0,8},{2,10},{4,12},{6,14},{8,0},{10,2},{12,4},{14,6},{1,9},{3,11}... | collective-permute-start | bytes 393224 | tf_op jit(solution)/shard_map/ppermute | solution.py:187
  10.5 17.7 %collective-permute-start.3 = (bf16[512,128]{1,0:T(8,128)(2,1)S(1)}, bf16[512,128]{1,0:T(8,128)(2,1)S(1)}, u32[]{:S(2)}, u32[]{:S(2)}) collective-permute-start(bf16[512,128]{1,0:T(8,128)(2,1)S(1)} %get-tuple-element.31), channel_id=1, source_target_pairs={{0,10},{2,8},{4,14},{6,12},{8,2},{10,0},{12,6},{14,4},{1,11},{3,9}... | collective-permute-start | bytes 393224 | tf_op jit(solution)/shard_map/ppermute | solution.py:187
  10.8 17.4 %collective-permute-start.4 = (bf16[512,128]{1,0:T(8,128)(2,1)S(1)}, bf16[512,128]{1,0:T(8,128)(2,1)S(1)}, u32[]{:S(2)}, u32[]{:S(2)}) collective-permute-start(bf16[512,128]{1,0:T(8,128)(2,1)S(1)} %get-tuple-element.32), channel_id=1, source_target_pairs={{0,12},{2,14},{4,8},{6,10},{8,4},{10,6},{12,0},{14,2},{1,13},{3,15... | collective-permute-start | bytes 393224 | tf_op jit(solution)/shard_map/ppermute | solution.py:187
  13.3 15.5 %collective-permute-start.6 = (bf16[512,128]{1,0:T(8,128)(2,1)S(1)}, bf16[512,128]{1,0:T(8,128)(2,1)S(1)}, u32[]{:S(2)}, u32[]{:S(2)}) collective-permute-start(bf16[512,128]{1,0:T(8,128)(2,1)S(1)} %get-tuple-element.37), channel_id=1, source_target_pairs={{0,14},{2,12},{4,10},{6,8},{8,6},{10,4},{12,2},{14,0},{1,15},{3,13... | collective-permute-start | bytes 393224 | tf_op jit(solution)/shard_map/ppermute | solution.py:187
  15.6 13.2 %collective-permute-start.5 = (bf16[512,128]{1,0:T(8,128)(2,1)S(1)}, bf16[512,128]{1,0:T(8,128)(2,1)S(1)}, u32[]{:S(2)}, u32[]{:S(2)}) collective-permute-start(bf16[512,128]{1,0:T(8,128)(2,1)S(1)} %get-tuple-element.35), channel_id=1, source_target_pairs={{0,6},{2,4},{4,2},{6,0},{8,14},{10,12},{12,10},{14,8},{1,7},{3,5},... | collective-permute-start | bytes 393224 | tf_op jit(solution)/shard_map/ppermute | solution.py:187
  29.1 1.3 %collective-permute-start.7 = (f32[128,128]{1,0:T(8,128)S(1)}, f32[128,128]{1,0:T(8,128)S(1)}, u32[]{:S(2)}, u32[]{:S(2)}) collective-permute-start(f32[128,128]{1,0:T(8,128)S(1)} %shard_map.71.mine), channel_id=1, source_target_pairs={{0,1},{1,0},{2,3},{3,2},{4,5},{5,4},{6,7},{7,6},{8,9},{9,8},{10,11... | collective-permute-start | bytes 196616 | tf_op jit(solution)/shard_map/ppermute | solution.py:193
  31.3 13.2 %collective-permute-start.8 = (bf16[512,128]{1,0:T(8,128)(2,1)S(1)}, bf16[512,128]{1,0:T(8,128)(2,1)S(1)}, u32[]{:S(2)}, u32[]{:S(2)}) collective-permute-start(bf16[512,128]{1,0:T(8,128)(2,1)S(1)} %get-tuple-element.38), channel_id=1, source_target_pairs={{0,2},{2,0},{4,6},{6,4},{8,10},{10,8},{12,14},{14,12},{1,3},{3,1},... | collective-permute-start | bytes 393224 | tf_op jit(solution)/shard_map/ppermute | solution.py:187
  33.4 13.4 %collective-permute-start.9 = (bf16[512,128]{1,0:T(8,128)(2,1)S(1)}, bf16[512,128]{1,0:T(8,128)(2,1)S(1)}, u32[]{:S(2)}, u32[]{:S(2)}) collective-permute-start(bf16[512,128]{1,0:T(8,128)(2,1)S(1)} %get-tuple-element.39), channel_id=1, source_target_pairs={{0,4},{2,6},{4,0},{6,2},{8,12},{10,14},{12,8},{14,10},{1,5},{3,7},... | collective-permute-start | bytes 393224 | tf_op jit(solution)/shard_map/ppermute | solution.py:187
  39.0 18.2 %collective-permute-start.10 = (bf16[512,128]{1,0:T(8,128)(2,1)S(1)}, bf16[512,128]{1,0:T(8,128)(2,1)S(1)}, u32[]{:S(2)}, u32[]{:S(2)}) collective-permute-start(bf16[512,128]{1,0:T(8,128)(2,1)S(1)} %get-tuple-element.40), channel_id=1, source_target_pairs={{0,8},{2,10},{4,12},{6,14},{8,0},{10,2},{12,4},{14,6},{1,9},{3,11}... | collective-permute-start | bytes 393224 | tf_op jit(solution)/shard_map/ppermute | solution.py:187
  40.1 19.8 %collective-permute-start.11 = (bf16[512,128]{1,0:T(8,128)(2,1)S(1)}, bf16[512,128]{1,0:T(8,128)(2,1)S(1)}, u32[]{:S(2)}, u32[]{:S(2)}) collective-permute-start(bf16[512,128]{1,0:T(8,128)(2,1)S(1)} %get-tuple-element.41), channel_id=1, source_target_pairs={{0,10},{2,8},{4,14},{6,12},{8,2},{10,0},{12,6},{14,4},{1,11},{3,9}... | collective-permute-start | bytes 393224 | tf_op jit(solution)/shard_map/ppermute | solution.py:187
  42.0 19.4 %collective-permute-start.12 = (bf16[512,128]{1,0:T(8,128)(2,1)S(1)}, bf16[512,128]{1,0:T(8,128)(2,1)S(1)}, u32[]{:S(2)}, u32[]{:S(2)}) collective-permute-start(bf16[512,128]{1,0:T(8,128)(2,1)S(1)} %get-tuple-element.42), channel_id=1, source_target_pairs={{0,12},{2,14},{4,8},{6,10},{8,4},{10,6},{12,0},{14,2},{1,13},{3,15... | collective-permute-start | bytes 393224 | tf_op jit(solution)/shard_map/ppermute | solution.py:187
  44.5 16.9 %collective-permute-start.13 = (bf16[512,128]{1,0:T(8,128)(2,1)S(1)}, bf16[512,128]{1,0:T(8,128)(2,1)S(1)}, u32[]{:S(2)}, u32[]{:S(2)}) collective-permute-start(bf16[512,128]{1,0:T(8,128)(2,1)S(1)} %get-tuple-element.47), channel_id=1, source_target_pairs={{0,14},{2,12},{4,10},{6,8},{8,6},{10,4},{12,2},{14,0},{1,15},{3,13... | collective-permute-start | bytes 393224 | tf_op jit(solution)/shard_map/ppermute | solution.py:187
  46.8 14.7 %collective-permute-start.14 = (bf16[512,128]{1,0:T(8,128)(2,1)S(1)}, bf16[512,128]{1,0:T(8,128)(2,1)S(1)}, u32[]{:S(2)}, u32[]{:S(2)}) collective-permute-start(bf16[512,128]{1,0:T(8,128)(2,1)S(1)} %get-tuple-element.48), channel_id=1, source_target_pairs={{0,6},{2,4},{4,2},{6,0},{8,14},{10,12},{12,10},{14,8},{1,7},{3,5},... | collective-permute-start | bytes 393224 | tf_op jit(solution)/shard_map/ppermute | solution.py:187

commit v17 on v15

--- a/solution.py
+++ b/solution.py
@@ -10,10 +10,10 @@
 adapter_alpha = 128.0
 FETCH = (1, 4, 2, 5, 6, 3, 7)
 FETCH_TIES = {}
-SEND = (1, 4, 2, 5, 6, 3, 7)
+SEND = (1, 6, 2, 7, 4, 5, 3)
 SEND_TIES = {}
 PREP_AFTER = 1
-LATE = (6, 3, 7)
+LATE = (4, 5, 3)
 RANK_LAST = (3, 7)
 SEND_FIRST = 2
 

time: 61 us -> 61.4 us (level); the launches traced: 59.8 us -> 61.2 us
  starting transfers between devices: 25.7 us -> 27.1 us
    ppermute x14, starting transfers between devices: 25.6 us -> 27 us  [exchange(): out[k] = lax.ppermute(piece, 'dp', [(i, i ^ k) for i in range(owners)])]
  transfers between devices with their start and end apart: 15 -> 15, of which waited for: 6 -> 5; matrix products, arithmetic and copies ran while one was open for 0% -> 0% of each run, Pallas kernels for 18% -> 17%
where the time goes in v17:
time: 61.4 us; the launch traced here: 61.2 us
  starting transfers between devices  27.1 us (44%)
  waiting for transfers between devices  17.5 us (29%)
  Pallas kernels  15 us (24%)
  local copies, waits for them, and re-layouts  0.81 us (1%)
  between operations  0.78 us (1%)
    ppermute x14, starting transfers between devices, exchange(): out[k] = lax.ppermute(piece, 'dp', [(i, i ^ k) for i in range(owners)])  27 us
    ppermute x14, waiting for transfers between devices, exchange(): out[k] = lax.ppermute(piece, 'dp', [(i, i ^ k) for i in range(owners)])  16.3 us
    pallas_call x1, Pallas kernels, with_kernels(): call(prep_kernel, [jax.ShapeDtypeStruct((owners, rows, 2 * tokens), bf16)...  5.35 us
    pallas_call x2, Pallas kernels, merge(): call(functools.partial(merge_kernel, tuple(merged), handled, others), jax...  2.82 us
    pallas_call x2, Pallas kernels, with_kernels(): call(functools.partial(piece_kernel, part, scale), [straight] * len(part)...  2.09 us
    pallas_call x1, Pallas kernels, with_kernels(): call(functools.partial(input_kernel, tuple(pairs), scale), jax.ShapeDtype...  1.99 us
    pallas_call x1, Pallas kernels, with_kernels(): call(functools.partial(gather_kernel, FETCH), [straight] * partners, [in_...  1.85 us
    ppermute x1, waiting for transfers between devices, across_cores(): return lax.ppermute(value, 'tensor', [(i, i ^ 1) for i in range(cores)])  1.24 us
  transfers between devices with their start and end apart: 15, of which 5 were waited for; matrix products, arithmetic and copies ran while one was open for 0% of the time, Pallas kernels for 17%

profile of v17, /device:TPU:0, one launch (start us, length us, event | category | flops | bytes accessed | tf_op | source)
XLA Modules:
  0.0 61.2 jit_solution(1966176700477574384)
XLA Ops:
  0.7 0.8 %copy-done.3 = s32[8,1]{0,1:T(1,128)S(1)} copy-done((s32[8,1]{0,1:T(1,128)S(1)}, s32[8,1]{0,1:T(1,128)}, u32[]{:S(2)}) %copy-start.3) | copy-done | bytes 56
  1.5 1.8 %shard_map.68 = (bf16[512,128]{1,0:T(8,128)(2,1)S(1)}, bf16[512,128]{1,0:T(8,128)(2,1)S(1)}, bf16[512,128]{1,0:T(8,128)(2,1)S(1)}, bf16[512,128]{1,0:T(8,128)(2,...) custom-call(s32[8]{0:T(128)S(1)} %bitcast.12, s32[1]{0:T(128)} %bitcast.here, ...), custom_call_target="tpu_custom_call" | custom-call | bytes 2097152 | tf_op jit(solution)/shard_map/pallas_call | solution.py:210
  3.3 0.0 copy-start.2
  3.3 3.0 %collective-permute-start = (bf16[512,128]{1,0:T(8,128)(2,1)S(1)}, bf16[512,128]{1,0:T(8,128)(2,1)S(1)}, u32[]{:S(2)}, u32[]{:S(2)}) collective-permute-start(bf16[512,128]{1,0:T(8,128)(2,1)S(1)} %get-tuple-element.22), channel_id=1, source_target_pairs={{0,2},{2,0},{4,6},{6,4},{8,10},{10,8},{12,14},{14,12},{1,3},{3,1},... | collective-permute-start | bytes 393224 | tf_op jit(solution)/shard_map/ppermute | solution.py:187
  6.3 2.6 %collective-permute-start.1 = (bf16[512,128]{1,0:T(8,128)(2,1)S(1)}, bf16[512,128]{1,0:T(8,128)(2,1)S(1)}, u32[]{:S(2)}, u32[]{:S(2)}) collective-permute-start(bf16[512,128]{1,0:T(8,128)(2,1)S(1)} %get-tuple-element.25), channel_id=1, source_target_pairs={{0,8},{2,10},{4,12},{6,14},{8,0},{10,2},{12,4},{14,6},{1,9},{3,11}... | collective-permute-start | bytes 393224 | tf_op jit(solution)/shard_map/ppermute | solution.py:187
  8.9 1.6 %collective-permute-start.2 = (bf16[512,128]{1,0:T(8,128)(2,1)S(1)}, bf16[512,128]{1,0:T(8,128)(2,1)S(1)}, u32[]{:S(2)}, u32[]{:S(2)}) collective-permute-start(bf16[512,128]{1,0:T(8,128)(2,1)S(1)} %get-tuple-element.26), channel_id=1, source_target_pairs={{0,4},{2,6},{4,0},{6,2},{8,12},{10,14},{12,8},{14,10},{1,5},{3,7},... | collective-permute-start | bytes 393224 | tf_op jit(solution)/shard_map/ppermute | solution.py:187
  10.5 0.3 collective-permute-start.3
  10.8 2.5 %collective-permute-start.4 = (bf16[512,128]{1,0:T(8,128)(2,1)S(1)}, bf16[512,128]{1,0:T(8,128)(2,1)S(1)}, u32[]{:S(2)}, u32[]{:S(2)}) collective-permute-start(bf16[512,128]{1,0:T(8,128)(2,1)S(1)} %get-tuple-element.28), channel_id=1, source_target_pairs={{0,12},{2,14},{4,8},{6,10},{8,4},{10,6},{12,0},{14,2},{1,13},{3,15... | collective-permute-start | bytes 393224 | tf_op jit(solution)/shard_map/ppermute | solution.py:187
  13.3 0.0 collective-permute-done.after.refs_0_
  13.3 1.6 %collective-permute-start.5 = (bf16[512,128]{1,0:T(8,128)(2,1)S(1)}, bf16[512,128]{1,0:T(8,128)(2,1)S(1)}, u32[]{:S(2)}, u32[]{:S(2)}) collective-permute-start(bf16[512,128]{1,0:T(8,128)(2,1)S(1)} %get-tuple-element.30), channel_id=1, source_target_pairs={{0,6},{2,4},{4,2},{6,0},{8,14},{10,12},{12,10},{14,8},{1,7},{3,5},... | collective-permute-start | bytes 393224 | tf_op jit(solution)/shard_map/ppermute | solution.py:187
  14.9 5.6 %collective-permute-done.1.refs_1_ = bf16[512,128]{1,0:T(8,128)(2,1)S(1)} collective-permute-done((bf16[512,128]{1,0:T(8,128)(2,1)S(1)}, bf16[512,128]{1,0:T(8,128)(2,1)S(1)}, u32[]{:S(2)}, u32[]{:S(2)}) %collective-permute-start.1) | collective-permute-done | bytes 131104 | tf_op jit(solution)/shard_map/ppermute | solution.py:187
  20.4 2.3 %collective-permute-start.6 = (bf16[512,128]{1,0:T(8,128)(2,1)S(1)}, bf16[512,128]{1,0:T(8,128)(2,1)S(1)}, u32[]{:S(2)}, u32[]{:S(2)}) collective-permute-start(bf16[512,128]{1,0:T(8,128)(2,1)S(1)} %get-tuple-element.31), channel_id=1, source_target_pairs={{0,14},{2,12},{4,10},{6,8},{8,6},{10,4},{12,2},{14,0},{1,15},{3,13... | collective-permute-start | bytes 393224 | tf_op jit(solution)/shard_map/ppermute | solution.py:187
  22.8 5.3 %shard_map.69 = (bf16[8,512,256]{2,1,0:T(8,128)(2,1)S(1)}, bf16[512,128]{1,0:T(8,128)(2,1)S(1)}, bf16[96,512,128]{2,1,0:T(8,128)(2,1)}) custom-call(s32[8]{0:T(128)S(1)} %bitcast.13, s32[1]{0:T(128)} %bitcast.here, bf16[96,512,128]{2,1,0:T(8,128)(2,1)} %bitcast.18, bf16[512,128]{1,0:T(8,128)(2,1)S(1)} %collective-permute-done.after.refs_0_, ...), custom_call_target="tpu_custom_call" | custom-call | bytes 16777216 | tf_op jit(solution)/shard_map/pallas_call | solution.py:222
  28.2 0.6 shard_map.70.so_far
  28.8 0.3 shard_map.71.mine
  29.1 0.1 collective-permute-start.7
  29.2 1.2 %collective-permute-done.7.other = f32[128,128]{1,0:T(8,128)S(1)} collective-permute-done((f32[128,128]{1,0:T(8,128)S(1)}, f32[128,128]{1,0:T(8,128)S(1)}, u32[]{:S(2)}, u32[]{:S(2)}) %collective-permute-start.7) | collective-permute-done | bytes 65568 | tf_op jit(solution)/shard_map/ppermute | solution.py:193
  30.4 0.9 %shard_map.72 = (bf16[512,128]{1,0:T(8,128)(2,1)S(1)}, bf16[512,128]{1,0:T(8,128)(2,1)S(1)}) custom-call(s32[1]{0:T(128)} %bitcast.here, s32[8]{0:T(128)S(1)} %bitcast.7, f32[128,128]{1,0:T(8,128)S(1)} %shard_map.71.mine, f32[128,128]{1,0:T(8,128)S(1)} %collective-permute-done.7.other, bf16[8,512,256]{2,1,0:T(8,128)(2,1)S(1)} %get-tuple-element.23.turned), custom_call_target="tpu_custom_call" | custom-call | bytes 1024 | tf_op jit(solution)/shard_map/pallas_call | solution.py:254
  31.3 1.6 %collective-permute-start.8 = (bf16[512,128]{1,0:T(8,128)(2,1)S(1)}, bf16[512,128]{1,0:T(8,128)(2,1)S(1)}, u32[]{:S(2)}, u32[]{:S(2)}) collective-permute-start(bf16[512,128]{1,0:T(8,128)(2,1)S(1)} %get-tuple-element.32), channel_id=1, source_target_pairs={{0,2},{2,0},{4,6},{6,4},{8,10},{10,8},{12,14},{14,12},{1,3},{3,1},... | collective-permute-start | bytes 393224 | tf_op jit(solution)/shard_map/ppermute | solution.py:187
  32.9 1.6 %collective-permute-start.9 = (bf16[512,128]{1,0:T(8,128)(2,1)S(1)}, bf16[512,128]{1,0:T(8,128)(2,1)S(1)}, u32[]{:S(2)}, u32[]{:S(2)}) collective-permute-start(bf16[512,128]{1,0:T(8,128)(2,1)S(1)} %get-tuple-element.33), channel_id=1, source_target_pairs={{0,12},{2,14},{4,8},{6,10},{8,4},{10,6},{12,0},{14,2},{1,13},{3,15... | collective-permute-start | bytes 393224 | tf_op jit(solution)/shard_map/ppermute | solution.py:187
  34.5 1.2 %shard_map.73 = (bf16[512,128]{1,0:T(8,128)(2,1)S(1)}, bf16[512,128]{1,0:T(8,128)(2,1)S(1)}, bf16[512,128]{1,0:T(8,128)(2,1)S(1)}, bf16[512,128]{1,0:T(8,128)(2,...) custom-call(s32[1]{0:T(128)} %bitcast.here, s32[8]{0:T(128)S(1)} %bitcast.8, ...), custom_call_target="tpu_custom_call" | custom-call | bytes 1024 | tf_op jit(solution)/shard_map/pallas_call | solution.py:254
  35.7 4.6 %collective-permute-start.10 = (bf16[512,128]{1,0:T(8,128)(2,1)S(1)}, bf16[512,128]{1,0:T(8,128)(2,1)S(1)}, u32[]{:S(2)}, u32[]{:S(2)}) collective-permute-start(bf16[512,128]{1,0:T(8,128)(2,1)S(1)} %get-tuple-element.34), channel_id=1, source_target_pairs={{0,4},{2,6},{4,0},{6,2},{8,12},{10,14},{12,8},{14,10},{1,5},{3,7},... | collective-permute-start | bytes 393224 | tf_op jit(solution)/shard_map/ppermute | solution.py:187
  40.3 0.9 %collective-permute-start.11 = (bf16[512,128]{1,0:T(8,128)(2,1)S(1)}, bf16[512,128]{1,0:T(8,128)(2,1)S(1)}, u32[]{:S(2)}, u32[]{:S(2)}) collective-permute-start(bf16[512,128]{1,0:T(8,128)(2,1)S(1)} %get-tuple-element.35), channel_id=1, source_target_pairs={{0,14},{2,12},{4,10},{6,8},{8,6},{10,4},{12,2},{14,0},{1,15},{3,13... | collective-permute-start | bytes 393224 | tf_op jit(solution)/shard_map/ppermute | solution.py:187
  41.2 0.6 %collective-permute-start.12 = (bf16[512,128]{1,0:T(8,128)(2,1)S(1)}, bf16[512,128]{1,0:T(8,128)(2,1)S(1)}, u32[]{:S(2)}, u32[]{:S(2)}) collective-permute-start(bf16[512,128]{1,0:T(8,128)(2,1)S(1)} %get-tuple-element.36), channel_id=1, source_target_pairs={{0,8},{2,10},{4,12},{6,14},{8,0},{10,2},{12,4},{14,6},{1,9},{3,11}... | collective-permute-start | bytes 393224 | tf_op jit(solution)/shard_map/ppermute | solution.py:187
  41.8 3.2 %collective-permute-start.13 = (bf16[512,128]{1,0:T(8,128)(2,1)S(1)}, bf16[512,128]{1,0:T(8,128)(2,1)S(1)}, u32[]{:S(2)}, u32[]{:S(2)}) collective-permute-start(bf16[512,128]{1,0:T(8,128)(2,1)S(1)} %get-tuple-element.37), channel_id=1, source_target_pairs={{0,10},{2,8},{4,14},{6,12},{8,2},{10,0},{12,6},{14,4},{1,11},{3,9}... | collective-permute-start | bytes 393224 | tf_op jit(solution)/shard_map/ppermute | solution.py:187
  45.0 0.6 %collective-permute-start.14 = (bf16[512,128]{1,0:T(8,128)(2,1)S(1)}, bf16[512,128]{1,0:T(8,128)(2,1)S(1)}, u32[]{:S(2)}, u32[]{:S(2)}) collective-permute-start(bf16[512,128]{1,0:T(8,128)(2,1)S(1)} %get-tuple-element.38), channel_id=1, source_target_pairs={{0,6},{2,4},{4,2},{6,0},{8,14},{10,12},{12,10},{14,8},{1,7},{3,5},... | collective-permute-start | bytes 393224 | tf_op jit(solution)/shard_map/ppermute | solution.py:187
  45.7 2.0 %shard_map.74 = bf16[128,4096]{1,0:T(8,128)(2,1)} custom-call(s32[1]{0:T(128)} %bitcast.here, s32[8]{0:T(128)S(1)} %bitcast.9, f32[128,128]{1,0:T(8,128)S(1)} %shard_map.71.mine, f32[128,128]{1,0:T(8,128)S(1)} %collective-permute-done.7.other, bf16[512,128]{1,0:T(8,128)(2,1)S(1)} %collective-permute-done.after.refs_0_, ...), custom_call_target="tpu_custom_call" | custom-call | flops 134217728 | bytes 2097152 | tf_op jit(solution)/shard_map/pallas_call | solution.py:264
  47.7 1.8 %collective-permute-done.11.refs_3_ = bf16[512,128]{1,0:T(8,128)(2,1)S(1)} collective-permute-done((bf16[512,128]{1,0:T(8,128)(2,1)S(1)}, bf16[512,128]{1,0:T(8,128)(2,1)S(1)}, u32[]{:S(2)}, u32[]{:S(2)}) %collective-permute-start.11) | collective-permute-done | bytes 131104 | tf_op jit(solution)/shard_map/ppermute | solution.py:187
  49.5 1.5 %shard_map.75.refs_8_ = bf16[96,512,128]{2,1,0:T(8,128)(2,1)} custom-call(s32[8]{0:T(128)S(1)} %bitcast.14, s32[1]{0:T(128)} %bitcast.here, s32[8]{0:T(128)S(1)} %bitcast.10, bf16[512,128]{1,0:T(8,128)(2,1)S(1)} %collective-permute-done.8.refs_0_, bf16[512,128]{1,0:T(8,128)(2,1)S(1)} %collective-permute-done.9.refs_1_, ...), custom_call_target="tpu_custom_call", output_to_operand_aliasing={{}: (8, {})} | custom-call | bytes 2097152 | tf_op jit(solution)/shard_map/pallas_call | solution.py:277
  51.0 6.6 %collective-permute-done.12.refs_4_ = bf16[512,128]{1,0:T(8,128)(2,1)S(1)} collective-permute-done((bf16[512,128]{1,0:T(8,128)(2,1)S(1)}, bf16[512,128]{1,0:T(8,128)(2,1)S(1)}, u32[]{:S(2)}, u32[]{:S(2)}) %collective-permute-start.12) | collective-permute-done | bytes 131104 | tf_op jit(solution)/shard_map/ppermute | solution.py:187
  57.6 2.2 %collective-permute-done.13.refs_5_ = bf16[512,128]{1,0:T(8,128)(2,1)S(1)} collective-permute-done((bf16[512,128]{1,0:T(8,128)(2,1)S(1)}, bf16[512,128]{1,0:T(8,128)(2,1)S(1)}, u32[]{:S(2)}, u32[]{:S(2)}) %collective-permute-start.13) | collective-permute-done | bytes 131104 | tf_op jit(solution)/shard_map/ppermute | solution.py:187
  59.8 1.4 %shard_map.76 = bf16[96,512,128]{2,1,0:T(8,128)(2,1)} custom-call(s32[8]{0:T(128)S(1)} %bitcast.15, s32[1]{0:T(128)} %bitcast.here, s32[8]{0:T(128)S(1)} %bitcast.11, bf16[512,128]{1,0:T(8,128)(2,1)S(1)} %collective-permute-done.8.refs_0_, bf16[512,128]{1,0:T(8,128)(2,1)S(1)} %collective-permute-done.9.refs_1_, ...), custom_call_target="tpu_custom_call", output_to_operand_aliasing={{}: (11, {})} | custom-call | bytes 2097152 | tf_op jit(solution)/shard_map/pallas_call | solution.py:277
  (16 shorter events, 0.0 us)
Async XLA Ops:
  0.6 22.2 %copy-start.1 = (bf16[128,4096]{1,0:T(8,128)(2,1)S(1)}, bf16[128,4096]{1,0:T(8,128)(2,1)}, u32[]{:S(2)}) copy-start(bf16[128,4096]{1,0:T(8,128)(2,1)} %y.5) | copy-start | bytes 3145732
  0.6 22.2 %copy-start = (bf16[128,4096]{1,0:T(8,128)(2,1)S(1)}, bf16[128,4096]{1,0:T(8,128)(2,1)}, u32[]{:S(2)}) copy-start(bf16[128,4096]{1,0:T(8,128)(2,1)} %x.3) | copy-start | bytes 3145732
  0.7 0.8 %copy-start.3 = (s32[8,1]{0,1:T(1,128)S(1)}, s32[8,1]{0,1:T(1,128)}, u32[]{:S(2)}) copy-start(s32[8,1]{0,1:T(1,128)} %param.8) | copy-start | bytes 100
  3.3 27.1 %copy-start.2 = (s32[8,1]{0,1:T(1,128)S(1)}, s32[8,1]{0,1:T(1,128)}, u32[]{:S(2)}) copy-start(s32[8,1]{0,1:T(1,128)} %param.9) | copy-start | bytes 100
  3.3 10.0 %collective-permute-start = (bf16[512,128]{1,0:T(8,128)(2,1)S(1)}, bf16[512,128]{1,0:T(8,128)(2,1)S(1)}, u32[]{:S(2)}, u32[]{:S(2)}) collective-permute-start(bf16[512,128]{1,0:T(8,128)(2,1)S(1)} %get-tuple-element.22), channel_id=1, source_target_pairs={{0,2},{2,0},{4,6},{6,4},{8,10},{10,8},{12,14},{14,12},{1,3},{3,1},... | collective-permute-start | bytes 393224 | tf_op jit(solution)/shard_map/ppermute | solution.py:187
  6.3 14.1 %collective-permute-start.1 = (bf16[512,128]{1,0:T(8,128)(2,1)S(1)}, bf16[512,128]{1,0:T(8,128)(2,1)S(1)}, u32[]{:S(2)}, u32[]{:S(2)}) collective-permute-start(bf16[512,128]{1,0:T(8,128)(2,1)S(1)} %get-tuple-element.25), channel_id=1, source_target_pairs={{0,8},{2,10},{4,12},{6,14},{8,0},{10,2},{12,4},{14,6},{1,9},{3,11}... | collective-permute-start | bytes 393224 | tf_op jit(solution)/shard_map/ppermute | solution.py:187
  8.9 19.2 %collective-permute-start.2 = (bf16[512,128]{1,0:T(8,128)(2,1)S(1)}, bf16[512,128]{1,0:T(8,128)(2,1)S(1)}, u32[]{:S(2)}, u32[]{:S(2)}) collective-permute-start(bf16[512,128]{1,0:T(8,128)(2,1)S(1)} %get-tuple-element.26), channel_id=1, source_target_pairs={{0,4},{2,6},{4,0},{6,2},{8,12},{10,14},{12,8},{14,10},{1,5},{3,7},... | collective-permute-start | bytes 393224 | tf_op jit(solution)/shard_map/ppermute | solution.py:187
  10.5 17.7 %collective-permute-start.3 = (bf16[512,128]{1,0:T(8,128)(2,1)S(1)}, bf16[512,128]{1,0:T(8,128)(2,1)S(1)}, u32[]{:S(2)}, u32[]{:S(2)}) collective-permute-start(bf16[512,128]{1,0:T(8,128)(2,1)S(1)} %get-tuple-element.27), channel_id=1, source_target_pairs={{0,10},{2,8},{4,14},{6,12},{8,2},{10,0},{12,6},{14,4},{1,11},{3,9}... | collective-permute-start | bytes 393224 | tf_op jit(solution)/shard_map/ppermute | solution.py:187
  10.8 17.4 %collective-permute-start.4 = (bf16[512,128]{1,0:T(8,128)(2,1)S(1)}, bf16[512,128]{1,0:T(8,128)(2,1)S(1)}, u32[]{:S(2)}, u32[]{:S(2)}) collective-permute-start(bf16[512,128]{1,0:T(8,128)(2,1)S(1)} %get-tuple-element.28), channel_id=1, source_target_pairs={{0,12},{2,14},{4,8},{6,10},{8,4},{10,6},{12,0},{14,2},{1,13},{3,15... | collective-permute-start | bytes 393224 | tf_op jit(solution)/shard_map/ppermute | solution.py:187
  13.3 15.5 %collective-permute-start.5 = (bf16[512,128]{1,0:T(8,128)(2,1)S(1)}, bf16[512,128]{1,0:T(8,128)(2,1)S(1)}, u32[]{:S(2)}, u32[]{:S(2)}) collective-permute-start(bf16[512,128]{1,0:T(8,128)(2,1)S(1)} %get-tuple-element.30), channel_id=1, source_target_pairs={{0,6},{2,4},{4,2},{6,0},{8,14},{10,12},{12,10},{14,8},{1,7},{3,5},... | collective-permute-start | bytes 393224 | tf_op jit(solution)/shard_map/ppermute | solution.py:187
  20.4 8.3 %collective-permute-start.6 = (bf16[512,128]{1,0:T(8,128)(2,1)S(1)}, bf16[512,128]{1,0:T(8,128)(2,1)S(1)}, u32[]{:S(2)}, u32[]{:S(2)}) collective-permute-start(bf16[512,128]{1,0:T(8,128)(2,1)S(1)} %get-tuple-element.31), channel_id=1, source_target_pairs={{0,14},{2,12},{4,10},{6,8},{8,6},{10,4},{12,2},{14,0},{1,15},{3,13... | collective-permute-start | bytes 393224 | tf_op jit(solution)/shard_map/ppermute | solution.py:187
  29.1 1.3 %collective-permute-start.7 = (f32[128,128]{1,0:T(8,128)S(1)}, f32[128,128]{1,0:T(8,128)S(1)}, u32[]{:S(2)}, u32[]{:S(2)}) collective-permute-start(f32[128,128]{1,0:T(8,128)S(1)} %shard_map.71.mine), channel_id=1, source_target_pairs={{0,1},{1,0},{2,3},{3,2},{4,5},{5,4},{6,7},{7,6},{8,9},{9,8},{10,11... | collective-permute-start | bytes 196616 | tf_op jit(solution)/shard_map/ppermute | solution.py:193
  31.3 10.5 %collective-permute-start.8 = (bf16[512,128]{1,0:T(8,128)(2,1)S(1)}, bf16[512,128]{1,0:T(8,128)(2,1)S(1)}, u32[]{:S(2)}, u32[]{:S(2)}) collective-permute-start(bf16[512,128]{1,0:T(8,128)(2,1)S(1)} %get-tuple-element.32), channel_id=1, source_target_pairs={{0,2},{2,0},{4,6},{6,4},{8,10},{10,8},{12,14},{14,12},{1,3},{3,1},... | collective-permute-start | bytes 393224 | tf_op jit(solution)/shard_map/ppermute | solution.py:187
  32.9 12.2 %collective-permute-start.9 = (bf16[512,128]{1,0:T(8,128)(2,1)S(1)}, bf16[512,128]{1,0:T(8,128)(2,1)S(1)}, u32[]{:S(2)}, u32[]{:S(2)}) collective-permute-start(bf16[512,128]{1,0:T(8,128)(2,1)S(1)} %get-tuple-element.33), channel_id=1, source_target_pairs={{0,12},{2,14},{4,8},{6,10},{8,4},{10,6},{12,0},{14,2},{1,13},{3,15... | collective-permute-start | bytes 393224 | tf_op jit(solution)/shard_map/ppermute | solution.py:187
  35.7 12.0 %collective-permute-start.10 = (bf16[512,128]{1,0:T(8,128)(2,1)S(1)}, bf16[512,128]{1,0:T(8,128)(2,1)S(1)}, u32[]{:S(2)}, u32[]{:S(2)}) collective-permute-start(bf16[512,128]{1,0:T(8,128)(2,1)S(1)} %get-tuple-element.34), channel_id=1, source_target_pairs={{0,4},{2,6},{4,0},{6,2},{8,12},{10,14},{12,8},{14,10},{1,5},{3,7},... | collective-permute-start | bytes 393224 | tf_op jit(solution)/shard_map/ppermute | solution.py:187
  40.3 9.2 %collective-permute-start.11 = (bf16[512,128]{1,0:T(8,128)(2,1)S(1)}, bf16[512,128]{1,0:T(8,128)(2,1)S(1)}, u32[]{:S(2)}, u32[]{:S(2)}) collective-permute-start(bf16[512,128]{1,0:T(8,128)(2,1)S(1)} %get-tuple-element.35), channel_id=1, source_target_pairs={{0,14},{2,12},{4,10},{6,8},{8,6},{10,4},{12,2},{14,0},{1,15},{3,13... | collective-permute-start | bytes 393224 | tf_op jit(solution)/shard_map/ppermute | solution.py:187
  41.2 16.4 %collective-permute-start.12 = (bf16[512,128]{1,0:T(8,128)(2,1)S(1)}, bf16[512,128]{1,0:T(8,128)(2,1)S(1)}, u32[]{:S(2)}, u32[]{:S(2)}) collective-permute-start(bf16[512,128]{1,0:T(8,128)(2,1)S(1)} %get-tuple-element.36), channel_id=1, source_target_pairs={{0,8},{2,10},{4,12},{6,14},{8,0},{10,2},{12,4},{14,6},{1,9},{3,11}... | collective-permute-start | bytes 393224 | tf_op jit(solution)/shard_map/ppermute | solution.py:187
  41.8 18.0 %collective-permute-start.13 = (bf16[512,128]{1,0:T(8,128)(2,1)S(1)}, bf16[512,128]{1,0:T(8,128)(2,1)S(1)}, u32[]{:S(2)}, u32[]{:S(2)}) collective-permute-start(bf16[512,128]{1,0:T(8,128)(2,1)S(1)} %get-tuple-element.37), channel_id=1, source_target_pairs={{0,10},{2,8},{4,14},{6,12},{8,2},{10,0},{12,6},{14,4},{1,11},{3,9}... | collective-permute-start | bytes 393224 | tf_op jit(solution)/shard_map/ppermute | solution.py:187
  45.0 14.8 %collective-permute-start.14 = (bf16[512,128]{1,0:T(8,128)(2,1)S(1)}, bf16[512,128]{1,0:T(8,128)(2,1)S(1)}, u32[]{:S(2)}, u32[]{:S(2)}) collective-permute-start(bf16[512,128]{1,0:T(8,128)(2,1)S(1)} %get-tuple-element.38), channel_id=1, source_target_pairs={{0,6},{2,4},{4,2},{6,0},{8,14},{10,12},{12,10},{14,8},{1,7},{3,5},... | collective-permute-start | bytes 393224 | tf_op jit(solution)/shard_map/ppermute | solution.py:187

commit v18 on v17

--- a/solution.py
+++ b/solution.py
@@ -8,14 +8,15 @@
 from jax.sharding import PartitionSpec as P
 
 adapter_alpha = 128.0
-FETCH = (1, 4, 2, 5, 6, 3, 7)
+FETCH = (4, 1, 2, 5, 6, 3, 7)
 FETCH_TIES = {}
-SEND = (1, 6, 2, 7, 4, 5, 3)
+SEND = (1, 6, 2, 4, 5, 3, 7)
 SEND_TIES = {}
 PREP_AFTER = 1
-LATE = (4, 5, 3)
+LATE = (5, 3, 7)
 RANK_LAST = (3, 7)
 SEND_FIRST = 2
+FETCH_FIRST = 1
 
 in_vmem = pl.BlockSpec(memory_space=pltpu.VMEM)
 in_smem = pl.BlockSpec(memory_space=pltpu.SMEM)
@@ -205,17 +206,19 @@
     straight = jax.ShapeDtypeStruct((rows, width), bf16)
     pair_bytes = owners * rows * width * 2
     token_bytes = tokens * features * 2
-    partners = len(FETCH)
-
-    sent = call(
-        functools.partial(gather_kernel, FETCH),
-        [straight] * partners,
-        [in_smem, in_smem, in_hbm],
-        [in_vmem] * partners,
-        [pltpu.SemaphoreType.DMA((partners,))],
-        moved=2 * pair_bytes,
-        vmem=53,
-    )(ids, here, table)
+
+    sent, me = [], here
+    for part in (FETCH[:FETCH_FIRST], FETCH[FETCH_FIRST:]):
+        sent += call(
+            functools.partial(gather_kernel, part),
+            [straight] * len(part),
+            [in_smem, in_smem, in_hbm],
+            [in_vmem] * len(part),
+            [pltpu.SemaphoreType.DMA((len(part),))],
+            moved=1024,
+            vmem=53,
+        )(ids, me, table)
+        me = lax.optimization_barrier((here, *sent))[0]
     pairs = exchange(dict(zip(FETCH, sent)), FETCH_TIES)
 
     step = 8

time: 61.4 us -> 58.9 us (0.959)
  waiting for transfers between devices: 17.5 us -> 13.1 us
  Pallas kernels: 15 us -> 16.4 us
  starting transfers between devices: 27.1 us -> 27.8 us
    ppermute x14, waiting for transfers between devices: 16.3 us -> 11.8 us  [exchange(): out[k] = lax.ppermute(piece, 'dp', [(i, i ^ k) for i in range(owners)])]
    pallas_call x1 -> x2, Pallas kernels: 1.85 us -> 3.34 us  [with_kernels(): call(functools.partial(gather_kernel, part), [straight] * len(part), [in_...]
    ppermute x14, starting transfers between devices: 27 us -> 27.7 us  [exchange(): out[k] = lax.ppermute(piece, 'dp', [(i, i ^ k) for i in range(owners)])]
  transfers between devices with their start and end apart: 15 -> 15, of which waited for: 5 -> 5; matrix products, arithmetic and copies ran while one was open for 0% -> 0% of each run, Pallas kernels for 17% -> 21%
where the time goes in v18:
time: 58.9 us; the launch traced here: 58.8 us
  starting transfers between devices  27.8 us (47%)
  Pallas kernels  16.4 us (28%)
  waiting for transfers between devices  13.1 us (22%)
  between operations  0.75 us (1%)
  local copies, waits for them, and re-layouts  0.67 us (1%)
    ppermute x14, starting transfers between devices, exchange(): out[k] = lax.ppermute(piece, 'dp', [(i, i ^ k) for i in range(owners)])  27.7 us
    ppermute x14, waiting for transfers between devices, exchange(): out[k] = lax.ppermute(piece, 'dp', [(i, i ^ k) for i in range(owners)])  11.8 us
    pallas_call x1, Pallas kernels, with_kernels(): call(prep_kernel, [jax.ShapeDtypeStruct((owners, rows, 2 * tokens), bf16)...  5.35 us
    pallas_call x2, Pallas kernels, with_kernels(): call(functools.partial(gather_kernel, part), [straight] * len(part), [in_...  3.34 us
    pallas_call x2, Pallas kernels, merge(): call(functools.partial(merge_kernel, tuple(merged), handled, others), jax...  2.82 us
    pallas_call x2, Pallas kernels, with_kernels(): call(functools.partial(piece_kernel, part, scale), [straight] * len(part)...  2.09 us
    pallas_call x1, Pallas kernels, with_kernels(): call(functools.partial(input_kernel, tuple(pairs), scale), jax.ShapeDtype...  1.99 us
    ppermute x1, waiting for transfers between devices, across_cores(): return lax.ppermute(value, 'tensor', [(i, i ^ 1) for i in range(cores)])  1.24 us
  transfers between devices with their start and end apart: 15, of which 5 were waited for; matrix products, arithmetic and copies ran while one was open for 0% of the time, Pallas kernels for 21%

profile of v18, /device:TPU:0, one launch (start us, length us, event | category | flops | bytes accessed | tf_op | source)
XLA Modules:
  0.0 58.8 jit_solution(6093768247102851088)
XLA Ops:
  0.6 0.6 %copy-done.2 = s32[8,1]{0,1:T(1,128)S(1)} copy-done((s32[8,1]{0,1:T(1,128)S(1)}, s32[8,1]{0,1:T(1,128)}, u32[]{:S(2)}) %copy-start.2) | copy-done | bytes 56
  1.3 1.5 %shard_map.68 = bf16[512,128]{1,0:T(8,128)(2,1)S(1)} custom-call(s32[8]{0:T(128)S(1)} %bitcast.7, s32[1]{0:T(128)} %bitcast.here, bf16[96,512,128]{2,1,0:T(8,128)(2,1)} %bitcast.17), custom_call_target="tpu_custom_call" | custom-call | bytes 1024 | tf_op jit(solution)/shard_map/pallas_call | solution.py:212
  2.8 4.1 %collective-permute-start.1 = (bf16[512,128]{1,0:T(8,128)(2,1)S(1)}, bf16[512,128]{1,0:T(8,128)(2,1)S(1)}, u32[]{:S(2)}, u32[]{:S(2)}) collective-permute-start(bf16[512,128]{1,0:T(8,128)(2,1)S(1)} %shard_map.68), channel_id=1, source_target_pairs={{0,8},{2,10},{4,12},{6,14},{8,0},{10,2},{12,4},{14,6},{1,9},{3,11}... | collective-permute-start | bytes 393224 | tf_op jit(solution)/shard_map/ppermute | solution.py:188
  6.9 1.8 %shard_map.69 = (bf16[512,128]{1,0:T(8,128)(2,1)S(1)}, bf16[512,128]{1,0:T(8,128)(2,1)S(1)}, bf16[512,128]{1,0:T(8,128)(2,1)S(1)}, bf16[512,128]{1,0:T(8,128)(2,...) custom-call(s32[8]{0:T(128)S(1)} %bitcast.8, s32[1]{0:T(128)} %bitcast.here, ...), custom_call_target="tpu_custom_call" | custom-call | bytes 1024 | tf_op jit(solution)/shard_map/pallas_call | solution.py:212
  8.8 0.0 copy-start.3
  8.8 1.6 %collective-permute-start = (bf16[512,128]{1,0:T(8,128)(2,1)S(1)}, bf16[512,128]{1,0:T(8,128)(2,1)S(1)}, u32[]{:S(2)}, u32[]{:S(2)}) collective-permute-start(bf16[512,128]{1,0:T(8,128)(2,1)S(1)} %get-tuple-element.23), channel_id=1, source_target_pairs={{0,2},{2,0},{4,6},{6,4},{8,10},{10,8},{12,14},{14,12},{1,3},{3,1},... | collective-permute-start | bytes 393224 | tf_op jit(solution)/shard_map/ppermute | solution.py:188
  10.3 1.6 %collective-permute-start.2 = (bf16[512,128]{1,0:T(8,128)(2,1)S(1)}, bf16[512,128]{1,0:T(8,128)(2,1)S(1)}, u32[]{:S(2)}, u32[]{:S(2)}) collective-permute-start(bf16[512,128]{1,0:T(8,128)(2,1)S(1)} %get-tuple-element.26), channel_id=1, source_target_pairs={{0,4},{2,6},{4,0},{6,2},{8,12},{10,14},{12,8},{14,10},{1,5},{3,7},... | collective-permute-start | bytes 393224 | tf_op jit(solution)/shard_map/ppermute | solution.py:188
  11.9 0.3 collective-permute-start.3
  12.2 2.5 %collective-permute-start.4 = (bf16[512,128]{1,0:T(8,128)(2,1)S(1)}, bf16[512,128]{1,0:T(8,128)(2,1)S(1)}, u32[]{:S(2)}, u32[]{:S(2)}) collective-permute-start(bf16[512,128]{1,0:T(8,128)(2,1)S(1)} %get-tuple-element.28), channel_id=1, source_target_pairs={{0,12},{2,14},{4,8},{6,10},{8,4},{10,6},{12,0},{14,2},{1,13},{3,15... | collective-permute-start | bytes 393224 | tf_op jit(solution)/shard_map/ppermute | solution.py:188
  14.7 1.6 %collective-permute-start.5 = (bf16[512,128]{1,0:T(8,128)(2,1)S(1)}, bf16[512,128]{1,0:T(8,128)(2,1)S(1)}, u32[]{:S(2)}, u32[]{:S(2)}) collective-permute-start(bf16[512,128]{1,0:T(8,128)(2,1)S(1)} %get-tuple-element.30), channel_id=1, source_target_pairs={{0,6},{2,4},{4,2},{6,0},{8,14},{10,12},{12,10},{14,8},{1,7},{3,5},... | collective-permute-start | bytes 393224 | tf_op jit(solution)/shard_map/ppermute | solution.py:188
  16.3 2.8 %collective-permute-start.6 = (bf16[512,128]{1,0:T(8,128)(2,1)S(1)}, bf16[512,128]{1,0:T(8,128)(2,1)S(1)}, u32[]{:S(2)}, u32[]{:S(2)}) collective-permute-start(bf16[512,128]{1,0:T(8,128)(2,1)S(1)} %get-tuple-element.31), channel_id=1, source_target_pairs={{0,14},{2,12},{4,10},{6,8},{8,6},{10,4},{12,2},{14,0},{1,15},{3,13... | collective-permute-start | bytes 393224 | tf_op jit(solution)/shard_map/ppermute | solution.py:188
  19.1 5.3 %shard_map.70 = (bf16[8,512,256]{2,1,0:T(8,128)(2,1)S(1)}, bf16[512,128]{1,0:T(8,128)(2,1)S(1)}, bf16[96,512,128]{2,1,0:T(8,128)(2,1)}) custom-call(s32[8]{0:T(128)S(1)} %bitcast.9, s32[1]{0:T(128)} %bitcast.here, bf16[96,512,128]{2,1,0:T(8,128)(2,1)} %bitcast.19, bf16[512,128]{1,0:T(8,128)(2,1)S(1)} %collective-permute-done.after.refs_1_, ...), custom_call_target="tpu_custom_call" | custom-call | bytes 16777216 | tf_op jit(solution)/shard_map/pallas_call | solution.py:225
  24.5 0.0 collective-permute-done.2.refs_2_
  24.5 2.2 %collective-permute-done.3.refs_3_ = bf16[512,128]{1,0:T(8,128)(2,1)S(1)} collective-permute-done((bf16[512,128]{1,0:T(8,128)(2,1)S(1)}, bf16[512,128]{1,0:T(8,128)(2,1)S(1)}, u32[]{:S(2)}, u32[]{:S(2)}) %collective-permute-start.3) | collective-permute-done | bytes 131104 | tf_op jit(solution)/shard_map/ppermute | solution.py:188
  26.7 0.6 shard_map.71.so_far
  27.2 0.6 collective-permute-done.5.refs_0_.refs_5_
  27.8 0.3 shard_map.72.mine
  28.1 0.1 collective-permute-start.7
  28.2 1.2 %collective-permute-done.7.other = f32[128,128]{1,0:T(8,128)S(1)} collective-permute-done((f32[128,128]{1,0:T(8,128)S(1)}, f32[128,128]{1,0:T(8,128)S(1)}, u32[]{:S(2)}, u32[]{:S(2)}) %collective-permute-start.7) | collective-permute-done | bytes 65568 | tf_op jit(solution)/shard_map/ppermute | solution.py:194
  29.5 0.9 %shard_map.73 = (bf16[512,128]{1,0:T(8,128)(2,1)S(1)}, bf16[512,128]{1,0:T(8,128)(2,1)S(1)}) custom-call(s32[1]{0:T(128)} %bitcast.here, s32[8]{0:T(128)S(1)} %bitcast.12, f32[128,128]{1,0:T(8,128)S(1)} %shard_map.72.mine, f32[128,128]{1,0:T(8,128)S(1)} %collective-permute-done.7.other, bf16[8,512,256]{2,1,0:T(8,128)(2,1)S(1)} %get-tuple-element.24.turned), custom_call_target="tpu_custom_call" | custom-call | bytes 1024 | tf_op jit(solution)/shard_map/pallas_call | solution.py:257
  30.4 1.0 %collective-permute-start.8 = (bf16[512,128]{1,0:T(8,128)(2,1)S(1)}, bf16[512,128]{1,0:T(8,128)(2,1)S(1)}, u32[]{:S(2)}, u32[]{:S(2)}) collective-permute-start(bf16[512,128]{1,0:T(8,128)(2,1)S(1)} %get-tuple-element.32), channel_id=1, source_target_pairs={{0,2},{2,0},{4,6},{6,4},{8,10},{10,8},{12,14},{14,12},{1,3},{3,1},... | collective-permute-start | bytes 393224 | tf_op jit(solution)/shard_map/ppermute | solution.py:188
  31.4 3.0 %collective-permute-start.9 = (bf16[512,128]{1,0:T(8,128)(2,1)S(1)}, bf16[512,128]{1,0:T(8,128)(2,1)S(1)}, u32[]{:S(2)}, u32[]{:S(2)}) collective-permute-start(bf16[512,128]{1,0:T(8,128)(2,1)S(1)} %get-tuple-element.33), channel_id=1, source_target_pairs={{0,12},{2,14},{4,8},{6,10},{8,4},{10,6},{12,0},{14,2},{1,13},{3,15... | collective-permute-start | bytes 393224 | tf_op jit(solution)/shard_map/ppermute | solution.py:188
  34.4 1.2 %shard_map.74 = (bf16[512,128]{1,0:T(8,128)(2,1)S(1)}, bf16[512,128]{1,0:T(8,128)(2,1)S(1)}, bf16[512,128]{1,0:T(8,128)(2,1)S(1)}, bf16[512,128]{1,0:T(8,128)(2,...) custom-call(s32[1]{0:T(128)} %bitcast.here, s32[8]{0:T(128)S(1)} %bitcast.13, ...), custom_call_target="tpu_custom_call" | custom-call | bytes 1024 | tf_op jit(solution)/shard_map/pallas_call | solution.py:257
  35.5 3.1 %collective-permute-start.10 = (bf16[512,128]{1,0:T(8,128)(2,1)S(1)}, bf16[512,128]{1,0:T(8,128)(2,1)S(1)}, u32[]{:S(2)}, u32[]{:S(2)}) collective-permute-start(bf16[512,128]{1,0:T(8,128)(2,1)S(1)} %get-tuple-element.34), channel_id=1, source_target_pairs={{0,4},{2,6},{4,0},{6,2},{8,12},{10,14},{12,8},{14,10},{1,5},{3,7},... | collective-permute-start | bytes 393224 | tf_op jit(solution)/shard_map/ppermute | solution.py:188
  38.7 3.8 %collective-permute-start.12 = (bf16[512,128]{1,0:T(8,128)(2,1)S(1)}, bf16[512,128]{1,0:T(8,128)(2,1)S(1)}, u32[]{:S(2)}, u32[]{:S(2)}) collective-permute-start(bf16[512,128]{1,0:T(8,128)(2,1)S(1)} %get-tuple-element.36), channel_id=1, source_target_pairs={{0,10},{2,8},{4,14},{6,12},{8,2},{10,0},{12,6},{14,4},{1,11},{3,9}... | collective-permute-start | bytes 393224 | tf_op jit(solution)/shard_map/ppermute | solution.py:188
  42.5 0.1 collective-permute-start.13
  42.6 2.3 %collective-permute-start.14 = (bf16[512,128]{1,0:T(8,128)(2,1)S(1)}, bf16[512,128]{1,0:T(8,128)(2,1)S(1)}, u32[]{:S(2)}, u32[]{:S(2)}) collective-permute-start(bf16[512,128]{1,0:T(8,128)(2,1)S(1)} %get-tuple-element.38), channel_id=1, source_target_pairs={{0,14},{2,12},{4,10},{6,8},{8,6},{10,4},{12,2},{14,0},{1,15},{3,13... | collective-permute-start | bytes 393224 | tf_op jit(solution)/shard_map/ppermute | solution.py:188
  44.9 2.0 %shard_map.75 = bf16[128,4096]{1,0:T(8,128)(2,1)} custom-call(s32[1]{0:T(128)} %bitcast.here, s32[8]{0:T(128)S(1)} %bitcast.14, f32[128,128]{1,0:T(8,128)S(1)} %shard_map.72.mine, f32[128,128]{1,0:T(8,128)S(1)} %collective-permute-done.7.other, bf16[512,128]{1,0:T(8,128)(2,1)S(1)} %collective-permute-done.1.refs_0_, ...), custom_call_target="tpu_custom_call" | custom-call | flops 134217728 | bytes 2097152 | tf_op jit(solution)/shard_map/pallas_call | solution.py:267
  46.9 4.8 %collective-permute-done.11.refs_3_ = bf16[512,128]{1,0:T(8,128)(2,1)S(1)} collective-permute-done((bf16[512,128]{1,0:T(8,128)(2,1)S(1)}, bf16[512,128]{1,0:T(8,128)(2,1)S(1)}, u32[]{:S(2)}, u32[]{:S(2)}) %collective-permute-start.11) | collective-permute-done | bytes 131104 | tf_op jit(solution)/shard_map/ppermute | solution.py:188
  51.7 1.5 %shard_map.76.refs_8_ = bf16[96,512,128]{2,1,0:T(8,128)(2,1)} custom-call(s32[8]{0:T(128)S(1)} %bitcast.10, s32[1]{0:T(128)} %bitcast.here, s32[8]{0:T(128)S(1)} %bitcast.15, bf16[512,128]{1,0:T(8,128)(2,1)S(1)} %collective-permute-done.8.refs_0_, bf16[512,128]{1,0:T(8,128)(2,1)S(1)} %collective-permute-done.9.refs_1_, ...), custom_call_target="tpu_custom_call", output_to_operand_aliasing={{}: (8, {})} | custom-call | bytes 2097152 | tf_op jit(solution)/shard_map/pallas_call | solution.py:280
  53.1 4.2 %collective-permute-done.12.refs_4_ = bf16[512,128]{1,0:T(8,128)(2,1)S(1)} collective-permute-done((bf16[512,128]{1,0:T(8,128)(2,1)S(1)}, bf16[512,128]{1,0:T(8,128)(2,1)S(1)}, u32[]{:S(2)}, u32[]{:S(2)}) %collective-permute-start.12) | collective-permute-done | bytes 131104 | tf_op jit(solution)/shard_map/ppermute | solution.py:188
  57.4 1.4 %shard_map.77 = bf16[96,512,128]{2,1,0:T(8,128)(2,1)} custom-call(s32[8]{0:T(128)S(1)} %bitcast.11, s32[1]{0:T(128)} %bitcast.here, s32[8]{0:T(128)S(1)} %bitcast.16, bf16[512,128]{1,0:T(8,128)(2,1)S(1)} %collective-permute-done.8.refs_0_, bf16[512,128]{1,0:T(8,128)(2,1)S(1)} %collective-permute-done.9.refs_1_, ...), custom_call_target="tpu_custom_call", output_to_operand_aliasing={{}: (11, {})} | custom-call | bytes 2097152 | tf_op jit(solution)/shard_map/pallas_call | solution.py:280
  (17 shorter events, 0.0 us)
Async XLA Ops:
  0.6 0.7 %copy-start.2 = (s32[8,1]{0,1:T(1,128)S(1)}, s32[8,1]{0,1:T(1,128)}, u32[]{:S(2)}) copy-start(s32[8,1]{0,1:T(1,128)} %param.8) | copy-start | bytes 100
  1.3 17.8 %copy-start = (bf16[128,4096]{1,0:T(8,128)(2,1)S(1)}, bf16[128,4096]{1,0:T(8,128)(2,1)}, u32[]{:S(2)}) copy-start(bf16[128,4096]{1,0:T(8,128)(2,1)} %x.3) | copy-start | bytes 3145732
  1.3 17.8 %copy-start.1 = (bf16[128,4096]{1,0:T(8,128)(2,1)S(1)}, bf16[128,4096]{1,0:T(8,128)(2,1)}, u32[]{:S(2)}) copy-start(bf16[128,4096]{1,0:T(8,128)(2,1)} %y.5) | copy-start | bytes 3145732
  2.8 11.8 %collective-permute-start.1 = (bf16[512,128]{1,0:T(8,128)(2,1)S(1)}, bf16[512,128]{1,0:T(8,128)(2,1)S(1)}, u32[]{:S(2)}, u32[]{:S(2)}) collective-permute-start(bf16[512,128]{1,0:T(8,128)(2,1)S(1)} %shard_map.68), channel_id=1, source_target_pairs={{0,8},{2,10},{4,12},{6,14},{8,0},{10,2},{12,4},{14,6},{1,9},{3,11}... | collective-permute-start | bytes 393224 | tf_op jit(solution)/shard_map/ppermute | solution.py:188
  8.8 20.7 %copy-start.3 = (s32[8,1]{0,1:T(1,128)S(1)}, s32[8,1]{0,1:T(1,128)}, u32[]{:S(2)}) copy-start(s32[8,1]{0,1:T(1,128)} %param.9) | copy-start | bytes 100
  8.8 7.5 %collective-permute-start = (bf16[512,128]{1,0:T(8,128)(2,1)S(1)}, bf16[512,128]{1,0:T(8,128)(2,1)S(1)}, u32[]{:S(2)}, u32[]{:S(2)}) collective-permute-start(bf16[512,128]{1,0:T(8,128)(2,1)S(1)} %get-tuple-element.23), channel_id=1, source_target_pairs={{0,2},{2,0},{4,6},{6,4},{8,10},{10,8},{12,14},{14,12},{1,3},{3,1},... | collective-permute-start | bytes 393224 | tf_op jit(solution)/shard_map/ppermute | solution.py:188
  10.3 14.1 %collective-permute-start.2 = (bf16[512,128]{1,0:T(8,128)(2,1)S(1)}, bf16[512,128]{1,0:T(8,128)(2,1)S(1)}, u32[]{:S(2)}, u32[]{:S(2)}) collective-permute-start(bf16[512,128]{1,0:T(8,128)(2,1)S(1)} %get-tuple-element.26), channel_id=1, source_target_pairs={{0,4},{2,6},{4,0},{6,2},{8,12},{10,14},{12,8},{14,10},{1,5},{3,7},... | collective-permute-start | bytes 393224 | tf_op jit(solution)/shard_map/ppermute | solution.py:188
  11.9 14.8 %collective-permute-start.3 = (bf16[512,128]{1,0:T(8,128)(2,1)S(1)}, bf16[512,128]{1,0:T(8,128)(2,1)S(1)}, u32[]{:S(2)}, u32[]{:S(2)}) collective-permute-start(bf16[512,128]{1,0:T(8,128)(2,1)S(1)} %get-tuple-element.27), channel_id=1, source_target_pairs={{0,10},{2,8},{4,14},{6,12},{8,2},{10,0},{12,6},{14,4},{1,11},{3,9}... | collective-permute-start | bytes 393224 | tf_op jit(solution)/shard_map/ppermute | solution.py:188
  12.2 14.5 %collective-permute-start.4 = (bf16[512,128]{1,0:T(8,128)(2,1)S(1)}, bf16[512,128]{1,0:T(8,128)(2,1)S(1)}, u32[]{:S(2)}, u32[]{:S(2)}) collective-permute-start(bf16[512,128]{1,0:T(8,128)(2,1)S(1)} %get-tuple-element.28), channel_id=1, source_target_pairs={{0,12},{2,14},{4,8},{6,10},{8,4},{10,6},{12,0},{14,2},{1,13},{3,15... | collective-permute-start | bytes 393224 | tf_op jit(solution)/shard_map/ppermute | solution.py:188
  14.7 13.1 %collective-permute-start.5 = (bf16[512,128]{1,0:T(8,128)(2,1)S(1)}, bf16[512,128]{1,0:T(8,128)(2,1)S(1)}, u32[]{:S(2)}, u32[]{:S(2)}) collective-permute-start(bf16[512,128]{1,0:T(8,128)(2,1)S(1)} %get-tuple-element.30), channel_id=1, source_target_pairs={{0,6},{2,4},{4,2},{6,0},{8,14},{10,12},{12,10},{14,8},{1,7},{3,5},... | collective-permute-start | bytes 393224 | tf_op jit(solution)/shard_map/ppermute | solution.py:188
  16.3 11.5 %collective-permute-start.6 = (bf16[512,128]{1,0:T(8,128)(2,1)S(1)}, bf16[512,128]{1,0:T(8,128)(2,1)S(1)}, u32[]{:S(2)}, u32[]{:S(2)}) collective-permute-start(bf16[512,128]{1,0:T(8,128)(2,1)S(1)} %get-tuple-element.31), channel_id=1, source_target_pairs={{0,14},{2,12},{4,10},{6,8},{8,6},{10,4},{12,2},{14,0},{1,15},{3,13... | collective-permute-start | bytes 393224 | tf_op jit(solution)/shard_map/ppermute | solution.py:188
  28.1 1.3 %collective-permute-start.7 = (f32[128,128]{1,0:T(8,128)S(1)}, f32[128,128]{1,0:T(8,128)S(1)}, u32[]{:S(2)}, u32[]{:S(2)}) collective-permute-start(f32[128,128]{1,0:T(8,128)S(1)} %shard_map.72.mine), channel_id=1, source_target_pairs={{0,1},{1,0},{2,3},{3,2},{4,5},{5,4},{6,7},{7,6},{8,9},{9,8},{10,11... | collective-permute-start | bytes 196616 | tf_op jit(solution)/shard_map/ppermute | solution.py:194
  30.4 12.1 %collective-permute-start.8 = (bf16[512,128]{1,0:T(8,128)(2,1)S(1)}, bf16[512,128]{1,0:T(8,128)(2,1)S(1)}, u32[]{:S(2)}, u32[]{:S(2)}) collective-permute-start(bf16[512,128]{1,0:T(8,128)(2,1)S(1)} %get-tuple-element.32), channel_id=1, source_target_pairs={{0,2},{2,0},{4,6},{6,4},{8,10},{10,8},{12,14},{14,12},{1,3},{3,1},... | collective-permute-start | bytes 393224 | tf_op jit(solution)/shard_map/ppermute | solution.py:188
  31.4 11.2 %collective-permute-start.9 = (bf16[512,128]{1,0:T(8,128)(2,1)S(1)}, bf16[512,128]{1,0:T(8,128)(2,1)S(1)}, u32[]{:S(2)}, u32[]{:S(2)}) collective-permute-start(bf16[512,128]{1,0:T(8,128)(2,1)S(1)} %get-tuple-element.33), channel_id=1, source_target_pairs={{0,12},{2,14},{4,8},{6,10},{8,4},{10,6},{12,0},{14,2},{1,13},{3,15... | collective-permute-start | bytes 393224 | tf_op jit(solution)/shard_map/ppermute | solution.py:188
  35.5 11.3 %collective-permute-start.10 = (bf16[512,128]{1,0:T(8,128)(2,1)S(1)}, bf16[512,128]{1,0:T(8,128)(2,1)S(1)}, u32[]{:S(2)}, u32[]{:S(2)}) collective-permute-start(bf16[512,128]{1,0:T(8,128)(2,1)S(1)} %get-tuple-element.34), channel_id=1, source_target_pairs={{0,4},{2,6},{4,0},{6,2},{8,12},{10,14},{12,8},{14,10},{1,5},{3,7},... | collective-permute-start | bytes 393224 | tf_op jit(solution)/shard_map/ppermute | solution.py:188
  38.7 13.0 %collective-permute-start.11 = (bf16[512,128]{1,0:T(8,128)(2,1)S(1)}, bf16[512,128]{1,0:T(8,128)(2,1)S(1)}, u32[]{:S(2)}, u32[]{:S(2)}) collective-permute-start(bf16[512,128]{1,0:T(8,128)(2,1)S(1)} %get-tuple-element.35), channel_id=1, source_target_pairs={{0,8},{2,10},{4,12},{6,14},{8,0},{10,2},{12,4},{14,6},{1,9},{3,11}... | collective-permute-start | bytes 393224 | tf_op jit(solution)/shard_map/ppermute | solution.py:188
  38.7 18.7 %collective-permute-start.12 = (bf16[512,128]{1,0:T(8,128)(2,1)S(1)}, bf16[512,128]{1,0:T(8,128)(2,1)S(1)}, u32[]{:S(2)}, u32[]{:S(2)}) collective-permute-start(bf16[512,128]{1,0:T(8,128)(2,1)S(1)} %get-tuple-element.36), channel_id=1, source_target_pairs={{0,10},{2,8},{4,14},{6,12},{8,2},{10,0},{12,6},{14,4},{1,11},{3,9}... | collective-permute-start | bytes 393224 | tf_op jit(solution)/shard_map/ppermute | solution.py:188
  42.5 14.9 %collective-permute-start.13 = (bf16[512,128]{1,0:T(8,128)(2,1)S(1)}, bf16[512,128]{1,0:T(8,128)(2,1)S(1)}, u32[]{:S(2)}, u32[]{:S(2)}) collective-permute-start(bf16[512,128]{1,0:T(8,128)(2,1)S(1)} %get-tuple-element.37), channel_id=1, source_target_pairs={{0,6},{2,4},{4,2},{6,0},{8,14},{10,12},{12,10},{14,8},{1,7},{3,5},... | collective-permute-start | bytes 393224 | tf_op jit(solution)/shard_map/ppermute | solution.py:188
  42.6 14.8 %collective-permute-start.14 = (bf16[512,128]{1,0:T(8,128)(2,1)S(1)}, bf16[512,128]{1,0:T(8,128)(2,1)S(1)}, u32[]{:S(2)}, u32[]{:S(2)}) collective-permute-start(bf16[512,128]{1,0:T(8,128)(2,1)S(1)} %get-tuple-element.38), channel_id=1, source_target_pairs={{0,14},{2,12},{4,10},{6,8},{8,6},{10,4},{12,2},{14,0},{1,15},{3,13... | collective-permute-start | bytes 393224 | tf_op jit(solution)/shard_map/ppermute | solution.py:188

commit v19 on v18

--- a/solution.py
+++ b/solution.py
@@ -10,12 +10,12 @@
 adapter_alpha = 128.0
 FETCH = (4, 1, 2, 5, 6, 3, 7)
 FETCH_TIES = {}
-SEND = (1, 6, 2, 4, 5, 3, 7)
-SEND_TIES = {}
+SEND = (6, 1, 2, 4, 5, 3, 7)
+SEND_TIES = {7: 6}
 PREP_AFTER = 1
 LATE = (5, 3, 7)
 RANK_LAST = (3, 7)
-SEND_FIRST = 2
+SEND_FIRST = 1
 FETCH_FIRST = 1
 
 in_vmem = pl.BlockSpec(memory_space=pltpu.VMEM)

time: 58.9 us -> 58.9 us (level)
  no operation moved by 1% of the time
where the time goes in v19:
time: 58.9 us; the launch traced here: 58.8 us
  starting transfers between devices  27.9 us (47%)
  Pallas kernels  16.5 us (28%)
  waiting for transfers between devices  13 us (22%)
  between operations  0.75 us (1%)
  local copies, waits for them, and re-layouts  0.67 us (1%)
    ppermute x14, starting transfers between devices, exchange(): out[k] = lax.ppermute(piece, 'dp', [(i, i ^ k) for i in range(owners)])  27.8 us
    ppermute x14, waiting for transfers between devices, exchange(): out[k] = lax.ppermute(piece, 'dp', [(i, i ^ k) for i in range(owners)])  11.8 us
    pallas_call x1, Pallas kernels, with_kernels(): call(prep_kernel, [jax.ShapeDtypeStruct((owners, rows, 2 * tokens), bf16)...  5.35 us
    pallas_call x2, Pallas kernels, with_kernels(): call(functools.partial(gather_kernel, part), [straight] * len(part), [in_...  3.34 us
    pallas_call x2, Pallas kernels, merge(): call(functools.partial(merge_kernel, tuple(merged), handled, others), jax...  2.82 us
    pallas_call x2, Pallas kernels, with_kernels(): call(functools.partial(piece_kernel, part, scale), [straight] * len(part)...  2.09 us
    pallas_call x1, Pallas kernels, with_kernels(): call(functools.partial(input_kernel, tuple(pairs), scale), jax.ShapeDtype...  1.99 us
    ppermute x1, waiting for transfers between devices, across_cores(): return lax.ppermute(value, 'tensor', [(i, i ^ 1) for i in range(cores)])  1.24 us
  transfers between devices with their start and end apart: 15, of which 5 were waited for; matrix products, arithmetic and copies ran while one was open for 0% of the time, Pallas kernels for 21%

profile of v19, /device:TPU:0, one launch (start us, length us, event | category | flops | bytes accessed | tf_op | source)
XLA Modules:
  0.0 58.8 jit_solution(10382202126497008702)
XLA Ops:
  0.6 0.6 %copy-done.2 = s32[8,1]{0,1:T(1,128)S(1)} copy-done((s32[8,1]{0,1:T(1,128)S(1)}, s32[8,1]{0,1:T(1,128)}, u32[]{:S(2)}) %copy-start.2) | copy-done | bytes 56
  1.3 1.5 %shard_map.68 = bf16[512,128]{1,0:T(8,128)(2,1)S(1)} custom-call(s32[8]{0:T(128)S(1)} %bitcast.7, s32[1]{0:T(128)} %bitcast.here, bf16[96,512,128]{2,1,0:T(8,128)(2,1)} %bitcast.17), custom_call_target="tpu_custom_call" | custom-call | bytes 1024 | tf_op jit(solution)/shard_map/pallas_call | solution.py:212
  2.8 4.1 %collective-permute-start.1 = (bf16[512,128]{1,0:T(8,128)(2,1)S(1)}, bf16[512,128]{1,0:T(8,128)(2,1)S(1)}, u32[]{:S(2)}, u32[]{:S(2)}) collective-permute-start(bf16[512,128]{1,0:T(8,128)(2,1)S(1)} %shard_map.68), channel_id=1, source_target_pairs={{0,8},{2,10},{4,12},{6,14},{8,0},{10,2},{12,4},{14,6},{1,9},{3,11}... | collective-permute-start | bytes 393224 | tf_op jit(solution)/shard_map/ppermute | solution.py:188
  6.9 1.8 %shard_map.69 = (bf16[512,128]{1,0:T(8,128)(2,1)S(1)}, bf16[512,128]{1,0:T(8,128)(2,1)S(1)}, bf16[512,128]{1,0:T(8,128)(2,1)S(1)}, bf16[512,128]{1,0:T(8,128)(2,...) custom-call(s32[8]{0:T(128)S(1)} %bitcast.8, s32[1]{0:T(128)} %bitcast.here, ...), custom_call_target="tpu_custom_call" | custom-call | bytes 1024 | tf_op jit(solution)/shard_map/pallas_call | solution.py:212
  8.8 0.0 copy-start.3
  8.8 1.6 %collective-permute-start = (bf16[512,128]{1,0:T(8,128)(2,1)S(1)}, bf16[512,128]{1,0:T(8,128)(2,1)S(1)}, u32[]{:S(2)}, u32[]{:S(2)}) collective-permute-start(bf16[512,128]{1,0:T(8,128)(2,1)S(1)} %get-tuple-element.23), channel_id=1, source_target_pairs={{0,2},{2,0},{4,6},{6,4},{8,10},{10,8},{12,14},{14,12},{1,3},{3,1},... | collective-permute-start | bytes 393224 | tf_op jit(solution)/shard_map/ppermute | solution.py:188
  10.3 1.6 %collective-permute-start.2 = (bf16[512,128]{1,0:T(8,128)(2,1)S(1)}, bf16[512,128]{1,0:T(8,128)(2,1)S(1)}, u32[]{:S(2)}, u32[]{:S(2)}) collective-permute-start(bf16[512,128]{1,0:T(8,128)(2,1)S(1)} %get-tuple-element.26), channel_id=1, source_target_pairs={{0,4},{2,6},{4,0},{6,2},{8,12},{10,14},{12,8},{14,10},{1,5},{3,7},... | collective-permute-start | bytes 393224 | tf_op jit(solution)/shard_map/ppermute | solution.py:188
  11.9 0.3 collective-permute-start.3
  12.2 2.5 %collective-permute-start.4 = (bf16[512,128]{1,0:T(8,128)(2,1)S(1)}, bf16[512,128]{1,0:T(8,128)(2,1)S(1)}, u32[]{:S(2)}, u32[]{:S(2)}) collective-permute-start(bf16[512,128]{1,0:T(8,128)(2,1)S(1)} %get-tuple-element.28), channel_id=1, source_target_pairs={{0,12},{2,14},{4,8},{6,10},{8,4},{10,6},{12,0},{14,2},{1,13},{3,15... | collective-permute-start | bytes 393224 | tf_op jit(solution)/shard_map/ppermute | solution.py:188
  14.7 1.6 %collective-permute-start.5 = (bf16[512,128]{1,0:T(8,128)(2,1)S(1)}, bf16[512,128]{1,0:T(8,128)(2,1)S(1)}, u32[]{:S(2)}, u32[]{:S(2)}) collective-permute-start(bf16[512,128]{1,0:T(8,128)(2,1)S(1)} %get-tuple-element.30), channel_id=1, source_target_pairs={{0,6},{2,4},{4,2},{6,0},{8,14},{10,12},{12,10},{14,8},{1,7},{3,5},... | collective-permute-start | bytes 393224 | tf_op jit(solution)/shard_map/ppermute | solution.py:188
  16.3 2.8 %collective-permute-start.6 = (bf16[512,128]{1,0:T(8,128)(2,1)S(1)}, bf16[512,128]{1,0:T(8,128)(2,1)S(1)}, u32[]{:S(2)}, u32[]{:S(2)}) collective-permute-start(bf16[512,128]{1,0:T(8,128)(2,1)S(1)} %get-tuple-element.31), channel_id=1, source_target_pairs={{0,14},{2,12},{4,10},{6,8},{8,6},{10,4},{12,2},{14,0},{1,15},{3,13... | collective-permute-start | bytes 393224 | tf_op jit(solution)/shard_map/ppermute | solution.py:188
  19.1 5.3 %shard_map.70 = (bf16[8,512,256]{2,1,0:T(8,128)(2,1)S(1)}, bf16[512,128]{1,0:T(8,128)(2,1)S(1)}, bf16[96,512,128]{2,1,0:T(8,128)(2,1)}) custom-call(s32[8]{0:T(128)S(1)} %bitcast.9, s32[1]{0:T(128)} %bitcast.here, bf16[96,512,128]{2,1,0:T(8,128)(2,1)} %bitcast.19, bf16[512,128]{1,0:T(8,128)(2,1)S(1)} %collective-permute-done.after.refs_1_, ...), custom_call_target="tpu_custom_call" | custom-call | bytes 16777216 | tf_op jit(solution)/shard_map/pallas_call | solution.py:225
  24.5 0.0 collective-permute-done.2.refs_2_
  24.5 2.2 %collective-permute-done.3.refs_3_ = bf16[512,128]{1,0:T(8,128)(2,1)S(1)} collective-permute-done((bf16[512,128]{1,0:T(8,128)(2,1)S(1)}, bf16[512,128]{1,0:T(8,128)(2,1)S(1)}, u32[]{:S(2)}, u32[]{:S(2)}) %collective-permute-start.3) | collective-permute-done | bytes 131104 | tf_op jit(solution)/shard_map/ppermute | solution.py:188
  26.7 0.0 collective-permute-done.4.refs_4_
  26.7 0.6 shard_map.71.so_far
  27.2 0.6 collective-permute-done.5.refs_0_.refs_5_
  27.8 0.3 shard_map.72.mine
  28.1 0.1 collective-permute-start.7
  28.2 1.2 %collective-permute-done.7.other = f32[128,128]{1,0:T(8,128)S(1)} collective-permute-done((f32[128,128]{1,0:T(8,128)S(1)}, f32[128,128]{1,0:T(8,128)S(1)}, u32[]{:S(2)}, u32[]{:S(2)}) %collective-permute-start.7) | collective-permute-done | bytes 65568 | tf_op jit(solution)/shard_map/ppermute | solution.py:194
  29.5 0.8 %shard_map.73 = bf16[512,128]{1,0:T(8,128)(2,1)S(1)} custom-call(s32[1]{0:T(128)} %bitcast.here, s32[8]{0:T(128)S(1)} %bitcast.12, f32[128,128]{1,0:T(8,128)S(1)} %shard_map.72.mine, f32[128,128]{1,0:T(8,128)S(1)} %collective-permute-done.7.other, bf16[8,512,256]{2,1,0:T(8,128)(2,1)S(1)} %get-tuple-element.24.turned), custom_call_target="tpu_custom_call" | custom-call | bytes 1024 | tf_op jit(solution)/shard_map/pallas_call | solution.py:257
  30.3 2.7 %collective-permute-start.8 = (bf16[512,128]{1,0:T(8,128)(2,1)S(1)}, bf16[512,128]{1,0:T(8,128)(2,1)S(1)}, u32[]{:S(2)}, u32[]{:S(2)}) collective-permute-start(bf16[512,128]{1,0:T(8,128)(2,1)S(1)} %shard_map.73), channel_id=1, source_target_pairs={{0,12},{2,14},{4,8},{6,10},{8,4},{10,6},{12,0},{14,2},{1,13},{3,15... | collective-permute-start | bytes 393224 | tf_op jit(solution)/shard_map/ppermute | solution.py:188
  33.0 1.3 %shard_map.74 = (bf16[512,128]{1,0:T(8,128)(2,1)S(1)}, bf16[512,128]{1,0:T(8,128)(2,1)S(1)}, bf16[512,128]{1,0:T(8,128)(2,1)S(1)}, bf16[512,128]{1,0:T(8,128)(2,...) custom-call(s32[1]{0:T(128)} %bitcast.here, s32[8]{0:T(128)S(1)} %bitcast.13, ...), custom_call_target="tpu_custom_call" | custom-call | bytes 1024 | tf_op jit(solution)/shard_map/pallas_call | solution.py:257
  34.3 1.3 %collective-permute-start.9 = (bf16[512,128]{1,0:T(8,128)(2,1)S(1)}, bf16[512,128]{1,0:T(8,128)(2,1)S(1)}, u32[]{:S(2)}, u32[]{:S(2)}) collective-permute-start(bf16[512,128]{1,0:T(8,128)(2,1)S(1)} %get-tuple-element.32), channel_id=1, source_target_pairs={{0,2},{2,0},{4,6},{6,4},{8,10},{10,8},{12,14},{14,12},{1,3},{3,1},... | collective-permute-start | bytes 393224 | tf_op jit(solution)/shard_map/ppermute | solution.py:188
  35.6 3.1 %collective-permute-start.10 = (bf16[512,128]{1,0:T(8,128)(2,1)S(1)}, bf16[512,128]{1,0:T(8,128)(2,1)S(1)}, u32[]{:S(2)}, u32[]{:S(2)}) collective-permute-start(bf16[512,128]{1,0:T(8,128)(2,1)S(1)} %get-tuple-element.33), channel_id=1, source_target_pairs={{0,4},{2,6},{4,0},{6,2},{8,12},{10,14},{12,8},{14,10},{1,5},{3,7},... | collective-permute-start | bytes 393224 | tf_op jit(solution)/shard_map/ppermute | solution.py:188
  38.7 3.8 %collective-permute-start.12 = (bf16[512,128]{1,0:T(8,128)(2,1)S(1)}, bf16[512,128]{1,0:T(8,128)(2,1)S(1)}, u32[]{:S(2)}, u32[]{:S(2)}) collective-permute-start(bf16[512,128]{1,0:T(8,128)(2,1)S(1)} %get-tuple-element.35), channel_id=1, source_target_pairs={{0,10},{2,8},{4,14},{6,12},{8,2},{10,0},{12,6},{14,4},{1,11},{3,9}... | collective-permute-start | bytes 393224 | tf_op jit(solution)/shard_map/ppermute | solution.py:188
  42.5 2.4 %collective-permute-start.14 = (bf16[512,128]{1,0:T(8,128)(2,1)S(1)}, bf16[512,128]{1,0:T(8,128)(2,1)S(1)}, u32[]{:S(2)}, u32[]{:S(2)}) collective-permute-start(bf16[512,128]{1,0:T(8,128)(2,1)S(1)} %get-tuple-element.40), channel_id=1, source_target_pairs={{0,14},{2,12},{4,10},{6,8},{8,6},{10,4},{12,2},{14,0},{1,15},{3,13... | collective-permute-start | bytes 393224 | tf_op jit(solution)/shard_map/ppermute | solution.py:188
  45.0 2.0 %shard_map.75 = bf16[128,4096]{1,0:T(8,128)(2,1)} custom-call(s32[1]{0:T(128)} %bitcast.here, s32[8]{0:T(128)S(1)} %bitcast.14, f32[128,128]{1,0:T(8,128)S(1)} %shard_map.72.mine, f32[128,128]{1,0:T(8,128)S(1)} %collective-permute-done.7.other, bf16[512,128]{1,0:T(8,128)(2,1)S(1)} %collective-permute-done.1.refs_0_, ...), custom_call_target="tpu_custom_call" | custom-call | flops 134217728 | bytes 2097152 | tf_op jit(solution)/shard_map/pallas_call | solution.py:267
  46.9 4.7 %collective-permute-done.11.refs_3_ = bf16[512,128]{1,0:T(8,128)(2,1)S(1)} collective-permute-done((bf16[512,128]{1,0:T(8,128)(2,1)S(1)}, bf16[512,128]{1,0:T(8,128)(2,1)S(1)}, u32[]{:S(2)}, u32[]{:S(2)}) %collective-permute-start.11) | collective-permute-done | bytes 131104 | tf_op jit(solution)/shard_map/ppermute | solution.py:188
  51.7 1.5 %shard_map.76.refs_8_ = bf16[96,512,128]{2,1,0:T(8,128)(2,1)} custom-call(s32[8]{0:T(128)S(1)} %bitcast.10, s32[1]{0:T(128)} %bitcast.here, s32[8]{0:T(128)S(1)} %bitcast.15, bf16[512,128]{1,0:T(8,128)(2,1)S(1)} %collective-permute-done.8.refs_0_, bf16[512,128]{1,0:T(8,128)(2,1)S(1)} %collective-permute-done.9.refs_1_, ...), custom_call_target="tpu_custom_call", output_to_operand_aliasing={{}: (8, {})} | custom-call | bytes 2097152 | tf_op jit(solution)/shard_map/pallas_call | solution.py:280
  53.1 4.2 %collective-permute-done.12.refs_4_ = bf16[512,128]{1,0:T(8,128)(2,1)S(1)} collective-permute-done((bf16[512,128]{1,0:T(8,128)(2,1)S(1)}, bf16[512,128]{1,0:T(8,128)(2,1)S(1)}, u32[]{:S(2)}, u32[]{:S(2)}) %collective-permute-start.12) | collective-permute-done | bytes 131104 | tf_op jit(solution)/shard_map/ppermute | solution.py:188
  57.4 1.4 %shard_map.77 = bf16[96,512,128]{2,1,0:T(8,128)(2,1)} custom-call(s32[8]{0:T(128)S(1)} %bitcast.11, s32[1]{0:T(128)} %bitcast.here, s32[8]{0:T(128)S(1)} %bitcast.16, bf16[512,128]{1,0:T(8,128)(2,1)S(1)} %collective-permute-done.8.refs_0_, bf16[512,128]{1,0:T(8,128)(2,1)S(1)} %collective-permute-done.9.refs_1_, ...), custom_call_target="tpu_custom_call", output_to_operand_aliasing={{}: (11, {})} | custom-call | bytes 2097152 | tf_op jit(solution)/shard_map/pallas_call | solution.py:280
  (17 shorter events, 0.0 us)
Async XLA Ops:
  0.6 0.7 %copy-start.2 = (s32[8,1]{0,1:T(1,128)S(1)}, s32[8,1]{0,1:T(1,128)}, u32[]{:S(2)}) copy-start(s32[8,1]{0,1:T(1,128)} %param.8) | copy-start | bytes 100
  1.3 17.8 %copy-start = (bf16[128,4096]{1,0:T(8,128)(2,1)S(1)}, bf16[128,4096]{1,0:T(8,128)(2,1)}, u32[]{:S(2)}) copy-start(bf16[128,4096]{1,0:T(8,128)(2,1)} %x.3) | copy-start | bytes 3145732
  1.3 17.8 %copy-start.1 = (bf16[128,4096]{1,0:T(8,128)(2,1)S(1)}, bf16[128,4096]{1,0:T(8,128)(2,1)}, u32[]{:S(2)}) copy-start(bf16[128,4096]{1,0:T(8,128)(2,1)} %y.5) | copy-start | bytes 3145732
  2.8 11.8 %collective-permute-start.1 = (bf16[512,128]{1,0:T(8,128)(2,1)S(1)}, bf16[512,128]{1,0:T(8,128)(2,1)S(1)}, u32[]{:S(2)}, u32[]{:S(2)}) collective-permute-start(bf16[512,128]{1,0:T(8,128)(2,1)S(1)} %shard_map.68), channel_id=1, source_target_pairs={{0,8},{2,10},{4,12},{6,14},{8,0},{10,2},{12,4},{14,6},{1,9},{3,11}... | collective-permute-start | bytes 393224 | tf_op jit(solution)/shard_map/ppermute | solution.py:188
  8.8 20.7 %copy-start.3 = (s32[8,1]{0,1:T(1,128)S(1)}, s32[8,1]{0,1:T(1,128)}, u32[]{:S(2)}) copy-start(s32[8,1]{0,1:T(1,128)} %param.9) | copy-start | bytes 100
  8.8 7.5 %collective-permute-start = (bf16[512,128]{1,0:T(8,128)(2,1)S(1)}, bf16[512,128]{1,0:T(8,128)(2,1)S(1)}, u32[]{:S(2)}, u32[]{:S(2)}) collective-permute-start(bf16[512,128]{1,0:T(8,128)(2,1)S(1)} %get-tuple-element.23), channel_id=1, source_target_pairs={{0,2},{2,0},{4,6},{6,4},{8,10},{10,8},{12,14},{14,12},{1,3},{3,1},... | collective-permute-start | bytes 393224 | tf_op jit(solution)/shard_map/ppermute | solution.py:188
  10.3 14.1 %collective-permute-start.2 = (bf16[512,128]{1,0:T(8,128)(2,1)S(1)}, bf16[512,128]{1,0:T(8,128)(2,1)S(1)}, u32[]{:S(2)}, u32[]{:S(2)}) collective-permute-start(bf16[512,128]{1,0:T(8,128)(2,1)S(1)} %get-tuple-element.26), channel_id=1, source_target_pairs={{0,4},{2,6},{4,0},{6,2},{8,12},{10,14},{12,8},{14,10},{1,5},{3,7},... | collective-permute-start | bytes 393224 | tf_op jit(solution)/shard_map/ppermute | solution.py:188
  11.9 14.8 %collective-permute-start.3 = (bf16[512,128]{1,0:T(8,128)(2,1)S(1)}, bf16[512,128]{1,0:T(8,128)(2,1)S(1)}, u32[]{:S(2)}, u32[]{:S(2)}) collective-permute-start(bf16[512,128]{1,0:T(8,128)(2,1)S(1)} %get-tuple-element.27), channel_id=1, source_target_pairs={{0,10},{2,8},{4,14},{6,12},{8,2},{10,0},{12,6},{14,4},{1,11},{3,9}... | collective-permute-start | bytes 393224 | tf_op jit(solution)/shard_map/ppermute | solution.py:188
  12.2 14.5 %collective-permute-start.4 = (bf16[512,128]{1,0:T(8,128)(2,1)S(1)}, bf16[512,128]{1,0:T(8,128)(2,1)S(1)}, u32[]{:S(2)}, u32[]{:S(2)}) collective-permute-start(bf16[512,128]{1,0:T(8,128)(2,1)S(1)} %get-tuple-element.28), channel_id=1, source_target_pairs={{0,12},{2,14},{4,8},{6,10},{8,4},{10,6},{12,0},{14,2},{1,13},{3,15... | collective-permute-start | bytes 393224 | tf_op jit(solution)/shard_map/ppermute | solution.py:188
  14.7 13.1 %collective-permute-start.5 = (bf16[512,128]{1,0:T(8,128)(2,1)S(1)}, bf16[512,128]{1,0:T(8,128)(2,1)S(1)}, u32[]{:S(2)}, u32[]{:S(2)}) collective-permute-start(bf16[512,128]{1,0:T(8,128)(2,1)S(1)} %get-tuple-element.30), channel_id=1, source_target_pairs={{0,6},{2,4},{4,2},{6,0},{8,14},{10,12},{12,10},{14,8},{1,7},{3,5},... | collective-permute-start | bytes 393224 | tf_op jit(solution)/shard_map/ppermute | solution.py:188
  16.3 11.5 %collective-permute-start.6 = (bf16[512,128]{1,0:T(8,128)(2,1)S(1)}, bf16[512,128]{1,0:T(8,128)(2,1)S(1)}, u32[]{:S(2)}, u32[]{:S(2)}) collective-permute-start(bf16[512,128]{1,0:T(8,128)(2,1)S(1)} %get-tuple-element.31), channel_id=1, source_target_pairs={{0,14},{2,12},{4,10},{6,8},{8,6},{10,4},{12,2},{14,0},{1,15},{3,13... | collective-permute-start | bytes 393224 | tf_op jit(solution)/shard_map/ppermute | solution.py:188
  28.1 1.3 %collective-permute-start.7 = (f32[128,128]{1,0:T(8,128)S(1)}, f32[128,128]{1,0:T(8,128)S(1)}, u32[]{:S(2)}, u32[]{:S(2)}) collective-permute-start(f32[128,128]{1,0:T(8,128)S(1)} %shard_map.72.mine), channel_id=1, source_target_pairs={{0,1},{1,0},{2,3},{3,2},{4,5},{5,4},{6,7},{7,6},{8,9},{9,8},{10,11... | collective-permute-start | bytes 196616 | tf_op jit(solution)/shard_map/ppermute | solution.py:194
  30.3 12.2 %collective-permute-start.8 = (bf16[512,128]{1,0:T(8,128)(2,1)S(1)}, bf16[512,128]{1,0:T(8,128)(2,1)S(1)}, u32[]{:S(2)}, u32[]{:S(2)}) collective-permute-start(bf16[512,128]{1,0:T(8,128)(2,1)S(1)} %shard_map.73), channel_id=1, source_target_pairs={{0,12},{2,14},{4,8},{6,10},{8,4},{10,6},{12,0},{14,2},{1,13},{3,15... | collective-permute-start | bytes 393224 | tf_op jit(solution)/shard_map/ppermute | solution.py:188
  34.3 8.2 %collective-permute-start.9 = (bf16[512,128]{1,0:T(8,128)(2,1)S(1)}, bf16[512,128]{1,0:T(8,128)(2,1)S(1)}, u32[]{:S(2)}, u32[]{:S(2)}) collective-permute-start(bf16[512,128]{1,0:T(8,128)(2,1)S(1)} %get-tuple-element.32), channel_id=1, source_target_pairs={{0,2},{2,0},{4,6},{6,4},{8,10},{10,8},{12,14},{14,12},{1,3},{3,1},... | collective-permute-start | bytes 393224 | tf_op jit(solution)/shard_map/ppermute | solution.py:188
  35.6 11.3 %collective-permute-start.10 = (bf16[512,128]{1,0:T(8,128)(2,1)S(1)}, bf16[512,128]{1,0:T(8,128)(2,1)S(1)}, u32[]{:S(2)}, u32[]{:S(2)}) collective-permute-start(bf16[512,128]{1,0:T(8,128)(2,1)S(1)} %get-tuple-element.33), channel_id=1, source_target_pairs={{0,4},{2,6},{4,0},{6,2},{8,12},{10,14},{12,8},{14,10},{1,5},{3,7},... | collective-permute-start | bytes 393224 | tf_op jit(solution)/shard_map/ppermute | solution.py:188
  38.7 13.0 %collective-permute-start.11 = (bf16[512,128]{1,0:T(8,128)(2,1)S(1)}, bf16[512,128]{1,0:T(8,128)(2,1)S(1)}, u32[]{:S(2)}, u32[]{:S(2)}) collective-permute-start(bf16[512,128]{1,0:T(8,128)(2,1)S(1)} %get-tuple-element.34), channel_id=1, source_target_pairs={{0,8},{2,10},{4,12},{6,14},{8,0},{10,2},{12,4},{14,6},{1,9},{3,11}... | collective-permute-start | bytes 393224 | tf_op jit(solution)/shard_map/ppermute | solution.py:188
  38.7 18.7 %collective-permute-start.12 = (bf16[512,128]{1,0:T(8,128)(2,1)S(1)}, bf16[512,128]{1,0:T(8,128)(2,1)S(1)}, u32[]{:S(2)}, u32[]{:S(2)}) collective-permute-start(bf16[512,128]{1,0:T(8,128)(2,1)S(1)} %get-tuple-element.35), channel_id=1, source_target_pairs={{0,10},{2,8},{4,14},{6,12},{8,2},{10,0},{12,6},{14,4},{1,11},{3,9}... | collective-permute-start | bytes 393224 | tf_op jit(solution)/shard_map/ppermute | solution.py:188
  42.5 14.9 %collective-permute-start.13 = (bf16[512,128]{1,0:T(8,128)(2,1)S(1)}, bf16[512,128]{1,0:T(8,128)(2,1)S(1)}, u32[]{:S(2)}, u32[]{:S(2)}) collective-permute-start(bf16[512,128]{1,0:T(8,128)(2,1)S(1)} %get-tuple-element.36), channel_id=1, source_target_pairs={{0,6},{2,4},{4,2},{6,0},{8,14},{10,12},{12,10},{14,8},{1,7},{3,5},... | collective-permute-start | bytes 393224 | tf_op jit(solution)/shard_map/ppermute | solution.py:188
  42.5 14.9 %collective-permute-start.14 = (bf16[512,128]{1,0:T(8,128)(2,1)S(1)}, bf16[512,128]{1,0:T(8,128)(2,1)S(1)}, u32[]{:S(2)}, u32[]{:S(2)}) collective-permute-start(bf16[512,128]{1,0:T(8,128)(2,1)S(1)} %get-tuple-element.40), channel_id=1, source_target_pairs={{0,14},{2,12},{4,10},{6,8},{8,6},{10,4},{12,2},{14,0},{1,15},{3,13... | collective-permute-start | bytes 393224 | tf_op jit(solution)/shard_map/ppermute | solution.py:188

commit v20 on v19

--- a/solution.py
+++ b/solution.py
@@ -52,10 +52,15 @@
         copy.wait()
 
 
-def prep_kernel(ids, here, table, after, x, y, turned, own, blank, zeros, sem, own_sem):
+def prep_kernel(ids, here, lengths, table, after, x, y, turned, own, live, blocks, blank, zeros, sem, own_sem):
     own_copy = pltpu.make_async_copy(table.at[ids[here[0]]], own, own_sem)
     own_copy.start()
     rows = own.shape[0]
+    marked = lax.broadcasted_iota(jnp.int32, live.shape, 0) < lengths[here[0]]
+    live[...] = jnp.where(marked, 1.0, 0.0)
+    for n in range(ids.shape[0]):
+        blocks[0, n] = ids[n]
+        blocks[1, n] = lengths[n]
     zeros[...] = jnp.zeros_like(zeros)
     step = zeros.shape[0]
     copies = [
@@ -89,21 +94,19 @@
     out[...] = jnp.where(low_lanes(tokens, width), x_rank, y_rank)
 
 
-def rounded(mine, other, length, scale):
+def rounded(mine, other, live, scale):
     total = mine[...] + other[...]
-    rows, width = total.shape
-    total = jnp.where(low_lanes(rows, width), total, scale * total)
-    live = lax.broadcasted_iota(jnp.int32, (rows, width), 0) < length
-    return jnp.where(live, total, 0.0)
+    total = jnp.where(low_lanes(*total.shape), total, scale * total)
+    return jnp.where(live[...] > 0.0, total, 0.0)
 
 
 def swap_halves(value):
     return pltpu.roll(value, value.shape[-1] // 2, 1)
 
 
-def piece_kernel(peers, scale, here, lengths, mine, other, turned, *refs):
+def piece_kernel(peers, scale, here, live, mine, other, turned, *refs):
     me = here[0]
-    both = swap_halves(rounded(mine, other, lengths[me], scale))
+    both = swap_halves(rounded(mine, other, live, scale))
     low = low_lanes(*both.shape)
     top = jnp.where(low, both, 0.0).astype(jnp.bfloat16)
     bottom = jnp.where(low, 0.0, both).astype(jnp.bfloat16)
@@ -113,10 +116,10 @@
         refs[n][...] = jnp.where(low_lanes(*piece.shape), piece, scale * piece).astype(jnp.bfloat16)
 
 
-def input_kernel(peers, scale, here, lengths, mine, other, *refs):
+def input_kernel(peers, scale, here, live, mine, other, *refs):
     pairs, out = refs[: len(peers)], refs[len(peers)]
     me = here[0]
-    both = swap_halves(rounded(mine, other, lengths[me], scale))
+    both = swap_halves(rounded(mine, other, live, scale))
     ranks = jnp.where(low_lanes(*both.shape), both, 0.0).astype(jnp.bfloat16)
     rows = pairs[0].shape[0]
     for n, k in enumerate(peers):
@@ -126,7 +129,7 @@
         ).astype(jnp.bfloat16)
 
 
-def merge_kernel(peers, handled, others, ids, here, lengths, *refs):
+def merge_kernel(peers, handled, others, blocks, here, *refs):
     pieces = dict(zip(peers, refs[:-5]))
     out, total, held, sems = refs[-4:]
     me = here[0]
@@ -141,9 +144,9 @@
 
     copies, chosen = [], []
     for n, k in enumerate(handled):
-        adapter = ids[me ^ k]
+        adapter = blocks[0, me ^ k]
         copies.append(pltpu.make_async_copy(held.at[n], out.at[adapter], sems.at[n]))
-        same = {other: ids[me ^ other] == adapter for other in (*handled, *others) if other != k}
+        same = {other: blocks[0, me ^ other] == adapter for other in (*handled, *others) if other != k}
         skip = either([same[other] for other in handled[:n]])
         adding = list(handled[n + 1 :])
         if others_here:
@@ -161,14 +164,14 @@
 
         @pl.when(chosen[n] & jnp.logical_not(more))
         def _():
-            store(value(k), lengths[me ^ k])
+            store(value(k), blocks[1, me ^ k])
 
         @pl.when(chosen[n] & more)
         def _():
             total[...] = value(k)
-            count = lengths[me ^ k]
+            count = blocks[1, me ^ k]
             for other in adding:
-                count += jnp.where(same[other], lengths[me ^ other], 0)
+                count += jnp.where(same[other], blocks[1, me ^ other], 0)
 
                 @pl.when(same[other])
                 def _():
@@ -222,22 +225,24 @@
     pairs = exchange(dict(zip(FETCH, sent)), FETCH_TIES)
 
     step = 8
-    turned, own, blank = call(
+    turned, own, live, blocks, blank = call(
         prep_kernel,
         [
             jax.ShapeDtypeStruct((owners, rows, 2 * tokens), bf16),
             straight,
+            jax.ShapeDtypeStruct((tokens, width), f32),
+            jax.ShapeDtypeStruct((2, owners), jnp.int32),
             jax.ShapeDtypeStruct(table.shape, bf16),
         ],
-        [in_smem, in_smem, in_hbm, in_hbm, in_vmem, in_vmem],
-        [in_vmem, in_vmem, in_hbm],
+        [in_smem, in_smem, in_smem, in_hbm, in_hbm, in_vmem, in_vmem],
+        [in_vmem, in_vmem, in_vmem, in_smem, in_hbm],
         [
             pltpu.VMEM((step, rows, width), bf16),
             pltpu.SemaphoreType.DMA((count // step,)),
             pltpu.SemaphoreType.DMA,
         ],
         moved=4 * token_bytes + 2 * count * rows * width,
-    )(ids, here, table, pairs[PREP_AFTER], activations, cotangent)
+    )(ids, here, lengths, table, pairs[PREP_AFTER], activations, cotangent)
     pairs[0] = own
 
     mine = jnp.zeros((tokens, width), f32)
@@ -257,21 +262,21 @@
         pieces += call(
             functools.partial(piece_kernel, part, scale),
             [straight] * len(part),
-            [in_smem] * 2 + [in_vmem] * 3,
+            [in_smem] + [in_vmem] * 4,
             [in_vmem] * len(part),
             moved=1024,
-        )(here, lengths, mine, other, turned)
+        )(here, live, mine, other, turned)
     arrived = exchange(dict(zip(SEND, pieces)), SEND_TIES)
     arrived[0] = pieces[-1]
 
     grad_input = call(
         functools.partial(input_kernel, tuple(pairs), scale),
         jax.ShapeDtypeStruct((tokens, features), bf16),
-        [in_smem] * 2 + [in_vmem] * (2 + owners),
+        [in_smem] + [in_vmem] * (3 + owners),
         in_vmem,
         flops=2 * tokens * features * width,
         moved=token_bytes + pair_bytes,
-    )(here, lengths, lax.optimization_barrier((mine, *pieces))[0], other, *pairs.values())
+    )(here, live, lax.optimization_barrier((mine, *pieces))[0], other, *pairs.values())
 
     late = tuple(k for k in peers if k in LATE)
     early = tuple(k for k in peers if k not in LATE)
@@ -280,7 +285,7 @@
         return call(
             functools.partial(merge_kernel, tuple(merged), handled, others),
             jax.ShapeDtypeStruct(table.shape, bf16),
-            [in_smem] * 3 + [in_vmem] * len(merged) + [in_hbm],
+            [in_smem] * 2 + [in_vmem] * len(merged) + [in_hbm],
             in_hbm,
             [
                 pltpu.VMEM((rows, width), f32),
@@ -288,8 +293,8 @@
                 pltpu.SemaphoreType.DMA((len(handled),)),
             ],
             moved=2 * pair_bytes,
-            aliases={3 + len(merged): 0},
-        )(ids, here, lengths, *merged.values(), so_far)
+            aliases={2 + len(merged): 0},
+        )(blocks, here, *merged.values(), so_far)
 
     early_pieces = {k: arrived[k] for k in early}
     gradient = merge(late, early, arrived, merge(early, late, early_pieces, blank))

time: 58.9 us -> 57.9 us (0.983)
  Pallas kernels: 16.5 us -> 15.5 us
  waiting for transfers between devices: 13 us -> 12.3 us
  starting transfers between devices: 27.9 us -> 28.5 us
    pallas_call x2, Pallas kernels: 2.09 us -> 1.02 us  [with_kernels(): call(functools.partial(piece_kernel, part, scale), [straight] * len(part)...]
    ppermute x14, waiting for transfers between devices: 11.8 us -> 11.1 us  [exchange(): out[k] = lax.ppermute(piece, 'dp', [(i, i ^ k) for i in range(owners)])]
    pallas_call x1, Pallas kernels: 5.35 us -> 5.95 us  [with_kernels(): call(prep_kernel, [jax.ShapeDtypeStruct((owners, rows, 2 * tokens), bf16)...]
where the time goes in v20:
time: 57.9 us; the launch traced here: 57.7 us
  starting transfers between devices  28.5 us (49%)
  Pallas kernels  15.5 us (27%)
  waiting for transfers between devices  12.3 us (21%)
  between operations  0.74 us (1%)
  local copies, waits for them, and re-layouts  0.66 us (1%)
    ppermute x14, starting transfers between devices, exchange(): out[k] = lax.ppermute(piece, 'dp', [(i, i ^ k) for i in range(owners)])  28.4 us
    ppermute x14, waiting for transfers between devices, exchange(): out[k] = lax.ppermute(piece, 'dp', [(i, i ^ k) for i in range(owners)])  11.1 us
    pallas_call x1, Pallas kernels, with_kernels(): call(prep_kernel, [jax.ShapeDtypeStruct((owners, rows, 2 * tokens), bf16)...  5.95 us
    pallas_call x2, Pallas kernels, with_kernels(): call(functools.partial(gather_kernel, part), [straight] * len(part), [in_...  3.35 us
    pallas_call x2, Pallas kernels, merge(): call(functools.partial(merge_kernel, tuple(merged), handled, others), jax...  2.85 us
    pallas_call x1, Pallas kernels, with_kernels(): call(functools.partial(input_kernel, tuple(pairs), scale), jax.ShapeDtype...  1.45 us
    ppermute x1, waiting for transfers between devices, across_cores(): return lax.ppermute(value, 'tensor', [(i, i ^ 1) for i in range(cores)])  1.24 us
  transfers between devices with their start and end apart: 15, of which 5 were waited for; matrix products, arithmetic and copies ran while one was open for 0% of the time, Pallas kernels for 21%

profile of v20, /device:TPU:0, one launch (start us, length us, event | category | flops | bytes accessed | tf_op | source)
XLA Modules:
  0.0 57.7 jit_solution(13050365170823778166)
XLA Ops:
  0.6 0.6 %copy-done.2 = s32[8,1]{0,1:T(1,128)S(1)} copy-done((s32[8,1]{0,1:T(1,128)S(1)}, s32[8,1]{0,1:T(1,128)}, u32[]{:S(2)}) %copy-start.2) | copy-done | bytes 56
  1.3 1.6 %shard_map.68 = bf16[512,128]{1,0:T(8,128)(2,1)S(1)} custom-call(s32[8]{0:T(128)S(1)} %bitcast.7, s32[1]{0:T(128)} %bitcast.here, bf16[96,512,128]{2,1,0:T(8,128)(2,1)} %bitcast.11), custom_call_target="tpu_custom_call" | custom-call | bytes 1024 | tf_op jit(solution)/shard_map/pallas_call | solution.py:215
  2.9 4.1 %collective-permute-start.1 = (bf16[512,128]{1,0:T(8,128)(2,1)S(1)}, bf16[512,128]{1,0:T(8,128)(2,1)S(1)}, u32[]{:S(2)}, u32[]{:S(2)}) collective-permute-start(bf16[512,128]{1,0:T(8,128)(2,1)S(1)} %shard_map.68), channel_id=1, source_target_pairs={{0,8},{2,10},{4,12},{6,14},{8,0},{10,2},{12,4},{14,6},{1,9},{3,11}... | collective-permute-start | bytes 393224 | tf_op jit(solution)/shard_map/ppermute | solution.py:191
  7.0 1.8 %shard_map.69 = (bf16[512,128]{1,0:T(8,128)(2,1)S(1)}, bf16[512,128]{1,0:T(8,128)(2,1)S(1)}, bf16[512,128]{1,0:T(8,128)(2,1)S(1)}, bf16[512,128]{1,0:T(8,128)(2,...) custom-call(s32[8]{0:T(128)S(1)} %bitcast.8, s32[1]{0:T(128)} %bitcast.here, ...), custom_call_target="tpu_custom_call" | custom-call | bytes 1024 | tf_op jit(solution)/shard_map/pallas_call | solution.py:215
  8.8 1.6 %collective-permute-start = (bf16[512,128]{1,0:T(8,128)(2,1)S(1)}, bf16[512,128]{1,0:T(8,128)(2,1)S(1)}, u32[]{:S(2)}, u32[]{:S(2)}) collective-permute-start(bf16[512,128]{1,0:T(8,128)(2,1)S(1)} %get-tuple-element.25), channel_id=1, source_target_pairs={{0,2},{2,0},{4,6},{6,4},{8,10},{10,8},{12,14},{14,12},{1,3},{3,1},... | collective-permute-start | bytes 393224 | tf_op jit(solution)/shard_map/ppermute | solution.py:191
  10.3 1.6 %collective-permute-start.2 = (bf16[512,128]{1,0:T(8,128)(2,1)S(1)}, bf16[512,128]{1,0:T(8,128)(2,1)S(1)}, u32[]{:S(2)}, u32[]{:S(2)}) collective-permute-start(bf16[512,128]{1,0:T(8,128)(2,1)S(1)} %get-tuple-element.29), channel_id=1, source_target_pairs={{0,4},{2,6},{4,0},{6,2},{8,12},{10,14},{12,8},{14,10},{1,5},{3,7},... | collective-permute-start | bytes 393224 | tf_op jit(solution)/shard_map/ppermute | solution.py:191
  11.9 0.3 collective-permute-start.3
  12.2 2.5 %collective-permute-start.4 = (bf16[512,128]{1,0:T(8,128)(2,1)S(1)}, bf16[512,128]{1,0:T(8,128)(2,1)S(1)}, u32[]{:S(2)}, u32[]{:S(2)}) collective-permute-start(bf16[512,128]{1,0:T(8,128)(2,1)S(1)} %get-tuple-element.31), channel_id=1, source_target_pairs={{0,12},{2,14},{4,8},{6,10},{8,4},{10,6},{12,0},{14,2},{1,13},{3,15... | collective-permute-start | bytes 393224 | tf_op jit(solution)/shard_map/ppermute | solution.py:191
  14.7 1.6 %collective-permute-start.5 = (bf16[512,128]{1,0:T(8,128)(2,1)S(1)}, bf16[512,128]{1,0:T(8,128)(2,1)S(1)}, u32[]{:S(2)}, u32[]{:S(2)}) collective-permute-start(bf16[512,128]{1,0:T(8,128)(2,1)S(1)} %get-tuple-element.33), channel_id=1, source_target_pairs={{0,6},{2,4},{4,2},{6,0},{8,14},{10,12},{12,10},{14,8},{1,7},{3,5},... | collective-permute-start | bytes 393224 | tf_op jit(solution)/shard_map/ppermute | solution.py:191
  16.3 2.8 %collective-permute-start.6 = (bf16[512,128]{1,0:T(8,128)(2,1)S(1)}, bf16[512,128]{1,0:T(8,128)(2,1)S(1)}, u32[]{:S(2)}, u32[]{:S(2)}) collective-permute-start(bf16[512,128]{1,0:T(8,128)(2,1)S(1)} %get-tuple-element.34), channel_id=1, source_target_pairs={{0,14},{2,12},{4,10},{6,8},{8,6},{10,4},{12,2},{14,0},{1,15},{3,13... | collective-permute-start | bytes 393224 | tf_op jit(solution)/shard_map/ppermute | solution.py:191
  19.1 5.9 %shard_map.70 = (bf16[8,512,256]{2,1,0:T(8,128)(2,1)S(1)}, bf16[512,128]{1,0:T(8,128)(2,1)S(1)}, f32[128,128]{1,0:T(8,128)S(1)}, s32[2,8]{1,0:T(2,128)S(1)}, bf16[96,512,128]{2,1,0:T(8,128)(2,1)}) custom-call(s32[8]{0:T(128)S(1)} %bitcast.9, s32[1]{0:T(128)} %bitcast.here, s32[8]{0:T(128)S(1)} %bitcast.10, bf16[96,512,128]{2,1,0:T(8,128)(2,1)} %bitcast.13, ...), custom_call_target="tpu_custom_call" | custom-call | bytes 16777216 | tf_op jit(solution)/shard_map/pallas_call | solution.py:228
  25.1 0.0 collective-permute-done.2.refs_2_
  25.1 1.6 %collective-permute-done.3.refs_3_ = bf16[512,128]{1,0:T(8,128)(2,1)S(1)} collective-permute-done((bf16[512,128]{1,0:T(8,128)(2,1)S(1)}, bf16[512,128]{1,0:T(8,128)(2,1)S(1)}, u32[]{:S(2)}, u32[]{:S(2)}) %collective-permute-start.3) | collective-permute-done | bytes 131104 | tf_op jit(solution)/shard_map/ppermute | solution.py:191
  26.7 0.0 collective-permute-done.4.refs_4_
  26.7 0.6 shard_map.71.so_far
  27.3 0.6 collective-permute-done.5.refs_0_.refs_5_
  27.8 0.3 shard_map.72.mine
  28.1 0.1 collective-permute-start.7
  28.2 1.2 %collective-permute-done.7.other = f32[128,128]{1,0:T(8,128)S(1)} collective-permute-done((f32[128,128]{1,0:T(8,128)S(1)}, f32[128,128]{1,0:T(8,128)S(1)}, u32[]{:S(2)}, u32[]{:S(2)}) %collective-permute-start.7) | collective-permute-done | bytes 65568 | tf_op jit(solution)/shard_map/ppermute | solution.py:197
  29.5 0.3 shard_map.73
  29.8 2.7 %collective-permute-start.8 = (bf16[512,128]{1,0:T(8,128)(2,1)S(1)}, bf16[512,128]{1,0:T(8,128)(2,1)S(1)}, u32[]{:S(2)}, u32[]{:S(2)}) collective-permute-start(bf16[512,128]{1,0:T(8,128)(2,1)S(1)} %shard_map.73), channel_id=1, source_target_pairs={{0,12},{2,14},{4,8},{6,10},{8,4},{10,6},{12,0},{14,2},{1,13},{3,15... | collective-permute-start | bytes 393224 | tf_op jit(solution)/shard_map/ppermute | solution.py:191
  32.5 0.7 %shard_map.74 = (bf16[512,128]{1,0:T(8,128)(2,1)S(1)}, bf16[512,128]{1,0:T(8,128)(2,1)S(1)}, bf16[512,128]{1,0:T(8,128)(2,1)S(1)}, bf16[512,128]{1,0:T(8,128)(2,...) custom-call(s32[1]{0:T(128)} %bitcast.here, ...), custom_call_target="tpu_custom_call" | custom-call | bytes 1024 | tf_op jit(solution)/shard_map/pallas_call | solution.py:262
  33.2 1.3 %collective-permute-start.9 = (bf16[512,128]{1,0:T(8,128)(2,1)S(1)}, bf16[512,128]{1,0:T(8,128)(2,1)S(1)}, u32[]{:S(2)}, u32[]{:S(2)}) collective-permute-start(bf16[512,128]{1,0:T(8,128)(2,1)S(1)} %get-tuple-element.35), channel_id=1, source_target_pairs={{0,2},{2,0},{4,6},{6,4},{8,10},{10,8},{12,14},{14,12},{1,3},{3,1},... | collective-permute-start | bytes 393224 | tf_op jit(solution)/shard_map/ppermute | solution.py:191
  34.5 3.1 %collective-permute-start.10 = (bf16[512,128]{1,0:T(8,128)(2,1)S(1)}, bf16[512,128]{1,0:T(8,128)(2,1)S(1)}, u32[]{:S(2)}, u32[]{:S(2)}) collective-permute-start(bf16[512,128]{1,0:T(8,128)(2,1)S(1)} %get-tuple-element.36), channel_id=1, source_target_pairs={{0,4},{2,6},{4,0},{6,2},{8,12},{10,14},{12,8},{14,10},{1,5},{3,7},... | collective-permute-start | bytes 393224 | tf_op jit(solution)/shard_map/ppermute | solution.py:191
  37.6 3.8 %collective-permute-start.12 = (bf16[512,128]{1,0:T(8,128)(2,1)S(1)}, bf16[512,128]{1,0:T(8,128)(2,1)S(1)}, u32[]{:S(2)}, u32[]{:S(2)}) collective-permute-start(bf16[512,128]{1,0:T(8,128)(2,1)S(1)} %get-tuple-element.38), channel_id=1, source_target_pairs={{0,10},{2,8},{4,14},{6,12},{8,2},{10,0},{12,6},{14,4},{1,11},{3,9}... | collective-permute-start | bytes 393224 | tf_op jit(solution)/shard_map/ppermute | solution.py:191
  41.5 3.0 %collective-permute-start.14 = (bf16[512,128]{1,0:T(8,128)(2,1)S(1)}, bf16[512,128]{1,0:T(8,128)(2,1)S(1)}, u32[]{:S(2)}, u32[]{:S(2)}) collective-permute-start(bf16[512,128]{1,0:T(8,128)(2,1)S(1)} %get-tuple-element.44), channel_id=1, source_target_pairs={{0,14},{2,12},{4,10},{6,8},{8,6},{10,4},{12,2},{14,0},{1,15},{3,13... | collective-permute-start | bytes 393224 | tf_op jit(solution)/shard_map/ppermute | solution.py:191
  44.4 1.5 %shard_map.75 = bf16[128,4096]{1,0:T(8,128)(2,1)} custom-call(s32[1]{0:T(128)} %bitcast.here, f32[128,128]{1,0:T(8,128)S(1)} %get-tuple-element.26.live, f32[128,128]{1,0:T(8,128)S(1)} %shard_map.72.mine, f32[128,128]{1,0:T(8,128)S(1)} %collective-permute-done.7.other, bf16[512,128]{1,0:T(8,128)(2,1)S(1)} %collective-permute-done.1.refs_0_, ...), custom_call_target="tpu_custom_call" | custom-call | flops 134217728 | bytes 2097152 | tf_op jit(solution)/shard_map/pallas_call | solution.py:272
  45.9 0.0 collective-permute-done.10.refs_2_
  45.9 4.7 %collective-permute-done.11.refs_3_ = bf16[512,128]{1,0:T(8,128)(2,1)S(1)} collective-permute-done((bf16[512,128]{1,0:T(8,128)(2,1)S(1)}, bf16[512,128]{1,0:T(8,128)(2,1)S(1)}, u32[]{:S(2)}, u32[]{:S(2)}) %collective-permute-start.11) | collective-permute-done | bytes 131104 | tf_op jit(solution)/shard_map/ppermute | solution.py:191
  50.6 1.5 %shard_map.76.refs_8_ = bf16[96,512,128]{2,1,0:T(8,128)(2,1)} custom-call(s32[2,8]{1,0:T(2,128)S(1)} %get-tuple-element.43.blocks, s32[1]{0:T(128)} %bitcast.here, bf16[512,128]{1,0:T(8,128)(2,1)S(1)} %collective-permute-done.8.refs_0_, bf16[512,128]{1,0:T(8,128)(2,1)S(1)} %collective-permute-done.9.refs_1_, ...), custom_call_target="tpu_custom_call", output_to_operand_aliasing={{}: (7, {})} | custom-call | bytes 2097152 | tf_op jit(solution)/shard_map/pallas_call | solution.py:285
  52.1 4.2 %collective-permute-done.12.refs_4_ = bf16[512,128]{1,0:T(8,128)(2,1)S(1)} collective-permute-done((bf16[512,128]{1,0:T(8,128)(2,1)S(1)}, bf16[512,128]{1,0:T(8,128)(2,1)S(1)}, u32[]{:S(2)}, u32[]{:S(2)}) %collective-permute-start.12) | collective-permute-done | bytes 131104 | tf_op jit(solution)/shard_map/ppermute | solution.py:191
  56.3 1.4 %shard_map.77 = bf16[96,512,128]{2,1,0:T(8,128)(2,1)} custom-call(s32[2,8]{1,0:T(2,128)S(1)} %get-tuple-element.43.blocks, s32[1]{0:T(128)} %bitcast.here, bf16[512,128]{1,0:T(8,128)(2,1)S(1)} %collective-permute-done.8.refs_0_, bf16[512,128]{1,0:T(8,128)(2,1)S(1)} %collective-permute-done.9.refs_1_, ...), custom_call_target="tpu_custom_call", output_to_operand_aliasing={{}: (10, {})} | custom-call | bytes 2097152 | tf_op jit(solution)/shard_map/pallas_call | solution.py:285
  (17 shorter events, 0.0 us)
Async XLA Ops:
  0.6 0.7 %copy-start.2 = (s32[8,1]{0,1:T(1,128)S(1)}, s32[8,1]{0,1:T(1,128)}, u32[]{:S(2)}) copy-start(s32[8,1]{0,1:T(1,128)} %param.8) | copy-start | bytes 100
  1.3 17.8 %copy-start = (bf16[128,4096]{1,0:T(8,128)(2,1)S(1)}, bf16[128,4096]{1,0:T(8,128)(2,1)}, u32[]{:S(2)}) copy-start(bf16[128,4096]{1,0:T(8,128)(2,1)} %x.3) | copy-start | bytes 3145732
  1.3 17.8 %copy-start.1 = (bf16[128,4096]{1,0:T(8,128)(2,1)S(1)}, bf16[128,4096]{1,0:T(8,128)(2,1)}, u32[]{:S(2)}) copy-start(bf16[128,4096]{1,0:T(8,128)(2,1)} %y.5) | copy-start | bytes 3145732
  1.3 17.8 %copy-start.3 = (s32[8,1]{0,1:T(1,128)S(1)}, s32[8,1]{0,1:T(1,128)}, u32[]{:S(2)}) copy-start(s32[8,1]{0,1:T(1,128)} %param.9) | copy-start | bytes 100
  2.9 11.8 %collective-permute-start.1 = (bf16[512,128]{1,0:T(8,128)(2,1)S(1)}, bf16[512,128]{1,0:T(8,128)(2,1)S(1)}, u32[]{:S(2)}, u32[]{:S(2)}) collective-permute-start(bf16[512,128]{1,0:T(8,128)(2,1)S(1)} %shard_map.68), channel_id=1, source_target_pairs={{0,8},{2,10},{4,12},{6,14},{8,0},{10,2},{12,4},{14,6},{1,9},{3,11}... | collective-permute-start | bytes 393224 | tf_op jit(solution)/shard_map/ppermute | solution.py:191
  8.8 7.5 %collective-permute-start = (bf16[512,128]{1,0:T(8,128)(2,1)S(1)}, bf16[512,128]{1,0:T(8,128)(2,1)S(1)}, u32[]{:S(2)}, u32[]{:S(2)}) collective-permute-start(bf16[512,128]{1,0:T(8,128)(2,1)S(1)} %get-tuple-element.25), channel_id=1, source_target_pairs={{0,2},{2,0},{4,6},{6,4},{8,10},{10,8},{12,14},{14,12},{1,3},{3,1},... | collective-permute-start | bytes 393224 | tf_op jit(solution)/shard_map/ppermute | solution.py:191
  10.3 14.8 %collective-permute-start.2 = (bf16[512,128]{1,0:T(8,128)(2,1)S(1)}, bf16[512,128]{1,0:T(8,128)(2,1)S(1)}, u32[]{:S(2)}, u32[]{:S(2)}) collective-permute-start(bf16[512,128]{1,0:T(8,128)(2,1)S(1)} %get-tuple-element.29), channel_id=1, source_target_pairs={{0,4},{2,6},{4,0},{6,2},{8,12},{10,14},{12,8},{14,10},{1,5},{3,7},... | collective-permute-start | bytes 393224 | tf_op jit(solution)/shard_map/ppermute | solution.py:191
  11.9 14.8 %collective-permute-start.3 = (bf16[512,128]{1,0:T(8,128)(2,1)S(1)}, bf16[512,128]{1,0:T(8,128)(2,1)S(1)}, u32[]{:S(2)}, u32[]{:S(2)}) collective-permute-start(bf16[512,128]{1,0:T(8,128)(2,1)S(1)} %get-tuple-element.30), channel_id=1, source_target_pairs={{0,10},{2,8},{4,14},{6,12},{8,2},{10,0},{12,6},{14,4},{1,11},{3,9}... | collective-permute-start | bytes 393224 | tf_op jit(solution)/shard_map/ppermute | solution.py:191
  12.2 14.5 %collective-permute-start.4 = (bf16[512,128]{1,0:T(8,128)(2,1)S(1)}, bf16[512,128]{1,0:T(8,128)(2,1)S(1)}, u32[]{:S(2)}, u32[]{:S(2)}) collective-permute-start(bf16[512,128]{1,0:T(8,128)(2,1)S(1)} %get-tuple-element.31), channel_id=1, source_target_pairs={{0,12},{2,14},{4,8},{6,10},{8,4},{10,6},{12,0},{14,2},{1,13},{3,15... | collective-permute-start | bytes 393224 | tf_op jit(solution)/shard_map/ppermute | solution.py:191
  14.7 13.1 %collective-permute-start.5 = (bf16[512,128]{1,0:T(8,128)(2,1)S(1)}, bf16[512,128]{1,0:T(8,128)(2,1)S(1)}, u32[]{:S(2)}, u32[]{:S(2)}) collective-permute-start(bf16[512,128]{1,0:T(8,128)(2,1)S(1)} %get-tuple-element.33), channel_id=1, source_target_pairs={{0,6},{2,4},{4,2},{6,0},{8,14},{10,12},{12,10},{14,8},{1,7},{3,5},... | collective-permute-start | bytes 393224 | tf_op jit(solution)/shard_map/ppermute | solution.py:191
  16.3 11.5 %collective-permute-start.6 = (bf16[512,128]{1,0:T(8,128)(2,1)S(1)}, bf16[512,128]{1,0:T(8,128)(2,1)S(1)}, u32[]{:S(2)}, u32[]{:S(2)}) collective-permute-start(bf16[512,128]{1,0:T(8,128)(2,1)S(1)} %get-tuple-element.34), channel_id=1, source_target_pairs={{0,14},{2,12},{4,10},{6,8},{8,6},{10,4},{12,2},{14,0},{1,15},{3,13... | collective-permute-start | bytes 393224 | tf_op jit(solution)/shard_map/ppermute | solution.py:191
  28.1 1.3 %collective-permute-start.7 = (f32[128,128]{1,0:T(8,128)S(1)}, f32[128,128]{1,0:T(8,128)S(1)}, u32[]{:S(2)}, u32[]{:S(2)}) collective-permute-start(f32[128,128]{1,0:T(8,128)S(1)} %shard_map.72.mine), channel_id=1, source_target_pairs={{0,1},{1,0},{2,3},{3,2},{4,5},{5,4},{6,7},{7,6},{8,9},{9,8},{10,11... | collective-permute-start | bytes 196616 | tf_op jit(solution)/shard_map/ppermute | solution.py:197
  29.8 11.7 %collective-permute-start.8 = (bf16[512,128]{1,0:T(8,128)(2,1)S(1)}, bf16[512,128]{1,0:T(8,128)(2,1)S(1)}, u32[]{:S(2)}, u32[]{:S(2)}) collective-permute-start(bf16[512,128]{1,0:T(8,128)(2,1)S(1)} %shard_map.73), channel_id=1, source_target_pairs={{0,12},{2,14},{4,8},{6,10},{8,4},{10,6},{12,0},{14,2},{1,13},{3,15... | collective-permute-start | bytes 393224 | tf_op jit(solution)/shard_map/ppermute | solution.py:191
  33.2 8.2 %collective-permute-start.9 = (bf16[512,128]{1,0:T(8,128)(2,1)S(1)}, bf16[512,128]{1,0:T(8,128)(2,1)S(1)}, u32[]{:S(2)}, u32[]{:S(2)}) collective-permute-start(bf16[512,128]{1,0:T(8,128)(2,1)S(1)} %get-tuple-element.35), channel_id=1, source_target_pairs={{0,2},{2,0},{4,6},{6,4},{8,10},{10,8},{12,14},{14,12},{1,3},{3,1},... | collective-permute-start | bytes 393224 | tf_op jit(solution)/shard_map/ppermute | solution.py:191
  34.5 11.4 %collective-permute-start.10 = (bf16[512,128]{1,0:T(8,128)(2,1)S(1)}, bf16[512,128]{1,0:T(8,128)(2,1)S(1)}, u32[]{:S(2)}, u32[]{:S(2)}) collective-permute-start(bf16[512,128]{1,0:T(8,128)(2,1)S(1)} %get-tuple-element.36), channel_id=1, source_target_pairs={{0,4},{2,6},{4,0},{6,2},{8,12},{10,14},{12,8},{14,10},{1,5},{3,7},... | collective-permute-start | bytes 393224 | tf_op jit(solution)/shard_map/ppermute | solution.py:191
  37.6 13.0 %collective-permute-start.11 = (bf16[512,128]{1,0:T(8,128)(2,1)S(1)}, bf16[512,128]{1,0:T(8,128)(2,1)S(1)}, u32[]{:S(2)}, u32[]{:S(2)}) collective-permute-start(bf16[512,128]{1,0:T(8,128)(2,1)S(1)} %get-tuple-element.37), channel_id=1, source_target_pairs={{0,8},{2,10},{4,12},{6,14},{8,0},{10,2},{12,4},{14,6},{1,9},{3,11}... | collective-permute-start | bytes 393224 | tf_op jit(solution)/shard_map/ppermute | solution.py:191
  37.6 18.7 %collective-permute-start.12 = (bf16[512,128]{1,0:T(8,128)(2,1)S(1)}, bf16[512,128]{1,0:T(8,128)(2,1)S(1)}, u32[]{:S(2)}, u32[]{:S(2)}) collective-permute-start(bf16[512,128]{1,0:T(8,128)(2,1)S(1)} %get-tuple-element.38), channel_id=1, source_target_pairs={{0,10},{2,8},{4,14},{6,12},{8,2},{10,0},{12,6},{14,4},{1,11},{3,9}... | collective-permute-start | bytes 393224 | tf_op jit(solution)/shard_map/ppermute | solution.py:191
  41.4 14.9 %collective-permute-start.13 = (bf16[512,128]{1,0:T(8,128)(2,1)S(1)}, bf16[512,128]{1,0:T(8,128)(2,1)S(1)}, u32[]{:S(2)}, u32[]{:S(2)}) collective-permute-start(bf16[512,128]{1,0:T(8,128)(2,1)S(1)} %get-tuple-element.39), channel_id=1, source_target_pairs={{0,6},{2,4},{4,2},{6,0},{8,14},{10,12},{12,10},{14,8},{1,7},{3,5},... | collective-permute-start | bytes 393224 | tf_op jit(solution)/shard_map/ppermute | solution.py:191
  41.5 14.9 %collective-permute-start.14 = (bf16[512,128]{1,0:T(8,128)(2,1)S(1)}, bf16[512,128]{1,0:T(8,128)(2,1)S(1)}, u32[]{:S(2)}, u32[]{:S(2)}) collective-permute-start(bf16[512,128]{1,0:T(8,128)(2,1)S(1)} %get-tuple-element.44), channel_id=1, source_target_pairs={{0,14},{2,12},{4,10},{6,8},{8,6},{10,4},{12,2},{14,0},{1,15},{3,13... | collective-permute-start | bytes 393224 | tf_op jit(solution)/shard_map/ppermute | solution.py:191

commit v21 on v20

--- a/solution.py
+++ b/solution.py
@@ -8,7 +8,7 @@
 from jax.sharding import PartitionSpec as P
 
 adapter_alpha = 128.0
-FETCH = (4, 1, 2, 5, 6, 3, 7)
+FETCH = (4, 1, 2, 6, 5, 3, 7)
 FETCH_TIES = {}
 SEND = (6, 1, 2, 4, 5, 3, 7)
 SEND_TIES = {7: 6}
@@ -52,15 +52,19 @@
         copy.wait()
 
 
-def prep_kernel(ids, here, lengths, table, after, x, y, turned, own, live, blocks, blank, zeros, sem, own_sem):
+def prep_kernel(ids, here, lengths, table, after, x, y, turned, own, live, parts, blocks, blank, zeros, sem, own_sem):
     own_copy = pltpu.make_async_copy(table.at[ids[here[0]]], own, own_sem)
     own_copy.start()
     rows = own.shape[0]
     marked = lax.broadcasted_iota(jnp.int32, live.shape, 0) < lengths[here[0]]
     live[...] = jnp.where(marked, 1.0, 0.0)
     for n in range(ids.shape[0]):
-        blocks[0, n] = ids[n]
-        blocks[1, n] = lengths[n]
+        blocks[n] = ids[n]
+        count = jnp.int32(0)
+        for other in range(ids.shape[0]):
+            count += jnp.where(ids[other] == ids[n], lengths[other], 0)
+        denom = jnp.maximum(count.astype(jnp.float32), 1.0)
+        parts[n : n + 1] = 1.0 / jnp.full((1, parts.shape[1]), denom)
     zeros[...] = jnp.zeros_like(zeros)
     step = zeros.shape[0]
     copies = [
@@ -129,24 +133,31 @@
         ).astype(jnp.bfloat16)
 
 
-def merge_kernel(peers, handled, others, blocks, here, *refs):
-    pieces = dict(zip(peers, refs[:-5]))
-    out, total, held, sems = refs[-4:]
+def merge_kernel(peers, handled, others, blocks, here, parts, *refs):
+    pieces = dict(zip(peers, refs[:-7]))
+    out, total, held, sems, ids, ids_sem = refs[-6:]
     me = here[0]
-    width = total.shape[1]
     others_here = all(k in pieces for k in others)
+    ids_copy = pltpu.make_async_copy(blocks, ids, ids_sem)
+    ids_copy.start()
 
     def value(k):
         return pieces[k][...].astype(jnp.float32)
 
+    def store(n, sum_of):
+        held[n] = (sum_of * parts[pl.ds(me ^ handled[n], 1), :]).astype(jnp.bfloat16)
+
     def either(conditions):
         return functools.reduce(jnp.logical_or, conditions, jnp.bool_(False))
 
+    for n, k in enumerate(handled):
+        store(n, value(k))
+    ids_copy.wait()
     copies, chosen = [], []
     for n, k in enumerate(handled):
-        adapter = blocks[0, me ^ k]
+        adapter = ids[me ^ k]
         copies.append(pltpu.make_async_copy(held.at[n], out.at[adapter], sems.at[n]))
-        same = {other: blocks[0, me ^ other] == adapter for other in (*handled, *others) if other != k}
+        same = {other: ids[me ^ other] == adapter for other in (*handled, *others) if other != k}
         skip = either([same[other] for other in handled[:n]])
         adding = list(handled[n + 1 :])
         if others_here:
@@ -156,28 +167,18 @@
         more = either([same[other] for other in adding])
         chosen.append(jnp.logical_not(skip))
 
-        def store(sum_of, count):
-            denom = jnp.maximum(count.astype(jnp.float32), 1.0)
-            part = 1.0 / jnp.full((1, width), denom)
-            held[n] = (sum_of * part).astype(jnp.bfloat16)
-            copies[n].start()
-
-        @pl.when(chosen[n] & jnp.logical_not(more))
-        def _():
-            store(value(k), blocks[1, me ^ k])
-
         @pl.when(chosen[n] & more)
         def _():
             total[...] = value(k)
-            count = blocks[1, me ^ k]
             for other in adding:
-                count += jnp.where(same[other], blocks[1, me ^ other], 0)
 
                 @pl.when(same[other])
                 def _():
                     total[...] += value(other)
 
-            store(total[...], count)
+            store(n, total[...])
+
+        pl.when(chosen[n])(copies[n].start)
 
     for n in range(len(handled)):
         pl.when(chosen[n])(copies[n].wait)
@@ -225,17 +226,18 @@
     pairs = exchange(dict(zip(FETCH, sent)), FETCH_TIES)
 
     step = 8
-    turned, own, live, blocks, blank = call(
+    turned, own, live, parts, blocks, blank = call(
         prep_kernel,
         [
             jax.ShapeDtypeStruct((owners, rows, 2 * tokens), bf16),
             straight,
             jax.ShapeDtypeStruct((tokens, width), f32),
-            jax.ShapeDtypeStruct((2, owners), jnp.int32),
+            jax.ShapeDtypeStruct((owners, width), f32),
+            jax.ShapeDtypeStruct((owners,), jnp.int32),
             jax.ShapeDtypeStruct(table.shape, bf16),
         ],
         [in_smem, in_smem, in_smem, in_hbm, in_hbm, in_vmem, in_vmem],
-        [in_vmem, in_vmem, in_vmem, in_smem, in_hbm],
+        [in_vmem, in_vmem, in_vmem, in_vmem, in_smem, in_hbm],
         [
             pltpu.VMEM((step, rows, width), bf16),
             pltpu.SemaphoreType.DMA((count // step,)),
@@ -285,16 +287,18 @@
         return call(
             functools.partial(merge_kernel, tuple(merged), handled, others),
             jax.ShapeDtypeStruct(table.shape, bf16),
-            [in_smem] * 2 + [in_vmem] * len(merged) + [in_hbm],
+            [in_hbm, in_smem, in_vmem] + [in_vmem] * len(merged) + [in_hbm],
             in_hbm,
             [
                 pltpu.VMEM((rows, width), f32),
                 pltpu.VMEM((len(handled), rows, width), bf16),
                 pltpu.SemaphoreType.DMA((len(handled),)),
+                pltpu.SMEM((owners,), jnp.int32),
+                pltpu.SemaphoreType.DMA,
             ],
             moved=2 * pair_bytes,
-            aliases={2 + len(merged): 0},
-        )(blocks, here, *merged.values(), so_far)
+            aliases={3 + len(merged): 0},
+        )(blocks, here, parts, *merged.values(), so_far)
 
     early_pieces = {k: arrived[k] for k in early}
     gradient = merge(late, early, arrived, merge(early, late, early_pieces, blank))

time: 57.9 us -> 58.4 us (level)
  starting transfers between devices: 28.5 us -> 29.2 us
    ppermute x14, starting transfers between devices: 28.4 us -> 29.1 us  [exchange(): out[k] = lax.ppermute(piece, 'dp', [(i, i ^ k) for i in range(owners)])]
  transfers between devices with their start and end apart: 15 -> 15, of which waited for: 5 -> 4; matrix products, arithmetic and copies ran while one was open for 0% -> 0% of each run, Pallas kernels for 21% -> 20%
where the time goes in v21:
time: 58.4 us; the launch traced here: 58.1 us
  starting transfers between devices  29.2 us (50%)
  Pallas kernels  15.4 us (26%)
  waiting for transfers between devices  12 us (21%)
  between operations  0.76 us (1%)
  local copies, waits for them, and re-layouts  0.66 us (1%)
    ppermute x14, starting transfers between devices, exchange(): out[k] = lax.ppermute(piece, 'dp', [(i, i ^ k) for i in range(owners)])  29.1 us
    ppermute x14, waiting for transfers between devices, exchange(): out[k] = lax.ppermute(piece, 'dp', [(i, i ^ k) for i in range(owners)])  10.8 us
    pallas_call x1, Pallas kernels, with_kernels(): call(prep_kernel, [jax.ShapeDtypeStruct((owners, rows, 2 * tokens), bf16)...  5.94 us
    pallas_call x2, Pallas kernels, with_kernels(): call(functools.partial(gather_kernel, part), [straight] * len(part), [in_...  3.35 us
    pallas_call x2, Pallas kernels, merge(): call(functools.partial(merge_kernel, tuple(merged), handled, others), jax...  2.84 us
    pallas_call x1, Pallas kernels, with_kernels(): call(functools.partial(input_kernel, tuple(pairs), scale), jax.ShapeDtype...  1.45 us
    ppermute x1, waiting for transfers between devices, across_cores(): return lax.ppermute(value, 'tensor', [(i, i ^ 1) for i in range(cores)])  1.24 us
  transfers between devices with their start and end apart: 15, of which 4 were waited for; matrix products, arithmetic and copies ran while one was open for 0% of the time, Pallas kernels for 20%

profile of v21, /device:TPU:0, one launch (start us, length us, event | category | flops | bytes accessed | tf_op | source)
XLA Modules:
  0.0 58.1 jit_solution(4008908325343162737)
XLA Ops:
  0.6 0.6 %copy-done.2 = s32[8,1]{0,1:T(1,128)S(1)} copy-done((s32[8,1]{0,1:T(1,128)S(1)}, s32[8,1]{0,1:T(1,128)}, u32[]{:S(2)}) %copy-start.2) | copy-done | bytes 56
  1.3 1.6 %shard_map.68 = bf16[512,128]{1,0:T(8,128)(2,1)S(1)} custom-call(s32[8]{0:T(128)S(1)} %bitcast.7, s32[1]{0:T(128)} %bitcast.here, bf16[96,512,128]{2,1,0:T(8,128)(2,1)} %bitcast.11), custom_call_target="tpu_custom_call" | custom-call | bytes 1024 | tf_op jit(solution)/shard_map/pallas_call | solution.py:216
  2.9 4.1 %collective-permute-start.1 = (bf16[512,128]{1,0:T(8,128)(2,1)S(1)}, bf16[512,128]{1,0:T(8,128)(2,1)S(1)}, u32[]{:S(2)}, u32[]{:S(2)}) collective-permute-start(bf16[512,128]{1,0:T(8,128)(2,1)S(1)} %shard_map.68), channel_id=1, source_target_pairs={{0,8},{2,10},{4,12},{6,14},{8,0},{10,2},{12,4},{14,6},{1,9},{3,11}... | collective-permute-start | bytes 393224 | tf_op jit(solution)/shard_map/ppermute | solution.py:192
  7.0 1.8 %shard_map.69 = (bf16[512,128]{1,0:T(8,128)(2,1)S(1)}, bf16[512,128]{1,0:T(8,128)(2,1)S(1)}, bf16[512,128]{1,0:T(8,128)(2,1)S(1)}, bf16[512,128]{1,0:T(8,128)(2,...) custom-call(s32[8]{0:T(128)S(1)} %bitcast.8, s32[1]{0:T(128)} %bitcast.here, ...), custom_call_target="tpu_custom_call" | custom-call | bytes 1024 | tf_op jit(solution)/shard_map/pallas_call | solution.py:216
  8.8 1.6 %collective-permute-start = (bf16[512,128]{1,0:T(8,128)(2,1)S(1)}, bf16[512,128]{1,0:T(8,128)(2,1)S(1)}, u32[]{:S(2)}, u32[]{:S(2)}) collective-permute-start(bf16[512,128]{1,0:T(8,128)(2,1)S(1)} %get-tuple-element.26), channel_id=1, source_target_pairs={{0,2},{2,0},{4,6},{6,4},{8,10},{10,8},{12,14},{14,12},{1,3},{3,1},... | collective-permute-start | bytes 393224 | tf_op jit(solution)/shard_map/ppermute | solution.py:192
  10.3 1.6 %collective-permute-start.2 = (bf16[512,128]{1,0:T(8,128)(2,1)S(1)}, bf16[512,128]{1,0:T(8,128)(2,1)S(1)}, u32[]{:S(2)}, u32[]{:S(2)}) collective-permute-start(bf16[512,128]{1,0:T(8,128)(2,1)S(1)} %get-tuple-element.30), channel_id=1, source_target_pairs={{0,4},{2,6},{4,0},{6,2},{8,12},{10,14},{12,8},{14,10},{1,5},{3,7},... | collective-permute-start | bytes 393224 | tf_op jit(solution)/shard_map/ppermute | solution.py:192
  11.9 0.2 collective-permute-start.3
  12.1 1.7 %collective-permute-start.4 = (bf16[512,128]{1,0:T(8,128)(2,1)S(1)}, bf16[512,128]{1,0:T(8,128)(2,1)S(1)}, u32[]{:S(2)}, u32[]{:S(2)}) collective-permute-start(bf16[512,128]{1,0:T(8,128)(2,1)S(1)} %get-tuple-element.32), channel_id=1, source_target_pairs={{0,10},{2,8},{4,14},{6,12},{8,2},{10,0},{12,6},{14,4},{1,11},{3,9}... | collective-permute-start | bytes 393224 | tf_op jit(solution)/shard_map/ppermute | solution.py:192
  13.8 3.4 %collective-permute-start.5 = (bf16[512,128]{1,0:T(8,128)(2,1)S(1)}, bf16[512,128]{1,0:T(8,128)(2,1)S(1)}, u32[]{:S(2)}, u32[]{:S(2)}) collective-permute-start(bf16[512,128]{1,0:T(8,128)(2,1)S(1)} %get-tuple-element.34), channel_id=1, source_target_pairs={{0,6},{2,4},{4,2},{6,0},{8,14},{10,12},{12,10},{14,8},{1,7},{3,5},... | collective-permute-start | bytes 393224 | tf_op jit(solution)/shard_map/ppermute | solution.py:192
  17.2 2.0 %collective-permute-start.6 = (bf16[512,128]{1,0:T(8,128)(2,1)S(1)}, bf16[512,128]{1,0:T(8,128)(2,1)S(1)}, u32[]{:S(2)}, u32[]{:S(2)}) collective-permute-start(bf16[512,128]{1,0:T(8,128)(2,1)S(1)} %get-tuple-element.35), channel_id=1, source_target_pairs={{0,14},{2,12},{4,10},{6,8},{8,6},{10,4},{12,2},{14,0},{1,15},{3,13... | collective-permute-start | bytes 393224 | tf_op jit(solution)/shard_map/ppermute | solution.py:192
  19.2 5.9 %shard_map.70 = (bf16[8,512,256]{2,1,0:T(8,128)(2,1)S(1)}, bf16[512,128]{1,0:T(8,128)(2,1)S(1)}, f32[128,128]{1,0:T(8,128)S(1)}, f32[8,128]{1,0:T(8,128)S(1)}, s...) custom-call(s32[8]{0:T(128)S(1)} %bitcast.9, s32[1]{0:T(128)} %bitcast.here, s32[8]{0:T(128)S(1)} %bitcast.10, ...), custom_call_target="tpu_custom_call" | custom-call | bytes 16777216 | tf_op jit(solution)/shard_map/pallas_call | solution.py:229
  25.1 0.0 collective-permute-done.2.refs_2_
  25.1 4.3 %collective-permute-done.4.refs_4_ = bf16[512,128]{1,0:T(8,128)(2,1)S(1)} collective-permute-done((bf16[512,128]{1,0:T(8,128)(2,1)S(1)}, bf16[512,128]{1,0:T(8,128)(2,1)S(1)}, u32[]{:S(2)}, u32[]{:S(2)}) %collective-permute-start.4) | collective-permute-done | bytes 131104 | tf_op jit(solution)/shard_map/ppermute | solution.py:192
  29.4 0.6 shard_map.71.so_far
  30.0 0.0 collective-permute-done.6.refs_1_.refs_6_
  30.0 0.3 shard_map.72.mine
  30.3 0.1 collective-permute-start.7
  30.4 1.2 %collective-permute-done.7.other = f32[128,128]{1,0:T(8,128)S(1)} collective-permute-done((f32[128,128]{1,0:T(8,128)S(1)}, f32[128,128]{1,0:T(8,128)S(1)}, u32[]{:S(2)}, u32[]{:S(2)}) %collective-permute-start.7) | collective-permute-done | bytes 65568 | tf_op jit(solution)/shard_map/ppermute | solution.py:198
  31.6 0.3 shard_map.73
  31.9 2.6 %collective-permute-start.8 = (bf16[512,128]{1,0:T(8,128)(2,1)S(1)}, bf16[512,128]{1,0:T(8,128)(2,1)S(1)}, u32[]{:S(2)}, u32[]{:S(2)}) collective-permute-start(bf16[512,128]{1,0:T(8,128)(2,1)S(1)} %shard_map.73), channel_id=1, source_target_pairs={{0,12},{2,14},{4,8},{6,10},{8,4},{10,6},{12,0},{14,2},{1,13},{3,15... | collective-permute-start | bytes 393224 | tf_op jit(solution)/shard_map/ppermute | solution.py:192
  34.5 0.7 %shard_map.74 = (bf16[512,128]{1,0:T(8,128)(2,1)S(1)}, bf16[512,128]{1,0:T(8,128)(2,1)S(1)}, bf16[512,128]{1,0:T(8,128)(2,1)S(1)}, bf16[512,128]{1,0:T(8,128)(2,...) custom-call(s32[1]{0:T(128)} %bitcast.here, ...), custom_call_target="tpu_custom_call" | custom-call | bytes 1024 | tf_op jit(solution)/shard_map/pallas_call | solution.py:264
  35.2 0.6 %collective-permute-start.9 = (bf16[512,128]{1,0:T(8,128)(2,1)S(1)}, bf16[512,128]{1,0:T(8,128)(2,1)S(1)}, u32[]{:S(2)}, u32[]{:S(2)}) collective-permute-start(bf16[512,128]{1,0:T(8,128)(2,1)S(1)} %get-tuple-element.36), channel_id=1, source_target_pairs={{0,2},{2,0},{4,6},{6,4},{8,10},{10,8},{12,14},{14,12},{1,3},{3,1},... | collective-permute-start | bytes 393224 | tf_op jit(solution)/shard_map/ppermute | solution.py:192
  35.8 1.8 %collective-permute-start.10 = (bf16[512,128]{1,0:T(8,128)(2,1)S(1)}, bf16[512,128]{1,0:T(8,128)(2,1)S(1)}, u32[]{:S(2)}, u32[]{:S(2)}) collective-permute-start(bf16[512,128]{1,0:T(8,128)(2,1)S(1)} %get-tuple-element.37), channel_id=1, source_target_pairs={{0,4},{2,6},{4,0},{6,2},{8,12},{10,14},{12,8},{14,10},{1,5},{3,7},... | collective-permute-start | bytes 393224 | tf_op jit(solution)/shard_map/ppermute | solution.py:192
  37.6 0.5 collective-permute-start.11
  38.1 3.4 %collective-permute-start.12 = (bf16[512,128]{1,0:T(8,128)(2,1)S(1)}, bf16[512,128]{1,0:T(8,128)(2,1)S(1)}, u32[]{:S(2)}, u32[]{:S(2)}) collective-permute-start(bf16[512,128]{1,0:T(8,128)(2,1)S(1)} %get-tuple-element.39), channel_id=1, source_target_pairs={{0,10},{2,8},{4,14},{6,12},{8,2},{10,0},{12,6},{14,4},{1,11},{3,9}... | collective-permute-start | bytes 393224 | tf_op jit(solution)/shard_map/ppermute | solution.py:192
  41.5 2.7 %collective-permute-start.13 = (bf16[512,128]{1,0:T(8,128)(2,1)S(1)}, bf16[512,128]{1,0:T(8,128)(2,1)S(1)}, u32[]{:S(2)}, u32[]{:S(2)}) collective-permute-start(bf16[512,128]{1,0:T(8,128)(2,1)S(1)} %get-tuple-element.40), channel_id=1, source_target_pairs={{0,6},{2,4},{4,2},{6,0},{8,14},{10,12},{12,10},{14,8},{1,7},{3,5},... | collective-permute-start | bytes 393224 | tf_op jit(solution)/shard_map/ppermute | solution.py:192
  44.2 3.1 %collective-permute-start.14 = (bf16[512,128]{1,0:T(8,128)(2,1)S(1)}, bf16[512,128]{1,0:T(8,128)(2,1)S(1)}, u32[]{:S(2)}, u32[]{:S(2)}) collective-permute-start(bf16[512,128]{1,0:T(8,128)(2,1)S(1)} %get-tuple-element.46), channel_id=1, source_target_pairs={{0,14},{2,12},{4,10},{6,8},{8,6},{10,4},{12,2},{14,0},{1,15},{3,13... | collective-permute-start | bytes 393224 | tf_op jit(solution)/shard_map/ppermute | solution.py:192
  47.3 1.5 %shard_map.75 = bf16[128,4096]{1,0:T(8,128)(2,1)} custom-call(s32[1]{0:T(128)} %bitcast.here, f32[128,128]{1,0:T(8,128)S(1)} %get-tuple-element.27.live, f32[128,128]{1,0:T(8,128)S(1)} %shard_map.72.mine, f32[128,128]{1,0:T(8,128)S(1)} %collective-permute-done.7.other, bf16[512,128]{1,0:T(8,128)(2,1)S(1)} %collective-permute-done.1.refs_0_, ...), custom_call_target="tpu_custom_call" | custom-call | flops 134217728 | bytes 2097152 | tf_op jit(solution)/shard_map/pallas_call | solution.py:274
  48.8 1.9 %collective-permute-done.11.refs_3_ = bf16[512,128]{1,0:T(8,128)(2,1)S(1)} collective-permute-done((bf16[512,128]{1,0:T(8,128)(2,1)S(1)}, bf16[512,128]{1,0:T(8,128)(2,1)S(1)}, u32[]{:S(2)}, u32[]{:S(2)}) %collective-permute-start.11) | collective-permute-done | bytes 131104 | tf_op jit(solution)/shard_map/ppermute | solution.py:192
  50.7 1.4 %shard_map.76.refs_8_ = bf16[96,512,128]{2,1,0:T(8,128)(2,1)} custom-call(s32[8]{0:T(128)S(1)} %get-tuple-element.44.blocks, s32[1]{0:T(128)} %bitcast.here, f32[8,128]{1,0:T(8,128)S(1)} %get-tuple-element.45.parts, bf16[512,128]{1,0:T(8,128)(2,1)S(1)} %collective-permute-done.8.refs_0_, ...), custom_call_target="tpu_custom_call", output_to_operand_aliasing={{}: (8, {})} | custom-call | bytes 2097152 | tf_op jit(solution)/shard_map/pallas_call | solution.py:287
  52.1 4.5 %collective-permute-done.12.refs_4_ = bf16[512,128]{1,0:T(8,128)(2,1)S(1)} collective-permute-done((bf16[512,128]{1,0:T(8,128)(2,1)S(1)}, bf16[512,128]{1,0:T(8,128)(2,1)S(1)}, u32[]{:S(2)}, u32[]{:S(2)}) %collective-permute-start.12) | collective-permute-done | bytes 131104 | tf_op jit(solution)/shard_map/ppermute | solution.py:192
  56.7 1.4 %shard_map.77 = bf16[96,512,128]{2,1,0:T(8,128)(2,1)} custom-call(s32[8]{0:T(128)S(1)} %get-tuple-element.44.blocks, s32[1]{0:T(128)} %bitcast.here, f32[8,128]{1,0:T(8,128)S(1)} %get-tuple-element.45.parts, bf16[512,128]{1,0:T(8,128)(2,1)S(1)} %collective-permute-done.8.refs_0_, ...), custom_call_target="tpu_custom_call", output_to_operand_aliasing={{}: (11, {})} | custom-call | bytes 2097152 | tf_op jit(solution)/shard_map/pallas_call | solution.py:287
  (17 shorter events, 0.0 us)
Async XLA Ops:
  0.6 0.7 %copy-start.2 = (s32[8,1]{0,1:T(1,128)S(1)}, s32[8,1]{0,1:T(1,128)}, u32[]{:S(2)}) copy-start(s32[8,1]{0,1:T(1,128)} %param.8) | copy-start | bytes 100
  1.3 17.9 %copy-start = (bf16[128,4096]{1,0:T(8,128)(2,1)S(1)}, bf16[128,4096]{1,0:T(8,128)(2,1)}, u32[]{:S(2)}) copy-start(bf16[128,4096]{1,0:T(8,128)(2,1)} %x.3) | copy-start | bytes 3145732
  1.3 17.9 %copy-start.1 = (bf16[128,4096]{1,0:T(8,128)(2,1)S(1)}, bf16[128,4096]{1,0:T(8,128)(2,1)}, u32[]{:S(2)}) copy-start(bf16[128,4096]{1,0:T(8,128)(2,1)} %y.5) | copy-start | bytes 3145732
  1.3 17.9 %copy-start.3 = (s32[8,1]{0,1:T(1,128)S(1)}, s32[8,1]{0,1:T(1,128)}, u32[]{:S(2)}) copy-start(s32[8,1]{0,1:T(1,128)} %param.9) | copy-start | bytes 100
  2.9 10.9 %collective-permute-start.1 = (bf16[512,128]{1,0:T(8,128)(2,1)S(1)}, bf16[512,128]{1,0:T(8,128)(2,1)S(1)}, u32[]{:S(2)}, u32[]{:S(2)}) collective-permute-start(bf16[512,128]{1,0:T(8,128)(2,1)S(1)} %shard_map.68), channel_id=1, source_target_pairs={{0,8},{2,10},{4,12},{6,14},{8,0},{10,2},{12,4},{14,6},{1,9},{3,11}... | collective-permute-start | bytes 393224 | tf_op jit(solution)/shard_map/ppermute | solution.py:192
  8.8 8.4 %collective-permute-start = (bf16[512,128]{1,0:T(8,128)(2,1)S(1)}, bf16[512,128]{1,0:T(8,128)(2,1)S(1)}, u32[]{:S(2)}, u32[]{:S(2)}) collective-permute-start(bf16[512,128]{1,0:T(8,128)(2,1)S(1)} %get-tuple-element.26), channel_id=1, source_target_pairs={{0,2},{2,0},{4,6},{6,4},{8,10},{10,8},{12,14},{14,12},{1,3},{3,1},... | collective-permute-start | bytes 393224 | tf_op jit(solution)/shard_map/ppermute | solution.py:192
  10.3 14.8 %collective-permute-start.2 = (bf16[512,128]{1,0:T(8,128)(2,1)S(1)}, bf16[512,128]{1,0:T(8,128)(2,1)S(1)}, u32[]{:S(2)}, u32[]{:S(2)}) collective-permute-start(bf16[512,128]{1,0:T(8,128)(2,1)S(1)} %get-tuple-element.30), channel_id=1, source_target_pairs={{0,4},{2,6},{4,0},{6,2},{8,12},{10,14},{12,8},{14,10},{1,5},{3,7},... | collective-permute-start | bytes 393224 | tf_op jit(solution)/shard_map/ppermute | solution.py:192
  11.9 13.2 %collective-permute-start.3 = (bf16[512,128]{1,0:T(8,128)(2,1)S(1)}, bf16[512,128]{1,0:T(8,128)(2,1)S(1)}, u32[]{:S(2)}, u32[]{:S(2)}) collective-permute-start(bf16[512,128]{1,0:T(8,128)(2,1)S(1)} %get-tuple-element.31), channel_id=1, source_target_pairs={{0,12},{2,14},{4,8},{6,10},{8,4},{10,6},{12,0},{14,2},{1,13},{3,15... | collective-permute-start | bytes 393224 | tf_op jit(solution)/shard_map/ppermute | solution.py:192
  12.1 17.3 %collective-permute-start.4 = (bf16[512,128]{1,0:T(8,128)(2,1)S(1)}, bf16[512,128]{1,0:T(8,128)(2,1)S(1)}, u32[]{:S(2)}, u32[]{:S(2)}) collective-permute-start(bf16[512,128]{1,0:T(8,128)(2,1)S(1)} %get-tuple-element.32), channel_id=1, source_target_pairs={{0,10},{2,8},{4,14},{6,12},{8,2},{10,0},{12,6},{14,4},{1,11},{3,9}... | collective-permute-start | bytes 393224 | tf_op jit(solution)/shard_map/ppermute | solution.py:192
  13.8 16.2 %collective-permute-start.5 = (bf16[512,128]{1,0:T(8,128)(2,1)S(1)}, bf16[512,128]{1,0:T(8,128)(2,1)S(1)}, u32[]{:S(2)}, u32[]{:S(2)}) collective-permute-start(bf16[512,128]{1,0:T(8,128)(2,1)S(1)} %get-tuple-element.34), channel_id=1, source_target_pairs={{0,6},{2,4},{4,2},{6,0},{8,14},{10,12},{12,10},{14,8},{1,7},{3,5},... | collective-permute-start | bytes 393224 | tf_op jit(solution)/shard_map/ppermute | solution.py:192
  17.2 12.8 %collective-permute-start.6 = (bf16[512,128]{1,0:T(8,128)(2,1)S(1)}, bf16[512,128]{1,0:T(8,128)(2,1)S(1)}, u32[]{:S(2)}, u32[]{:S(2)}) collective-permute-start(bf16[512,128]{1,0:T(8,128)(2,1)S(1)} %get-tuple-element.35), channel_id=1, source_target_pairs={{0,14},{2,12},{4,10},{6,8},{8,6},{10,4},{12,2},{14,0},{1,15},{3,13... | collective-permute-start | bytes 393224 | tf_op jit(solution)/shard_map/ppermute | solution.py:192
  30.3 1.3 %collective-permute-start.7 = (f32[128,128]{1,0:T(8,128)S(1)}, f32[128,128]{1,0:T(8,128)S(1)}, u32[]{:S(2)}, u32[]{:S(2)}) collective-permute-start(f32[128,128]{1,0:T(8,128)S(1)} %shard_map.72.mine), channel_id=1, source_target_pairs={{0,1},{1,0},{2,3},{3,2},{4,5},{5,4},{6,7},{7,6},{8,9},{9,8},{10,11... | collective-permute-start | bytes 196616 | tf_op jit(solution)/shard_map/ppermute | solution.py:198
  31.9 9.5 %collective-permute-start.8 = (bf16[512,128]{1,0:T(8,128)(2,1)S(1)}, bf16[512,128]{1,0:T(8,128)(2,1)S(1)}, u32[]{:S(2)}, u32[]{:S(2)}) collective-permute-start(bf16[512,128]{1,0:T(8,128)(2,1)S(1)} %shard_map.73), channel_id=1, source_target_pairs={{0,12},{2,14},{4,8},{6,10},{8,4},{10,6},{12,0},{14,2},{1,13},{3,15... | collective-permute-start | bytes 393224 | tf_op jit(solution)/shard_map/ppermute | solution.py:192
  35.2 9.0 %collective-permute-start.9 = (bf16[512,128]{1,0:T(8,128)(2,1)S(1)}, bf16[512,128]{1,0:T(8,128)(2,1)S(1)}, u32[]{:S(2)}, u32[]{:S(2)}) collective-permute-start(bf16[512,128]{1,0:T(8,128)(2,1)S(1)} %get-tuple-element.36), channel_id=1, source_target_pairs={{0,2},{2,0},{4,6},{6,4},{8,10},{10,8},{12,14},{14,12},{1,3},{3,1},... | collective-permute-start | bytes 393224 | tf_op jit(solution)/shard_map/ppermute | solution.py:192
  35.8 13.0 %collective-permute-start.10 = (bf16[512,128]{1,0:T(8,128)(2,1)S(1)}, bf16[512,128]{1,0:T(8,128)(2,1)S(1)}, u32[]{:S(2)}, u32[]{:S(2)}) collective-permute-start(bf16[512,128]{1,0:T(8,128)(2,1)S(1)} %get-tuple-element.37), channel_id=1, source_target_pairs={{0,4},{2,6},{4,0},{6,2},{8,12},{10,14},{12,8},{14,10},{1,5},{3,7},... | collective-permute-start | bytes 393224 | tf_op jit(solution)/shard_map/ppermute | solution.py:192
  37.6 13.1 %collective-permute-start.11 = (bf16[512,128]{1,0:T(8,128)(2,1)S(1)}, bf16[512,128]{1,0:T(8,128)(2,1)S(1)}, u32[]{:S(2)}, u32[]{:S(2)}) collective-permute-start(bf16[512,128]{1,0:T(8,128)(2,1)S(1)} %get-tuple-element.38), channel_id=1, source_target_pairs={{0,8},{2,10},{4,12},{6,14},{8,0},{10,2},{12,4},{14,6},{1,9},{3,11}... | collective-permute-start | bytes 393224 | tf_op jit(solution)/shard_map/ppermute | solution.py:192
  38.1 18.6 %collective-permute-start.12 = (bf16[512,128]{1,0:T(8,128)(2,1)S(1)}, bf16[512,128]{1,0:T(8,128)(2,1)S(1)}, u32[]{:S(2)}, u32[]{:S(2)}) collective-permute-start(bf16[512,128]{1,0:T(8,128)(2,1)S(1)} %get-tuple-element.39), channel_id=1, source_target_pairs={{0,10},{2,8},{4,14},{6,12},{8,2},{10,0},{12,6},{14,4},{1,11},{3,9}... | collective-permute-start | bytes 393224 | tf_op jit(solution)/shard_map/ppermute | solution.py:192
  41.5 15.2 %collective-permute-start.13 = (bf16[512,128]{1,0:T(8,128)(2,1)S(1)}, bf16[512,128]{1,0:T(8,128)(2,1)S(1)}, u32[]{:S(2)}, u32[]{:S(2)}) collective-permute-start(bf16[512,128]{1,0:T(8,128)(2,1)S(1)} %get-tuple-element.40), channel_id=1, source_target_pairs={{0,6},{2,4},{4,2},{6,0},{8,14},{10,12},{12,10},{14,8},{1,7},{3,5},... | collective-permute-start | bytes 393224 | tf_op jit(solution)/shard_map/ppermute | solution.py:192
  44.2 12.5 %collective-permute-start.14 = (bf16[512,128]{1,0:T(8,128)(2,1)S(1)}, bf16[512,128]{1,0:T(8,128)(2,1)S(1)}, u32[]{:S(2)}, u32[]{:S(2)}) collective-permute-start(bf16[512,128]{1,0:T(8,128)(2,1)S(1)} %get-tuple-element.46), channel_id=1, source_target_pairs={{0,14},{2,12},{4,10},{6,8},{8,6},{10,4},{12,2},{14,0},{1,15},{3,13... | collective-permute-start | bytes 393224 | tf_op jit(solution)/shard_map/ppermute | solution.py:192

commit v22 on v21

--- a/solution.py
+++ b/solution.py
@@ -8,10 +8,10 @@
 from jax.sharding import PartitionSpec as P
 
 adapter_alpha = 128.0
-FETCH = (4, 1, 2, 6, 5, 3, 7)
+FETCH = (4, 1, 2, 5, 6, 3, 7)
 FETCH_TIES = {}
 SEND = (6, 1, 2, 4, 5, 3, 7)
-SEND_TIES = {7: 6}
+SEND_TIES = {3: 6}
 PREP_AFTER = 1
 LATE = (5, 3, 7)
 RANK_LAST = (3, 7)

time: 58.4 us -> 57.9 us (level)
  starting transfers between devices: 29.2 us -> 27.6 us
  waiting for transfers between devices: 12 us -> 13.3 us
    ppermute x14, starting transfers between devices: 29.1 us -> 27.5 us  [exchange(): out[k] = lax.ppermute(piece, 'dp', [(i, i ^ k) for i in range(owners)])]
    ppermute x14, waiting for transfers between devices: 10.8 us -> 12.1 us  [exchange(): out[k] = lax.ppermute(piece, 'dp', [(i, i ^ k) for i in range(owners)])]
  transfers between devices with their start and end apart: 15 -> 15, of which waited for: 4 -> 5; matrix products, arithmetic and copies ran while one was open for 0% -> 0% of each run, Pallas kernels for 20% -> 21%
where the time goes in v22:
time: 57.9 us; the launch traced here: 57.7 us
  starting transfers between devices  27.6 us (48%)
  Pallas kernels  15.4 us (27%)
  waiting for transfers between devices  13.3 us (23%)
  between operations  0.74 us (1%)
  local copies, waits for them, and re-layouts  0.66 us (1%)
    ppermute x14, starting transfers between devices, exchange(): out[k] = lax.ppermute(piece, 'dp', [(i, i ^ k) for i in range(owners)])  27.5 us
    ppermute x14, waiting for transfers between devices, exchange(): out[k] = lax.ppermute(piece, 'dp', [(i, i ^ k) for i in range(owners)])  12.1 us
    pallas_call x1, Pallas kernels, with_kernels(): call(prep_kernel, [jax.ShapeDtypeStruct((owners, rows, 2 * tokens), bf16)...  5.94 us
    pallas_call x2, Pallas kernels, with_kernels(): call(functools.partial(gather_kernel, part), [straight] * len(part), [in_...  3.35 us
    pallas_call x2, Pallas kernels, merge(): call(functools.partial(merge_kernel, tuple(merged), handled, others), jax...  2.82 us
    pallas_call x1, Pallas kernels, with_kernels(): call(functools.partial(input_kernel, tuple(pairs), scale), jax.ShapeDtype...  1.45 us
    ppermute x1, waiting for transfers between devices, across_cores(): return lax.ppermute(value, 'tensor', [(i, i ^ 1) for i in range(cores)])  1.24 us
  transfers between devices with their start and end apart: 15, of which 5 were waited for; matrix products, arithmetic and copies ran while one was open for 0% of the time, Pallas kernels for 21%

profile of v22, /device:TPU:0, one launch (start us, length us, event | category | flops | bytes accessed | tf_op | source)
XLA Modules:
  0.0 57.7 jit_solution(12693234626747722698)
XLA Ops:
  0.6 0.6 %copy-done.2 = s32[8,1]{0,1:T(1,128)S(1)} copy-done((s32[8,1]{0,1:T(1,128)S(1)}, s32[8,1]{0,1:T(1,128)}, u32[]{:S(2)}) %copy-start.2) | copy-done | bytes 56
  1.3 1.6 %shard_map.68 = bf16[512,128]{1,0:T(8,128)(2,1)S(1)} custom-call(s32[8]{0:T(128)S(1)} %bitcast.7, s32[1]{0:T(128)} %bitcast.here, bf16[96,512,128]{2,1,0:T(8,128)(2,1)} %bitcast.11), custom_call_target="tpu_custom_call" | custom-call | bytes 1024 | tf_op jit(solution)/shard_map/pallas_call | solution.py:216
  2.9 4.1 %collective-permute-start.1 = (bf16[512,128]{1,0:T(8,128)(2,1)S(1)}, bf16[512,128]{1,0:T(8,128)(2,1)S(1)}, u32[]{:S(2)}, u32[]{:S(2)}) collective-permute-start(bf16[512,128]{1,0:T(8,128)(2,1)S(1)} %shard_map.68), channel_id=1, source_target_pairs={{0,8},{2,10},{4,12},{6,14},{8,0},{10,2},{12,4},{14,6},{1,9},{3,11}... | collective-permute-start | bytes 393224 | tf_op jit(solution)/shard_map/ppermute | solution.py:192
  7.0 1.8 %shard_map.69 = (bf16[512,128]{1,0:T(8,128)(2,1)S(1)}, bf16[512,128]{1,0:T(8,128)(2,1)S(1)}, bf16[512,128]{1,0:T(8,128)(2,1)S(1)}, bf16[512,128]{1,0:T(8,128)(2,...) custom-call(s32[8]{0:T(128)S(1)} %bitcast.8, s32[1]{0:T(128)} %bitcast.here, ...), custom_call_target="tpu_custom_call" | custom-call | bytes 1024 | tf_op jit(solution)/shard_map/pallas_call | solution.py:216
  8.8 1.6 %collective-permute-start = (bf16[512,128]{1,0:T(8,128)(2,1)S(1)}, bf16[512,128]{1,0:T(8,128)(2,1)S(1)}, u32[]{:S(2)}, u32[]{:S(2)}) collective-permute-start(bf16[512,128]{1,0:T(8,128)(2,1)S(1)} %get-tuple-element.26), channel_id=1, source_target_pairs={{0,2},{2,0},{4,6},{6,4},{8,10},{10,8},{12,14},{14,12},{1,3},{3,1},... | collective-permute-start | bytes 393224 | tf_op jit(solution)/shard_map/ppermute | solution.py:192
  10.3 1.6 %collective-permute-start.2 = (bf16[512,128]{1,0:T(8,128)(2,1)S(1)}, bf16[512,128]{1,0:T(8,128)(2,1)S(1)}, u32[]{:S(2)}, u32[]{:S(2)}) collective-permute-start(bf16[512,128]{1,0:T(8,128)(2,1)S(1)} %get-tuple-element.30), channel_id=1, source_target_pairs={{0,4},{2,6},{4,0},{6,2},{8,12},{10,14},{12,8},{14,10},{1,5},{3,7},... | collective-permute-start | bytes 393224 | tf_op jit(solution)/shard_map/ppermute | solution.py:192
  11.9 0.3 collective-permute-start.3
  12.2 2.5 %collective-permute-start.4 = (bf16[512,128]{1,0:T(8,128)(2,1)S(1)}, bf16[512,128]{1,0:T(8,128)(2,1)S(1)}, u32[]{:S(2)}, u32[]{:S(2)}) collective-permute-start(bf16[512,128]{1,0:T(8,128)(2,1)S(1)} %get-tuple-element.32), channel_id=1, source_target_pairs={{0,12},{2,14},{4,8},{6,10},{8,4},{10,6},{12,0},{14,2},{1,13},{3,15... | collective-permute-start | bytes 393224 | tf_op jit(solution)/shard_map/ppermute | solution.py:192
  14.7 1.6 %collective-permute-start.5 = (bf16[512,128]{1,0:T(8,128)(2,1)S(1)}, bf16[512,128]{1,0:T(8,128)(2,1)S(1)}, u32[]{:S(2)}, u32[]{:S(2)}) collective-permute-start(bf16[512,128]{1,0:T(8,128)(2,1)S(1)} %get-tuple-element.34), channel_id=1, source_target_pairs={{0,6},{2,4},{4,2},{6,0},{8,14},{10,12},{12,10},{14,8},{1,7},{3,5},... | collective-permute-start | bytes 393224 | tf_op jit(solution)/shard_map/ppermute | solution.py:192
  16.3 2.8 %collective-permute-start.6 = (bf16[512,128]{1,0:T(8,128)(2,1)S(1)}, bf16[512,128]{1,0:T(8,128)(2,1)S(1)}, u32[]{:S(2)}, u32[]{:S(2)}) collective-permute-start(bf16[512,128]{1,0:T(8,128)(2,1)S(1)} %get-tuple-element.35), channel_id=1, source_target_pairs={{0,14},{2,12},{4,10},{6,8},{8,6},{10,4},{12,2},{14,0},{1,15},{3,13... | collective-permute-start | bytes 393224 | tf_op jit(solution)/shard_map/ppermute | solution.py:192
  19.1 5.9 %shard_map.70 = (bf16[8,512,256]{2,1,0:T(8,128)(2,1)S(1)}, bf16[512,128]{1,0:T(8,128)(2,1)S(1)}, f32[128,128]{1,0:T(8,128)S(1)}, f32[8,128]{1,0:T(8,128)S(1)}, s...) custom-call(s32[8]{0:T(128)S(1)} %bitcast.9, s32[1]{0:T(128)} %bitcast.here, s32[8]{0:T(128)S(1)} %bitcast.10, ...), custom_call_target="tpu_custom_call" | custom-call | bytes 16777216 | tf_op jit(solution)/shard_map/pallas_call | solution.py:229
  25.1 0.0 collective-permute-done.2.refs_2_
  25.1 1.6 %collective-permute-done.3.refs_3_ = bf16[512,128]{1,0:T(8,128)(2,1)S(1)} collective-permute-done((bf16[512,128]{1,0:T(8,128)(2,1)S(1)}, bf16[512,128]{1,0:T(8,128)(2,1)S(1)}, u32[]{:S(2)}, u32[]{:S(2)}) %collective-permute-start.3) | collective-permute-done | bytes 131104 | tf_op jit(solution)/shard_map/ppermute | solution.py:192
  26.7 0.0 collective-permute-done.4.refs_4_
  26.7 0.6 shard_map.71.so_far
  27.3 0.6 collective-permute-done.5.refs_0_.refs_5_
  27.8 0.3 shard_map.72.mine
  28.1 0.1 collective-permute-start.7
  28.2 1.2 %collective-permute-done.7.other = f32[128,128]{1,0:T(8,128)S(1)} collective-permute-done((f32[128,128]{1,0:T(8,128)S(1)}, f32[128,128]{1,0:T(8,128)S(1)}, u32[]{:S(2)}, u32[]{:S(2)}) %collective-permute-start.7) | collective-permute-done | bytes 65568 | tf_op jit(solution)/shard_map/ppermute | solution.py:198
  29.5 0.3 shard_map.73
  29.8 2.7 %collective-permute-start.8 = (bf16[512,128]{1,0:T(8,128)(2,1)S(1)}, bf16[512,128]{1,0:T(8,128)(2,1)S(1)}, u32[]{:S(2)}, u32[]{:S(2)}) collective-permute-start(bf16[512,128]{1,0:T(8,128)(2,1)S(1)} %shard_map.73), channel_id=1, source_target_pairs={{0,12},{2,14},{4,8},{6,10},{8,4},{10,6},{12,0},{14,2},{1,13},{3,15... | collective-permute-start | bytes 393224 | tf_op jit(solution)/shard_map/ppermute | solution.py:192
  32.5 0.7 %shard_map.74 = (bf16[512,128]{1,0:T(8,128)(2,1)S(1)}, bf16[512,128]{1,0:T(8,128)(2,1)S(1)}, bf16[512,128]{1,0:T(8,128)(2,1)S(1)}, bf16[512,128]{1,0:T(8,128)(2,...) custom-call(s32[1]{0:T(128)} %bitcast.here, ...), custom_call_target="tpu_custom_call" | custom-call | bytes 1024 | tf_op jit(solution)/shard_map/pallas_call | solution.py:264
  33.2 1.3 %collective-permute-start.9 = (bf16[512,128]{1,0:T(8,128)(2,1)S(1)}, bf16[512,128]{1,0:T(8,128)(2,1)S(1)}, u32[]{:S(2)}, u32[]{:S(2)}) collective-permute-start(bf16[512,128]{1,0:T(8,128)(2,1)S(1)} %get-tuple-element.36), channel_id=1, source_target_pairs={{0,2},{2,0},{4,6},{6,4},{8,10},{10,8},{12,14},{14,12},{1,3},{3,1},... | collective-permute-start | bytes 393224 | tf_op jit(solution)/shard_map/ppermute | solution.py:192
  34.5 3.1 %collective-permute-start.10 = (bf16[512,128]{1,0:T(8,128)(2,1)S(1)}, bf16[512,128]{1,0:T(8,128)(2,1)S(1)}, u32[]{:S(2)}, u32[]{:S(2)}) collective-permute-start(bf16[512,128]{1,0:T(8,128)(2,1)S(1)} %get-tuple-element.37), channel_id=1, source_target_pairs={{0,4},{2,6},{4,0},{6,2},{8,12},{10,14},{12,8},{14,10},{1,5},{3,7},... | collective-permute-start | bytes 393224 | tf_op jit(solution)/shard_map/ppermute | solution.py:192
  37.6 3.8 %collective-permute-start.12 = (bf16[512,128]{1,0:T(8,128)(2,1)S(1)}, bf16[512,128]{1,0:T(8,128)(2,1)S(1)}, u32[]{:S(2)}, u32[]{:S(2)}) collective-permute-start(bf16[512,128]{1,0:T(8,128)(2,1)S(1)} %get-tuple-element.39), channel_id=1, source_target_pairs={{0,10},{2,8},{4,14},{6,12},{8,2},{10,0},{12,6},{14,4},{1,11},{3,9}... | collective-permute-start | bytes 393224 | tf_op jit(solution)/shard_map/ppermute | solution.py:192
  41.4 1.3 %collective-permute-start.14 = (bf16[512,128]{1,0:T(8,128)(2,1)S(1)}, bf16[512,128]{1,0:T(8,128)(2,1)S(1)}, u32[]{:S(2)}, u32[]{:S(2)}) collective-permute-start(bf16[512,128]{1,0:T(8,128)(2,1)S(1)} %get-tuple-element.41), channel_id=1, source_target_pairs={{0,14},{2,12},{4,10},{6,8},{8,6},{10,4},{12,2},{14,0},{1,15},{3,13... | collective-permute-start | bytes 393224 | tf_op jit(solution)/shard_map/ppermute | solution.py:192
  42.7 0.8 %collective-permute-start.13 = (bf16[512,128]{1,0:T(8,128)(2,1)S(1)}, bf16[512,128]{1,0:T(8,128)(2,1)S(1)}, u32[]{:S(2)}, u32[]{:S(2)}) collective-permute-start(bf16[512,128]{1,0:T(8,128)(2,1)S(1)} %get-tuple-element.46), channel_id=1, source_target_pairs={{0,6},{2,4},{4,2},{6,0},{8,14},{10,12},{12,10},{14,8},{1,7},{3,5},... | collective-permute-start | bytes 393224 | tf_op jit(solution)/shard_map/ppermute | solution.py:192
  43.5 1.4 %shard_map.75 = bf16[128,4096]{1,0:T(8,128)(2,1)} custom-call(s32[1]{0:T(128)} %bitcast.here, f32[128,128]{1,0:T(8,128)S(1)} %get-tuple-element.27.live, f32[128,128]{1,0:T(8,128)S(1)} %shard_map.72.mine, f32[128,128]{1,0:T(8,128)S(1)} %collective-permute-done.7.other, bf16[512,128]{1,0:T(8,128)(2,1)S(1)} %collective-permute-done.1.refs_0_, ...), custom_call_target="tpu_custom_call" | custom-call | flops 134217728 | bytes 2097152 | tf_op jit(solution)/shard_map/pallas_call | solution.py:274
  45.0 7.7 %collective-permute-done.11.refs_3_ = bf16[512,128]{1,0:T(8,128)(2,1)S(1)} collective-permute-done((bf16[512,128]{1,0:T(8,128)(2,1)S(1)}, bf16[512,128]{1,0:T(8,128)(2,1)S(1)}, u32[]{:S(2)}, u32[]{:S(2)}) %collective-permute-start.11) | collective-permute-done | bytes 131104 | tf_op jit(solution)/shard_map/ppermute | solution.py:192
  52.6 1.4 %shard_map.76.refs_8_ = bf16[96,512,128]{2,1,0:T(8,128)(2,1)} custom-call(s32[8]{0:T(128)S(1)} %get-tuple-element.44.blocks, s32[1]{0:T(128)} %bitcast.here, f32[8,128]{1,0:T(8,128)S(1)} %get-tuple-element.45.parts, bf16[512,128]{1,0:T(8,128)(2,1)S(1)} %collective-permute-done.8.refs_0_, ...), custom_call_target="tpu_custom_call", output_to_operand_aliasing={{}: (8, {})} | custom-call | bytes 2097152 | tf_op jit(solution)/shard_map/pallas_call | solution.py:287
  54.0 2.3 %collective-permute-done.12.refs_4_ = bf16[512,128]{1,0:T(8,128)(2,1)S(1)} collective-permute-done((bf16[512,128]{1,0:T(8,128)(2,1)S(1)}, bf16[512,128]{1,0:T(8,128)(2,1)S(1)}, u32[]{:S(2)}, u32[]{:S(2)}) %collective-permute-start.12) | collective-permute-done | bytes 131104 | tf_op jit(solution)/shard_map/ppermute | solution.py:192
  56.3 1.4 %shard_map.77 = bf16[96,512,128]{2,1,0:T(8,128)(2,1)} custom-call(s32[8]{0:T(128)S(1)} %get-tuple-element.44.blocks, s32[1]{0:T(128)} %bitcast.here, f32[8,128]{1,0:T(8,128)S(1)} %get-tuple-element.45.parts, bf16[512,128]{1,0:T(8,128)(2,1)S(1)} %collective-permute-done.8.refs_0_, ...), custom_call_target="tpu_custom_call", output_to_operand_aliasing={{}: (11, {})} | custom-call | bytes 2097152 | tf_op jit(solution)/shard_map/pallas_call | solution.py:287
  (17 shorter events, 0.0 us)
Async XLA Ops:
  0.6 0.7 %copy-start.2 = (s32[8,1]{0,1:T(1,128)S(1)}, s32[8,1]{0,1:T(1,128)}, u32[]{:S(2)}) copy-start(s32[8,1]{0,1:T(1,128)} %param.8) | copy-start | bytes 100
  1.3 17.8 %copy-start = (bf16[128,4096]{1,0:T(8,128)(2,1)S(1)}, bf16[128,4096]{1,0:T(8,128)(2,1)}, u32[]{:S(2)}) copy-start(bf16[128,4096]{1,0:T(8,128)(2,1)} %x.3) | copy-start | bytes 3145732
  1.3 17.8 %copy-start.1 = (bf16[128,4096]{1,0:T(8,128)(2,1)S(1)}, bf16[128,4096]{1,0:T(8,128)(2,1)}, u32[]{:S(2)}) copy-start(bf16[128,4096]{1,0:T(8,128)(2,1)} %y.5) | copy-start | bytes 3145732
  1.3 17.8 %copy-start.3 = (s32[8,1]{0,1:T(1,128)S(1)}, s32[8,1]{0,1:T(1,128)}, u32[]{:S(2)}) copy-start(s32[8,1]{0,1:T(1,128)} %param.9) | copy-start | bytes 100
  2.9 11.8 %collective-permute-start.1 = (bf16[512,128]{1,0:T(8,128)(2,1)S(1)}, bf16[512,128]{1,0:T(8,128)(2,1)S(1)}, u32[]{:S(2)}, u32[]{:S(2)}) collective-permute-start(bf16[512,128]{1,0:T(8,128)(2,1)S(1)} %shard_map.68), channel_id=1, source_target_pairs={{0,8},{2,10},{4,12},{6,14},{8,0},{10,2},{12,4},{14,6},{1,9},{3,11}... | collective-permute-start | bytes 393224 | tf_op jit(solution)/shard_map/ppermute | solution.py:192
  8.8 7.5 %collective-permute-start = (bf16[512,128]{1,0:T(8,128)(2,1)S(1)}, bf16[512,128]{1,0:T(8,128)(2,1)S(1)}, u32[]{:S(2)}, u32[]{:S(2)}) collective-permute-start(bf16[512,128]{1,0:T(8,128)(2,1)S(1)} %get-tuple-element.26), channel_id=1, source_target_pairs={{0,2},{2,0},{4,6},{6,4},{8,10},{10,8},{12,14},{14,12},{1,3},{3,1},... | collective-permute-start | bytes 393224 | tf_op jit(solution)/shard_map/ppermute | solution.py:192
  10.3 14.8 %collective-permute-start.2 = (bf16[512,128]{1,0:T(8,128)(2,1)S(1)}, bf16[512,128]{1,0:T(8,128)(2,1)S(1)}, u32[]{:S(2)}, u32[]{:S(2)}) collective-permute-start(bf16[512,128]{1,0:T(8,128)(2,1)S(1)} %get-tuple-element.30), channel_id=1, source_target_pairs={{0,4},{2,6},{4,0},{6,2},{8,12},{10,14},{12,8},{14,10},{1,5},{3,7},... | collective-permute-start | bytes 393224 | tf_op jit(solution)/shard_map/ppermute | solution.py:192
  11.9 14.8 %collective-permute-start.3 = (bf16[512,128]{1,0:T(8,128)(2,1)S(1)}, bf16[512,128]{1,0:T(8,128)(2,1)S(1)}, u32[]{:S(2)}, u32[]{:S(2)}) collective-permute-start(bf16[512,128]{1,0:T(8,128)(2,1)S(1)} %get-tuple-element.31), channel_id=1, source_target_pairs={{0,10},{2,8},{4,14},{6,12},{8,2},{10,0},{12,6},{14,4},{1,11},{3,9}... | collective-permute-start | bytes 393224 | tf_op jit(solution)/shard_map/ppermute | solution.py:192
  12.2 14.5 %collective-permute-start.4 = (bf16[512,128]{1,0:T(8,128)(2,1)S(1)}, bf16[512,128]{1,0:T(8,128)(2,1)S(1)}, u32[]{:S(2)}, u32[]{:S(2)}) collective-permute-start(bf16[512,128]{1,0:T(8,128)(2,1)S(1)} %get-tuple-element.32), channel_id=1, source_target_pairs={{0,12},{2,14},{4,8},{6,10},{8,4},{10,6},{12,0},{14,2},{1,13},{3,15... | collective-permute-start | bytes 393224 | tf_op jit(solution)/shard_map/ppermute | solution.py:192
  14.7 13.1 %collective-permute-start.5 = (bf16[512,128]{1,0:T(8,128)(2,1)S(1)}, bf16[512,128]{1,0:T(8,128)(2,1)S(1)}, u32[]{:S(2)}, u32[]{:S(2)}) collective-permute-start(bf16[512,128]{1,0:T(8,128)(2,1)S(1)} %get-tuple-element.34), channel_id=1, source_target_pairs={{0,6},{2,4},{4,2},{6,0},{8,14},{10,12},{12,10},{14,8},{1,7},{3,5},... | collective-permute-start | bytes 393224 | tf_op jit(solution)/shard_map/ppermute | solution.py:192
  16.3 11.5 %collective-permute-start.6 = (bf16[512,128]{1,0:T(8,128)(2,1)S(1)}, bf16[512,128]{1,0:T(8,128)(2,1)S(1)}, u32[]{:S(2)}, u32[]{:S(2)}) collective-permute-start(bf16[512,128]{1,0:T(8,128)(2,1)S(1)} %get-tuple-element.35), channel_id=1, source_target_pairs={{0,14},{2,12},{4,10},{6,8},{8,6},{10,4},{12,2},{14,0},{1,15},{3,13... | collective-permute-start | bytes 393224 | tf_op jit(solution)/shard_map/ppermute | solution.py:192
  28.1 1.3 %collective-permute-start.7 = (f32[128,128]{1,0:T(8,128)S(1)}, f32[128,128]{1,0:T(8,128)S(1)}, u32[]{:S(2)}, u32[]{:S(2)}) collective-permute-start(f32[128,128]{1,0:T(8,128)S(1)} %shard_map.72.mine), channel_id=1, source_target_pairs={{0,1},{1,0},{2,3},{3,2},{4,5},{5,4},{6,7},{7,6},{8,9},{9,8},{10,11... | collective-permute-start | bytes 196616 | tf_op jit(solution)/shard_map/ppermute | solution.py:198
  29.8 11.7 %collective-permute-start.8 = (bf16[512,128]{1,0:T(8,128)(2,1)S(1)}, bf16[512,128]{1,0:T(8,128)(2,1)S(1)}, u32[]{:S(2)}, u32[]{:S(2)}) collective-permute-start(bf16[512,128]{1,0:T(8,128)(2,1)S(1)} %shard_map.73), channel_id=1, source_target_pairs={{0,12},{2,14},{4,8},{6,10},{8,4},{10,6},{12,0},{14,2},{1,13},{3,15... | collective-permute-start | bytes 393224 | tf_op jit(solution)/shard_map/ppermute | solution.py:192
  33.2 9.5 %collective-permute-start.9 = (bf16[512,128]{1,0:T(8,128)(2,1)S(1)}, bf16[512,128]{1,0:T(8,128)(2,1)S(1)}, u32[]{:S(2)}, u32[]{:S(2)}) collective-permute-start(bf16[512,128]{1,0:T(8,128)(2,1)S(1)} %get-tuple-element.36), channel_id=1, source_target_pairs={{0,2},{2,0},{4,6},{6,4},{8,10},{10,8},{12,14},{14,12},{1,3},{3,1},... | collective-permute-start | bytes 393224 | tf_op jit(solution)/shard_map/ppermute | solution.py:192
  34.5 10.5 %collective-permute-start.10 = (bf16[512,128]{1,0:T(8,128)(2,1)S(1)}, bf16[512,128]{1,0:T(8,128)(2,1)S(1)}, u32[]{:S(2)}, u32[]{:S(2)}) collective-permute-start(bf16[512,128]{1,0:T(8,128)(2,1)S(1)} %get-tuple-element.37), channel_id=1, source_target_pairs={{0,4},{2,6},{4,0},{6,2},{8,12},{10,14},{12,8},{14,10},{1,5},{3,7},... | collective-permute-start | bytes 393224 | tf_op jit(solution)/shard_map/ppermute | solution.py:192
  37.6 15.0 %collective-permute-start.11 = (bf16[512,128]{1,0:T(8,128)(2,1)S(1)}, bf16[512,128]{1,0:T(8,128)(2,1)S(1)}, u32[]{:S(2)}, u32[]{:S(2)}) collective-permute-start(bf16[512,128]{1,0:T(8,128)(2,1)S(1)} %get-tuple-element.38), channel_id=1, source_target_pairs={{0,8},{2,10},{4,12},{6,14},{8,0},{10,2},{12,4},{14,6},{1,9},{3,11}... | collective-permute-start | bytes 393224 | tf_op jit(solution)/shard_map/ppermute | solution.py:192
  37.6 18.7 %collective-permute-start.12 = (bf16[512,128]{1,0:T(8,128)(2,1)S(1)}, bf16[512,128]{1,0:T(8,128)(2,1)S(1)}, u32[]{:S(2)}, u32[]{:S(2)}) collective-permute-start(bf16[512,128]{1,0:T(8,128)(2,1)S(1)} %get-tuple-element.39), channel_id=1, source_target_pairs={{0,10},{2,8},{4,14},{6,12},{8,2},{10,0},{12,6},{14,4},{1,11},{3,9}... | collective-permute-start | bytes 393224 | tf_op jit(solution)/shard_map/ppermute | solution.py:192
  41.4 14.9 %collective-permute-start.14 = (bf16[512,128]{1,0:T(8,128)(2,1)S(1)}, bf16[512,128]{1,0:T(8,128)(2,1)S(1)}, u32[]{:S(2)}, u32[]{:S(2)}) collective-permute-start(bf16[512,128]{1,0:T(8,128)(2,1)S(1)} %get-tuple-element.41), channel_id=1, source_target_pairs={{0,14},{2,12},{4,10},{6,8},{8,6},{10,4},{12,2},{14,0},{1,15},{3,13... | collective-permute-start | bytes 393224 | tf_op jit(solution)/shard_map/ppermute | solution.py:192
  42.7 13.6 %collective-permute-start.13 = (bf16[512,128]{1,0:T(8,128)(2,1)S(1)}, bf16[512,128]{1,0:T(8,128)(2,1)S(1)}, u32[]{:S(2)}, u32[]{:S(2)}) collective-permute-start(bf16[512,128]{1,0:T(8,128)(2,1)S(1)} %get-tuple-element.46), channel_id=1, source_target_pairs={{0,6},{2,4},{4,2},{6,0},{8,14},{10,12},{12,10},{14,8},{1,7},{3,5},... | collective-permute-start | bytes 393224 | tf_op jit(solution)/shard_map/ppermute | solution.py:192

commit v23 on v22

--- a/solution.py
+++ b/solution.py
@@ -8,14 +8,15 @@
 from jax.sharding import PartitionSpec as P
 
 adapter_alpha = 128.0
-FETCH = (4, 1, 2, 5, 6, 3, 7)
+FETCH = (4, 1, 2, 5, 7, 3, 6)
 FETCH_TIES = {}
 SEND = (6, 1, 2, 4, 5, 3, 7)
 SEND_TIES = {3: 6}
 PREP_AFTER = 1
 LATE = (5, 3, 7)
-RANK_LAST = (3, 7)
+RANK_LAST = (3, 6)
 SEND_FIRST = 1
+FIRST_VMEM = 63
 FETCH_FIRST = 1
 
 in_vmem = pl.BlockSpec(memory_space=pltpu.VMEM)
@@ -217,10 +218,10 @@
             functools.partial(gather_kernel, part),
             [straight] * len(part),
             [in_smem, in_smem, in_hbm],
-            [in_vmem] * len(part),
+            [in_vmem if sent else in_hbm] * len(part),
             [pltpu.SemaphoreType.DMA((len(part),))],
             moved=1024,
-            vmem=53,
+            vmem=53 if sent else FIRST_VMEM,
         )(ids, me, table)
         me = lax.optimization_barrier((here, *sent))[0]
     pairs = exchange(dict(zip(FETCH, sent)), FETCH_TIES)

time: 57.9 us -> 61 us (1.054)
  Pallas kernels: 15.4 us -> 19.7 us
  starting transfers between devices: 27.6 us -> 26 us
  waiting for transfers between devices: 13.3 us -> 14.1 us
  local copies, waits for them, and re-layouts: 0.66 us -> 0.03 us
    pallas_call x2, Pallas kernels: 3.35 us -> 7.68 us  [with_kernels(): call(functools.partial(gather_kernel, part), [straight] * len(part), [in_...]
    ppermute x14, starting transfers between devices: 27.5 us -> 26 us  [exchange(): out[k] = lax.ppermute(piece, 'dp', [(i, i ^ k) for i in range(owners)])]
    ppermute x14, waiting for transfers between devices: 12.1 us -> 12.9 us  [exchange(): out[k] = lax.ppermute(piece, 'dp', [(i, i ^ k) for i in range(owners)])]
    unnamed x8, local copies, waits for them, and re-layouts: 0.66 us -> 0.02 us
  transfers between devices with their start and end apart: 15 -> 15, of which waited for: 5 -> 5; matrix products, arithmetic and copies ran while one was open for 0% -> 0% of each run, Pallas kernels for 21% -> 20%
where the time goes in v23:
time: 61 us; the launch traced here: 60.7 us
  starting transfers between devices  26 us (43%)
  Pallas kernels  19.7 us (32%)
  waiting for transfers between devices  14.1 us (23%)
  between operations  0.76 us (1%)
    ppermute x14, starting transfers between devices, exchange(): out[k] = lax.ppermute(piece, 'dp', [(i, i ^ k) for i in range(owners)])  26 us
    ppermute x14, waiting for transfers between devices, exchange(): out[k] = lax.ppermute(piece, 'dp', [(i, i ^ k) for i in range(owners)])  12.9 us
    pallas_call x2, Pallas kernels, with_kernels(): call(functools.partial(gather_kernel, part), [straight] * len(part), [in_...  7.68 us
    pallas_call x1, Pallas kernels, with_kernels(): call(prep_kernel, [jax.ShapeDtypeStruct((owners, rows, 2 * tokens), bf16)...  5.94 us
    pallas_call x2, Pallas kernels, merge(): call(functools.partial(merge_kernel, tuple(merged), handled, others), jax...  2.77 us
    pallas_call x1, Pallas kernels, with_kernels(): call(functools.partial(input_kernel, tuple(pairs), scale), jax.ShapeDtype...  1.45 us
    ppermute x1, waiting for transfers between devices, across_cores(): return lax.ppermute(value, 'tensor', [(i, i ^ 1) for i in range(cores)])  1.24 us
  transfers between devices with their start and end apart: 15, of which 5 were waited for; matrix products, arithmetic and copies ran while one was open for 0% of the time, Pallas kernels for 20%

profile of v23, /device:TPU:0, one launch (start us, length us, event | category | flops | bytes accessed | tf_op | source)
XLA Modules:
  0.0 60.7 jit_solution(17045828891809316927)
XLA Ops:
  0.7 5.9 %shard_map.68 = bf16[512,128]{1,0:T(8,128)(2,1)} custom-call(s32[8]{0:T(128)} %bitcast.7, s32[1]{0:T(128)} %bitcast.here, bf16[96,512,128]{2,1,0:T(8,128)(2,1)} %bitcast.11), custom_call_target="tpu_custom_call" | custom-call | bytes 1024 | tf_op jit(solution)/shard_map/pallas_call | solution.py:217
  6.5 0.0 copy-start
  6.6 0.0 copy-start.1
  6.6 4.1 %collective-permute-start.1 = (bf16[512,128]{1,0:T(8,128)(2,1)}, bf16[512,128]{1,0:T(8,128)(2,1)S(1)}, u32[]{:S(2)}, u32[]{:S(2)}) collective-permute-start(bf16[512,128]{1,0:T(8,128)(2,1)} %shard_map.68), channel_id=1, source_target_pairs={{0,8},{2,10},{4,12},{6,14},{8,0},{10,2},{12,4},{14,6},{1,9},{3,11}... | collective-permute-start | bytes 393224 | tf_op jit(solution)/shard_map/ppermute | solution.py:193
  10.7 1.8 %shard_map.69 = (bf16[512,128]{1,0:T(8,128)(2,1)S(1)}, bf16[512,128]{1,0:T(8,128)(2,1)S(1)}, bf16[512,128]{1,0:T(8,128)(2,1)S(1)}, bf16[512,128]{1,0:T(8,128)(2,...) custom-call(s32[8]{0:T(128)S(1)} %bitcast.8, s32[1]{0:T(128)} %bitcast.here, ...), custom_call_target="tpu_custom_call" | custom-call | bytes 1024 | tf_op jit(solution)/shard_map/pallas_call | solution.py:217
  12.5 1.6 %collective-permute-start = (bf16[512,128]{1,0:T(8,128)(2,1)S(1)}, bf16[512,128]{1,0:T(8,128)(2,1)S(1)}, u32[]{:S(2)}, u32[]{:S(2)}) collective-permute-start(bf16[512,128]{1,0:T(8,128)(2,1)S(1)} %get-tuple-element.26), channel_id=1, source_target_pairs={{0,2},{2,0},{4,6},{6,4},{8,10},{10,8},{12,14},{14,12},{1,3},{3,1},... | collective-permute-start | bytes 393224 | tf_op jit(solution)/shard_map/ppermute | solution.py:193
  14.0 1.6 %collective-permute-start.2 = (bf16[512,128]{1,0:T(8,128)(2,1)S(1)}, bf16[512,128]{1,0:T(8,128)(2,1)S(1)}, u32[]{:S(2)}, u32[]{:S(2)}) collective-permute-start(bf16[512,128]{1,0:T(8,128)(2,1)S(1)} %get-tuple-element.30), channel_id=1, source_target_pairs={{0,4},{2,6},{4,0},{6,2},{8,12},{10,14},{12,8},{14,10},{1,5},{3,7},... | collective-permute-start | bytes 393224 | tf_op jit(solution)/shard_map/ppermute | solution.py:193
  15.6 0.3 collective-permute-start.3
  15.9 3.4 %collective-permute-start.4 = (bf16[512,128]{1,0:T(8,128)(2,1)S(1)}, bf16[512,128]{1,0:T(8,128)(2,1)S(1)}, u32[]{:S(2)}, u32[]{:S(2)}) collective-permute-start(bf16[512,128]{1,0:T(8,128)(2,1)S(1)} %get-tuple-element.32), channel_id=1, source_target_pairs={{0,14},{2,12},{4,10},{6,8},{8,6},{10,4},{12,2},{14,0},{1,15},{3,13... | collective-permute-start | bytes 393224 | tf_op jit(solution)/shard_map/ppermute | solution.py:193
  19.3 0.9 %collective-permute-start.5 = (bf16[512,128]{1,0:T(8,128)(2,1)S(1)}, bf16[512,128]{1,0:T(8,128)(2,1)S(1)}, u32[]{:S(2)}, u32[]{:S(2)}) collective-permute-start(bf16[512,128]{1,0:T(8,128)(2,1)S(1)} %get-tuple-element.34), channel_id=1, source_target_pairs={{0,6},{2,4},{4,2},{6,0},{8,14},{10,12},{12,10},{14,8},{1,7},{3,5},... | collective-permute-start | bytes 393224 | tf_op jit(solution)/shard_map/ppermute | solution.py:193
  20.2 0.0 collective-permute-done.after.refs_1_
  20.2 1.2 %collective-permute-start.6 = (bf16[512,128]{1,0:T(8,128)(2,1)S(1)}, bf16[512,128]{1,0:T(8,128)(2,1)S(1)}, u32[]{:S(2)}, u32[]{:S(2)}) collective-permute-start(bf16[512,128]{1,0:T(8,128)(2,1)S(1)} %get-tuple-element.35), channel_id=1, source_target_pairs={{0,12},{2,14},{4,8},{6,10},{8,4},{10,6},{12,0},{14,2},{1,13},{3,15... | collective-permute-start | bytes 393224 | tf_op jit(solution)/shard_map/ppermute | solution.py:193
  21.4 5.9 %shard_map.70 = (bf16[8,512,256]{2,1,0:T(8,128)(2,1)S(1)}, bf16[512,128]{1,0:T(8,128)(2,1)S(1)}, f32[128,128]{1,0:T(8,128)S(1)}, f32[8,128]{1,0:T(8,128)S(1)}, s...) custom-call(s32[8]{0:T(128)S(1)} %bitcast.9, s32[1]{0:T(128)} %bitcast.here, s32[8]{0:T(128)S(1)} %bitcast.10, ...), custom_call_target="tpu_custom_call" | custom-call | bytes 16777216 | tf_op jit(solution)/shard_map/pallas_call | solution.py:230
  27.4 1.4 %collective-permute-done.3.refs_3_ = bf16[512,128]{1,0:T(8,128)(2,1)S(1)} collective-permute-done((bf16[512,128]{1,0:T(8,128)(2,1)S(1)}, bf16[512,128]{1,0:T(8,128)(2,1)S(1)}, u32[]{:S(2)}, u32[]{:S(2)}) %collective-permute-start.3) | collective-permute-done | bytes 131104 | tf_op jit(solution)/shard_map/ppermute | solution.py:193
  28.8 0.6 shard_map.71.so_far
  29.3 2.4 %collective-permute-done.5.refs_0_.refs_5_ = bf16[512,128]{1,0:T(8,128)(2,1)S(1)} collective-permute-done((bf16[512,128]{1,0:T(8,128)(2,1)S(1)}, bf16[512,128]{1,0:T(8,128)(2,1)S(1)}, u32[]{:S(2)}, u32[]{:S(2)}) %collective-permute-start.5) | collective-permute-done | bytes 131104 | tf_op jit(solution)/shard_map/ppermute | solution.py:193
  31.8 0.3 shard_map.72.mine
  32.0 0.1 collective-permute-start.7
  32.1 1.2 %collective-permute-done.7.other = f32[128,128]{1,0:T(8,128)S(1)} collective-permute-done((f32[128,128]{1,0:T(8,128)S(1)}, f32[128,128]{1,0:T(8,128)S(1)}, u32[]{:S(2)}, u32[]{:S(2)}) %collective-permute-start.7) | collective-permute-done | bytes 65568 | tf_op jit(solution)/shard_map/ppermute | solution.py:199
  33.4 0.3 shard_map.73
  33.7 2.9 %collective-permute-start.8 = (bf16[512,128]{1,0:T(8,128)(2,1)S(1)}, bf16[512,128]{1,0:T(8,128)(2,1)S(1)}, u32[]{:S(2)}, u32[]{:S(2)}) collective-permute-start(bf16[512,128]{1,0:T(8,128)(2,1)S(1)} %shard_map.73), channel_id=1, source_target_pairs={{0,12},{2,14},{4,8},{6,10},{8,4},{10,6},{12,0},{14,2},{1,13},{3,15... | collective-permute-start | bytes 393224 | tf_op jit(solution)/shard_map/ppermute | solution.py:193
  36.5 0.7 %shard_map.74 = (bf16[512,128]{1,0:T(8,128)(2,1)S(1)}, bf16[512,128]{1,0:T(8,128)(2,1)S(1)}, bf16[512,128]{1,0:T(8,128)(2,1)S(1)}, bf16[512,128]{1,0:T(8,128)(2,...) custom-call(s32[1]{0:T(128)} %bitcast.here, ...), custom_call_target="tpu_custom_call" | custom-call | bytes 1024 | tf_op jit(solution)/shard_map/pallas_call | solution.py:265
  37.3 1.2 %collective-permute-start.9 = (bf16[512,128]{1,0:T(8,128)(2,1)S(1)}, bf16[512,128]{1,0:T(8,128)(2,1)S(1)}, u32[]{:S(2)}, u32[]{:S(2)}) collective-permute-start(bf16[512,128]{1,0:T(8,128)(2,1)S(1)} %get-tuple-element.36), channel_id=1, source_target_pairs={{0,2},{2,0},{4,6},{6,4},{8,10},{10,8},{12,14},{14,12},{1,3},{3,1},... | collective-permute-start | bytes 393224 | tf_op jit(solution)/shard_map/ppermute | solution.py:193
  38.5 3.0 %collective-permute-start.10 = (bf16[512,128]{1,0:T(8,128)(2,1)S(1)}, bf16[512,128]{1,0:T(8,128)(2,1)S(1)}, u32[]{:S(2)}, u32[]{:S(2)}) collective-permute-start(bf16[512,128]{1,0:T(8,128)(2,1)S(1)} %get-tuple-element.37), channel_id=1, source_target_pairs={{0,4},{2,6},{4,0},{6,2},{8,12},{10,14},{12,8},{14,10},{1,5},{3,7},... | collective-permute-start | bytes 393224 | tf_op jit(solution)/shard_map/ppermute | solution.py:193
  41.6 2.9 %collective-permute-start.12 = (bf16[512,128]{1,0:T(8,128)(2,1)S(1)}, bf16[512,128]{1,0:T(8,128)(2,1)S(1)}, u32[]{:S(2)}, u32[]{:S(2)}) collective-permute-start(bf16[512,128]{1,0:T(8,128)(2,1)S(1)} %get-tuple-element.39), channel_id=1, source_target_pairs={{0,10},{2,8},{4,14},{6,12},{8,2},{10,0},{12,6},{14,4},{1,11},{3,9}... | collective-permute-start | bytes 393224 | tf_op jit(solution)/shard_map/ppermute | solution.py:193
  44.4 2.1 %collective-permute-start.14 = (bf16[512,128]{1,0:T(8,128)(2,1)S(1)}, bf16[512,128]{1,0:T(8,128)(2,1)S(1)}, u32[]{:S(2)}, u32[]{:S(2)}) collective-permute-start(bf16[512,128]{1,0:T(8,128)(2,1)S(1)} %get-tuple-element.41), channel_id=1, source_target_pairs={{0,14},{2,12},{4,10},{6,8},{8,6},{10,4},{12,2},{14,0},{1,15},{3,13... | collective-permute-start | bytes 393224 | tf_op jit(solution)/shard_map/ppermute | solution.py:193
  46.5 0.8 %collective-permute-start.13 = (bf16[512,128]{1,0:T(8,128)(2,1)S(1)}, bf16[512,128]{1,0:T(8,128)(2,1)S(1)}, u32[]{:S(2)}, u32[]{:S(2)}) collective-permute-start(bf16[512,128]{1,0:T(8,128)(2,1)S(1)} %get-tuple-element.46), channel_id=1, source_target_pairs={{0,6},{2,4},{4,2},{6,0},{8,14},{10,12},{12,10},{14,8},{1,7},{3,5},... | collective-permute-start | bytes 393224 | tf_op jit(solution)/shard_map/ppermute | solution.py:193
  47.4 1.4 %shard_map.75 = bf16[128,4096]{1,0:T(8,128)(2,1)} custom-call(s32[1]{0:T(128)} %bitcast.here, f32[128,128]{1,0:T(8,128)S(1)} %get-tuple-element.27.live, f32[128,128]{1,0:T(8,128)S(1)} %shard_map.72.mine, f32[128,128]{1,0:T(8,128)S(1)} %collective-permute-done.7.other, bf16[512,128]{1,0:T(8,128)(2,1)S(1)} %collective-permute-done.1.refs_0_, ...), custom_call_target="tpu_custom_call" | custom-call | flops 134217728 | bytes 2097152 | tf_op jit(solution)/shard_map/pallas_call | solution.py:275
  48.8 7.7 %collective-permute-done.11.refs_3_ = bf16[512,128]{1,0:T(8,128)(2,1)S(1)} collective-permute-done((bf16[512,128]{1,0:T(8,128)(2,1)S(1)}, bf16[512,128]{1,0:T(8,128)(2,1)S(1)}, u32[]{:S(2)}, u32[]{:S(2)}) %collective-permute-start.11) | collective-permute-done | bytes 131104 | tf_op jit(solution)/shard_map/ppermute | solution.py:193
  56.5 1.4 %shard_map.76.refs_8_ = bf16[96,512,128]{2,1,0:T(8,128)(2,1)} custom-call(s32[8]{0:T(128)S(1)} %get-tuple-element.44.blocks, s32[1]{0:T(128)} %bitcast.here, f32[8,128]{1,0:T(8,128)S(1)} %get-tuple-element.45.parts, bf16[512,128]{1,0:T(8,128)(2,1)S(1)} %collective-permute-done.8.refs_0_, ...), custom_call_target="tpu_custom_call", output_to_operand_aliasing={{}: (8, {})} | custom-call | bytes 2097152 | tf_op jit(solution)/shard_map/pallas_call | solution.py:288
  57.9 1.4 %collective-permute-done.12.refs_4_ = bf16[512,128]{1,0:T(8,128)(2,1)S(1)} collective-permute-done((bf16[512,128]{1,0:T(8,128)(2,1)S(1)}, bf16[512,128]{1,0:T(8,128)(2,1)S(1)}, u32[]{:S(2)}, u32[]{:S(2)}) %collective-permute-start.12) | collective-permute-done | bytes 131104 | tf_op jit(solution)/shard_map/ppermute | solution.py:193
  59.3 1.3 %shard_map.77 = bf16[96,512,128]{2,1,0:T(8,128)(2,1)} custom-call(s32[8]{0:T(128)S(1)} %get-tuple-element.44.blocks, s32[1]{0:T(128)} %bitcast.here, f32[8,128]{1,0:T(8,128)S(1)} %get-tuple-element.45.parts, bf16[512,128]{1,0:T(8,128)(2,1)S(1)} %collective-permute-done.8.refs_0_, ...), custom_call_target="tpu_custom_call", output_to_operand_aliasing={{}: (11, {})} | custom-call | bytes 2097152 | tf_op jit(solution)/shard_map/pallas_call | solution.py:288
  (17 shorter events, 0.0 us)
Async XLA Ops:
  0.6 10.0 %copy-start.2 = (s32[8,1]{0,1:T(1,128)S(1)}, s32[8,1]{0,1:T(1,128)}, u32[]{:S(2)}) copy-start(s32[8,1]{0,1:T(1,128)} %param.8) | copy-start | bytes 100
  0.6 20.8 %copy-start.3 = (s32[8,1]{0,1:T(1,128)S(1)}, s32[8,1]{0,1:T(1,128)}, u32[]{:S(2)}) copy-start(s32[8,1]{0,1:T(1,128)} %param.9) | copy-start | bytes 100
  6.5 14.9 %copy-start = (bf16[128,4096]{1,0:T(8,128)(2,1)S(1)}, bf16[128,4096]{1,0:T(8,128)(2,1)}, u32[]{:S(2)}) copy-start(bf16[128,4096]{1,0:T(8,128)(2,1)} %x.3) | copy-start | bytes 3145732
  6.6 14.9 %copy-start.1 = (bf16[128,4096]{1,0:T(8,128)(2,1)S(1)}, bf16[128,4096]{1,0:T(8,128)(2,1)}, u32[]{:S(2)}) copy-start(bf16[128,4096]{1,0:T(8,128)(2,1)} %y.5) | copy-start | bytes 3145732
  6.6 12.8 %collective-permute-start.1 = (bf16[512,128]{1,0:T(8,128)(2,1)}, bf16[512,128]{1,0:T(8,128)(2,1)S(1)}, u32[]{:S(2)}, u32[]{:S(2)}) collective-permute-start(bf16[512,128]{1,0:T(8,128)(2,1)} %shard_map.68), channel_id=1, source_target_pairs={{0,8},{2,10},{4,12},{6,14},{8,0},{10,2},{12,4},{14,6},{1,9},{3,11}... | collective-permute-start | bytes 393224 | tf_op jit(solution)/shard_map/ppermute | solution.py:193
  12.5 7.8 %collective-permute-start = (bf16[512,128]{1,0:T(8,128)(2,1)S(1)}, bf16[512,128]{1,0:T(8,128)(2,1)S(1)}, u32[]{:S(2)}, u32[]{:S(2)}) collective-permute-start(bf16[512,128]{1,0:T(8,128)(2,1)S(1)} %get-tuple-element.26), channel_id=1, source_target_pairs={{0,2},{2,0},{4,6},{6,4},{8,10},{10,8},{12,14},{14,12},{1,3},{3,1},... | collective-permute-start | bytes 393224 | tf_op jit(solution)/shard_map/ppermute | solution.py:193
  14.0 13.3 %collective-permute-start.2 = (bf16[512,128]{1,0:T(8,128)(2,1)S(1)}, bf16[512,128]{1,0:T(8,128)(2,1)S(1)}, u32[]{:S(2)}, u32[]{:S(2)}) collective-permute-start(bf16[512,128]{1,0:T(8,128)(2,1)S(1)} %get-tuple-element.30), channel_id=1, source_target_pairs={{0,4},{2,6},{4,0},{6,2},{8,12},{10,14},{12,8},{14,10},{1,5},{3,7},... | collective-permute-start | bytes 393224 | tf_op jit(solution)/shard_map/ppermute | solution.py:193
  15.6 13.1 %collective-permute-start.3 = (bf16[512,128]{1,0:T(8,128)(2,1)S(1)}, bf16[512,128]{1,0:T(8,128)(2,1)S(1)}, u32[]{:S(2)}, u32[]{:S(2)}) collective-permute-start(bf16[512,128]{1,0:T(8,128)(2,1)S(1)} %get-tuple-element.31), channel_id=1, source_target_pairs={{0,10},{2,8},{4,14},{6,12},{8,2},{10,0},{12,6},{14,4},{1,11},{3,9}... | collective-permute-start | bytes 393224 | tf_op jit(solution)/shard_map/ppermute | solution.py:193
  15.9 12.8 %collective-permute-start.4 = (bf16[512,128]{1,0:T(8,128)(2,1)S(1)}, bf16[512,128]{1,0:T(8,128)(2,1)S(1)}, u32[]{:S(2)}, u32[]{:S(2)}) collective-permute-start(bf16[512,128]{1,0:T(8,128)(2,1)S(1)} %get-tuple-element.32), channel_id=1, source_target_pairs={{0,14},{2,12},{4,10},{6,8},{8,6},{10,4},{12,2},{14,0},{1,15},{3,13... | collective-permute-start | bytes 393224 | tf_op jit(solution)/shard_map/ppermute | solution.py:193
  19.3 12.4 %collective-permute-start.5 = (bf16[512,128]{1,0:T(8,128)(2,1)S(1)}, bf16[512,128]{1,0:T(8,128)(2,1)S(1)}, u32[]{:S(2)}, u32[]{:S(2)}) collective-permute-start(bf16[512,128]{1,0:T(8,128)(2,1)S(1)} %get-tuple-element.34), channel_id=1, source_target_pairs={{0,6},{2,4},{4,2},{6,0},{8,14},{10,12},{12,10},{14,8},{1,7},{3,5},... | collective-permute-start | bytes 393224 | tf_op jit(solution)/shard_map/ppermute | solution.py:193
  20.2 11.5 %collective-permute-start.6 = (bf16[512,128]{1,0:T(8,128)(2,1)S(1)}, bf16[512,128]{1,0:T(8,128)(2,1)S(1)}, u32[]{:S(2)}, u32[]{:S(2)}) collective-permute-start(bf16[512,128]{1,0:T(8,128)(2,1)S(1)} %get-tuple-element.35), channel_id=1, source_target_pairs={{0,12},{2,14},{4,8},{6,10},{8,4},{10,6},{12,0},{14,2},{1,13},{3,15... | collective-permute-start | bytes 393224 | tf_op jit(solution)/shard_map/ppermute | solution.py:193
  32.0 1.3 %collective-permute-start.7 = (f32[128,128]{1,0:T(8,128)S(1)}, f32[128,128]{1,0:T(8,128)S(1)}, u32[]{:S(2)}, u32[]{:S(2)}) collective-permute-start(f32[128,128]{1,0:T(8,128)S(1)} %shard_map.72.mine), channel_id=1, source_target_pairs={{0,1},{1,0},{2,3},{3,2},{4,5},{5,4},{6,7},{7,6},{8,9},{9,8},{10,11... | collective-permute-start | bytes 196616 | tf_op jit(solution)/shard_map/ppermute | solution.py:199
  33.7 10.8 %collective-permute-start.8 = (bf16[512,128]{1,0:T(8,128)(2,1)S(1)}, bf16[512,128]{1,0:T(8,128)(2,1)S(1)}, u32[]{:S(2)}, u32[]{:S(2)}) collective-permute-start(bf16[512,128]{1,0:T(8,128)(2,1)S(1)} %shard_map.73), channel_id=1, source_target_pairs={{0,12},{2,14},{4,8},{6,10},{8,4},{10,6},{12,0},{14,2},{1,13},{3,15... | collective-permute-start | bytes 393224 | tf_op jit(solution)/shard_map/ppermute | solution.py:193
  37.3 9.2 %collective-permute-start.9 = (bf16[512,128]{1,0:T(8,128)(2,1)S(1)}, bf16[512,128]{1,0:T(8,128)(2,1)S(1)}, u32[]{:S(2)}, u32[]{:S(2)}) collective-permute-start(bf16[512,128]{1,0:T(8,128)(2,1)S(1)} %get-tuple-element.36), channel_id=1, source_target_pairs={{0,2},{2,0},{4,6},{6,4},{8,10},{10,8},{12,14},{14,12},{1,3},{3,1},... | collective-permute-start | bytes 393224 | tf_op jit(solution)/shard_map/ppermute | solution.py:193
  38.5 10.3 %collective-permute-start.10 = (bf16[512,128]{1,0:T(8,128)(2,1)S(1)}, bf16[512,128]{1,0:T(8,128)(2,1)S(1)}, u32[]{:S(2)}, u32[]{:S(2)}) collective-permute-start(bf16[512,128]{1,0:T(8,128)(2,1)S(1)} %get-tuple-element.37), channel_id=1, source_target_pairs={{0,4},{2,6},{4,0},{6,2},{8,12},{10,14},{12,8},{14,10},{1,5},{3,7},... | collective-permute-start | bytes 393224 | tf_op jit(solution)/shard_map/ppermute | solution.py:193
  41.5 14.9 %collective-permute-start.11 = (bf16[512,128]{1,0:T(8,128)(2,1)S(1)}, bf16[512,128]{1,0:T(8,128)(2,1)S(1)}, u32[]{:S(2)}, u32[]{:S(2)}) collective-permute-start(bf16[512,128]{1,0:T(8,128)(2,1)S(1)} %get-tuple-element.38), channel_id=1, source_target_pairs={{0,8},{2,10},{4,12},{6,14},{8,0},{10,2},{12,4},{14,6},{1,9},{3,11}... | collective-permute-start | bytes 393224 | tf_op jit(solution)/shard_map/ppermute | solution.py:193
  41.6 17.8 %collective-permute-start.12 = (bf16[512,128]{1,0:T(8,128)(2,1)S(1)}, bf16[512,128]{1,0:T(8,128)(2,1)S(1)}, u32[]{:S(2)}, u32[]{:S(2)}) collective-permute-start(bf16[512,128]{1,0:T(8,128)(2,1)S(1)} %get-tuple-element.39), channel_id=1, source_target_pairs={{0,10},{2,8},{4,14},{6,12},{8,2},{10,0},{12,6},{14,4},{1,11},{3,9}... | collective-permute-start | bytes 393224 | tf_op jit(solution)/shard_map/ppermute | solution.py:193
  44.4 14.9 %collective-permute-start.14 = (bf16[512,128]{1,0:T(8,128)(2,1)S(1)}, bf16[512,128]{1,0:T(8,128)(2,1)S(1)}, u32[]{:S(2)}, u32[]{:S(2)}) collective-permute-start(bf16[512,128]{1,0:T(8,128)(2,1)S(1)} %get-tuple-element.41), channel_id=1, source_target_pairs={{0,14},{2,12},{4,10},{6,8},{8,6},{10,4},{12,2},{14,0},{1,15},{3,13... | collective-permute-start | bytes 393224 | tf_op jit(solution)/shard_map/ppermute | solution.py:193
  46.5 12.8 %collective-permute-start.13 = (bf16[512,128]{1,0:T(8,128)(2,1)S(1)}, bf16[512,128]{1,0:T(8,128)(2,1)S(1)}, u32[]{:S(2)}, u32[]{:S(2)}) collective-permute-start(bf16[512,128]{1,0:T(8,128)(2,1)S(1)} %get-tuple-element.46), channel_id=1, source_target_pairs={{0,6},{2,4},{4,2},{6,0},{8,14},{10,12},{12,10},{14,8},{1,7},{3,5},... | collective-permute-start | bytes 393224 | tf_op jit(solution)/shard_map/ppermute | solution.py:193

commit v24 on v22

--- a/solution.py
+++ b/solution.py
@@ -52,14 +52,13 @@
         copy.wait()
 
 
-def prep_kernel(ids, here, lengths, table, after, x, y, turned, own, live, parts, blocks, blank, zeros, sem, own_sem):
+def prep_kernel(ids, here, lengths, table, after, x, y, turned, own, live, parts, blank, zeros, sem, own_sem):
     own_copy = pltpu.make_async_copy(table.at[ids[here[0]]], own, own_sem)
     own_copy.start()
     rows = own.shape[0]
     marked = lax.broadcasted_iota(jnp.int32, live.shape, 0) < lengths[here[0]]
     live[...] = jnp.where(marked, 1.0, 0.0)
     for n in range(ids.shape[0]):
-        blocks[n] = ids[n]
         count = jnp.int32(0)
         for other in range(ids.shape[0]):
             count += jnp.where(ids[other] == ids[n], lengths[other], 0)
@@ -133,13 +132,30 @@
         ).astype(jnp.bfloat16)
 
 
-def merge_kernel(peers, handled, others, blocks, here, parts, *refs):
-    pieces = dict(zip(peers, refs[:-7]))
-    out, total, held, sems, ids, ids_sem = refs[-6:]
+def adapter_words(ids, bits):
+    per_word = 31 // bits
+    words = []
+    for start in range(0, ids.shape[0], per_word):
+        group = ids[start : start + per_word]
+        words.append(jnp.sum(group << (bits * jnp.arange(group.shape[0], dtype=jnp.int32))))
+    return words
+
+
+def adapter_from(words, bits, block):
+    per_word = 31 // bits
+    word = words[0][0]
+    for n in range(1, len(words)):
+        word = jnp.where(block >= n * per_word, words[n][0], word)
+    return (word >> (bits * lax.rem(block, per_word))) & (2**bits - 1)
+
+
+def merge_kernel(peers, handled, others, bits, n_words, *refs):
+    words, (here, parts), refs = refs[:n_words], refs[n_words : n_words + 2], refs[n_words + 2 :]
+    pieces = dict(zip(peers, refs[:-5]))
+    out, total, held, sems = refs[-4:]
     me = here[0]
     others_here = all(k in pieces for k in others)
-    ids_copy = pltpu.make_async_copy(blocks, ids, ids_sem)
-    ids_copy.start()
+    ids = {k: adapter_from(words, bits, me ^ k) for k in (*handled, *others)}
 
     def value(k):
         return pieces[k][...].astype(jnp.float32)
@@ -152,12 +168,11 @@
 
     for n, k in enumerate(handled):
         store(n, value(k))
-    ids_copy.wait()
     copies, chosen = [], []
     for n, k in enumerate(handled):
-        adapter = ids[me ^ k]
+        adapter = ids[k]
         copies.append(pltpu.make_async_copy(held.at[n], out.at[adapter], sems.at[n]))
-        same = {other: ids[me ^ other] == adapter for other in (*handled, *others) if other != k}
+        same = {other: ids[other] == adapter for other in (*handled, *others) if other != k}
         skip = either([same[other] for other in handled[:n]])
         adding = list(handled[n + 1 :])
         if others_here:
@@ -226,18 +241,17 @@
     pairs = exchange(dict(zip(FETCH, sent)), FETCH_TIES)
 
     step = 8
-    turned, own, live, parts, blocks, blank = call(
+    turned, own, live, parts, blank = call(
         prep_kernel,
         [
             jax.ShapeDtypeStruct((owners, rows, 2 * tokens), bf16),
             straight,
             jax.ShapeDtypeStruct((tokens, width), f32),
             jax.ShapeDtypeStruct((owners, width), f32),
-            jax.ShapeDtypeStruct((owners,), jnp.int32),
             jax.ShapeDtypeStruct(table.shape, bf16),
         ],
         [in_smem, in_smem, in_smem, in_hbm, in_hbm, in_vmem, in_vmem],
-        [in_vmem, in_vmem, in_vmem, in_vmem, in_smem, in_hbm],
+        [in_vmem, in_vmem, in_vmem, in_vmem, in_hbm],
         [
             pltpu.VMEM((step, rows, width), bf16),
             pltpu.SemaphoreType.DMA((count // step,)),
@@ -280,25 +294,25 @@
         moved=token_bytes + pair_bytes,
     )(here, live, lax.optimization_barrier((mine, *pieces))[0], other, *pairs.values())
 
+    bits = (count - 1).bit_length()
+    words = [word.reshape(1) for word in adapter_words(ids, bits)]
     late = tuple(k for k in peers if k in LATE)
     early = tuple(k for k in peers if k not in LATE)
 
     def merge(handled, others, merged, so_far):
         return call(
-            functools.partial(merge_kernel, tuple(merged), handled, others),
+            functools.partial(merge_kernel, tuple(merged), handled, others, bits, len(words)),
             jax.ShapeDtypeStruct(table.shape, bf16),
-            [in_hbm, in_smem, in_vmem] + [in_vmem] * len(merged) + [in_hbm],
+            [in_smem] * (len(words) + 1) + [in_vmem] * (1 + len(merged)) + [in_hbm],
             in_hbm,
             [
                 pltpu.VMEM((rows, width), f32),
                 pltpu.VMEM((len(handled), rows, width), bf16),
                 pltpu.SemaphoreType.DMA((len(handled),)),
-                pltpu.SMEM((owners,), jnp.int32),
-                pltpu.SemaphoreType.DMA,
             ],
             moved=2 * pair_bytes,
-            aliases={3 + len(merged): 0},
-        )(blocks, here, parts, *merged.values(), so_far)
+            aliases={2 + len(words) + len(merged): 0},
+        )(*words, here, parts, *merged.values(), so_far)
 
     early_pieces = {k: arrived[k] for k in early}
     gradient = merge(late, early, arrived, merge(early, late, early_pieces, blank))

time: 57.9 us -> 58.8 us (1.016)
  Pallas kernels: 15.4 us -> 16.6 us
  waiting for transfers between devices: 13.3 us -> 12.2 us
  other arithmetic: 0 us -> 0.78 us
    pallas_call x2, Pallas kernels: 2.82 us -> 4.58 us  [merge(): call(functools.partial(merge_kernel, tuple(merged), handled, others, bits...]
    ppermute x14, waiting for transfers between devices: 12.1 us -> 10.9 us  [exchange(): out[k] = lax.ppermute(piece, 'dp', [(i, i ^ k) for i in range(owners)])]
    reduce_sum x0 -> x1, other arithmetic: none -> 0.78 us  [adapter_words(): jnp.sum(group << bits * jnp.arange(group.shape[0], dtype=jnp.int32))]
    pallas_call x1, Pallas kernels: 5.94 us -> 5.35 us  [with_kernels(): call(prep_kernel, [jax.ShapeDtypeStruct((owners, rows, 2 * tokens), bf16)...]
  transfers between devices with their start and end apart: 15 -> 15, of which waited for: 5 -> 5; matrix products, arithmetic and copies ran while one was open for 0% -> 1% of each run, Pallas kernels for 21% -> 21%
where the time goes in v24:
time: 58.8 us; the launch traced here: 58.5 us
  starting transfers between devices  27.6 us (47%)
  Pallas kernels  16.6 us (28%)
  waiting for transfers between devices  12.2 us (21%)
  other arithmetic  0.78 us (1%)
  between operations  0.74 us (1%)
  local copies, waits for them, and re-layouts  0.66 us (1%)
    ppermute x14, starting transfers between devices, exchange(): out[k] = lax.ppermute(piece, 'dp', [(i, i ^ k) for i in range(owners)])  27.5 us
    ppermute x14, waiting for transfers between devices, exchange(): out[k] = lax.ppermute(piece, 'dp', [(i, i ^ k) for i in range(owners)])  10.9 us
    pallas_call x1, Pallas kernels, with_kernels(): call(prep_kernel, [jax.ShapeDtypeStruct((owners, rows, 2 * tokens), bf16)...  5.35 us
    pallas_call x2, Pallas kernels, merge(): call(functools.partial(merge_kernel, tuple(merged), handled, others, bits...  4.58 us
    pallas_call x2, Pallas kernels, with_kernels(): call(functools.partial(gather_kernel, part), [straight] * len(part), [in_...  3.35 us
    pallas_call x1, Pallas kernels, with_kernels(): call(functools.partial(input_kernel, tuple(pairs), scale), jax.ShapeDtype...  1.45 us
    ppermute x1, waiting for transfers between devices, across_cores(): return lax.ppermute(value, 'tensor', [(i, i ^ 1) for i in range(cores)])  1.24 us
  transfers between devices with their start and end apart: 15, of which 5 were waited for; matrix products, arithmetic and copies ran while one was open for 1% of the time, Pallas kernels for 21%

profile of v24, /device:TPU:0, one launch (start us, length us, event | category | flops | bytes accessed | tf_op | source)
XLA Modules:
  0.0 58.5 jit_solution(18273234627284338450)
XLA Ops:
  0.6 0.6 %copy-done.2 = s32[8,1]{0,1:T(1,128)S(1)} copy-done((s32[8,1]{0,1:T(1,128)S(1)}, s32[8,1]{0,1:T(1,128)}, u32[]{:S(2)}) %copy-start.2) | copy-done | bytes 56
  1.3 1.6 %shard_map.68 = bf16[512,128]{1,0:T(8,128)(2,1)S(1)} custom-call(s32[8]{0:T(128)S(1)} %bitcast.17, s32[1]{0:T(128)} %bitcast.here.refs_2_, bf16[96,512,128]{2,1,0:T(8,128)(2,1)} %bitcast.21), custom_call_target="tpu_custom_call" | custom-call | bytes 1024 | tf_op jit(solution)/shard_map/pallas_call | solution.py:231
  2.9 4.1 %collective-permute-start.1 = (bf16[512,128]{1,0:T(8,128)(2,1)S(1)}, bf16[512,128]{1,0:T(8,128)(2,1)S(1)}, u32[]{:S(2)}, u32[]{:S(2)}) collective-permute-start(bf16[512,128]{1,0:T(8,128)(2,1)S(1)} %shard_map.68), channel_id=1, source_target_pairs={{0,8},{2,10},{4,12},{6,14},{8,0},{10,2},{12,4},{14,6},{1,9},{3,11}... | collective-permute-start | bytes 393224 | tf_op jit(solution)/shard_map/ppermute | solution.py:207
  7.0 1.8 %shard_map.69 = (bf16[512,128]{1,0:T(8,128)(2,1)S(1)}, bf16[512,128]{1,0:T(8,128)(2,1)S(1)}, bf16[512,128]{1,0:T(8,128)(2,1)S(1)}, bf16[512,128]{1,0:T(8,128)(2,...) custom-call(s32[8]{0:T(128)S(1)} %bitcast.18, s32[1]{0:T(128)} %bitcast.here.refs_2_, ...), custom_call_target="tpu_custom_call" | custom-call | bytes 1024 | tf_op jit(solution)/shard_map/pallas_call | solution.py:231
  8.8 1.6 %collective-permute-start = (bf16[512,128]{1,0:T(8,128)(2,1)S(1)}, bf16[512,128]{1,0:T(8,128)(2,1)S(1)}, u32[]{:S(2)}, u32[]{:S(2)}) collective-permute-start(bf16[512,128]{1,0:T(8,128)(2,1)S(1)} %get-tuple-element.25), channel_id=1, source_target_pairs={{0,2},{2,0},{4,6},{6,4},{8,10},{10,8},{12,14},{14,12},{1,3},{3,1},... | collective-permute-start | bytes 393224 | tf_op jit(solution)/shard_map/ppermute | solution.py:207
  10.3 1.6 %collective-permute-start.2 = (bf16[512,128]{1,0:T(8,128)(2,1)S(1)}, bf16[512,128]{1,0:T(8,128)(2,1)S(1)}, u32[]{:S(2)}, u32[]{:S(2)}) collective-permute-start(bf16[512,128]{1,0:T(8,128)(2,1)S(1)} %get-tuple-element.29), channel_id=1, source_target_pairs={{0,4},{2,6},{4,0},{6,2},{8,12},{10,14},{12,8},{14,10},{1,5},{3,7},... | collective-permute-start | bytes 393224 | tf_op jit(solution)/shard_map/ppermute | solution.py:207
  11.9 0.3 collective-permute-start.3
  12.2 2.5 %collective-permute-start.4 = (bf16[512,128]{1,0:T(8,128)(2,1)S(1)}, bf16[512,128]{1,0:T(8,128)(2,1)S(1)}, u32[]{:S(2)}, u32[]{:S(2)}) collective-permute-start(bf16[512,128]{1,0:T(8,128)(2,1)S(1)} %get-tuple-element.31), channel_id=1, source_target_pairs={{0,12},{2,14},{4,8},{6,10},{8,4},{10,6},{12,0},{14,2},{1,13},{3,15... | collective-permute-start | bytes 393224 | tf_op jit(solution)/shard_map/ppermute | solution.py:207
  14.7 1.6 %collective-permute-start.5 = (bf16[512,128]{1,0:T(8,128)(2,1)S(1)}, bf16[512,128]{1,0:T(8,128)(2,1)S(1)}, u32[]{:S(2)}, u32[]{:S(2)}) collective-permute-start(bf16[512,128]{1,0:T(8,128)(2,1)S(1)} %get-tuple-element.33), channel_id=1, source_target_pairs={{0,6},{2,4},{4,2},{6,0},{8,14},{10,12},{12,10},{14,8},{1,7},{3,5},... | collective-permute-start | bytes 393224 | tf_op jit(solution)/shard_map/ppermute | solution.py:207
  16.3 2.8 %collective-permute-start.6 = (bf16[512,128]{1,0:T(8,128)(2,1)S(1)}, bf16[512,128]{1,0:T(8,128)(2,1)S(1)}, u32[]{:S(2)}, u32[]{:S(2)}) collective-permute-start(bf16[512,128]{1,0:T(8,128)(2,1)S(1)} %get-tuple-element.34), channel_id=1, source_target_pairs={{0,14},{2,12},{4,10},{6,8},{8,6},{10,4},{12,2},{14,0},{1,15},{3,13... | collective-permute-start | bytes 393224 | tf_op jit(solution)/shard_map/ppermute | solution.py:207
  19.1 5.3 %shard_map.70 = (bf16[8,512,256]{2,1,0:T(8,128)(2,1)S(1)}, bf16[512,128]{1,0:T(8,128)(2,1)S(1)}, f32[128,128]{1,0:T(8,128)S(1)}, f32[8,128]{1,0:T(8,128)S(1)}, bf16[96,512,128]{2,1,0:T(8,128)(2,1)}) custom-call(s32[8]{0:T(128)S(1)} %bitcast.19, s32[1]{0:T(128)} %bitcast.here.refs_2_, s32[8]{0:T(128)S(1)} %bitcast.20, bf16[96,512,128]{2,1,0:T(8,128)(2,1)} %bitcast.23, ...), custom_call_target="tpu_custom_call" | custom-call | bytes 16777216 | tf_op jit(solution)/shard_map/pallas_call | solution.py:244
  24.5 2.2 %collective-permute-done.3.refs_3_ = bf16[512,128]{1,0:T(8,128)(2,1)S(1)} collective-permute-done((bf16[512,128]{1,0:T(8,128)(2,1)S(1)}, bf16[512,128]{1,0:T(8,128)(2,1)S(1)}, u32[]{:S(2)}, u32[]{:S(2)}) %collective-permute-start.3) | collective-permute-done | bytes 131104 | tf_op jit(solution)/shard_map/ppermute | solution.py:207
  26.7 0.0 collective-permute-done.4.refs_4_
  26.7 0.6 shard_map.71.so_far
  27.3 0.6 collective-permute-done.5.refs_0_.refs_5_
  27.8 0.3 shard_map.72.mine
  28.1 0.1 collective-permute-start.7
  28.2 1.2 %collective-permute-done.7.other = f32[128,128]{1,0:T(8,128)S(1)} collective-permute-done((f32[128,128]{1,0:T(8,128)S(1)}, f32[128,128]{1,0:T(8,128)S(1)}, u32[]{:S(2)}, u32[]{:S(2)}) %collective-permute-start.7) | collective-permute-done | bytes 65568 | tf_op jit(solution)/shard_map/ppermute | solution.py:213
  29.5 0.3 shard_map.73
  29.8 2.7 %collective-permute-start.8 = (bf16[512,128]{1,0:T(8,128)(2,1)S(1)}, bf16[512,128]{1,0:T(8,128)(2,1)S(1)}, u32[]{:S(2)}, u32[]{:S(2)}) collective-permute-start(bf16[512,128]{1,0:T(8,128)(2,1)S(1)} %shard_map.73), channel_id=1, source_target_pairs={{0,12},{2,14},{4,8},{6,10},{8,4},{10,6},{12,0},{14,2},{1,13},{3,15... | collective-permute-start | bytes 393224 | tf_op jit(solution)/shard_map/ppermute | solution.py:207
  32.5 0.7 %shard_map.74 = (bf16[512,128]{1,0:T(8,128)(2,1)S(1)}, bf16[512,128]{1,0:T(8,128)(2,1)S(1)}, bf16[512,128]{1,0:T(8,128)(2,1)S(1)}, bf16[512,128]{1,0:T(8,128)(2,...) custom-call(s32[1]{0:T(128)} %bitcast.here.refs_2_, ...), custom_call_target="tpu_custom_call" | custom-call | bytes 1024 | tf_op jit(solution)/shard_map/pallas_call | solution.py:278
  33.2 1.3 %collective-permute-start.9 = (bf16[512,128]{1,0:T(8,128)(2,1)S(1)}, bf16[512,128]{1,0:T(8,128)(2,1)S(1)}, u32[]{:S(2)}, u32[]{:S(2)}) collective-permute-start(bf16[512,128]{1,0:T(8,128)(2,1)S(1)} %get-tuple-element.35), channel_id=1, source_target_pairs={{0,2},{2,0},{4,6},{6,4},{8,10},{10,8},{12,14},{14,12},{1,3},{3,1},... | collective-permute-start | bytes 393224 | tf_op jit(solution)/shard_map/ppermute | solution.py:207
  34.5 3.1 %collective-permute-start.10 = (bf16[512,128]{1,0:T(8,128)(2,1)S(1)}, bf16[512,128]{1,0:T(8,128)(2,1)S(1)}, u32[]{:S(2)}, u32[]{:S(2)}) collective-permute-start(bf16[512,128]{1,0:T(8,128)(2,1)S(1)} %get-tuple-element.36), channel_id=1, source_target_pairs={{0,4},{2,6},{4,0},{6,2},{8,12},{10,14},{12,8},{14,10},{1,5},{3,7},... | collective-permute-start | bytes 393224 | tf_op jit(solution)/shard_map/ppermute | solution.py:207
  37.6 3.8 %collective-permute-start.12 = (bf16[512,128]{1,0:T(8,128)(2,1)S(1)}, bf16[512,128]{1,0:T(8,128)(2,1)S(1)}, u32[]{:S(2)}, u32[]{:S(2)}) collective-permute-start(bf16[512,128]{1,0:T(8,128)(2,1)S(1)} %get-tuple-element.38), channel_id=1, source_target_pairs={{0,10},{2,8},{4,14},{6,12},{8,2},{10,0},{12,6},{14,4},{1,11},{3,9}... | collective-permute-start | bytes 393224 | tf_op jit(solution)/shard_map/ppermute | solution.py:207
  41.4 1.3 %collective-permute-start.14 = (bf16[512,128]{1,0:T(8,128)(2,1)S(1)}, bf16[512,128]{1,0:T(8,128)(2,1)S(1)}, u32[]{:S(2)}, u32[]{:S(2)}) collective-permute-start(bf16[512,128]{1,0:T(8,128)(2,1)S(1)} %get-tuple-element.40), channel_id=1, source_target_pairs={{0,14},{2,12},{4,10},{6,8},{8,6},{10,4},{12,2},{14,0},{1,15},{3,13... | collective-permute-start | bytes 393224 | tf_op jit(solution)/shard_map/ppermute | solution.py:207
  42.7 0.8 %collective-permute-start.13 = (bf16[512,128]{1,0:T(8,128)(2,1)S(1)}, bf16[512,128]{1,0:T(8,128)(2,1)S(1)}, u32[]{:S(2)}, u32[]{:S(2)}) collective-permute-start(bf16[512,128]{1,0:T(8,128)(2,1)S(1)} %get-tuple-element.44), channel_id=1, source_target_pairs={{0,6},{2,4},{4,2},{6,0},{8,14},{10,12},{12,10},{14,8},{1,7},{3,5},... | collective-permute-start | bytes 393224 | tf_op jit(solution)/shard_map/ppermute | solution.py:207
  43.5 0.8 %fusion = (s32[]{:T(128)}, s32[]{:T(128)}) fusion(s32[8,1]{0,1:T(1,128)S(1)} %copy-done.2), kind=kLoop, calls=%fused_computation.1 | loop fusion | flops 18 | bytes 40 | tf_op jit(solution)/shard_map/reduce_sum | solution.py:140
  44.3 1.4 %shard_map.75 = bf16[128,4096]{1,0:T(8,128)(2,1)} custom-call(s32[1]{0:T(128)} %bitcast.here.refs_2_, f32[128,128]{1,0:T(8,128)S(1)} %get-tuple-element.26.live, f32[128,128]{1,0:T(8,128)S(1)} %shard_map.72.mine, f32[128,128]{1,0:T(8,128)S(1)} %collective-permute-done.7.other, bf16[512,128]{1,0:T(8,128)(2,1)S(1)} %collective-permute-done.1.refs_0_, ...), custom_call_target="tpu_custom_call" | custom-call | flops 134217728 | bytes 2097152 | tf_op jit(solution)/shard_map/pallas_call | solution.py:288
  45.8 6.9 %collective-permute-done.11.refs_7_ = bf16[512,128]{1,0:T(8,128)(2,1)S(1)} collective-permute-done((bf16[512,128]{1,0:T(8,128)(2,1)S(1)}, bf16[512,128]{1,0:T(8,128)(2,1)S(1)}, u32[]{:S(2)}, u32[]{:S(2)}) %collective-permute-start.11) | collective-permute-done | bytes 131104 | tf_op jit(solution)/shard_map/ppermute | solution.py:207
  52.6 2.4 %shard_map.76.refs_12_ = bf16[96,512,128]{2,1,0:T(8,128)(2,1)} custom-call(s32[1]{0:T(128)} %bitcast.5.refs_0_, s32[1]{0:T(128)} %bitcast.7.refs_1_, s32[1]{0:T(128)} %bitcast.here.refs_2_, f32[8,128]{1,0:T(8,128)S(1)} %get-tuple-element.43.refs_3_, bf16[512,128]{1,0:T(8,128)(2,1)S(1)} %collective-permute-done.8.refs_4_, ...), custom_call_target="tpu_custom_call", output_to_operand_aliasing={{}: (9, {})} | custom-call | bytes 2097152 | tf_op jit(solution)/shard_map/pallas_call | solution.py:303
  55.0 1.3 %collective-permute-done.12.refs_8_ = bf16[512,128]{1,0:T(8,128)(2,1)S(1)} collective-permute-done((bf16[512,128]{1,0:T(8,128)(2,1)S(1)}, bf16[512,128]{1,0:T(8,128)(2,1)S(1)}, u32[]{:S(2)}, u32[]{:S(2)}) %collective-permute-start.12) | collective-permute-done | bytes 131104 | tf_op jit(solution)/shard_map/ppermute | solution.py:207
  56.3 2.2 %shard_map.77 = bf16[96,512,128]{2,1,0:T(8,128)(2,1)} custom-call(s32[1]{0:T(128)} %bitcast.5.refs_0_, s32[1]{0:T(128)} %bitcast.7.refs_1_, s32[1]{0:T(128)} %bitcast.here.refs_2_, f32[8,128]{1,0:T(8,128)S(1)} %get-tuple-element.43.refs_3_, bf16[512,128]{1,0:T(8,128)(2,1)S(1)} %collective-permute-done.8.refs_4_, ...), custom_call_target="tpu_custom_call", output_to_operand_aliasing={{}: (12, {})} | custom-call | bytes 2097152 | tf_op jit(solution)/shard_map/pallas_call | solution.py:303
  (18 shorter events, 0.0 us)
Async XLA Ops:
  0.6 0.7 %copy-start.2 = (s32[8,1]{0,1:T(1,128)S(1)}, s32[8,1]{0,1:T(1,128)}, u32[]{:S(2)}) copy-start(s32[8,1]{0,1:T(1,128)} %param.8) | copy-start | bytes 100
  1.3 17.8 %copy-start = (bf16[128,4096]{1,0:T(8,128)(2,1)S(1)}, bf16[128,4096]{1,0:T(8,128)(2,1)}, u32[]{:S(2)}) copy-start(bf16[128,4096]{1,0:T(8,128)(2,1)} %x.3) | copy-start | bytes 3145732
  1.3 17.8 %copy-start.1 = (bf16[128,4096]{1,0:T(8,128)(2,1)S(1)}, bf16[128,4096]{1,0:T(8,128)(2,1)}, u32[]{:S(2)}) copy-start(bf16[128,4096]{1,0:T(8,128)(2,1)} %y.5) | copy-start | bytes 3145732
  1.3 17.8 %copy-start.3 = (s32[8,1]{0,1:T(1,128)S(1)}, s32[8,1]{0,1:T(1,128)}, u32[]{:S(2)}) copy-start(s32[8,1]{0,1:T(1,128)} %param.9) | copy-start | bytes 100
  2.9 11.8 %collective-permute-start.1 = (bf16[512,128]{1,0:T(8,128)(2,1)S(1)}, bf16[512,128]{1,0:T(8,128)(2,1)S(1)}, u32[]{:S(2)}, u32[]{:S(2)}) collective-permute-start(bf16[512,128]{1,0:T(8,128)(2,1)S(1)} %shard_map.68), channel_id=1, source_target_pairs={{0,8},{2,10},{4,12},{6,14},{8,0},{10,2},{12,4},{14,6},{1,9},{3,11}... | collective-permute-start | bytes 393224 | tf_op jit(solution)/shard_map/ppermute | solution.py:207
  8.8 7.5 %collective-permute-start = (bf16[512,128]{1,0:T(8,128)(2,1)S(1)}, bf16[512,128]{1,0:T(8,128)(2,1)S(1)}, u32[]{:S(2)}, u32[]{:S(2)}) collective-permute-start(bf16[512,128]{1,0:T(8,128)(2,1)S(1)} %get-tuple-element.25), channel_id=1, source_target_pairs={{0,2},{2,0},{4,6},{6,4},{8,10},{10,8},{12,14},{14,12},{1,3},{3,1},... | collective-permute-start | bytes 393224 | tf_op jit(solution)/shard_map/ppermute | solution.py:207
  10.3 14.2 %collective-permute-start.2 = (bf16[512,128]{1,0:T(8,128)(2,1)S(1)}, bf16[512,128]{1,0:T(8,128)(2,1)S(1)}, u32[]{:S(2)}, u32[]{:S(2)}) collective-permute-start(bf16[512,128]{1,0:T(8,128)(2,1)S(1)} %get-tuple-element.29), channel_id=1, source_target_pairs={{0,4},{2,6},{4,0},{6,2},{8,12},{10,14},{12,8},{14,10},{1,5},{3,7},... | collective-permute-start | bytes 393224 | tf_op jit(solution)/shard_map/ppermute | solution.py:207
  11.9 14.8 %collective-permute-start.3 = (bf16[512,128]{1,0:T(8,128)(2,1)S(1)}, bf16[512,128]{1,0:T(8,128)(2,1)S(1)}, u32[]{:S(2)}, u32[]{:S(2)}) collective-permute-start(bf16[512,128]{1,0:T(8,128)(2,1)S(1)} %get-tuple-element.30), channel_id=1, source_target_pairs={{0,10},{2,8},{4,14},{6,12},{8,2},{10,0},{12,6},{14,4},{1,11},{3,9}... | collective-permute-start | bytes 393224 | tf_op jit(solution)/shard_map/ppermute | solution.py:207
  12.2 14.5 %collective-permute-start.4 = (bf16[512,128]{1,0:T(8,128)(2,1)S(1)}, bf16[512,128]{1,0:T(8,128)(2,1)S(1)}, u32[]{:S(2)}, u32[]{:S(2)}) collective-permute-start(bf16[512,128]{1,0:T(8,128)(2,1)S(1)} %get-tuple-element.31), channel_id=1, source_target_pairs={{0,12},{2,14},{4,8},{6,10},{8,4},{10,6},{12,0},{14,2},{1,13},{3,15... | collective-permute-start | bytes 393224 | tf_op jit(solution)/shard_map/ppermute | solution.py:207
  14.7 13.1 %collective-permute-start.5 = (bf16[512,128]{1,0:T(8,128)(2,1)S(1)}, bf16[512,128]{1,0:T(8,128)(2,1)S(1)}, u32[]{:S(2)}, u32[]{:S(2)}) collective-permute-start(bf16[512,128]{1,0:T(8,128)(2,1)S(1)} %get-tuple-element.33), channel_id=1, source_target_pairs={{0,6},{2,4},{4,2},{6,0},{8,14},{10,12},{12,10},{14,8},{1,7},{3,5},... | collective-permute-start | bytes 393224 | tf_op jit(solution)/shard_map/ppermute | solution.py:207
  16.3 11.5 %collective-permute-start.6 = (bf16[512,128]{1,0:T(8,128)(2,1)S(1)}, bf16[512,128]{1,0:T(8,128)(2,1)S(1)}, u32[]{:S(2)}, u32[]{:S(2)}) collective-permute-start(bf16[512,128]{1,0:T(8,128)(2,1)S(1)} %get-tuple-element.34), channel_id=1, source_target_pairs={{0,14},{2,12},{4,10},{6,8},{8,6},{10,4},{12,2},{14,0},{1,15},{3,13... | collective-permute-start | bytes 393224 | tf_op jit(solution)/shard_map/ppermute | solution.py:207
  28.1 1.3 %collective-permute-start.7 = (f32[128,128]{1,0:T(8,128)S(1)}, f32[128,128]{1,0:T(8,128)S(1)}, u32[]{:S(2)}, u32[]{:S(2)}) collective-permute-start(f32[128,128]{1,0:T(8,128)S(1)} %shard_map.72.mine), channel_id=1, source_target_pairs={{0,1},{1,0},{2,3},{3,2},{4,5},{5,4},{6,7},{7,6},{8,9},{9,8},{10,11... | collective-permute-start | bytes 196616 | tf_op jit(solution)/shard_map/ppermute | solution.py:213
  29.8 11.7 %collective-permute-start.8 = (bf16[512,128]{1,0:T(8,128)(2,1)S(1)}, bf16[512,128]{1,0:T(8,128)(2,1)S(1)}, u32[]{:S(2)}, u32[]{:S(2)}) collective-permute-start(bf16[512,128]{1,0:T(8,128)(2,1)S(1)} %shard_map.73), channel_id=1, source_target_pairs={{0,12},{2,14},{4,8},{6,10},{8,4},{10,6},{12,0},{14,2},{1,13},{3,15... | collective-permute-start | bytes 393224 | tf_op jit(solution)/shard_map/ppermute | solution.py:207
  33.2 9.5 %collective-permute-start.9 = (bf16[512,128]{1,0:T(8,128)(2,1)S(1)}, bf16[512,128]{1,0:T(8,128)(2,1)S(1)}, u32[]{:S(2)}, u32[]{:S(2)}) collective-permute-start(bf16[512,128]{1,0:T(8,128)(2,1)S(1)} %get-tuple-element.35), channel_id=1, source_target_pairs={{0,2},{2,0},{4,6},{6,4},{8,10},{10,8},{12,14},{14,12},{1,3},{3,1},... | collective-permute-start | bytes 393224 | tf_op jit(solution)/shard_map/ppermute | solution.py:207
  34.5 11.2 %collective-permute-start.10 = (bf16[512,128]{1,0:T(8,128)(2,1)S(1)}, bf16[512,128]{1,0:T(8,128)(2,1)S(1)}, u32[]{:S(2)}, u32[]{:S(2)}) collective-permute-start(bf16[512,128]{1,0:T(8,128)(2,1)S(1)} %get-tuple-element.36), channel_id=1, source_target_pairs={{0,4},{2,6},{4,0},{6,2},{8,12},{10,14},{12,8},{14,10},{1,5},{3,7},... | collective-permute-start | bytes 393224 | tf_op jit(solution)/shard_map/ppermute | solution.py:207
  37.6 15.0 %collective-permute-start.11 = (bf16[512,128]{1,0:T(8,128)(2,1)S(1)}, bf16[512,128]{1,0:T(8,128)(2,1)S(1)}, u32[]{:S(2)}, u32[]{:S(2)}) collective-permute-start(bf16[512,128]{1,0:T(8,128)(2,1)S(1)} %get-tuple-element.37), channel_id=1, source_target_pairs={{0,8},{2,10},{4,12},{6,14},{8,0},{10,2},{12,4},{14,6},{1,9},{3,11}... | collective-permute-start | bytes 393224 | tf_op jit(solution)/shard_map/ppermute | solution.py:207
  37.6 18.7 %collective-permute-start.12 = (bf16[512,128]{1,0:T(8,128)(2,1)S(1)}, bf16[512,128]{1,0:T(8,128)(2,1)S(1)}, u32[]{:S(2)}, u32[]{:S(2)}) collective-permute-start(bf16[512,128]{1,0:T(8,128)(2,1)S(1)} %get-tuple-element.38), channel_id=1, source_target_pairs={{0,10},{2,8},{4,14},{6,12},{8,2},{10,0},{12,6},{14,4},{1,11},{3,9}... | collective-permute-start | bytes 393224 | tf_op jit(solution)/shard_map/ppermute | solution.py:207
  41.4 14.9 %collective-permute-start.14 = (bf16[512,128]{1,0:T(8,128)(2,1)S(1)}, bf16[512,128]{1,0:T(8,128)(2,1)S(1)}, u32[]{:S(2)}, u32[]{:S(2)}) collective-permute-start(bf16[512,128]{1,0:T(8,128)(2,1)S(1)} %get-tuple-element.40), channel_id=1, source_target_pairs={{0,14},{2,12},{4,10},{6,8},{8,6},{10,4},{12,2},{14,0},{1,15},{3,13... | collective-permute-start | bytes 393224 | tf_op jit(solution)/shard_map/ppermute | solution.py:207
  42.7 13.6 %collective-permute-start.13 = (bf16[512,128]{1,0:T(8,128)(2,1)S(1)}, bf16[512,128]{1,0:T(8,128)(2,1)S(1)}, u32[]{:S(2)}, u32[]{:S(2)}) collective-permute-start(bf16[512,128]{1,0:T(8,128)(2,1)S(1)} %get-tuple-element.44), channel_id=1, source_target_pairs={{0,6},{2,4},{4,2},{6,0},{8,14},{10,12},{12,10},{14,8},{1,7},{3,5},... | collective-permute-start | bytes 393224 | tf_op jit(solution)/shard_map/ppermute | solution.py:207

commit v25 on v22

--- a/solution.py
+++ b/solution.py
@@ -52,7 +52,11 @@
         copy.wait()
 
 
-def prep_kernel(ids, here, lengths, table, after, x, y, turned, own, live, parts, blocks, blank, zeros, sem, own_sem):
+def either(conditions):
+    return functools.reduce(jnp.logical_or, conditions, jnp.bool_(False))
+
+
+def prep_kernel(groups, ids, here, lengths, table, after, x, y, turned, own, live, parts, words, blocks, blank, zeros, sem, own_sem):
     own_copy = pltpu.make_async_copy(table.at[ids[here[0]]], own, own_sem)
     own_copy.start()
     rows = own.shape[0]
@@ -65,6 +69,21 @@
             count += jnp.where(ids[other] == ids[n], lengths[other], 0)
         denom = jnp.maximum(count.astype(jnp.float32), 1.0)
         parts[n : n + 1] = 1.0 / jnp.full((1, parts.shape[1]), denom)
+    me = here[0]
+    early, late = groups
+    for k in range(ids.shape[0]):
+        same = {other: ids[me ^ other] == ids[me ^ k] for other in range(ids.shape[0]) if other != k}
+        group, others = (late, early) if k in late else (early, late)
+        place = group.index(k)
+        skip = either([same[other] for other in group[:place]])
+        adding = list(group[place + 1 :])
+        if k in late:
+            adding += others
+        else:
+            skip |= either([same[other] for other in others])
+        more = either([same[other] for other in adding])
+        word = ids[me ^ k] + jnp.where(skip, 2**16, 0) + jnp.where(more, 2**17, 0)
+        words[k : k + 1] = jnp.full((1, words.shape[1]), word)
     zeros[...] = jnp.zeros_like(zeros)
     step = zeros.shape[0]
     copies = [
@@ -133,13 +152,11 @@
         ).astype(jnp.bfloat16)
 
 
-def merge_kernel(peers, handled, others, blocks, here, parts, *refs):
+def merge_kernel(peers, handled, others, blocks, here, parts, words, *refs):
     pieces = dict(zip(peers, refs[:-7]))
     out, total, held, sems, ids, ids_sem = refs[-6:]
     me = here[0]
     others_here = all(k in pieces for k in others)
-    ids_copy = pltpu.make_async_copy(blocks, ids, ids_sem)
-    ids_copy.start()
 
     def value(k):
         return pieces[k][...].astype(jnp.float32)
@@ -147,32 +164,24 @@
     def store(n, sum_of):
         held[n] = (sum_of * parts[pl.ds(me ^ handled[n], 1), :]).astype(jnp.bfloat16)
 
-    def either(conditions):
-        return functools.reduce(jnp.logical_or, conditions, jnp.bool_(False))
-
-    for n, k in enumerate(handled):
-        store(n, value(k))
-    ids_copy.wait()
     copies, chosen = [], []
     for n, k in enumerate(handled):
-        adapter = ids[me ^ k]
+        word = jnp.max(words[k : k + 1, :])
+        adapter = word & (2**16 - 1)
+        more = (word >> 17) == 1
         copies.append(pltpu.make_async_copy(held.at[n], out.at[adapter], sems.at[n]))
-        same = {other: ids[me ^ other] == adapter for other in (*handled, *others) if other != k}
-        skip = either([same[other] for other in handled[:n]])
-        adding = list(handled[n + 1 :])
-        if others_here:
-            adding += others
-        else:
-            skip |= either([same[other] for other in others])
-        more = either([same[other] for other in adding])
-        chosen.append(jnp.logical_not(skip))
+        chosen.append(((word >> 16) & 1) == 0)
+        store(n, value(k))
 
         @pl.when(chosen[n] & more)
         def _():
+            ids_copy = pltpu.make_async_copy(blocks, ids, ids_sem)
+            ids_copy.start()
+            ids_copy.wait()
             total[...] = value(k)
-            for other in adding:
-
-                @pl.when(same[other])
+            for other in (*handled[n + 1 :], *(others if others_here else ())):
+
+                @pl.when(ids[me ^ other] == adapter)
                 def _():
                     total[...] += value(other)
 
@@ -225,19 +234,23 @@
         me = lax.optimization_barrier((here, *sent))[0]
     pairs = exchange(dict(zip(FETCH, sent)), FETCH_TIES)
 
+    peers = (*SEND, 0)
+    late = tuple(k for k in peers if k in LATE)
+    early = tuple(k for k in peers if k not in LATE)
     step = 8
-    turned, own, live, parts, blocks, blank = call(
-        prep_kernel,
+    turned, own, live, parts, words, blocks, blank = call(
+        functools.partial(prep_kernel, (early, late)),
         [
             jax.ShapeDtypeStruct((owners, rows, 2 * tokens), bf16),
             straight,
             jax.ShapeDtypeStruct((tokens, width), f32),
             jax.ShapeDtypeStruct((owners, width), f32),
+            jax.ShapeDtypeStruct((owners, width), jnp.int32),
             jax.ShapeDtypeStruct((owners,), jnp.int32),
             jax.ShapeDtypeStruct(table.shape, bf16),
         ],
         [in_smem, in_smem, in_smem, in_hbm, in_hbm, in_vmem, in_vmem],
-        [in_vmem, in_vmem, in_vmem, in_vmem, in_smem, in_hbm],
+        [in_vmem, in_vmem, in_vmem, in_vmem, in_vmem, in_smem, in_hbm],
         [
             pltpu.VMEM((step, rows, width), bf16),
             pltpu.SemaphoreType.DMA((count // step,)),
@@ -258,7 +271,6 @@
         )(here, lax.optimization_barrier((activations, turned))[0], cotangent, mine, *[pairs[k] for k in part])
     other = across_cores(mine)
 
-    peers = (*SEND, 0)
     pieces = []
     for part in (peers[:SEND_FIRST], peers[SEND_FIRST:]):
         pieces += call(
@@ -280,14 +292,12 @@
         moved=token_bytes + pair_bytes,
     )(here, live, lax.optimization_barrier((mine, *pieces))[0], other, *pairs.values())
 
-    late = tuple(k for k in peers if k in LATE)
-    early = tuple(k for k in peers if k not in LATE)
 
     def merge(handled, others, merged, so_far):
         return call(
             functools.partial(merge_kernel, tuple(merged), handled, others),
             jax.ShapeDtypeStruct(table.shape, bf16),
-            [in_hbm, in_smem, in_vmem] + [in_vmem] * len(merged) + [in_hbm],
+            [in_hbm, in_smem] + [in_vmem] * (2 + len(merged)) + [in_hbm],
             in_hbm,
             [
                 pltpu.VMEM((rows, width), f32),
@@ -297,8 +307,8 @@
                 pltpu.SemaphoreType.DMA,
             ],
             moved=2 * pair_bytes,
-            aliases={3 + len(merged): 0},
-        )(blocks, here, parts, *merged.values(), so_far)
+            aliases={4 + len(merged): 0},
+        )(blocks, here, parts, words, *merged.values(), so_far)
 
     early_pieces = {k: arrived[k] for k in early}
     gradient = merge(late, early, arrived, merge(early, late, early_pieces, blank))

time: 57.9 us -> 57.8 us (level)
  no operation moved by 1% of the time
where the time goes in v25:
time: 57.8 us; the launch traced here: 57.6 us
  starting transfers between devices  27.6 us (48%)
  Pallas kernels  15.6 us (27%)
  waiting for transfers between devices  13 us (22%)
  between operations  0.74 us (1%)
  local copies, waits for them, and re-layouts  0.66 us (1%)
    ppermute x14, starting transfers between devices, exchange(): out[k] = lax.ppermute(piece, 'dp', [(i, i ^ k) for i in range(owners)])  27.5 us
    ppermute x14, waiting for transfers between devices, exchange(): out[k] = lax.ppermute(piece, 'dp', [(i, i ^ k) for i in range(owners)])  11.8 us
    pallas_call x1, Pallas kernels, with_kernels(): call(functools.partial(prep_kernel, (early, late)), [jax.ShapeDtypeStruct...  5.94 us
    pallas_call x2, Pallas kernels, with_kernels(): call(functools.partial(gather_kernel, part), [straight] * len(part), [in_...  3.35 us
    pallas_call x2, Pallas kernels, merge(): call(functools.partial(merge_kernel, tuple(merged), handled, others), jax...  3.03 us
    pallas_call x1, Pallas kernels, with_kernels(): call(functools.partial(input_kernel, tuple(pairs), scale), jax.ShapeDtype...  1.45 us
    ppermute x1, waiting for transfers between devices, across_cores(): return lax.ppermute(value, 'tensor', [(i, i ^ 1) for i in range(cores)])  1.24 us
  transfers between devices with their start and end apart: 15, of which 5 were waited for; matrix products, arithmetic and copies ran while one was open for 0% of the time, Pallas kernels for 21%

profile of v25, /device:TPU:0, one launch (start us, length us, event | category | flops | bytes accessed | tf_op | source)
XLA Modules:
  0.0 57.6 jit_solution(16312565524167428702)
XLA Ops:
  0.6 0.6 %copy-done.2 = s32[8,1]{0,1:T(1,128)S(1)} copy-done((s32[8,1]{0,1:T(1,128)S(1)}, s32[8,1]{0,1:T(1,128)}, u32[]{:S(2)}) %copy-start.2) | copy-done | bytes 56
  1.3 1.6 %shard_map.68 = bf16[512,128]{1,0:T(8,128)(2,1)S(1)} custom-call(s32[8]{0:T(128)S(1)} %bitcast.7, s32[1]{0:T(128)} %bitcast.here, bf16[96,512,128]{2,1,0:T(8,128)(2,1)} %bitcast.11), custom_call_target="tpu_custom_call" | custom-call | bytes 1024 | tf_op jit(solution)/shard_map/pallas_call | solution.py:225
  2.9 4.1 %collective-permute-start.1 = (bf16[512,128]{1,0:T(8,128)(2,1)S(1)}, bf16[512,128]{1,0:T(8,128)(2,1)S(1)}, u32[]{:S(2)}, u32[]{:S(2)}) collective-permute-start(bf16[512,128]{1,0:T(8,128)(2,1)S(1)} %shard_map.68), channel_id=1, source_target_pairs={{0,8},{2,10},{4,12},{6,14},{8,0},{10,2},{12,4},{14,6},{1,9},{3,11}... | collective-permute-start | bytes 393224 | tf_op jit(solution)/shard_map/ppermute | solution.py:201
  7.0 1.8 %shard_map.69 = (bf16[512,128]{1,0:T(8,128)(2,1)S(1)}, bf16[512,128]{1,0:T(8,128)(2,1)S(1)}, bf16[512,128]{1,0:T(8,128)(2,1)S(1)}, bf16[512,128]{1,0:T(8,128)(2,...) custom-call(s32[8]{0:T(128)S(1)} %bitcast.8, s32[1]{0:T(128)} %bitcast.here, ...), custom_call_target="tpu_custom_call" | custom-call | bytes 1024 | tf_op jit(solution)/shard_map/pallas_call | solution.py:225
  8.8 1.6 %collective-permute-start = (bf16[512,128]{1,0:T(8,128)(2,1)S(1)}, bf16[512,128]{1,0:T(8,128)(2,1)S(1)}, u32[]{:S(2)}, u32[]{:S(2)}) collective-permute-start(bf16[512,128]{1,0:T(8,128)(2,1)S(1)} %get-tuple-element.27), channel_id=1, source_target_pairs={{0,2},{2,0},{4,6},{6,4},{8,10},{10,8},{12,14},{14,12},{1,3},{3,1},... | collective-permute-start | bytes 393224 | tf_op jit(solution)/shard_map/ppermute | solution.py:201
  10.3 1.6 %collective-permute-start.2 = (bf16[512,128]{1,0:T(8,128)(2,1)S(1)}, bf16[512,128]{1,0:T(8,128)(2,1)S(1)}, u32[]{:S(2)}, u32[]{:S(2)}) collective-permute-start(bf16[512,128]{1,0:T(8,128)(2,1)S(1)} %get-tuple-element.31), channel_id=1, source_target_pairs={{0,4},{2,6},{4,0},{6,2},{8,12},{10,14},{12,8},{14,10},{1,5},{3,7},... | collective-permute-start | bytes 393224 | tf_op jit(solution)/shard_map/ppermute | solution.py:201
  11.9 0.3 collective-permute-start.3
  12.2 2.5 %collective-permute-start.4 = (bf16[512,128]{1,0:T(8,128)(2,1)S(1)}, bf16[512,128]{1,0:T(8,128)(2,1)S(1)}, u32[]{:S(2)}, u32[]{:S(2)}) collective-permute-start(bf16[512,128]{1,0:T(8,128)(2,1)S(1)} %get-tuple-element.33), channel_id=1, source_target_pairs={{0,12},{2,14},{4,8},{6,10},{8,4},{10,6},{12,0},{14,2},{1,13},{3,15... | collective-permute-start | bytes 393224 | tf_op jit(solution)/shard_map/ppermute | solution.py:201
  14.7 0.0 collective-permute-done.1.refs_0_
  14.7 1.6 %collective-permute-start.5 = (bf16[512,128]{1,0:T(8,128)(2,1)S(1)}, bf16[512,128]{1,0:T(8,128)(2,1)S(1)}, u32[]{:S(2)}, u32[]{:S(2)}) collective-permute-start(bf16[512,128]{1,0:T(8,128)(2,1)S(1)} %get-tuple-element.35), channel_id=1, source_target_pairs={{0,6},{2,4},{4,2},{6,0},{8,14},{10,12},{12,10},{14,8},{1,7},{3,5},... | collective-permute-start | bytes 393224 | tf_op jit(solution)/shard_map/ppermute | solution.py:201
  16.3 0.0 collective-permute-done.after.refs_1_
  16.3 2.8 %collective-permute-start.6 = (bf16[512,128]{1,0:T(8,128)(2,1)S(1)}, bf16[512,128]{1,0:T(8,128)(2,1)S(1)}, u32[]{:S(2)}, u32[]{:S(2)}) collective-permute-start(bf16[512,128]{1,0:T(8,128)(2,1)S(1)} %get-tuple-element.36), channel_id=1, source_target_pairs={{0,14},{2,12},{4,10},{6,8},{8,6},{10,4},{12,2},{14,0},{1,15},{3,13... | collective-permute-start | bytes 393224 | tf_op jit(solution)/shard_map/ppermute | solution.py:201
  19.1 5.9 %shard_map.70 = (bf16[8,512,256]{2,1,0:T(8,128)(2,1)S(1)}, bf16[512,128]{1,0:T(8,128)(2,1)S(1)}, f32[128,128]{1,0:T(8,128)S(1)}, f32[8,128]{1,0:T(8,128)S(1)}, s...) custom-call(s32[8]{0:T(128)S(1)} %bitcast.9, s32[1]{0:T(128)} %bitcast.here, s32[8]{0:T(128)S(1)} %bitcast.10, ...), custom_call_target="tpu_custom_call" | custom-call | bytes 16777216 | tf_op jit(solution)/shard_map/pallas_call | solution.py:241
  25.1 1.6 %collective-permute-done.3.refs_3_ = bf16[512,128]{1,0:T(8,128)(2,1)S(1)} collective-permute-done((bf16[512,128]{1,0:T(8,128)(2,1)S(1)}, bf16[512,128]{1,0:T(8,128)(2,1)S(1)}, u32[]{:S(2)}, u32[]{:S(2)}) %collective-permute-start.3) | collective-permute-done | bytes 131104 | tf_op jit(solution)/shard_map/ppermute | solution.py:201
  26.7 0.6 shard_map.71.so_far
  27.3 0.6 collective-permute-done.5.refs_0_.refs_5_
  27.8 0.3 shard_map.72.mine
  28.1 0.1 collective-permute-start.7
  28.2 1.2 %collective-permute-done.7.other = f32[128,128]{1,0:T(8,128)S(1)} collective-permute-done((f32[128,128]{1,0:T(8,128)S(1)}, f32[128,128]{1,0:T(8,128)S(1)}, u32[]{:S(2)}, u32[]{:S(2)}) %collective-permute-start.7) | collective-permute-done | bytes 65568 | tf_op jit(solution)/shard_map/ppermute | solution.py:207
  29.5 0.3 shard_map.73
  29.8 2.7 %collective-permute-start.8 = (bf16[512,128]{1,0:T(8,128)(2,1)S(1)}, bf16[512,128]{1,0:T(8,128)(2,1)S(1)}, u32[]{:S(2)}, u32[]{:S(2)}) collective-permute-start(bf16[512,128]{1,0:T(8,128)(2,1)S(1)} %shard_map.73), channel_id=1, source_target_pairs={{0,12},{2,14},{4,8},{6,10},{8,4},{10,6},{12,0},{14,2},{1,13},{3,15... | collective-permute-start | bytes 393224 | tf_op jit(solution)/shard_map/ppermute | solution.py:201
  32.5 0.7 %shard_map.74 = (bf16[512,128]{1,0:T(8,128)(2,1)S(1)}, bf16[512,128]{1,0:T(8,128)(2,1)S(1)}, bf16[512,128]{1,0:T(8,128)(2,1)S(1)}, bf16[512,128]{1,0:T(8,128)(2,...) custom-call(s32[1]{0:T(128)} %bitcast.here, ...), custom_call_target="tpu_custom_call" | custom-call | bytes 1024 | tf_op jit(solution)/shard_map/pallas_call | solution.py:276
  33.2 1.3 %collective-permute-start.9 = (bf16[512,128]{1,0:T(8,128)(2,1)S(1)}, bf16[512,128]{1,0:T(8,128)(2,1)S(1)}, u32[]{:S(2)}, u32[]{:S(2)}) collective-permute-start(bf16[512,128]{1,0:T(8,128)(2,1)S(1)} %get-tuple-element.37), channel_id=1, source_target_pairs={{0,2},{2,0},{4,6},{6,4},{8,10},{10,8},{12,14},{14,12},{1,3},{3,1},... | collective-permute-start | bytes 393224 | tf_op jit(solution)/shard_map/ppermute | solution.py:201
  34.5 3.1 %collective-permute-start.10 = (bf16[512,128]{1,0:T(8,128)(2,1)S(1)}, bf16[512,128]{1,0:T(8,128)(2,1)S(1)}, u32[]{:S(2)}, u32[]{:S(2)}) collective-permute-start(bf16[512,128]{1,0:T(8,128)(2,1)S(1)} %get-tuple-element.38), channel_id=1, source_target_pairs={{0,4},{2,6},{4,0},{6,2},{8,12},{10,14},{12,8},{14,10},{1,5},{3,7},... | collective-permute-start | bytes 393224 | tf_op jit(solution)/shard_map/ppermute | solution.py:201
  37.6 3.8 %collective-permute-start.12 = (bf16[512,128]{1,0:T(8,128)(2,1)S(1)}, bf16[512,128]{1,0:T(8,128)(2,1)S(1)}, u32[]{:S(2)}, u32[]{:S(2)}) collective-permute-start(bf16[512,128]{1,0:T(8,128)(2,1)S(1)} %get-tuple-element.40), channel_id=1, source_target_pairs={{0,10},{2,8},{4,14},{6,12},{8,2},{10,0},{12,6},{14,4},{1,11},{3,9}... | collective-permute-start | bytes 393224 | tf_op jit(solution)/shard_map/ppermute | solution.py:201
  41.4 1.3 %collective-permute-start.14 = (bf16[512,128]{1,0:T(8,128)(2,1)S(1)}, bf16[512,128]{1,0:T(8,128)(2,1)S(1)}, u32[]{:S(2)}, u32[]{:S(2)}) collective-permute-start(bf16[512,128]{1,0:T(8,128)(2,1)S(1)} %get-tuple-element.42), channel_id=1, source_target_pairs={{0,14},{2,12},{4,10},{6,8},{8,6},{10,4},{12,2},{14,0},{1,15},{3,13... | collective-permute-start | bytes 393224 | tf_op jit(solution)/shard_map/ppermute | solution.py:201
  42.7 0.8 %collective-permute-start.13 = (bf16[512,128]{1,0:T(8,128)(2,1)S(1)}, bf16[512,128]{1,0:T(8,128)(2,1)S(1)}, u32[]{:S(2)}, u32[]{:S(2)}) collective-permute-start(bf16[512,128]{1,0:T(8,128)(2,1)S(1)} %get-tuple-element.48), channel_id=1, source_target_pairs={{0,6},{2,4},{4,2},{6,0},{8,14},{10,12},{12,10},{14,8},{1,7},{3,5},... | collective-permute-start | bytes 393224 | tf_op jit(solution)/shard_map/ppermute | solution.py:201
  43.5 1.4 %shard_map.75 = bf16[128,4096]{1,0:T(8,128)(2,1)} custom-call(s32[1]{0:T(128)} %bitcast.here, f32[128,128]{1,0:T(8,128)S(1)} %get-tuple-element.28.live, f32[128,128]{1,0:T(8,128)S(1)} %shard_map.72.mine, f32[128,128]{1,0:T(8,128)S(1)} %collective-permute-done.7.other, bf16[512,128]{1,0:T(8,128)(2,1)S(1)} %collective-permute-done.1.refs_0_, ...), custom_call_target="tpu_custom_call" | custom-call | flops 134217728 | bytes 2097152 | tf_op jit(solution)/shard_map/pallas_call | solution.py:286
  45.0 7.7 %collective-permute-done.11.refs_3_ = bf16[512,128]{1,0:T(8,128)(2,1)S(1)} collective-permute-done((bf16[512,128]{1,0:T(8,128)(2,1)S(1)}, bf16[512,128]{1,0:T(8,128)(2,1)S(1)}, u32[]{:S(2)}, u32[]{:S(2)}) %collective-permute-start.11) | collective-permute-done | bytes 131104 | tf_op jit(solution)/shard_map/ppermute | solution.py:201
  52.6 1.7 %shard_map.76.refs_8_ = bf16[96,512,128]{2,1,0:T(8,128)(2,1)} custom-call(s32[8]{0:T(128)S(1)} %get-tuple-element.45.blocks, s32[1]{0:T(128)} %bitcast.here, f32[8,128]{1,0:T(8,128)S(1)} %get-tuple-element.46.parts, s32[8,128]{1,0:T(8,128)S(1)} %get-tuple-element.47.words, ...), custom_call_target="tpu_custom_call", output_to_operand_aliasing={{}: (9, {})} | custom-call | bytes 2097152 | tf_op jit(solution)/shard_map/pallas_call | solution.py:297
  54.4 1.9 %collective-permute-done.12.refs_4_ = bf16[512,128]{1,0:T(8,128)(2,1)S(1)} collective-permute-done((bf16[512,128]{1,0:T(8,128)(2,1)S(1)}, bf16[512,128]{1,0:T(8,128)(2,1)S(1)}, u32[]{:S(2)}, u32[]{:S(2)}) %collective-permute-start.12) | collective-permute-done | bytes 131104 | tf_op jit(solution)/shard_map/ppermute | solution.py:201
  56.3 1.3 %shard_map.77 = bf16[96,512,128]{2,1,0:T(8,128)(2,1)} custom-call(s32[8]{0:T(128)S(1)} %get-tuple-element.45.blocks, s32[1]{0:T(128)} %bitcast.here, f32[8,128]{1,0:T(8,128)S(1)} %get-tuple-element.46.parts, s32[8,128]{1,0:T(8,128)S(1)} %get-tuple-element.47.words, ...), custom_call_target="tpu_custom_call", output_to_operand_aliasing={{}: (12, {})} | custom-call | bytes 2097152 | tf_op jit(solution)/shard_map/pallas_call | solution.py:297
  (17 shorter events, 0.0 us)
Async XLA Ops:
  0.6 0.7 %copy-start.2 = (s32[8,1]{0,1:T(1,128)S(1)}, s32[8,1]{0,1:T(1,128)}, u32[]{:S(2)}) copy-start(s32[8,1]{0,1:T(1,128)} %param.8) | copy-start | bytes 100
  1.3 17.8 %copy-start = (bf16[128,4096]{1,0:T(8,128)(2,1)S(1)}, bf16[128,4096]{1,0:T(8,128)(2,1)}, u32[]{:S(2)}) copy-start(bf16[128,4096]{1,0:T(8,128)(2,1)} %x.3) | copy-start | bytes 3145732
  1.3 17.8 %copy-start.1 = (bf16[128,4096]{1,0:T(8,128)(2,1)S(1)}, bf16[128,4096]{1,0:T(8,128)(2,1)}, u32[]{:S(2)}) copy-start(bf16[128,4096]{1,0:T(8,128)(2,1)} %y.5) | copy-start | bytes 3145732
  1.3 17.8 %copy-start.3 = (s32[8,1]{0,1:T(1,128)S(1)}, s32[8,1]{0,1:T(1,128)}, u32[]{:S(2)}) copy-start(s32[8,1]{0,1:T(1,128)} %param.9) | copy-start | bytes 100
  2.9 11.8 %collective-permute-start.1 = (bf16[512,128]{1,0:T(8,128)(2,1)S(1)}, bf16[512,128]{1,0:T(8,128)(2,1)S(1)}, u32[]{:S(2)}, u32[]{:S(2)}) collective-permute-start(bf16[512,128]{1,0:T(8,128)(2,1)S(1)} %shard_map.68), channel_id=1, source_target_pairs={{0,8},{2,10},{4,12},{6,14},{8,0},{10,2},{12,4},{14,6},{1,9},{3,11}... | collective-permute-start | bytes 393224 | tf_op jit(solution)/shard_map/ppermute | solution.py:201
  8.8 7.5 %collective-permute-start = (bf16[512,128]{1,0:T(8,128)(2,1)S(1)}, bf16[512,128]{1,0:T(8,128)(2,1)S(1)}, u32[]{:S(2)}, u32[]{:S(2)}) collective-permute-start(bf16[512,128]{1,0:T(8,128)(2,1)S(1)} %get-tuple-element.27), channel_id=1, source_target_pairs={{0,2},{2,0},{4,6},{6,4},{8,10},{10,8},{12,14},{14,12},{1,3},{3,1},... | collective-permute-start | bytes 393224 | tf_op jit(solution)/shard_map/ppermute | solution.py:201
  10.3 14.8 %collective-permute-start.2 = (bf16[512,128]{1,0:T(8,128)(2,1)S(1)}, bf16[512,128]{1,0:T(8,128)(2,1)S(1)}, u32[]{:S(2)}, u32[]{:S(2)}) collective-permute-start(bf16[512,128]{1,0:T(8,128)(2,1)S(1)} %get-tuple-element.31), channel_id=1, source_target_pairs={{0,4},{2,6},{4,0},{6,2},{8,12},{10,14},{12,8},{14,10},{1,5},{3,7},... | collective-permute-start | bytes 393224 | tf_op jit(solution)/shard_map/ppermute | solution.py:201
  11.9 14.8 %collective-permute-start.3 = (bf16[512,128]{1,0:T(8,128)(2,1)S(1)}, bf16[512,128]{1,0:T(8,128)(2,1)S(1)}, u32[]{:S(2)}, u32[]{:S(2)}) collective-permute-start(bf16[512,128]{1,0:T(8,128)(2,1)S(1)} %get-tuple-element.32), channel_id=1, source_target_pairs={{0,10},{2,8},{4,14},{6,12},{8,2},{10,0},{12,6},{14,4},{1,11},{3,9}... | collective-permute-start | bytes 393224 | tf_op jit(solution)/shard_map/ppermute | solution.py:201
  12.2 14.5 %collective-permute-start.4 = (bf16[512,128]{1,0:T(8,128)(2,1)S(1)}, bf16[512,128]{1,0:T(8,128)(2,1)S(1)}, u32[]{:S(2)}, u32[]{:S(2)}) collective-permute-start(bf16[512,128]{1,0:T(8,128)(2,1)S(1)} %get-tuple-element.33), channel_id=1, source_target_pairs={{0,12},{2,14},{4,8},{6,10},{8,4},{10,6},{12,0},{14,2},{1,13},{3,15... | collective-permute-start | bytes 393224 | tf_op jit(solution)/shard_map/ppermute | solution.py:201
  14.7 13.1 %collective-permute-start.5 = (bf16[512,128]{1,0:T(8,128)(2,1)S(1)}, bf16[512,128]{1,0:T(8,128)(2,1)S(1)}, u32[]{:S(2)}, u32[]{:S(2)}) collective-permute-start(bf16[512,128]{1,0:T(8,128)(2,1)S(1)} %get-tuple-element.35), channel_id=1, source_target_pairs={{0,6},{2,4},{4,2},{6,0},{8,14},{10,12},{12,10},{14,8},{1,7},{3,5},... | collective-permute-start | bytes 393224 | tf_op jit(solution)/shard_map/ppermute | solution.py:201
  16.3 11.5 %collective-permute-start.6 = (bf16[512,128]{1,0:T(8,128)(2,1)S(1)}, bf16[512,128]{1,0:T(8,128)(2,1)S(1)}, u32[]{:S(2)}, u32[]{:S(2)}) collective-permute-start(bf16[512,128]{1,0:T(8,128)(2,1)S(1)} %get-tuple-element.36), channel_id=1, source_target_pairs={{0,14},{2,12},{4,10},{6,8},{8,6},{10,4},{12,2},{14,0},{1,15},{3,13... | collective-permute-start | bytes 393224 | tf_op jit(solution)/shard_map/ppermute | solution.py:201
  28.1 1.3 %collective-permute-start.7 = (f32[128,128]{1,0:T(8,128)S(1)}, f32[128,128]{1,0:T(8,128)S(1)}, u32[]{:S(2)}, u32[]{:S(2)}) collective-permute-start(f32[128,128]{1,0:T(8,128)S(1)} %shard_map.72.mine), channel_id=1, source_target_pairs={{0,1},{1,0},{2,3},{3,2},{4,5},{5,4},{6,7},{7,6},{8,9},{9,8},{10,11... | collective-permute-start | bytes 196616 | tf_op jit(solution)/shard_map/ppermute | solution.py:207
  29.8 11.7 %collective-permute-start.8 = (bf16[512,128]{1,0:T(8,128)(2,1)S(1)}, bf16[512,128]{1,0:T(8,128)(2,1)S(1)}, u32[]{:S(2)}, u32[]{:S(2)}) collective-permute-start(bf16[512,128]{1,0:T(8,128)(2,1)S(1)} %shard_map.73), channel_id=1, source_target_pairs={{0,12},{2,14},{4,8},{6,10},{8,4},{10,6},{12,0},{14,2},{1,13},{3,15... | collective-permute-start | bytes 393224 | tf_op jit(solution)/shard_map/ppermute | solution.py:201
  33.2 9.5 %collective-permute-start.9 = (bf16[512,128]{1,0:T(8,128)(2,1)S(1)}, bf16[512,128]{1,0:T(8,128)(2,1)S(1)}, u32[]{:S(2)}, u32[]{:S(2)}) collective-permute-start(bf16[512,128]{1,0:T(8,128)(2,1)S(1)} %get-tuple-element.37), channel_id=1, source_target_pairs={{0,2},{2,0},{4,6},{6,4},{8,10},{10,8},{12,14},{14,12},{1,3},{3,1},... | collective-permute-start | bytes 393224 | tf_op jit(solution)/shard_map/ppermute | solution.py:201
  34.5 10.5 %collective-permute-start.10 = (bf16[512,128]{1,0:T(8,128)(2,1)S(1)}, bf16[512,128]{1,0:T(8,128)(2,1)S(1)}, u32[]{:S(2)}, u32[]{:S(2)}) collective-permute-start(bf16[512,128]{1,0:T(8,128)(2,1)S(1)} %get-tuple-element.38), channel_id=1, source_target_pairs={{0,4},{2,6},{4,0},{6,2},{8,12},{10,14},{12,8},{14,10},{1,5},{3,7},... | collective-permute-start | bytes 393224 | tf_op jit(solution)/shard_map/ppermute | solution.py:201
  37.6 15.0 %collective-permute-start.11 = (bf16[512,128]{1,0:T(8,128)(2,1)S(1)}, bf16[512,128]{1,0:T(8,128)(2,1)S(1)}, u32[]{:S(2)}, u32[]{:S(2)}) collective-permute-start(bf16[512,128]{1,0:T(8,128)(2,1)S(1)} %get-tuple-element.39), channel_id=1, source_target_pairs={{0,8},{2,10},{4,12},{6,14},{8,0},{10,2},{12,4},{14,6},{1,9},{3,11}... | collective-permute-start | bytes 393224 | tf_op jit(solution)/shard_map/ppermute | solution.py:201
  37.6 18.7 %collective-permute-start.12 = (bf16[512,128]{1,0:T(8,128)(2,1)S(1)}, bf16[512,128]{1,0:T(8,128)(2,1)S(1)}, u32[]{:S(2)}, u32[]{:S(2)}) collective-permute-start(bf16[512,128]{1,0:T(8,128)(2,1)S(1)} %get-tuple-element.40), channel_id=1, source_target_pairs={{0,10},{2,8},{4,14},{6,12},{8,2},{10,0},{12,6},{14,4},{1,11},{3,9}... | collective-permute-start | bytes 393224 | tf_op jit(solution)/shard_map/ppermute | solution.py:201
  41.4 14.9 %collective-permute-start.14 = (bf16[512,128]{1,0:T(8,128)(2,1)S(1)}, bf16[512,128]{1,0:T(8,128)(2,1)S(1)}, u32[]{:S(2)}, u32[]{:S(2)}) collective-permute-start(bf16[512,128]{1,0:T(8,128)(2,1)S(1)} %get-tuple-element.42), channel_id=1, source_target_pairs={{0,14},{2,12},{4,10},{6,8},{8,6},{10,4},{12,2},{14,0},{1,15},{3,13... | collective-permute-start | bytes 393224 | tf_op jit(solution)/shard_map/ppermute | solution.py:201
  42.7 13.6 %collective-permute-start.13 = (bf16[512,128]{1,0:T(8,128)(2,1)S(1)}, bf16[512,128]{1,0:T(8,128)(2,1)S(1)}, u32[]{:S(2)}, u32[]{:S(2)}) collective-permute-start(bf16[512,128]{1,0:T(8,128)(2,1)S(1)} %get-tuple-element.48), channel_id=1, source_target_pairs={{0,6},{2,4},{4,2},{6,0},{8,14},{10,12},{12,10},{14,8},{1,7},{3,5},... | collective-permute-start | bytes 393224 | tf_op jit(solution)/shard_map/ppermute | solution.py:201

commit v26 on v22

--- a/solution.py
+++ b/solution.py
@@ -9,7 +9,7 @@
 
 adapter_alpha = 128.0
 FETCH = (4, 1, 2, 5, 6, 3, 7)
-FETCH_TIES = {}
+FETCH_TIES = {3: 4}
 SEND = (6, 1, 2, 4, 5, 3, 7)
 SEND_TIES = {3: 6}
 PREP_AFTER = 1

time: 57.9 us -> 57.8 us (level)
  starting transfers between devices: 27.6 us -> 26.4 us
  waiting for transfers between devices: 13.3 us -> 14.5 us
    ppermute x14, starting transfers between devices: 27.5 us -> 26.3 us  [exchange(): out[k] = lax.ppermute(piece, 'dp', [(i, i ^ k) for i in range(owners)])]
    ppermute x14, waiting for transfers between devices: 12.1 us -> 13.2 us  [exchange(): out[k] = lax.ppermute(piece, 'dp', [(i, i ^ k) for i in range(owners)])]
where the time goes in v26:
time: 57.8 us; the launch traced here: 57.6 us
  starting transfers between devices  26.4 us (46%)
  Pallas kernels  15.4 us (27%)
  waiting for transfers between devices  14.5 us (25%)
  between operations  0.76 us (1%)
  local copies, waits for them, and re-layouts  0.66 us (1%)
    ppermute x14, starting transfers between devices, exchange(): out[k] = lax.ppermute(piece, 'dp', [(i, i ^ k) for i in range(owners)])  26.3 us
    ppermute x14, waiting for transfers between devices, exchange(): out[k] = lax.ppermute(piece, 'dp', [(i, i ^ k) for i in range(owners)])  13.2 us
    pallas_call x1, Pallas kernels, with_kernels(): call(prep_kernel, [jax.ShapeDtypeStruct((owners, rows, 2 * tokens), bf16)...  5.95 us
    pallas_call x2, Pallas kernels, with_kernels(): call(functools.partial(gather_kernel, part), [straight] * len(part), [in_...  3.35 us
    pallas_call x2, Pallas kernels, merge(): call(functools.partial(merge_kernel, tuple(merged), handled, others), jax...  2.77 us
    pallas_call x1, Pallas kernels, with_kernels(): call(functools.partial(input_kernel, tuple(pairs), scale), jax.ShapeDtype...  1.45 us
    ppermute x1, waiting for transfers between devices, across_cores(): return lax.ppermute(value, 'tensor', [(i, i ^ 1) for i in range(cores)])  1.24 us
  transfers between devices with their start and end apart: 15, of which 5 were waited for; matrix products, arithmetic and copies ran while one was open for 0% of the time, Pallas kernels for 21%

profile of v26, /device:TPU:0, one launch (start us, length us, event | category | flops | bytes accessed | tf_op | source)
XLA Modules:
  0.0 57.6 jit_solution(12062378846138962362)
XLA Ops:
  0.6 0.6 %copy-done.2 = s32[8,1]{0,1:T(1,128)S(1)} copy-done((s32[8,1]{0,1:T(1,128)S(1)}, s32[8,1]{0,1:T(1,128)}, u32[]{:S(2)}) %copy-start.2) | copy-done | bytes 56
  1.3 1.6 %shard_map.68 = bf16[512,128]{1,0:T(8,128)(2,1)S(1)} custom-call(s32[8]{0:T(128)S(1)} %bitcast.7, s32[1]{0:T(128)} %bitcast.here, bf16[96,512,128]{2,1,0:T(8,128)(2,1)} %bitcast.11), custom_call_target="tpu_custom_call" | custom-call | bytes 1024 | tf_op jit(solution)/shard_map/pallas_call | solution.py:216
  2.9 4.1 %collective-permute-start.1 = (bf16[512,128]{1,0:T(8,128)(2,1)S(1)}, bf16[512,128]{1,0:T(8,128)(2,1)S(1)}, u32[]{:S(2)}, u32[]{:S(2)}) collective-permute-start(bf16[512,128]{1,0:T(8,128)(2,1)S(1)} %shard_map.68), channel_id=1, source_target_pairs={{0,8},{2,10},{4,12},{6,14},{8,0},{10,2},{12,4},{14,6},{1,9},{3,11}... | collective-permute-start | bytes 393224 | tf_op jit(solution)/shard_map/ppermute | solution.py:192
  7.0 1.8 %shard_map.69 = (bf16[512,128]{1,0:T(8,128)(2,1)S(1)}, bf16[512,128]{1,0:T(8,128)(2,1)S(1)}, bf16[512,128]{1,0:T(8,128)(2,1)S(1)}, bf16[512,128]{1,0:T(8,128)(2,...) custom-call(s32[8]{0:T(128)S(1)} %bitcast.8, s32[1]{0:T(128)} %bitcast.here, ...), custom_call_target="tpu_custom_call" | custom-call | bytes 1024 | tf_op jit(solution)/shard_map/pallas_call | solution.py:216
  8.8 1.6 %collective-permute-start = (bf16[512,128]{1,0:T(8,128)(2,1)S(1)}, bf16[512,128]{1,0:T(8,128)(2,1)S(1)}, u32[]{:S(2)}, u32[]{:S(2)}) collective-permute-start(bf16[512,128]{1,0:T(8,128)(2,1)S(1)} %get-tuple-element.27), channel_id=1, source_target_pairs={{0,2},{2,0},{4,6},{6,4},{8,10},{10,8},{12,14},{14,12},{1,3},{3,1},... | collective-permute-start | bytes 393224 | tf_op jit(solution)/shard_map/ppermute | solution.py:192
  10.3 1.6 %collective-permute-start.2 = (bf16[512,128]{1,0:T(8,128)(2,1)S(1)}, bf16[512,128]{1,0:T(8,128)(2,1)S(1)}, u32[]{:S(2)}, u32[]{:S(2)}) collective-permute-start(bf16[512,128]{1,0:T(8,128)(2,1)S(1)} %get-tuple-element.31), channel_id=1, source_target_pairs={{0,4},{2,6},{4,0},{6,2},{8,12},{10,14},{12,8},{14,10},{1,5},{3,7},... | collective-permute-start | bytes 393224 | tf_op jit(solution)/shard_map/ppermute | solution.py:192
  11.9 0.3 collective-permute-start.3
  12.2 2.5 %collective-permute-start.4 = (bf16[512,128]{1,0:T(8,128)(2,1)S(1)}, bf16[512,128]{1,0:T(8,128)(2,1)S(1)}, u32[]{:S(2)}, u32[]{:S(2)}) collective-permute-start(bf16[512,128]{1,0:T(8,128)(2,1)S(1)} %get-tuple-element.33), channel_id=1, source_target_pairs={{0,12},{2,14},{4,8},{6,10},{8,4},{10,6},{12,0},{14,2},{1,13},{3,15... | collective-permute-start | bytes 393224 | tf_op jit(solution)/shard_map/ppermute | solution.py:192
  14.7 4.4 %collective-permute-start.6 = (bf16[512,128]{1,0:T(8,128)(2,1)S(1)}, bf16[512,128]{1,0:T(8,128)(2,1)S(1)}, u32[]{:S(2)}, u32[]{:S(2)}) collective-permute-start(bf16[512,128]{1,0:T(8,128)(2,1)S(1)} %get-tuple-element.37), channel_id=1, source_target_pairs={{0,14},{2,12},{4,10},{6,8},{8,6},{10,4},{12,2},{14,0},{1,15},{3,13... | collective-permute-start | bytes 393224 | tf_op jit(solution)/shard_map/ppermute | solution.py:192
  19.1 0.0 collective-permute-done.after.refs_1_
  19.1 0.0 collective-permute-start.5
  19.1 5.9 %shard_map.70 = (bf16[8,512,256]{2,1,0:T(8,128)(2,1)S(1)}, bf16[512,128]{1,0:T(8,128)(2,1)S(1)}, f32[128,128]{1,0:T(8,128)S(1)}, f32[8,128]{1,0:T(8,128)S(1)}, s...) custom-call(s32[8]{0:T(128)S(1)} %bitcast.9, s32[1]{0:T(128)} %bitcast.here, s32[8]{0:T(128)S(1)} %bitcast.10, ...), custom_call_target="tpu_custom_call" | custom-call | bytes 16777216 | tf_op jit(solution)/shard_map/pallas_call | solution.py:229
  25.1 1.6 %collective-permute-done.3.refs_3_ = bf16[512,128]{1,0:T(8,128)(2,1)S(1)} collective-permute-done((bf16[512,128]{1,0:T(8,128)(2,1)S(1)}, bf16[512,128]{1,0:T(8,128)(2,1)S(1)}, u32[]{:S(2)}, u32[]{:S(2)}) %collective-permute-start.3) | collective-permute-done | bytes 131104 | tf_op jit(solution)/shard_map/ppermute | solution.py:192
  26.7 0.6 shard_map.71.so_far
  27.3 2.0 %collective-permute-done.5.refs_0_.refs_5_ = bf16[512,128]{1,0:T(8,128)(2,1)S(1)} collective-permute-done((bf16[512,128]{1,0:T(8,128)(2,1)S(1)}, bf16[512,128]{1,0:T(8,128)(2,1)S(1)}, u32[]{:S(2)}, u32[]{:S(2)}) %collective-permute-start.5) | collective-permute-done | bytes 131104 | tf_op jit(solution)/shard_map/ppermute | solution.py:192
  29.3 0.3 shard_map.72.mine
  29.6 0.1 collective-permute-start.7
  29.7 1.2 %collective-permute-done.7.other = f32[128,128]{1,0:T(8,128)S(1)} collective-permute-done((f32[128,128]{1,0:T(8,128)S(1)}, f32[128,128]{1,0:T(8,128)S(1)}, u32[]{:S(2)}, u32[]{:S(2)}) %collective-permute-start.7) | collective-permute-done | bytes 65568 | tf_op jit(solution)/shard_map/ppermute | solution.py:198
  30.9 0.3 shard_map.73
  31.2 1.7 %collective-permute-start.8 = (bf16[512,128]{1,0:T(8,128)(2,1)S(1)}, bf16[512,128]{1,0:T(8,128)(2,1)S(1)}, u32[]{:S(2)}, u32[]{:S(2)}) collective-permute-start(bf16[512,128]{1,0:T(8,128)(2,1)S(1)} %shard_map.73), channel_id=1, source_target_pairs={{0,12},{2,14},{4,8},{6,10},{8,4},{10,6},{12,0},{14,2},{1,13},{3,15... | collective-permute-start | bytes 393224 | tf_op jit(solution)/shard_map/ppermute | solution.py:192
  32.9 0.7 %shard_map.74 = (bf16[512,128]{1,0:T(8,128)(2,1)S(1)}, bf16[512,128]{1,0:T(8,128)(2,1)S(1)}, bf16[512,128]{1,0:T(8,128)(2,1)S(1)}, bf16[512,128]{1,0:T(8,128)(2,...) custom-call(s32[1]{0:T(128)} %bitcast.here, ...), custom_call_target="tpu_custom_call" | custom-call | bytes 1024 | tf_op jit(solution)/shard_map/pallas_call | solution.py:264
  33.6 0.9 %collective-permute-start.9 = (bf16[512,128]{1,0:T(8,128)(2,1)S(1)}, bf16[512,128]{1,0:T(8,128)(2,1)S(1)}, u32[]{:S(2)}, u32[]{:S(2)}) collective-permute-start(bf16[512,128]{1,0:T(8,128)(2,1)S(1)} %get-tuple-element.38), channel_id=1, source_target_pairs={{0,2},{2,0},{4,6},{6,4},{8,10},{10,8},{12,14},{14,12},{1,3},{3,1},... | collective-permute-start | bytes 393224 | tf_op jit(solution)/shard_map/ppermute | solution.py:192
  34.5 3.1 %collective-permute-start.10 = (bf16[512,128]{1,0:T(8,128)(2,1)S(1)}, bf16[512,128]{1,0:T(8,128)(2,1)S(1)}, u32[]{:S(2)}, u32[]{:S(2)}) collective-permute-start(bf16[512,128]{1,0:T(8,128)(2,1)S(1)} %get-tuple-element.39), channel_id=1, source_target_pairs={{0,4},{2,6},{4,0},{6,2},{8,12},{10,14},{12,8},{14,10},{1,5},{3,7},... | collective-permute-start | bytes 393224 | tf_op jit(solution)/shard_map/ppermute | solution.py:192
  37.6 3.8 %collective-permute-start.12 = (bf16[512,128]{1,0:T(8,128)(2,1)S(1)}, bf16[512,128]{1,0:T(8,128)(2,1)S(1)}, u32[]{:S(2)}, u32[]{:S(2)}) collective-permute-start(bf16[512,128]{1,0:T(8,128)(2,1)S(1)} %get-tuple-element.41), channel_id=1, source_target_pairs={{0,10},{2,8},{4,14},{6,12},{8,2},{10,0},{12,6},{14,4},{1,11},{3,9}... | collective-permute-start | bytes 393224 | tf_op jit(solution)/shard_map/ppermute | solution.py:192
  41.4 0.0 collective-permute-done.8.refs_0_
  41.4 1.3 %collective-permute-start.14 = (bf16[512,128]{1,0:T(8,128)(2,1)S(1)}, bf16[512,128]{1,0:T(8,128)(2,1)S(1)}, u32[]{:S(2)}, u32[]{:S(2)}) collective-permute-start(bf16[512,128]{1,0:T(8,128)(2,1)S(1)} %get-tuple-element.43), channel_id=1, source_target_pairs={{0,14},{2,12},{4,10},{6,8},{8,6},{10,4},{12,2},{14,0},{1,15},{3,13... | collective-permute-start | bytes 393224 | tf_op jit(solution)/shard_map/ppermute | solution.py:192
  42.7 1.1 %collective-permute-start.13 = (bf16[512,128]{1,0:T(8,128)(2,1)S(1)}, bf16[512,128]{1,0:T(8,128)(2,1)S(1)}, u32[]{:S(2)}, u32[]{:S(2)}) collective-permute-start(bf16[512,128]{1,0:T(8,128)(2,1)S(1)} %get-tuple-element.48), channel_id=1, source_target_pairs={{0,6},{2,4},{4,2},{6,0},{8,14},{10,12},{12,10},{14,8},{1,7},{3,5},... | collective-permute-start | bytes 393224 | tf_op jit(solution)/shard_map/ppermute | solution.py:192
  43.8 1.5 %shard_map.75 = bf16[128,4096]{1,0:T(8,128)(2,1)} custom-call(s32[1]{0:T(128)} %bitcast.here, f32[128,128]{1,0:T(8,128)S(1)} %get-tuple-element.28.live, f32[128,128]{1,0:T(8,128)S(1)} %shard_map.72.mine, f32[128,128]{1,0:T(8,128)S(1)} %collective-permute-done.7.other, bf16[512,128]{1,0:T(8,128)(2,1)S(1)} %collective-permute-done.1.refs_0_, ...), custom_call_target="tpu_custom_call" | custom-call | flops 134217728 | bytes 2097152 | tf_op jit(solution)/shard_map/pallas_call | solution.py:274
  45.3 7.6 %collective-permute-done.11.refs_3_ = bf16[512,128]{1,0:T(8,128)(2,1)S(1)} collective-permute-done((bf16[512,128]{1,0:T(8,128)(2,1)S(1)}, bf16[512,128]{1,0:T(8,128)(2,1)S(1)}, u32[]{:S(2)}, u32[]{:S(2)}) %collective-permute-start.11) | collective-permute-done | bytes 131104 | tf_op jit(solution)/shard_map/ppermute | solution.py:192
  52.9 1.4 %shard_map.76.refs_8_ = bf16[96,512,128]{2,1,0:T(8,128)(2,1)} custom-call(s32[8]{0:T(128)S(1)} %get-tuple-element.46.blocks, s32[1]{0:T(128)} %bitcast.here, f32[8,128]{1,0:T(8,128)S(1)} %get-tuple-element.47.parts, bf16[512,128]{1,0:T(8,128)(2,1)S(1)} %collective-permute-done.8.refs_0_, ...), custom_call_target="tpu_custom_call", output_to_operand_aliasing={{}: (8, {})} | custom-call | bytes 2097152 | tf_op jit(solution)/shard_map/pallas_call | solution.py:287
  54.3 2.0 %collective-permute-done.12.refs_4_ = bf16[512,128]{1,0:T(8,128)(2,1)S(1)} collective-permute-done((bf16[512,128]{1,0:T(8,128)(2,1)S(1)}, bf16[512,128]{1,0:T(8,128)(2,1)S(1)}, u32[]{:S(2)}, u32[]{:S(2)}) %collective-permute-start.12) | collective-permute-done | bytes 131104 | tf_op jit(solution)/shard_map/ppermute | solution.py:192
  56.3 1.3 %shard_map.77 = bf16[96,512,128]{2,1,0:T(8,128)(2,1)} custom-call(s32[8]{0:T(128)S(1)} %get-tuple-element.46.blocks, s32[1]{0:T(128)} %bitcast.here, f32[8,128]{1,0:T(8,128)S(1)} %get-tuple-element.47.parts, bf16[512,128]{1,0:T(8,128)(2,1)S(1)} %collective-permute-done.8.refs_0_, ...), custom_call_target="tpu_custom_call", output_to_operand_aliasing={{}: (11, {})} | custom-call | bytes 2097152 | tf_op jit(solution)/shard_map/pallas_call | solution.py:287
  (17 shorter events, 0.0 us)
Async XLA Ops:
  0.6 0.7 %copy-start.2 = (s32[8,1]{0,1:T(1,128)S(1)}, s32[8,1]{0,1:T(1,128)}, u32[]{:S(2)}) copy-start(s32[8,1]{0,1:T(1,128)} %param.8) | copy-start | bytes 100
  1.3 17.8 %copy-start = (bf16[128,4096]{1,0:T(8,128)(2,1)S(1)}, bf16[128,4096]{1,0:T(8,128)(2,1)}, u32[]{:S(2)}) copy-start(bf16[128,4096]{1,0:T(8,128)(2,1)} %x.3) | copy-start | bytes 3145732
  1.3 17.8 %copy-start.1 = (bf16[128,4096]{1,0:T(8,128)(2,1)S(1)}, bf16[128,4096]{1,0:T(8,128)(2,1)}, u32[]{:S(2)}) copy-start(bf16[128,4096]{1,0:T(8,128)(2,1)} %y.5) | copy-start | bytes 3145732
  1.3 17.8 %copy-start.3 = (s32[8,1]{0,1:T(1,128)S(1)}, s32[8,1]{0,1:T(1,128)}, u32[]{:S(2)}) copy-start(s32[8,1]{0,1:T(1,128)} %param.9) | copy-start | bytes 100
  2.9 11.8 %collective-permute-start.1 = (bf16[512,128]{1,0:T(8,128)(2,1)S(1)}, bf16[512,128]{1,0:T(8,128)(2,1)S(1)}, u32[]{:S(2)}, u32[]{:S(2)}) collective-permute-start(bf16[512,128]{1,0:T(8,128)(2,1)S(1)} %shard_map.68), channel_id=1, source_target_pairs={{0,8},{2,10},{4,12},{6,14},{8,0},{10,2},{12,4},{14,6},{1,9},{3,11}... | collective-permute-start | bytes 393224 | tf_op jit(solution)/shard_map/ppermute | solution.py:192
  8.8 10.4 %collective-permute-start = (bf16[512,128]{1,0:T(8,128)(2,1)S(1)}, bf16[512,128]{1,0:T(8,128)(2,1)S(1)}, u32[]{:S(2)}, u32[]{:S(2)}) collective-permute-start(bf16[512,128]{1,0:T(8,128)(2,1)S(1)} %get-tuple-element.27), channel_id=1, source_target_pairs={{0,2},{2,0},{4,6},{6,4},{8,10},{10,8},{12,14},{14,12},{1,3},{3,1},... | collective-permute-start | bytes 393224 | tf_op jit(solution)/shard_map/ppermute | solution.py:192
  10.3 14.8 %collective-permute-start.2 = (bf16[512,128]{1,0:T(8,128)(2,1)S(1)}, bf16[512,128]{1,0:T(8,128)(2,1)S(1)}, u32[]{:S(2)}, u32[]{:S(2)}) collective-permute-start(bf16[512,128]{1,0:T(8,128)(2,1)S(1)} %get-tuple-element.31), channel_id=1, source_target_pairs={{0,4},{2,6},{4,0},{6,2},{8,12},{10,14},{12,8},{14,10},{1,5},{3,7},... | collective-permute-start | bytes 393224 | tf_op jit(solution)/shard_map/ppermute | solution.py:192
  11.9 14.8 %collective-permute-start.3 = (bf16[512,128]{1,0:T(8,128)(2,1)S(1)}, bf16[512,128]{1,0:T(8,128)(2,1)S(1)}, u32[]{:S(2)}, u32[]{:S(2)}) collective-permute-start(bf16[512,128]{1,0:T(8,128)(2,1)S(1)} %get-tuple-element.32), channel_id=1, source_target_pairs={{0,10},{2,8},{4,14},{6,12},{8,2},{10,0},{12,6},{14,4},{1,11},{3,9}... | collective-permute-start | bytes 393224 | tf_op jit(solution)/shard_map/ppermute | solution.py:192
  12.2 14.5 %collective-permute-start.4 = (bf16[512,128]{1,0:T(8,128)(2,1)S(1)}, bf16[512,128]{1,0:T(8,128)(2,1)S(1)}, u32[]{:S(2)}, u32[]{:S(2)}) collective-permute-start(bf16[512,128]{1,0:T(8,128)(2,1)S(1)} %get-tuple-element.33), channel_id=1, source_target_pairs={{0,12},{2,14},{4,8},{6,10},{8,4},{10,6},{12,0},{14,2},{1,13},{3,15... | collective-permute-start | bytes 393224 | tf_op jit(solution)/shard_map/ppermute | solution.py:192
  14.7 12.6 %collective-permute-start.6 = (bf16[512,128]{1,0:T(8,128)(2,1)S(1)}, bf16[512,128]{1,0:T(8,128)(2,1)S(1)}, u32[]{:S(2)}, u32[]{:S(2)}) collective-permute-start(bf16[512,128]{1,0:T(8,128)(2,1)S(1)} %get-tuple-element.37), channel_id=1, source_target_pairs={{0,14},{2,12},{4,10},{6,8},{8,6},{10,4},{12,2},{14,0},{1,15},{3,13... | collective-permute-start | bytes 393224 | tf_op jit(solution)/shard_map/ppermute | solution.py:192
  19.1 10.2 %collective-permute-start.5 = (bf16[512,128]{1,0:T(8,128)(2,1)S(1)}, bf16[512,128]{1,0:T(8,128)(2,1)S(1)}, u32[]{:S(2)}, u32[]{:S(2)}) collective-permute-start(bf16[512,128]{1,0:T(8,128)(2,1)S(1)} %get-tuple-element.36), channel_id=1, source_target_pairs={{0,6},{2,4},{4,2},{6,0},{8,14},{10,12},{12,10},{14,8},{1,7},{3,5},... | collective-permute-start | bytes 393224 | tf_op jit(solution)/shard_map/ppermute | solution.py:192
  29.6 1.3 %collective-permute-start.7 = (f32[128,128]{1,0:T(8,128)S(1)}, f32[128,128]{1,0:T(8,128)S(1)}, u32[]{:S(2)}, u32[]{:S(2)}) collective-permute-start(f32[128,128]{1,0:T(8,128)S(1)} %shard_map.72.mine), channel_id=1, source_target_pairs={{0,1},{1,0},{2,3},{3,2},{4,5},{5,4},{6,7},{7,6},{8,9},{9,8},{10,11... | collective-permute-start | bytes 196616 | tf_op jit(solution)/shard_map/ppermute | solution.py:198
  31.2 10.2 %collective-permute-start.8 = (bf16[512,128]{1,0:T(8,128)(2,1)S(1)}, bf16[512,128]{1,0:T(8,128)(2,1)S(1)}, u32[]{:S(2)}, u32[]{:S(2)}) collective-permute-start(bf16[512,128]{1,0:T(8,128)(2,1)S(1)} %shard_map.73), channel_id=1, source_target_pairs={{0,12},{2,14},{4,8},{6,10},{8,4},{10,6},{12,0},{14,2},{1,13},{3,15... | collective-permute-start | bytes 393224 | tf_op jit(solution)/shard_map/ppermute | solution.py:192
  33.6 9.1 %collective-permute-start.9 = (bf16[512,128]{1,0:T(8,128)(2,1)S(1)}, bf16[512,128]{1,0:T(8,128)(2,1)S(1)}, u32[]{:S(2)}, u32[]{:S(2)}) collective-permute-start(bf16[512,128]{1,0:T(8,128)(2,1)S(1)} %get-tuple-element.38), channel_id=1, source_target_pairs={{0,2},{2,0},{4,6},{6,4},{8,10},{10,8},{12,14},{14,12},{1,3},{3,1},... | collective-permute-start | bytes 393224 | tf_op jit(solution)/shard_map/ppermute | solution.py:192
  34.5 10.7 %collective-permute-start.10 = (bf16[512,128]{1,0:T(8,128)(2,1)S(1)}, bf16[512,128]{1,0:T(8,128)(2,1)S(1)}, u32[]{:S(2)}, u32[]{:S(2)}) collective-permute-start(bf16[512,128]{1,0:T(8,128)(2,1)S(1)} %get-tuple-element.39), channel_id=1, source_target_pairs={{0,4},{2,6},{4,0},{6,2},{8,12},{10,14},{12,8},{14,10},{1,5},{3,7},... | collective-permute-start | bytes 393224 | tf_op jit(solution)/shard_map/ppermute | solution.py:192
  37.6 15.3 %collective-permute-start.11 = (bf16[512,128]{1,0:T(8,128)(2,1)S(1)}, bf16[512,128]{1,0:T(8,128)(2,1)S(1)}, u32[]{:S(2)}, u32[]{:S(2)}) collective-permute-start(bf16[512,128]{1,0:T(8,128)(2,1)S(1)} %get-tuple-element.40), channel_id=1, source_target_pairs={{0,8},{2,10},{4,12},{6,14},{8,0},{10,2},{12,4},{14,6},{1,9},{3,11}... | collective-permute-start | bytes 393224 | tf_op jit(solution)/shard_map/ppermute | solution.py:192
  37.6 18.7 %collective-permute-start.12 = (bf16[512,128]{1,0:T(8,128)(2,1)S(1)}, bf16[512,128]{1,0:T(8,128)(2,1)S(1)}, u32[]{:S(2)}, u32[]{:S(2)}) collective-permute-start(bf16[512,128]{1,0:T(8,128)(2,1)S(1)} %get-tuple-element.41), channel_id=1, source_target_pairs={{0,10},{2,8},{4,14},{6,12},{8,2},{10,0},{12,6},{14,4},{1,11},{3,9}... | collective-permute-start | bytes 393224 | tf_op jit(solution)/shard_map/ppermute | solution.py:192
  41.4 14.9 %collective-permute-start.14 = (bf16[512,128]{1,0:T(8,128)(2,1)S(1)}, bf16[512,128]{1,0:T(8,128)(2,1)S(1)}, u32[]{:S(2)}, u32[]{:S(2)}) collective-permute-start(bf16[512,128]{1,0:T(8,128)(2,1)S(1)} %get-tuple-element.43), channel_id=1, source_target_pairs={{0,14},{2,12},{4,10},{6,8},{8,6},{10,4},{12,2},{14,0},{1,15},{3,13... | collective-permute-start | bytes 393224 | tf_op jit(solution)/shard_map/ppermute | solution.py:192
  42.7 13.6 %collective-permute-start.13 = (bf16[512,128]{1,0:T(8,128)(2,1)S(1)}, bf16[512,128]{1,0:T(8,128)(2,1)S(1)}, u32[]{:S(2)}, u32[]{:S(2)}) collective-permute-start(bf16[512,128]{1,0:T(8,128)(2,1)S(1)} %get-tuple-element.48), channel_id=1, source_target_pairs={{0,6},{2,4},{4,2},{6,0},{8,14},{10,12},{12,10},{14,8},{1,7},{3,5},... | collective-permute-start | bytes 393224 | tf_op jit(solution)/shard_map/ppermute | solution.py:192

commit v27 on v22

--- a/solution.py
+++ b/solution.py
@@ -10,10 +10,10 @@
 adapter_alpha = 128.0
 FETCH = (4, 1, 2, 5, 6, 3, 7)
 FETCH_TIES = {}
-SEND = (6, 1, 2, 4, 5, 3, 7)
+SEND = (6, 1, 2, 7, 4, 3, 5)
 SEND_TIES = {3: 6}
 PREP_AFTER = 1
-LATE = (5, 3, 7)
+LATE = (4, 3, 5)
 RANK_LAST = (3, 7)
 SEND_FIRST = 1
 FETCH_FIRST = 1

time: 57.9 us -> 58.8 us (1.016)
  starting transfers between devices: 27.6 us -> 28.5 us
    ppermute x14, starting transfers between devices: 27.5 us -> 28.4 us  [exchange(): out[k] = lax.ppermute(piece, 'dp', [(i, i ^ k) for i in range(owners)])]
  transfers between devices with their start and end apart: 15 -> 15, of which waited for: 5 -> 6; matrix products, arithmetic and copies ran while one was open for 0% -> 0% of each run, Pallas kernels for 21% -> 20%
where the time goes in v27:
time: 58.8 us; the launch traced here: 58.6 us
  starting transfers between devices  28.5 us (48%)
  Pallas kernels  15.4 us (26%)
  waiting for transfers between devices  13.3 us (23%)
  between operations  0.74 us (1%)
  local copies, waits for them, and re-layouts  0.66 us (1%)
    ppermute x14, starting transfers between devices, exchange(): out[k] = lax.ppermute(piece, 'dp', [(i, i ^ k) for i in range(owners)])  28.4 us
    ppermute x14, waiting for transfers between devices, exchange(): out[k] = lax.ppermute(piece, 'dp', [(i, i ^ k) for i in range(owners)])  12.1 us
    pallas_call x1, Pallas kernels, with_kernels(): call(prep_kernel, [jax.ShapeDtypeStruct((owners, rows, 2 * tokens), bf16)...  5.94 us
    pallas_call x2, Pallas kernels, with_kernels(): call(functools.partial(gather_kernel, part), [straight] * len(part), [in_...  3.35 us
    pallas_call x2, Pallas kernels, merge(): call(functools.partial(merge_kernel, tuple(merged), handled, others), jax...  2.76 us
    pallas_call x1, Pallas kernels, with_kernels(): call(functools.partial(input_kernel, tuple(pairs), scale), jax.ShapeDtype...  1.45 us
    ppermute x1, waiting for transfers between devices, across_cores(): return lax.ppermute(value, 'tensor', [(i, i ^ 1) for i in range(cores)])  1.24 us
  transfers between devices with their start and end apart: 15, of which 6 were waited for; matrix products, arithmetic and copies ran while one was open for 0% of the time, Pallas kernels for 20%

profile of v27, /device:TPU:0, one launch (start us, length us, event | category | flops | bytes accessed | tf_op | source)
XLA Modules:
  0.0 58.6 jit_solution(12718049469457251342)
XLA Ops:
  0.6 0.6 %copy-done.2 = s32[8,1]{0,1:T(1,128)S(1)} copy-done((s32[8,1]{0,1:T(1,128)S(1)}, s32[8,1]{0,1:T(1,128)}, u32[]{:S(2)}) %copy-start.2) | copy-done | bytes 56
  1.3 1.6 %shard_map.68 = bf16[512,128]{1,0:T(8,128)(2,1)S(1)} custom-call(s32[8]{0:T(128)S(1)} %bitcast.7, s32[1]{0:T(128)} %bitcast.here, bf16[96,512,128]{2,1,0:T(8,128)(2,1)} %bitcast.11), custom_call_target="tpu_custom_call" | custom-call | bytes 1024 | tf_op jit(solution)/shard_map/pallas_call | solution.py:216
  2.9 4.1 %collective-permute-start.1 = (bf16[512,128]{1,0:T(8,128)(2,1)S(1)}, bf16[512,128]{1,0:T(8,128)(2,1)S(1)}, u32[]{:S(2)}, u32[]{:S(2)}) collective-permute-start(bf16[512,128]{1,0:T(8,128)(2,1)S(1)} %shard_map.68), channel_id=1, source_target_pairs={{0,8},{2,10},{4,12},{6,14},{8,0},{10,2},{12,4},{14,6},{1,9},{3,11}... | collective-permute-start | bytes 393224 | tf_op jit(solution)/shard_map/ppermute | solution.py:192
  7.0 1.8 %shard_map.69 = (bf16[512,128]{1,0:T(8,128)(2,1)S(1)}, bf16[512,128]{1,0:T(8,128)(2,1)S(1)}, bf16[512,128]{1,0:T(8,128)(2,1)S(1)}, bf16[512,128]{1,0:T(8,128)(2,...) custom-call(s32[8]{0:T(128)S(1)} %bitcast.8, s32[1]{0:T(128)} %bitcast.here, ...), custom_call_target="tpu_custom_call" | custom-call | bytes 1024 | tf_op jit(solution)/shard_map/pallas_call | solution.py:216
  8.8 1.6 %collective-permute-start = (bf16[512,128]{1,0:T(8,128)(2,1)S(1)}, bf16[512,128]{1,0:T(8,128)(2,1)S(1)}, u32[]{:S(2)}, u32[]{:S(2)}) collective-permute-start(bf16[512,128]{1,0:T(8,128)(2,1)S(1)} %get-tuple-element.26), channel_id=1, source_target_pairs={{0,2},{2,0},{4,6},{6,4},{8,10},{10,8},{12,14},{14,12},{1,3},{3,1},... | collective-permute-start | bytes 393224 | tf_op jit(solution)/shard_map/ppermute | solution.py:192
  10.3 1.6 %collective-permute-start.2 = (bf16[512,128]{1,0:T(8,128)(2,1)S(1)}, bf16[512,128]{1,0:T(8,128)(2,1)S(1)}, u32[]{:S(2)}, u32[]{:S(2)}) collective-permute-start(bf16[512,128]{1,0:T(8,128)(2,1)S(1)} %get-tuple-element.30), channel_id=1, source_target_pairs={{0,4},{2,6},{4,0},{6,2},{8,12},{10,14},{12,8},{14,10},{1,5},{3,7},... | collective-permute-start | bytes 393224 | tf_op jit(solution)/shard_map/ppermute | solution.py:192
  11.9 0.3 collective-permute-start.3
  12.2 2.5 %collective-permute-start.4 = (bf16[512,128]{1,0:T(8,128)(2,1)S(1)}, bf16[512,128]{1,0:T(8,128)(2,1)S(1)}, u32[]{:S(2)}, u32[]{:S(2)}) collective-permute-start(bf16[512,128]{1,0:T(8,128)(2,1)S(1)} %get-tuple-element.32), channel_id=1, source_target_pairs={{0,12},{2,14},{4,8},{6,10},{8,4},{10,6},{12,0},{14,2},{1,13},{3,15... | collective-permute-start | bytes 393224 | tf_op jit(solution)/shard_map/ppermute | solution.py:192
  14.7 1.6 %collective-permute-start.5 = (bf16[512,128]{1,0:T(8,128)(2,1)S(1)}, bf16[512,128]{1,0:T(8,128)(2,1)S(1)}, u32[]{:S(2)}, u32[]{:S(2)}) collective-permute-start(bf16[512,128]{1,0:T(8,128)(2,1)S(1)} %get-tuple-element.34), channel_id=1, source_target_pairs={{0,6},{2,4},{4,2},{6,0},{8,14},{10,12},{12,10},{14,8},{1,7},{3,5},... | collective-permute-start | bytes 393224 | tf_op jit(solution)/shard_map/ppermute | solution.py:192
  16.3 2.8 %collective-permute-start.6 = (bf16[512,128]{1,0:T(8,128)(2,1)S(1)}, bf16[512,128]{1,0:T(8,128)(2,1)S(1)}, u32[]{:S(2)}, u32[]{:S(2)}) collective-permute-start(bf16[512,128]{1,0:T(8,128)(2,1)S(1)} %get-tuple-element.35), channel_id=1, source_target_pairs={{0,14},{2,12},{4,10},{6,8},{8,6},{10,4},{12,2},{14,0},{1,15},{3,13... | collective-permute-start | bytes 393224 | tf_op jit(solution)/shard_map/ppermute | solution.py:192
  19.1 5.9 %shard_map.70 = (bf16[8,512,256]{2,1,0:T(8,128)(2,1)S(1)}, bf16[512,128]{1,0:T(8,128)(2,1)S(1)}, f32[128,128]{1,0:T(8,128)S(1)}, f32[8,128]{1,0:T(8,128)S(1)}, s...) custom-call(s32[8]{0:T(128)S(1)} %bitcast.9, s32[1]{0:T(128)} %bitcast.here, s32[8]{0:T(128)S(1)} %bitcast.10, ...), custom_call_target="tpu_custom_call" | custom-call | bytes 16777216 | tf_op jit(solution)/shard_map/pallas_call | solution.py:229
  25.1 1.6 %collective-permute-done.3.refs_3_ = bf16[512,128]{1,0:T(8,128)(2,1)S(1)} collective-permute-done((bf16[512,128]{1,0:T(8,128)(2,1)S(1)}, bf16[512,128]{1,0:T(8,128)(2,1)S(1)}, u32[]{:S(2)}, u32[]{:S(2)}) %collective-permute-start.3) | collective-permute-done | bytes 131104 | tf_op jit(solution)/shard_map/ppermute | solution.py:192
  26.7 0.6 shard_map.71.so_far
  27.3 0.6 collective-permute-done.5.refs_0_.refs_5_
  27.8 0.3 shard_map.72.mine
  28.1 0.1 collective-permute-start.7
  28.2 1.2 %collective-permute-done.7.other = f32[128,128]{1,0:T(8,128)S(1)} collective-permute-done((f32[128,128]{1,0:T(8,128)S(1)}, f32[128,128]{1,0:T(8,128)S(1)}, u32[]{:S(2)}, u32[]{:S(2)}) %collective-permute-start.7) | collective-permute-done | bytes 65568 | tf_op jit(solution)/shard_map/ppermute | solution.py:198
  29.5 0.3 shard_map.73
  29.8 2.7 %collective-permute-start.8 = (bf16[512,128]{1,0:T(8,128)(2,1)S(1)}, bf16[512,128]{1,0:T(8,128)(2,1)S(1)}, u32[]{:S(2)}, u32[]{:S(2)}) collective-permute-start(bf16[512,128]{1,0:T(8,128)(2,1)S(1)} %shard_map.73), channel_id=1, source_target_pairs={{0,12},{2,14},{4,8},{6,10},{8,4},{10,6},{12,0},{14,2},{1,13},{3,15... | collective-permute-start | bytes 393224 | tf_op jit(solution)/shard_map/ppermute | solution.py:192
  32.5 0.7 %shard_map.74 = (bf16[512,128]{1,0:T(8,128)(2,1)S(1)}, bf16[512,128]{1,0:T(8,128)(2,1)S(1)}, bf16[512,128]{1,0:T(8,128)(2,1)S(1)}, bf16[512,128]{1,0:T(8,128)(2,...) custom-call(s32[1]{0:T(128)} %bitcast.here, ...), custom_call_target="tpu_custom_call" | custom-call | bytes 1024 | tf_op jit(solution)/shard_map/pallas_call | solution.py:264
  33.2 1.3 %collective-permute-start.9 = (bf16[512,128]{1,0:T(8,128)(2,1)S(1)}, bf16[512,128]{1,0:T(8,128)(2,1)S(1)}, u32[]{:S(2)}, u32[]{:S(2)}) collective-permute-start(bf16[512,128]{1,0:T(8,128)(2,1)S(1)} %get-tuple-element.36), channel_id=1, source_target_pairs={{0,2},{2,0},{4,6},{6,4},{8,10},{10,8},{12,14},{14,12},{1,3},{3,1},... | collective-permute-start | bytes 393224 | tf_op jit(solution)/shard_map/ppermute | solution.py:192
  34.5 3.1 %collective-permute-start.10 = (bf16[512,128]{1,0:T(8,128)(2,1)S(1)}, bf16[512,128]{1,0:T(8,128)(2,1)S(1)}, u32[]{:S(2)}, u32[]{:S(2)}) collective-permute-start(bf16[512,128]{1,0:T(8,128)(2,1)S(1)} %get-tuple-element.37), channel_id=1, source_target_pairs={{0,4},{2,6},{4,0},{6,2},{8,12},{10,14},{12,8},{14,10},{1,5},{3,7},... | collective-permute-start | bytes 393224 | tf_op jit(solution)/shard_map/ppermute | solution.py:192
  37.6 2.3 %collective-permute-start.11 = (bf16[512,128]{1,0:T(8,128)(2,1)S(1)}, bf16[512,128]{1,0:T(8,128)(2,1)S(1)}, u32[]{:S(2)}, u32[]{:S(2)}) collective-permute-start(bf16[512,128]{1,0:T(8,128)(2,1)S(1)} %get-tuple-element.38), channel_id=1, source_target_pairs={{0,14},{2,12},{4,10},{6,8},{8,6},{10,4},{12,2},{14,0},{1,15},{3,13... | collective-permute-start | bytes 393224 | tf_op jit(solution)/shard_map/ppermute | solution.py:192
  39.9 0.1 collective-permute-start.12
  40.0 2.7 %collective-permute-start.14 = (bf16[512,128]{1,0:T(8,128)(2,1)S(1)}, bf16[512,128]{1,0:T(8,128)(2,1)S(1)}, u32[]{:S(2)}, u32[]{:S(2)}) collective-permute-start(bf16[512,128]{1,0:T(8,128)(2,1)S(1)} %get-tuple-element.41), channel_id=1, source_target_pairs={{0,10},{2,8},{4,14},{6,12},{8,2},{10,0},{12,6},{14,4},{1,11},{3,9}... | collective-permute-start | bytes 393224 | tf_op jit(solution)/shard_map/ppermute | solution.py:192
  42.7 1.7 %collective-permute-start.13 = (bf16[512,128]{1,0:T(8,128)(2,1)S(1)}, bf16[512,128]{1,0:T(8,128)(2,1)S(1)}, u32[]{:S(2)}, u32[]{:S(2)}) collective-permute-start(bf16[512,128]{1,0:T(8,128)(2,1)S(1)} %get-tuple-element.46), channel_id=1, source_target_pairs={{0,6},{2,4},{4,2},{6,0},{8,14},{10,12},{12,10},{14,8},{1,7},{3,5},... | collective-permute-start | bytes 393224 | tf_op jit(solution)/shard_map/ppermute | solution.py:192
  44.4 1.5 %shard_map.75 = bf16[128,4096]{1,0:T(8,128)(2,1)} custom-call(s32[1]{0:T(128)} %bitcast.here, f32[128,128]{1,0:T(8,128)S(1)} %get-tuple-element.27.live, f32[128,128]{1,0:T(8,128)S(1)} %shard_map.72.mine, f32[128,128]{1,0:T(8,128)S(1)} %collective-permute-done.7.other, bf16[512,128]{1,0:T(8,128)(2,1)S(1)} %collective-permute-done.1.refs_0_, ...), custom_call_target="tpu_custom_call" | custom-call | flops 134217728 | bytes 2097152 | tf_op jit(solution)/shard_map/pallas_call | solution.py:274
  45.9 0.8 %collective-permute-done.11.refs_3_ = bf16[512,128]{1,0:T(8,128)(2,1)S(1)} collective-permute-done((bf16[512,128]{1,0:T(8,128)(2,1)S(1)}, bf16[512,128]{1,0:T(8,128)(2,1)S(1)}, u32[]{:S(2)}, u32[]{:S(2)}) %collective-permute-start.11) | collective-permute-done | bytes 131104 | tf_op jit(solution)/shard_map/ppermute | solution.py:192
  46.7 1.4 %shard_map.76.refs_8_ = bf16[96,512,128]{2,1,0:T(8,128)(2,1)} custom-call(s32[8]{0:T(128)S(1)} %get-tuple-element.44.blocks, s32[1]{0:T(128)} %bitcast.here, f32[8,128]{1,0:T(8,128)S(1)} %get-tuple-element.45.parts, bf16[512,128]{1,0:T(8,128)(2,1)S(1)} %collective-permute-done.8.refs_0_, ...), custom_call_target="tpu_custom_call", output_to_operand_aliasing={{}: (8, {})} | custom-call | bytes 2097152 | tf_op jit(solution)/shard_map/pallas_call | solution.py:287
  48.2 6.8 %collective-permute-done.12.refs_4_ = bf16[512,128]{1,0:T(8,128)(2,1)S(1)} collective-permute-done((bf16[512,128]{1,0:T(8,128)(2,1)S(1)}, bf16[512,128]{1,0:T(8,128)(2,1)S(1)}, u32[]{:S(2)}, u32[]{:S(2)}) %collective-permute-start.12) | collective-permute-done | bytes 131104 | tf_op jit(solution)/shard_map/ppermute | solution.py:192
  55.0 2.3 %collective-permute-done.14.refs_6_ = bf16[512,128]{1,0:T(8,128)(2,1)S(1)} collective-permute-done((bf16[512,128]{1,0:T(8,128)(2,1)S(1)}, bf16[512,128]{1,0:T(8,128)(2,1)S(1)}, u32[]{:S(2)}, u32[]{:S(2)}) %collective-permute-start.14) | collective-permute-done | bytes 131104 | tf_op jit(solution)/shard_map/ppermute | solution.py:192
  57.3 1.3 %shard_map.77 = bf16[96,512,128]{2,1,0:T(8,128)(2,1)} custom-call(s32[8]{0:T(128)S(1)} %get-tuple-element.44.blocks, s32[1]{0:T(128)} %bitcast.here, f32[8,128]{1,0:T(8,128)S(1)} %get-tuple-element.45.parts, bf16[512,128]{1,0:T(8,128)(2,1)S(1)} %collective-permute-done.8.refs_0_, ...), custom_call_target="tpu_custom_call", output_to_operand_aliasing={{}: (11, {})} | custom-call | bytes 2097152 | tf_op jit(solution)/shard_map/pallas_call | solution.py:287
  (17 shorter events, 0.0 us)
Async XLA Ops:
  0.6 0.7 %copy-start.2 = (s32[8,1]{0,1:T(1,128)S(1)}, s32[8,1]{0,1:T(1,128)}, u32[]{:S(2)}) copy-start(s32[8,1]{0,1:T(1,128)} %param.8) | copy-start | bytes 100
  1.3 17.8 %copy-start = (bf16[128,4096]{1,0:T(8,128)(2,1)S(1)}, bf16[128,4096]{1,0:T(8,128)(2,1)}, u32[]{:S(2)}) copy-start(bf16[128,4096]{1,0:T(8,128)(2,1)} %x.3) | copy-start | bytes 3145732
  1.3 17.8 %copy-start.1 = (bf16[128,4096]{1,0:T(8,128)(2,1)S(1)}, bf16[128,4096]{1,0:T(8,128)(2,1)}, u32[]{:S(2)}) copy-start(bf16[128,4096]{1,0:T(8,128)(2,1)} %y.5) | copy-start | bytes 3145732
  1.3 17.8 %copy-start.3 = (s32[8,1]{0,1:T(1,128)S(1)}, s32[8,1]{0,1:T(1,128)}, u32[]{:S(2)}) copy-start(s32[8,1]{0,1:T(1,128)} %param.9) | copy-start | bytes 100
  2.9 11.8 %collective-permute-start.1 = (bf16[512,128]{1,0:T(8,128)(2,1)S(1)}, bf16[512,128]{1,0:T(8,128)(2,1)S(1)}, u32[]{:S(2)}, u32[]{:S(2)}) collective-permute-start(bf16[512,128]{1,0:T(8,128)(2,1)S(1)} %shard_map.68), channel_id=1, source_target_pairs={{0,8},{2,10},{4,12},{6,14},{8,0},{10,2},{12,4},{14,6},{1,9},{3,11}... | collective-permute-start | bytes 393224 | tf_op jit(solution)/shard_map/ppermute | solution.py:192
  8.8 7.5 %collective-permute-start = (bf16[512,128]{1,0:T(8,128)(2,1)S(1)}, bf16[512,128]{1,0:T(8,128)(2,1)S(1)}, u32[]{:S(2)}, u32[]{:S(2)}) collective-permute-start(bf16[512,128]{1,0:T(8,128)(2,1)S(1)} %get-tuple-element.26), channel_id=1, source_target_pairs={{0,2},{2,0},{4,6},{6,4},{8,10},{10,8},{12,14},{14,12},{1,3},{3,1},... | collective-permute-start | bytes 393224 | tf_op jit(solution)/shard_map/ppermute | solution.py:192
  10.3 14.8 %collective-permute-start.2 = (bf16[512,128]{1,0:T(8,128)(2,1)S(1)}, bf16[512,128]{1,0:T(8,128)(2,1)S(1)}, u32[]{:S(2)}, u32[]{:S(2)}) collective-permute-start(bf16[512,128]{1,0:T(8,128)(2,1)S(1)} %get-tuple-element.30), channel_id=1, source_target_pairs={{0,4},{2,6},{4,0},{6,2},{8,12},{10,14},{12,8},{14,10},{1,5},{3,7},... | collective-permute-start | bytes 393224 | tf_op jit(solution)/shard_map/ppermute | solution.py:192
  11.9 14.8 %collective-permute-start.3 = (bf16[512,128]{1,0:T(8,128)(2,1)S(1)}, bf16[512,128]{1,0:T(8,128)(2,1)S(1)}, u32[]{:S(2)}, u32[]{:S(2)}) collective-permute-start(bf16[512,128]{1,0:T(8,128)(2,1)S(1)} %get-tuple-element.31), channel_id=1, source_target_pairs={{0,10},{2,8},{4,14},{6,12},{8,2},{10,0},{12,6},{14,4},{1,11},{3,9}... | collective-permute-start | bytes 393224 | tf_op jit(solution)/shard_map/ppermute | solution.py:192
  12.2 14.5 %collective-permute-start.4 = (bf16[512,128]{1,0:T(8,128)(2,1)S(1)}, bf16[512,128]{1,0:T(8,128)(2,1)S(1)}, u32[]{:S(2)}, u32[]{:S(2)}) collective-permute-start(bf16[512,128]{1,0:T(8,128)(2,1)S(1)} %get-tuple-element.32), channel_id=1, source_target_pairs={{0,12},{2,14},{4,8},{6,10},{8,4},{10,6},{12,0},{14,2},{1,13},{3,15... | collective-permute-start | bytes 393224 | tf_op jit(solution)/shard_map/ppermute | solution.py:192
  14.7 13.1 %collective-permute-start.5 = (bf16[512,128]{1,0:T(8,128)(2,1)S(1)}, bf16[512,128]{1,0:T(8,128)(2,1)S(1)}, u32[]{:S(2)}, u32[]{:S(2)}) collective-permute-start(bf16[512,128]{1,0:T(8,128)(2,1)S(1)} %get-tuple-element.34), channel_id=1, source_target_pairs={{0,6},{2,4},{4,2},{6,0},{8,14},{10,12},{12,10},{14,8},{1,7},{3,5},... | collective-permute-start | bytes 393224 | tf_op jit(solution)/shard_map/ppermute | solution.py:192
  16.3 11.5 %collective-permute-start.6 = (bf16[512,128]{1,0:T(8,128)(2,1)S(1)}, bf16[512,128]{1,0:T(8,128)(2,1)S(1)}, u32[]{:S(2)}, u32[]{:S(2)}) collective-permute-start(bf16[512,128]{1,0:T(8,128)(2,1)S(1)} %get-tuple-element.35), channel_id=1, source_target_pairs={{0,14},{2,12},{4,10},{6,8},{8,6},{10,4},{12,2},{14,0},{1,15},{3,13... | collective-permute-start | bytes 393224 | tf_op jit(solution)/shard_map/ppermute | solution.py:192
  28.1 1.3 %collective-permute-start.7 = (f32[128,128]{1,0:T(8,128)S(1)}, f32[128,128]{1,0:T(8,128)S(1)}, u32[]{:S(2)}, u32[]{:S(2)}) collective-permute-start(f32[128,128]{1,0:T(8,128)S(1)} %shard_map.72.mine), channel_id=1, source_target_pairs={{0,1},{1,0},{2,3},{3,2},{4,5},{5,4},{6,7},{7,6},{8,9},{9,8},{10,11... | collective-permute-start | bytes 196616 | tf_op jit(solution)/shard_map/ppermute | solution.py:198
  29.8 10.2 %collective-permute-start.8 = (bf16[512,128]{1,0:T(8,128)(2,1)S(1)}, bf16[512,128]{1,0:T(8,128)(2,1)S(1)}, u32[]{:S(2)}, u32[]{:S(2)}) collective-permute-start(bf16[512,128]{1,0:T(8,128)(2,1)S(1)} %shard_map.73), channel_id=1, source_target_pairs={{0,12},{2,14},{4,8},{6,10},{8,4},{10,6},{12,0},{14,2},{1,13},{3,15... | collective-permute-start | bytes 393224 | tf_op jit(solution)/shard_map/ppermute | solution.py:192
  33.2 9.5 %collective-permute-start.9 = (bf16[512,128]{1,0:T(8,128)(2,1)S(1)}, bf16[512,128]{1,0:T(8,128)(2,1)S(1)}, u32[]{:S(2)}, u32[]{:S(2)}) collective-permute-start(bf16[512,128]{1,0:T(8,128)(2,1)S(1)} %get-tuple-element.36), channel_id=1, source_target_pairs={{0,2},{2,0},{4,6},{6,4},{8,10},{10,8},{12,14},{14,12},{1,3},{3,1},... | collective-permute-start | bytes 393224 | tf_op jit(solution)/shard_map/ppermute | solution.py:192
  34.5 11.4 %collective-permute-start.10 = (bf16[512,128]{1,0:T(8,128)(2,1)S(1)}, bf16[512,128]{1,0:T(8,128)(2,1)S(1)}, u32[]{:S(2)}, u32[]{:S(2)}) collective-permute-start(bf16[512,128]{1,0:T(8,128)(2,1)S(1)} %get-tuple-element.37), channel_id=1, source_target_pairs={{0,4},{2,6},{4,0},{6,2},{8,12},{10,14},{12,8},{14,10},{1,5},{3,7},... | collective-permute-start | bytes 393224 | tf_op jit(solution)/shard_map/ppermute | solution.py:192
  37.6 9.1 %collective-permute-start.11 = (bf16[512,128]{1,0:T(8,128)(2,1)S(1)}, bf16[512,128]{1,0:T(8,128)(2,1)S(1)}, u32[]{:S(2)}, u32[]{:S(2)}) collective-permute-start(bf16[512,128]{1,0:T(8,128)(2,1)S(1)} %get-tuple-element.38), channel_id=1, source_target_pairs={{0,14},{2,12},{4,10},{6,8},{8,6},{10,4},{12,2},{14,0},{1,15},{3,13... | collective-permute-start | bytes 393224 | tf_op jit(solution)/shard_map/ppermute | solution.py:192
  39.9 15.1 %collective-permute-start.12 = (bf16[512,128]{1,0:T(8,128)(2,1)S(1)}, bf16[512,128]{1,0:T(8,128)(2,1)S(1)}, u32[]{:S(2)}, u32[]{:S(2)}) collective-permute-start(bf16[512,128]{1,0:T(8,128)(2,1)S(1)} %get-tuple-element.39), channel_id=1, source_target_pairs={{0,8},{2,10},{4,12},{6,14},{8,0},{10,2},{12,4},{14,6},{1,9},{3,11}... | collective-permute-start | bytes 393224 | tf_op jit(solution)/shard_map/ppermute | solution.py:192
  40.0 17.3 %collective-permute-start.14 = (bf16[512,128]{1,0:T(8,128)(2,1)S(1)}, bf16[512,128]{1,0:T(8,128)(2,1)S(1)}, u32[]{:S(2)}, u32[]{:S(2)}) collective-permute-start(bf16[512,128]{1,0:T(8,128)(2,1)S(1)} %get-tuple-element.41), channel_id=1, source_target_pairs={{0,10},{2,8},{4,14},{6,12},{8,2},{10,0},{12,6},{14,4},{1,11},{3,9}... | collective-permute-start | bytes 393224 | tf_op jit(solution)/shard_map/ppermute | solution.py:192
  42.7 14.5 %collective-permute-start.13 = (bf16[512,128]{1,0:T(8,128)(2,1)S(1)}, bf16[512,128]{1,0:T(8,128)(2,1)S(1)}, u32[]{:S(2)}, u32[]{:S(2)}) collective-permute-start(bf16[512,128]{1,0:T(8,128)(2,1)S(1)} %get-tuple-element.46), channel_id=1, source_target_pairs={{0,6},{2,4},{4,2},{6,0},{8,14},{10,12},{12,10},{14,8},{1,7},{3,5},... | collective-permute-start | bytes 393224 | tf_op jit(solution)/shard_map/ppermute | solution.py:192

commit v28 on v26

--- a/solution.py
+++ b/solution.py
@@ -10,7 +10,7 @@
 adapter_alpha = 128.0
 FETCH = (4, 1, 2, 5, 6, 3, 7)
 FETCH_TIES = {3: 4}
-SEND = (6, 1, 2, 4, 5, 3, 7)
+SEND = (6, 1, 4, 2, 5, 3, 7)
 SEND_TIES = {3: 6}
 PREP_AFTER = 1
 LATE = (5, 3, 7)

time: 57.8 us -> 57.8 us (level)
  waiting for transfers between devices: 14.5 us -> 11.5 us
  starting transfers between devices: 26.4 us -> 29.3 us
    ppermute x14, waiting for transfers between devices: 13.2 us -> 10.3 us  [exchange(): out[k] = lax.ppermute(piece, 'dp', [(i, i ^ k) for i in range(owners)])]
    ppermute x14, starting transfers between devices: 26.3 us -> 29.2 us  [exchange(): out[k] = lax.ppermute(piece, 'dp', [(i, i ^ k) for i in range(owners)])]
  transfers between devices with their start and end apart: 15 -> 15, of which waited for: 5 -> 6; matrix products, arithmetic and copies ran while one was open for 0% -> 0% of each run, Pallas kernels for 21% -> 21%
where the time goes in v28:
time: 57.8 us; the launch traced here: 57.6 us
  starting transfers between devices  29.3 us (51%)
  Pallas kernels  15.4 us (27%)
  waiting for transfers between devices  11.5 us (20%)
  between operations  0.76 us (1%)
  local copies, waits for them, and re-layouts  0.66 us (1%)
    ppermute x14, starting transfers between devices, exchange(): out[k] = lax.ppermute(piece, 'dp', [(i, i ^ k) for i in range(owners)])  29.2 us
    ppermute x14, waiting for transfers between devices, exchange(): out[k] = lax.ppermute(piece, 'dp', [(i, i ^ k) for i in range(owners)])  10.3 us
    pallas_call x1, Pallas kernels, with_kernels(): call(prep_kernel, [jax.ShapeDtypeStruct((owners, rows, 2 * tokens), bf16)...  5.95 us
    pallas_call x2, Pallas kernels, with_kernels(): call(functools.partial(gather_kernel, part), [straight] * len(part), [in_...  3.35 us
    pallas_call x2, Pallas kernels, merge(): call(functools.partial(merge_kernel, tuple(merged), handled, others), jax...  2.76 us
    pallas_call x1, Pallas kernels, with_kernels(): call(functools.partial(input_kernel, tuple(pairs), scale), jax.ShapeDtype...  1.45 us
    ppermute x1, waiting for transfers between devices, across_cores(): return lax.ppermute(value, 'tensor', [(i, i ^ 1) for i in range(cores)])  1.24 us
  transfers between devices with their start and end apart: 15, of which 6 were waited for; matrix products, arithmetic and copies ran while one was open for 0% of the time, Pallas kernels for 21%

profile of v28, /device:TPU:0, one launch (start us, length us, event | category | flops | bytes accessed | tf_op | source)
XLA Modules:
  0.0 57.6 jit_solution(6669869463020959050)
XLA Ops:
  0.6 0.6 %copy-done.2 = s32[8,1]{0,1:T(1,128)S(1)} copy-done((s32[8,1]{0,1:T(1,128)S(1)}, s32[8,1]{0,1:T(1,128)}, u32[]{:S(2)}) %copy-start.2) | copy-done | bytes 56
  1.3 1.6 %shard_map.68 = bf16[512,128]{1,0:T(8,128)(2,1)S(1)} custom-call(s32[8]{0:T(128)S(1)} %bitcast.7, s32[1]{0:T(128)} %bitcast.here, bf16[96,512,128]{2,1,0:T(8,128)(2,1)} %bitcast.11), custom_call_target="tpu_custom_call" | custom-call | bytes 1024 | tf_op jit(solution)/shard_map/pallas_call | solution.py:216
  2.9 4.1 %collective-permute-start.1 = (bf16[512,128]{1,0:T(8,128)(2,1)S(1)}, bf16[512,128]{1,0:T(8,128)(2,1)S(1)}, u32[]{:S(2)}, u32[]{:S(2)}) collective-permute-start(bf16[512,128]{1,0:T(8,128)(2,1)S(1)} %shard_map.68), channel_id=1, source_target_pairs={{0,8},{2,10},{4,12},{6,14},{8,0},{10,2},{12,4},{14,6},{1,9},{3,11}... | collective-permute-start | bytes 393224 | tf_op jit(solution)/shard_map/ppermute | solution.py:192
  7.0 1.8 %shard_map.69 = (bf16[512,128]{1,0:T(8,128)(2,1)S(1)}, bf16[512,128]{1,0:T(8,128)(2,1)S(1)}, bf16[512,128]{1,0:T(8,128)(2,1)S(1)}, bf16[512,128]{1,0:T(8,128)(2,...) custom-call(s32[8]{0:T(128)S(1)} %bitcast.8, s32[1]{0:T(128)} %bitcast.here, ...), custom_call_target="tpu_custom_call" | custom-call | bytes 1024 | tf_op jit(solution)/shard_map/pallas_call | solution.py:216
  8.8 1.6 %collective-permute-start = (bf16[512,128]{1,0:T(8,128)(2,1)S(1)}, bf16[512,128]{1,0:T(8,128)(2,1)S(1)}, u32[]{:S(2)}, u32[]{:S(2)}) collective-permute-start(bf16[512,128]{1,0:T(8,128)(2,1)S(1)} %get-tuple-element.27), channel_id=1, source_target_pairs={{0,2},{2,0},{4,6},{6,4},{8,10},{10,8},{12,14},{14,12},{1,3},{3,1},... | collective-permute-start | bytes 393224 | tf_op jit(solution)/shard_map/ppermute | solution.py:192
  10.3 1.6 %collective-permute-start.2 = (bf16[512,128]{1,0:T(8,128)(2,1)S(1)}, bf16[512,128]{1,0:T(8,128)(2,1)S(1)}, u32[]{:S(2)}, u32[]{:S(2)}) collective-permute-start(bf16[512,128]{1,0:T(8,128)(2,1)S(1)} %get-tuple-element.31), channel_id=1, source_target_pairs={{0,4},{2,6},{4,0},{6,2},{8,12},{10,14},{12,8},{14,10},{1,5},{3,7},... | collective-permute-start | bytes 393224 | tf_op jit(solution)/shard_map/ppermute | solution.py:192
  11.9 0.3 collective-permute-start.3
  12.2 2.5 %collective-permute-start.4 = (bf16[512,128]{1,0:T(8,128)(2,1)S(1)}, bf16[512,128]{1,0:T(8,128)(2,1)S(1)}, u32[]{:S(2)}, u32[]{:S(2)}) collective-permute-start(bf16[512,128]{1,0:T(8,128)(2,1)S(1)} %get-tuple-element.33), channel_id=1, source_target_pairs={{0,12},{2,14},{4,8},{6,10},{8,4},{10,6},{12,0},{14,2},{1,13},{3,15... | collective-permute-start | bytes 393224 | tf_op jit(solution)/shard_map/ppermute | solution.py:192
  14.7 4.4 %collective-permute-start.6 = (bf16[512,128]{1,0:T(8,128)(2,1)S(1)}, bf16[512,128]{1,0:T(8,128)(2,1)S(1)}, u32[]{:S(2)}, u32[]{:S(2)}) collective-permute-start(bf16[512,128]{1,0:T(8,128)(2,1)S(1)} %get-tuple-element.37), channel_id=1, source_target_pairs={{0,14},{2,12},{4,10},{6,8},{8,6},{10,4},{12,2},{14,0},{1,15},{3,13... | collective-permute-start | bytes 393224 | tf_op jit(solution)/shard_map/ppermute | solution.py:192
  19.1 0.0 collective-permute-done.after.refs_1_
  19.1 5.9 %shard_map.70 = (bf16[8,512,256]{2,1,0:T(8,128)(2,1)S(1)}, bf16[512,128]{1,0:T(8,128)(2,1)S(1)}, f32[128,128]{1,0:T(8,128)S(1)}, f32[8,128]{1,0:T(8,128)S(1)}, s...) custom-call(s32[8]{0:T(128)S(1)} %bitcast.9, s32[1]{0:T(128)} %bitcast.here, s32[8]{0:T(128)S(1)} %bitcast.10, ...), custom_call_target="tpu_custom_call" | custom-call | bytes 16777216 | tf_op jit(solution)/shard_map/pallas_call | solution.py:229
  25.1 1.6 %collective-permute-done.3.refs_3_ = bf16[512,128]{1,0:T(8,128)(2,1)S(1)} collective-permute-done((bf16[512,128]{1,0:T(8,128)(2,1)S(1)}, bf16[512,128]{1,0:T(8,128)(2,1)S(1)}, u32[]{:S(2)}, u32[]{:S(2)}) %collective-permute-start.3) | collective-permute-done | bytes 131104 | tf_op jit(solution)/shard_map/ppermute | solution.py:192
  26.7 0.6 shard_map.71.so_far
  27.3 2.0 %collective-permute-done.5.refs_0_.refs_5_ = bf16[512,128]{1,0:T(8,128)(2,1)S(1)} collective-permute-done((bf16[512,128]{1,0:T(8,128)(2,1)S(1)}, bf16[512,128]{1,0:T(8,128)(2,1)S(1)}, u32[]{:S(2)}, u32[]{:S(2)}) %collective-permute-start.5) | collective-permute-done | bytes 131104 | tf_op jit(solution)/shard_map/ppermute | solution.py:192
  29.3 0.3 shard_map.72.mine
  29.6 0.1 collective-permute-start.7
  29.7 1.2 %collective-permute-done.7.other = f32[128,128]{1,0:T(8,128)S(1)} collective-permute-done((f32[128,128]{1,0:T(8,128)S(1)}, f32[128,128]{1,0:T(8,128)S(1)}, u32[]{:S(2)}, u32[]{:S(2)}) %collective-permute-start.7) | collective-permute-done | bytes 65568 | tf_op jit(solution)/shard_map/ppermute | solution.py:198
  30.9 0.3 shard_map.73
  31.2 1.7 %collective-permute-start.8 = (bf16[512,128]{1,0:T(8,128)(2,1)S(1)}, bf16[512,128]{1,0:T(8,128)(2,1)S(1)}, u32[]{:S(2)}, u32[]{:S(2)}) collective-permute-start(bf16[512,128]{1,0:T(8,128)(2,1)S(1)} %shard_map.73), channel_id=1, source_target_pairs={{0,12},{2,14},{4,8},{6,10},{8,4},{10,6},{12,0},{14,2},{1,13},{3,15... | collective-permute-start | bytes 393224 | tf_op jit(solution)/shard_map/ppermute | solution.py:192
  32.9 0.7 %shard_map.74 = (bf16[512,128]{1,0:T(8,128)(2,1)S(1)}, bf16[512,128]{1,0:T(8,128)(2,1)S(1)}, bf16[512,128]{1,0:T(8,128)(2,1)S(1)}, bf16[512,128]{1,0:T(8,128)(2,...) custom-call(s32[1]{0:T(128)} %bitcast.here, ...), custom_call_target="tpu_custom_call" | custom-call | bytes 1024 | tf_op jit(solution)/shard_map/pallas_call | solution.py:264
  33.6 0.9 %collective-permute-start.9 = (bf16[512,128]{1,0:T(8,128)(2,1)S(1)}, bf16[512,128]{1,0:T(8,128)(2,1)S(1)}, u32[]{:S(2)}, u32[]{:S(2)}) collective-permute-start(bf16[512,128]{1,0:T(8,128)(2,1)S(1)} %get-tuple-element.38), channel_id=1, source_target_pairs={{0,2},{2,0},{4,6},{6,4},{8,10},{10,8},{12,14},{14,12},{1,3},{3,1},... | collective-permute-start | bytes 393224 | tf_op jit(solution)/shard_map/ppermute | solution.py:192
  34.5 2.9 %collective-permute-start.10 = (bf16[512,128]{1,0:T(8,128)(2,1)S(1)}, bf16[512,128]{1,0:T(8,128)(2,1)S(1)}, u32[]{:S(2)}, u32[]{:S(2)}) collective-permute-start(bf16[512,128]{1,0:T(8,128)(2,1)S(1)} %get-tuple-element.39), channel_id=1, source_target_pairs={{0,8},{2,10},{4,12},{6,14},{8,0},{10,2},{12,4},{14,6},{1,9},{3,11}... | collective-permute-start | bytes 393224 | tf_op jit(solution)/shard_map/ppermute | solution.py:192
  37.4 0.2 collective-permute-start.11
  37.6 3.8 %collective-permute-start.12 = (bf16[512,128]{1,0:T(8,128)(2,1)S(1)}, bf16[512,128]{1,0:T(8,128)(2,1)S(1)}, u32[]{:S(2)}, u32[]{:S(2)}) collective-permute-start(bf16[512,128]{1,0:T(8,128)(2,1)S(1)} %get-tuple-element.41), channel_id=1, source_target_pairs={{0,10},{2,8},{4,14},{6,12},{8,2},{10,0},{12,6},{14,4},{1,11},{3,9}... | collective-permute-start | bytes 393224 | tf_op jit(solution)/shard_map/ppermute | solution.py:192
  41.4 1.3 %collective-permute-start.14 = (bf16[512,128]{1,0:T(8,128)(2,1)S(1)}, bf16[512,128]{1,0:T(8,128)(2,1)S(1)}, u32[]{:S(2)}, u32[]{:S(2)}) collective-permute-start(bf16[512,128]{1,0:T(8,128)(2,1)S(1)} %get-tuple-element.43), channel_id=1, source_target_pairs={{0,14},{2,12},{4,10},{6,8},{8,6},{10,4},{12,2},{14,0},{1,15},{3,13... | collective-permute-start | bytes 393224 | tf_op jit(solution)/shard_map/ppermute | solution.py:192
  42.7 4.0 %collective-permute-start.13 = (bf16[512,128]{1,0:T(8,128)(2,1)S(1)}, bf16[512,128]{1,0:T(8,128)(2,1)S(1)}, u32[]{:S(2)}, u32[]{:S(2)}) collective-permute-start(bf16[512,128]{1,0:T(8,128)(2,1)S(1)} %get-tuple-element.48), channel_id=1, source_target_pairs={{0,6},{2,4},{4,2},{6,0},{8,14},{10,12},{12,10},{14,8},{1,7},{3,5},... | collective-permute-start | bytes 393224 | tf_op jit(solution)/shard_map/ppermute | solution.py:192
  46.7 1.5 %shard_map.75 = bf16[128,4096]{1,0:T(8,128)(2,1)} custom-call(s32[1]{0:T(128)} %bitcast.here, f32[128,128]{1,0:T(8,128)S(1)} %get-tuple-element.28.live, f32[128,128]{1,0:T(8,128)S(1)} %shard_map.72.mine, f32[128,128]{1,0:T(8,128)S(1)} %collective-permute-done.7.other, bf16[512,128]{1,0:T(8,128)(2,1)S(1)} %collective-permute-done.1.refs_0_, ...), custom_call_target="tpu_custom_call" | custom-call | flops 134217728 | bytes 2097152 | tf_op jit(solution)/shard_map/pallas_call | solution.py:274
  48.2 4.7 %collective-permute-done.10.refs_2_ = bf16[512,128]{1,0:T(8,128)(2,1)S(1)} collective-permute-done((bf16[512,128]{1,0:T(8,128)(2,1)S(1)}, bf16[512,128]{1,0:T(8,128)(2,1)S(1)}, u32[]{:S(2)}, u32[]{:S(2)}) %collective-permute-start.10) | collective-permute-done | bytes 131104 | tf_op jit(solution)/shard_map/ppermute | solution.py:192
  52.9 1.4 %shard_map.76.refs_8_ = bf16[96,512,128]{2,1,0:T(8,128)(2,1)} custom-call(s32[8]{0:T(128)S(1)} %get-tuple-element.46.blocks, s32[1]{0:T(128)} %bitcast.here, f32[8,128]{1,0:T(8,128)S(1)} %get-tuple-element.47.parts, bf16[512,128]{1,0:T(8,128)(2,1)S(1)} %collective-permute-done.8.refs_0_, ...), custom_call_target="tpu_custom_call", output_to_operand_aliasing={{}: (8, {})} | custom-call | bytes 2097152 | tf_op jit(solution)/shard_map/pallas_call | solution.py:287
  54.3 1.2 %collective-permute-done.12.refs_4_ = bf16[512,128]{1,0:T(8,128)(2,1)S(1)} collective-permute-done((bf16[512,128]{1,0:T(8,128)(2,1)S(1)}, bf16[512,128]{1,0:T(8,128)(2,1)S(1)}, u32[]{:S(2)}, u32[]{:S(2)}) %collective-permute-start.12) | collective-permute-done | bytes 131104 | tf_op jit(solution)/shard_map/ppermute | solution.py:192
  55.5 0.8 %collective-permute-done.13.refs_5_ = bf16[512,128]{1,0:T(8,128)(2,1)S(1)} collective-permute-done((bf16[512,128]{1,0:T(8,128)(2,1)S(1)}, bf16[512,128]{1,0:T(8,128)(2,1)S(1)}, u32[]{:S(2)}, u32[]{:S(2)}) %collective-permute-start.13) | collective-permute-done | bytes 131104 | tf_op jit(solution)/shard_map/ppermute | solution.py:192
  56.3 1.3 %shard_map.77 = bf16[96,512,128]{2,1,0:T(8,128)(2,1)} custom-call(s32[8]{0:T(128)S(1)} %get-tuple-element.46.blocks, s32[1]{0:T(128)} %bitcast.here, f32[8,128]{1,0:T(8,128)S(1)} %get-tuple-element.47.parts, bf16[512,128]{1,0:T(8,128)(2,1)S(1)} %collective-permute-done.8.refs_0_, ...), custom_call_target="tpu_custom_call", output_to_operand_aliasing={{}: (11, {})} | custom-call | bytes 2097152 | tf_op jit(solution)/shard_map/pallas_call | solution.py:287
  (17 shorter events, 0.0 us)
Async XLA Ops:
  0.6 0.7 %copy-start.2 = (s32[8,1]{0,1:T(1,128)S(1)}, s32[8,1]{0,1:T(1,128)}, u32[]{:S(2)}) copy-start(s32[8,1]{0,1:T(1,128)} %param.8) | copy-start | bytes 100
  1.3 17.8 %copy-start = (bf16[128,4096]{1,0:T(8,128)(2,1)S(1)}, bf16[128,4096]{1,0:T(8,128)(2,1)}, u32[]{:S(2)}) copy-start(bf16[128,4096]{1,0:T(8,128)(2,1)} %x.3) | copy-start | bytes 3145732
  1.3 17.8 %copy-start.1 = (bf16[128,4096]{1,0:T(8,128)(2,1)S(1)}, bf16[128,4096]{1,0:T(8,128)(2,1)}, u32[]{:S(2)}) copy-start(bf16[128,4096]{1,0:T(8,128)(2,1)} %y.5) | copy-start | bytes 3145732
  1.3 17.8 %copy-start.3 = (s32[8,1]{0,1:T(1,128)S(1)}, s32[8,1]{0,1:T(1,128)}, u32[]{:S(2)}) copy-start(s32[8,1]{0,1:T(1,128)} %param.9) | copy-start | bytes 100
  2.9 11.8 %collective-permute-start.1 = (bf16[512,128]{1,0:T(8,128)(2,1)S(1)}, bf16[512,128]{1,0:T(8,128)(2,1)S(1)}, u32[]{:S(2)}, u32[]{:S(2)}) collective-permute-start(bf16[512,128]{1,0:T(8,128)(2,1)S(1)} %shard_map.68), channel_id=1, source_target_pairs={{0,8},{2,10},{4,12},{6,14},{8,0},{10,2},{12,4},{14,6},{1,9},{3,11}... | collective-permute-start | bytes 393224 | tf_op jit(solution)/shard_map/ppermute | solution.py:192
  8.8 10.4 %collective-permute-start = (bf16[512,128]{1,0:T(8,128)(2,1)S(1)}, bf16[512,128]{1,0:T(8,128)(2,1)S(1)}, u32[]{:S(2)}, u32[]{:S(2)}) collective-permute-start(bf16[512,128]{1,0:T(8,128)(2,1)S(1)} %get-tuple-element.27), channel_id=1, source_target_pairs={{0,2},{2,0},{4,6},{6,4},{8,10},{10,8},{12,14},{14,12},{1,3},{3,1},... | collective-permute-start | bytes 393224 | tf_op jit(solution)/shard_map/ppermute | solution.py:192
  10.3 14.8 %collective-permute-start.2 = (bf16[512,128]{1,0:T(8,128)(2,1)S(1)}, bf16[512,128]{1,0:T(8,128)(2,1)S(1)}, u32[]{:S(2)}, u32[]{:S(2)}) collective-permute-start(bf16[512,128]{1,0:T(8,128)(2,1)S(1)} %get-tuple-element.31), channel_id=1, source_target_pairs={{0,4},{2,6},{4,0},{6,2},{8,12},{10,14},{12,8},{14,10},{1,5},{3,7},... | collective-permute-start | bytes 393224 | tf_op jit(solution)/shard_map/ppermute | solution.py:192
  11.9 14.8 %collective-permute-start.3 = (bf16[512,128]{1,0:T(8,128)(2,1)S(1)}, bf16[512,128]{1,0:T(8,128)(2,1)S(1)}, u32[]{:S(2)}, u32[]{:S(2)}) collective-permute-start(bf16[512,128]{1,0:T(8,128)(2,1)S(1)} %get-tuple-element.32), channel_id=1, source_target_pairs={{0,10},{2,8},{4,14},{6,12},{8,2},{10,0},{12,6},{14,4},{1,11},{3,9}... | collective-permute-start | bytes 393224 | tf_op jit(solution)/shard_map/ppermute | solution.py:192
  12.2 14.5 %collective-permute-start.4 = (bf16[512,128]{1,0:T(8,128)(2,1)S(1)}, bf16[512,128]{1,0:T(8,128)(2,1)S(1)}, u32[]{:S(2)}, u32[]{:S(2)}) collective-permute-start(bf16[512,128]{1,0:T(8,128)(2,1)S(1)} %get-tuple-element.33), channel_id=1, source_target_pairs={{0,12},{2,14},{4,8},{6,10},{8,4},{10,6},{12,0},{14,2},{1,13},{3,15... | collective-permute-start | bytes 393224 | tf_op jit(solution)/shard_map/ppermute | solution.py:192
  14.7 12.6 %collective-permute-start.6 = (bf16[512,128]{1,0:T(8,128)(2,1)S(1)}, bf16[512,128]{1,0:T(8,128)(2,1)S(1)}, u32[]{:S(2)}, u32[]{:S(2)}) collective-permute-start(bf16[512,128]{1,0:T(8,128)(2,1)S(1)} %get-tuple-element.37), channel_id=1, source_target_pairs={{0,14},{2,12},{4,10},{6,8},{8,6},{10,4},{12,2},{14,0},{1,15},{3,13... | collective-permute-start | bytes 393224 | tf_op jit(solution)/shard_map/ppermute | solution.py:192
  19.1 10.2 %collective-permute-start.5 = (bf16[512,128]{1,0:T(8,128)(2,1)S(1)}, bf16[512,128]{1,0:T(8,128)(2,1)S(1)}, u32[]{:S(2)}, u32[]{:S(2)}) collective-permute-start(bf16[512,128]{1,0:T(8,128)(2,1)S(1)} %get-tuple-element.36), channel_id=1, source_target_pairs={{0,6},{2,4},{4,2},{6,0},{8,14},{10,12},{12,10},{14,8},{1,7},{3,5},... | collective-permute-start | bytes 393224 | tf_op jit(solution)/shard_map/ppermute | solution.py:192
  29.6 1.3 %collective-permute-start.7 = (f32[128,128]{1,0:T(8,128)S(1)}, f32[128,128]{1,0:T(8,128)S(1)}, u32[]{:S(2)}, u32[]{:S(2)}) collective-permute-start(f32[128,128]{1,0:T(8,128)S(1)} %shard_map.72.mine), channel_id=1, source_target_pairs={{0,1},{1,0},{2,3},{3,2},{4,5},{5,4},{6,7},{7,6},{8,9},{9,8},{10,11... | collective-permute-start | bytes 196616 | tf_op jit(solution)/shard_map/ppermute | solution.py:198
  31.2 10.2 %collective-permute-start.8 = (bf16[512,128]{1,0:T(8,128)(2,1)S(1)}, bf16[512,128]{1,0:T(8,128)(2,1)S(1)}, u32[]{:S(2)}, u32[]{:S(2)}) collective-permute-start(bf16[512,128]{1,0:T(8,128)(2,1)S(1)} %shard_map.73), channel_id=1, source_target_pairs={{0,12},{2,14},{4,8},{6,10},{8,4},{10,6},{12,0},{14,2},{1,13},{3,15... | collective-permute-start | bytes 393224 | tf_op jit(solution)/shard_map/ppermute | solution.py:192
  33.6 9.1 %collective-permute-start.9 = (bf16[512,128]{1,0:T(8,128)(2,1)S(1)}, bf16[512,128]{1,0:T(8,128)(2,1)S(1)}, u32[]{:S(2)}, u32[]{:S(2)}) collective-permute-start(bf16[512,128]{1,0:T(8,128)(2,1)S(1)} %get-tuple-element.38), channel_id=1, source_target_pairs={{0,2},{2,0},{4,6},{6,4},{8,10},{10,8},{12,14},{14,12},{1,3},{3,1},... | collective-permute-start | bytes 393224 | tf_op jit(solution)/shard_map/ppermute | solution.py:192
  34.5 18.3 %collective-permute-start.10 = (bf16[512,128]{1,0:T(8,128)(2,1)S(1)}, bf16[512,128]{1,0:T(8,128)(2,1)S(1)}, u32[]{:S(2)}, u32[]{:S(2)}) collective-permute-start(bf16[512,128]{1,0:T(8,128)(2,1)S(1)} %get-tuple-element.39), channel_id=1, source_target_pairs={{0,8},{2,10},{4,12},{6,14},{8,0},{10,2},{12,4},{14,6},{1,9},{3,11}... | collective-permute-start | bytes 393224 | tf_op jit(solution)/shard_map/ppermute | solution.py:192
  37.4 15.4 %collective-permute-start.11 = (bf16[512,128]{1,0:T(8,128)(2,1)S(1)}, bf16[512,128]{1,0:T(8,128)(2,1)S(1)}, u32[]{:S(2)}, u32[]{:S(2)}) collective-permute-start(bf16[512,128]{1,0:T(8,128)(2,1)S(1)} %get-tuple-element.40), channel_id=1, source_target_pairs={{0,4},{2,6},{4,0},{6,2},{8,12},{10,14},{12,8},{14,10},{1,5},{3,7},... | collective-permute-start | bytes 393224 | tf_op jit(solution)/shard_map/ppermute | solution.py:192
  37.6 17.9 %collective-permute-start.12 = (bf16[512,128]{1,0:T(8,128)(2,1)S(1)}, bf16[512,128]{1,0:T(8,128)(2,1)S(1)}, u32[]{:S(2)}, u32[]{:S(2)}) collective-permute-start(bf16[512,128]{1,0:T(8,128)(2,1)S(1)} %get-tuple-element.41), channel_id=1, source_target_pairs={{0,10},{2,8},{4,14},{6,12},{8,2},{10,0},{12,6},{14,4},{1,11},{3,9}... | collective-permute-start | bytes 393224 | tf_op jit(solution)/shard_map/ppermute | solution.py:192
  41.4 14.1 %collective-permute-start.14 = (bf16[512,128]{1,0:T(8,128)(2,1)S(1)}, bf16[512,128]{1,0:T(8,128)(2,1)S(1)}, u32[]{:S(2)}, u32[]{:S(2)}) collective-permute-start(bf16[512,128]{1,0:T(8,128)(2,1)S(1)} %get-tuple-element.43), channel_id=1, source_target_pairs={{0,14},{2,12},{4,10},{6,8},{8,6},{10,4},{12,2},{14,0},{1,15},{3,13... | collective-permute-start | bytes 393224 | tf_op jit(solution)/shard_map/ppermute | solution.py:192
  42.7 13.6 %collective-permute-start.13 = (bf16[512,128]{1,0:T(8,128)(2,1)S(1)}, bf16[512,128]{1,0:T(8,128)(2,1)S(1)}, u32[]{:S(2)}, u32[]{:S(2)}) collective-permute-start(bf16[512,128]{1,0:T(8,128)(2,1)S(1)} %get-tuple-element.48), channel_id=1, source_target_pairs={{0,6},{2,4},{4,2},{6,0},{8,14},{10,12},{12,10},{14,8},{1,7},{3,5},... | collective-permute-start | bytes 393224 | tf_op jit(solution)/shard_map/ppermute | solution.py:192

commit v29 on v28

--- a/solution.py
+++ b/solution.py
@@ -9,7 +9,7 @@
 
 adapter_alpha = 128.0
 FETCH = (4, 1, 2, 5, 6, 3, 7)
-FETCH_TIES = {3: 4}
+FETCH_TIES = {}
 SEND = (6, 1, 4, 2, 5, 3, 7)
 SEND_TIES = {3: 6}
 PREP_AFTER = 1

time: 57.8 us -> 57.1 us (0.988); the launches traced: 57.6 us -> 56.1 us
  waiting for transfers between devices: 11.5 us -> 8.81 us
  starting transfers between devices: 29.3 us -> 30.5 us
    ppermute x14, waiting for transfers between devices: 10.3 us -> 7.57 us  [exchange(): out[k] = lax.ppermute(piece, 'dp', [(i, i ^ k) for i in range(owners)])]
    ppermute x14, starting transfers between devices: 29.2 us -> 30.4 us  [exchange(): out[k] = lax.ppermute(piece, 'dp', [(i, i ^ k) for i in range(owners)])]
where the time goes in v29:
time: 57.1 us; the launch traced here: 56.1 us
  starting transfers between devices  30.5 us (53%)
  Pallas kernels  15.4 us (27%)
  waiting for transfers between devices  8.81 us (15%)
  between operations  0.74 us (1%)
  local copies, waits for them, and re-layouts  0.66 us (1%)
    ppermute x14, starting transfers between devices, exchange(): out[k] = lax.ppermute(piece, 'dp', [(i, i ^ k) for i in range(owners)])  30.4 us
    ppermute x14, waiting for transfers between devices, exchange(): out[k] = lax.ppermute(piece, 'dp', [(i, i ^ k) for i in range(owners)])  7.57 us
    pallas_call x1, Pallas kernels, with_kernels(): call(prep_kernel, [jax.ShapeDtypeStruct((owners, rows, 2 * tokens), bf16)...  5.94 us
    pallas_call x2, Pallas kernels, with_kernels(): call(functools.partial(gather_kernel, part), [straight] * len(part), [in_...  3.35 us
    pallas_call x2, Pallas kernels, merge(): call(functools.partial(merge_kernel, tuple(merged), handled, others), jax...  2.76 us
    pallas_call x1, Pallas kernels, with_kernels(): call(functools.partial(input_kernel, tuple(pairs), scale), jax.ShapeDtype...  1.45 us
    ppermute x1, waiting for transfers between devices, across_cores(): return lax.ppermute(value, 'tensor', [(i, i ^ 1) for i in range(cores)])  1.24 us
  transfers between devices with their start and end apart: 15, of which 6 were waited for; matrix products, arithmetic and copies ran while one was open for 0% of the time, Pallas kernels for 21%

profile of v29, /device:TPU:0, one launch (start us, length us, event | category | flops | bytes accessed | tf_op | source)
XLA Modules:
  0.0 56.1 jit_solution(1929315318654406947)
XLA Ops:
  0.6 0.6 %copy-done.2 = s32[8,1]{0,1:T(1,128)S(1)} copy-done((s32[8,1]{0,1:T(1,128)S(1)}, s32[8,1]{0,1:T(1,128)}, u32[]{:S(2)}) %copy-start.2) | copy-done | bytes 56
  1.3 1.6 %shard_map.68 = bf16[512,128]{1,0:T(8,128)(2,1)S(1)} custom-call(s32[8]{0:T(128)S(1)} %bitcast.7, s32[1]{0:T(128)} %bitcast.here, bf16[96,512,128]{2,1,0:T(8,128)(2,1)} %bitcast.11), custom_call_target="tpu_custom_call" | custom-call | bytes 1024 | tf_op jit(solution)/shard_map/pallas_call | solution.py:216
  2.9 4.1 %collective-permute-start.1 = (bf16[512,128]{1,0:T(8,128)(2,1)S(1)}, bf16[512,128]{1,0:T(8,128)(2,1)S(1)}, u32[]{:S(2)}, u32[]{:S(2)}) collective-permute-start(bf16[512,128]{1,0:T(8,128)(2,1)S(1)} %shard_map.68), channel_id=1, source_target_pairs={{0,8},{2,10},{4,12},{6,14},{8,0},{10,2},{12,4},{14,6},{1,9},{3,11}... | collective-permute-start | bytes 393224 | tf_op jit(solution)/shard_map/ppermute | solution.py:192
  7.0 1.8 %shard_map.69 = (bf16[512,128]{1,0:T(8,128)(2,1)S(1)}, bf16[512,128]{1,0:T(8,128)(2,1)S(1)}, bf16[512,128]{1,0:T(8,128)(2,1)S(1)}, bf16[512,128]{1,0:T(8,128)(2,...) custom-call(s32[8]{0:T(128)S(1)} %bitcast.8, s32[1]{0:T(128)} %bitcast.here, ...), custom_call_target="tpu_custom_call" | custom-call | bytes 1024 | tf_op jit(solution)/shard_map/pallas_call | solution.py:216
  8.8 1.6 %collective-permute-start = (bf16[512,128]{1,0:T(8,128)(2,1)S(1)}, bf16[512,128]{1,0:T(8,128)(2,1)S(1)}, u32[]{:S(2)}, u32[]{:S(2)}) collective-permute-start(bf16[512,128]{1,0:T(8,128)(2,1)S(1)} %get-tuple-element.26), channel_id=1, source_target_pairs={{0,2},{2,0},{4,6},{6,4},{8,10},{10,8},{12,14},{14,12},{1,3},{3,1},... | collective-permute-start | bytes 393224 | tf_op jit(solution)/shard_map/ppermute | solution.py:192
  10.3 1.6 %collective-permute-start.2 = (bf16[512,128]{1,0:T(8,128)(2,1)S(1)}, bf16[512,128]{1,0:T(8,128)(2,1)S(1)}, u32[]{:S(2)}, u32[]{:S(2)}) collective-permute-start(bf16[512,128]{1,0:T(8,128)(2,1)S(1)} %get-tuple-element.30), channel_id=1, source_target_pairs={{0,4},{2,6},{4,0},{6,2},{8,12},{10,14},{12,8},{14,10},{1,5},{3,7},... | collective-permute-start | bytes 393224 | tf_op jit(solution)/shard_map/ppermute | solution.py:192
  11.9 0.3 collective-permute-start.3
  12.2 2.5 %collective-permute-start.4 = (bf16[512,128]{1,0:T(8,128)(2,1)S(1)}, bf16[512,128]{1,0:T(8,128)(2,1)S(1)}, u32[]{:S(2)}, u32[]{:S(2)}) collective-permute-start(bf16[512,128]{1,0:T(8,128)(2,1)S(1)} %get-tuple-element.32), channel_id=1, source_target_pairs={{0,12},{2,14},{4,8},{6,10},{8,4},{10,6},{12,0},{14,2},{1,13},{3,15... | collective-permute-start | bytes 393224 | tf_op jit(solution)/shard_map/ppermute | solution.py:192
  14.7 1.6 %collective-permute-start.5 = (bf16[512,128]{1,0:T(8,128)(2,1)S(1)}, bf16[512,128]{1,0:T(8,128)(2,1)S(1)}, u32[]{:S(2)}, u32[]{:S(2)}) collective-permute-start(bf16[512,128]{1,0:T(8,128)(2,1)S(1)} %get-tuple-element.34), channel_id=1, source_target_pairs={{0,6},{2,4},{4,2},{6,0},{8,14},{10,12},{12,10},{14,8},{1,7},{3,5},... | collective-permute-start | bytes 393224 | tf_op jit(solution)/shard_map/ppermute | solution.py:192
  16.3 2.8 %collective-permute-start.6 = (bf16[512,128]{1,0:T(8,128)(2,1)S(1)}, bf16[512,128]{1,0:T(8,128)(2,1)S(1)}, u32[]{:S(2)}, u32[]{:S(2)}) collective-permute-start(bf16[512,128]{1,0:T(8,128)(2,1)S(1)} %get-tuple-element.35), channel_id=1, source_target_pairs={{0,14},{2,12},{4,10},{6,8},{8,6},{10,4},{12,2},{14,0},{1,15},{3,13... | collective-permute-start | bytes 393224 | tf_op jit(solution)/shard_map/ppermute | solution.py:192
  19.1 5.9 %shard_map.70 = (bf16[8,512,256]{2,1,0:T(8,128)(2,1)S(1)}, bf16[512,128]{1,0:T(8,128)(2,1)S(1)}, f32[128,128]{1,0:T(8,128)S(1)}, f32[8,128]{1,0:T(8,128)S(1)}, s...) custom-call(s32[8]{0:T(128)S(1)} %bitcast.9, s32[1]{0:T(128)} %bitcast.here, s32[8]{0:T(128)S(1)} %bitcast.10, ...), custom_call_target="tpu_custom_call" | custom-call | bytes 16777216 | tf_op jit(solution)/shard_map/pallas_call | solution.py:229
  25.1 1.6 %collective-permute-done.3.refs_3_ = bf16[512,128]{1,0:T(8,128)(2,1)S(1)} collective-permute-done((bf16[512,128]{1,0:T(8,128)(2,1)S(1)}, bf16[512,128]{1,0:T(8,128)(2,1)S(1)}, u32[]{:S(2)}, u32[]{:S(2)}) %collective-permute-start.3) | collective-permute-done | bytes 131104 | tf_op jit(solution)/shard_map/ppermute | solution.py:192
  26.7 0.6 %shard_map.71.so_far = f32[128,128]{1,0:T(8,128)S(1)} custom-call(s32[1]{0:T(128)} %bitcast.here, bf16[128,4096]{1,0:T(8,128)(2,1)S(1)} %copy-done, bf16[128,4096]{1,0:T(8,128)(2,1)S(1)} %copy-done.1, f32[128,128]{1,0:T(8,128)S(1)} %broadcast_in_dim.6.so_far, bf16[512,128]{1,0:T(8,128)(2,1)S(1)} %collective-permute-done.1.refs_0_, ...), custom_call_target="tpu_custom_call" | custom-call | bytes 1024 | tf_op jit(solution)/shard_map/pallas_call | solution.py:252
  27.3 0.6 %collective-permute-done.5.refs_0_.refs_5_ = bf16[512,128]{1,0:T(8,128)(2,1)S(1)} collective-permute-done((bf16[512,128]{1,0:T(8,128)(2,1)S(1)}, bf16[512,128]{1,0:T(8,128)(2,1)S(1)}, u32[]{:S(2)}, u32[]{:S(2)}) %collective-permute-start.5) | collective-permute-done | bytes 131104 | tf_op jit(solution)/shard_map/ppermute | solution.py:192
  27.8 0.3 shard_map.72.mine
  28.1 0.1 collective-permute-start.7
  28.2 1.2 %collective-permute-done.7.other = f32[128,128]{1,0:T(8,128)S(1)} collective-permute-done((f32[128,128]{1,0:T(8,128)S(1)}, f32[128,128]{1,0:T(8,128)S(1)}, u32[]{:S(2)}, u32[]{:S(2)}) %collective-permute-start.7) | collective-permute-done | bytes 65568 | tf_op jit(solution)/shard_map/ppermute | solution.py:198
  29.5 0.3 shard_map.73
  29.8 2.7 %collective-permute-start.8 = (bf16[512,128]{1,0:T(8,128)(2,1)S(1)}, bf16[512,128]{1,0:T(8,128)(2,1)S(1)}, u32[]{:S(2)}, u32[]{:S(2)}) collective-permute-start(bf16[512,128]{1,0:T(8,128)(2,1)S(1)} %shard_map.73), channel_id=1, source_target_pairs={{0,12},{2,14},{4,8},{6,10},{8,4},{10,6},{12,0},{14,2},{1,13},{3,15... | collective-permute-start | bytes 393224 | tf_op jit(solution)/shard_map/ppermute | solution.py:192
  32.5 0.7 %shard_map.74 = (bf16[512,128]{1,0:T(8,128)(2,1)S(1)}, bf16[512,128]{1,0:T(8,128)(2,1)S(1)}, bf16[512,128]{1,0:T(8,128)(2,1)S(1)}, bf16[512,128]{1,0:T(8,128)(2,...) custom-call(s32[1]{0:T(128)} %bitcast.here, ...), custom_call_target="tpu_custom_call" | custom-call | bytes 1024 | tf_op jit(solution)/shard_map/pallas_call | solution.py:264
  33.2 1.3 %collective-permute-start.9 = (bf16[512,128]{1,0:T(8,128)(2,1)S(1)}, bf16[512,128]{1,0:T(8,128)(2,1)S(1)}, u32[]{:S(2)}, u32[]{:S(2)}) collective-permute-start(bf16[512,128]{1,0:T(8,128)(2,1)S(1)} %get-tuple-element.36), channel_id=1, source_target_pairs={{0,2},{2,0},{4,6},{6,4},{8,10},{10,8},{12,14},{14,12},{1,3},{3,1},... | collective-permute-start | bytes 393224 | tf_op jit(solution)/shard_map/ppermute | solution.py:192
  34.5 2.9 %collective-permute-start.10 = (bf16[512,128]{1,0:T(8,128)(2,1)S(1)}, bf16[512,128]{1,0:T(8,128)(2,1)S(1)}, u32[]{:S(2)}, u32[]{:S(2)}) collective-permute-start(bf16[512,128]{1,0:T(8,128)(2,1)S(1)} %get-tuple-element.37), channel_id=1, source_target_pairs={{0,8},{2,10},{4,12},{6,14},{8,0},{10,2},{12,4},{14,6},{1,9},{3,11}... | collective-permute-start | bytes 393224 | tf_op jit(solution)/shard_map/ppermute | solution.py:192
  37.4 0.2 collective-permute-start.11
  37.6 3.8 %collective-permute-start.12 = (bf16[512,128]{1,0:T(8,128)(2,1)S(1)}, bf16[512,128]{1,0:T(8,128)(2,1)S(1)}, u32[]{:S(2)}, u32[]{:S(2)}) collective-permute-start(bf16[512,128]{1,0:T(8,128)(2,1)S(1)} %get-tuple-element.39), channel_id=1, source_target_pairs={{0,10},{2,8},{4,14},{6,12},{8,2},{10,0},{12,6},{14,4},{1,11},{3,9}... | collective-permute-start | bytes 393224 | tf_op jit(solution)/shard_map/ppermute | solution.py:192
  41.4 1.3 %collective-permute-start.14 = (bf16[512,128]{1,0:T(8,128)(2,1)S(1)}, bf16[512,128]{1,0:T(8,128)(2,1)S(1)}, u32[]{:S(2)}, u32[]{:S(2)}) collective-permute-start(bf16[512,128]{1,0:T(8,128)(2,1)S(1)} %get-tuple-element.41), channel_id=1, source_target_pairs={{0,14},{2,12},{4,10},{6,8},{8,6},{10,4},{12,2},{14,0},{1,15},{3,13... | collective-permute-start | bytes 393224 | tf_op jit(solution)/shard_map/ppermute | solution.py:192
  42.7 3.7 %collective-permute-start.13 = (bf16[512,128]{1,0:T(8,128)(2,1)S(1)}, bf16[512,128]{1,0:T(8,128)(2,1)S(1)}, u32[]{:S(2)}, u32[]{:S(2)}) collective-permute-start(bf16[512,128]{1,0:T(8,128)(2,1)S(1)} %get-tuple-element.46), channel_id=1, source_target_pairs={{0,6},{2,4},{4,2},{6,0},{8,14},{10,12},{12,10},{14,8},{1,7},{3,5},... | collective-permute-start | bytes 393224 | tf_op jit(solution)/shard_map/ppermute | solution.py:192
  46.4 1.5 %shard_map.75 = bf16[128,4096]{1,0:T(8,128)(2,1)} custom-call(s32[1]{0:T(128)} %bitcast.here, f32[128,128]{1,0:T(8,128)S(1)} %get-tuple-element.27.live, f32[128,128]{1,0:T(8,128)S(1)} %shard_map.72.mine, f32[128,128]{1,0:T(8,128)S(1)} %collective-permute-done.7.other, bf16[512,128]{1,0:T(8,128)(2,1)S(1)} %collective-permute-done.1.refs_0_, ...), custom_call_target="tpu_custom_call" | custom-call | flops 134217728 | bytes 2097152 | tf_op jit(solution)/shard_map/pallas_call | solution.py:274
  47.9 2.9 %collective-permute-done.10.refs_2_ = bf16[512,128]{1,0:T(8,128)(2,1)S(1)} collective-permute-done((bf16[512,128]{1,0:T(8,128)(2,1)S(1)}, bf16[512,128]{1,0:T(8,128)(2,1)S(1)}, u32[]{:S(2)}, u32[]{:S(2)}) %collective-permute-start.10) | collective-permute-done | bytes 131104 | tf_op jit(solution)/shard_map/ppermute | solution.py:192
  50.8 1.4 %shard_map.76.refs_8_ = bf16[96,512,128]{2,1,0:T(8,128)(2,1)} custom-call(s32[8]{0:T(128)S(1)} %get-tuple-element.44.blocks, s32[1]{0:T(128)} %bitcast.here, f32[8,128]{1,0:T(8,128)S(1)} %get-tuple-element.45.parts, bf16[512,128]{1,0:T(8,128)(2,1)S(1)} %collective-permute-done.8.refs_0_, ...), custom_call_target="tpu_custom_call", output_to_operand_aliasing={{}: (8, {})} | custom-call | bytes 2097152 | tf_op jit(solution)/shard_map/pallas_call | solution.py:287
  52.2 2.3 %collective-permute-done.12.refs_4_ = bf16[512,128]{1,0:T(8,128)(2,1)S(1)} collective-permute-done((bf16[512,128]{1,0:T(8,128)(2,1)S(1)}, bf16[512,128]{1,0:T(8,128)(2,1)S(1)}, u32[]{:S(2)}, u32[]{:S(2)}) %collective-permute-start.12) | collective-permute-done | bytes 131104 | tf_op jit(solution)/shard_map/ppermute | solution.py:192
  54.5 0.2 collective-permute-done.13.refs_5_
  54.7 1.3 %shard_map.77 = bf16[96,512,128]{2,1,0:T(8,128)(2,1)} custom-call(s32[8]{0:T(128)S(1)} %get-tuple-element.44.blocks, s32[1]{0:T(128)} %bitcast.here, f32[8,128]{1,0:T(8,128)S(1)} %get-tuple-element.45.parts, bf16[512,128]{1,0:T(8,128)(2,1)S(1)} %collective-permute-done.8.refs_0_, ...), custom_call_target="tpu_custom_call", output_to_operand_aliasing={{}: (11, {})} | custom-call | bytes 2097152 | tf_op jit(solution)/shard_map/pallas_call | solution.py:287
  (17 shorter events, 0.0 us)
Async XLA Ops:
  0.6 0.7 %copy-start.2 = (s32[8,1]{0,1:T(1,128)S(1)}, s32[8,1]{0,1:T(1,128)}, u32[]{:S(2)}) copy-start(s32[8,1]{0,1:T(1,128)} %param.8) | copy-start | bytes 100
  1.3 17.8 %copy-start = (bf16[128,4096]{1,0:T(8,128)(2,1)S(1)}, bf16[128,4096]{1,0:T(8,128)(2,1)}, u32[]{:S(2)}) copy-start(bf16[128,4096]{1,0:T(8,128)(2,1)} %x.3) | copy-start | bytes 3145732
  1.3 17.8 %copy-start.1 = (bf16[128,4096]{1,0:T(8,128)(2,1)S(1)}, bf16[128,4096]{1,0:T(8,128)(2,1)}, u32[]{:S(2)}) copy-start(bf16[128,4096]{1,0:T(8,128)(2,1)} %y.5) | copy-start | bytes 3145732
  1.3 17.8 %copy-start.3 = (s32[8,1]{0,1:T(1,128)S(1)}, s32[8,1]{0,1:T(1,128)}, u32[]{:S(2)}) copy-start(s32[8,1]{0,1:T(1,128)} %param.9) | copy-start | bytes 100
  2.9 11.8 %collective-permute-start.1 = (bf16[512,128]{1,0:T(8,128)(2,1)S(1)}, bf16[512,128]{1,0:T(8,128)(2,1)S(1)}, u32[]{:S(2)}, u32[]{:S(2)}) collective-permute-start(bf16[512,128]{1,0:T(8,128)(2,1)S(1)} %shard_map.68), channel_id=1, source_target_pairs={{0,8},{2,10},{4,12},{6,14},{8,0},{10,2},{12,4},{14,6},{1,9},{3,11}... | collective-permute-start | bytes 393224 | tf_op jit(solution)/shard_map/ppermute | solution.py:192
  8.8 7.5 %collective-permute-start = (bf16[512,128]{1,0:T(8,128)(2,1)S(1)}, bf16[512,128]{1,0:T(8,128)(2,1)S(1)}, u32[]{:S(2)}, u32[]{:S(2)}) collective-permute-start(bf16[512,128]{1,0:T(8,128)(2,1)S(1)} %get-tuple-element.26), channel_id=1, source_target_pairs={{0,2},{2,0},{4,6},{6,4},{8,10},{10,8},{12,14},{14,12},{1,3},{3,1},... | collective-permute-start | bytes 393224 | tf_op jit(solution)/shard_map/ppermute | solution.py:192
  10.3 14.8 %collective-permute-start.2 = (bf16[512,128]{1,0:T(8,128)(2,1)S(1)}, bf16[512,128]{1,0:T(8,128)(2,1)S(1)}, u32[]{:S(2)}, u32[]{:S(2)}) collective-permute-start(bf16[512,128]{1,0:T(8,128)(2,1)S(1)} %get-tuple-element.30), channel_id=1, source_target_pairs={{0,4},{2,6},{4,0},{6,2},{8,12},{10,14},{12,8},{14,10},{1,5},{3,7},... | collective-permute-start | bytes 393224 | tf_op jit(solution)/shard_map/ppermute | solution.py:192
  11.9 14.8 %collective-permute-start.3 = (bf16[512,128]{1,0:T(8,128)(2,1)S(1)}, bf16[512,128]{1,0:T(8,128)(2,1)S(1)}, u32[]{:S(2)}, u32[]{:S(2)}) collective-permute-start(bf16[512,128]{1,0:T(8,128)(2,1)S(1)} %get-tuple-element.31), channel_id=1, source_target_pairs={{0,10},{2,8},{4,14},{6,12},{8,2},{10,0},{12,6},{14,4},{1,11},{3,9}... | collective-permute-start | bytes 393224 | tf_op jit(solution)/shard_map/ppermute | solution.py:192
  12.2 14.5 %collective-permute-start.4 = (bf16[512,128]{1,0:T(8,128)(2,1)S(1)}, bf16[512,128]{1,0:T(8,128)(2,1)S(1)}, u32[]{:S(2)}, u32[]{:S(2)}) collective-permute-start(bf16[512,128]{1,0:T(8,128)(2,1)S(1)} %get-tuple-element.32), channel_id=1, source_target_pairs={{0,12},{2,14},{4,8},{6,10},{8,4},{10,6},{12,0},{14,2},{1,13},{3,15... | collective-permute-start | bytes 393224 | tf_op jit(solution)/shard_map/ppermute | solution.py:192
  14.7 13.1 %collective-permute-start.5 = (bf16[512,128]{1,0:T(8,128)(2,1)S(1)}, bf16[512,128]{1,0:T(8,128)(2,1)S(1)}, u32[]{:S(2)}, u32[]{:S(2)}) collective-permute-start(bf16[512,128]{1,0:T(8,128)(2,1)S(1)} %get-tuple-element.34), channel_id=1, source_target_pairs={{0,6},{2,4},{4,2},{6,0},{8,14},{10,12},{12,10},{14,8},{1,7},{3,5},... | collective-permute-start | bytes 393224 | tf_op jit(solution)/shard_map/ppermute | solution.py:192
  16.3 11.5 %collective-permute-start.6 = (bf16[512,128]{1,0:T(8,128)(2,1)S(1)}, bf16[512,128]{1,0:T(8,128)(2,1)S(1)}, u32[]{:S(2)}, u32[]{:S(2)}) collective-permute-start(bf16[512,128]{1,0:T(8,128)(2,1)S(1)} %get-tuple-element.35), channel_id=1, source_target_pairs={{0,14},{2,12},{4,10},{6,8},{8,6},{10,4},{12,2},{14,0},{1,15},{3,13... | collective-permute-start | bytes 393224 | tf_op jit(solution)/shard_map/ppermute | solution.py:192
  28.1 1.3 %collective-permute-start.7 = (f32[128,128]{1,0:T(8,128)S(1)}, f32[128,128]{1,0:T(8,128)S(1)}, u32[]{:S(2)}, u32[]{:S(2)}) collective-permute-start(f32[128,128]{1,0:T(8,128)S(1)} %shard_map.72.mine), channel_id=1, source_target_pairs={{0,1},{1,0},{2,3},{3,2},{4,5},{5,4},{6,7},{7,6},{8,9},{9,8},{10,11... | collective-permute-start | bytes 196616 | tf_op jit(solution)/shard_map/ppermute | solution.py:198
  29.8 11.7 %collective-permute-start.8 = (bf16[512,128]{1,0:T(8,128)(2,1)S(1)}, bf16[512,128]{1,0:T(8,128)(2,1)S(1)}, u32[]{:S(2)}, u32[]{:S(2)}) collective-permute-start(bf16[512,128]{1,0:T(8,128)(2,1)S(1)} %shard_map.73), channel_id=1, source_target_pairs={{0,12},{2,14},{4,8},{6,10},{8,4},{10,6},{12,0},{14,2},{1,13},{3,15... | collective-permute-start | bytes 393224 | tf_op jit(solution)/shard_map/ppermute | solution.py:192
  33.2 9.5 %collective-permute-start.9 = (bf16[512,128]{1,0:T(8,128)(2,1)S(1)}, bf16[512,128]{1,0:T(8,128)(2,1)S(1)}, u32[]{:S(2)}, u32[]{:S(2)}) collective-permute-start(bf16[512,128]{1,0:T(8,128)(2,1)S(1)} %get-tuple-element.36), channel_id=1, source_target_pairs={{0,2},{2,0},{4,6},{6,4},{8,10},{10,8},{12,14},{14,12},{1,3},{3,1},... | collective-permute-start | bytes 393224 | tf_op jit(solution)/shard_map/ppermute | solution.py:192
  34.5 16.2 %collective-permute-start.10 = (bf16[512,128]{1,0:T(8,128)(2,1)S(1)}, bf16[512,128]{1,0:T(8,128)(2,1)S(1)}, u32[]{:S(2)}, u32[]{:S(2)}) collective-permute-start(bf16[512,128]{1,0:T(8,128)(2,1)S(1)} %get-tuple-element.37), channel_id=1, source_target_pairs={{0,8},{2,10},{4,12},{6,14},{8,0},{10,2},{12,4},{14,6},{1,9},{3,11}... | collective-permute-start | bytes 393224 | tf_op jit(solution)/shard_map/ppermute | solution.py:192
  37.4 13.3 %collective-permute-start.11 = (bf16[512,128]{1,0:T(8,128)(2,1)S(1)}, bf16[512,128]{1,0:T(8,128)(2,1)S(1)}, u32[]{:S(2)}, u32[]{:S(2)}) collective-permute-start(bf16[512,128]{1,0:T(8,128)(2,1)S(1)} %get-tuple-element.38), channel_id=1, source_target_pairs={{0,4},{2,6},{4,0},{6,2},{8,12},{10,14},{12,8},{14,10},{1,5},{3,7},... | collective-permute-start | bytes 393224 | tf_op jit(solution)/shard_map/ppermute | solution.py:192
  37.6 16.9 %collective-permute-start.12 = (bf16[512,128]{1,0:T(8,128)(2,1)S(1)}, bf16[512,128]{1,0:T(8,128)(2,1)S(1)}, u32[]{:S(2)}, u32[]{:S(2)}) collective-permute-start(bf16[512,128]{1,0:T(8,128)(2,1)S(1)} %get-tuple-element.39), channel_id=1, source_target_pairs={{0,10},{2,8},{4,14},{6,12},{8,2},{10,0},{12,6},{14,4},{1,11},{3,9}... | collective-permute-start | bytes 393224 | tf_op jit(solution)/shard_map/ppermute | solution.py:192
  41.4 13.1 %collective-permute-start.14 = (bf16[512,128]{1,0:T(8,128)(2,1)S(1)}, bf16[512,128]{1,0:T(8,128)(2,1)S(1)}, u32[]{:S(2)}, u32[]{:S(2)}) collective-permute-start(bf16[512,128]{1,0:T(8,128)(2,1)S(1)} %get-tuple-element.41), channel_id=1, source_target_pairs={{0,14},{2,12},{4,10},{6,8},{8,6},{10,4},{12,2},{14,0},{1,15},{3,13... | collective-permute-start | bytes 393224 | tf_op jit(solution)/shard_map/ppermute | solution.py:192
  42.7 12.0 %collective-permute-start.13 = (bf16[512,128]{1,0:T(8,128)(2,1)S(1)}, bf16[512,128]{1,0:T(8,128)(2,1)S(1)}, u32[]{:S(2)}, u32[]{:S(2)}) collective-permute-start(bf16[512,128]{1,0:T(8,128)(2,1)S(1)} %get-tuple-element.46), channel_id=1, source_target_pairs={{0,6},{2,4},{4,2},{6,0},{8,14},{10,12},{12,10},{14,8},{1,7},{3,5},... | collective-permute-start | bytes 393224 | tf_op jit(solution)/shard_map/ppermute | solution.py:192
